TPU v7x, 256 devices: a whole 4x4x8 slice. The times are simulated.
256 devices in a mesh: batch: 32 (over x, y, core), head: 8 (over z).
Axes of the slice: x: 4, y: 4, z: 8, core: 2. Of those that a mesh axis runs over, the one named last changes fastest.
Arguments:
- queries: bfloat16 [1024, 16384], P('batch', 'head'), may hold values from -16 to 16
- new_kv: bfloat16 [2, 1024, 1024], P(None, 'batch', 'head'), may hold values from -16 to 16
- prefix_kv: bfloat16 [2, 65536, 1024], P(None, 'batch', 'head'), may hold values from -16 to 16
- suffix_kv: bfloat16 [2, 8192, 16, 1024], P(None, 'batch', None, 'head'), may hold values from -16 to 16
- page_table: int32 [1024, 8], P('batch'), may hold values from 0 to 8191, as said below
- suffix_len: int32 [1024], P('batch'), may hold values from 1 to 128
- prompt_of: int32 [1024], P('batch'), may hold values from 0 to 7, as said below
- out_weight: bfloat16 [16384, 16384], P('head', 'batch'), may hold values from -0.046875 to 0.046875
Outputs:
- projected: bfloat16 [1024, 16384], P('head', 'batch')
Inputs may be any that keep to these rules, and one draw needn't show every extreme that they name: `prompt_of`: each aligned block of 32 completions holds exactly 4 completions of every prompt. `page_table`: the rows of an aligned block b of 32 completions name every page of [b * 32 * 8, (b + 1) * 32 * 8) once.
All inputs are finite; a program needn't handle non-finite values.
Results may differ from a plain program's by a relative error of at most 0.0057.
Values may be sent and summed in bfloat16 or wider, within the bound.
No kernel may reach another device: no remote copies, remote signals or barrier semaphores. Data moves between devices by JAX's collectives and lax.ppermute only.
A program may use at most 64 MiB of HBM per device.

v0:
```python
import jax
import jax.numpy as jnp
from jax import lax
from jax.sharding import PartitionSpec as P

DH = 128
SAMPLES = 128


big_negative = -1e30


def prefix_partial(query_rows, prefix_keys, prefix_values, scale):
    scores = (
        jnp.einsum("rhge,khe->rhgk", query_rows, prefix_keys, preferred_element_type=jnp.float32)
        * scale
    )
    peak = jnp.max(scores, axis=3)
    weights = jnp.exp(scores - peak[..., None])
    total = jnp.sum(weights, axis=3)
    mixed = jnp.einsum(
        "rhgk,khe->rhge",
        weights.astype(jnp.bfloat16),
        prefix_values,
        preferred_element_type=jnp.float32,
    )
    return (mixed, peak, total)


def suffix_partial(local_q, new_kv, suffix_kv, page_table, suffix_len, offset, scale):
    count, heads, group, size = local_q.shape
    local_ids = page_table - offset
    pages = suffix_kv[:, local_ids]
    span_len = pages.shape[2] * pages.shape[3]
    pages = pages.reshape(2, count, span_len, heads, size)
    scores = (
        jnp.einsum("chge,cshe->chgs", local_q, pages[0], preferred_element_type=jnp.float32) * scale
    )
    valid = jnp.arange(span_len, dtype=jnp.int32)[None, :] < suffix_len[:, None]
    scores = jnp.where(valid[:, None, None, :], scores, big_negative)
    own_keys = new_kv[0].reshape(count, heads, size)
    own_values = new_kv[1].reshape(count, heads, size)
    own = jnp.einsum("chge,che->chg", local_q, own_keys, preferred_element_type=jnp.float32) * scale
    peak = jnp.maximum(jnp.max(scores, axis=3), own)
    weights = jnp.exp(scores - peak[..., None])
    own_weight = jnp.exp(own - peak)
    total = jnp.sum(weights, axis=3) + own_weight
    own_rounded = lax.optimization_barrier(own_weight.astype(jnp.bfloat16)).astype(jnp.float32)
    mixed = jnp.einsum(
        "chgs,cshe->chge",
        weights.astype(jnp.bfloat16),
        pages[1],
        preferred_element_type=jnp.float32,
    )
    mixed = mixed + own_rounded[..., None] * own_values.astype(jnp.float32)[:, :, None, :]
    return (mixed, peak, total)


def shards(queries, new_kv, prefix_kv, suffix_kv, page_table, suffix_len, prompt_of, out_weight):
    count = queries.shape[0]
    width = queries.shape[1]
    heads = new_kv.shape[2] // DH
    group = width // (heads * DH)
    scale = DH ** (-0.5)
    me = lax.axis_index("batch")
    local_q = queries.reshape(count, heads, group, DH)
    smixed, speak, stotal = suffix_partial(
        local_q, new_kv, suffix_kv, page_table, suffix_len, me * suffix_kv.shape[1], scale
    )
    prefix_keys = prefix_kv[0].reshape(-1, heads, DH)
    prefix_values = prefix_kv[1].reshape(-1, heads, DH)
    span = SAMPLES // count
    all_q, all_map = (
        lax.all_gather(queries, "batch", axis=0, tiled=True),
        lax.all_gather(prompt_of, "batch", axis=0, tiled=True),
    )
    every = all_q.shape[0]
    mine = me // span
    sort_keys = jnp.where(all_map == mine, 0, 1) * every + jnp.arange(every, dtype=jnp.int32)
    chosen = jnp.argsort(sort_keys)[:SAMPLES]
    mixed, peak, total = prefix_partial(
        all_q[chosen].reshape(SAMPLES, heads, group, DH), prefix_keys, prefix_values, scale
    )
    peak_all = jnp.full((every, heads, group), big_negative, jnp.float32).at[chosen].set(peak)
    top = lax.pmax(peak_all.astype(jnp.bfloat16), "batch").astype(peak_all.dtype)
    factor = jnp.exp(peak - top[chosen])
    mixed_all = (
        jnp.zeros((every, heads, group, DH), jnp.float32).at[chosen].set(mixed * factor[..., None])
    )
    total_all = jnp.zeros((every, heads, group), jnp.float32).at[chosen].set(total * factor)
    pmixed, ptotal = (
        lax.psum_scatter(mixed_all, "batch", scatter_dimension=0, tiled=True),
        lax.psum_scatter(total_all, "batch", scatter_dimension=0, tiled=True),
    )
    ppeak = lax.dynamic_slice_in_dim(top, me * count, count, 0)
    joint = jnp.maximum(ppeak, speak)
    first = jnp.exp(ppeak - joint)
    second = jnp.exp(speak - joint)
    attended = (pmixed * first[..., None] + smixed * second[..., None]) / (
        ptotal * first + stotal * second
    )[..., None]
    attended = attended.astype(jnp.bfloat16).reshape(count, width)
    all_rows = lax.all_gather(attended, "batch", axis=0, tiled=True)
    return lax.psum_scatter(
        jnp.dot(all_rows, out_weight, preferred_element_type=jnp.float32),
        "head",
        scatter_dimension=0,
        tiled=True,
    ).astype(jnp.bfloat16)


def solution(mesh):
    placed = (
        P("batch", "head"),
        P(None, "batch", "head"),
        P(None, "batch", "head"),
        P(None, "batch", None, "head"),
        P("batch", None),
        P("batch"),
        P("batch"),
        P("head", "batch"),
    )
    return jax.shard_map(
        shards, mesh=mesh, in_specs=placed, out_specs=P("head", "batch"), check_vma=False
    )
```

profile of v0, /device:TPU:1, one launch (start us, length us, event | category | flops | bytes accessed | tf_op | source)
XLA Modules:
  0.0 508.6 jit_solution(8338726278704231999)
XLA Ops:
  6.5 0.0 copy-start
  6.5 0.0 all-gather.3.cloned.1.call-start
  6.5 0.7 all-gather.3.cloned.1.call-update
  7.3 0.0 reduce-scatter.6.cloned.1.call-start
  7.3 1.3 dynamic-slice
  9.3 0.9 dynamic-update-slice
  10.1 14.5 %all-reduce = s32[1024]{0:T(1024)S(1)} all-reduce(s32[1024]{0:T(1024)S(1)} %dynamic-update-slice), channel_id=1, replica_groups=mesh['batch'=32,'head'=8] {'batch'}, use_global_device_ids=true, to_apply=%add | all-reduce | flops 1024 | bytes 8192
  24.6 4.4 sort.17
  29.0 36.4 %all-gather.3.cloned.1.call-done = bf16[1024,2048]{1,0:T(8,128)(2,1)} async-done(((bf16[32,2048]{1,0:T(8,128)(2,1)}), bf16[1024,2048]{1,0:T(8,128)(2,1)}) %all-gather.3.cloned.1.call-update) | async-done | bytes 4194320 | tf_op jit(solution)/shard_map/all_gather | solution.py:74
  65.4 4.2 gather_fusion
  69.5 9.1 %bitcast_reduce_fusion = (f32[128,16]{0,1:T(8,128)S(1)}, f32[128,16,2048]{2,0,1:T(8,128)}) fusion(bf16[2,2048,128]{2,1,0:T(8,128)(2,1)} %param.10, bf16[128,2048]{1,0:T(8,128)(2,1)S(1)} %gather_fusion), kind=kOutput, calls=%fused_computation.7 | convolution fusion | flops 1082128384 | bytes 17833984 | tf_op jit(solution)/shard_map/rhge,khe->rhgk/dot_general | solution.py:15
  78.6 0.1 copy.35
  78.7 7.5 %fusion.1 = f32[128,16]{0,1:T(8,128)S(1)} fusion(f32[128,16,2048]{2,0,1:T(8,128)} %get-tuple-element.20, f32[128,16]{0,1:T(8,128)S(1)} %get-tuple-element.19), kind=kLoop, calls=%fused_computation.9 | loop fusion | flops 12580864 | bytes 16793600 | tf_op jit(solution)/shard_map/reduce_sum | solution.py:20
  86.3 1.0 scatter_custom_fusion
  87.3 122.4 %pmax.7 = bf16[1024,1,16]{2,0,1:T(8,128)(2,1)S(1)} all-reduce(bf16[1024,1,16]{2,0,1:T(8,128)(2,1)S(1)} %convert_bitcast_fusion), channel_id=1, replica_groups=mesh['batch'=32,'head'=8] {'batch'}, use_global_device_ids=true, to_apply=%region_3.4 | all-reduce | flops 16384 | bytes 65536 | tf_op jit(solution)/shard_map/pmax | solution.py:85
  209.7 0.9 fusion.48
  210.6 0.6 gather_fusion.1
  211.3 0.1 copy.40
  211.4 1.7 scatter_custom_fusion.2
  213.1 0.0 reduce-scatter.6.cloned.1.call-update
  213.1 0.0 reduce-scatter.4.cloned.1.call-start
  213.2 7.4 %fusion.12 = f32[128,16,128]{2,0,1:T(8,128)S(1)} fusion(f32[128,16,2048]{2,0,1:T(8,128)} %get-tuple-element.20, f32[128,16]{0,1:T(8,128)S(1)} %get-tuple-element.19, f32[128,16]{0,1:T(8,128)S(1)} %get-tuple-element.10, bf16[2,2048,128]{2,1,0:T(8,128)(2,1)} %param.10), kind=kOutput, calls=%fused_computation.16 | convolution fusion | flops 1086586880 | bytes 18366464 | tf_op jit(solution)/shard_map/rhgk,khe->rhge/dot_general | solution.py:21
  220.6 0.6 copy.37
  221.2 3.8 broadcast.49
  225.0 13.7 %scatter_fusion = f32[1024,16,128]{2,1,0:T(8,128)} fusion(f32[1024,16,128]{2,1,0:T(8,128)} %broadcast.49, s32[128]{0:T(128)S(1)} %compare_select_fusion.1, f32[128,16,128]{2,1,0:T(8,128)S(1)} %copy.37), kind=kCustom, calls=%fused_computation.4 | custom fusion | bytes 3146240 | tf_op jit(solution)/shard_map/scatter | solution.py:88
  238.7 0.0 copy-start.3
  238.7 0.0 copy-start.1
  238.7 0.0 copy-start.4
  238.7 0.0 copy-start.2
  238.7 0.0 reduce-scatter.4.cloned.1.call-update
  238.8 0.2 all-gather.5.cloned.1.call-start
  239.0 0.4 copy-done.3
  239.4 0.1 copy.38
  239.5 0.1 reshape.192
  239.6 0.0 copy-done
  239.6 2.3 gather_fusion.2
  241.9 3.5 copy.56
  245.5 0.0 copy-done.1
  245.5 0.0 copy-done.4
  245.5 0.1 iota_compare_fusion
  245.6 0.0 copy-done.2
  245.6 0.6 bitcast_convert_fusion
  246.2 0.2 fusion.41
  246.4 1.9 fusion.47
  248.3 0.7 fusion.49
  249.0 0.7 fusion.44
  249.8 0.2 fusion.33
  250.1 47.6 %reduce-scatter.6.cloned.1.call-done = f32[32,1,16]{2,0,1:T(8,128)} async-done(((f32[1024,1,16]{2,0,1:T(8,128)}), f32[32,1,16]{2,0,1:T(8,128)}) %reduce-scatter.6.cloned.1.call-update) | async-done | bytes 2064 | tf_op jit(solution)/shard_map/reduce_scatter | solution.py:93
  297.6 0.8 fusion.43
  298.4 103.0 %reduce-scatter.4.cloned.1.call-done = f32[32,1,16,128]{3,2,0,1:T(8,128)} async-done(((f32[1024,1,16,128]{3,2,0,1:T(8,128)}), f32[32,1,16,128]{3,2,0,1:T(8,128)}) %reduce-scatter.4.cloned.1.call-update) | async-done | bytes 262160 | tf_op jit(solution)/shard_map/reduce_scatter | solution.py:92
  401.4 1.4 fusion.21
  402.8 0.7 copy.57
  403.5 0.0 all-gather.5.cloned.1.call-update
  403.5 0.0 reduce-scatter.8.cloned.1.call-start
  403.5 53.2 %all-gather.5.cloned.1.call-done = bf16[1024,2048]{1,0:T(8,128)(2,1)} async-done(((bf16[32,2048]{1,0:T(8,128)(2,1)}), bf16[1024,2048]{1,0:T(8,128)(2,1)}) %all-gather.5.cloned.1.call-update) | async-done | bytes 4194320 | tf_op jit(solution)/shard_map/all_gather | solution.py:103
  456.7 6.5 %fusion.50 = f32[1024,512]{1,0:T(8,128)} fusion(bf16[1024,2048]{1,0:T(8,128)(2,1)} %all-gather.5.cloned.1.call-done, bf16[2048,512]{1,0:T(8,128)(2,1)} %param.15), kind=kOutput, calls=%fused_computation.73 | convolution fusion | flops 2147483648 | bytes 8388608 | tf_op jit(solution)/shard_map/dot_general | solution.py:105
  463.2 0.0 reduce-scatter.8.cloned.1.call-update
  463.3 37.2 %reduce-scatter.8.cloned.1.call-done = f32[128,512]{1,0:T(8,128)} async-done(((f32[1024,512]{1,0:T(8,128)}), f32[128,512]{1,0:T(8,128)}) %reduce-scatter.8.cloned.1.call-update) | async-done | bytes 262160 | tf_op jit(solution)/shard_map/reduce_scatter | solution.py:104
  500.5 1.6 convert_element_type.47
  (13 shorter events, 0.2 us)
Async XLA Ops:
  6.5 233.1 %copy-start = (bf16[2,256,16,128]{3,2,1,0:T(8,128)(2,1)S(1)}, bf16[2,256,16,128]{3,2,1,0:T(8,128)(2,1)}, u32[]{:S(2)}) copy-start(bf16[2,256,16,128]{3,2,1,0:T(8,128)(2,1)} %param.11) | copy-start | bytes 6291460
  6.5 58.8 %all-gather.3.cloned.1.call-start = ((), (), s32[]{:S(2)}) async-start(), calls=%async_computation.3 | async-start | bytes 4325376 | tf_op jit(solution)/shard_map/all_gather | solution.py:74
  7.3 290.4 %reduce-scatter.6.cloned.1.call-start = ((), (), s32[]{:S(2)}) async-start(), calls=%async_computation.5 | async-start | bytes 540672 | tf_op jit(solution)/shard_map/reduce_scatter | solution.py:93
  213.1 188.3 %reduce-scatter.4.cloned.1.call-start = ((), (), s32[]{:S(2)}) async-start(), calls=%async_computation.4 | async-start | bytes 8650752 | tf_op jit(solution)/shard_map/reduce_scatter | solution.py:92
  238.7 0.7 copy-start.3
  238.7 6.7 %copy-start.1 = (bf16[32,2048]{1,0:T(8,128)(2,1)S(1)}, bf16[32,2048]{1,0:T(8,128)(2,1)}, u32[]{:S(2)}) copy-start(bf16[32,2048]{1,0:T(8,128)(2,1)} %param.8) | copy-start | bytes 393220
  238.7 6.8 %copy-start.4 = (s32[32]{0:T(128)S(1)}, s32[32]{0:T(128)}, u32[]{:S(2)}) copy-start(s32[32]{0:T(128)} %param.13) | copy-start | bytes 388
  238.7 6.8 %copy-start.2 = (bf16[2,32,128]{2,1,0:T(8,128)(2,1)S(1)}, bf16[2,32,128]{2,1,0:T(8,128)(2,1)}, u32[]{:S(2)}) copy-start(bf16[2,32,128]{2,1,0:T(8,128)(2,1)} %param.9) | copy-start | bytes 49156
  238.8 218.0 %all-gather.5.cloned.1.call-start = ((), (), s32[]{:S(2)}) async-start(), calls=%async_computation.6 | async-start | bytes 4325376 | tf_op jit(solution)/shard_map/all_gather | solution.py:103
  403.5 97.0 %reduce-scatter.8.cloned.1.call-start = ((), (), s32[]{:S(2)}) async-start(), calls=%async_computation.7 | async-start | bytes 2359296 | tf_op jit(solution)/shard_map/reduce_scatter | solution.py:104
Sparse Core Ops, SparseCore 0:
  9.9 55.3 all-gather.2
  213.2 84.3 reduce-scatter.5
  301.6 99.6 reduce-scatter.3
  404.1 52.5 all-gather.4
  463.4 37.0 reduce-scatter.7
where the time goes:
time: 513 us; the launch traced here: 509 us
  waiting for transfers between devices  278 us (54%)
  blocking collectives  137 us (27%)
  local copies, waits for them, and re-layouts  37.1 us (7%)
  matrix products  25.4 us (5%)
  other arithmetic  16.9 us (3%)
  between operations  14 us (3%)
    pmax x1, blocking collectives, shards(): lax.pmax(peak_all.astype(jnp.bfloat16), 'batch').astype(peak_all.dtype)  122 us
    reduce_scatter x1, waiting for transfers between devices, shards(): lax.psum_scatter(mixed_all, 'batch', scatter_dimension=0, tiled=True)  103 us
    all_gather x1, waiting for transfers between devices, shards(): all_rows = lax.all_gather(attended, 'batch', axis=0, tiled=True)  53.2 us
    reduce_scatter x1, waiting for transfers between devices, shards(): lax.psum_scatter(total_all, 'batch', scatter_dimension=0, tiled=True)  47.6 us
    reduce_scatter x1, waiting for transfers between devices, shards(): lax.psum_scatter(jnp.dot(all_rows, out_weight, preferred_element_type=jnp...  37.2 us
    all_gather x1, waiting for transfers between devices, shards(): lax.all_gather(queries, 'batch', axis=0, tiled=True)  36.4 us
    unnamed x1, blocking collectives  14.5 us
    scatter x1, local copies, waits for them, and re-layouts, shards(): jnp.zeros((every, heads, group, DH), jnp.float32).at[chosen]  13.7 us
  transfers between devices with their start and end apart: 5, of which 5 were waited for; matrix products, arithmetic and copies ran while one was open for 9% of the time, Pallas kernels for 0%

commit v1 on v0

v1 whole, which is shorter than its diff:
```python
import jax
import jax.numpy as jnp
from jax import lax
from jax.experimental import pallas as pl
from jax.experimental.pallas import tpu as pltpu
from jax.sharding import PartitionSpec as P

DH = 128
GROUP = 16
SCALE = DH**-0.5
LOG2E = 1.4426950408889634
BATCH = 32
HEADS = 8
VMEM = pl.BlockSpec(memory_space=pltpu.VMEM)
SMEM = pl.BlockSpec(memory_space=pltpu.SMEM)
F32 = jnp.float32
BF16 = jnp.bfloat16
NT = (((1,), (1,)), ((), ()))
NN = (((1,), (0,)), ((), ()))


def params():
    return pltpu.CompilerParams(vmem_limit_bytes=48 * 1024 * 1024)


def dot(a, b, dims=NN):
    return lax.dot_general(a, b, dims, preferred_element_type=F32)


def lanes():
    return lax.broadcasted_iota(jnp.int32, (GROUP, DH), 1)


def split_tile(tile, step):
    high = tile.astype(BF16).astype(F32)
    rest = tile - high
    middle = rest.astype(BF16).astype(F32)
    low = rest - middle
    joined = high + pltpu.roll(middle, step, 1) + pltpu.roll(low, 2 * step, 1)
    return joined.astype(BF16)


def join_tile(tile, step):
    wide = tile.astype(F32)
    return (wide + pltpu.roll(wide, DH - step, 1)) + pltpu.roll(wide, DH - 2 * step, 1)


def sort_body(place, prompt, q, o0, o1, o2, o3, held, seen):
    lane = lanes()
    tile = jnp.zeros((GROUP, DH), F32)
    for p in range(8):
        seen[p] = 0
    for r in range(32):
        p = prompt[r]
        k = seen[p]
        seen[p] = k + 1
        held[(4 * p + k) ^ place[0]] = q[r]
        tile = jnp.where(lane == r, (4 * p + k).astype(F32), tile)
    for i, out in enumerate((o0, o1, o2, o3)):
        out[0:8] = held[8 * i : 8 * i + 8]
        out[8] = tile.astype(BF16)


def sort_queries(place, prompt, q):
    out = jax.ShapeDtypeStruct((9, GROUP, DH), BF16)
    return pl.pallas_call(
        sort_body,
        out_shape=[out] * 4,
        in_specs=[SMEM, SMEM, VMEM],
        out_specs=[VMEM] * 4,
        scratch_shapes=[pltpu.VMEM((32, GROUP, DH), BF16), pltpu.SMEM((8,), jnp.int32)],
        compiler_params=params(),
        name="sort_queries",
    )(place, prompt, q)


def regroup_body(place, a0, a1, a2, a3, same, other):
    for i, a in enumerate((a0, a1, a2, a3)):
        same[4 * i : 4 * i + 4] = a[0:4]
        other[4 * i : 4 * i + 4] = a[4:8]

    for i, a in enumerate((a0, a1, a2, a3)):

        @pl.when(place[2] ^ (place[4] >> 1) == i)
        def _(a=a):
            same[16] = a[8]
            other[16] = a[8]


def regroup(place, parts):
    out = jax.ShapeDtypeStruct((17, GROUP, DH), BF16)
    return pl.pallas_call(
        regroup_body,
        out_shape=[out, out],
        in_specs=[SMEM] + [VMEM] * 4,
        out_specs=[VMEM] * 2,
        compiler_params=params(),
        name="regroup",
    )(place, *parts)


def suffix_body(place, prompt, table, length, q, new, pool, o0, o1, o2, o3, scores, weights, held, tiles, seen):
    lane = lanes()
    base = place[1]
    for n in range(32):
        keys = jnp.concatenate([pool[0, table[n, j] - base] for j in range(8)], axis=0)
        s = dot(q[n], keys, NT) * SCALE
        scores[n] = jnp.where(lane < length[n], s, -1e30)
    own_keys = new[0].astype(F32)
    own_values = new[1].astype(F32)
    own = jnp.stack(
        [
            jnp.sum(q[n].astype(F32) * own_keys[n : n + 1], axis=1, keepdims=True)
            for n in range(32)
        ]
    ) * SCALE
    s = scores[...]
    peak = jnp.maximum(jnp.max(s, axis=2, keepdims=True), own)
    w = jnp.exp(s - peak)
    own_weight = jnp.exp(own - peak)
    total = jnp.sum(w, axis=2, keepdims=True) + own_weight
    weights[...] = w.astype(BF16)
    own_weight = own_weight.astype(BF16).astype(F32)
    mass = peak + jnp.log(total)
    inverse = 1.0 / total
    tiles[...] = jnp.zeros_like(tiles)
    for p in range(8):
        seen[p] = 0
    for n in range(32):
        values = jnp.concatenate([pool[1, table[n, j] - base] for j in range(8)], axis=0)
        mixed = dot(weights[n], values) + own_weight[n] * own_values[n : n + 1]
        p = prompt[n]
        k = seen[p]
        seen[p] = k + 1
        slot = (4 * p + k) ^ place[0]
        held[slot] = (mixed * inverse[n]).astype(BF16)
        at = slot >> 3
        tiles[at] = jnp.where(lane == (slot & 7), mass[n], tiles[at])
    for i, out in enumerate((o0, o1, o2, o3)):
        out[0:8] = held[8 * i : 8 * i + 8]
        out[8] = split_tile(tiles[i], 8)


def suffix_parts(place, prompt, table, length, q, new, pool):
    out = jax.ShapeDtypeStruct((9, GROUP, DH), BF16)
    return pl.pallas_call(
        suffix_body,
        out_shape=[out] * 4,
        in_specs=[SMEM, SMEM, SMEM, SMEM, VMEM, VMEM, VMEM],
        out_specs=[VMEM] * 4,
        scratch_shapes=[
            pltpu.VMEM((32, GROUP, DH), F32),
            pltpu.VMEM((32, GROUP, DH), BF16),
            pltpu.VMEM((32, GROUP, DH), BF16),
            pltpu.VMEM((4, GROUP, DH), F32),
            pltpu.SMEM((8,), jnp.int32),
        ],
        compiler_params=params(),
        cost_estimate=pl.CostEstimate(flops=40_000_000, bytes_accessed=3_000_000, transcendentals=70000),
        name="suffix_parts",
    )(place, prompt, table, length, q, new, pool)


ROWS = 128


def prefix_block(q, kv0, kv1):
    s0 = dot(q, kv0[0], NT)
    s1 = dot(q, kv1[0], NT)
    peak = jnp.maximum(jnp.max(s0, axis=1, keepdims=True), jnp.max(s1, axis=1, keepdims=True))
    w0 = jnp.exp2((s0 - peak) * (SCALE * LOG2E))
    w1 = jnp.exp2((s1 - peak) * (SCALE * LOG2E))
    total = jnp.sum(w0, axis=1, keepdims=True) + jnp.sum(w1, axis=1, keepdims=True)
    mixed = dot(w0.astype(BF16), kv0[1]) + dot(w1.astype(BF16), kv1[1])
    return mixed / total, peak * SCALE + jnp.log(total)


def prefix_send_body(qa, qb, kv0, kv1, out):
    lane = lanes()
    tile = jnp.zeros((GROUP, DH), F32)
    count = ROWS // GROUP
    for half, q in enumerate((qa, qb)):
        for i in range(256 // ROWS):
            rows = q[i * count : (i + 1) * count].reshape(ROWS, DH)
            mixed, mass = prefix_block(rows, kv0, kv1)
            at = half * 16 + i * count
            out[at : at + count] = mixed.reshape(count, GROUP, DH).astype(BF16)
            for n in range(count):
                tile = jnp.where(lane == at + n, mass[n * GROUP : (n + 1) * GROUP], tile)
    out[32] = split_tile(tile, 32)


def prefix_keep_body(qa, qb, kv0, kv1, out, masses):
    count = ROWS // GROUP
    for half, q in enumerate((qa, qb)):
        for i in range(256 // ROWS):
            rows = q[i * count : (i + 1) * count].reshape(ROWS, DH)
            mixed, mass = prefix_block(rows, kv0, kv1)
            at = half * 16 + i * count
            out[at : at + count] = mixed.reshape(count, GROUP, DH)
            masses[at : at + count] = jnp.broadcast_to(mass, (ROWS, DH)).reshape(count, GROUP, DH)


PREFIX_COST = pl.CostEstimate(
    flops=4 * 512 * 4096 * 128, bytes_accessed=2_500_000, transcendentals=512 * 4096
)


def prefix_send(qa, qb, kv0, kv1):
    return pl.pallas_call(
        prefix_send_body,
        out_shape=jax.ShapeDtypeStruct((33, GROUP, DH), BF16),
        in_specs=[VMEM] * 4,
        out_specs=VMEM,
        compiler_params=params(),
        cost_estimate=PREFIX_COST,
        name="prefix_send",
    )(qa, qb, kv0, kv1)


def prefix_keep(qa, qb, kv0, kv1):
    out = jax.ShapeDtypeStruct((32, GROUP, DH), F32)
    return pl.pallas_call(
        prefix_keep_body,
        out_shape=[out, out],
        in_specs=[VMEM] * 4,
        out_specs=[VMEM, VMEM],
        compiler_params=params(),
        cost_estimate=PREFIX_COST,
        name="prefix_keep",
    )(qa, qb, kv0, kv1)


def combine_body(place, mine, masses, message, s0, s1, s2, s3, far, out, held):
    x, y_high, z = place[2], place[3], place[4]
    theirs = join_tile(message[32], 32)
    near = [join_tile(s[8], 8) for s in (s0, s1, s2, s3)]
    across = [join_tile(far[5 * i + 4], 8) for i in range(4)]
    for g in range(2):
        for kx in range(4):
            for k in range(4):
                n = g * 16 + kx * 4 + k
                a, la = mine[n], masses[n]
                b = message[n].astype(F32)
                lb = jnp.broadcast_to(theirs[:, n : n + 1], (GROUP, DH))
                if g == 0:
                    s = (s0, s1, s2, s3)[kx][k].astype(F32)
                    ls = jnp.broadcast_to(near[kx][:, k : k + 1], (GROUP, DH))
                else:
                    s = far[5 * kx + k].astype(F32)
                    ls = jnp.broadcast_to(across[kx][:, 4 + k : 5 + k], (GROUP, DH))
                top = jnp.maximum(jnp.maximum(la, lb), ls)
                ea, eb, es = jnp.exp(la - top), jnp.exp(lb - top), jnp.exp(ls - top)
                row = (ea * a + eb * b + es * s) / (ea + eb + es)
                target = (x ^ kx) * 2 + (y_high ^ g)
                held[((target - z) & 7) * 4 + k] = row
    for h in range(GROUP):
        out[:, h * DH : (h + 1) * DH] = held[:, h, :].astype(BF16)


def combine(place, mine, masses, message, near, far):
    return pl.pallas_call(
        combine_body,
        out_shape=jax.ShapeDtypeStruct((32, GROUP * DH), BF16),
        in_specs=[SMEM] + [VMEM] * 8,
        out_specs=VMEM,
        scratch_shapes=[pltpu.VMEM((32, GROUP, DH), F32)],
        compiler_params=params(),
        name="combine",
    )(place, mine, masses, message, *near, far)


def project_body(*refs):
    blocks, weight, out, left, right = refs[:8], refs[8], refs[9], refs[10], refs[11]
    low = lax.broadcasted_iota(jnp.int32, (8, 512), 0) < 4
    for i, block in enumerate(blocks):
        total = dot(block[...], weight[...])
        for g in range(4):
            even, odd = [], []
            for j in (0, 2):
                first = total[j * 32 + g * 8 : j * 32 + g * 8 + 8]
                second = total[(j + 1) * 32 + g * 8 : (j + 1) * 32 + g * 8 + 8]
                even.append(jnp.where(low, first, pltpu.roll(second, 4, 0)))
                odd.append(jnp.where(low, pltpu.roll(first, 4, 0), second))
            even, odd = jnp.concatenate(even, axis=0), jnp.concatenate(odd, axis=0)
            out[2 * g, i * 16 : i * 16 + 16] = even
            out[2 * g + 1, i * 16 : i * 16 + 16] = odd
            if g == 2:
                left[i * 16 : i * 16 + 16] = even[:, :256].astype(BF16)
                right[i * 16 : i * 16 + 16] = even[:, 256:].astype(BF16)


def project(blocks, weight):
    half = jax.ShapeDtypeStruct((128, 256), BF16)
    return pl.pallas_call(
        project_body,
        out_shape=[jax.ShapeDtypeStruct((8, 128, 512), F32), half, half],
        in_specs=[VMEM] * 9,
        out_specs=[VMEM] * 3,
        compiler_params=params(),
        name="project",
    )(*blocks, weight)


def finish_body(place, own, left, right, orders, out):
    x, y, core, z = place[2], place[3] * 2 + place[5], place[6], place[4]
    lane = lanes()
    order = jnp.zeros((GROUP, DH), F32)
    for block in range(4):
        dy = (2 * (z & 1) + block // 2) ^ y
        tile = orders[((block % 2) ^ core) * 4 + dy].astype(F32)
        order = jnp.where(lane >> 5 == block, pltpu.roll(tile, 32 * block, 1), order)
    order = order.astype(jnp.int32)
    prompt, k = order >> 2, order & 3
    block = lane >> 5
    far = block & 1
    dx = (prompt >> 1) ^ x
    dy = (2 * (prompt & 1) + (block >> 1)) ^ y
    first = jnp.where(far == 0, dx, dy)
    second = jnp.where(far == 0, dy, dx)
    source = ((far ^ core) * 16 + second * 4 + first) * 4 + k
    row = lax.broadcasted_iota(jnp.int32, (128, 128), 0)
    pick = (row == source[0:1]).astype(F32).astype(BF16)
    total = own[...] + left[...].astype(F32) + right[...].astype(F32)
    out[...] = dot(pick, total.astype(BF16), (((0,), (0,)), ((), ()))).astype(BF16)


def finish(place, own, left, right, orders):
    return pl.pallas_call(
        finish_body,
        out_shape=jax.ShapeDtypeStruct((128, 512), BF16),
        in_specs=[SMEM] + [VMEM] * 4,
        out_specs=VMEM,
        compiler_params=params(),
        name="finish",
    )(place, own, left, right, orders)


def along(value, shift, k):
    return lax.ppermute(value, "batch", [(i, i ^ (k << shift)) for i in range(BATCH)])


def along_x(value, k):
    return along(value, 3, k)


def along_y(value, k):
    return along(value, 1, k)


def other_core(value):
    return along(value, 0, 1)


def turned(value, k, phase):
    pairs = [(i, i ^ (k << (3 if (i & 1) == phase else 1))) for i in range(BATCH)]
    return lax.ppermute(value, "batch", pairs)


def up(value):
    return lax.ppermute(value, "head", [(i, (i + 1) % HEADS) for i in range(HEADS)])


def down(value):
    return lax.ppermute(value, "head", [(i, (i - 1) % HEADS) for i in range(HEADS)])


def shards(queries, new_kv, prefix_kv, suffix_kv, page_table, suffix_len, prompt_of, out_weight):
    me = lax.axis_index("batch")
    z = lax.axis_index("head")
    x, y, core = me // 8, (me // 2) % 4, me % 2
    place = [8 * x + 4 * (y // 2), me * 256, x, y // 2, z, y % 2, core]
    place = jnp.stack(place).astype(jnp.int32)

    prefix_other = other_core(prefix_kv)

    q = queries.reshape(32, GROUP, DH)
    sent = sort_queries(place, prompt_of, q)
    by_x = [sent[0]] + [along_x(sent[k], k) for k in (1, 2, 3)]
    same, other = regroup(place, by_x)
    from1, from3, from2 = along_y(same, 1), along_y(other, 3), along_y(other, 2)
    orders = jnp.stack([same[16], from1[16], from2[16], from3[16]])
    orders = jnp.concatenate([orders, other_core(orders)], axis=0)

    suffix = suffix_parts(place, prompt_of, page_table, suffix_len, q, new_kv, suffix_kv)
    near = [suffix[0]] + [along_x(suffix[k], k) for k in (1, 2, 3)]
    far = along_y(jnp.concatenate([a[4:] for a in near], axis=0), 2)

    message = along_y(prefix_send(from1, from3, prefix_kv, prefix_other), 1)
    mine, masses = prefix_keep(same, from2, prefix_kv, prefix_other)
    attended = combine(place, mine, masses, message, near, far)

    parts = [attended] + [turned(attended, k, 0) for k in (1, 2, 3)]
    ring0 = jnp.concatenate(parts, axis=0)
    ring1, ring3 = turned(ring0, 1, 1), turned(ring0, 3, 1)
    ring2 = jnp.concatenate([turned(ring3[:64], 1, 1), turned(ring1[64:], 3, 1)], axis=0)
    mine_all = [ring0, ring1, ring2, ring3]
    blocks = mine_all + [other_core(a) for a in mine_all]

    partial, left, right = project(blocks, out_weight)
    from_up, from_down = down(left), up(right)
    low = jnp.concatenate([partial[5][:, :256] + from_up.astype(F32), partial[5][:, 256:]], axis=1)
    high = jnp.concatenate([partial[3][:, :256], partial[3][:, 256:] + from_down.astype(F32)], axis=1)
    from_up, from_down = down(low.astype(BF16)), up(high.astype(BF16))
    for step in (2, 1):
        low = partial[8 - step] + from_up.astype(F32)
        high = partial[step] + from_down.astype(F32)
        from_up, from_down = down(low.astype(BF16)), up(high.astype(BF16))

    return finish(place, partial[0], from_up, from_down, orders)


def solution(mesh):
    placed = (
        P("batch", "head"),
        P(None, "batch", "head"),
        P(None, "batch", "head"),
        P(None, "batch", None, "head"),
        P("batch", None),
        P("batch"),
        P("batch"),
        P("head", "batch"),
    )
    return jax.shard_map(
        shards, mesh=mesh, in_specs=placed, out_specs=P("head", "batch"), check_vma=False
    )
```

time: 513 us -> 113 us (0.22)
  the two profiles are of different devices: /device:TPU:1 before, /device:TPU:4 now
where the time goes in v1:
time: 113 us
  waiting for transfers between devices  46.2 us (41%)
  starting transfers between devices  38.7 us (34%)
  Pallas kernels  20 us (18%)
  local copies, waits for them, and re-layouts  7.35 us (7%)
    ppermute x7, waiting for transfers between devices, turned(): return lax.ppermute(value, 'batch', pairs)  19.5 us
    ppermute x17, starting transfers between devices, along(): lax.ppermute(value, 'batch', [(i, i ^ k << shift) for i in range(BATCH)])  18 us
    ppermute x4, waiting for transfers between devices, up(): lax.ppermute(value, 'head', [(i, (i + 1) % HEADS) for i in range(HEADS)])  13.2 us
    ppermute x4, starting transfers between devices, down(): lax.ppermute(value, 'head', [(i, (i - 1) % HEADS) for i in range(HEADS)])  10.3 us
    ppermute x7, starting transfers between devices, turned(): return lax.ppermute(value, 'batch', pairs)  8.18 us
    ppermute x17, waiting for transfers between devices, along(): lax.ppermute(value, 'batch', [(i, i ^ k << shift) for i in range(BATCH)])  7.01 us
    ppermute x4, waiting for transfers between devices, down(): lax.ppermute(value, 'head', [(i, (i - 1) % HEADS) for i in range(HEADS)])  6.45 us
    unnamed x17, local copies, waits for them, and re-layouts  5.98 us
  transfers between devices with their start and end apart: 32, of which 14 were waited for; matrix products, arithmetic and copies ran while one was open for 3% of the time, Pallas kernels for 11%

profile of v1, /device:TPU:4, one launch (start us, length us, event | category | flops | bytes accessed | tf_op | source)
XLA Modules:
  0.0 112.8 jit_solution(360402123243477174)
XLA Ops:
  0.0 0.9 copy.10
  1.0 0.1 stack.34.place
  1.0 0.7 copy-done.2
  1.7 0.7 sort_queries.1
  2.4 1.3 %collective-permute-start = (bf16[9,16,128]{2,1,0:T(8,128)(2,1)S(1)}, bf16[9,16,128]{2,1,0:T(8,128)(2,1)S(1)}, u32[]{:S(2)}, u32[]{:S(2)}) collective-permute-start(bf16[9,16,128]{2,1,0:T(8,128)(2,1)S(1)} %get-tuple-element.21), channel_id=1, source_target_pairs={{0,64},{8,72},{16,80},{24,88},{32,96},{40,104},{48,112},{56,120},{... | collective-permute-start | bytes 110600 | tf_op jit(solution)/shard_map/ppermute | solution.py:340
  3.7 1.1 %collective-permute-start.1 = (bf16[9,16,128]{2,1,0:T(8,128)(2,1)S(1)}, bf16[9,16,128]{2,1,0:T(8,128)(2,1)S(1)}, u32[]{:S(2)}, u32[]{:S(2)}) collective-permute-start(bf16[9,16,128]{2,1,0:T(8,128)(2,1)S(1)} %get-tuple-element.22), channel_id=1, source_target_pairs={{0,128},{8,136},{16,144},{24,152},{32,160},{40,168},{48,176},{56,1... | collective-permute-start | bytes 110600 | tf_op jit(solution)/shard_map/ppermute | solution.py:340
  4.8 1.1 %collective-permute-start.2 = (bf16[9,16,128]{2,1,0:T(8,128)(2,1)S(1)}, bf16[9,16,128]{2,1,0:T(8,128)(2,1)S(1)}, u32[]{:S(2)}, u32[]{:S(2)}) collective-permute-start(bf16[9,16,128]{2,1,0:T(8,128)(2,1)S(1)} %get-tuple-element.23), channel_id=1, source_target_pairs={{0,192},{8,200},{16,208},{24,216},{32,224},{40,232},{48,240},{56,2... | collective-permute-start | bytes 110600 | tf_op jit(solution)/shard_map/ppermute | solution.py:340
  6.0 0.8 copy.9.table
  6.8 1.6 %copy-done = bf16[2,256,16,128]{3,2,1,0:T(8,128)(2,1)S(1)} copy-done((bf16[2,256,16,128]{3,2,1,0:T(8,128)(2,1)S(1)}, bf16[2,256,16,128]{3,2,1,0:T(8,128)(2,1)}, u32[]{:S(2)}) %copy-start) | copy-done | bytes 2097176
  8.3 0.7 copy-done.1
  9.1 0.7 copy-done.3
  9.7 0.7 copy-done.4
  10.4 2.4 %suffix_parts.1 = (bf16[9,16,128]{2,1,0:T(8,128)(2,1)S(1)}, bf16[9,16,128]{2,1,0:T(8,128)(2,1)S(1)}, bf16[9,16,128]{2,1,0:T(8,128)(2,1)S(1)}, bf16[9,16,128]{2,1,0:T(8,128)(2,1)S(1)}) custom-call(s32[7]{0:T(128)S(1)} %stack.34.place, s32[32]{0:T(128)S(1)} %copy-done.3, s32[32,8]{1,0:T(8,128)S(1)} %copy.9.table, s32[32]{0:T(128)S(1)} %copy-done.4, ...), custom_call_target="tpu_custom_call" | custom-call | flops 40000000 | bytes 3000000 | tf_op jit(solution)/shard_map/suffix_parts/pallas_call | solution.py:146
  12.7 2.5 %collective-permute-start.8 = (bf16[9,16,128]{2,1,0:T(8,128)(2,1)S(1)}, bf16[9,16,128]{2,1,0:T(8,128)(2,1)S(1)}, u32[]{:S(2)}, u32[]{:S(2)}) collective-permute-start(bf16[9,16,128]{2,1,0:T(8,128)(2,1)S(1)} %get-tuple-element.29), channel_id=1, source_target_pairs={{0,64},{8,72},{16,80},{24,88},{32,96},{40,104},{48,112},{56,120},{... | collective-permute-start | bytes 110600 | tf_op jit(solution)/shard_map/ppermute | solution.py:340
  15.2 0.0 collective-permute-done.a1
  15.2 0.0 collective-permute-done.1.a2
  15.2 0.0 collective-permute-done.2.a3
  15.2 0.6 regroup.1
  15.8 3.1 %collective-permute-start.6 = (bf16[17,16,128]{2,1,0:T(8,128)(2,1)S(1)}, bf16[17,16,128]{2,1,0:T(8,128)(2,1)S(1)}, u32[]{:S(2)}, u32[]{:S(2)}) collective-permute-start(bf16[17,16,128]{2,1,0:T(8,128)(2,1)S(1)} %get-tuple-element.25), channel_id=1, source_target_pairs={{0,48},{8,56},{16,32},{24,40},{32,16},{40,24},{48,0},{56,8},{64,11... | collective-permute-start | bytes 208904 | tf_op jit(solution)/shard_map/ppermute | solution.py:340
  18.9 0.1 collective-permute-start.5
  19.1 0.0 collective-permute-start.9
  19.1 0.0 collective-permute-done.8.s1
  19.1 1.5 %collective-permute-start.10 = (bf16[9,16,128]{2,1,0:T(8,128)(2,1)S(1)}, bf16[9,16,128]{2,1,0:T(8,128)(2,1)S(1)}, u32[]{:S(2)}, u32[]{:S(2)}) collective-permute-start(bf16[9,16,128]{2,1,0:T(8,128)(2,1)S(1)} %get-tuple-element.31), channel_id=1, source_target_pairs={{0,192},{8,200},{16,208},{24,216},{32,224},{40,232},{48,240},{56,2... | collective-permute-start | bytes 110600 | tf_op jit(solution)/shard_map/ppermute | solution.py:340
  20.6 4.0 %collective-permute-done.9.s2 = bf16[9,16,128]{2,1,0:T(8,128)(2,1)S(1)} collective-permute-done((bf16[9,16,128]{2,1,0:T(8,128)(2,1)S(1)}, bf16[9,16,128]{2,1,0:T(8,128)(2,1)S(1)}, u32[]{:S(2)}, u32[]{:S(2)}) %collective-permute-start.9) | collective-permute-done | bytes 36896 | tf_op jit(solution)/shard_map/ppermute | solution.py:340
  24.5 1.5 %collective-permute-start.3 = (bf16[17,16,128]{2,1,0:T(8,128)(2,1)S(1)}, bf16[17,16,128]{2,1,0:T(8,128)(2,1)S(1)}, u32[]{:S(2)}, u32[]{:S(2)}) collective-permute-start(bf16[17,16,128]{2,1,0:T(8,128)(2,1)S(1)} %get-tuple-element.25), channel_id=1, source_target_pairs={{0,32},{8,40},{16,48},{24,56},{32,0},{40,8},{48,16},{56,24},{64,96... | collective-permute-start | bytes 208904 | tf_op jit(solution)/shard_map/ppermute | solution.py:340
  26.1 0.0 collective-permute-done.10.s3
  26.1 4.2 %prefix_send.1 = bf16[33,16,128]{2,1,0:T(8,128)(2,1)S(1)} custom-call(bf16[17,16,128]{2,1,0:T(8,128)(2,1)S(1)} %collective-permute-done.5.qa, bf16[17,16,128]{2,1,0:T(8,128)(2,1)S(1)} %collective-permute-done.6.qb, bf16[2,2048,128]{2,1,0:T(8,128)(2,1)S(1)} %copy-done.5, bf16[2,2048,128]{2,1,0:T(8,128)(2,1)S(1)} %collective-permute-done.4.kv1), custom_call_target="tpu_custom_call" | custom-call | flops 1073741824 | bytes 2500000 | tf_op jit(solution)/shard_map/prefix_send/pallas_call | solution.py:210
  30.3 0.4 collective-permute-start.7
  30.8 4.4 %collective-permute-start.11 = (bf16[20,16,128]{2,1,0:T(8,128)(2,1)S(1)}, bf16[20,16,128]{2,1,0:T(8,128)(2,1)S(1)}, u32[]{:S(2)}, u32[]{:S(2)}) collective-permute-start(bf16[20,16,128]{2,1,0:T(8,128)(2,1)S(1)} %pad_maximum_fusion.3), channel_id=1, source_target_pairs={{0,32},{8,40},{16,48},{24,56},{32,0},{40,8},{48,16},{56,24},{64,96... | collective-permute-start | bytes 245768 | tf_op jit(solution)/shard_map/ppermute | solution.py:340
  35.2 4.2 %prefix_keep.1 = (f32[32,16,128]{2,1,0:T(8,128)S(1)}, f32[32,16,128]{2,1,0:T(8,128)S(1)}) custom-call(bf16[17,16,128]{2,1,0:T(8,128)(2,1)S(1)} %get-tuple-element.24.qa, bf16[17,16,128]{2,1,0:T(8,128)(2,1)S(1)} %collective-permute-done.3.qb, bf16[2,2048,128]{2,1,0:T(8,128)(2,1)S(1)} %copy-done.5, bf16[2,2048,128]{2,1,0:T(8,128)(2,1)S(1)} %collective-permute-done.4.kv1), custom_call_target="tpu_custom_call" | custom-call | flops 1073741824 | bytes 2500000 | tf_op jit(solution)/shard_map/prefix_keep/pallas_call | solution.py:223
  39.4 1.2 %combine.1 = bf16[32,2048]{1,0:T(8,128)(2,1)S(1)} custom-call(s32[7]{0:T(128)S(1)} %stack.34.place, f32[32,16,128]{2,1,0:T(8,128)S(1)} %get-tuple-element.26.mine, f32[32,16,128]{2,1,0:T(8,128)S(1)} %get-tuple-element.27.masses, bf16[33,16,128]{2,1,0:T(8,128)(2,1)S(1)} %collective-permute-done.7.message, bf16[9,16,128]{2,1,0:T(8,128)(2,1)S(1)} %get-tuple-element.28.s0, ...), custom_call_target="tpu_custom_call" | custom-call | tf_op jit(solution)/shard_map/combine/pallas_call | solution.py:262
  40.6 0.1 collective-permute-start.14
  40.7 2.1 %collective-permute-start.13 = (bf16[32,2048]{1,0:T(8,128)(2,1)S(1)}, bf16[32,2048]{1,0:T(8,128)(2,1)S(1)}, u32[]{:S(2)}, u32[]{:S(2)}) collective-permute-start(bf16[32,2048]{1,0:T(8,128)(2,1)S(1)} %combine.1), channel_id=1, source_target_pairs={{0,128},{8,40},{16,144},{24,56},{32,160},{40,8},{48,176},{56,24},{... | collective-permute-start | bytes 393224 | tf_op jit(solution)/shard_map/ppermute | solution.py:357
  42.8 2.0 %collective-permute-start.12 = (bf16[32,2048]{1,0:T(8,128)(2,1)S(1)}, bf16[32,2048]{1,0:T(8,128)(2,1)S(1)}, u32[]{:S(2)}, u32[]{:S(2)}) collective-permute-start(bf16[32,2048]{1,0:T(8,128)(2,1)S(1)} %combine.1), channel_id=1, source_target_pairs={{0,64},{8,24},{16,80},{24,8},{32,96},{40,56},{48,112},{56,40},{64,... | collective-permute-start | bytes 393224 | tf_op jit(solution)/shard_map/ppermute | solution.py:357
  44.8 0.9 collective-permute-done.14
  45.7 1.6 %collective-permute-done.13 = bf16[32,2048]{1,0:T(8,128)(2,1)S(1)} collective-permute-done((bf16[32,2048]{1,0:T(8,128)(2,1)S(1)}, bf16[32,2048]{1,0:T(8,128)(2,1)S(1)}, u32[]{:S(2)}, u32[]{:S(2)}) %collective-permute-start.13) | collective-permute-done | bytes 131104 | tf_op jit(solution)/shard_map/ppermute | solution.py:357
  47.3 3.3 %collective-permute-done.12 = bf16[32,2048]{1,0:T(8,128)(2,1)S(1)} collective-permute-done((bf16[32,2048]{1,0:T(8,128)(2,1)S(1)}, bf16[32,2048]{1,0:T(8,128)(2,1)S(1)}, u32[]{:S(2)}, u32[]{:S(2)}) %collective-permute-start.12) | collective-permute-done | bytes 131104 | tf_op jit(solution)/shard_map/ppermute | solution.py:357
  50.6 0.1 collective-permute-start.16
  50.7 1.8 %collective-permute-start.15 = (bf16[128,2048]{1,0:T(8,128)(2,1)S(1)}, bf16[128,2048]{1,0:T(8,128)(2,1)S(1)}, u32[]{:S(2)}, u32[]{:S(2)}) collective-permute-start(bf16[128,2048]{1,0:T(8,128)(2,1)S(1)} %pad_maximum_fusion.refs_0_), channel_id=1, source_target_pairs={{0,16},{8,72},{16,0},{24,88},{32,48},{40,104},{48,32},{56,120},{64... | collective-permute-start | bytes 1572872 | tf_op jit(solution)/shard_map/ppermute | solution.py:357
  52.6 8.5 %collective-permute-done.16.refs_3_ = bf16[128,2048]{1,0:T(8,128)(2,1)S(1)} collective-permute-done((bf16[128,2048]{1,0:T(8,128)(2,1)S(1)}, bf16[128,2048]{1,0:T(8,128)(2,1)S(1)}, u32[]{:S(2)}, u32[]{:S(2)}) %collective-permute-start.16) | collective-permute-done | bytes 524320 | tf_op jit(solution)/shard_map/ppermute | solution.py:357
  61.1 0.1 collective-permute-start.17
  61.3 2.0 %collective-permute-start.18 = (bf16[64,2048]{1,0:T(8,128)(2,1)S(1)}, bf16[64,2048]{1,0:T(8,128)(2,1)S(1)}, u32[]{:S(2)}, u32[]{:S(2)}) collective-permute-start(bf16[64,2048]{1,0:T(8,128)(2,1)S(1)} %slice.92), channel_id=1, source_target_pairs={{0,48},{8,200},{16,32},{24,216},{32,16},{40,232},{48,0},{56,248},{... | collective-permute-start | bytes 786440 | tf_op jit(solution)/shard_map/ppermute | solution.py:357
  63.2 0.5 collective-permute-start.22
  63.7 3.8 %collective-permute-done.17 = bf16[64,2048]{1,0:T(8,128)(2,1)S(1)} collective-permute-done((bf16[64,2048]{1,0:T(8,128)(2,1)S(1)}, bf16[64,2048]{1,0:T(8,128)(2,1)S(1)}, u32[]{:S(2)}, u32[]{:S(2)}) %collective-permute-start.17) | collective-permute-done | bytes 262176 | tf_op jit(solution)/shard_map/ppermute | solution.py:357
  67.6 1.3 %collective-permute-done.18 = bf16[64,2048]{1,0:T(8,128)(2,1)S(1)} collective-permute-done((bf16[64,2048]{1,0:T(8,128)(2,1)S(1)}, bf16[64,2048]{1,0:T(8,128)(2,1)S(1)}, u32[]{:S(2)}, u32[]{:S(2)}) %collective-permute-start.18) | collective-permute-done | bytes 262176 | tf_op jit(solution)/shard_map/ppermute | solution.py:357
  68.9 0.3 collective-permute-start.21
  69.3 1.8 %collective-permute-done.21.refs_6_ = bf16[128,2048]{1,0:T(8,128)(2,1)S(1)} collective-permute-done((bf16[128,2048]{1,0:T(8,128)(2,1)S(1)}, bf16[128,2048]{1,0:T(8,128)(2,1)S(1)}, u32[]{:S(2)}, u32[]{:S(2)}) %collective-permute-start.21) | collective-permute-done | bytes 524320 | tf_op jit(solution)/shard_map/ppermute | solution.py:340
  71.2 5.3 %project.1 = (f32[8,128,512]{2,1,0:T(8,128)}, bf16[128,256]{1,0:T(8,128)(2,1)S(1)}, bf16[128,256]{1,0:T(8,128)(2,1)S(1)}) custom-call(bf16[128,2048]{1,0:T(8,128)(2,1)S(1)} %pad_maximum_fusion.refs_0_, bf16[128,2048]{1,0:T(8,128)(2,1)S(1)} %collective-permute-done.15.refs_1_, bf16[128,2048]{1,0:T(8,128)(2,1)S(1)} %constant_dynamic-update-slice_fusion.refs_2_, ...), custom_call_target="tpu_custom_call" | custom-call | tf_op jit(solution)/shard_map/project/pallas_call | solution.py:295
  76.4 5.9 %collective-permute-start.23 = (bf16[128,256]{1,0:T(8,128)(2,1)S(1)}, bf16[128,256]{1,0:T(8,128)(2,1)S(1)}, u32[]{:S(2)}, u32[]{:S(2)}) collective-permute-start(bf16[128,256]{1,0:T(8,128)(2,1)S(1)} %get-tuple-element.33), channel_id=1, source_target_pairs={{0,7},{1,0},{2,1},{3,2},{4,3},{5,4},{6,5},{7,6},{8,15},{9,8},{10,9... | collective-permute-start | bytes 196616 | tf_op jit(solution)/shard_map/ppermute | solution.py:365
  82.3 1.2 %slice_bitcast_fusion = (f32[128,512]{1,0:T(8,128)S(1)}, f32[128,512]{1,0:T(8,128)S(1)}, f32[128,512]{1,0:T(8,128)S(1)}) fusion(f32[8,128,512]{2,1,0:T(8,128)} %get-tuple-element.32), kind=kLoop, calls=%fused_computation.9 | loop fusion | bytes 1572864 | tf_op jit(solution)/shard_map/squeeze | solution.py:403
  83.5 4.3 %collective-permute-done.27 = bf16[128,256]{1,0:T(8,128)(2,1)S(1)} collective-permute-done((bf16[128,256]{1,0:T(8,128)(2,1)S(1)}, bf16[128,256]{1,0:T(8,128)(2,1)S(1)}, u32[]{:S(2)}, u32[]{:S(2)}) %collective-permute-start.27) | collective-permute-done | bytes 65568 | tf_op jit(solution)/shard_map/ppermute | solution.py:361
  87.8 0.1 collective-permute-start.28
  88.0 3.3 %collective-permute-start.24 = (bf16[128,512]{1,0:T(8,128)(2,1)S(1)}, bf16[128,512]{1,0:T(8,128)(2,1)S(1)}, u32[]{:S(2)}, u32[]{:S(2)}) collective-permute-start(bf16[128,512]{1,0:T(8,128)(2,1)S(1)} %pad_maximum_fusion.1), channel_id=1, source_target_pairs={{0,7},{1,0},{2,1},{3,2},{4,3},{5,4},{6,5},{7,6},{8,15},{9,8},{10,9... | collective-permute-start | bytes 393224 | tf_op jit(solution)/shard_map/ppermute | solution.py:365
  91.3 2.8 %collective-permute-done.28 = bf16[128,512]{1,0:T(8,128)(2,1)S(1)} collective-permute-done((bf16[128,512]{1,0:T(8,128)(2,1)S(1)}, bf16[128,512]{1,0:T(8,128)(2,1)S(1)}, u32[]{:S(2)}, u32[]{:S(2)}) %collective-permute-start.28) | collective-permute-done | bytes 131104 | tf_op jit(solution)/shard_map/ppermute | solution.py:361
  94.1 0.1 collective-permute-start.29
  94.2 6.1 %collective-permute-done.29 = bf16[128,512]{1,0:T(8,128)(2,1)S(1)} collective-permute-done((bf16[128,512]{1,0:T(8,128)(2,1)S(1)}, bf16[128,512]{1,0:T(8,128)(2,1)S(1)}, u32[]{:S(2)}, u32[]{:S(2)}) %collective-permute-start.29) | collective-permute-done | bytes 131104 | tf_op jit(solution)/shard_map/ppermute | solution.py:361
  100.4 0.1 fusion.1
  100.4 0.1 collective-permute-start.25
  100.6 2.0 %collective-permute-start.30 = (bf16[128,512]{1,0:T(8,128)(2,1)S(1)}, bf16[128,512]{1,0:T(8,128)(2,1)S(1)}, u32[]{:S(2)}, u32[]{:S(2)}) collective-permute-start(bf16[128,512]{1,0:T(8,128)(2,1)S(1)} %get-tuple-element.35), channel_id=1, source_target_pairs={{0,1},{1,2},{2,3},{3,4},{4,5},{5,6},{6,7},{7,0},{8,9},{9,10},{10,1... | collective-permute-start | bytes 393224 | tf_op jit(solution)/shard_map/ppermute | solution.py:361
  102.6 3.7 %collective-permute-done.25 = bf16[128,512]{1,0:T(8,128)(2,1)S(1)} collective-permute-done((bf16[128,512]{1,0:T(8,128)(2,1)S(1)}, bf16[128,512]{1,0:T(8,128)(2,1)S(1)}, u32[]{:S(2)}, u32[]{:S(2)}) %collective-permute-start.25) | collective-permute-done | bytes 131104 | tf_op jit(solution)/shard_map/ppermute | solution.py:365
  106.3 1.1 collective-permute-start.26
  107.4 1.2 %collective-permute-done.31 = bf16[4,16,128]{2,1,0:T(8,128)(2,1)S(1)} collective-permute-done((bf16[4,16,128]{2,1,0:T(8,128)(2,1)S(1)}, bf16[4,16,128]{2,1,0:T(8,128)(2,1)S(1)}, u32[]{:S(2)}, u32[]{:S(2)}) %collective-permute-start.31) | collective-permute-done | bytes 16416 | tf_op jit(solution)/shard_map/ppermute | solution.py:340
  108.6 2.7 %collective-permute-done.26.left = bf16[128,512]{1,0:T(8,128)(2,1)S(1)} collective-permute-done((bf16[128,512]{1,0:T(8,128)(2,1)S(1)}, bf16[128,512]{1,0:T(8,128)(2,1)S(1)}, u32[]{:S(2)}, u32[]{:S(2)}) %collective-permute-start.26) | collective-permute-done | bytes 131104 | tf_op jit(solution)/shard_map/ppermute | solution.py:365
  111.3 1.5 %finish.1 = bf16[128,512]{1,0:T(8,128)(2,1)} custom-call(s32[7]{0:T(128)S(1)} %stack.34.place, f32[128,512]{1,0:T(8,128)S(1)} %get-tuple-element.39.own, bf16[128,512]{1,0:T(8,128)(2,1)S(1)} %collective-permute-done.26.left, bf16[128,512]{1,0:T(8,128)(2,1)S(1)} %collective-permute-done.30.right, ...), custom_call_target="tpu_custom_call" | custom-call | tf_op jit(solution)/shard_map/finish/pallas_call | solution.py:329
  (51 shorter events, 0.4 us)
Async XLA Ops:
  0.0 26.1 %collective-permute-start.4 = (bf16[2,2048,128]{2,1,0:T(8,128)(2,1)}, bf16[2,2048,128]{2,1,0:T(8,128)(2,1)S(1)}, u32[]{:S(2)}, u32[]{:S(2)}) collective-permute-start(bf16[2,2048,128]{2,1,0:T(8,128)(2,1)} %kv0.3), channel_id=1, source_target_pairs={{0,8},{8,0},{16,24},{24,16},{32,40},{40,32},{48,56},{56,48},{64,72... | collective-permute-start | bytes 3145736 | tf_op jit(solution)/shard_map/ppermute | solution.py:340
  1.0 0.7 copy-start.2
  2.4 12.8 %collective-permute-start = (bf16[9,16,128]{2,1,0:T(8,128)(2,1)S(1)}, bf16[9,16,128]{2,1,0:T(8,128)(2,1)S(1)}, u32[]{:S(2)}, u32[]{:S(2)}) collective-permute-start(bf16[9,16,128]{2,1,0:T(8,128)(2,1)S(1)} %get-tuple-element.21), channel_id=1, source_target_pairs={{0,64},{8,72},{16,80},{24,88},{32,96},{40,104},{48,112},{56,120},{... | collective-permute-start | bytes 110600 | tf_op jit(solution)/shard_map/ppermute | solution.py:340
  3.7 11.5 %collective-permute-start.1 = (bf16[9,16,128]{2,1,0:T(8,128)(2,1)S(1)}, bf16[9,16,128]{2,1,0:T(8,128)(2,1)S(1)}, u32[]{:S(2)}, u32[]{:S(2)}) collective-permute-start(bf16[9,16,128]{2,1,0:T(8,128)(2,1)S(1)} %get-tuple-element.22), channel_id=1, source_target_pairs={{0,128},{8,136},{16,144},{24,152},{32,160},{40,168},{48,176},{56,1... | collective-permute-start | bytes 110600 | tf_op jit(solution)/shard_map/ppermute | solution.py:340
  4.8 10.4 %collective-permute-start.2 = (bf16[9,16,128]{2,1,0:T(8,128)(2,1)S(1)}, bf16[9,16,128]{2,1,0:T(8,128)(2,1)S(1)}, u32[]{:S(2)}, u32[]{:S(2)}) collective-permute-start(bf16[9,16,128]{2,1,0:T(8,128)(2,1)S(1)} %get-tuple-element.23), channel_id=1, source_target_pairs={{0,192},{8,200},{16,208},{24,216},{32,224},{40,232},{48,240},{56,2... | collective-permute-start | bytes 110600 | tf_op jit(solution)/shard_map/ppermute | solution.py:340
  6.8 1.6 %copy-start = (bf16[2,256,16,128]{3,2,1,0:T(8,128)(2,1)S(1)}, bf16[2,256,16,128]{3,2,1,0:T(8,128)(2,1)}, u32[]{:S(2)}) copy-start(bf16[2,256,16,128]{3,2,1,0:T(8,128)(2,1)} %pool.1) | copy-start | bytes 6291460
  8.3 0.7 copy-start.1
  9.1 0.7 copy-start.3
  9.7 0.7 copy-start.4
  10.4 15.8 %copy-start.5 = (bf16[2,2048,128]{2,1,0:T(8,128)(2,1)S(1)}, bf16[2,2048,128]{2,1,0:T(8,128)(2,1)}, u32[]{:S(2)}) copy-start(bf16[2,2048,128]{2,1,0:T(8,128)(2,1)} %kv0.3) | copy-start | bytes 3145732
  12.7 6.3 %collective-permute-start.8 = (bf16[9,16,128]{2,1,0:T(8,128)(2,1)S(1)}, bf16[9,16,128]{2,1,0:T(8,128)(2,1)S(1)}, u32[]{:S(2)}, u32[]{:S(2)}) collective-permute-start(bf16[9,16,128]{2,1,0:T(8,128)(2,1)S(1)} %get-tuple-element.29), channel_id=1, source_target_pairs={{0,64},{8,72},{16,80},{24,88},{32,96},{40,104},{48,112},{56,120},{... | collective-permute-start | bytes 110600 | tf_op jit(solution)/shard_map/ppermute | solution.py:340
  15.8 10.3 %collective-permute-start.6 = (bf16[17,16,128]{2,1,0:T(8,128)(2,1)S(1)}, bf16[17,16,128]{2,1,0:T(8,128)(2,1)S(1)}, u32[]{:S(2)}, u32[]{:S(2)}) collective-permute-start(bf16[17,16,128]{2,1,0:T(8,128)(2,1)S(1)} %get-tuple-element.25), channel_id=1, source_target_pairs={{0,48},{8,56},{16,32},{24,40},{32,16},{40,24},{48,0},{56,8},{64,11... | collective-permute-start | bytes 208904 | tf_op jit(solution)/shard_map/ppermute | solution.py:340
  18.9 7.2 %collective-permute-start.5 = (bf16[17,16,128]{2,1,0:T(8,128)(2,1)S(1)}, bf16[17,16,128]{2,1,0:T(8,128)(2,1)S(1)}, u32[]{:S(2)}, u32[]{:S(2)}) collective-permute-start(bf16[17,16,128]{2,1,0:T(8,128)(2,1)S(1)} %get-tuple-element.24.qa), channel_id=1, source_target_pairs={{0,16},{8,24},{16,0},{24,8},{32,48},{40,56},{48,32},{56,40},{64,80... | collective-permute-start | bytes 208904 | tf_op jit(solution)/shard_map/ppermute | solution.py:340
  19.1 5.5 %collective-permute-start.9 = (bf16[9,16,128]{2,1,0:T(8,128)(2,1)S(1)}, bf16[9,16,128]{2,1,0:T(8,128)(2,1)S(1)}, u32[]{:S(2)}, u32[]{:S(2)}) collective-permute-start(bf16[9,16,128]{2,1,0:T(8,128)(2,1)S(1)} %get-tuple-element.30), channel_id=1, source_target_pairs={{0,128},{8,136},{16,144},{24,152},{32,160},{40,168},{48,176},{56,1... | collective-permute-start | bytes 110600 | tf_op jit(solution)/shard_map/ppermute | solution.py:340
  19.1 7.0 %collective-permute-start.10 = (bf16[9,16,128]{2,1,0:T(8,128)(2,1)S(1)}, bf16[9,16,128]{2,1,0:T(8,128)(2,1)S(1)}, u32[]{:S(2)}, u32[]{:S(2)}) collective-permute-start(bf16[9,16,128]{2,1,0:T(8,128)(2,1)S(1)} %get-tuple-element.31), channel_id=1, source_target_pairs={{0,192},{8,200},{16,208},{24,216},{32,224},{40,232},{48,240},{56,2... | collective-permute-start | bytes 110600 | tf_op jit(solution)/shard_map/ppermute | solution.py:340
  24.5 10.7 %collective-permute-start.3 = (bf16[17,16,128]{2,1,0:T(8,128)(2,1)S(1)}, bf16[17,16,128]{2,1,0:T(8,128)(2,1)S(1)}, u32[]{:S(2)}, u32[]{:S(2)}) collective-permute-start(bf16[17,16,128]{2,1,0:T(8,128)(2,1)S(1)} %get-tuple-element.25), channel_id=1, source_target_pairs={{0,32},{8,40},{16,48},{24,56},{32,0},{40,8},{48,16},{56,24},{64,96... | collective-permute-start | bytes 208904 | tf_op jit(solution)/shard_map/ppermute | solution.py:340
  30.3 9.1 %collective-permute-start.7 = (bf16[33,16,128]{2,1,0:T(8,128)(2,1)S(1)}, bf16[33,16,128]{2,1,0:T(8,128)(2,1)S(1)}, u32[]{:S(2)}, u32[]{:S(2)}) collective-permute-start(bf16[33,16,128]{2,1,0:T(8,128)(2,1)S(1)} %prefix_send.1), channel_id=1, source_target_pairs={{0,16},{8,24},{16,0},{24,8},{32,48},{40,56},{48,32},{56,40},{64,80... | collective-permute-start | bytes 405512 | tf_op jit(solution)/shard_map/ppermute | solution.py:340
  30.8 8.6 %collective-permute-start.11 = (bf16[20,16,128]{2,1,0:T(8,128)(2,1)S(1)}, bf16[20,16,128]{2,1,0:T(8,128)(2,1)S(1)}, u32[]{:S(2)}, u32[]{:S(2)}) collective-permute-start(bf16[20,16,128]{2,1,0:T(8,128)(2,1)S(1)} %pad_maximum_fusion.3), channel_id=1, source_target_pairs={{0,32},{8,40},{16,48},{24,56},{32,0},{40,8},{48,16},{56,24},{64,96... | collective-permute-start | bytes 245768 | tf_op jit(solution)/shard_map/ppermute | solution.py:340
  40.6 5.1 %collective-permute-start.14 = (bf16[32,2048]{1,0:T(8,128)(2,1)S(1)}, bf16[32,2048]{1,0:T(8,128)(2,1)S(1)}, u32[]{:S(2)}, u32[]{:S(2)}) collective-permute-start(bf16[32,2048]{1,0:T(8,128)(2,1)S(1)} %combine.1), channel_id=1, source_target_pairs={{0,192},{8,56},{16,208},{24,40},{32,224},{40,24},{48,240},{56,8},{... | collective-permute-start | bytes 393224 | tf_op jit(solution)/shard_map/ppermute | solution.py:357
  40.7 6.6 %collective-permute-start.13 = (bf16[32,2048]{1,0:T(8,128)(2,1)S(1)}, bf16[32,2048]{1,0:T(8,128)(2,1)S(1)}, u32[]{:S(2)}, u32[]{:S(2)}) collective-permute-start(bf16[32,2048]{1,0:T(8,128)(2,1)S(1)} %combine.1), channel_id=1, source_target_pairs={{0,128},{8,40},{16,144},{24,56},{32,160},{40,8},{48,176},{56,24},{... | collective-permute-start | bytes 393224 | tf_op jit(solution)/shard_map/ppermute | solution.py:357
  42.8 7.8 %collective-permute-start.12 = (bf16[32,2048]{1,0:T(8,128)(2,1)S(1)}, bf16[32,2048]{1,0:T(8,128)(2,1)S(1)}, u32[]{:S(2)}, u32[]{:S(2)}) collective-permute-start(bf16[32,2048]{1,0:T(8,128)(2,1)S(1)} %combine.1), channel_id=1, source_target_pairs={{0,64},{8,24},{16,80},{24,8},{32,96},{40,56},{48,112},{56,40},{64,... | collective-permute-start | bytes 393224 | tf_op jit(solution)/shard_map/ppermute | solution.py:357
  50.6 10.5 %collective-permute-start.16 = (bf16[128,2048]{1,0:T(8,128)(2,1)S(1)}, bf16[128,2048]{1,0:T(8,128)(2,1)S(1)}, u32[]{:S(2)}, u32[]{:S(2)}) collective-permute-start(bf16[128,2048]{1,0:T(8,128)(2,1)S(1)} %pad_maximum_fusion.refs_0_), channel_id=1, source_target_pairs={{0,48},{8,200},{16,32},{24,216},{32,16},{40,232},{48,0},{56,248},{... | collective-permute-start | bytes 1572872 | tf_op jit(solution)/shard_map/ppermute | solution.py:357
  50.7 10.5 %collective-permute-start.15 = (bf16[128,2048]{1,0:T(8,128)(2,1)S(1)}, bf16[128,2048]{1,0:T(8,128)(2,1)S(1)}, u32[]{:S(2)}, u32[]{:S(2)}) collective-permute-start(bf16[128,2048]{1,0:T(8,128)(2,1)S(1)} %pad_maximum_fusion.refs_0_), channel_id=1, source_target_pairs={{0,16},{8,72},{16,0},{24,88},{32,48},{40,104},{48,32},{56,120},{64... | collective-permute-start | bytes 1572872 | tf_op jit(solution)/shard_map/ppermute | solution.py:357
  61.1 6.5 %collective-permute-start.17 = (bf16[64,2048]{1,0:T(8,128)(2,1)S(1)}, bf16[64,2048]{1,0:T(8,128)(2,1)S(1)}, u32[]{:S(2)}, u32[]{:S(2)}) collective-permute-start(bf16[64,2048]{1,0:T(8,128)(2,1)S(1)} %slice.91), channel_id=1, source_target_pairs={{0,16},{8,72},{16,0},{24,88},{32,48},{40,104},{48,32},{56,120},{64... | collective-permute-start | bytes 786440 | tf_op jit(solution)/shard_map/ppermute | solution.py:357
  61.3 7.7 %collective-permute-start.18 = (bf16[64,2048]{1,0:T(8,128)(2,1)S(1)}, bf16[64,2048]{1,0:T(8,128)(2,1)S(1)}, u32[]{:S(2)}, u32[]{:S(2)}) collective-permute-start(bf16[64,2048]{1,0:T(8,128)(2,1)S(1)} %slice.92), channel_id=1, source_target_pairs={{0,48},{8,200},{16,32},{24,216},{32,16},{40,232},{48,0},{56,248},{... | collective-permute-start | bytes 786440 | tf_op jit(solution)/shard_map/ppermute | solution.py:357
  63.2 6.1 %collective-permute-start.19 = (bf16[128,2048]{1,0:T(8,128)(2,1)S(1)}, bf16[128,2048]{1,0:T(8,128)(2,1)S(1)}, u32[]{:S(2)}, u32[]{:S(2)}) collective-permute-start(bf16[128,2048]{1,0:T(8,128)(2,1)S(1)} %pad_maximum_fusion.refs_0_), channel_id=1, source_target_pairs={{0,8},{8,0},{16,24},{24,16},{32,40},{40,32},{48,56},{56,48},{64,72... | collective-permute-start | bytes 1572872 | tf_op jit(solution)/shard_map/ppermute | solution.py:340
  63.2 6.1 %collective-permute-start.22 = (bf16[128,2048]{1,0:T(8,128)(2,1)S(1)}, bf16[128,2048]{1,0:T(8,128)(2,1)S(1)}, u32[]{:S(2)}, u32[]{:S(2)}) collective-permute-start(bf16[128,2048]{1,0:T(8,128)(2,1)S(1)} %collective-permute-done.16.refs_3_), channel_id=1, source_target_pairs={{0,8},{8,0},{16,24},{24,16},{32,40},{40,32},{48,56},{56,48},{64,72... | collective-permute-start | bytes 1572872 | tf_op jit(solution)/shard_map/ppermute | solution.py:340
  63.7 5.6 %collective-permute-start.20 = (bf16[128,2048]{1,0:T(8,128)(2,1)S(1)}, bf16[128,2048]{1,0:T(8,128)(2,1)S(1)}, u32[]{:S(2)}, u32[]{:S(2)}) collective-permute-start(bf16[128,2048]{1,0:T(8,128)(2,1)S(1)} %collective-permute-done.15.refs_1_), channel_id=1, source_target_pairs={{0,8},{8,0},{16,24},{24,16},{32,40},{40,32},{48,56},{56,48},{64,72... | collective-permute-start | bytes 1572872 | tf_op jit(solution)/shard_map/ppermute | solution.py:340
  68.9 2.2 %collective-permute-start.21 = (bf16[128,2048]{1,0:T(8,128)(2,1)S(1)}, bf16[128,2048]{1,0:T(8,128)(2,1)S(1)}, u32[]{:S(2)}, u32[]{:S(2)}) collective-permute-start(bf16[128,2048]{1,0:T(8,128)(2,1)S(1)} %constant_dynamic-update-slice_fusion.refs_2_), channel_id=1, source_target_pairs={{0,8},{8,0},{16,24},{24,16},{32,40},{40,32},{48,56},{56,48},{64,72... | collective-permute-start | bytes 1572872 | tf_op jit(solution)/shard_map/ppermute | solution.py:340
  76.4 17.6 %copy-start.6 = (f32[8,128,512]{2,1,0:T(8,128)S(1)}, f32[8,128,512]{2,1,0:T(8,128)}, u32[]{:S(2)}) copy-start(f32[8,128,512]{2,1,0:T(8,128)} %get-tuple-element.32) | copy-start | bytes 6291460
  76.4 11.5 %collective-permute-start.23 = (bf16[128,256]{1,0:T(8,128)(2,1)S(1)}, bf16[128,256]{1,0:T(8,128)(2,1)S(1)}, u32[]{:S(2)}, u32[]{:S(2)}) collective-permute-start(bf16[128,256]{1,0:T(8,128)(2,1)S(1)} %get-tuple-element.33), channel_id=1, source_target_pairs={{0,7},{1,0},{2,1},{3,2},{4,3},{5,4},{6,5},{7,6},{8,15},{9,8},{10,9... | collective-permute-start | bytes 196616 | tf_op jit(solution)/shard_map/ppermute | solution.py:365
  82.3 5.5 %collective-permute-start.27 = (bf16[128,256]{1,0:T(8,128)(2,1)S(1)}, bf16[128,256]{1,0:T(8,128)(2,1)S(1)}, u32[]{:S(2)}, u32[]{:S(2)}) collective-permute-start(bf16[128,256]{1,0:T(8,128)(2,1)S(1)} %get-tuple-element.34), channel_id=1, source_target_pairs={{0,1},{1,2},{2,3},{3,4},{4,5},{5,6},{6,7},{7,0},{8,9},{9,10},{10,1... | collective-permute-start | bytes 196616 | tf_op jit(solution)/shard_map/ppermute | solution.py:361
  87.8 6.3 %collective-permute-start.28 = (bf16[128,512]{1,0:T(8,128)(2,1)S(1)}, bf16[128,512]{1,0:T(8,128)(2,1)S(1)}, u32[]{:S(2)}, u32[]{:S(2)}) collective-permute-start(bf16[128,512]{1,0:T(8,128)(2,1)S(1)} %pad_maximum_fusion.2), channel_id=1, source_target_pairs={{0,1},{1,2},{2,3},{3,4},{4,5},{5,6},{6,7},{7,0},{8,9},{9,10},{10,1... | collective-permute-start | bytes 393224 | tf_op jit(solution)/shard_map/ppermute | solution.py:361
  88.0 6.3 %collective-permute-start.24 = (bf16[128,512]{1,0:T(8,128)(2,1)S(1)}, bf16[128,512]{1,0:T(8,128)(2,1)S(1)}, u32[]{:S(2)}, u32[]{:S(2)}) collective-permute-start(bf16[128,512]{1,0:T(8,128)(2,1)S(1)} %pad_maximum_fusion.1), channel_id=1, source_target_pairs={{0,7},{1,0},{2,1},{3,2},{4,3},{5,4},{6,5},{7,6},{8,15},{9,8},{10,9... | collective-permute-start | bytes 393224 | tf_op jit(solution)/shard_map/ppermute | solution.py:365
  94.1 6.3 %collective-permute-start.29 = (bf16[128,512]{1,0:T(8,128)(2,1)S(1)}, bf16[128,512]{1,0:T(8,128)(2,1)S(1)}, u32[]{:S(2)}, u32[]{:S(2)}) collective-permute-start(bf16[128,512]{1,0:T(8,128)(2,1)S(1)} %fusion), channel_id=1, source_target_pairs={{0,1},{1,2},{2,3},{3,4},{4,5},{5,6},{6,7},{7,0},{8,9},{9,10},{10,1... | collective-permute-start | bytes 393224 | tf_op jit(solution)/shard_map/ppermute | solution.py:361
  100.4 5.8 %collective-permute-start.25 = (bf16[128,512]{1,0:T(8,128)(2,1)S(1)}, bf16[128,512]{1,0:T(8,128)(2,1)S(1)}, u32[]{:S(2)}, u32[]{:S(2)}) collective-permute-start(bf16[128,512]{1,0:T(8,128)(2,1)S(1)} %get-tuple-element.36), channel_id=1, source_target_pairs={{0,7},{1,0},{2,1},{3,2},{4,3},{5,4},{6,5},{7,6},{8,15},{9,8},{10,9... | collective-permute-start | bytes 393224 | tf_op jit(solution)/shard_map/ppermute | solution.py:365
  100.6 8.0 %collective-permute-start.30 = (bf16[128,512]{1,0:T(8,128)(2,1)S(1)}, bf16[128,512]{1,0:T(8,128)(2,1)S(1)}, u32[]{:S(2)}, u32[]{:S(2)}) collective-permute-start(bf16[128,512]{1,0:T(8,128)(2,1)S(1)} %get-tuple-element.35), channel_id=1, source_target_pairs={{0,1},{1,2},{2,3},{3,4},{4,5},{5,6},{6,7},{7,0},{8,9},{9,10},{10,1... | collective-permute-start | bytes 393224 | tf_op jit(solution)/shard_map/ppermute | solution.py:361
  106.3 5.0 %collective-permute-start.26 = (bf16[128,512]{1,0:T(8,128)(2,1)S(1)}, bf16[128,512]{1,0:T(8,128)(2,1)S(1)}, u32[]{:S(2)}, u32[]{:S(2)}) collective-permute-start(bf16[128,512]{1,0:T(8,128)(2,1)S(1)} %fusion.3), channel_id=1, source_target_pairs={{0,7},{1,0},{2,1},{3,2},{4,3},{5,4},{6,5},{7,6},{8,15},{9,8},{10,9... | collective-permute-start | bytes 393224 | tf_op jit(solution)/shard_map/ppermute | solution.py:365
  107.4 1.2 %collective-permute-start.31 = (bf16[4,16,128]{2,1,0:T(8,128)(2,1)S(1)}, bf16[4,16,128]{2,1,0:T(8,128)(2,1)S(1)}, u32[]{:S(2)}, u32[]{:S(2)}) collective-permute-start(bf16[4,16,128]{2,1,0:T(8,128)(2,1)S(1)} %pad_maximum_fusion.4), channel_id=1, source_target_pairs={{0,8},{8,0},{16,24},{24,16},{32,40},{40,32},{48,56},{56,48},{64,72... | collective-permute-start | bytes 49160 | tf_op jit(solution)/shard_map/ppermute | solution.py:340

commit v2 on v1

--- a/solution.py
+++ b/solution.py
@@ -19,8 +19,11 @@
 NN = (((1,), (0,)), ((), ()))
 
 
-def params():
-    return pltpu.CompilerParams(vmem_limit_bytes=48 * 1024 * 1024)
+ANY = pl.BlockSpec(memory_space=pl.ANY)
+
+
+def params(mib=16):
+    return pltpu.CompilerParams(vmem_limit_bytes=mib * 1024 * 1024)
 
 
 def dot(a, b, dims=NN):
@@ -45,16 +48,28 @@
     return (wide + pltpu.roll(wide, DH - step, 1)) + pltpu.roll(wide, DH - 2 * step, 1)
 
 
-def sort_body(place, prompt, q, o0, o1, o2, o3, held, seen):
+def sort_body(place, prompt_in, q_in, o0, o1, o2, o3, q_out, prompt, q, wide, held, seen, sems):
+    copies = [
+        pltpu.make_async_copy(prompt_in, prompt, sems.at[0]),
+        pltpu.make_async_copy(q_in, q, sems.at[1]),
+    ]
+    for copy in copies:
+        copy.start()
+    for copy in copies:
+        copy.wait()
     lane = lanes()
     tile = jnp.zeros((GROUP, DH), F32)
     for p in range(8):
         seen[p] = 0
+    for h in range(GROUP):
+        wide[:, h, :] = q[:, h * DH : (h + 1) * DH].astype(F32)
     for r in range(32):
         p = prompt[r]
         k = seen[p]
         seen[p] = k + 1
-        held[(4 * p + k) ^ place[0]] = q[r]
+        row = wide[r].astype(BF16)
+        q_out[r] = row
+        held[(4 * p + k) ^ place[0]] = row
         tile = jnp.where(lane == r, (4 * p + k).astype(F32), tile)
     for i, out in enumerate((o0, o1, o2, o3)):
         out[0:8] = held[8 * i : 8 * i + 8]
@@ -65,10 +80,17 @@
     out = jax.ShapeDtypeStruct((9, GROUP, DH), BF16)
     return pl.pallas_call(
         sort_body,
-        out_shape=[out] * 4,
-        in_specs=[SMEM, SMEM, VMEM],
-        out_specs=[VMEM] * 4,
-        scratch_shapes=[pltpu.VMEM((32, GROUP, DH), BF16), pltpu.SMEM((8,), jnp.int32)],
+        out_shape=[out] * 4 + [jax.ShapeDtypeStruct((32, GROUP, DH), BF16)],
+        in_specs=[SMEM, ANY, ANY],
+        out_specs=[VMEM] * 5,
+        scratch_shapes=[
+            pltpu.SMEM((32,), jnp.int32),
+            pltpu.VMEM((32, GROUP * DH), BF16),
+            pltpu.VMEM((32, GROUP, DH), F32),
+            pltpu.VMEM((32, GROUP, DH), BF16),
+            pltpu.SMEM((8,), jnp.int32),
+            pltpu.SemaphoreType.DMA((2,)),
+        ],
         compiler_params=params(),
         name="sort_queries",
     )(place, prompt, q)
@@ -99,7 +121,23 @@
     )(place, *parts)
 
 
-def suffix_body(place, prompt, table, length, q, new, pool, o0, o1, o2, o3, scores, weights, held, tiles, seen):
+def suffix_body(
+    place, prompt_in, table_in, length_in, q, new_in, pool_in, o0, o1, o2, o3,
+    prompt, table, length, new, pool, scores, weights, held, tiles, seen, sems,
+):
+    pairs = [
+        (pool_in.at[0], pool.at[0]),
+        (table_in, table),
+        (length_in, length),
+        (new_in, new),
+        (prompt_in, prompt),
+        (pool_in.at[1], pool.at[1]),
+    ]
+    copies = [pltpu.make_async_copy(a, b, sems.at[i]) for i, (a, b) in enumerate(pairs)]
+    for copy in copies:
+        copy.start()
+    for copy in copies[:5]:
+        copy.wait()
     lane = lanes()
     base = place[1]
     for n in range(32):
@@ -124,6 +162,7 @@
     mass = peak + jnp.log(total)
     inverse = 1.0 / total
     tiles[...] = jnp.zeros_like(tiles)
+    copies[5].wait()
     for p in range(8):
         seen[p] = 0
     for n in range(32):
@@ -146,14 +185,20 @@
     return pl.pallas_call(
         suffix_body,
         out_shape=[out] * 4,
-        in_specs=[SMEM, SMEM, SMEM, SMEM, VMEM, VMEM, VMEM],
+        in_specs=[SMEM, ANY, ANY, ANY, VMEM, ANY, ANY],
         out_specs=[VMEM] * 4,
         scratch_shapes=[
+            pltpu.SMEM((32,), jnp.int32),
+            pltpu.SMEM((32, 8), jnp.int32),
+            pltpu.SMEM((32,), jnp.int32),
+            pltpu.VMEM((2, 32, DH), BF16),
+            pltpu.VMEM((2, 256, GROUP, DH), BF16),
             pltpu.VMEM((32, GROUP, DH), F32),
             pltpu.VMEM((32, GROUP, DH), BF16),
             pltpu.VMEM((32, GROUP, DH), BF16),
             pltpu.VMEM((4, GROUP, DH), F32),
             pltpu.SMEM((8,), jnp.int32),
+            pltpu.SemaphoreType.DMA((6,)),
         ],
         compiler_params=params(),
         cost_estimate=pl.CostEstimate(flops=40_000_000, bytes_accessed=3_000_000, transcendentals=70000),
@@ -164,15 +209,20 @@
 ROWS = 128
 
 
+def prefix_part(q, kv):
+    s = dot(q, kv[0], NT)
+    peak = jnp.max(s, axis=1, keepdims=True)
+    w = jnp.exp2((s - peak) * (SCALE * LOG2E))
+    return dot(w.astype(BF16), kv[1]), peak * SCALE, jnp.sum(w, axis=1, keepdims=True)
+
+
 def prefix_block(q, kv0, kv1):
-    s0 = dot(q, kv0[0], NT)
-    s1 = dot(q, kv1[0], NT)
-    peak = jnp.maximum(jnp.max(s0, axis=1, keepdims=True), jnp.max(s1, axis=1, keepdims=True))
-    w0 = jnp.exp2((s0 - peak) * (SCALE * LOG2E))
-    w1 = jnp.exp2((s1 - peak) * (SCALE * LOG2E))
-    total = jnp.sum(w0, axis=1, keepdims=True) + jnp.sum(w1, axis=1, keepdims=True)
-    mixed = dot(w0.astype(BF16), kv0[1]) + dot(w1.astype(BF16), kv1[1])
-    return mixed / total, peak * SCALE + jnp.log(total)
+    mixed0, peak0, total0 = prefix_part(q, kv0)
+    mixed1, peak1, total1 = prefix_part(q, kv1)
+    top = jnp.maximum(peak0, peak1)
+    f0, f1 = jnp.exp(peak0 - top), jnp.exp(peak1 - top)
+    total = total0 * f0 + total1 * f1
+    return (mixed0 * f0 + mixed1 * f1) * (1.0 / total), top + jnp.log(total)
 
 
 def prefix_send_body(qa, qb, kv0, kv1, out):
@@ -212,7 +262,7 @@
         out_shape=jax.ShapeDtypeStruct((33, GROUP, DH), BF16),
         in_specs=[VMEM] * 4,
         out_specs=VMEM,
-        compiler_params=params(),
+        compiler_params=params(24),
         cost_estimate=PREFIX_COST,
         name="prefix_send",
     )(qa, qb, kv0, kv1)
@@ -225,7 +275,7 @@
         out_shape=[out, out],
         in_specs=[VMEM] * 4,
         out_specs=[VMEM, VMEM],
-        compiler_params=params(),
+        compiler_params=params(24),
         cost_estimate=PREFIX_COST,
         name="prefix_keep",
     )(qa, qb, kv0, kv1)
@@ -270,39 +320,115 @@
     )(place, mine, masses, message, *near, far)
 
 
-def project_body(*refs):
-    blocks, weight, out, left, right = refs[:8], refs[8], refs[9], refs[10], refs[11]
-    low = lax.broadcasted_iota(jnp.int32, (8, 512), 0) < 4
+def by_target(total):
+    low = lax.broadcasted_iota(jnp.int32, (8, total.shape[1]), 0) < 4
+    chunks = []
+    for g in range(4):
+        even, odd = [], []
+        for j in (0, 2):
+            first = total[j * 32 + g * 8 : j * 32 + g * 8 + 8]
+            second = total[(j + 1) * 32 + g * 8 : (j + 1) * 32 + g * 8 + 8]
+            even.append(jnp.where(low, first, pltpu.roll(second, 4, 0)))
+            odd.append(jnp.where(low, pltpu.roll(first, 4, 0), second))
+        chunks += [jnp.concatenate(even, axis=0), jnp.concatenate(odd, axis=0)]
+    return chunks
+
+
+def project_body(count, *refs):
+    blocks, weights, out = refs[:count], refs[count : count + 2], refs[count + 2]
     for i, block in enumerate(blocks):
-        total = dot(block[...], weight[...])
-        for g in range(4):
-            even, odd = [], []
-            for j in (0, 2):
-                first = total[j * 32 + g * 8 : j * 32 + g * 8 + 8]
-                second = total[(j + 1) * 32 + g * 8 : (j + 1) * 32 + g * 8 + 8]
-                even.append(jnp.where(low, first, pltpu.roll(second, 4, 0)))
-                odd.append(jnp.where(low, pltpu.roll(first, 4, 0), second))
-            even, odd = jnp.concatenate(even, axis=0), jnp.concatenate(odd, axis=0)
-            out[2 * g, i * 16 : i * 16 + 16] = even
-            out[2 * g + 1, i * 16 : i * 16 + 16] = odd
-            if g == 2:
-                left[i * 16 : i * 16 + 16] = even[:, :256].astype(BF16)
-                right[i * 16 : i * 16 + 16] = even[:, 256:].astype(BF16)
-
-
-def project(blocks, weight):
-    half = jax.ShapeDtypeStruct((128, 256), BF16)
-    return pl.pallas_call(
-        project_body,
-        out_shape=[jax.ShapeDtypeStruct((8, 128, 512), F32), half, half],
-        in_specs=[VMEM] * 9,
-        out_specs=[VMEM] * 3,
-        compiler_params=params(),
+        for side, weight in enumerate(weights):
+            for d, chunk in enumerate(by_target(dot(block[...], weight[...]))):
+                out[d, i * 16 : i * 16 + 16, side * 512 : side * 512 + 512] = chunk
+
+
+def project(blocks, weights):
+    count = len(blocks)
+    return pl.pallas_call(
+        lambda *refs: project_body(count, *refs),
+        out_shape=jax.ShapeDtypeStruct((8, 16 * count, 1024), F32),
+        in_specs=[VMEM] * (count + 2),
+        out_specs=VMEM,
+        compiler_params=params(),
+        cost_estimate=pl.CostEstimate(
+            flops=count * 2 * 128 * 2048 * 1024, bytes_accessed=4_500_000, transcendentals=0
+        ),
         name="project",
-    )(*blocks, weight)
-
-
-def finish_body(place, own, left, right, orders, out):
+    )(*blocks, *weights)
+
+
+def last_body(block, w0, w1, first, second, up, down, up4, down4, keep):
+    for side, weight in enumerate((w0, w1)):
+        columns = slice(side * 512, side * 512 + 512)
+        chunks = by_target(dot(block[...], weight[...]))
+        for d, chunk in enumerate(chunks):
+            whole = jnp.concatenate([first[d, :, columns], second[d, :, columns], chunk], axis=0)
+            if d in (0, 2, 6):
+                keep[(0, 2, 6).index(d), :, columns] = whole
+            elif d in (3, 1):
+                up[(3, 1).index(d), :, columns] = whole.astype(BF16)
+            elif d in (5, 7):
+                down[(5, 7).index(d), :, columns] = whole.astype(BF16)
+            elif side == 0:
+                up4[...] = whole.astype(BF16)
+            else:
+                down4[...] = whole.astype(BF16)
+
+
+def project_last(block, weights, first, second):
+    pair = jax.ShapeDtypeStruct((2, 64, 1024), BF16)
+    half = jax.ShapeDtypeStruct((64, 512), BF16)
+    return pl.pallas_call(
+        last_body,
+        out_shape=[pair, pair, half, half, jax.ShapeDtypeStruct((3, 64, 1024), F32)],
+        in_specs=[VMEM] * 5,
+        out_specs=[VMEM] * 5,
+        compiler_params=params(),
+        name="project_last",
+    )(block, *weights, first, second)
+
+
+def middle_body(keep, below, above, below4, above4, up, down):
+    u = keep[1] + below[0].astype(F32)
+    up[:, :512] = (u[:, :512] + below4[...].astype(F32)).astype(BF16)
+    up[:, 512:] = u[:, 512:].astype(BF16)
+    d = keep[2] + above[0].astype(F32)
+    down[:, :512] = d[:, :512].astype(BF16)
+    down[:, 512:] = (d[:, 512:] + above4[...].astype(F32)).astype(BF16)
+
+
+def middle(keep, below, above, below4, above4):
+    out = jax.ShapeDtypeStruct((64, 1024), BF16)
+    return pl.pallas_call(
+        middle_body,
+        out_shape=[out, out],
+        in_specs=[VMEM] * 5,
+        out_specs=[VMEM] * 2,
+        compiler_params=params(),
+        name="middle",
+    )(keep, below, above, below4, above4)
+
+
+def total_body(keep, below, above, below2, above2, own, other):
+    near = keep[0] + below[1].astype(F32) + above[1].astype(F32)
+    total = (near + below2[...].astype(F32) + above2[...].astype(F32)).astype(BF16)
+    own[...] = total[:, :512]
+    other[...] = total[:, 512:]
+
+
+def total(keep, below, above, below2, above2):
+    out = jax.ShapeDtypeStruct((64, 512), BF16)
+    return pl.pallas_call(
+        total_body,
+        out_shape=[out, out],
+        in_specs=[VMEM] * 5,
+        out_specs=[VMEM] * 2,
+        compiler_params=params(),
+        name="total",
+    )(keep, below, above, below2, above2)
+
+
+def order_body(place, orders, pick):
     x, y, core, z = place[2], place[3] * 2 + place[5], place[6], place[4]
     lane = lanes()
     order = jnp.zeros((GROUP, DH), F32)
@@ -318,22 +444,38 @@
     dy = (2 * (prompt & 1) + (block >> 1)) ^ y
     first = jnp.where(far == 0, dx, dy)
     second = jnp.where(far == 0, dy, dx)
+    second = jnp.where(second >= 2, 5 - second, second)
     source = ((far ^ core) * 16 + second * 4 + first) * 4 + k
     row = lax.broadcasted_iota(jnp.int32, (128, 128), 0)
-    pick = (row == source[0:1]).astype(F32).astype(BF16)
-    total = own[...] + left[...].astype(F32) + right[...].astype(F32)
-    out[...] = dot(pick, total.astype(BF16), (((0,), (0,)), ((), ()))).astype(BF16)
-
-
-def finish(place, own, left, right, orders):
+    pick[...] = (row == source[0:1]).astype(F32).astype(BF16)
+
+
+def order_rows(place, orders):
+    return pl.pallas_call(
+        order_body,
+        out_shape=jax.ShapeDtypeStruct((128, 128), BF16),
+        in_specs=[SMEM, VMEM],
+        out_specs=VMEM,
+        compiler_params=params(),
+        name="order_rows",
+    )(place, orders)
+
+
+def finish_body(own, other, pick, out):
+    dims = (((0,), (0,)), ((), ()))
+    mixed = dot(pick[0:64], own[...], dims) + dot(pick[64:128], other[...], dims)
+    out[...] = mixed.astype(BF16)
+
+
+def finish(own, other, pick):
     return pl.pallas_call(
         finish_body,
         out_shape=jax.ShapeDtypeStruct((128, 512), BF16),
-        in_specs=[SMEM] + [VMEM] * 4,
+        in_specs=[VMEM] * 3,
         out_specs=VMEM,
         compiler_params=params(),
         name="finish",
-    )(place, own, left, right, orders)
+    )(own, other, pick)
 
 
 def along(value, shift, k):
@@ -357,12 +499,8 @@
     return lax.ppermute(value, "batch", pairs)
 
 
-def up(value):
-    return lax.ppermute(value, "head", [(i, (i + 1) % HEADS) for i in range(HEADS)])
-
-
-def down(value):
-    return lax.ppermute(value, "head", [(i, (i - 1) % HEADS) for i in range(HEADS)])
+def along_z(value, k):
+    return lax.ppermute(value, "head", [(i, (i + k) % HEADS) for i in range(HEADS)])
 
 
 def shards(queries, new_kv, prefix_kv, suffix_kv, page_table, suffix_len, prompt_of, out_weight):
@@ -373,15 +511,14 @@
     place = jnp.stack(place).astype(jnp.int32)
 
     prefix_other = other_core(prefix_kv)
-
-    q = queries.reshape(32, GROUP, DH)
-    sent = sort_queries(place, prompt_of, q)
+    weights = [out_weight, other_core(out_weight)]
+
+    *sent, q = sort_queries(place, prompt_of, queries)
     by_x = [sent[0]] + [along_x(sent[k], k) for k in (1, 2, 3)]
     same, other = regroup(place, by_x)
     from1, from3, from2 = along_y(same, 1), along_y(other, 3), along_y(other, 2)
-    orders = jnp.stack([same[16], from1[16], from2[16], from3[16]])
-    orders = jnp.concatenate([orders, other_core(orders)], axis=0)
-
+
+    q, same = lax.optimization_barrier((q, same))
     suffix = suffix_parts(place, prompt_of, page_table, suffix_len, q, new_kv, suffix_kv)
     near = [suffix[0]] + [along_x(suffix[k], k) for k in (1, 2, 3)]
     far = along_y(jnp.concatenate([a[4:] for a in near], axis=0), 2)
@@ -389,25 +526,25 @@
     message = along_y(prefix_send(from1, from3, prefix_kv, prefix_other), 1)
     mine, masses = prefix_keep(same, from2, prefix_kv, prefix_other)
     attended = combine(place, mine, masses, message, near, far)
+
+    orders = jnp.stack([same[16], from1[16], from2[16], from3[16]])
+    orders = jnp.concatenate([orders, other_core(orders)], axis=0)
+    pick = order_rows(place, orders)
 
     parts = [attended] + [turned(attended, k, 0) for k in (1, 2, 3)]
     ring0 = jnp.concatenate(parts, axis=0)
     ring1, ring3 = turned(ring0, 1, 1), turned(ring0, 3, 1)
     ring2 = jnp.concatenate([turned(ring3[:64], 1, 1), turned(ring1[64:], 3, 1)], axis=0)
-    mine_all = [ring0, ring1, ring2, ring3]
-    blocks = mine_all + [other_core(a) for a in mine_all]
-
-    partial, left, right = project(blocks, out_weight)
-    from_up, from_down = down(left), up(right)
-    low = jnp.concatenate([partial[5][:, :256] + from_up.astype(F32), partial[5][:, 256:]], axis=1)
-    high = jnp.concatenate([partial[3][:, :256], partial[3][:, 256:] + from_down.astype(F32)], axis=1)
-    from_up, from_down = down(low.astype(BF16)), up(high.astype(BF16))
-    for step in (2, 1):
-        low = partial[8 - step] + from_up.astype(F32)
-        high = partial[step] + from_down.astype(F32)
-        from_up, from_down = down(low.astype(BF16)), up(high.astype(BF16))
-
-    return finish(place, partial[0], from_up, from_down, orders)
+    first = project([ring0], weights)
+    second = project([ring1, ring3], weights)
+    up, down, up4, down4, keep = project_last(ring2, weights, first, second)
+
+    below4, above4 = along_z(up4, 2), along_z(down4, -2)
+    below, above = along_z(up, 1), along_z(down, -1)
+    up2, down2 = middle(keep, below, above, below4, above4)
+    below2, above2 = along_z(up2, 2), along_z(down2, -2)
+    own, other = total(keep, below, above, below2, above2)
+    return finish(own, other_core(other), pick)
 
 
 def solution(mesh):

time: 113 us -> 107 us (0.947)
  the two profiles are of different devices: /device:TPU:4 before, /device:TPU:1 now
where the time goes in v2:
time: 107 us; the launch traced here: 106 us
  starting transfers between devices  57.4 us (54%)
  waiting for transfers between devices  23.5 us (22%)
  Pallas kernels  18.9 us (18%)
  local copies, waits for them, and re-layouts  6.11 us (6%)
    ppermute x15, starting transfers between devices, along(): lax.ppermute(value, 'batch', [(i, i ^ k << shift) for i in range(BATCH)])  37.5 us
    ppermute x7, waiting for transfers between devices, turned(): return lax.ppermute(value, 'batch', pairs)  16.6 us
    ppermute x6, starting transfers between devices, along_z(): lax.ppermute(value, 'head', [(i, (i + k) % HEADS) for i in range(HEADS)])  13.2 us
    ppermute x7, starting transfers between devices, turned(): return lax.ppermute(value, 'batch', pairs)  6.75 us
    unnamed x17, local copies, waits for them, and re-layouts  5.94 us
    pallas_call x1, Pallas kernels, prefix_keep(): pl.pallas_call(prefix_keep_body, out_shape=[out, out], in_specs=[VMEM] *...  4.15 us
    pallas_call x1, Pallas kernels, prefix_send(): pl.pallas_call(prefix_send_body, out_shape=jax.ShapeDtypeStruct((33, GROU...  4.14 us
    ppermute x15, waiting for transfers between devices, along(): lax.ppermute(value, 'batch', [(i, i ^ k << shift) for i in range(BATCH)])  4.08 us
  transfers between devices with their start and end apart: 28, of which 10 were waited for; matrix products, arithmetic and copies ran while one was open for 1% of the time, Pallas kernels for 16%

profile of v2, /device:TPU:1, one launch (start us, length us, event | category | flops | bytes accessed | tf_op | source)
XLA Modules:
  0.0 106.3 jit_solution(15262792786447952714)
XLA Ops:
  0.0 3.2 %collective-permute-start.4 = (bf16[2,2048,128]{2,1,0:T(8,128)(2,1)}, bf16[2,2048,128]{2,1,0:T(8,128)(2,1)S(1)}, u32[]{:S(2)}, u32[]{:S(2)}) collective-permute-start(bf16[2,2048,128]{2,1,0:T(8,128)(2,1)} %kv0.3), channel_id=1, source_target_pairs={{0,8},{8,0},{16,24},{24,16},{32,40},{40,32},{48,56},{56,48},{64,72... | collective-permute-start | bytes 3145736 | tf_op jit(solution)/shard_map/ppermute | solution.py:482
  3.2 0.0 collective-permute-start.19
  3.2 0.1 stack.34.place
  3.3 0.9 copy-done.2
  4.2 0.7 copy-done.4
  4.9 1.4 %sort_queries.1 = (bf16[9,16,128]{2,1,0:T(8,128)(2,1)S(1)}, bf16[9,16,128]{2,1,0:T(8,128)(2,1)S(1)}, bf16[9,16,128]{2,1,0:T(8,128)(2,1)S(1)}, bf16[9,16,128]{2,1,0:T(8,128)(2,1)S(1)}, bf16[32,16,128]{2,1,0:T(8,128)(2,1)S(1)}) custom-call(s32[7]{0:T(128)S(1)} %stack.34.place, s32[32]{0:T(128)S(1)} %copy-done.4, bf16[32,2048]{1,0:T(8,128)(2,1)S(1)} %copy-done.2), custom_call_target="tpu_custom_call" | custom-call | tf_op jit(solution)/shard_map/sort_queries/pallas_call | solution.py:81
  6.2 0.1 collective-permute-start
  6.4 1.9 %collective-permute-start.1 = (bf16[9,16,128]{2,1,0:T(8,128)(2,1)S(1)}, bf16[9,16,128]{2,1,0:T(8,128)(2,1)S(1)}, u32[]{:S(2)}, u32[]{:S(2)}) collective-permute-start(bf16[9,16,128]{2,1,0:T(8,128)(2,1)S(1)} %get-tuple-element.32), channel_id=1, source_target_pairs={{0,128},{8,136},{16,144},{24,152},{32,160},{40,168},{48,176},{56,1... | collective-permute-start | bytes 110600 | tf_op jit(solution)/shard_map/ppermute | solution.py:482
  8.3 1.9 %collective-permute-start.2 = (bf16[9,16,128]{2,1,0:T(8,128)(2,1)S(1)}, bf16[9,16,128]{2,1,0:T(8,128)(2,1)S(1)}, u32[]{:S(2)}, u32[]{:S(2)}) collective-permute-start(bf16[9,16,128]{2,1,0:T(8,128)(2,1)S(1)} %get-tuple-element.33), channel_id=1, source_target_pairs={{0,192},{8,200},{16,208},{24,216},{32,224},{40,232},{48,240},{56,2... | collective-permute-start | bytes 110600 | tf_op jit(solution)/shard_map/ppermute | solution.py:482
  10.2 0.8 copy.9.table_in
  11.0 0.0 collective-permute-done.a1
  11.0 0.0 collective-permute-done.1.a2
  11.0 1.3 %collective-permute-done.2.a3 = bf16[9,16,128]{2,1,0:T(8,128)(2,1)S(1)} collective-permute-done((bf16[9,16,128]{2,1,0:T(8,128)(2,1)S(1)}, bf16[9,16,128]{2,1,0:T(8,128)(2,1)S(1)}, u32[]{:S(2)}, u32[]{:S(2)}) %collective-permute-start.2) | collective-permute-done | bytes 36896 | tf_op jit(solution)/shard_map/ppermute | solution.py:482
  12.3 0.6 regroup.1
  12.9 0.0 copy-start.1
  12.9 1.6 %copy-done.1 = bf16[2,256,16,128]{3,2,1,0:T(8,128)(2,1)S(1)} copy-done((bf16[2,256,16,128]{3,2,1,0:T(8,128)(2,1)S(1)}, bf16[2,256,16,128]{3,2,1,0:T(8,128)(2,1)}, u32[]{:S(2)}) %copy-start.1) | copy-done | bytes 2097176
  14.5 0.7 copy-done.3
  15.2 0.7 copy-done.5
  15.8 0.7 copy-done.6
  16.5 3.0 %suffix_parts.1 = (bf16[9,16,128]{2,1,0:T(8,128)(2,1)S(1)}, bf16[9,16,128]{2,1,0:T(8,128)(2,1)S(1)}, bf16[9,16,128]{2,1,0:T(8,128)(2,1)S(1)}, bf16[9,16,128]{2,1,0:T(8,128)(2,1)S(1)}) custom-call(s32[7]{0:T(128)S(1)} %stack.34.place, s32[32]{0:T(128)S(1)} %copy-done.5, s32[32,8]{1,0:T(8,128)S(1)} %copy.9.table_in, s32[32]{0:T(128)S(1)} %copy-done.6, ...), custom_call_target="tpu_custom_call" | custom-call | flops 40000000 | bytes 3000000 | tf_op jit(solution)/shard_map/suffix_parts/pallas_call | solution.py:185
  19.5 0.1 collective-permute-start.8
  19.6 3.1 %collective-permute-start.9 = (bf16[9,16,128]{2,1,0:T(8,128)(2,1)S(1)}, bf16[9,16,128]{2,1,0:T(8,128)(2,1)S(1)}, u32[]{:S(2)}, u32[]{:S(2)}) collective-permute-start(bf16[9,16,128]{2,1,0:T(8,128)(2,1)S(1)} %get-tuple-element.42), channel_id=1, source_target_pairs={{0,128},{8,136},{16,144},{24,152},{32,160},{40,168},{48,176},{56,1... | collective-permute-start | bytes 110600 | tf_op jit(solution)/shard_map/ppermute | solution.py:482
  22.7 0.0 collective-permute-start.5
  22.7 2.4 %collective-permute-start.6 = (bf16[17,16,128]{2,1,0:T(8,128)(2,1)S(1)}, bf16[17,16,128]{2,1,0:T(8,128)(2,1)S(1)}, u32[]{:S(2)}, u32[]{:S(2)}) collective-permute-start(bf16[17,16,128]{2,1,0:T(8,128)(2,1)S(1)} %get-tuple-element.36), channel_id=1, source_target_pairs={{0,48},{8,56},{16,32},{24,40},{32,16},{40,24},{48,0},{56,8},{64,11... | collective-permute-start | bytes 208904 | tf_op jit(solution)/shard_map/ppermute | solution.py:482
  25.1 0.0 collective-permute-done.9.s2
  25.1 1.5 %collective-permute-start.10 = (bf16[9,16,128]{2,1,0:T(8,128)(2,1)S(1)}, bf16[9,16,128]{2,1,0:T(8,128)(2,1)S(1)}, u32[]{:S(2)}, u32[]{:S(2)}) collective-permute-start(bf16[9,16,128]{2,1,0:T(8,128)(2,1)S(1)} %get-tuple-element.43), channel_id=1, source_target_pairs={{0,192},{8,200},{16,208},{24,216},{32,224},{40,232},{48,240},{56,2... | collective-permute-start | bytes 110600 | tf_op jit(solution)/shard_map/ppermute | solution.py:482
  26.6 2.5 %collective-permute-done.10.s3 = bf16[9,16,128]{2,1,0:T(8,128)(2,1)S(1)} collective-permute-done((bf16[9,16,128]{2,1,0:T(8,128)(2,1)S(1)}, bf16[9,16,128]{2,1,0:T(8,128)(2,1)S(1)}, u32[]{:S(2)}, u32[]{:S(2)}) %collective-permute-start.10) | collective-permute-done | bytes 36896 | tf_op jit(solution)/shard_map/ppermute | solution.py:482
  29.1 1.8 %collective-permute-start.3 = (bf16[17,16,128]{2,1,0:T(8,128)(2,1)S(1)}, bf16[17,16,128]{2,1,0:T(8,128)(2,1)S(1)}, u32[]{:S(2)}, u32[]{:S(2)}) collective-permute-start(bf16[17,16,128]{2,1,0:T(8,128)(2,1)S(1)} %get-tuple-element.36), channel_id=1, source_target_pairs={{0,32},{8,40},{16,48},{24,56},{32,0},{40,8},{48,16},{56,24},{64,96... | collective-permute-start | bytes 208904 | tf_op jit(solution)/shard_map/ppermute | solution.py:482
  30.9 0.0 collective-permute-done.5.qa
  30.9 0.0 collective-permute-done.6.qb
  30.9 4.1 %prefix_send.1 = bf16[33,16,128]{2,1,0:T(8,128)(2,1)S(1)} custom-call(bf16[17,16,128]{2,1,0:T(8,128)(2,1)S(1)} %collective-permute-done.5.qa, bf16[17,16,128]{2,1,0:T(8,128)(2,1)S(1)} %collective-permute-done.6.qb, bf16[2,2048,128]{2,1,0:T(8,128)(2,1)S(1)} %copy-done.7, bf16[2,2048,128]{2,1,0:T(8,128)(2,1)S(1)} %collective-permute-done.4.kv1), custom_call_target="tpu_custom_call" | custom-call | flops 1073741824 | bytes 2500000 | tf_op jit(solution)/shard_map/prefix_send/pallas_call | solution.py:260
  35.1 0.7 collective-permute-start.7
  35.8 1.7 %collective-permute-start.11 = (bf16[20,16,128]{2,1,0:T(8,128)(2,1)S(1)}, bf16[20,16,128]{2,1,0:T(8,128)(2,1)S(1)}, u32[]{:S(2)}, u32[]{:S(2)}) collective-permute-start(bf16[20,16,128]{2,1,0:T(8,128)(2,1)S(1)} %pad_maximum_fusion.2), channel_id=1, source_target_pairs={{0,32},{8,40},{16,48},{24,56},{32,0},{40,8},{48,16},{56,24},{64,96... | collective-permute-start | bytes 245768 | tf_op jit(solution)/shard_map/ppermute | solution.py:482
  37.4 4.1 %prefix_keep.1 = (f32[32,16,128]{2,1,0:T(8,128)S(1)}, f32[32,16,128]{2,1,0:T(8,128)S(1)}) custom-call(bf16[17,16,128]{2,1,0:T(8,128)(2,1)S(1)} %get-tuple-element.35.qa, bf16[17,16,128]{2,1,0:T(8,128)(2,1)S(1)} %collective-permute-done.3.qb, bf16[2,2048,128]{2,1,0:T(8,128)(2,1)S(1)} %copy-done.7, bf16[2,2048,128]{2,1,0:T(8,128)(2,1)S(1)} %collective-permute-done.4.kv1), custom_call_target="tpu_custom_call" | custom-call | flops 1073741824 | bytes 2500000 | tf_op jit(solution)/shard_map/prefix_keep/pallas_call | solution.py:273
  41.6 0.0 copy-start
  41.6 1.2 %combine.1 = bf16[32,2048]{1,0:T(8,128)(2,1)S(1)} custom-call(s32[7]{0:T(128)S(1)} %stack.34.place, f32[32,16,128]{2,1,0:T(8,128)S(1)} %get-tuple-element.37.mine, f32[32,16,128]{2,1,0:T(8,128)S(1)} %get-tuple-element.38.masses, bf16[33,16,128]{2,1,0:T(8,128)(2,1)S(1)} %collective-permute-done.7.message, bf16[9,16,128]{2,1,0:T(8,128)(2,1)S(1)} %get-tuple-element.40.s0, ...), custom_call_target="tpu_custom_call" | custom-call | tf_op jit(solution)/shard_map/combine/pallas_call | solution.py:312
  42.8 2.0 %collective-permute-start.14 = (bf16[32,2048]{1,0:T(8,128)(2,1)S(1)}, bf16[32,2048]{1,0:T(8,128)(2,1)S(1)}, u32[]{:S(2)}, u32[]{:S(2)}) collective-permute-start(bf16[32,2048]{1,0:T(8,128)(2,1)S(1)} %combine.1), channel_id=1, source_target_pairs={{0,192},{8,56},{16,208},{24,40},{32,224},{40,24},{48,240},{56,8},{... | collective-permute-start | bytes 393224 | tf_op jit(solution)/shard_map/ppermute | solution.py:499
  44.8 1.3 %collective-permute-start.12 = (bf16[32,2048]{1,0:T(8,128)(2,1)S(1)}, bf16[32,2048]{1,0:T(8,128)(2,1)S(1)}, u32[]{:S(2)}, u32[]{:S(2)}) collective-permute-start(bf16[32,2048]{1,0:T(8,128)(2,1)S(1)} %combine.1), channel_id=1, source_target_pairs={{0,64},{8,24},{16,80},{24,8},{32,96},{40,56},{48,112},{56,40},{64,... | collective-permute-start | bytes 393224 | tf_op jit(solution)/shard_map/ppermute | solution.py:499
  46.2 2.0 %collective-permute-done.14 = bf16[32,2048]{1,0:T(8,128)(2,1)S(1)} collective-permute-done((bf16[32,2048]{1,0:T(8,128)(2,1)S(1)}, bf16[32,2048]{1,0:T(8,128)(2,1)S(1)}, u32[]{:S(2)}, u32[]{:S(2)}) %collective-permute-start.14) | collective-permute-done | bytes 131104 | tf_op jit(solution)/shard_map/ppermute | solution.py:499
  48.1 2.0 %collective-permute-done.13 = bf16[32,2048]{1,0:T(8,128)(2,1)S(1)} collective-permute-done((bf16[32,2048]{1,0:T(8,128)(2,1)S(1)}, bf16[32,2048]{1,0:T(8,128)(2,1)S(1)}, u32[]{:S(2)}, u32[]{:S(2)}) %collective-permute-start.13) | collective-permute-done | bytes 131104 | tf_op jit(solution)/shard_map/ppermute | solution.py:499
  50.2 0.9 collective-permute-start.17
  51.1 0.8 collective-permute-start.15
  51.9 9.2 %collective-permute-done.17.refs_0_ = bf16[128,2048]{1,0:T(8,128)(2,1)S(1)} collective-permute-done((bf16[128,2048]{1,0:T(8,128)(2,1)S(1)}, bf16[128,2048]{1,0:T(8,128)(2,1)S(1)}, u32[]{:S(2)}, u32[]{:S(2)}) %collective-permute-start.17) | collective-permute-done | bytes 524320 | tf_op jit(solution)/shard_map/ppermute | solution.py:499
  61.1 1.6 %collective-permute-start.18 = (bf16[64,2048]{1,0:T(8,128)(2,1)S(1)}, bf16[64,2048]{1,0:T(8,128)(2,1)S(1)}, u32[]{:S(2)}, u32[]{:S(2)}) collective-permute-start(bf16[64,2048]{1,0:T(8,128)(2,1)S(1)} %slice.44), channel_id=1, source_target_pairs={{0,48},{8,200},{16,32},{24,216},{32,16},{40,232},{48,0},{56,248},{... | collective-permute-start | bytes 786440 | tf_op jit(solution)/shard_map/ppermute | solution.py:499
  62.8 0.1 collective-permute-start.16
  62.9 0.7 project.2.first
  63.6 1.3 %project.3.second = f32[8,32,1024]{2,1,0:T(8,128)S(1)} custom-call(bf16[128,2048]{1,0:T(8,128)(2,1)S(1)} %collective-permute-done.17.refs_0_, bf16[128,2048]{1,0:T(8,128)(2,1)S(1)} %collective-permute-done.15.refs_1_, bf16[2048,512]{1,0:T(8,128)(2,1)S(1)} %copy-done, bf16[2048,512]{1,0:T(8,128)(2,1)S(1)} %collective-permute-done.19.refs_2_.refs_3_.w1), custom_call_target="tpu_custom_call" | custom-call | flops 1073741824 | bytes 4500000 | tf_op jit(solution)/shard_map/project/pallas_call | solution.py:347
  65.0 3.0 %collective-permute-done.18 = bf16[64,2048]{1,0:T(8,128)(2,1)S(1)} collective-permute-done((bf16[64,2048]{1,0:T(8,128)(2,1)S(1)}, bf16[64,2048]{1,0:T(8,128)(2,1)S(1)}, u32[]{:S(2)}, u32[]{:S(2)}) %collective-permute-start.18) | collective-permute-done | bytes 262176 | tf_op jit(solution)/shard_map/ppermute | solution.py:499
  67.9 0.4 collective-permute-done.16
  68.4 0.8 project_last.1
  69.2 1.7 %collective-permute-start.20 = (bf16[2,64,1024]{2,1,0:T(8,128)(2,1)S(1)}, bf16[2,64,1024]{2,1,0:T(8,128)(2,1)S(1)}, u32[]{:S(2)}, u32[]{:S(2)}) collective-permute-start(bf16[2,64,1024]{2,1,0:T(8,128)(2,1)S(1)} %get-tuple-element.45), channel_id=1, source_target_pairs={{0,1},{1,2},{2,3},{3,4},{4,5},{5,6},{6,7},{7,0},{8,9},{9,10},{10,1... | collective-permute-start | bytes 786440 | tf_op jit(solution)/shard_map/ppermute | solution.py:503
  70.9 4.2 %collective-permute-start.21 = (bf16[2,64,1024]{2,1,0:T(8,128)(2,1)S(1)}, bf16[2,64,1024]{2,1,0:T(8,128)(2,1)S(1)}, u32[]{:S(2)}, u32[]{:S(2)}) collective-permute-start(bf16[2,64,1024]{2,1,0:T(8,128)(2,1)S(1)} %get-tuple-element.46), channel_id=1, source_target_pairs={{0,7},{1,0},{2,1},{3,2},{4,3},{5,4},{6,5},{7,6},{8,15},{9,8},{10,9... | collective-permute-start | bytes 786440 | tf_op jit(solution)/shard_map/ppermute | solution.py:503
  75.2 3.6 %collective-permute-start.23 = (bf16[64,512]{1,0:T(8,128)(2,1)S(1)}, bf16[64,512]{1,0:T(8,128)(2,1)S(1)}, u32[]{:S(2)}, u32[]{:S(2)}) collective-permute-start(bf16[64,512]{1,0:T(8,128)(2,1)S(1)} %get-tuple-element.48), channel_id=1, source_target_pairs={{0,6},{1,7},{2,0},{3,1},{4,2},{5,3},{6,4},{7,5},{8,14},{9,15},{10,... | collective-permute-start | bytes 196616 | tf_op jit(solution)/shard_map/ppermute | solution.py:503
  78.8 2.3 %collective-permute-done.22.below4 = bf16[64,512]{1,0:T(8,128)(2,1)S(1)} collective-permute-done((bf16[64,512]{1,0:T(8,128)(2,1)S(1)}, bf16[64,512]{1,0:T(8,128)(2,1)S(1)}, u32[]{:S(2)}, u32[]{:S(2)}) %collective-permute-start.22) | collective-permute-done | bytes 65568 | tf_op jit(solution)/shard_map/ppermute | solution.py:503
  81.0 0.5 collective-permute-done.23.above4
  81.5 0.1 middle.1
  81.6 3.1 %collective-permute-start.24 = (bf16[64,1024]{1,0:T(8,128)(2,1)S(1)}, bf16[64,1024]{1,0:T(8,128)(2,1)S(1)}, u32[]{:S(2)}, u32[]{:S(2)}) collective-permute-start(bf16[64,1024]{1,0:T(8,128)(2,1)S(1)} %get-tuple-element.49), channel_id=1, source_target_pairs={{0,2},{1,3},{2,4},{3,5},{4,6},{5,7},{6,0},{7,1},{8,10},{9,11},{10,... | collective-permute-start | bytes 393224 | tf_op jit(solution)/shard_map/ppermute | solution.py:503
  84.7 0.5 collective-permute-start.25
  85.3 12.6 %collective-permute-start.27 = (bf16[4,16,128]{2,1,0:T(8,128)(2,1)S(1)}, bf16[4,16,128]{2,1,0:T(8,128)(2,1)S(1)}, u32[]{:S(2)}, u32[]{:S(2)}) collective-permute-start(bf16[4,16,128]{2,1,0:T(8,128)(2,1)S(1)} %pad_maximum_fusion.3), channel_id=1, source_target_pairs={{0,8},{8,0},{16,24},{24,16},{32,40},{40,32},{48,56},{56,48},{64,72... | collective-permute-start | bytes 49160 | tf_op jit(solution)/shard_map/ppermute | solution.py:482
  97.9 0.1 total.1
  98.0 6.5 %collective-permute-start.26 = (bf16[64,512]{1,0:T(8,128)(2,1)S(1)}, bf16[64,512]{1,0:T(8,128)(2,1)S(1)}, u32[]{:S(2)}, u32[]{:S(2)}) collective-permute-start(bf16[64,512]{1,0:T(8,128)(2,1)S(1)} %get-tuple-element.52), channel_id=1, source_target_pairs={{0,8},{8,0},{16,24},{24,16},{32,40},{40,32},{48,56},{56,48},{64,72... | collective-permute-start | bytes 196616 | tf_op jit(solution)/shard_map/ppermute | solution.py:482
  104.5 0.6 order_rows.1.pick
  105.1 0.2 collective-permute-done.26.other
  105.4 0.9 finish.1
  (38 shorter events, 0.2 us)
Async XLA Ops:
  0.0 30.9 %collective-permute-start.4 = (bf16[2,2048,128]{2,1,0:T(8,128)(2,1)}, bf16[2,2048,128]{2,1,0:T(8,128)(2,1)S(1)}, u32[]{:S(2)}, u32[]{:S(2)}) collective-permute-start(bf16[2,2048,128]{2,1,0:T(8,128)(2,1)} %kv0.3), channel_id=1, source_target_pairs={{0,8},{8,0},{16,24},{24,16},{32,40},{40,32},{48,56},{56,48},{64,72... | collective-permute-start | bytes 3145736 | tf_op jit(solution)/shard_map/ppermute | solution.py:482
  3.2 59.6 %collective-permute-start.19 = (bf16[2048,512]{1,0:T(8,128)(2,1)}, bf16[2048,512]{1,0:T(8,128)(2,1)S(1)}, u32[]{:S(2)}, u32[]{:S(2)}) collective-permute-start(bf16[2048,512]{1,0:T(8,128)(2,1)} %w0.1), channel_id=1, source_target_pairs={{0,8},{8,0},{16,24},{24,16},{32,40},{40,32},{48,56},{56,48},{64,72... | collective-permute-start | bytes 6291464 | tf_op jit(solution)/shard_map/ppermute | solution.py:482
  3.3 0.9 copy-start.2
  4.2 0.7 copy-start.4
  6.2 4.7 %collective-permute-start = (bf16[9,16,128]{2,1,0:T(8,128)(2,1)S(1)}, bf16[9,16,128]{2,1,0:T(8,128)(2,1)S(1)}, u32[]{:S(2)}, u32[]{:S(2)}) collective-permute-start(bf16[9,16,128]{2,1,0:T(8,128)(2,1)S(1)} %get-tuple-element.31), channel_id=1, source_target_pairs={{0,64},{8,72},{16,80},{24,88},{32,96},{40,104},{48,112},{56,120},{... | collective-permute-start | bytes 110600 | tf_op jit(solution)/shard_map/ppermute | solution.py:482
  6.4 4.6 %collective-permute-start.1 = (bf16[9,16,128]{2,1,0:T(8,128)(2,1)S(1)}, bf16[9,16,128]{2,1,0:T(8,128)(2,1)S(1)}, u32[]{:S(2)}, u32[]{:S(2)}) collective-permute-start(bf16[9,16,128]{2,1,0:T(8,128)(2,1)S(1)} %get-tuple-element.32), channel_id=1, source_target_pairs={{0,128},{8,136},{16,144},{24,152},{32,160},{40,168},{48,176},{56,1... | collective-permute-start | bytes 110600 | tf_op jit(solution)/shard_map/ppermute | solution.py:482
  8.3 4.0 %collective-permute-start.2 = (bf16[9,16,128]{2,1,0:T(8,128)(2,1)S(1)}, bf16[9,16,128]{2,1,0:T(8,128)(2,1)S(1)}, u32[]{:S(2)}, u32[]{:S(2)}) collective-permute-start(bf16[9,16,128]{2,1,0:T(8,128)(2,1)S(1)} %get-tuple-element.33), channel_id=1, source_target_pairs={{0,192},{8,200},{16,208},{24,216},{32,224},{40,232},{48,240},{56,2... | collective-permute-start | bytes 110600 | tf_op jit(solution)/shard_map/ppermute | solution.py:482
  12.9 1.6 %copy-start.1 = (bf16[2,256,16,128]{3,2,1,0:T(8,128)(2,1)S(1)}, bf16[2,256,16,128]{3,2,1,0:T(8,128)(2,1)}, u32[]{:S(2)}) copy-start(bf16[2,256,16,128]{3,2,1,0:T(8,128)(2,1)} %pool_in.1) | copy-start | bytes 6291460
  14.5 0.7 copy-start.3
  15.2 0.7 copy-start.5
  15.8 0.7 copy-start.6
  16.5 14.4 %copy-start.7 = (bf16[2,2048,128]{2,1,0:T(8,128)(2,1)S(1)}, bf16[2,2048,128]{2,1,0:T(8,128)(2,1)}, u32[]{:S(2)}) copy-start(bf16[2,2048,128]{2,1,0:T(8,128)(2,1)} %kv0.3) | copy-start | bytes 3145732
  19.5 3.2 %collective-permute-start.8 = (bf16[9,16,128]{2,1,0:T(8,128)(2,1)S(1)}, bf16[9,16,128]{2,1,0:T(8,128)(2,1)S(1)}, u32[]{:S(2)}, u32[]{:S(2)}) collective-permute-start(bf16[9,16,128]{2,1,0:T(8,128)(2,1)S(1)} %get-tuple-element.41), channel_id=1, source_target_pairs={{0,64},{8,72},{16,80},{24,88},{32,96},{40,104},{48,112},{56,120},{... | collective-permute-start | bytes 110600 | tf_op jit(solution)/shard_map/ppermute | solution.py:482
  19.6 5.5 %collective-permute-start.9 = (bf16[9,16,128]{2,1,0:T(8,128)(2,1)S(1)}, bf16[9,16,128]{2,1,0:T(8,128)(2,1)S(1)}, u32[]{:S(2)}, u32[]{:S(2)}) collective-permute-start(bf16[9,16,128]{2,1,0:T(8,128)(2,1)S(1)} %get-tuple-element.42), channel_id=1, source_target_pairs={{0,128},{8,136},{16,144},{24,152},{32,160},{40,168},{48,176},{56,1... | collective-permute-start | bytes 110600 | tf_op jit(solution)/shard_map/ppermute | solution.py:482
  22.7 8.2 %collective-permute-start.5 = (bf16[17,16,128]{2,1,0:T(8,128)(2,1)S(1)}, bf16[17,16,128]{2,1,0:T(8,128)(2,1)S(1)}, u32[]{:S(2)}, u32[]{:S(2)}) collective-permute-start(bf16[17,16,128]{2,1,0:T(8,128)(2,1)S(1)} %get-tuple-element.35.qa), channel_id=1, source_target_pairs={{0,16},{8,24},{16,0},{24,8},{32,48},{40,56},{48,32},{56,40},{64,80... | collective-permute-start | bytes 208904 | tf_op jit(solution)/shard_map/ppermute | solution.py:482
  22.7 8.2 %collective-permute-start.6 = (bf16[17,16,128]{2,1,0:T(8,128)(2,1)S(1)}, bf16[17,16,128]{2,1,0:T(8,128)(2,1)S(1)}, u32[]{:S(2)}, u32[]{:S(2)}) collective-permute-start(bf16[17,16,128]{2,1,0:T(8,128)(2,1)S(1)} %get-tuple-element.36), channel_id=1, source_target_pairs={{0,48},{8,56},{16,32},{24,40},{32,16},{40,24},{48,0},{56,8},{64,11... | collective-permute-start | bytes 208904 | tf_op jit(solution)/shard_map/ppermute | solution.py:482
  25.1 4.0 %collective-permute-start.10 = (bf16[9,16,128]{2,1,0:T(8,128)(2,1)S(1)}, bf16[9,16,128]{2,1,0:T(8,128)(2,1)S(1)}, u32[]{:S(2)}, u32[]{:S(2)}) collective-permute-start(bf16[9,16,128]{2,1,0:T(8,128)(2,1)S(1)} %get-tuple-element.43), channel_id=1, source_target_pairs={{0,192},{8,200},{16,208},{24,216},{32,224},{40,232},{48,240},{56,2... | collective-permute-start | bytes 110600 | tf_op jit(solution)/shard_map/ppermute | solution.py:482
  29.1 8.3 %collective-permute-start.3 = (bf16[17,16,128]{2,1,0:T(8,128)(2,1)S(1)}, bf16[17,16,128]{2,1,0:T(8,128)(2,1)S(1)}, u32[]{:S(2)}, u32[]{:S(2)}) collective-permute-start(bf16[17,16,128]{2,1,0:T(8,128)(2,1)S(1)} %get-tuple-element.36), channel_id=1, source_target_pairs={{0,32},{8,40},{16,48},{24,56},{32,0},{40,8},{48,16},{56,24},{64,96... | collective-permute-start | bytes 208904 | tf_op jit(solution)/shard_map/ppermute | solution.py:482
  35.1 6.5 %collective-permute-start.7 = (bf16[33,16,128]{2,1,0:T(8,128)(2,1)S(1)}, bf16[33,16,128]{2,1,0:T(8,128)(2,1)S(1)}, u32[]{:S(2)}, u32[]{:S(2)}) collective-permute-start(bf16[33,16,128]{2,1,0:T(8,128)(2,1)S(1)} %prefix_send.1), channel_id=1, source_target_pairs={{0,16},{8,24},{16,0},{24,8},{32,48},{40,56},{48,32},{56,40},{64,80... | collective-permute-start | bytes 405512 | tf_op jit(solution)/shard_map/ppermute | solution.py:482
  35.8 5.8 %collective-permute-start.11 = (bf16[20,16,128]{2,1,0:T(8,128)(2,1)S(1)}, bf16[20,16,128]{2,1,0:T(8,128)(2,1)S(1)}, u32[]{:S(2)}, u32[]{:S(2)}) collective-permute-start(bf16[20,16,128]{2,1,0:T(8,128)(2,1)S(1)} %pad_maximum_fusion.2), channel_id=1, source_target_pairs={{0,32},{8,40},{16,48},{24,56},{32,0},{40,8},{48,16},{56,24},{64,96... | collective-permute-start | bytes 245768 | tf_op jit(solution)/shard_map/ppermute | solution.py:482
  41.6 21.3 %copy-start = (bf16[2048,512]{1,0:T(8,128)(2,1)S(1)}, bf16[2048,512]{1,0:T(8,128)(2,1)}, u32[]{:S(2)}) copy-start(bf16[2048,512]{1,0:T(8,128)(2,1)} %w0.1) | copy-start | bytes 6291460
  42.8 5.3 %collective-permute-start.14 = (bf16[32,2048]{1,0:T(8,128)(2,1)S(1)}, bf16[32,2048]{1,0:T(8,128)(2,1)S(1)}, u32[]{:S(2)}, u32[]{:S(2)}) collective-permute-start(bf16[32,2048]{1,0:T(8,128)(2,1)S(1)} %combine.1), channel_id=1, source_target_pairs={{0,192},{8,56},{16,208},{24,40},{32,224},{40,24},{48,240},{56,8},{... | collective-permute-start | bytes 393224 | tf_op jit(solution)/shard_map/ppermute | solution.py:499
  44.8 5.3 %collective-permute-start.13 = (bf16[32,2048]{1,0:T(8,128)(2,1)S(1)}, bf16[32,2048]{1,0:T(8,128)(2,1)S(1)}, u32[]{:S(2)}, u32[]{:S(2)}) collective-permute-start(bf16[32,2048]{1,0:T(8,128)(2,1)S(1)} %combine.1), channel_id=1, source_target_pairs={{0,128},{8,40},{16,144},{24,56},{32,160},{40,8},{48,176},{56,24},{... | collective-permute-start | bytes 393224 | tf_op jit(solution)/shard_map/ppermute | solution.py:499
  44.8 5.3 %collective-permute-start.12 = (bf16[32,2048]{1,0:T(8,128)(2,1)S(1)}, bf16[32,2048]{1,0:T(8,128)(2,1)S(1)}, u32[]{:S(2)}, u32[]{:S(2)}) collective-permute-start(bf16[32,2048]{1,0:T(8,128)(2,1)S(1)} %combine.1), channel_id=1, source_target_pairs={{0,64},{8,24},{16,80},{24,8},{32,96},{40,56},{48,112},{56,40},{64,... | collective-permute-start | bytes 393224 | tf_op jit(solution)/shard_map/ppermute | solution.py:499
  50.2 10.9 %collective-permute-start.17 = (bf16[128,2048]{1,0:T(8,128)(2,1)S(1)}, bf16[128,2048]{1,0:T(8,128)(2,1)S(1)}, u32[]{:S(2)}, u32[]{:S(2)}) collective-permute-start(bf16[128,2048]{1,0:T(8,128)(2,1)S(1)} %pad_maximum_fusion.refs_0_), channel_id=1, source_target_pairs={{0,16},{8,72},{16,0},{24,88},{32,48},{40,104},{48,32},{56,120},{64... | collective-permute-start | bytes 1572872 | tf_op jit(solution)/shard_map/ppermute | solution.py:499
  51.1 11.6 %collective-permute-start.15 = (bf16[128,2048]{1,0:T(8,128)(2,1)S(1)}, bf16[128,2048]{1,0:T(8,128)(2,1)S(1)}, u32[]{:S(2)}, u32[]{:S(2)}) collective-permute-start(bf16[128,2048]{1,0:T(8,128)(2,1)S(1)} %pad_maximum_fusion.refs_0_), channel_id=1, source_target_pairs={{0,48},{8,200},{16,32},{24,216},{32,16},{40,232},{48,0},{56,248},{... | collective-permute-start | bytes 1572872 | tf_op jit(solution)/shard_map/ppermute | solution.py:499
  61.1 6.8 %collective-permute-start.18 = (bf16[64,2048]{1,0:T(8,128)(2,1)S(1)}, bf16[64,2048]{1,0:T(8,128)(2,1)S(1)}, u32[]{:S(2)}, u32[]{:S(2)}) collective-permute-start(bf16[64,2048]{1,0:T(8,128)(2,1)S(1)} %slice.44), channel_id=1, source_target_pairs={{0,48},{8,200},{16,32},{24,216},{32,16},{40,232},{48,0},{56,248},{... | collective-permute-start | bytes 786440 | tf_op jit(solution)/shard_map/ppermute | solution.py:499
  62.8 5.6 %collective-permute-start.16 = (bf16[64,2048]{1,0:T(8,128)(2,1)S(1)}, bf16[64,2048]{1,0:T(8,128)(2,1)S(1)}, u32[]{:S(2)}, u32[]{:S(2)}) collective-permute-start(bf16[64,2048]{1,0:T(8,128)(2,1)S(1)} %slice.43), channel_id=1, source_target_pairs={{0,16},{8,72},{16,0},{24,88},{32,48},{40,104},{48,32},{56,120},{64... | collective-permute-start | bytes 786440 | tf_op jit(solution)/shard_map/ppermute | solution.py:499
  69.2 12.3 %collective-permute-start.20 = (bf16[2,64,1024]{2,1,0:T(8,128)(2,1)S(1)}, bf16[2,64,1024]{2,1,0:T(8,128)(2,1)S(1)}, u32[]{:S(2)}, u32[]{:S(2)}) collective-permute-start(bf16[2,64,1024]{2,1,0:T(8,128)(2,1)S(1)} %get-tuple-element.45), channel_id=1, source_target_pairs={{0,1},{1,2},{2,3},{3,4},{4,5},{5,6},{6,7},{7,0},{8,9},{9,10},{10,1... | collective-permute-start | bytes 786440 | tf_op jit(solution)/shard_map/ppermute | solution.py:503
  70.9 10.6 %collective-permute-start.21 = (bf16[2,64,1024]{2,1,0:T(8,128)(2,1)S(1)}, bf16[2,64,1024]{2,1,0:T(8,128)(2,1)S(1)}, u32[]{:S(2)}, u32[]{:S(2)}) collective-permute-start(bf16[2,64,1024]{2,1,0:T(8,128)(2,1)S(1)} %get-tuple-element.46), channel_id=1, source_target_pairs={{0,7},{1,0},{2,1},{3,2},{4,3},{5,4},{6,5},{7,6},{8,15},{9,8},{10,9... | collective-permute-start | bytes 786440 | tf_op jit(solution)/shard_map/ppermute | solution.py:503
  75.2 5.9 %collective-permute-start.22 = (bf16[64,512]{1,0:T(8,128)(2,1)S(1)}, bf16[64,512]{1,0:T(8,128)(2,1)S(1)}, u32[]{:S(2)}, u32[]{:S(2)}) collective-permute-start(bf16[64,512]{1,0:T(8,128)(2,1)S(1)} %get-tuple-element.47), channel_id=1, source_target_pairs={{0,2},{1,3},{2,4},{3,5},{4,6},{5,7},{6,0},{7,1},{8,10},{9,11},{10,... | collective-permute-start | bytes 196616 | tf_op jit(solution)/shard_map/ppermute | solution.py:503
  75.2 6.4 %collective-permute-start.23 = (bf16[64,512]{1,0:T(8,128)(2,1)S(1)}, bf16[64,512]{1,0:T(8,128)(2,1)S(1)}, u32[]{:S(2)}, u32[]{:S(2)}) collective-permute-start(bf16[64,512]{1,0:T(8,128)(2,1)S(1)} %get-tuple-element.48), channel_id=1, source_target_pairs={{0,6},{1,7},{2,0},{3,1},{4,2},{5,3},{6,4},{7,5},{8,14},{9,15},{10,... | collective-permute-start | bytes 196616 | tf_op jit(solution)/shard_map/ppermute | solution.py:503
  81.6 16.3 %collective-permute-start.24 = (bf16[64,1024]{1,0:T(8,128)(2,1)S(1)}, bf16[64,1024]{1,0:T(8,128)(2,1)S(1)}, u32[]{:S(2)}, u32[]{:S(2)}) collective-permute-start(bf16[64,1024]{1,0:T(8,128)(2,1)S(1)} %get-tuple-element.49), channel_id=1, source_target_pairs={{0,2},{1,3},{2,4},{3,5},{4,6},{5,7},{6,0},{7,1},{8,10},{9,11},{10,... | collective-permute-start | bytes 393224 | tf_op jit(solution)/shard_map/ppermute | solution.py:503
  84.7 13.2 %collective-permute-start.25 = (bf16[64,1024]{1,0:T(8,128)(2,1)S(1)}, bf16[64,1024]{1,0:T(8,128)(2,1)S(1)}, u32[]{:S(2)}, u32[]{:S(2)}) collective-permute-start(bf16[64,1024]{1,0:T(8,128)(2,1)S(1)} %get-tuple-element.50), channel_id=1, source_target_pairs={{0,6},{1,7},{2,0},{3,1},{4,2},{5,3},{6,4},{7,5},{8,14},{9,15},{10,... | collective-permute-start | bytes 393224 | tf_op jit(solution)/shard_map/ppermute | solution.py:503
  85.3 19.2 %collective-permute-start.27 = (bf16[4,16,128]{2,1,0:T(8,128)(2,1)S(1)}, bf16[4,16,128]{2,1,0:T(8,128)(2,1)S(1)}, u32[]{:S(2)}, u32[]{:S(2)}) collective-permute-start(bf16[4,16,128]{2,1,0:T(8,128)(2,1)S(1)} %pad_maximum_fusion.3), channel_id=1, source_target_pairs={{0,8},{8,0},{16,24},{24,16},{32,40},{40,32},{48,56},{56,48},{64,72... | collective-permute-start | bytes 49160 | tf_op jit(solution)/shard_map/ppermute | solution.py:482
  98.0 7.4 %collective-permute-start.26 = (bf16[64,512]{1,0:T(8,128)(2,1)S(1)}, bf16[64,512]{1,0:T(8,128)(2,1)S(1)}, u32[]{:S(2)}, u32[]{:S(2)}) collective-permute-start(bf16[64,512]{1,0:T(8,128)(2,1)S(1)} %get-tuple-element.52), channel_id=1, source_target_pairs={{0,8},{8,0},{16,24},{24,16},{32,40},{40,32},{48,56},{56,48},{64,72... | collective-permute-start | bytes 196616 | tf_op jit(solution)/shard_map/ppermute | solution.py:482

commit v3 on v2

v3 whole, which is shorter than its diff:
```python
import jax
import jax.numpy as jnp
from jax import lax
from jax.experimental import pallas as pl
from jax.experimental.pallas import tpu as pltpu
from jax.sharding import PartitionSpec as P

DH = 128
GROUP = 16
SCALE = DH**-0.5
LOG2E = 1.4426950408889634
BATCH = 32
HEADS = 8
VMEM = pl.BlockSpec(memory_space=pltpu.VMEM)
SMEM = pl.BlockSpec(memory_space=pltpu.SMEM)
F32 = jnp.float32
BF16 = jnp.bfloat16
NT = (((1,), (1,)), ((), ()))
NN = (((1,), (0,)), ((), ()))


ANY = pl.BlockSpec(memory_space=pl.ANY)


def params(mib=16):
    return pltpu.CompilerParams(vmem_limit_bytes=mib * 1024 * 1024)


def dot(a, b, dims=NN):
    return lax.dot_general(a, b, dims, preferred_element_type=F32)


def lanes():
    return lax.broadcasted_iota(jnp.int32, (GROUP, DH), 1)


def split_tile(tile, step):
    high = tile.astype(BF16).astype(F32)
    rest = tile - high
    middle = rest.astype(BF16).astype(F32)
    low = rest - middle
    joined = high + pltpu.roll(middle, step, 1) + pltpu.roll(low, 2 * step, 1)
    return joined.astype(BF16)


def join_tile(tile, step):
    wide = tile.astype(F32)
    return (wide + pltpu.roll(wide, DH - step, 1)) + pltpu.roll(wide, DH - 2 * step, 1)


def local_body(
    place, q_in, prompt_in, table_in, length_in, new_in, pool_in, o0, o1, o2, o3,
    q, prompt, table, length, new, pool, wide, scores, weights, slots, sems,
):
    pairs = [
        (q_in, q),
        (prompt_in, prompt),
        (table_in, table),
        (length_in, length),
        (new_in, new),
        (pool_in.at[0], pool.at[0]),
        (pool_in.at[1], pool.at[1]),
    ]
    copies = [pltpu.make_async_copy(a, b, sems.at[i]) for i, (a, b) in enumerate(pairs)]
    for copy in copies:
        copy.start()
    outs = (o0, o1, o2, o3)
    lane = lanes()
    copies[0].wait()
    for h in range(GROUP):
        wide[:, h, :] = q[:, h * DH : (h + 1) * DH].astype(F32)
    copies[1].wait()
    for p in range(8):
        slots[32 + p] = 0
    order = jnp.zeros((GROUP, DH), F32)
    for n in range(32):
        p = prompt[n]
        k = slots[32 + p]
        slots[32 + p] = k + 1
        slots[n] = (4 * p + k) ^ place[0]
        order = jnp.where(lane == n, (4 * p + k).astype(F32), order)
    for copy in copies[2:6]:
        copy.wait()
    base = place[1]
    for n in range(32):
        keys = jnp.concatenate([pool[0, table[n, j] - base] for j in range(8)], axis=0)
        s = dot(wide[n].astype(BF16), keys, NT) * SCALE
        scores[n] = jnp.where(lane < length[n], s, -1e30)
    own_keys = new[0].astype(F32)
    own_values = new[1].astype(F32)
    own = jnp.stack(
        [jnp.sum(wide[n] * own_keys[n : n + 1], axis=1, keepdims=True) for n in range(32)]
    ) * SCALE
    s = scores[...]
    peak = jnp.maximum(jnp.max(s, axis=2, keepdims=True), own)
    w = jnp.exp(s - peak)
    own_weight = jnp.exp(own - peak)
    total = jnp.sum(w, axis=2, keepdims=True) + own_weight
    weights[...] = w.astype(BF16)
    own_weight = own_weight.astype(BF16).astype(F32)
    mass = peak + jnp.log(total)
    inverse = 1.0 / total
    copies[6].wait()
    for n in range(32):
        values = jnp.concatenate([pool[1, table[n, j] - base] for j in range(8)], axis=0)
        mixed = dot(weights[n], values) + own_weight[n] * own_values[n : n + 1]
        scores[slots[n]] = mixed * inverse[n]
    held = [jnp.zeros((GROUP, DH), F32) for _ in range(4)]
    for n in range(32):
        slot = slots[n]
        weights[slot] = wide[n].astype(BF16)
        for i in range(4):
            held[i] = jnp.where(lane + 8 * i == slot, jnp.where(lane < 8, mass[n], 0.0), held[i])
    for i, out in enumerate(outs):
        out[0:8] = weights[8 * i : 8 * i + 8]
        out[8] = order.astype(BF16)
        out[9:17] = scores[8 * i : 8 * i + 8].astype(BF16)
        out[17] = split_tile(jnp.where(lane < 8, held[i], 0.0), 8)


def local_parts(place, q, prompt, table, length, new, pool):
    out = jax.ShapeDtypeStruct((18, GROUP, DH), BF16)
    return pl.pallas_call(
        local_body,
        out_shape=[out] * 4,
        in_specs=[SMEM] + [ANY] * 6,
        out_specs=[VMEM] * 4,
        scratch_shapes=[
            pltpu.VMEM((32, GROUP * DH), BF16),
            pltpu.SMEM((32,), jnp.int32),
            pltpu.SMEM((32, 8), jnp.int32),
            pltpu.SMEM((32,), jnp.int32),
            pltpu.VMEM((2, 32, DH), BF16),
            pltpu.VMEM((2, 256, GROUP, DH), BF16),
            pltpu.VMEM((32, GROUP, DH), F32),
            pltpu.VMEM((32, GROUP, DH), F32),
            pltpu.VMEM((32, GROUP, DH), BF16),
            pltpu.SMEM((40,), jnp.int32),
            pltpu.SemaphoreType.DMA((7,)),
        ],
        compiler_params=params(56),
        name="local_parts",
    )(place, q, prompt, table, length, new, pool)


def regroup_body(place, a0, a1, a2, a3, same, other, far):
    for i, a in enumerate((a0, a1, a2, a3)):
        same[4 * i : 4 * i + 4] = a[0:4]
        other[4 * i : 4 * i + 4] = a[4:8]
        far[5 * i : 5 * i + 5] = a[13:18]

        @pl.when(place[2] ^ (place[4] >> 1) == i)
        def _(a=a):
            same[16] = a[8]
            other[16] = a[8]


def regroup(place, parts):
    out = jax.ShapeDtypeStruct((17, GROUP, DH), BF16)
    return pl.pallas_call(
        regroup_body,
        out_shape=[out, out, jax.ShapeDtypeStruct((20, GROUP, DH), BF16)],
        in_specs=[SMEM] + [VMEM] * 4,
        out_specs=[VMEM] * 3,
        compiler_params=params(),
        name="regroup",
    )(place, *parts)


ROWS = 128


def prefix_part(q, kv):
    s = dot(q, kv[0], NT)
    peak = jnp.max(s, axis=1, keepdims=True)
    w = jnp.exp2((s - peak) * (SCALE * LOG2E))
    return dot(w.astype(BF16), kv[1]), peak * SCALE, jnp.sum(w, axis=1, keepdims=True)


def prefix_block(q, kv0, kv1):
    mixed0, peak0, total0 = prefix_part(q, kv0)
    mixed1, peak1, total1 = prefix_part(q, kv1)
    top = jnp.maximum(peak0, peak1)
    f0, f1 = jnp.exp(peak0 - top), jnp.exp(peak1 - top)
    total = total0 * f0 + total1 * f1
    return (mixed0 * f0 + mixed1 * f1) * (1.0 / total), top + jnp.log(total)


COUNT = ROWS // GROUP


def prefix_send_body(qa, qb, kv0, kv1, after, out):
    lane = lanes()
    tile = jnp.zeros((GROUP, DH), F32)
    for half, q in enumerate((qa, qb)):
        for i in range(256 // ROWS):
            rows = q[i * COUNT : (i + 1) * COUNT].reshape(ROWS, DH)
            mixed, mass = prefix_block(rows, kv0, kv1)
            at = half * 16 + i * COUNT
            out[at : at + COUNT] = mixed.reshape(COUNT, GROUP, DH).astype(BF16)
            for n in range(COUNT):
                tile = jnp.where(lane == at + n, mass[n * GROUP : (n + 1) * GROUP], tile)
    out[32] = split_tile(tile, 32)


def prefix_keep_body(q, kv0, kv1, out, masses):
    for i in range(256 // ROWS):
        rows = q[i * COUNT : (i + 1) * COUNT].reshape(ROWS, DH)
        mixed, mass = prefix_block(rows, kv0, kv1)
        at = i * COUNT
        out[at : at + COUNT] = mixed.reshape(COUNT, GROUP, DH)
        masses[at : at + COUNT] = jnp.broadcast_to(mass, (ROWS, DH)).reshape(COUNT, GROUP, DH)


def prefix_cost(rows):
    return pl.CostEstimate(
        flops=4 * rows * 4096 * 128, bytes_accessed=2_500_000, transcendentals=rows * 4096
    )


def prefix_send(qa, qb, kv0, kv1, after):
    return pl.pallas_call(
        prefix_send_body,
        out_shape=jax.ShapeDtypeStruct((33, GROUP, DH), BF16),
        in_specs=[VMEM] * 4 + [ANY],
        out_specs=VMEM,
        compiler_params=params(24),
        cost_estimate=prefix_cost(512),
        name="prefix_send",
    )(qa, qb, kv0, kv1, after)


def prefix_keep(q, kv0, kv1):
    out = jax.ShapeDtypeStruct((16, GROUP, DH), F32)
    return pl.pallas_call(
        prefix_keep_body,
        out_shape=[out, out],
        in_specs=[VMEM] * 3,
        out_specs=[VMEM, VMEM],
        compiler_params=params(24),
        cost_estimate=prefix_cost(256),
        name="prefix_keep",
    )(q, kv0, kv1)


def combine_body(
    place, own, own_masses, cross, cross_masses, message, s0, s1, s2, s3, far, out, held
):
    x, y_high, z = place[2], place[3], place[4]
    theirs = join_tile(message[32], 32)
    near = [join_tile(s[17], 8) for s in (s0, s1, s2, s3)]
    across = [join_tile(far[5 * i + 4], 8) for i in range(4)]
    for g in range(2):
        for kx in range(4):
            for k in range(4):
                n = g * 16 + kx * 4 + k
                at = kx * 4 + k
                a, la = ((own, own_masses), (cross, cross_masses))[g]
                a, la = a[at], la[at]
                b = message[n].astype(F32)
                lb = jnp.broadcast_to(theirs[:, n : n + 1], (GROUP, DH))
                if g == 0:
                    s = (s0, s1, s2, s3)[kx][9 + k].astype(F32)
                    ls = jnp.broadcast_to(near[kx][:, k : k + 1], (GROUP, DH))
                else:
                    s = far[5 * kx + k].astype(F32)
                    ls = jnp.broadcast_to(across[kx][:, 4 + k : 5 + k], (GROUP, DH))
                top = jnp.maximum(jnp.maximum(la, lb), ls)
                ea, eb, es = jnp.exp(la - top), jnp.exp(lb - top), jnp.exp(ls - top)
                row = (ea * a + eb * b + es * s) / (ea + eb + es)
                target = (x ^ kx) * 2 + (y_high ^ g)
                held[((target - z) & 7) * 4 + k] = row
    for h in range(GROUP):
        out[:, h * DH : (h + 1) * DH] = held[:, h, :].astype(BF16)


def combine(place, own, cross, message, near, far):
    return pl.pallas_call(
        combine_body,
        out_shape=jax.ShapeDtypeStruct((32, GROUP * DH), BF16),
        in_specs=[SMEM] + [VMEM] * 10,
        out_specs=VMEM,
        scratch_shapes=[pltpu.VMEM((32, GROUP, DH), F32)],
        compiler_params=params(),
        name="combine",
    )(place, *own, *cross, message, *near, far)


def by_target(total):
    low = lax.broadcasted_iota(jnp.int32, (8, total.shape[1]), 0) < 4
    chunks = []
    for g in range(4):
        even, odd = [], []
        for j in (0, 2):
            first = total[j * 32 + g * 8 : j * 32 + g * 8 + 8]
            second = total[(j + 1) * 32 + g * 8 : (j + 1) * 32 + g * 8 + 8]
            even.append(jnp.where(low, first, pltpu.roll(second, 4, 0)))
            odd.append(jnp.where(low, pltpu.roll(first, 4, 0), second))
        chunks += [jnp.concatenate(even, axis=0), jnp.concatenate(odd, axis=0)]
    return chunks


def project_body(count, *refs):
    blocks, weights, out = refs[:count], refs[count : count + 2], refs[count + 2]
    for i, block in enumerate(blocks):
        for side, weight in enumerate(weights):
            for d, chunk in enumerate(by_target(dot(block[...], weight[...]))):
                out[d, i * 16 : i * 16 + 16, side * 512 : side * 512 + 512] = chunk


def project(blocks, weights):
    count = len(blocks)
    return pl.pallas_call(
        lambda *refs: project_body(count, *refs),
        out_shape=jax.ShapeDtypeStruct((8, 16 * count, 1024), F32),
        in_specs=[VMEM] * (count + 2),
        out_specs=VMEM,
        compiler_params=params(),
        cost_estimate=pl.CostEstimate(
            flops=count * 2 * 128 * 2048 * 1024, bytes_accessed=4_500_000, transcendentals=0
        ),
        name="project",
    )(*blocks, *weights)


def last_body(block, w0, w1, first, second, up, down, keep):
    for side, weight in enumerate((w0, w1)):
        columns = slice(side * 512, side * 512 + 512)
        chunks = by_target(dot(block[...], weight[...]))
        for d, chunk in enumerate(chunks):
            whole = jnp.concatenate([first[d, :, columns], second[d, :, columns], chunk], axis=0)
            if d in (0, 3, 5):
                keep[(0, 3, 5).index(d), :, columns] = whole
            elif d in (1, 6):
                up[2 * (1, 6).index(d) + side] = whole.astype(BF16)
            elif d in (7, 2):
                down[2 * (7, 2).index(d) + side] = whole.astype(BF16)
            elif side == 0:
                up[4] = whole.astype(BF16)
            else:
                down[4] = whole.astype(BF16)


def project_last(block, weights, first, second):
    out = jax.ShapeDtypeStruct((5, 64, 512), BF16)
    return pl.pallas_call(
        last_body,
        out_shape=[out, out, jax.ShapeDtypeStruct((3, 64, 1024), F32)],
        in_specs=[VMEM] * 5,
        out_specs=[VMEM] * 3,
        compiler_params=params(),
        name="project_last",
    )(block, *weights, first, second)


def middle_body(keep, below, above, up, down):
    far = below[4].astype(F32), above[4].astype(F32)
    up[:, :512] = (keep[1, :, :512] + above[2].astype(F32) + far[0]).astype(BF16)
    up[:, 512:] = (keep[1, :, 512:] + above[3].astype(F32)).astype(BF16)
    down[:, :512] = (keep[2, :, :512] + below[2].astype(F32)).astype(BF16)
    down[:, 512:] = (keep[2, :, 512:] + below[3].astype(F32) + far[1]).astype(BF16)


def middle(keep, below, above):
    out = jax.ShapeDtypeStruct((64, 1024), BF16)
    return pl.pallas_call(
        middle_body,
        out_shape=[out, out],
        in_specs=[VMEM] * 3,
        out_specs=[VMEM] * 2,
        compiler_params=params(),
        name="middle",
    )(keep, below, above)


def total_body(keep, below, above, below3, above3, own, other):
    for side, out in enumerate((own, other)):
        columns = slice(side * 512, side * 512 + 512)
        near = keep[0, :, columns] + below[side].astype(F32) + above[side].astype(F32)
        far = below3[:, columns].astype(F32) + above3[:, columns].astype(F32)
        out[...] = (near + far).astype(BF16)


def total(keep, below, above, below3, above3):
    out = jax.ShapeDtypeStruct((64, 512), BF16)
    return pl.pallas_call(
        total_body,
        out_shape=[out, out],
        in_specs=[VMEM] * 5,
        out_specs=[VMEM] * 2,
        compiler_params=params(),
        name="total",
    )(keep, below, above, below3, above3)


def order_body(place, orders, pick):
    x, y, core, z = place[2], place[3] * 2 + place[5], place[6], place[4]
    lane = lanes()
    order = jnp.zeros((GROUP, DH), F32)
    for block in range(4):
        dy = (2 * (z & 1) + block // 2) ^ y
        tile = orders[((block % 2) ^ core) * 4 + dy].astype(F32)
        order = jnp.where(lane >> 5 == block, pltpu.roll(tile, 32 * block, 1), order)
    order = order.astype(jnp.int32)
    prompt, k = order >> 2, order & 3
    block = lane >> 5
    far = block & 1
    dx = (prompt >> 1) ^ x
    dy = (2 * (prompt & 1) + (block >> 1)) ^ y
    first = jnp.where(far == 0, dx, dy)
    second = jnp.where(far == 0, dy, dx)
    first = jnp.where(first >= 2, 5 - first, first)
    second = jnp.where(second >= 2, 5 - second, second)
    source = ((far ^ core) * 16 + second * 4 + first) * 4 + k
    row = lax.broadcasted_iota(jnp.int32, (128, 128), 0)
    pick[...] = (row == source[0:1]).astype(F32).astype(BF16)


def order_rows(place, orders):
    return pl.pallas_call(
        order_body,
        out_shape=jax.ShapeDtypeStruct((128, 128), BF16),
        in_specs=[SMEM, VMEM],
        out_specs=VMEM,
        compiler_params=params(),
        name="order_rows",
    )(place, orders)


def finish_body(own, other, pick, out):
    dims = (((0,), (0,)), ((), ()))
    mixed = dot(pick[0:64], own[...], dims) + dot(pick[64:128], other[...], dims)
    out[...] = mixed.astype(BF16)


def finish(own, other, pick):
    return pl.pallas_call(
        finish_body,
        out_shape=jax.ShapeDtypeStruct((128, 512), BF16),
        in_specs=[VMEM] * 3,
        out_specs=VMEM,
        compiler_params=params(),
        name="finish",
    )(own, other, pick)


def along(value, shift, k):
    return lax.ppermute(value, "batch", [(i, i ^ (k << shift)) for i in range(BATCH)])


def along_x(value, k):
    return along(value, 3, k)


def along_y(value, k):
    return along(value, 1, k)


def other_core(value):
    return along(value, 0, 1)


def turned(value, k, phase):
    pairs = [(i, i ^ (k << (3 if (i & 1) == phase else 1))) for i in range(BATCH)]
    return lax.ppermute(value, "batch", pairs)


def along_z(value, k):
    return lax.ppermute(value, "head", [(i, (i + k) % HEADS) for i in range(HEADS)])


def shards(queries, new_kv, prefix_kv, suffix_kv, page_table, suffix_len, prompt_of, out_weight):
    me = lax.axis_index("batch")
    z = lax.axis_index("head")
    x, y, core = me // 8, (me // 2) % 4, me % 2
    place = [8 * x + 4 * (y // 2), me * 256, x, y // 2, z, y % 2, core]
    place = jnp.stack(place).astype(jnp.int32)

    prefix_other = other_core(prefix_kv)
    weights = [out_weight, other_core(out_weight)]

    sent = local_parts(place, queries, prompt_of, page_table, suffix_len, new_kv, suffix_kv)
    by_x = [sent[0]] + [along_x(sent[k], k) for k in (1, 2, 3)]
    same, other, far = regroup(place, by_x)
    from1, from3, from2 = along_y(same, 1), along_y(other, 3), along_y(other, 2)
    far = along_y(far, 2)

    own = prefix_keep(same, prefix_kv, prefix_other)
    message = along_y(prefix_send(from1, from3, prefix_kv, prefix_other, own[1]), 1)
    cross = prefix_keep(from2, prefix_kv, prefix_other)
    attended = combine(place, own, cross, message, by_x, far)

    orders = jnp.stack([same[16], from1[16], from2[16], from3[16]])
    orders = jnp.concatenate([orders, other_core(orders)], axis=0)
    pick = order_rows(place, orders)

    pair = jnp.concatenate([attended, turned(attended, 1, 0)], axis=0)
    ring0 = jnp.concatenate([pair, turned(pair, 3, 0)], axis=0)
    ring1, ring3 = turned(ring0, 1, 1), turned(ring0, 3, 1)
    ring2 = jnp.concatenate([turned(ring3[:64], 1, 1), turned(ring1[64:], 3, 1)], axis=0)
    first = project([ring0], weights)
    second = project([ring1, ring3], weights)
    up, down, keep = project_last(ring2, weights, first, second)

    below, above = along_z(up, 1), along_z(down, -1)
    up3, down3 = middle(keep, below, above)
    below3, above3 = along_z(up3, 3), along_z(down3, -3)
    own, other = total(keep, below, above, below3, above3)
    return finish(own, other_core(other), pick)


def solution(mesh):
    placed = (
        P("batch", "head"),
        P(None, "batch", "head"),
        P(None, "batch", "head"),
        P(None, "batch", None, "head"),
        P("batch", None),
        P("batch"),
        P("batch"),
        P("head", "batch"),
    )
    return jax.shard_map(
        shards, mesh=mesh, in_specs=placed, out_specs=P("head", "batch"), check_vma=False
    )
```

time: 107 us -> 108 us (level)
  the two profiles are of different devices: /device:TPU:1 before, /device:TPU:33 now
where the time goes in v3:
time: 108 us
  starting transfers between devices  50.4 us (47%)
  waiting for transfers between devices  31.9 us (30%)
  Pallas kernels  22.6 us (21%)
  local copies, waits for them, and re-layouts  2.94 us (3%)
    ppermute x12, starting transfers between devices, along(): lax.ppermute(value, 'batch', [(i, i ^ k << shift) for i in range(BATCH)])  37.7 us
    ppermute x6, waiting for transfers between devices, turned(): return lax.ppermute(value, 'batch', pairs)  18.7 us
    ppermute x12, waiting for transfers between devices, along(): lax.ppermute(value, 'batch', [(i, i ^ k << shift) for i in range(BATCH)])  6.89 us
    pallas_call x2, Pallas kernels, prefix_keep(): pl.pallas_call(prefix_keep_body, out_shape=[out, out], in_specs=[VMEM] *...  6.8 us
    ppermute x4, starting transfers between devices, along_z(): lax.ppermute(value, 'head', [(i, (i + k) % HEADS) for i in range(HEADS)])  6.46 us
    ppermute x4, waiting for transfers between devices, along_z(): lax.ppermute(value, 'head', [(i, (i + k) % HEADS) for i in range(HEADS)])  6.38 us
    ppermute x6, starting transfers between devices, turned(): return lax.ppermute(value, 'batch', pairs)  6.25 us
    pallas_call x1, Pallas kernels, prefix_send(): pl.pallas_call(prefix_send_body, out_shape=jax.ShapeDtypeStruct((33, GROU...  5.36 us
  transfers between devices with their start and end apart: 22, of which 12 were waited for; matrix products, arithmetic and copies ran while one was open for 2% of the time, Pallas kernels for 19%

profile of v3, /device:TPU:33, one launch (start us, length us, event | category | flops | bytes accessed | tf_op | source)
XLA Modules:
  0.0 108.1 jit_solution(8064239974753767175)
XLA Ops:
  0.0 0.7 collective-permute-start.3
  0.7 0.1 collective-permute-start.15
  0.8 1.4 %copy.9.table_in = s32[32,8]{1,0:T(8,128)} copy(s32[32,8]{0,1:T(8,128)} %param.12) | data formatting | bytes 2048 | tf_op args[4]
  2.1 0.6 stack.34.place
  2.7 4.2 %local_parts.1 = (bf16[18,16,128]{2,1,0:T(8,128)(2,1)}, bf16[18,16,128]{2,1,0:T(8,128)(2,1)}, bf16[18,16,128]{2,1,0:T(8,128)(2,1)}, bf16[18,16,128]{2,1,0:T(8,128)(2,1)}) custom-call(s32[7]{0:T(128)} %stack.34.place, bf16[32,2048]{1,0:T(8,128)(2,1)} %q_in.1, s32[32]{0:T(128)} %prompt_in.1, s32[32,8]{1,0:T(8,128)} %copy.9.table_in, s32[32]{0:T(128)} %length_in.1, ...), custom_call_target="tpu_custom_call" | custom-call | tf_op jit(solution)/shard_map/local_parts/pallas_call | solution.py:123
  7.0 1.3 %collective-permute-start = (bf16[18,16,128]{2,1,0:T(8,128)(2,1)}, bf16[18,16,128]{2,1,0:T(8,128)(2,1)S(1)}, u32[]{:S(2)}, u32[]{:S(2)}) collective-permute-start(bf16[18,16,128]{2,1,0:T(8,128)(2,1)} %get-tuple-element.24), channel_id=1, source_target_pairs={{0,64},{8,72},{16,80},{24,88},{32,96},{40,104},{48,112},{56,120},{... | collective-permute-start | bytes 221192 | tf_op jit(solution)/shard_map/ppermute | solution.py:448
  8.3 2.4 %collective-permute-start.1 = (bf16[18,16,128]{2,1,0:T(8,128)(2,1)}, bf16[18,16,128]{2,1,0:T(8,128)(2,1)S(1)}, u32[]{:S(2)}, u32[]{:S(2)}) collective-permute-start(bf16[18,16,128]{2,1,0:T(8,128)(2,1)} %get-tuple-element.25), channel_id=1, source_target_pairs={{0,128},{8,136},{16,144},{24,152},{32,160},{40,168},{48,176},{56,1... | collective-permute-start | bytes 221192 | tf_op jit(solution)/shard_map/ppermute | solution.py:448
  10.7 0.2 collective-permute-start.2
  10.9 0.0 collective-permute-done.a1.s1
  10.9 3.2 %collective-permute-done.1.a2.s2 = bf16[18,16,128]{2,1,0:T(8,128)(2,1)S(1)} collective-permute-done((bf16[18,16,128]{2,1,0:T(8,128)(2,1)}, bf16[18,16,128]{2,1,0:T(8,128)(2,1)S(1)}, u32[]{:S(2)}, u32[]{:S(2)}) %collective-permute-start.1) | collective-permute-done | bytes 73760 | tf_op jit(solution)/shard_map/ppermute | solution.py:448
  14.1 1.7 %collective-permute-done.2.a3.s3 = bf16[18,16,128]{2,1,0:T(8,128)(2,1)S(1)} collective-permute-done((bf16[18,16,128]{2,1,0:T(8,128)(2,1)}, bf16[18,16,128]{2,1,0:T(8,128)(2,1)S(1)}, u32[]{:S(2)}, u32[]{:S(2)}) %collective-permute-start.2) | collective-permute-done | bytes 73760 | tf_op jit(solution)/shard_map/ppermute | solution.py:448
  15.8 0.0 copy-done.4
  15.8 0.9 copy-done.2
  16.7 0.6 regroup.1
  17.3 2.8 %collective-permute-start.6 = (bf16[17,16,128]{2,1,0:T(8,128)(2,1)S(1)}, bf16[17,16,128]{2,1,0:T(8,128)(2,1)S(1)}, u32[]{:S(2)}, u32[]{:S(2)}) collective-permute-start(bf16[17,16,128]{2,1,0:T(8,128)(2,1)S(1)} %get-tuple-element.30), channel_id=1, source_target_pairs={{0,48},{8,56},{16,32},{24,40},{32,16},{40,24},{48,0},{56,8},{64,11... | collective-permute-start | bytes 208904 | tf_op jit(solution)/shard_map/ppermute | solution.py:448
  20.1 0.0 collective-permute-start.5
  20.1 0.0 collective-permute-done.3.kv1
  20.1 0.0 copy-done.1
  20.1 3.4 %prefix_keep.2 = (f32[16,16,128]{2,1,0:T(8,128)S(1)}, f32[16,16,128]{2,1,0:T(8,128)S(1)}) custom-call(bf16[17,16,128]{2,1,0:T(8,128)(2,1)S(1)} %get-tuple-element.27.q, bf16[2,2048,128]{2,1,0:T(8,128)(2,1)S(1)} %copy-done.1, bf16[2,2048,128]{2,1,0:T(8,128)(2,1)} %collective-permute-done.3.kv1), custom_call_target="tpu_custom_call" | custom-call | flops 536870912 | bytes 2500000 | tf_op jit(solution)/shard_map/prefix_keep/pallas_call | solution.py:235
  23.5 0.0 collective-permute-done.6.qb
  23.5 0.0 collective-permute-done.5.qa
  23.6 5.4 %prefix_send.1 = bf16[33,16,128]{2,1,0:T(8,128)(2,1)S(1)} custom-call(bf16[17,16,128]{2,1,0:T(8,128)(2,1)S(1)} %collective-permute-done.5.qa, bf16[17,16,128]{2,1,0:T(8,128)(2,1)S(1)} %collective-permute-done.6.qb, bf16[2,2048,128]{2,1,0:T(8,128)(2,1)S(1)} %copy-done.1, bf16[2,2048,128]{2,1,0:T(8,128)(2,1)} %collective-permute-done.3.kv1, ...), custom_call_target="tpu_custom_call" | custom-call | flops 1073741824 | bytes 2500000 | tf_op jit(solution)/shard_map/prefix_send/pallas_call | solution.py:222
  28.9 1.6 %collective-permute-start.7 = (bf16[33,16,128]{2,1,0:T(8,128)(2,1)S(1)}, bf16[33,16,128]{2,1,0:T(8,128)(2,1)S(1)}, u32[]{:S(2)}, u32[]{:S(2)}) collective-permute-start(bf16[33,16,128]{2,1,0:T(8,128)(2,1)S(1)} %prefix_send.1), channel_id=1, source_target_pairs={{0,16},{8,24},{16,0},{24,8},{32,48},{40,56},{48,32},{56,40},{64,80... | collective-permute-start | bytes 405512 | tf_op jit(solution)/shard_map/ppermute | solution.py:448
  30.5 0.6 collective-permute-start.4
  31.1 2.3 %collective-permute-start.8 = (bf16[20,16,128]{2,1,0:T(8,128)(2,1)S(1)}, bf16[20,16,128]{2,1,0:T(8,128)(2,1)S(1)}, u32[]{:S(2)}, u32[]{:S(2)}) collective-permute-start(bf16[20,16,128]{2,1,0:T(8,128)(2,1)S(1)} %get-tuple-element.33), channel_id=1, source_target_pairs={{0,32},{8,40},{16,48},{24,56},{32,0},{40,8},{48,16},{56,24},{64,96... | collective-permute-start | bytes 245768 | tf_op jit(solution)/shard_map/ppermute | solution.py:448
  33.5 1.7 %collective-permute-done.4.q = bf16[17,16,128]{2,1,0:T(8,128)(2,1)S(1)} collective-permute-done((bf16[17,16,128]{2,1,0:T(8,128)(2,1)S(1)}, bf16[17,16,128]{2,1,0:T(8,128)(2,1)S(1)}, u32[]{:S(2)}, u32[]{:S(2)}) %collective-permute-start.4) | collective-permute-done | bytes 69664 | tf_op jit(solution)/shard_map/ppermute | solution.py:448
  35.1 3.4 %prefix_keep.3 = (f32[16,16,128]{2,1,0:T(8,128)S(1)}, f32[16,16,128]{2,1,0:T(8,128)S(1)}) custom-call(bf16[17,16,128]{2,1,0:T(8,128)(2,1)S(1)} %collective-permute-done.4.q, bf16[2,2048,128]{2,1,0:T(8,128)(2,1)S(1)} %copy-done.1, bf16[2,2048,128]{2,1,0:T(8,128)(2,1)} %collective-permute-done.3.kv1), custom_call_target="tpu_custom_call" | custom-call | flops 536870912 | bytes 2500000 | tf_op jit(solution)/shard_map/prefix_keep/pallas_call | solution.py:235
  38.6 0.0 copy-start
  38.6 0.0 collective-permute-done.8.far
  38.6 0.0 collective-permute-done.7.message
  38.6 0.0 copy-done.3
  38.6 1.2 %combine.1 = bf16[32,2048]{1,0:T(8,128)(2,1)S(1)} custom-call(s32[7]{0:T(128)S(1)} %copy-done.4, f32[16,16,128]{2,1,0:T(8,128)S(1)} %get-tuple-element.28.own, f32[16,16,128]{2,1,0:T(8,128)S(1)} %get-tuple-element.29.after.own_masses, f32[16,16,128]{2,1,0:T(8,128)S(1)} %get-tuple-element.31.cross, f32[16,16,128]{2,1,0:T(8,128)S(1)} %get-tuple-element.32.cross_masses, ...), custom_call_target="tpu_custom_call" | custom-call | tf_op jit(solution)/shard_map/combine/pallas_call | solution.py:278
  39.8 1.1 %collective-permute-start.9 = (bf16[32,2048]{1,0:T(8,128)(2,1)S(1)}, bf16[32,2048]{1,0:T(8,128)(2,1)S(1)}, u32[]{:S(2)}, u32[]{:S(2)}) collective-permute-start(bf16[32,2048]{1,0:T(8,128)(2,1)S(1)} %combine.1), channel_id=1, source_target_pairs={{0,64},{8,24},{16,80},{24,8},{32,96},{40,56},{48,112},{56,40},{64,... | collective-permute-start | bytes 393224 | tf_op jit(solution)/shard_map/ppermute | solution.py:465
  40.9 2.8 %collective-permute-done.9 = bf16[32,2048]{1,0:T(8,128)(2,1)S(1)} collective-permute-done((bf16[32,2048]{1,0:T(8,128)(2,1)S(1)}, bf16[32,2048]{1,0:T(8,128)(2,1)S(1)}, u32[]{:S(2)}, u32[]{:S(2)}) %collective-permute-start.9) | collective-permute-done | bytes 131104 | tf_op jit(solution)/shard_map/ppermute | solution.py:465
  43.7 1.0 collective-permute-start.10
  44.7 5.6 %collective-permute-done.10 = bf16[64,2048]{1,0:T(8,128)(2,1)S(1)} collective-permute-done((bf16[64,2048]{1,0:T(8,128)(2,1)S(1)}, bf16[64,2048]{1,0:T(8,128)(2,1)S(1)}, u32[]{:S(2)}, u32[]{:S(2)}) %collective-permute-start.10) | collective-permute-done | bytes 262176 | tf_op jit(solution)/shard_map/ppermute | solution.py:465
  50.3 0.4 collective-permute-start.13
  50.7 1.7 %collective-permute-start.11 = (bf16[128,2048]{1,0:T(8,128)(2,1)S(1)}, bf16[128,2048]{1,0:T(8,128)(2,1)S(1)}, u32[]{:S(2)}, u32[]{:S(2)}) collective-permute-start(bf16[128,2048]{1,0:T(8,128)(2,1)S(1)} %pad_maximum_fusion.refs_0_), channel_id=1, source_target_pairs={{0,48},{8,200},{16,32},{24,216},{32,16},{40,232},{48,0},{56,248},{... | collective-permute-start | bytes 1572872 | tf_op jit(solution)/shard_map/ppermute | solution.py:465
  52.4 6.0 %collective-permute-done.13.refs_0_ = bf16[128,2048]{1,0:T(8,128)(2,1)S(1)} collective-permute-done((bf16[128,2048]{1,0:T(8,128)(2,1)S(1)}, bf16[128,2048]{1,0:T(8,128)(2,1)S(1)}, u32[]{:S(2)}, u32[]{:S(2)}) %collective-permute-start.13) | collective-permute-done | bytes 524320 | tf_op jit(solution)/shard_map/ppermute | solution.py:465
  58.4 2.0 %collective-permute-start.14 = (bf16[64,2048]{1,0:T(8,128)(2,1)S(1)}, bf16[64,2048]{1,0:T(8,128)(2,1)S(1)}, u32[]{:S(2)}, u32[]{:S(2)}) collective-permute-start(bf16[64,2048]{1,0:T(8,128)(2,1)S(1)} %slice.25), channel_id=1, source_target_pairs={{0,48},{8,200},{16,32},{24,216},{32,16},{40,232},{48,0},{56,248},{... | collective-permute-start | bytes 786440 | tf_op jit(solution)/shard_map/ppermute | solution.py:465
  60.4 0.8 collective-permute-done.11.refs_1_
  61.3 0.1 collective-permute-start.12
  61.4 0.0 collective-permute-done.15.refs_2_.refs_3_.w1
  61.4 0.7 project.2.first
  62.1 1.3 %project.3.second = f32[8,32,1024]{2,1,0:T(8,128)S(1)} custom-call(bf16[128,2048]{1,0:T(8,128)(2,1)S(1)} %collective-permute-done.13.refs_0_, bf16[128,2048]{1,0:T(8,128)(2,1)S(1)} %collective-permute-done.11.refs_1_, bf16[2048,512]{1,0:T(8,128)(2,1)S(1)} %copy-done, bf16[2048,512]{1,0:T(8,128)(2,1)S(1)} %collective-permute-done.15.refs_2_.refs_3_.w1), custom_call_target="tpu_custom_call" | custom-call | flops 1073741824 | bytes 4500000 | tf_op jit(solution)/shard_map/project/pallas_call | solution.py:313
  63.4 1.8 %collective-permute-done.14 = bf16[64,2048]{1,0:T(8,128)(2,1)S(1)} collective-permute-done((bf16[64,2048]{1,0:T(8,128)(2,1)S(1)}, bf16[64,2048]{1,0:T(8,128)(2,1)S(1)}, u32[]{:S(2)}, u32[]{:S(2)}) %collective-permute-start.14) | collective-permute-done | bytes 262176 | tf_op jit(solution)/shard_map/ppermute | solution.py:465
  65.2 1.6 %collective-permute-done.12 = bf16[64,2048]{1,0:T(8,128)(2,1)S(1)} collective-permute-done((bf16[64,2048]{1,0:T(8,128)(2,1)S(1)}, bf16[64,2048]{1,0:T(8,128)(2,1)S(1)}, u32[]{:S(2)}, u32[]{:S(2)}) %collective-permute-start.12) | collective-permute-done | bytes 262176 | tf_op jit(solution)/shard_map/ppermute | solution.py:465
  66.9 0.7 project_last.1
  67.7 1.7 %collective-permute-start.16 = (bf16[5,64,512]{2,1,0:T(8,128)(2,1)S(1)}, bf16[5,64,512]{2,1,0:T(8,128)(2,1)S(1)}, u32[]{:S(2)}, u32[]{:S(2)}) collective-permute-start(bf16[5,64,512]{2,1,0:T(8,128)(2,1)S(1)} %get-tuple-element.35), channel_id=1, source_target_pairs={{0,1},{1,2},{2,3},{3,4},{4,5},{5,6},{6,7},{7,0},{8,9},{9,10},{10,1... | collective-permute-start | bytes 983048 | tf_op jit(solution)/shard_map/ppermute | solution.py:469
  69.4 0.0 collective-permute-start.17
  69.4 4.6 %collective-permute-done.16.below = bf16[5,64,512]{2,1,0:T(8,128)(2,1)S(1)} collective-permute-done((bf16[5,64,512]{2,1,0:T(8,128)(2,1)S(1)}, bf16[5,64,512]{2,1,0:T(8,128)(2,1)S(1)}, u32[]{:S(2)}, u32[]{:S(2)}) %collective-permute-start.16) | collective-permute-done | bytes 327712 | tf_op jit(solution)/shard_map/ppermute | solution.py:469
  74.0 1.8 %collective-permute-done.17.above = bf16[5,64,512]{2,1,0:T(8,128)(2,1)S(1)} collective-permute-done((bf16[5,64,512]{2,1,0:T(8,128)(2,1)S(1)}, bf16[5,64,512]{2,1,0:T(8,128)(2,1)S(1)}, u32[]{:S(2)}, u32[]{:S(2)}) %collective-permute-start.17) | collective-permute-done | bytes 327712 | tf_op jit(solution)/shard_map/ppermute | solution.py:469
  75.8 0.1 middle.1
  75.8 4.8 %collective-permute-start.18 = (bf16[64,1024]{1,0:T(8,128)(2,1)S(1)}, bf16[64,1024]{1,0:T(8,128)(2,1)S(1)}, u32[]{:S(2)}, u32[]{:S(2)}) collective-permute-start(bf16[64,1024]{1,0:T(8,128)(2,1)S(1)} %get-tuple-element.37), channel_id=1, source_target_pairs={{0,3},{1,4},{2,5},{3,6},{4,7},{5,0},{6,1},{7,2},{8,11},{9,12},{10,... | collective-permute-start | bytes 393224 | tf_op jit(solution)/shard_map/ppermute | solution.py:469
  80.6 0.0 collective-permute-start.19
  80.6 15.7 %collective-permute-start.21 = (bf16[4,16,128]{2,1,0:T(8,128)(2,1)S(1)}, bf16[4,16,128]{2,1,0:T(8,128)(2,1)S(1)}, u32[]{:S(2)}, u32[]{:S(2)}) collective-permute-start(bf16[4,16,128]{2,1,0:T(8,128)(2,1)S(1)} %pad_maximum_fusion.3), channel_id=1, source_target_pairs={{0,8},{8,0},{16,24},{24,16},{32,40},{40,32},{48,56},{56,48},{64,72... | collective-permute-start | bytes 49160 | tf_op jit(solution)/shard_map/ppermute | solution.py:448
  96.3 0.0 collective-permute-done.18.below3
  96.3 0.0 collective-permute-done.19.above3
  96.3 0.1 total.1
  96.4 9.9 %collective-permute-start.20 = (bf16[64,512]{1,0:T(8,128)(2,1)S(1)}, bf16[64,512]{1,0:T(8,128)(2,1)S(1)}, u32[]{:S(2)}, u32[]{:S(2)}) collective-permute-start(bf16[64,512]{1,0:T(8,128)(2,1)S(1)} %get-tuple-element.40), channel_id=1, source_target_pairs={{0,8},{8,0},{16,24},{24,16},{32,40},{40,32},{48,56},{56,48},{64,72... | collective-permute-start | bytes 196616 | tf_op jit(solution)/shard_map/ppermute | solution.py:448
  106.3 0.0 collective-permute-done.21
  106.3 0.6 order_rows.1.pick
  107.0 0.2 collective-permute-done.20.other
  107.2 0.9 finish.1
  (16 shorter events, 0.2 us)
Async XLA Ops:
  0.0 20.1 %copy-start.1 = (bf16[2,2048,128]{2,1,0:T(8,128)(2,1)S(1)}, bf16[2,2048,128]{2,1,0:T(8,128)(2,1)}, u32[]{:S(2)}) copy-start(bf16[2,2048,128]{2,1,0:T(8,128)(2,1)} %kv0.5) | copy-start | bytes 3145732
  0.0 20.1 %collective-permute-start.3 = (bf16[2,2048,128]{2,1,0:T(8,128)(2,1)}, bf16[2,2048,128]{2,1,0:T(8,128)(2,1)}, u32[]{:S(2)}, u32[]{:S(2)}) collective-permute-start(bf16[2,2048,128]{2,1,0:T(8,128)(2,1)} %kv0.5), channel_id=1, source_target_pairs={{0,8},{8,0},{16,24},{24,16},{32,40},{40,32},{48,56},{56,48},{64,72... | collective-permute-start | bytes 3145736 | tf_op jit(solution)/shard_map/ppermute | solution.py:448
  0.7 60.7 %collective-permute-start.15 = (bf16[2048,512]{1,0:T(8,128)(2,1)}, bf16[2048,512]{1,0:T(8,128)(2,1)S(1)}, u32[]{:S(2)}, u32[]{:S(2)}) collective-permute-start(bf16[2048,512]{1,0:T(8,128)(2,1)} %w0.1), channel_id=1, source_target_pairs={{0,8},{8,0},{16,24},{24,16},{32,40},{40,32},{48,56},{56,48},{64,72... | collective-permute-start | bytes 6291464 | tf_op jit(solution)/shard_map/ppermute | solution.py:448
  2.7 13.1 %copy-start.4 = (s32[7]{0:T(128)S(1)}, s32[7]{0:T(128)}, u32[]{:S(2)}) copy-start(s32[7]{0:T(128)} %stack.34.place) | copy-start | bytes 88
  7.0 3.9 %collective-permute-start = (bf16[18,16,128]{2,1,0:T(8,128)(2,1)}, bf16[18,16,128]{2,1,0:T(8,128)(2,1)S(1)}, u32[]{:S(2)}, u32[]{:S(2)}) collective-permute-start(bf16[18,16,128]{2,1,0:T(8,128)(2,1)} %get-tuple-element.24), channel_id=1, source_target_pairs={{0,64},{8,72},{16,80},{24,88},{32,96},{40,104},{48,112},{56,120},{... | collective-permute-start | bytes 221192 | tf_op jit(solution)/shard_map/ppermute | solution.py:448
  8.3 5.9 %collective-permute-start.1 = (bf16[18,16,128]{2,1,0:T(8,128)(2,1)}, bf16[18,16,128]{2,1,0:T(8,128)(2,1)S(1)}, u32[]{:S(2)}, u32[]{:S(2)}) collective-permute-start(bf16[18,16,128]{2,1,0:T(8,128)(2,1)} %get-tuple-element.25), channel_id=1, source_target_pairs={{0,128},{8,136},{16,144},{24,152},{32,160},{40,168},{48,176},{56,1... | collective-permute-start | bytes 221192 | tf_op jit(solution)/shard_map/ppermute | solution.py:448
  10.7 5.1 %collective-permute-start.2 = (bf16[18,16,128]{2,1,0:T(8,128)(2,1)}, bf16[18,16,128]{2,1,0:T(8,128)(2,1)S(1)}, u32[]{:S(2)}, u32[]{:S(2)}) collective-permute-start(bf16[18,16,128]{2,1,0:T(8,128)(2,1)} %get-tuple-element.26), channel_id=1, source_target_pairs={{0,192},{8,200},{16,208},{24,216},{32,224},{40,232},{48,240},{56,2... | collective-permute-start | bytes 221192 | tf_op jit(solution)/shard_map/ppermute | solution.py:448
  15.8 0.9 copy-start.2
  17.3 6.2 %collective-permute-start.6 = (bf16[17,16,128]{2,1,0:T(8,128)(2,1)S(1)}, bf16[17,16,128]{2,1,0:T(8,128)(2,1)S(1)}, u32[]{:S(2)}, u32[]{:S(2)}) collective-permute-start(bf16[17,16,128]{2,1,0:T(8,128)(2,1)S(1)} %get-tuple-element.30), channel_id=1, source_target_pairs={{0,48},{8,56},{16,32},{24,40},{32,16},{40,24},{48,0},{56,8},{64,11... | collective-permute-start | bytes 208904 | tf_op jit(solution)/shard_map/ppermute | solution.py:448
  20.1 3.5 %collective-permute-start.5 = (bf16[17,16,128]{2,1,0:T(8,128)(2,1)S(1)}, bf16[17,16,128]{2,1,0:T(8,128)(2,1)S(1)}, u32[]{:S(2)}, u32[]{:S(2)}) collective-permute-start(bf16[17,16,128]{2,1,0:T(8,128)(2,1)S(1)} %get-tuple-element.27.q), channel_id=1, source_target_pairs={{0,16},{8,24},{16,0},{24,8},{32,48},{40,56},{48,32},{56,40},{64,80... | collective-permute-start | bytes 208904 | tf_op jit(solution)/shard_map/ppermute | solution.py:448
  23.6 15.0 %copy-start.3 = (bf16[18,16,128]{2,1,0:T(8,128)(2,1)S(1)}, bf16[18,16,128]{2,1,0:T(8,128)(2,1)}, u32[]{:S(2)}) copy-start(bf16[18,16,128]{2,1,0:T(8,128)(2,1)} %get-tuple-element.23.a0.s0) | copy-start | bytes 221188
  28.9 9.7 %collective-permute-start.7 = (bf16[33,16,128]{2,1,0:T(8,128)(2,1)S(1)}, bf16[33,16,128]{2,1,0:T(8,128)(2,1)S(1)}, u32[]{:S(2)}, u32[]{:S(2)}) collective-permute-start(bf16[33,16,128]{2,1,0:T(8,128)(2,1)S(1)} %prefix_send.1), channel_id=1, source_target_pairs={{0,16},{8,24},{16,0},{24,8},{32,48},{40,56},{48,32},{56,40},{64,80... | collective-permute-start | bytes 405512 | tf_op jit(solution)/shard_map/ppermute | solution.py:448
  30.5 4.7 %collective-permute-start.4 = (bf16[17,16,128]{2,1,0:T(8,128)(2,1)S(1)}, bf16[17,16,128]{2,1,0:T(8,128)(2,1)S(1)}, u32[]{:S(2)}, u32[]{:S(2)}) collective-permute-start(bf16[17,16,128]{2,1,0:T(8,128)(2,1)S(1)} %get-tuple-element.30), channel_id=1, source_target_pairs={{0,32},{8,40},{16,48},{24,56},{32,0},{40,8},{48,16},{56,24},{64,96... | collective-permute-start | bytes 208904 | tf_op jit(solution)/shard_map/ppermute | solution.py:448
  31.1 7.5 %collective-permute-start.8 = (bf16[20,16,128]{2,1,0:T(8,128)(2,1)S(1)}, bf16[20,16,128]{2,1,0:T(8,128)(2,1)S(1)}, u32[]{:S(2)}, u32[]{:S(2)}) collective-permute-start(bf16[20,16,128]{2,1,0:T(8,128)(2,1)S(1)} %get-tuple-element.33), channel_id=1, source_target_pairs={{0,32},{8,40},{16,48},{24,56},{32,0},{40,8},{48,16},{56,24},{64,96... | collective-permute-start | bytes 245768 | tf_op jit(solution)/shard_map/ppermute | solution.py:448
  38.6 22.8 %copy-start = (bf16[2048,512]{1,0:T(8,128)(2,1)S(1)}, bf16[2048,512]{1,0:T(8,128)(2,1)}, u32[]{:S(2)}) copy-start(bf16[2048,512]{1,0:T(8,128)(2,1)} %w0.1) | copy-start | bytes 6291460
  39.8 3.9 %collective-permute-start.9 = (bf16[32,2048]{1,0:T(8,128)(2,1)S(1)}, bf16[32,2048]{1,0:T(8,128)(2,1)S(1)}, u32[]{:S(2)}, u32[]{:S(2)}) collective-permute-start(bf16[32,2048]{1,0:T(8,128)(2,1)S(1)} %combine.1), channel_id=1, source_target_pairs={{0,64},{8,24},{16,80},{24,8},{32,96},{40,56},{48,112},{56,40},{64,... | collective-permute-start | bytes 393224 | tf_op jit(solution)/shard_map/ppermute | solution.py:465
  43.7 6.5 %collective-permute-start.10 = (bf16[64,2048]{1,0:T(8,128)(2,1)S(1)}, bf16[64,2048]{1,0:T(8,128)(2,1)S(1)}, u32[]{:S(2)}, u32[]{:S(2)}) collective-permute-start(bf16[64,2048]{1,0:T(8,128)(2,1)S(1)} %pad_maximum_fusion.2), channel_id=1, source_target_pairs={{0,192},{8,56},{16,208},{24,40},{32,224},{40,24},{48,240},{56,8},{... | collective-permute-start | bytes 786440 | tf_op jit(solution)/shard_map/ppermute | solution.py:465
  50.3 8.1 %collective-permute-start.13 = (bf16[128,2048]{1,0:T(8,128)(2,1)S(1)}, bf16[128,2048]{1,0:T(8,128)(2,1)S(1)}, u32[]{:S(2)}, u32[]{:S(2)}) collective-permute-start(bf16[128,2048]{1,0:T(8,128)(2,1)S(1)} %pad_maximum_fusion.refs_0_), channel_id=1, source_target_pairs={{0,16},{8,72},{16,0},{24,88},{32,48},{40,104},{48,32},{56,120},{64... | collective-permute-start | bytes 1572872 | tf_op jit(solution)/shard_map/ppermute | solution.py:465
  50.7 10.6 %collective-permute-start.11 = (bf16[128,2048]{1,0:T(8,128)(2,1)S(1)}, bf16[128,2048]{1,0:T(8,128)(2,1)S(1)}, u32[]{:S(2)}, u32[]{:S(2)}) collective-permute-start(bf16[128,2048]{1,0:T(8,128)(2,1)S(1)} %pad_maximum_fusion.refs_0_), channel_id=1, source_target_pairs={{0,48},{8,200},{16,32},{24,216},{32,16},{40,232},{48,0},{56,248},{... | collective-permute-start | bytes 1572872 | tf_op jit(solution)/shard_map/ppermute | solution.py:465
  58.4 6.8 %collective-permute-start.14 = (bf16[64,2048]{1,0:T(8,128)(2,1)S(1)}, bf16[64,2048]{1,0:T(8,128)(2,1)S(1)}, u32[]{:S(2)}, u32[]{:S(2)}) collective-permute-start(bf16[64,2048]{1,0:T(8,128)(2,1)S(1)} %slice.25), channel_id=1, source_target_pairs={{0,48},{8,200},{16,32},{24,216},{32,16},{40,232},{48,0},{56,248},{... | collective-permute-start | bytes 786440 | tf_op jit(solution)/shard_map/ppermute | solution.py:465
  61.3 5.6 %collective-permute-start.12 = (bf16[64,2048]{1,0:T(8,128)(2,1)S(1)}, bf16[64,2048]{1,0:T(8,128)(2,1)S(1)}, u32[]{:S(2)}, u32[]{:S(2)}) collective-permute-start(bf16[64,2048]{1,0:T(8,128)(2,1)S(1)} %slice.24), channel_id=1, source_target_pairs={{0,16},{8,72},{16,0},{24,88},{32,48},{40,104},{48,32},{56,120},{64... | collective-permute-start | bytes 786440 | tf_op jit(solution)/shard_map/ppermute | solution.py:465
  67.7 6.3 %collective-permute-start.16 = (bf16[5,64,512]{2,1,0:T(8,128)(2,1)S(1)}, bf16[5,64,512]{2,1,0:T(8,128)(2,1)S(1)}, u32[]{:S(2)}, u32[]{:S(2)}) collective-permute-start(bf16[5,64,512]{2,1,0:T(8,128)(2,1)S(1)} %get-tuple-element.35), channel_id=1, source_target_pairs={{0,1},{1,2},{2,3},{3,4},{4,5},{5,6},{6,7},{7,0},{8,9},{9,10},{10,1... | collective-permute-start | bytes 983048 | tf_op jit(solution)/shard_map/ppermute | solution.py:469
  69.4 6.4 %collective-permute-start.17 = (bf16[5,64,512]{2,1,0:T(8,128)(2,1)S(1)}, bf16[5,64,512]{2,1,0:T(8,128)(2,1)S(1)}, u32[]{:S(2)}, u32[]{:S(2)}) collective-permute-start(bf16[5,64,512]{2,1,0:T(8,128)(2,1)S(1)} %get-tuple-element.36), channel_id=1, source_target_pairs={{0,7},{1,0},{2,1},{3,2},{4,3},{5,4},{6,5},{7,6},{8,15},{9,8},{10,9... | collective-permute-start | bytes 983048 | tf_op jit(solution)/shard_map/ppermute | solution.py:469
  75.8 20.5 %collective-permute-start.18 = (bf16[64,1024]{1,0:T(8,128)(2,1)S(1)}, bf16[64,1024]{1,0:T(8,128)(2,1)S(1)}, u32[]{:S(2)}, u32[]{:S(2)}) collective-permute-start(bf16[64,1024]{1,0:T(8,128)(2,1)S(1)} %get-tuple-element.37), channel_id=1, source_target_pairs={{0,3},{1,4},{2,5},{3,6},{4,7},{5,0},{6,1},{7,2},{8,11},{9,12},{10,... | collective-permute-start | bytes 393224 | tf_op jit(solution)/shard_map/ppermute | solution.py:469
  80.6 15.8 %collective-permute-start.19 = (bf16[64,1024]{1,0:T(8,128)(2,1)S(1)}, bf16[64,1024]{1,0:T(8,128)(2,1)S(1)}, u32[]{:S(2)}, u32[]{:S(2)}) collective-permute-start(bf16[64,1024]{1,0:T(8,128)(2,1)S(1)} %get-tuple-element.38), channel_id=1, source_target_pairs={{0,5},{1,6},{2,7},{3,0},{4,1},{5,2},{6,3},{7,4},{8,13},{9,14},{10,... | collective-permute-start | bytes 393224 | tf_op jit(solution)/shard_map/ppermute | solution.py:469
  80.6 25.7 %collective-permute-start.21 = (bf16[4,16,128]{2,1,0:T(8,128)(2,1)S(1)}, bf16[4,16,128]{2,1,0:T(8,128)(2,1)S(1)}, u32[]{:S(2)}, u32[]{:S(2)}) collective-permute-start(bf16[4,16,128]{2,1,0:T(8,128)(2,1)S(1)} %pad_maximum_fusion.3), channel_id=1, source_target_pairs={{0,8},{8,0},{16,24},{24,16},{32,40},{40,32},{48,56},{56,48},{64,72... | collective-permute-start | bytes 49160 | tf_op jit(solution)/shard_map/ppermute | solution.py:448
  96.4 10.8 %collective-permute-start.20 = (bf16[64,512]{1,0:T(8,128)(2,1)S(1)}, bf16[64,512]{1,0:T(8,128)(2,1)S(1)}, u32[]{:S(2)}, u32[]{:S(2)}) collective-permute-start(bf16[64,512]{1,0:T(8,128)(2,1)S(1)} %get-tuple-element.40), channel_id=1, source_target_pairs={{0,8},{8,0},{16,24},{24,16},{32,40},{40,32},{48,56},{56,48},{64,72... | collective-permute-start | bytes 196616 | tf_op jit(solution)/shard_map/ppermute | solution.py:448

commit v4 on v3

--- a/solution.py
+++ b/solution.py
@@ -20,6 +20,7 @@
 
 
 ANY = pl.BlockSpec(memory_space=pl.ANY)
+HBM = pl.BlockSpec(memory_space=pltpu.HBM)
 
 
 def params(mib=16):
@@ -83,7 +84,7 @@
         copy.wait()
     base = place[1]
     for n in range(32):
-        keys = jnp.concatenate([pool[0, table[n, j] - base] for j in range(8)], axis=0)
+        keys = jnp.concatenate([pool[0, table[j, n] - base] for j in range(8)], axis=0)
         s = dot(wide[n].astype(BF16), keys, NT) * SCALE
         scores[n] = jnp.where(lane < length[n], s, -1e30)
     own_keys = new[0].astype(F32)
@@ -102,7 +103,7 @@
     inverse = 1.0 / total
     copies[6].wait()
     for n in range(32):
-        values = jnp.concatenate([pool[1, table[n, j] - base] for j in range(8)], axis=0)
+        values = jnp.concatenate([pool[1, table[j, n] - base] for j in range(8)], axis=0)
         mixed = dot(weights[n], values) + own_weight[n] * own_values[n : n + 1]
         scores[slots[n]] = mixed * inverse[n]
     held = [jnp.zeros((GROUP, DH), F32) for _ in range(4)]
@@ -123,12 +124,12 @@
     return pl.pallas_call(
         local_body,
         out_shape=[out] * 4,
-        in_specs=[SMEM] + [ANY] * 6,
+        in_specs=[SMEM] + [HBM] * 6,
         out_specs=[VMEM] * 4,
         scratch_shapes=[
             pltpu.VMEM((32, GROUP * DH), BF16),
             pltpu.SMEM((32,), jnp.int32),
-            pltpu.SMEM((32, 8), jnp.int32),
+            pltpu.SMEM((8, 32), jnp.int32),
             pltpu.SMEM((32,), jnp.int32),
             pltpu.VMEM((2, 32, DH), BF16),
             pltpu.VMEM((2, 256, GROUP, DH), BF16),
@@ -189,7 +190,7 @@
 COUNT = ROWS // GROUP
 
 
-def prefix_send_body(qa, qb, kv0, kv1, after, out):
+def prefix_send_body(qa, qb, kv0, kv1, later, out):
     lane = lanes()
     tile = jnp.zeros((GROUP, DH), F32)
     for half, q in enumerate((qa, qb)):
@@ -212,13 +213,25 @@
         masses[at : at + COUNT] = jnp.broadcast_to(mass, (ROWS, DH)).reshape(COUNT, GROUP, DH)
 
 
+def prefix_first_body(q, kv0_in, kv1_in, out, masses, kv0, kv1, sems):
+    copies = [
+        pltpu.make_async_copy(kv0_in, kv0, sems.at[0]),
+        pltpu.make_async_copy(kv1_in, kv1, sems.at[1]),
+    ]
+    for copy in copies:
+        copy.start()
+    for copy in copies:
+        copy.wait()
+    prefix_keep_body(q, kv0, kv1, out, masses)
+
+
 def prefix_cost(rows):
     return pl.CostEstimate(
         flops=4 * rows * 4096 * 128, bytes_accessed=2_500_000, transcendentals=rows * 4096
     )
 
 
-def prefix_send(qa, qb, kv0, kv1, after):
+def prefix_send(qa, qb, kv0, kv1, later):
     return pl.pallas_call(
         prefix_send_body,
         out_shape=jax.ShapeDtypeStruct((33, GROUP, DH), BF16),
@@ -227,7 +240,7 @@
         compiler_params=params(24),
         cost_estimate=prefix_cost(512),
         name="prefix_send",
-    )(qa, qb, kv0, kv1, after)
+    )(qa, qb, kv0, kv1, later)
 
 
 def prefix_keep(q, kv0, kv1):
@@ -240,6 +253,21 @@
         compiler_params=params(24),
         cost_estimate=prefix_cost(256),
         name="prefix_keep",
+    )(q, kv0, kv1)
+
+
+def prefix_first(q, kv0, kv1):
+    out = jax.ShapeDtypeStruct((16, GROUP, DH), F32)
+    held = jax.ShapeDtypeStruct(kv0.shape, BF16)
+    return pl.pallas_call(
+        prefix_first_body,
+        out_shape=[out, out, held, held],
+        in_specs=[VMEM, HBM, HBM],
+        out_specs=[VMEM] * 4,
+        scratch_shapes=[pltpu.SemaphoreType.DMA((2,))],
+        compiler_params=params(24),
+        cost_estimate=prefix_cost(256),
+        name="prefix_first",
     )(q, kv0, kv1)
 
 
@@ -300,97 +328,101 @@
     return chunks
 
 
-def project_body(count, *refs):
-    blocks, weights, out = refs[:count], refs[count : count + 2], refs[count + 2]
-    for i, block in enumerate(blocks):
+def project_body(sizes, *refs):
+    blocks, weights, out = refs[: sum(sizes)], refs[sum(sizes) : sum(sizes) + 2], refs[-1]
+    at = 0
+    for i, size in enumerate(sizes):
+        block = jnp.concatenate([b[...] for b in blocks[at : at + size]], axis=0)
+        at += size
         for side, weight in enumerate(weights):
-            for d, chunk in enumerate(by_target(dot(block[...], weight[...]))):
+            for d, chunk in enumerate(by_target(dot(block, weight[...]))):
                 out[d, i * 16 : i * 16 + 16, side * 512 : side * 512 + 512] = chunk
 
 
 def project(blocks, weights):
-    count = len(blocks)
-    return pl.pallas_call(
-        lambda *refs: project_body(count, *refs),
-        out_shape=jax.ShapeDtypeStruct((8, 16 * count, 1024), F32),
-        in_specs=[VMEM] * (count + 2),
+    sizes = [len(block) for block in blocks]
+    pieces = [piece for block in blocks for piece in block]
+    return pl.pallas_call(
+        lambda *refs: project_body(sizes, *refs),
+        out_shape=jax.ShapeDtypeStruct((8, 16 * len(sizes), 1024), F32),
+        in_specs=[VMEM] * (len(pieces) + 2),
         out_specs=VMEM,
         compiler_params=params(),
         cost_estimate=pl.CostEstimate(
-            flops=count * 2 * 128 * 2048 * 1024, bytes_accessed=4_500_000, transcendentals=0
+            flops=len(sizes) * 2 * 128 * 2048 * 1024, bytes_accessed=4_500_000, transcendentals=0
         ),
         name="project",
-    )(*blocks, *weights)
-
-
-def last_body(block, w0, w1, first, second, up, down, keep):
+    )(*pieces, *weights)
+
+
+def last_body(*refs):
+    pieces, (w0, w1, first, second, up, down, keep) = refs[:-7], refs[-7:]
+    block = jnp.concatenate([piece[...] for piece in pieces], axis=0)
     for side, weight in enumerate((w0, w1)):
         columns = slice(side * 512, side * 512 + 512)
-        chunks = by_target(dot(block[...], weight[...]))
-        for d, chunk in enumerate(chunks):
+        for d, chunk in enumerate(by_target(dot(block, weight[...]))):
             whole = jnp.concatenate([first[d, :, columns], second[d, :, columns], chunk], axis=0)
-            if d in (0, 3, 5):
-                keep[(0, 3, 5).index(d), :, columns] = whole
-            elif d in (1, 6):
-                up[2 * (1, 6).index(d) + side] = whole.astype(BF16)
-            elif d in (7, 2):
-                down[2 * (7, 2).index(d) + side] = whole.astype(BF16)
+            if d != 4:
+                keep[d, :, columns] = whole
             elif side == 0:
-                up[4] = whole.astype(BF16)
+                up[...] = whole.astype(BF16)
             else:
-                down[4] = whole.astype(BF16)
-
-
-def project_last(block, weights, first, second):
-    out = jax.ShapeDtypeStruct((5, 64, 512), BF16)
+                down[...] = whole.astype(BF16)
+
+
+def project_last(pieces, weights, first, second):
+    out = jax.ShapeDtypeStruct((64, 512), BF16)
     return pl.pallas_call(
         last_body,
-        out_shape=[out, out, jax.ShapeDtypeStruct((3, 64, 1024), F32)],
-        in_specs=[VMEM] * 5,
+        out_shape=[out, out, jax.ShapeDtypeStruct((8, 64, 1024), F32)],
+        in_specs=[VMEM] * (len(pieces) + 4),
         out_specs=[VMEM] * 3,
         compiler_params=params(),
         name="project_last",
-    )(block, *weights, first, second)
-
-
-def middle_body(keep, below, above, up, down):
-    far = below[4].astype(F32), above[4].astype(F32)
-    up[:, :512] = (keep[1, :, :512] + above[2].astype(F32) + far[0]).astype(BF16)
-    up[:, 512:] = (keep[1, :, 512:] + above[3].astype(F32)).astype(BF16)
-    down[:, :512] = (keep[2, :, :512] + below[2].astype(F32)).astype(BF16)
-    down[:, 512:] = (keep[2, :, 512:] + below[3].astype(F32) + far[1]).astype(BF16)
-
-
-def middle(keep, below, above):
+    )(*pieces, *weights, first, second)
+
+
+def step_body(near, keep, below, above, up, down):
+    low, high = keep.at[near], keep.at[8 - near]
+    if below.shape[1] == 512:
+        up[:, :512] = (low[:, :512] + below[...].astype(F32)).astype(BF16)
+        up[:, 512:] = low[:, 512:].astype(BF16)
+        down[:, :512] = high[:, :512].astype(BF16)
+        down[:, 512:] = (high[:, 512:] + above[...].astype(F32)).astype(BF16)
+    else:
+        up[...] = (low[...] + below[...].astype(F32)).astype(BF16)
+        down[...] = (high[...] + above[...].astype(F32)).astype(BF16)
+
+
+def step(near, keep, below, above):
     out = jax.ShapeDtypeStruct((64, 1024), BF16)
     return pl.pallas_call(
-        middle_body,
+        lambda *refs: step_body(near, *refs),
         out_shape=[out, out],
         in_specs=[VMEM] * 3,
         out_specs=[VMEM] * 2,
         compiler_params=params(),
-        name="middle",
+        name="step",
     )(keep, below, above)
 
 
-def total_body(keep, below, above, below3, above3, own, other):
+def total_body(keep, below, above, own, other):
     for side, out in enumerate((own, other)):
         columns = slice(side * 512, side * 512 + 512)
-        near = keep[0, :, columns] + below[side].astype(F32) + above[side].astype(F32)
-        far = below3[:, columns].astype(F32) + above3[:, columns].astype(F32)
-        out[...] = (near + far).astype(BF16)
-
-
-def total(keep, below, above, below3, above3):
+        near = below[:, columns].astype(F32) + above[:, columns].astype(F32)
+        out[...] = (keep[0, :, columns] + near).astype(BF16)
+
+
+def total(keep, below, above):
     out = jax.ShapeDtypeStruct((64, 512), BF16)
     return pl.pallas_call(
         total_body,
         out_shape=[out, out],
-        in_specs=[VMEM] * 5,
+        in_specs=[VMEM] * 3,
         out_specs=[VMEM] * 2,
         compiler_params=params(),
         name="total",
-    )(keep, below, above, below3, above3)
+    )(keep, below, above)
 
 
 def order_body(place, orders, pick):
@@ -479,33 +511,36 @@
     prefix_other = other_core(prefix_kv)
     weights = [out_weight, other_core(out_weight)]
 
-    sent = local_parts(place, queries, prompt_of, page_table, suffix_len, new_kv, suffix_kv)
+    sent = local_parts(place, queries, prompt_of, page_table.T, suffix_len, new_kv, suffix_kv)
     by_x = [sent[0]] + [along_x(sent[k], k) for k in (1, 2, 3)]
     same, other, far = regroup(place, by_x)
     from1, from3, from2 = along_y(same, 1), along_y(other, 3), along_y(other, 2)
     far = along_y(far, 2)
 
-    own = prefix_keep(same, prefix_kv, prefix_other)
-    message = along_y(prefix_send(from1, from3, prefix_kv, prefix_other, own[1]), 1)
-    cross = prefix_keep(from2, prefix_kv, prefix_other)
+    *own, kv0, kv1 = prefix_first(same, prefix_kv, prefix_other)
+    message = along_y(prefix_send(from1, from3, kv0, kv1, from2), 1)
+    cross = prefix_keep(from2, kv0, kv1)
     attended = combine(place, own, cross, message, by_x, far)
 
     orders = jnp.stack([same[16], from1[16], from2[16], from3[16]])
     orders = jnp.concatenate([orders, other_core(orders)], axis=0)
     pick = order_rows(place, orders)
 
-    pair = jnp.concatenate([attended, turned(attended, 1, 0)], axis=0)
-    ring0 = jnp.concatenate([pair, turned(pair, 3, 0)], axis=0)
-    ring1, ring3 = turned(ring0, 1, 1), turned(ring0, 3, 1)
-    ring2 = jnp.concatenate([turned(ring3[:64], 1, 1), turned(ring1[64:], 3, 1)], axis=0)
-    first = project([ring0], weights)
-    second = project([ring1, ring3], weights)
-    up, down, keep = project_last(ring2, weights, first, second)
-
-    below, above = along_z(up, 1), along_z(down, -1)
-    up3, down3 = middle(keep, below, above)
-    below3, above3 = along_z(up3, 3), along_z(down3, -3)
-    own, other = total(keep, below, above, below3, above3)
+    next1 = turned(attended, 1, 0)
+    lower = jnp.concatenate([attended, next1], axis=0)
+    upper = jnp.concatenate([turned(attended, 3, 0), turned(next1, 3, 0)], axis=0)
+    low1, low3 = turned(lower, 1, 1), turned(lower, 3, 1)
+    high1, high3 = turned(upper, 1, 1), turned(upper, 3, 1)
+    low2 = [turned(low3[:32], 1, 1), turned(low3[32:], 1, 1)]
+    high2 = [turned(high1[:32], 3, 1), turned(high1[32:], 3, 1)]
+    first = project([[lower, upper]], weights)
+    second = project([[low1, high1], [low3, high3]], weights)
+    below, above, keep = project_last(low2 + high2, weights, first, second)
+
+    for near in (3, 2, 1):
+        below, above = along_z(below, 1), along_z(above, -1)
+        below, above = step(near, keep, below, above)
+    own, other = total(keep, along_z(below, 1), along_z(above, -1))
     return finish(own, other_core(other), pick)
 
 

time: 108 us -> 105 us (0.972)
  the two profiles are of different devices: /device:TPU:33 before, /device:TPU:1 now
where the time goes in v4:
time: 105 us
  starting transfers between devices  58.9 us (56%)
  waiting for transfers between devices  23.6 us (22%)
  Pallas kernels  19.2 us (18%)
  local copies, waits for them, and re-layouts  2.83 us (3%)
    ppermute x12, starting transfers between devices, along(): lax.ppermute(value, 'batch', [(i, i ^ k << shift) for i in range(BATCH)])  33.8 us
    ppermute x8, starting transfers between devices, along_z(): lax.ppermute(value, 'head', [(i, (i + k) % HEADS) for i in range(HEADS)])  14.4 us
    ppermute x11, waiting for transfers between devices, turned(): return lax.ppermute(value, 'batch', pairs)  11.6 us
    ppermute x11, starting transfers between devices, turned(): return lax.ppermute(value, 'batch', pairs)  10.6 us
    ppermute x8, waiting for transfers between devices, along_z(): lax.ppermute(value, 'head', [(i, (i + k) % HEADS) for i in range(HEADS)])  7.35 us
    ppermute x12, waiting for transfers between devices, along(): lax.ppermute(value, 'batch', [(i, i ^ k << shift) for i in range(BATCH)])  4.65 us
    pallas_call x1, Pallas kernels, local_parts(): pl.pallas_call(local_body, out_shape=[out] * 4, in_specs=[SMEM] + [HBM] *...  4.23 us
    pallas_call x1, Pallas kernels, prefix_send(): pl.pallas_call(prefix_send_body, out_shape=jax.ShapeDtypeStruct((33, GROU...  4.13 us
  transfers between devices with their start and end apart: 31, of which 14 were waited for; matrix products, arithmetic and copies ran while one was open for 1% of the time, Pallas kernels for 17%

profile of v4, /device:TPU:1, one launch (start us, length us, event | category | flops | bytes accessed | tf_op | source)
XLA Modules:
  0.0 104.7 jit_solution(17596562629021137636)
XLA Ops:
  0.0 3.2 %collective-permute-start.3 = (bf16[2,2048,128]{2,1,0:T(8,128)(2,1)}, bf16[2,2048,128]{2,1,0:T(8,128)(2,1)S(1)}, u32[]{:S(2)}, u32[]{:S(2)}) collective-permute-start(bf16[2,2048,128]{2,1,0:T(8,128)(2,1)} %kv0_in.1), channel_id=1, source_target_pairs={{0,8},{8,0},{16,24},{24,16},{32,40},{40,32},{48,56},{56,48},{64,72... | collective-permute-start | bytes 3145736 | tf_op jit(solution)/shard_map/ppermute | solution.py:480
  3.2 0.6 stack.34.place
  3.9 4.2 %local_parts.1 = (bf16[18,16,128]{2,1,0:T(8,128)(2,1)}, bf16[18,16,128]{2,1,0:T(8,128)(2,1)}, bf16[18,16,128]{2,1,0:T(8,128)(2,1)}, bf16[18,16,128]{2,1,0:T(8,128)(2,1)}) custom-call(s32[7]{0:T(128)} %stack.34.place, bf16[32,2048]{1,0:T(8,128)(2,1)} %q_in.1, s32[32]{0:T(128)} %prompt_in.1, s32[8,32]{1,0:T(8,128)} %bitcast.8, s32[32]{0:T(128)} %length_in.1, ...), custom_call_target="tpu_custom_call" | custom-call | tf_op jit(solution)/shard_map/local_parts/pallas_call | solution.py:124
  8.1 0.1 collective-permute-start
  8.2 1.9 %collective-permute-start.1 = (bf16[18,16,128]{2,1,0:T(8,128)(2,1)}, bf16[18,16,128]{2,1,0:T(8,128)(2,1)S(1)}, u32[]{:S(2)}, u32[]{:S(2)}) collective-permute-start(bf16[18,16,128]{2,1,0:T(8,128)(2,1)} %get-tuple-element.31), channel_id=1, source_target_pairs={{0,128},{8,136},{16,144},{24,152},{32,160},{40,168},{48,176},{56,1... | collective-permute-start | bytes 221192 | tf_op jit(solution)/shard_map/ppermute | solution.py:480
  10.1 1.9 %collective-permute-start.2 = (bf16[18,16,128]{2,1,0:T(8,128)(2,1)}, bf16[18,16,128]{2,1,0:T(8,128)(2,1)S(1)}, u32[]{:S(2)}, u32[]{:S(2)}) collective-permute-start(bf16[18,16,128]{2,1,0:T(8,128)(2,1)} %get-tuple-element.32), channel_id=1, source_target_pairs={{0,192},{8,200},{16,208},{24,216},{32,224},{40,232},{48,240},{56,2... | collective-permute-start | bytes 221192 | tf_op jit(solution)/shard_map/ppermute | solution.py:480
  12.1 0.8 collective-permute-start.18
  12.9 0.0 collective-permute-done.a1.s1
  12.9 1.4 %collective-permute-done.1.a2.s2 = bf16[18,16,128]{2,1,0:T(8,128)(2,1)S(1)} collective-permute-done((bf16[18,16,128]{2,1,0:T(8,128)(2,1)}, bf16[18,16,128]{2,1,0:T(8,128)(2,1)S(1)}, u32[]{:S(2)}, u32[]{:S(2)}) %collective-permute-start.1) | collective-permute-done | bytes 73760 | tf_op jit(solution)/shard_map/ppermute | solution.py:480
  14.4 1.4 %collective-permute-done.2.a3.s3 = bf16[18,16,128]{2,1,0:T(8,128)(2,1)S(1)} collective-permute-done((bf16[18,16,128]{2,1,0:T(8,128)(2,1)}, bf16[18,16,128]{2,1,0:T(8,128)(2,1)S(1)}, u32[]{:S(2)}, u32[]{:S(2)}) %collective-permute-start.2) | collective-permute-done | bytes 73760 | tf_op jit(solution)/shard_map/ppermute | solution.py:480
  15.8 0.9 copy-done.2
  16.7 0.6 regroup.1
  17.3 2.8 %collective-permute-start.6 = (bf16[17,16,128]{2,1,0:T(8,128)(2,1)S(1)}, bf16[17,16,128]{2,1,0:T(8,128)(2,1)S(1)}, u32[]{:S(2)}, u32[]{:S(2)}) collective-permute-start(bf16[17,16,128]{2,1,0:T(8,128)(2,1)S(1)} %get-tuple-element.36), channel_id=1, source_target_pairs={{0,48},{8,56},{16,32},{24,40},{32,16},{40,24},{48,0},{56,8},{64,11... | collective-permute-start | bytes 208904 | tf_op jit(solution)/shard_map/ppermute | solution.py:480
  20.1 0.3 collective-permute-start.4
  20.4 0.3 collective-permute-start.5
  20.7 0.0 collective-permute-done.3.kv1_in
  20.7 1.2 %copy-done.1 = bf16[2,2048,128]{2,1,0:T(8,128)(2,1)S(1)} copy-done((bf16[2,2048,128]{2,1,0:T(8,128)(2,1)S(1)}, bf16[2,2048,128]{2,1,0:T(8,128)(2,1)}, u32[]{:S(2)}) %copy-start.1) | copy-done | bytes 1048600
  22.0 2.3 %prefix_first.1 = (f32[16,16,128]{2,1,0:T(8,128)S(1)}, f32[16,16,128]{2,1,0:T(8,128)S(1)}, bf16[2,2048,128]{2,1,0:T(8,128)(2,1)S(1)}, bf16[2,2048,128]{2,1,0:T(8,128)(2,1)S(1)}) custom-call(bf16[17,16,128]{2,1,0:T(8,128)(2,1)S(1)} %get-tuple-element.33.q, bf16[2,2048,128]{2,1,0:T(8,128)(2,1)S(1)} %copy-done.1, ...), custom_call_target="tpu_custom_call" | custom-call | flops 536870912 | bytes 2500000 | tf_op jit(solution)/shard_map/prefix_first/pallas_call | solution.py:262
  24.3 0.0 collective-permute-done.6.qb
  24.3 0.4 collective-permute-done.4.q.later
  24.7 4.1 %prefix_send.1 = bf16[33,16,128]{2,1,0:T(8,128)(2,1)S(1)} custom-call(bf16[17,16,128]{2,1,0:T(8,128)(2,1)S(1)} %collective-permute-done.5.qa, bf16[17,16,128]{2,1,0:T(8,128)(2,1)S(1)} %collective-permute-done.6.qb, bf16[2,2048,128]{2,1,0:T(8,128)(2,1)S(1)} %get-tuple-element.37.kv0, bf16[2,2048,128]{2,1,0:T(8,128)(2,1)S(1)} %get-tuple-element.38.kv1, ...), custom_call_target="tpu_custom_call" | custom-call | flops 1073741824 | bytes 2500000 | tf_op jit(solution)/shard_map/prefix_send/pallas_call | solution.py:235
  28.9 1.0 collective-permute-start.7
  29.9 2.6 %collective-permute-start.8 = (bf16[20,16,128]{2,1,0:T(8,128)(2,1)S(1)}, bf16[20,16,128]{2,1,0:T(8,128)(2,1)S(1)}, u32[]{:S(2)}, u32[]{:S(2)}) collective-permute-start(bf16[20,16,128]{2,1,0:T(8,128)(2,1)S(1)} %get-tuple-element.41), channel_id=1, source_target_pairs={{0,32},{8,40},{16,48},{24,56},{32,0},{40,8},{48,16},{56,24},{64,96... | collective-permute-start | bytes 245768 | tf_op jit(solution)/shard_map/ppermute | solution.py:480
  32.5 2.2 %prefix_keep.1 = (f32[16,16,128]{2,1,0:T(8,128)S(1)}, f32[16,16,128]{2,1,0:T(8,128)S(1)}) custom-call(bf16[17,16,128]{2,1,0:T(8,128)(2,1)S(1)} %collective-permute-done.4.q.later, bf16[2,2048,128]{2,1,0:T(8,128)(2,1)S(1)} %get-tuple-element.37.kv0, bf16[2,2048,128]{2,1,0:T(8,128)(2,1)S(1)} %get-tuple-element.38.kv1), custom_call_target="tpu_custom_call" | custom-call | flops 536870912 | bytes 2500000 | tf_op jit(solution)/shard_map/prefix_keep/pallas_call | solution.py:248
  34.7 1.1 %collective-permute-done.8.far = bf16[20,16,128]{2,1,0:T(8,128)(2,1)S(1)} collective-permute-done((bf16[20,16,128]{2,1,0:T(8,128)(2,1)S(1)}, bf16[20,16,128]{2,1,0:T(8,128)(2,1)S(1)}, u32[]{:S(2)}, u32[]{:S(2)}) %collective-permute-start.8) | collective-permute-done | bytes 81952 | tf_op jit(solution)/shard_map/ppermute | solution.py:480
  35.8 0.0 collective-permute-done.7.message
  35.8 1.2 %combine.1 = bf16[32,2048]{1,0:T(8,128)(2,1)S(1)} custom-call(s32[7]{0:T(128)S(1)} %copy-done.4, f32[16,16,128]{2,1,0:T(8,128)S(1)} %get-tuple-element.34.own, f32[16,16,128]{2,1,0:T(8,128)S(1)} %get-tuple-element.35.own_masses, f32[16,16,128]{2,1,0:T(8,128)S(1)} %get-tuple-element.39.cross, f32[16,16,128]{2,1,0:T(8,128)S(1)} %get-tuple-element.40.cross_masses, ...), custom_call_target="tpu_custom_call" | custom-call | tf_op jit(solution)/shard_map/combine/pallas_call | solution.py:306
  37.0 0.1 collective-permute-start.9
  37.1 2.6 %collective-permute-start.13 = (bf16[32,2048]{1,0:T(8,128)(2,1)S(1)}, bf16[32,2048]{1,0:T(8,128)(2,1)S(1)}, u32[]{:S(2)}, u32[]{:S(2)}) collective-permute-start(bf16[32,2048]{1,0:T(8,128)(2,1)S(1)} %combine.1), channel_id=1, source_target_pairs={{0,192},{8,56},{16,208},{24,40},{32,224},{40,24},{48,240},{56,8},{... | collective-permute-start | bytes 393224 | tf_op jit(solution)/shard_map/ppermute | solution.py:497
  39.7 1.2 %collective-permute-done.9 = bf16[32,2048]{1,0:T(8,128)(2,1)S(1)} collective-permute-done((bf16[32,2048]{1,0:T(8,128)(2,1)S(1)}, bf16[32,2048]{1,0:T(8,128)(2,1)S(1)}, u32[]{:S(2)}, u32[]{:S(2)}) %collective-permute-start.9) | collective-permute-done | bytes 131104 | tf_op jit(solution)/shard_map/ppermute | solution.py:497
  41.0 0.2 collective-permute-start.19
  41.1 1.7 %collective-permute-start.10 = (bf16[64,2048]{1,0:T(8,128)(2,1)S(1)}, bf16[64,2048]{1,0:T(8,128)(2,1)S(1)}, u32[]{:S(2)}, u32[]{:S(2)}) collective-permute-start(bf16[64,2048]{1,0:T(8,128)(2,1)S(1)} %pad_maximum_fusion.refs_0_), channel_id=1, source_target_pairs={{0,48},{8,200},{16,32},{24,216},{32,16},{40,232},{48,0},{56,248},{... | collective-permute-start | bytes 786440 | tf_op jit(solution)/shard_map/ppermute | solution.py:497
  42.8 0.7 collective-permute-start.14
  43.5 4.3 %collective-permute-done.14 = bf16[32,2048]{1,0:T(8,128)(2,1)S(1)} collective-permute-done((bf16[32,2048]{1,0:T(8,128)(2,1)S(1)}, bf16[32,2048]{1,0:T(8,128)(2,1)S(1)}, u32[]{:S(2)}, u32[]{:S(2)}) %collective-permute-start.14) | collective-permute-done | bytes 131104 | tf_op jit(solution)/shard_map/ppermute | solution.py:497
  47.8 1.1 %collective-permute-start.20 = (bf16[64,2048]{1,0:T(8,128)(2,1)S(1)}, bf16[64,2048]{1,0:T(8,128)(2,1)S(1)}, u32[]{:S(2)}, u32[]{:S(2)}) collective-permute-start(bf16[64,2048]{1,0:T(8,128)(2,1)S(1)} %constant_dynamic-update-slice_fusion.refs_1_), channel_id=1, source_target_pairs={{0,48},{8,200},{16,32},{24,216},{32,16},{40,232},{48,0},{56,248},{... | collective-permute-start | bytes 786440 | tf_op jit(solution)/shard_map/ppermute | solution.py:497
  49.0 0.2 collective-permute-start.15
  49.1 1.4 %collective-permute-start.12 = (bf16[32,2048]{1,0:T(8,128)(2,1)S(1)}, bf16[32,2048]{1,0:T(8,128)(2,1)S(1)}, u32[]{:S(2)}, u32[]{:S(2)}) collective-permute-start(bf16[32,2048]{1,0:T(8,128)(2,1)S(1)} %get-tuple-element.55), channel_id=1, source_target_pairs={{0,16},{8,72},{16,0},{24,88},{32,48},{40,104},{48,32},{56,120},{64... | collective-permute-start | bytes 393224 | tf_op jit(solution)/shard_map/ppermute | solution.py:497
  50.5 3.9 %collective-permute-done.15.refs_1_ = bf16[64,2048]{1,0:T(8,128)(2,1)S(1)} collective-permute-done((bf16[64,2048]{1,0:T(8,128)(2,1)S(1)}, bf16[64,2048]{1,0:T(8,128)(2,1)S(1)}, u32[]{:S(2)}, u32[]{:S(2)}) %collective-permute-start.15) | collective-permute-done | bytes 262176 | tf_op jit(solution)/shard_map/ppermute | solution.py:497
  54.5 0.0 collective-permute-start.11
  54.5 0.0 collective-permute-done.19.refs_0_
  54.5 1.6 %collective-permute-start.17 = (bf16[32,2048]{1,0:T(8,128)(2,1)S(1)}, bf16[32,2048]{1,0:T(8,128)(2,1)S(1)}, u32[]{:S(2)}, u32[]{:S(2)}) collective-permute-start(bf16[32,2048]{1,0:T(8,128)(2,1)S(1)} %get-tuple-element.53), channel_id=1, source_target_pairs={{0,48},{8,200},{16,32},{24,216},{32,16},{40,232},{48,0},{56,248},{... | collective-permute-start | bytes 393224 | tf_op jit(solution)/shard_map/ppermute | solution.py:497
  56.1 1.2 %collective-permute-start.16 = (bf16[32,2048]{1,0:T(8,128)(2,1)S(1)}, bf16[32,2048]{1,0:T(8,128)(2,1)S(1)}, u32[]{:S(2)}, u32[]{:S(2)}) collective-permute-start(bf16[32,2048]{1,0:T(8,128)(2,1)S(1)} %get-tuple-element.54), channel_id=1, source_target_pairs={{0,48},{8,200},{16,32},{24,216},{32,16},{40,232},{48,0},{56,248},{... | collective-permute-start | bytes 393224 | tf_op jit(solution)/shard_map/ppermute | solution.py:497
  57.3 0.7 project.2.refs_6_
  58.0 1.3 %project.3.refs_7_ = f32[8,32,1024]{2,1,0:T(8,128)S(1)} custom-call(bf16[64,2048]{1,0:T(8,128)(2,1)S(1)} %collective-permute-done.19.refs_0_, bf16[64,2048]{1,0:T(8,128)(2,1)S(1)} %collective-permute-done.15.refs_1_, bf16[64,2048]{1,0:T(8,128)(2,1)S(1)} %collective-permute-done.10.refs_2_, bf16[64,2048]{1,0:T(8,128)(2,1)S(1)} %collective-permute-done.20.refs_3_, ...), custom_call_target="tpu_custom_call" | custom-call | flops 1073741824 | bytes 4500000 | tf_op jit(solution)/shard_map/project/pallas_call | solution.py:345
  59.3 0.3 collective-permute-done.17.refs_3_
  59.6 1.8 %collective-permute-done.16.refs_2_ = bf16[32,2048]{1,0:T(8,128)(2,1)S(1)} collective-permute-done((bf16[32,2048]{1,0:T(8,128)(2,1)S(1)}, bf16[32,2048]{1,0:T(8,128)(2,1)S(1)}, u32[]{:S(2)}, u32[]{:S(2)}) %collective-permute-start.16) | collective-permute-done | bytes 131104 | tf_op jit(solution)/shard_map/ppermute | solution.py:497
  61.4 0.8 project_last.1
  62.2 1.7 %collective-permute-start.21 = (bf16[64,512]{1,0:T(8,128)(2,1)S(1)}, bf16[64,512]{1,0:T(8,128)(2,1)S(1)}, u32[]{:S(2)}, u32[]{:S(2)}) collective-permute-start(bf16[64,512]{1,0:T(8,128)(2,1)S(1)} %get-tuple-element.43), channel_id=1, source_target_pairs={{0,1},{1,2},{2,3},{3,4},{4,5},{5,6},{6,7},{7,0},{8,9},{9,10},{10,1... | collective-permute-start | bytes 196616 | tf_op jit(solution)/shard_map/ppermute | solution.py:501
  63.9 4.2 %collective-permute-start.22 = (bf16[64,512]{1,0:T(8,128)(2,1)S(1)}, bf16[64,512]{1,0:T(8,128)(2,1)S(1)}, u32[]{:S(2)}, u32[]{:S(2)}) collective-permute-start(bf16[64,512]{1,0:T(8,128)(2,1)S(1)} %get-tuple-element.44), channel_id=1, source_target_pairs={{0,7},{1,0},{2,1},{3,2},{4,3},{5,4},{6,5},{7,6},{8,15},{9,8},{10,9... | collective-permute-start | bytes 196616 | tf_op jit(solution)/shard_map/ppermute | solution.py:501
  68.2 1.6 %collective-permute-done.21.refs_1_ = bf16[64,512]{1,0:T(8,128)(2,1)S(1)} collective-permute-done((bf16[64,512]{1,0:T(8,128)(2,1)S(1)}, bf16[64,512]{1,0:T(8,128)(2,1)S(1)}, u32[]{:S(2)}, u32[]{:S(2)}) %collective-permute-start.21) | collective-permute-done | bytes 65568 | tf_op jit(solution)/shard_map/ppermute | solution.py:501
  69.8 0.1 collective-permute-start.23
  69.9 2.8 %collective-permute-start.24 = (bf16[64,1024]{1,0:T(8,128)(2,1)S(1)}, bf16[64,1024]{1,0:T(8,128)(2,1)S(1)}, u32[]{:S(2)}, u32[]{:S(2)}) collective-permute-start(bf16[64,1024]{1,0:T(8,128)(2,1)S(1)} %get-tuple-element.46), channel_id=1, source_target_pairs={{0,7},{1,0},{2,1},{3,2},{4,3},{5,4},{6,5},{7,6},{8,15},{9,8},{10,9... | collective-permute-start | bytes 393224 | tf_op jit(solution)/shard_map/ppermute | solution.py:501
  72.7 2.3 %collective-permute-done.23.refs_1_ = bf16[64,1024]{1,0:T(8,128)(2,1)S(1)} collective-permute-done((bf16[64,1024]{1,0:T(8,128)(2,1)S(1)}, bf16[64,1024]{1,0:T(8,128)(2,1)S(1)}, u32[]{:S(2)}, u32[]{:S(2)}) %collective-permute-start.23) | collective-permute-done | bytes 131104 | tf_op jit(solution)/shard_map/ppermute | solution.py:501
  75.0 2.6 %collective-permute-start.25 = (bf16[64,1024]{1,0:T(8,128)(2,1)S(1)}, bf16[64,1024]{1,0:T(8,128)(2,1)S(1)}, u32[]{:S(2)}, u32[]{:S(2)}) collective-permute-start(bf16[64,1024]{1,0:T(8,128)(2,1)S(1)} %get-tuple-element.47), channel_id=1, source_target_pairs={{0,1},{1,2},{2,3},{3,4},{4,5},{5,6},{6,7},{7,0},{8,9},{9,10},{10,1... | collective-permute-start | bytes 393224 | tf_op jit(solution)/shard_map/ppermute | solution.py:501
  77.6 0.4 collective-permute-start.26
  78.0 3.0 %collective-permute-done.25.refs_1_ = bf16[64,1024]{1,0:T(8,128)(2,1)S(1)} collective-permute-done((bf16[64,1024]{1,0:T(8,128)(2,1)S(1)}, bf16[64,1024]{1,0:T(8,128)(2,1)S(1)}, u32[]{:S(2)}, u32[]{:S(2)}) %collective-permute-start.25) | collective-permute-done | bytes 131104 | tf_op jit(solution)/shard_map/ppermute | solution.py:501
  80.9 0.5 collective-permute-done.26.refs_2_
  81.5 1.2 %collective-permute-start.27 = (bf16[64,1024]{1,0:T(8,128)(2,1)S(1)}, bf16[64,1024]{1,0:T(8,128)(2,1)S(1)}, u32[]{:S(2)}, u32[]{:S(2)}) collective-permute-start(bf16[64,1024]{1,0:T(8,128)(2,1)S(1)} %get-tuple-element.49), channel_id=1, source_target_pairs={{0,1},{1,2},{2,3},{3,4},{4,5},{5,6},{6,7},{7,0},{8,9},{9,10},{10,1... | collective-permute-start | bytes 393224 | tf_op jit(solution)/shard_map/ppermute | solution.py:501
  82.7 1.5 %collective-permute-start.28 = (bf16[64,1024]{1,0:T(8,128)(2,1)S(1)}, bf16[64,1024]{1,0:T(8,128)(2,1)S(1)}, u32[]{:S(2)}, u32[]{:S(2)}) collective-permute-start(bf16[64,1024]{1,0:T(8,128)(2,1)S(1)} %get-tuple-element.50), channel_id=1, source_target_pairs={{0,7},{1,0},{2,1},{3,2},{4,3},{5,4},{6,5},{7,6},{8,15},{9,8},{10,9... | collective-permute-start | bytes 393224 | tf_op jit(solution)/shard_map/ppermute | solution.py:501
  84.2 15.2 %collective-permute-start.30 = (bf16[4,16,128]{2,1,0:T(8,128)(2,1)S(1)}, bf16[4,16,128]{2,1,0:T(8,128)(2,1)S(1)}, u32[]{:S(2)}, u32[]{:S(2)}) collective-permute-start(bf16[4,16,128]{2,1,0:T(8,128)(2,1)S(1)} %pad_maximum_fusion.1), channel_id=1, source_target_pairs={{0,8},{8,0},{16,24},{24,16},{32,40},{40,32},{48,56},{56,48},{64,72... | collective-permute-start | bytes 49160 | tf_op jit(solution)/shard_map/ppermute | solution.py:480
  99.5 3.5 %collective-permute-start.29 = (bf16[64,512]{1,0:T(8,128)(2,1)S(1)}, bf16[64,512]{1,0:T(8,128)(2,1)S(1)}, u32[]{:S(2)}, u32[]{:S(2)}) collective-permute-start(bf16[64,512]{1,0:T(8,128)(2,1)S(1)} %get-tuple-element.52), channel_id=1, source_target_pairs={{0,8},{8,0},{16,24},{24,16},{32,40},{40,32},{48,56},{56,48},{64,72... | collective-permute-start | bytes 196616 | tf_op jit(solution)/shard_map/ppermute | solution.py:480
  102.9 0.6 order_rows.1.pick
  103.6 0.2 collective-permute-done.29.other
  103.8 0.9 finish.1
  (35 shorter events, 0.3 us)
Async XLA Ops:
  0.0 12.1 %copy-start = (bf16[2048,512]{1,0:T(8,128)(2,1)S(1)}, bf16[2048,512]{1,0:T(8,128)(2,1)}, u32[]{:S(2)}) copy-start(bf16[2048,512]{1,0:T(8,128)(2,1)} %refs_4_.3) | copy-start | bytes 6291460
  0.0 20.7 %collective-permute-start.3 = (bf16[2,2048,128]{2,1,0:T(8,128)(2,1)}, bf16[2,2048,128]{2,1,0:T(8,128)(2,1)S(1)}, u32[]{:S(2)}, u32[]{:S(2)}) collective-permute-start(bf16[2,2048,128]{2,1,0:T(8,128)(2,1)} %kv0_in.1), channel_id=1, source_target_pairs={{0,8},{8,0},{16,24},{24,16},{32,40},{40,32},{48,56},{56,48},{64,72... | collective-permute-start | bytes 3145736 | tf_op jit(solution)/shard_map/ppermute | solution.py:480
  3.9 11.9 %copy-start.4 = (s32[7]{0:T(128)S(1)}, s32[7]{0:T(128)}, u32[]{:S(2)}) copy-start(s32[7]{0:T(128)} %stack.34.place) | copy-start | bytes 88
  8.1 4.8 %collective-permute-start = (bf16[18,16,128]{2,1,0:T(8,128)(2,1)}, bf16[18,16,128]{2,1,0:T(8,128)(2,1)S(1)}, u32[]{:S(2)}, u32[]{:S(2)}) collective-permute-start(bf16[18,16,128]{2,1,0:T(8,128)(2,1)} %get-tuple-element.30), channel_id=1, source_target_pairs={{0,64},{8,72},{16,80},{24,88},{32,96},{40,104},{48,112},{56,120},{... | collective-permute-start | bytes 221192 | tf_op jit(solution)/shard_map/ppermute | solution.py:480
  8.2 6.1 %collective-permute-start.1 = (bf16[18,16,128]{2,1,0:T(8,128)(2,1)}, bf16[18,16,128]{2,1,0:T(8,128)(2,1)S(1)}, u32[]{:S(2)}, u32[]{:S(2)}) collective-permute-start(bf16[18,16,128]{2,1,0:T(8,128)(2,1)} %get-tuple-element.31), channel_id=1, source_target_pairs={{0,128},{8,136},{16,144},{24,152},{32,160},{40,168},{48,176},{56,1... | collective-permute-start | bytes 221192 | tf_op jit(solution)/shard_map/ppermute | solution.py:480
  10.1 5.7 %collective-permute-start.2 = (bf16[18,16,128]{2,1,0:T(8,128)(2,1)}, bf16[18,16,128]{2,1,0:T(8,128)(2,1)S(1)}, u32[]{:S(2)}, u32[]{:S(2)}) collective-permute-start(bf16[18,16,128]{2,1,0:T(8,128)(2,1)} %get-tuple-element.32), channel_id=1, source_target_pairs={{0,192},{8,200},{16,208},{24,216},{32,224},{40,232},{48,240},{56,2... | collective-permute-start | bytes 221192 | tf_op jit(solution)/shard_map/ppermute | solution.py:480
  12.1 44.1 %collective-permute-start.18 = (bf16[2048,512]{1,0:T(8,128)(2,1)S(1)}, bf16[2048,512]{1,0:T(8,128)(2,1)S(1)}, u32[]{:S(2)}, u32[]{:S(2)}) collective-permute-start(bf16[2048,512]{1,0:T(8,128)(2,1)S(1)} %copy-done), channel_id=1, source_target_pairs={{0,8},{8,0},{16,24},{24,16},{32,40},{40,32},{48,56},{56,48},{64,72... | collective-permute-start | bytes 6291464 | tf_op jit(solution)/shard_map/ppermute | solution.py:480
  15.8 0.9 copy-start.2
  17.3 7.1 %collective-permute-start.6 = (bf16[17,16,128]{2,1,0:T(8,128)(2,1)S(1)}, bf16[17,16,128]{2,1,0:T(8,128)(2,1)S(1)}, u32[]{:S(2)}, u32[]{:S(2)}) collective-permute-start(bf16[17,16,128]{2,1,0:T(8,128)(2,1)S(1)} %get-tuple-element.36), channel_id=1, source_target_pairs={{0,48},{8,56},{16,32},{24,40},{32,16},{40,24},{48,0},{56,8},{64,11... | collective-permute-start | bytes 208904 | tf_op jit(solution)/shard_map/ppermute | solution.py:480
  20.1 4.7 %collective-permute-start.4 = (bf16[17,16,128]{2,1,0:T(8,128)(2,1)S(1)}, bf16[17,16,128]{2,1,0:T(8,128)(2,1)S(1)}, u32[]{:S(2)}, u32[]{:S(2)}) collective-permute-start(bf16[17,16,128]{2,1,0:T(8,128)(2,1)S(1)} %get-tuple-element.36), channel_id=1, source_target_pairs={{0,32},{8,40},{16,48},{24,56},{32,0},{40,8},{48,16},{56,24},{64,96... | collective-permute-start | bytes 208904 | tf_op jit(solution)/shard_map/ppermute | solution.py:480
  20.4 4.3 %collective-permute-start.5 = (bf16[17,16,128]{2,1,0:T(8,128)(2,1)S(1)}, bf16[17,16,128]{2,1,0:T(8,128)(2,1)S(1)}, u32[]{:S(2)}, u32[]{:S(2)}) collective-permute-start(bf16[17,16,128]{2,1,0:T(8,128)(2,1)S(1)} %get-tuple-element.33.q), channel_id=1, source_target_pairs={{0,16},{8,24},{16,0},{24,8},{32,48},{40,56},{48,32},{56,40},{64,80... | collective-permute-start | bytes 208904 | tf_op jit(solution)/shard_map/ppermute | solution.py:480
  20.7 1.2 %copy-start.1 = (bf16[2,2048,128]{2,1,0:T(8,128)(2,1)S(1)}, bf16[2,2048,128]{2,1,0:T(8,128)(2,1)}, u32[]{:S(2)}) copy-start(bf16[2,2048,128]{2,1,0:T(8,128)(2,1)} %kv0_in.1) | copy-start | bytes 3145732
  24.7 11.1 %copy-start.3 = (bf16[18,16,128]{2,1,0:T(8,128)(2,1)S(1)}, bf16[18,16,128]{2,1,0:T(8,128)(2,1)}, u32[]{:S(2)}) copy-start(bf16[18,16,128]{2,1,0:T(8,128)(2,1)} %get-tuple-element.29.a0.s0) | copy-start | bytes 221188
  28.9 7.0 %collective-permute-start.7 = (bf16[33,16,128]{2,1,0:T(8,128)(2,1)S(1)}, bf16[33,16,128]{2,1,0:T(8,128)(2,1)S(1)}, u32[]{:S(2)}, u32[]{:S(2)}) collective-permute-start(bf16[33,16,128]{2,1,0:T(8,128)(2,1)S(1)} %prefix_send.1), channel_id=1, source_target_pairs={{0,16},{8,24},{16,0},{24,8},{32,48},{40,56},{48,32},{56,40},{64,80... | collective-permute-start | bytes 405512 | tf_op jit(solution)/shard_map/ppermute | solution.py:480
  29.9 5.9 %collective-permute-start.8 = (bf16[20,16,128]{2,1,0:T(8,128)(2,1)S(1)}, bf16[20,16,128]{2,1,0:T(8,128)(2,1)S(1)}, u32[]{:S(2)}, u32[]{:S(2)}) collective-permute-start(bf16[20,16,128]{2,1,0:T(8,128)(2,1)S(1)} %get-tuple-element.41), channel_id=1, source_target_pairs={{0,32},{8,40},{16,48},{24,56},{32,0},{40,8},{48,16},{56,24},{64,96... | collective-permute-start | bytes 245768 | tf_op jit(solution)/shard_map/ppermute | solution.py:480
  37.0 3.9 %collective-permute-start.9 = (bf16[32,2048]{1,0:T(8,128)(2,1)S(1)}, bf16[32,2048]{1,0:T(8,128)(2,1)S(1)}, u32[]{:S(2)}, u32[]{:S(2)}) collective-permute-start(bf16[32,2048]{1,0:T(8,128)(2,1)S(1)} %combine.1), channel_id=1, source_target_pairs={{0,64},{8,24},{16,80},{24,8},{32,96},{40,56},{48,112},{56,40},{64,... | collective-permute-start | bytes 393224 | tf_op jit(solution)/shard_map/ppermute | solution.py:497
  37.1 6.4 %collective-permute-start.13 = (bf16[32,2048]{1,0:T(8,128)(2,1)S(1)}, bf16[32,2048]{1,0:T(8,128)(2,1)S(1)}, u32[]{:S(2)}, u32[]{:S(2)}) collective-permute-start(bf16[32,2048]{1,0:T(8,128)(2,1)S(1)} %combine.1), channel_id=1, source_target_pairs={{0,192},{8,56},{16,208},{24,40},{32,224},{40,24},{48,240},{56,8},{... | collective-permute-start | bytes 393224 | tf_op jit(solution)/shard_map/ppermute | solution.py:497
  41.0 13.5 %collective-permute-start.19 = (bf16[64,2048]{1,0:T(8,128)(2,1)S(1)}, bf16[64,2048]{1,0:T(8,128)(2,1)S(1)}, u32[]{:S(2)}, u32[]{:S(2)}) collective-permute-start(bf16[64,2048]{1,0:T(8,128)(2,1)S(1)} %pad_maximum_fusion.refs_0_), channel_id=1, source_target_pairs={{0,16},{8,72},{16,0},{24,88},{32,48},{40,104},{48,32},{56,120},{64... | collective-permute-start | bytes 786440 | tf_op jit(solution)/shard_map/ppermute | solution.py:497
  41.1 8.0 %collective-permute-start.10 = (bf16[64,2048]{1,0:T(8,128)(2,1)S(1)}, bf16[64,2048]{1,0:T(8,128)(2,1)S(1)}, u32[]{:S(2)}, u32[]{:S(2)}) collective-permute-start(bf16[64,2048]{1,0:T(8,128)(2,1)S(1)} %pad_maximum_fusion.refs_0_), channel_id=1, source_target_pairs={{0,48},{8,200},{16,32},{24,216},{32,16},{40,232},{48,0},{56,248},{... | collective-permute-start | bytes 786440 | tf_op jit(solution)/shard_map/ppermute | solution.py:497
  42.8 5.0 %collective-permute-start.14 = (bf16[32,2048]{1,0:T(8,128)(2,1)S(1)}, bf16[32,2048]{1,0:T(8,128)(2,1)S(1)}, u32[]{:S(2)}, u32[]{:S(2)}) collective-permute-start(bf16[32,2048]{1,0:T(8,128)(2,1)S(1)} %collective-permute-done.9), channel_id=1, source_target_pairs={{0,192},{8,56},{16,208},{24,40},{32,224},{40,24},{48,240},{56,8},{... | collective-permute-start | bytes 393224 | tf_op jit(solution)/shard_map/ppermute | solution.py:497
  47.8 10.2 %collective-permute-start.20 = (bf16[64,2048]{1,0:T(8,128)(2,1)S(1)}, bf16[64,2048]{1,0:T(8,128)(2,1)S(1)}, u32[]{:S(2)}, u32[]{:S(2)}) collective-permute-start(bf16[64,2048]{1,0:T(8,128)(2,1)S(1)} %constant_dynamic-update-slice_fusion.refs_1_), channel_id=1, source_target_pairs={{0,48},{8,200},{16,32},{24,216},{32,16},{40,232},{48,0},{56,248},{... | collective-permute-start | bytes 786440 | tf_op jit(solution)/shard_map/ppermute | solution.py:497
  49.0 5.5 %collective-permute-start.15 = (bf16[64,2048]{1,0:T(8,128)(2,1)S(1)}, bf16[64,2048]{1,0:T(8,128)(2,1)S(1)}, u32[]{:S(2)}, u32[]{:S(2)}) collective-permute-start(bf16[64,2048]{1,0:T(8,128)(2,1)S(1)} %constant_dynamic-update-slice_fusion.refs_1_), channel_id=1, source_target_pairs={{0,16},{8,72},{16,0},{24,88},{32,48},{40,104},{48,32},{56,120},{64... | collective-permute-start | bytes 786440 | tf_op jit(solution)/shard_map/ppermute | solution.py:497
  49.1 10.2 %collective-permute-start.12 = (bf16[32,2048]{1,0:T(8,128)(2,1)S(1)}, bf16[32,2048]{1,0:T(8,128)(2,1)S(1)}, u32[]{:S(2)}, u32[]{:S(2)}) collective-permute-start(bf16[32,2048]{1,0:T(8,128)(2,1)S(1)} %get-tuple-element.55), channel_id=1, source_target_pairs={{0,16},{8,72},{16,0},{24,88},{32,48},{40,104},{48,32},{56,120},{64... | collective-permute-start | bytes 393224 | tf_op jit(solution)/shard_map/ppermute | solution.py:497
  54.5 4.9 %collective-permute-start.11 = (bf16[32,2048]{1,0:T(8,128)(2,1)S(1)}, bf16[32,2048]{1,0:T(8,128)(2,1)S(1)}, u32[]{:S(2)}, u32[]{:S(2)}) collective-permute-start(bf16[32,2048]{1,0:T(8,128)(2,1)S(1)} %get-tuple-element.56), channel_id=1, source_target_pairs={{0,16},{8,72},{16,0},{24,88},{32,48},{40,104},{48,32},{56,120},{64... | collective-permute-start | bytes 393224 | tf_op jit(solution)/shard_map/ppermute | solution.py:497
  54.5 5.1 %collective-permute-start.17 = (bf16[32,2048]{1,0:T(8,128)(2,1)S(1)}, bf16[32,2048]{1,0:T(8,128)(2,1)S(1)}, u32[]{:S(2)}, u32[]{:S(2)}) collective-permute-start(bf16[32,2048]{1,0:T(8,128)(2,1)S(1)} %get-tuple-element.53), channel_id=1, source_target_pairs={{0,48},{8,200},{16,32},{24,216},{32,16},{40,232},{48,0},{56,248},{... | collective-permute-start | bytes 393224 | tf_op jit(solution)/shard_map/ppermute | solution.py:497
  56.1 5.3 %collective-permute-start.16 = (bf16[32,2048]{1,0:T(8,128)(2,1)S(1)}, bf16[32,2048]{1,0:T(8,128)(2,1)S(1)}, u32[]{:S(2)}, u32[]{:S(2)}) collective-permute-start(bf16[32,2048]{1,0:T(8,128)(2,1)S(1)} %get-tuple-element.54), channel_id=1, source_target_pairs={{0,48},{8,200},{16,32},{24,216},{32,16},{40,232},{48,0},{56,248},{... | collective-permute-start | bytes 393224 | tf_op jit(solution)/shard_map/ppermute | solution.py:497
  62.2 7.6 %collective-permute-start.21 = (bf16[64,512]{1,0:T(8,128)(2,1)S(1)}, bf16[64,512]{1,0:T(8,128)(2,1)S(1)}, u32[]{:S(2)}, u32[]{:S(2)}) collective-permute-start(bf16[64,512]{1,0:T(8,128)(2,1)S(1)} %get-tuple-element.43), channel_id=1, source_target_pairs={{0,1},{1,2},{2,3},{3,4},{4,5},{5,6},{6,7},{7,0},{8,9},{9,10},{10,1... | collective-permute-start | bytes 196616 | tf_op jit(solution)/shard_map/ppermute | solution.py:501
  63.9 5.9 %collective-permute-start.22 = (bf16[64,512]{1,0:T(8,128)(2,1)S(1)}, bf16[64,512]{1,0:T(8,128)(2,1)S(1)}, u32[]{:S(2)}, u32[]{:S(2)}) collective-permute-start(bf16[64,512]{1,0:T(8,128)(2,1)S(1)} %get-tuple-element.44), channel_id=1, source_target_pairs={{0,7},{1,0},{2,1},{3,2},{4,3},{5,4},{6,5},{7,6},{8,15},{9,8},{10,9... | collective-permute-start | bytes 196616 | tf_op jit(solution)/shard_map/ppermute | solution.py:501
  69.8 5.1 %collective-permute-start.23 = (bf16[64,1024]{1,0:T(8,128)(2,1)S(1)}, bf16[64,1024]{1,0:T(8,128)(2,1)S(1)}, u32[]{:S(2)}, u32[]{:S(2)}) collective-permute-start(bf16[64,1024]{1,0:T(8,128)(2,1)S(1)} %get-tuple-element.45), channel_id=1, source_target_pairs={{0,1},{1,2},{2,3},{3,4},{4,5},{5,6},{6,7},{7,0},{8,9},{9,10},{10,1... | collective-permute-start | bytes 393224 | tf_op jit(solution)/shard_map/ppermute | solution.py:501
  69.9 5.0 %collective-permute-start.24 = (bf16[64,1024]{1,0:T(8,128)(2,1)S(1)}, bf16[64,1024]{1,0:T(8,128)(2,1)S(1)}, u32[]{:S(2)}, u32[]{:S(2)}) collective-permute-start(bf16[64,1024]{1,0:T(8,128)(2,1)S(1)} %get-tuple-element.46), channel_id=1, source_target_pairs={{0,7},{1,0},{2,1},{3,2},{4,3},{5,4},{6,5},{7,6},{8,15},{9,8},{10,9... | collective-permute-start | bytes 393224 | tf_op jit(solution)/shard_map/ppermute | solution.py:501
  75.0 5.9 %collective-permute-start.25 = (bf16[64,1024]{1,0:T(8,128)(2,1)S(1)}, bf16[64,1024]{1,0:T(8,128)(2,1)S(1)}, u32[]{:S(2)}, u32[]{:S(2)}) collective-permute-start(bf16[64,1024]{1,0:T(8,128)(2,1)S(1)} %get-tuple-element.47), channel_id=1, source_target_pairs={{0,1},{1,2},{2,3},{3,4},{4,5},{5,6},{6,7},{7,0},{8,9},{9,10},{10,1... | collective-permute-start | bytes 393224 | tf_op jit(solution)/shard_map/ppermute | solution.py:501
  77.6 3.8 %collective-permute-start.26 = (bf16[64,1024]{1,0:T(8,128)(2,1)S(1)}, bf16[64,1024]{1,0:T(8,128)(2,1)S(1)}, u32[]{:S(2)}, u32[]{:S(2)}) collective-permute-start(bf16[64,1024]{1,0:T(8,128)(2,1)S(1)} %get-tuple-element.48), channel_id=1, source_target_pairs={{0,7},{1,0},{2,1},{3,2},{4,3},{5,4},{6,5},{7,6},{8,15},{9,8},{10,9... | collective-permute-start | bytes 393224 | tf_op jit(solution)/shard_map/ppermute | solution.py:501
  81.5 18.0 %collective-permute-start.27 = (bf16[64,1024]{1,0:T(8,128)(2,1)S(1)}, bf16[64,1024]{1,0:T(8,128)(2,1)S(1)}, u32[]{:S(2)}, u32[]{:S(2)}) collective-permute-start(bf16[64,1024]{1,0:T(8,128)(2,1)S(1)} %get-tuple-element.49), channel_id=1, source_target_pairs={{0,1},{1,2},{2,3},{3,4},{4,5},{5,6},{6,7},{7,0},{8,9},{9,10},{10,1... | collective-permute-start | bytes 393224 | tf_op jit(solution)/shard_map/ppermute | solution.py:501
  82.7 16.7 %collective-permute-start.28 = (bf16[64,1024]{1,0:T(8,128)(2,1)S(1)}, bf16[64,1024]{1,0:T(8,128)(2,1)S(1)}, u32[]{:S(2)}, u32[]{:S(2)}) collective-permute-start(bf16[64,1024]{1,0:T(8,128)(2,1)S(1)} %get-tuple-element.50), channel_id=1, source_target_pairs={{0,7},{1,0},{2,1},{3,2},{4,3},{5,4},{6,5},{7,6},{8,15},{9,8},{10,9... | collective-permute-start | bytes 393224 | tf_op jit(solution)/shard_map/ppermute | solution.py:501
  84.2 18.7 %collective-permute-start.30 = (bf16[4,16,128]{2,1,0:T(8,128)(2,1)S(1)}, bf16[4,16,128]{2,1,0:T(8,128)(2,1)S(1)}, u32[]{:S(2)}, u32[]{:S(2)}) collective-permute-start(bf16[4,16,128]{2,1,0:T(8,128)(2,1)S(1)} %pad_maximum_fusion.1), channel_id=1, source_target_pairs={{0,8},{8,0},{16,24},{24,16},{32,40},{40,32},{48,56},{56,48},{64,72... | collective-permute-start | bytes 49160 | tf_op jit(solution)/shard_map/ppermute | solution.py:480
  99.5 4.4 %collective-permute-start.29 = (bf16[64,512]{1,0:T(8,128)(2,1)S(1)}, bf16[64,512]{1,0:T(8,128)(2,1)S(1)}, u32[]{:S(2)}, u32[]{:S(2)}) collective-permute-start(bf16[64,512]{1,0:T(8,128)(2,1)S(1)} %get-tuple-element.52), channel_id=1, source_target_pairs={{0,8},{8,0},{16,24},{24,16},{32,40},{40,32},{48,56},{56,48},{64,72... | collective-permute-start | bytes 196616 | tf_op jit(solution)/shard_map/ppermute | solution.py:480

commit v5 on v4

--- a/solution.py
+++ b/solution.py
@@ -144,23 +144,25 @@
     )(place, q, prompt, table, length, new, pool)
 
 
-def regroup_body(place, a0, a1, a2, a3, same, other, far):
+def regroup_body(place, a0, a1, a2, a3, same, other, across):
     for i, a in enumerate((a0, a1, a2, a3)):
         same[4 * i : 4 * i + 4] = a[0:4]
         other[4 * i : 4 * i + 4] = a[4:8]
-        far[5 * i : 5 * i + 5] = a[13:18]
+        across[4 * i : 4 * i + 4] = a[4:8]
+        across[17 + 5 * i : 22 + 5 * i] = a[13:18]
 
         @pl.when(place[2] ^ (place[4] >> 1) == i)
         def _(a=a):
             same[16] = a[8]
             other[16] = a[8]
+            across[16] = a[8]
 
 
 def regroup(place, parts):
     out = jax.ShapeDtypeStruct((17, GROUP, DH), BF16)
     return pl.pallas_call(
         regroup_body,
-        out_shape=[out, out, jax.ShapeDtypeStruct((20, GROUP, DH), BF16)],
+        out_shape=[out, out, jax.ShapeDtypeStruct((37, GROUP, DH), BF16)],
         in_specs=[SMEM] + [VMEM] * 4,
         out_specs=[VMEM] * 3,
         compiler_params=params(),
@@ -262,7 +264,7 @@
     return pl.pallas_call(
         prefix_first_body,
         out_shape=[out, out, held, held],
-        in_specs=[VMEM, HBM, HBM],
+        in_specs=[VMEM, VMEM, VMEM],
         out_specs=[VMEM] * 4,
         scratch_shapes=[pltpu.SemaphoreType.DMA((2,))],
         compiler_params=params(24),
@@ -277,7 +279,7 @@
     x, y_high, z = place[2], place[3], place[4]
     theirs = join_tile(message[32], 32)
     near = [join_tile(s[17], 8) for s in (s0, s1, s2, s3)]
-    across = [join_tile(far[5 * i + 4], 8) for i in range(4)]
+    across = [join_tile(far[21 + 5 * i], 8) for i in range(4)]
     for g in range(2):
         for kx in range(4):
             for k in range(4):
@@ -291,7 +293,7 @@
                     s = (s0, s1, s2, s3)[kx][9 + k].astype(F32)
                     ls = jnp.broadcast_to(near[kx][:, k : k + 1], (GROUP, DH))
                 else:
-                    s = far[5 * kx + k].astype(F32)
+                    s = far[17 + 5 * kx + k].astype(F32)
                     ls = jnp.broadcast_to(across[kx][:, 4 + k : 5 + k], (GROUP, DH))
                 top = jnp.maximum(jnp.maximum(la, lb), ls)
                 ea, eb, es = jnp.exp(la - top), jnp.exp(lb - top), jnp.exp(ls - top)
@@ -356,73 +358,75 @@
 
 
 def last_body(*refs):
-    pieces, (w0, w1, first, second, up, down, keep) = refs[:-7], refs[-7:]
+    pieces, (w0, w1, first, second, up, down, up4, down4, keep) = refs[:-9], refs[-9:]
     block = jnp.concatenate([piece[...] for piece in pieces], axis=0)
     for side, weight in enumerate((w0, w1)):
         columns = slice(side * 512, side * 512 + 512)
         for d, chunk in enumerate(by_target(dot(block, weight[...]))):
             whole = jnp.concatenate([first[d, :, columns], second[d, :, columns], chunk], axis=0)
-            if d != 4:
-                keep[d, :, columns] = whole
+            if d in (0, 2, 6):
+                keep[(0, 2, 6).index(d), :, columns] = whole
+            elif d in (3, 1):
+                up[(3, 1).index(d), :, columns] = whole.astype(BF16)
+            elif d in (5, 7):
+                down[(5, 7).index(d), :, columns] = whole.astype(BF16)
             elif side == 0:
-                up[...] = whole.astype(BF16)
+                up4[...] = whole.astype(BF16)
             else:
-                down[...] = whole.astype(BF16)
+                down4[...] = whole.astype(BF16)
 
 
 def project_last(pieces, weights, first, second):
-    out = jax.ShapeDtypeStruct((64, 512), BF16)
+    pair = jax.ShapeDtypeStruct((2, 64, 1024), BF16)
+    half = jax.ShapeDtypeStruct((64, 512), BF16)
     return pl.pallas_call(
         last_body,
-        out_shape=[out, out, jax.ShapeDtypeStruct((8, 64, 1024), F32)],
+        out_shape=[pair, pair, half, half, jax.ShapeDtypeStruct((3, 64, 1024), F32)],
         in_specs=[VMEM] * (len(pieces) + 4),
-        out_specs=[VMEM] * 3,
+        out_specs=[VMEM] * 5,
         compiler_params=params(),
         name="project_last",
     )(*pieces, *weights, first, second)
 
 
-def step_body(near, keep, below, above, up, down):
-    low, high = keep.at[near], keep.at[8 - near]
-    if below.shape[1] == 512:
-        up[:, :512] = (low[:, :512] + below[...].astype(F32)).astype(BF16)
-        up[:, 512:] = low[:, 512:].astype(BF16)
-        down[:, :512] = high[:, :512].astype(BF16)
-        down[:, 512:] = (high[:, 512:] + above[...].astype(F32)).astype(BF16)
-    else:
-        up[...] = (low[...] + below[...].astype(F32)).astype(BF16)
-        down[...] = (high[...] + above[...].astype(F32)).astype(BF16)
-
-
-def step(near, keep, below, above):
+def middle_body(keep, below, above, below4, above4, up, down):
+    u = keep[1] + below[0].astype(F32)
+    up[:, :512] = (u[:, :512] + below4[...].astype(F32)).astype(BF16)
+    up[:, 512:] = u[:, 512:].astype(BF16)
+    d = keep[2] + above[0].astype(F32)
+    down[:, :512] = d[:, :512].astype(BF16)
+    down[:, 512:] = (d[:, 512:] + above4[...].astype(F32)).astype(BF16)
+
+
+def middle(keep, below, above, below4, above4):
     out = jax.ShapeDtypeStruct((64, 1024), BF16)
     return pl.pallas_call(
-        lambda *refs: step_body(near, *refs),
+        middle_body,
         out_shape=[out, out],
-        in_specs=[VMEM] * 3,
+        in_specs=[VMEM] * 5,
         out_specs=[VMEM] * 2,
         compiler_params=params(),
-        name="step",
-    )(keep, below, above)
-
-
-def total_body(keep, below, above, own, other):
-    for side, out in enumerate((own, other)):
-        columns = slice(side * 512, side * 512 + 512)
-        near = below[:, columns].astype(F32) + above[:, columns].astype(F32)
-        out[...] = (keep[0, :, columns] + near).astype(BF16)
-
-
-def total(keep, below, above):
+        name="middle",
+    )(keep, below, above, below4, above4)
+
+
+def total_body(keep, below, above, below2, above2, own, other):
+    near = keep[0] + below[1].astype(F32) + above[1].astype(F32)
+    whole = (near + below2[...].astype(F32) + above2[...].astype(F32)).astype(BF16)
+    own[...] = whole[:, :512]
+    other[...] = whole[:, 512:]
+
+
+def total(keep, below, above, below2, above2):
     out = jax.ShapeDtypeStruct((64, 512), BF16)
     return pl.pallas_call(
         total_body,
         out_shape=[out, out],
-        in_specs=[VMEM] * 3,
+        in_specs=[VMEM] * 5,
         out_specs=[VMEM] * 2,
         compiler_params=params(),
         name="total",
-    )(keep, below, above)
+    )(keep, below, above, below2, above2)
 
 
 def order_body(place, orders, pick):
@@ -441,7 +445,6 @@
     dy = (2 * (prompt & 1) + (block >> 1)) ^ y
     first = jnp.where(far == 0, dx, dy)
     second = jnp.where(far == 0, dy, dx)
-    first = jnp.where(first >= 2, 5 - first, first)
     second = jnp.where(second >= 2, 5 - second, second)
     source = ((far ^ core) * 16 + second * 4 + first) * 4 + k
     row = lax.broadcasted_iota(jnp.int32, (128, 128), 0)
@@ -513,34 +516,29 @@
 
     sent = local_parts(place, queries, prompt_of, page_table.T, suffix_len, new_kv, suffix_kv)
     by_x = [sent[0]] + [along_x(sent[k], k) for k in (1, 2, 3)]
-    same, other, far = regroup(place, by_x)
-    from1, from3, from2 = along_y(same, 1), along_y(other, 3), along_y(other, 2)
-    far = along_y(far, 2)
+    same, other, across = regroup(place, by_x)
+    from1, from3, from2 = along_y(same, 1), along_y(other, 3), along_y(across, 2)
 
     *own, kv0, kv1 = prefix_first(same, prefix_kv, prefix_other)
     message = along_y(prefix_send(from1, from3, kv0, kv1, from2), 1)
     cross = prefix_keep(from2, kv0, kv1)
-    attended = combine(place, own, cross, message, by_x, far)
+    attended = combine(place, own, cross, message, by_x, from2)
 
     orders = jnp.stack([same[16], from1[16], from2[16], from3[16]])
     orders = jnp.concatenate([orders, other_core(orders)], axis=0)
     pick = order_rows(place, orders)
 
-    next1 = turned(attended, 1, 0)
-    lower = jnp.concatenate([attended, next1], axis=0)
-    upper = jnp.concatenate([turned(attended, 3, 0), turned(next1, 3, 0)], axis=0)
-    low1, low3 = turned(lower, 1, 1), turned(lower, 3, 1)
-    high1, high3 = turned(upper, 1, 1), turned(upper, 3, 1)
-    low2 = [turned(low3[:32], 1, 1), turned(low3[32:], 1, 1)]
-    high2 = [turned(high1[:32], 3, 1), turned(high1[32:], 3, 1)]
-    first = project([[lower, upper]], weights)
-    second = project([[low1, high1], [low3, high3]], weights)
-    below, above, keep = project_last(low2 + high2, weights, first, second)
-
-    for near in (3, 2, 1):
-        below, above = along_z(below, 1), along_z(above, -1)
-        below, above = step(near, keep, below, above)
-    own, other = total(keep, along_z(below, 1), along_z(above, -1))
+    ring0 = jnp.concatenate([attended] + [turned(attended, k, 0) for k in (1, 2, 3)], axis=0)
+    ring1, ring3 = turned(ring0, 1, 1), turned(ring0, 3, 1)
+    ring2 = [turned(ring3[:64], 1, 1), turned(ring1[64:], 3, 1)]
+    first = project([[ring0]], weights)
+    second = project([[ring1], [ring3]], weights)
+    up, down, up4, down4, keep = project_last(ring2, weights, first, second)
+
+    below4, above4 = along_z(up4, 2), along_z(down4, -2)
+    below, above = along_z(up, 1), along_z(down, -1)
+    up2, down2 = middle(keep, below, above, below4, above4)
+    own, other = total(keep, below, above, along_z(up2, 2), along_z(down2, -2))
     return finish(own, other_core(other), pick)
 
 

time: 105 us -> 94.5 us (0.900)
  starting transfers between devices: 58.9 us -> 49.6 us
  waiting for transfers between devices: 23.6 us -> 22.4 us
  local copies, waits for them, and re-layouts: 2.83 us -> 1.64 us
  Pallas kernels: 19.2 us -> 20.3 us
    ppermute x12 -> x11, starting transfers between devices: 33.8 us -> 27.4 us  [along(): lax.ppermute(value, 'batch', [(i, i ^ k << shift) for i in range(BATCH)])]
    ppermute x8 -> x6, waiting for transfers between devices: 7.35 us -> 3.41 us  [along_z(): lax.ppermute(value, 'head', [(i, (i + k) % HEADS) for i in range(HEADS)])]
    ppermute x8 -> x6, starting transfers between devices: 14.4 us -> 12.9 us  [along_z(): lax.ppermute(value, 'head', [(i, (i + k) % HEADS) for i in range(HEADS)])]
    ppermute x11 -> x7, waiting for transfers between devices: 11.6 us -> 13 us  [turned(): return lax.ppermute(value, 'batch', pairs)]
    ppermute x12 -> x11, waiting for transfers between devices: 4.65 us -> 6 us  [along(): lax.ppermute(value, 'batch', [(i, i ^ k << shift) for i in range(BATCH)])]
    ppermute x11 -> x7, starting transfers between devices: 10.6 us -> 9.3 us  [turned(): return lax.ppermute(value, 'batch', pairs)]
    pallas_call x1, Pallas kernels: 2.34 us -> 3.58 us  [prefix_first(): pl.pallas_call(prefix_first_body, out_shape=[out, out, held, held], in_sp...]
    unnamed x11 -> x10, local copies, waits for them, and re-layouts: 2.13 us -> 0.9 us
  transfers between devices with their start and end apart: 31 -> 24, of which waited for: 14 -> 13; matrix products, arithmetic and copies ran while one was open for 1% -> 1% of each run, Pallas kernels for 17% -> 20%
where the time goes in v5:
time: 94.5 us; the launch traced here: 94.2 us
  starting transfers between devices  49.6 us (52%)
  waiting for transfers between devices  22.4 us (24%)
  Pallas kernels  20.3 us (21%)
  local copies, waits for them, and re-layouts  1.64 us (2%)
    ppermute x11, starting transfers between devices, along(): lax.ppermute(value, 'batch', [(i, i ^ k << shift) for i in range(BATCH)])  27.4 us
    ppermute x7, waiting for transfers between devices, turned(): return lax.ppermute(value, 'batch', pairs)  13 us
    ppermute x6, starting transfers between devices, along_z(): lax.ppermute(value, 'head', [(i, (i + k) % HEADS) for i in range(HEADS)])  12.9 us
    ppermute x7, starting transfers between devices, turned(): return lax.ppermute(value, 'batch', pairs)  9.3 us
    ppermute x11, waiting for transfers between devices, along(): lax.ppermute(value, 'batch', [(i, i ^ k << shift) for i in range(BATCH)])  6 us
    pallas_call x1, Pallas kernels, local_parts(): pl.pallas_call(local_body, out_shape=[out] * 4, in_specs=[SMEM] + [HBM] *...  4.22 us
    pallas_call x1, Pallas kernels, prefix_send(): pl.pallas_call(prefix_send_body, out_shape=jax.ShapeDtypeStruct((33, GROU...  4.14 us
    pallas_call x1, Pallas kernels, prefix_first(): pl.pallas_call(prefix_first_body, out_shape=[out, out, held, held], in_sp...  3.58 us
  transfers between devices with their start and end apart: 24, of which 13 were waited for; matrix products, arithmetic and copies ran while one was open for 1% of the time, Pallas kernels for 20%

profile of v5, /device:TPU:1, one launch (start us, length us, event | category | flops | bytes accessed | tf_op | source)
XLA Modules:
  0.0 94.2 jit_solution(9924851085020702517)
XLA Ops:
  0.0 3.2 %collective-permute-start.3 = (bf16[2,2048,128]{2,1,0:T(8,128)(2,1)}, bf16[2,2048,128]{2,1,0:T(8,128)(2,1)}, u32[]{:S(2)}, u32[]{:S(2)}) collective-permute-start(bf16[2,2048,128]{2,1,0:T(8,128)(2,1)} %kv0_in.1), channel_id=1, source_target_pairs={{0,8},{8,0},{16,24},{24,16},{32,40},{40,32},{48,56},{56,48},{64,72... | collective-permute-start | bytes 3145736 | tf_op jit(solution)/shard_map/ppermute | solution.py:483
  3.2 0.0 collective-permute-start.15
  3.2 0.7 stack.34.place
  3.9 4.2 %local_parts.1 = (bf16[18,16,128]{2,1,0:T(8,128)(2,1)}, bf16[18,16,128]{2,1,0:T(8,128)(2,1)}, bf16[18,16,128]{2,1,0:T(8,128)(2,1)}, bf16[18,16,128]{2,1,0:T(8,128)(2,1)}) custom-call(s32[7]{0:T(128)} %stack.34.place, bf16[32,2048]{1,0:T(8,128)(2,1)} %q_in.1, s32[32]{0:T(128)} %prompt_in.1, s32[8,32]{1,0:T(8,128)} %bitcast.8, s32[32]{0:T(128)} %length_in.1, ...), custom_call_target="tpu_custom_call" | custom-call | tf_op jit(solution)/shard_map/local_parts/pallas_call | solution.py:124
  8.1 0.1 collective-permute-start
  8.2 2.0 %collective-permute-start.1 = (bf16[18,16,128]{2,1,0:T(8,128)(2,1)}, bf16[18,16,128]{2,1,0:T(8,128)(2,1)S(1)}, u32[]{:S(2)}, u32[]{:S(2)}) collective-permute-start(bf16[18,16,128]{2,1,0:T(8,128)(2,1)} %get-tuple-element.29), channel_id=1, source_target_pairs={{0,128},{8,136},{16,144},{24,152},{32,160},{40,168},{48,176},{56,1... | collective-permute-start | bytes 221192 | tf_op jit(solution)/shard_map/ppermute | solution.py:483
  10.2 1.9 %collective-permute-start.2 = (bf16[18,16,128]{2,1,0:T(8,128)(2,1)}, bf16[18,16,128]{2,1,0:T(8,128)(2,1)S(1)}, u32[]{:S(2)}, u32[]{:S(2)}) collective-permute-start(bf16[18,16,128]{2,1,0:T(8,128)(2,1)} %get-tuple-element.30), channel_id=1, source_target_pairs={{0,192},{8,200},{16,208},{24,216},{32,224},{40,232},{48,240},{56,2... | collective-permute-start | bytes 221192 | tf_op jit(solution)/shard_map/ppermute | solution.py:483
  12.1 0.0 collective-permute-done.a1.s1
  12.1 2.2 %collective-permute-done.1.a2.s2 = bf16[18,16,128]{2,1,0:T(8,128)(2,1)S(1)} collective-permute-done((bf16[18,16,128]{2,1,0:T(8,128)(2,1)}, bf16[18,16,128]{2,1,0:T(8,128)(2,1)S(1)}, u32[]{:S(2)}, u32[]{:S(2)}) %collective-permute-start.1) | collective-permute-done | bytes 73760 | tf_op jit(solution)/shard_map/ppermute | solution.py:483
  14.3 1.1 %collective-permute-done.2.a3.s3 = bf16[18,16,128]{2,1,0:T(8,128)(2,1)S(1)} collective-permute-done((bf16[18,16,128]{2,1,0:T(8,128)(2,1)}, bf16[18,16,128]{2,1,0:T(8,128)(2,1)S(1)}, u32[]{:S(2)}, u32[]{:S(2)}) %collective-permute-start.2) | collective-permute-done | bytes 73760 | tf_op jit(solution)/shard_map/ppermute | solution.py:483
  15.5 0.9 copy-done.2
  16.3 0.6 regroup.1
  16.9 2.9 %collective-permute-start.4 = (bf16[37,16,128]{2,1,0:T(8,128)(2,1)S(1)}, bf16[37,16,128]{2,1,0:T(8,128)(2,1)S(1)}, u32[]{:S(2)}, u32[]{:S(2)}) collective-permute-start(bf16[37,16,128]{2,1,0:T(8,128)(2,1)S(1)} %get-tuple-element.34), channel_id=1, source_target_pairs={{0,32},{8,40},{16,48},{24,56},{32,0},{40,8},{48,16},{56,24},{64,96... | collective-permute-start | bytes 454664 | tf_op jit(solution)/shard_map/ppermute | solution.py:483
  19.8 0.8 collective-permute-start.6
  20.6 0.0 collective-permute-start.5
  20.6 0.0 collective-permute-done.3.kv1_in
  20.6 3.6 %prefix_first.1 = (f32[16,16,128]{2,1,0:T(8,128)S(1)}, f32[16,16,128]{2,1,0:T(8,128)S(1)}, bf16[2,2048,128]{2,1,0:T(8,128)(2,1)S(1)}, bf16[2,2048,128]{2,1,0:T(8,128)(2,1)S(1)}) custom-call(bf16[17,16,128]{2,1,0:T(8,128)(2,1)S(1)} %get-tuple-element.31.q, bf16[2,2048,128]{2,1,0:T(8,128)(2,1)S(1)} %copy-done.1, ...), custom_call_target="tpu_custom_call" | custom-call | flops 536870912 | bytes 2500000 | tf_op jit(solution)/shard_map/prefix_first/pallas_call | solution.py:264
  24.2 1.1 %collective-permute-done.6.qb = bf16[17,16,128]{2,1,0:T(8,128)(2,1)S(1)} collective-permute-done((bf16[17,16,128]{2,1,0:T(8,128)(2,1)S(1)}, bf16[17,16,128]{2,1,0:T(8,128)(2,1)S(1)}, u32[]{:S(2)}, u32[]{:S(2)}) %collective-permute-start.6) | collective-permute-done | bytes 69664 | tf_op jit(solution)/shard_map/ppermute | solution.py:483
  25.3 0.0 collective-permute-done.5.qa
  25.3 0.0 collective-permute-done.4.q.later.far
  25.3 4.1 %prefix_send.1 = bf16[33,16,128]{2,1,0:T(8,128)(2,1)S(1)} custom-call(bf16[17,16,128]{2,1,0:T(8,128)(2,1)S(1)} %collective-permute-done.5.qa, bf16[17,16,128]{2,1,0:T(8,128)(2,1)S(1)} %collective-permute-done.6.qb, bf16[2,2048,128]{2,1,0:T(8,128)(2,1)S(1)} %get-tuple-element.35.kv0, bf16[2,2048,128]{2,1,0:T(8,128)(2,1)S(1)} %get-tuple-element.36.kv1, ...), custom_call_target="tpu_custom_call" | custom-call | flops 1073741824 | bytes 2500000 | tf_op jit(solution)/shard_map/prefix_send/pallas_call | solution.py:237
  29.5 0.0 copy-start.3
  29.5 0.7 collective-permute-start.7
  30.1 2.2 %prefix_keep.1 = (f32[16,16,128]{2,1,0:T(8,128)S(1)}, f32[16,16,128]{2,1,0:T(8,128)S(1)}) custom-call(bf16[37,16,128]{2,1,0:T(8,128)(2,1)S(1)} %collective-permute-done.4.q.later.far, bf16[2,2048,128]{2,1,0:T(8,128)(2,1)S(1)} %get-tuple-element.35.kv0, bf16[2,2048,128]{2,1,0:T(8,128)(2,1)S(1)} %get-tuple-element.36.kv1), custom_call_target="tpu_custom_call" | custom-call | flops 536870912 | bytes 2500000 | tf_op jit(solution)/shard_map/prefix_keep/pallas_call | solution.py:250
  32.3 0.0 copy-start
  32.3 1.3 %collective-permute-done.7.message = bf16[33,16,128]{2,1,0:T(8,128)(2,1)S(1)} collective-permute-done((bf16[33,16,128]{2,1,0:T(8,128)(2,1)S(1)}, bf16[33,16,128]{2,1,0:T(8,128)(2,1)S(1)}, u32[]{:S(2)}, u32[]{:S(2)}) %collective-permute-start.7) | collective-permute-done | bytes 135200 | tf_op jit(solution)/shard_map/ppermute | solution.py:483
  33.6 1.2 %combine.1 = bf16[32,2048]{1,0:T(8,128)(2,1)S(1)} custom-call(s32[7]{0:T(128)S(1)} %copy-done.4, f32[16,16,128]{2,1,0:T(8,128)S(1)} %get-tuple-element.32.own, f32[16,16,128]{2,1,0:T(8,128)S(1)} %get-tuple-element.33.own_masses, f32[16,16,128]{2,1,0:T(8,128)S(1)} %get-tuple-element.37.cross, f32[16,16,128]{2,1,0:T(8,128)S(1)} %get-tuple-element.38.cross_masses, ...), custom_call_target="tpu_custom_call" | custom-call | tf_op jit(solution)/shard_map/combine/pallas_call | solution.py:308
  34.8 1.3 %collective-permute-start.10 = (bf16[32,2048]{1,0:T(8,128)(2,1)S(1)}, bf16[32,2048]{1,0:T(8,128)(2,1)S(1)}, u32[]{:S(2)}, u32[]{:S(2)}) collective-permute-start(bf16[32,2048]{1,0:T(8,128)(2,1)S(1)} %combine.1), channel_id=1, source_target_pairs={{0,192},{8,56},{16,208},{24,40},{32,224},{40,24},{48,240},{56,8},{... | collective-permute-start | bytes 393224 | tf_op jit(solution)/shard_map/ppermute | solution.py:500
  36.1 1.0 %collective-permute-start.9 = (bf16[32,2048]{1,0:T(8,128)(2,1)S(1)}, bf16[32,2048]{1,0:T(8,128)(2,1)S(1)}, u32[]{:S(2)}, u32[]{:S(2)}) collective-permute-start(bf16[32,2048]{1,0:T(8,128)(2,1)S(1)} %combine.1), channel_id=1, source_target_pairs={{0,128},{8,40},{16,144},{24,56},{32,160},{40,8},{48,176},{56,24},{... | collective-permute-start | bytes 393224 | tf_op jit(solution)/shard_map/ppermute | solution.py:500
  37.1 1.1 %collective-permute-start.8 = (bf16[32,2048]{1,0:T(8,128)(2,1)S(1)}, bf16[32,2048]{1,0:T(8,128)(2,1)S(1)}, u32[]{:S(2)}, u32[]{:S(2)}) collective-permute-start(bf16[32,2048]{1,0:T(8,128)(2,1)S(1)} %combine.1), channel_id=1, source_target_pairs={{0,64},{8,24},{16,80},{24,8},{32,96},{40,56},{48,112},{56,40},{64,... | collective-permute-start | bytes 393224 | tf_op jit(solution)/shard_map/ppermute | solution.py:500
  38.1 1.8 %collective-permute-done.10 = bf16[32,2048]{1,0:T(8,128)(2,1)S(1)} collective-permute-done((bf16[32,2048]{1,0:T(8,128)(2,1)S(1)}, bf16[32,2048]{1,0:T(8,128)(2,1)S(1)}, u32[]{:S(2)}, u32[]{:S(2)}) %collective-permute-start.10) | collective-permute-done | bytes 131104 | tf_op jit(solution)/shard_map/ppermute | solution.py:500
  39.9 1.5 %collective-permute-done.9 = bf16[32,2048]{1,0:T(8,128)(2,1)S(1)} collective-permute-done((bf16[32,2048]{1,0:T(8,128)(2,1)S(1)}, bf16[32,2048]{1,0:T(8,128)(2,1)S(1)}, u32[]{:S(2)}, u32[]{:S(2)}) %collective-permute-start.9) | collective-permute-done | bytes 131104 | tf_op jit(solution)/shard_map/ppermute | solution.py:500
  41.4 0.5 collective-permute-done.8
  41.9 1.9 %collective-permute-start.13 = (bf16[128,2048]{1,0:T(8,128)(2,1)S(1)}, bf16[128,2048]{1,0:T(8,128)(2,1)S(1)}, u32[]{:S(2)}, u32[]{:S(2)}) collective-permute-start(bf16[128,2048]{1,0:T(8,128)(2,1)S(1)} %pad_maximum_fusion.refs_0_), channel_id=1, source_target_pairs={{0,16},{8,72},{16,0},{24,88},{32,48},{40,104},{48,32},{56,120},{64... | collective-permute-start | bytes 1572872 | tf_op jit(solution)/shard_map/ppermute | solution.py:500
  43.8 1.8 %collective-permute-start.11 = (bf16[128,2048]{1,0:T(8,128)(2,1)S(1)}, bf16[128,2048]{1,0:T(8,128)(2,1)S(1)}, u32[]{:S(2)}, u32[]{:S(2)}) collective-permute-start(bf16[128,2048]{1,0:T(8,128)(2,1)S(1)} %pad_maximum_fusion.refs_0_), channel_id=1, source_target_pairs={{0,48},{8,200},{16,32},{24,216},{32,16},{40,232},{48,0},{56,248},{... | collective-permute-start | bytes 1572872 | tf_op jit(solution)/shard_map/ppermute | solution.py:500
  45.6 6.1 %collective-permute-done.13.refs_0_ = bf16[128,2048]{1,0:T(8,128)(2,1)S(1)} collective-permute-done((bf16[128,2048]{1,0:T(8,128)(2,1)S(1)}, bf16[128,2048]{1,0:T(8,128)(2,1)S(1)}, u32[]{:S(2)}, u32[]{:S(2)}) %collective-permute-start.13) | collective-permute-done | bytes 524320 | tf_op jit(solution)/shard_map/ppermute | solution.py:500
  51.7 2.2 %collective-permute-start.14 = (bf16[64,2048]{1,0:T(8,128)(2,1)S(1)}, bf16[64,2048]{1,0:T(8,128)(2,1)S(1)}, u32[]{:S(2)}, u32[]{:S(2)}) collective-permute-start(bf16[64,2048]{1,0:T(8,128)(2,1)S(1)} %slice.25), channel_id=1, source_target_pairs={{0,48},{8,200},{16,32},{24,216},{32,16},{40,232},{48,0},{56,248},{... | collective-permute-start | bytes 786440 | tf_op jit(solution)/shard_map/ppermute | solution.py:500
  53.9 0.0 collective-permute-done.11.refs_1_
  53.9 0.1 collective-permute-start.12
  54.1 0.0 collective-permute-done.15.refs_2_.refs_3_
  54.1 0.7 project.2.refs_4_
  54.8 1.3 %project.3.refs_5_ = f32[8,32,1024]{2,1,0:T(8,128)S(1)} custom-call(bf16[128,2048]{1,0:T(8,128)(2,1)S(1)} %collective-permute-done.13.refs_0_, bf16[128,2048]{1,0:T(8,128)(2,1)S(1)} %collective-permute-done.11.refs_1_, bf16[2048,512]{1,0:T(8,128)(2,1)S(1)} %copy-done, bf16[2048,512]{1,0:T(8,128)(2,1)S(1)} %collective-permute-done.15.refs_2_.refs_3_), custom_call_target="tpu_custom_call" | custom-call | flops 1073741824 | bytes 4500000 | tf_op jit(solution)/shard_map/project/pallas_call | solution.py:347
  56.1 2.4 %collective-permute-done.14.refs_1_ = bf16[64,2048]{1,0:T(8,128)(2,1)S(1)} collective-permute-done((bf16[64,2048]{1,0:T(8,128)(2,1)S(1)}, bf16[64,2048]{1,0:T(8,128)(2,1)S(1)}, u32[]{:S(2)}, u32[]{:S(2)}) %collective-permute-start.14) | collective-permute-done | bytes 262176 | tf_op jit(solution)/shard_map/ppermute | solution.py:500
  58.5 0.7 collective-permute-done.12.refs_0_
  59.3 0.8 project_last.1
  60.0 2.0 %collective-permute-start.16 = (bf16[2,64,1024]{2,1,0:T(8,128)(2,1)S(1)}, bf16[2,64,1024]{2,1,0:T(8,128)(2,1)S(1)}, u32[]{:S(2)}, u32[]{:S(2)}) collective-permute-start(bf16[2,64,1024]{2,1,0:T(8,128)(2,1)S(1)} %get-tuple-element.41), channel_id=1, source_target_pairs={{0,1},{1,2},{2,3},{3,4},{4,5},{5,6},{6,7},{7,0},{8,9},{9,10},{10,1... | collective-permute-start | bytes 786440 | tf_op jit(solution)/shard_map/ppermute | solution.py:504
  62.0 3.7 %collective-permute-start.17 = (bf16[2,64,1024]{2,1,0:T(8,128)(2,1)S(1)}, bf16[2,64,1024]{2,1,0:T(8,128)(2,1)S(1)}, u32[]{:S(2)}, u32[]{:S(2)}) collective-permute-start(bf16[2,64,1024]{2,1,0:T(8,128)(2,1)S(1)} %get-tuple-element.42), channel_id=1, source_target_pairs={{0,7},{1,0},{2,1},{3,2},{4,3},{5,4},{6,5},{7,6},{8,15},{9,8},{10,9... | collective-permute-start | bytes 786440 | tf_op jit(solution)/shard_map/ppermute | solution.py:504
  65.8 0.0 collective-permute-start.18
  65.8 3.6 %collective-permute-start.19 = (bf16[64,512]{1,0:T(8,128)(2,1)S(1)}, bf16[64,512]{1,0:T(8,128)(2,1)S(1)}, u32[]{:S(2)}, u32[]{:S(2)}) collective-permute-start(bf16[64,512]{1,0:T(8,128)(2,1)S(1)} %get-tuple-element.44), channel_id=1, source_target_pairs={{0,6},{1,7},{2,0},{3,1},{4,2},{5,3},{6,4},{7,5},{8,14},{9,15},{10,... | collective-permute-start | bytes 196616 | tf_op jit(solution)/shard_map/ppermute | solution.py:504
  69.3 2.5 %collective-permute-done.18.below4 = bf16[64,512]{1,0:T(8,128)(2,1)S(1)} collective-permute-done((bf16[64,512]{1,0:T(8,128)(2,1)S(1)}, bf16[64,512]{1,0:T(8,128)(2,1)S(1)}, u32[]{:S(2)}, u32[]{:S(2)}) %collective-permute-start.18) | collective-permute-done | bytes 65568 | tf_op jit(solution)/shard_map/ppermute | solution.py:504
  71.8 0.9 collective-permute-done.19.above4
  72.7 0.0 collective-permute-done.16.below
  72.7 0.0 collective-permute-done.17.above
  72.7 0.1 middle.1
  72.8 2.8 %collective-permute-start.20 = (bf16[64,1024]{1,0:T(8,128)(2,1)S(1)}, bf16[64,1024]{1,0:T(8,128)(2,1)S(1)}, u32[]{:S(2)}, u32[]{:S(2)}) collective-permute-start(bf16[64,1024]{1,0:T(8,128)(2,1)S(1)} %get-tuple-element.45), channel_id=1, source_target_pairs={{0,2},{1,3},{2,4},{3,5},{4,6},{5,7},{6,0},{7,1},{8,10},{9,11},{10,... | collective-permute-start | bytes 393224 | tf_op jit(solution)/shard_map/ppermute | solution.py:504
  75.7 0.8 collective-permute-start.21
  76.5 10.3 %collective-permute-start.23 = (bf16[4,16,128]{2,1,0:T(8,128)(2,1)S(1)}, bf16[4,16,128]{2,1,0:T(8,128)(2,1)S(1)}, u32[]{:S(2)}, u32[]{:S(2)}) collective-permute-start(bf16[4,16,128]{2,1,0:T(8,128)(2,1)S(1)} %pad_maximum_fusion.1), channel_id=1, source_target_pairs={{0,8},{8,0},{16,24},{24,16},{32,40},{40,32},{48,56},{56,48},{64,72... | collective-permute-start | bytes 49160 | tf_op jit(solution)/shard_map/ppermute | solution.py:483
  86.7 0.0 collective-permute-done.20.below2
  86.8 0.1 total.1
  86.8 5.6 %collective-permute-start.22 = (bf16[64,512]{1,0:T(8,128)(2,1)S(1)}, bf16[64,512]{1,0:T(8,128)(2,1)S(1)}, u32[]{:S(2)}, u32[]{:S(2)}) collective-permute-start(bf16[64,512]{1,0:T(8,128)(2,1)S(1)} %get-tuple-element.48), channel_id=1, source_target_pairs={{0,8},{8,0},{16,24},{24,16},{32,40},{40,32},{48,56},{56,48},{64,72... | collective-permute-start | bytes 196616 | tf_op jit(solution)/shard_map/ppermute | solution.py:483
  92.4 0.0 collective-permute-done.23
  92.4 0.6 order_rows.1.pick
  93.1 0.2 collective-permute-done.22.other
  93.3 0.9 finish.1
  (17 shorter events, 0.1 us)
Async XLA Ops:
  0.0 20.6 %copy-start.1 = (bf16[2,2048,128]{2,1,0:T(8,128)(2,1)S(1)}, bf16[2,2048,128]{2,1,0:T(8,128)(2,1)}, u32[]{:S(2)}) copy-start(bf16[2,2048,128]{2,1,0:T(8,128)(2,1)} %kv0_in.1) | copy-start | bytes 3145732
  0.0 20.6 %collective-permute-start.3 = (bf16[2,2048,128]{2,1,0:T(8,128)(2,1)}, bf16[2,2048,128]{2,1,0:T(8,128)(2,1)}, u32[]{:S(2)}, u32[]{:S(2)}) collective-permute-start(bf16[2,2048,128]{2,1,0:T(8,128)(2,1)} %kv0_in.1), channel_id=1, source_target_pairs={{0,8},{8,0},{16,24},{24,16},{32,40},{40,32},{48,56},{56,48},{64,72... | collective-permute-start | bytes 3145736 | tf_op jit(solution)/shard_map/ppermute | solution.py:483
  3.2 50.8 %collective-permute-start.15 = (bf16[2048,512]{1,0:T(8,128)(2,1)}, bf16[2048,512]{1,0:T(8,128)(2,1)S(1)}, u32[]{:S(2)}, u32[]{:S(2)}) collective-permute-start(bf16[2048,512]{1,0:T(8,128)(2,1)} %refs_2_.3), channel_id=1, source_target_pairs={{0,8},{8,0},{16,24},{24,16},{32,40},{40,32},{48,56},{56,48},{64,72... | collective-permute-start | bytes 6291464 | tf_op jit(solution)/shard_map/ppermute | solution.py:483
  3.9 11.5 %copy-start.4 = (s32[7]{0:T(128)S(1)}, s32[7]{0:T(128)}, u32[]{:S(2)}) copy-start(s32[7]{0:T(128)} %stack.34.place) | copy-start | bytes 88
  8.1 3.9 %collective-permute-start = (bf16[18,16,128]{2,1,0:T(8,128)(2,1)}, bf16[18,16,128]{2,1,0:T(8,128)(2,1)S(1)}, u32[]{:S(2)}, u32[]{:S(2)}) collective-permute-start(bf16[18,16,128]{2,1,0:T(8,128)(2,1)} %get-tuple-element.28), channel_id=1, source_target_pairs={{0,64},{8,72},{16,80},{24,88},{32,96},{40,104},{48,112},{56,120},{... | collective-permute-start | bytes 221192 | tf_op jit(solution)/shard_map/ppermute | solution.py:483
  8.2 6.1 %collective-permute-start.1 = (bf16[18,16,128]{2,1,0:T(8,128)(2,1)}, bf16[18,16,128]{2,1,0:T(8,128)(2,1)S(1)}, u32[]{:S(2)}, u32[]{:S(2)}) collective-permute-start(bf16[18,16,128]{2,1,0:T(8,128)(2,1)} %get-tuple-element.29), channel_id=1, source_target_pairs={{0,128},{8,136},{16,144},{24,152},{32,160},{40,168},{48,176},{56,1... | collective-permute-start | bytes 221192 | tf_op jit(solution)/shard_map/ppermute | solution.py:483
  10.2 5.2 %collective-permute-start.2 = (bf16[18,16,128]{2,1,0:T(8,128)(2,1)}, bf16[18,16,128]{2,1,0:T(8,128)(2,1)S(1)}, u32[]{:S(2)}, u32[]{:S(2)}) collective-permute-start(bf16[18,16,128]{2,1,0:T(8,128)(2,1)} %get-tuple-element.30), channel_id=1, source_target_pairs={{0,192},{8,200},{16,208},{24,216},{32,224},{40,232},{48,240},{56,2... | collective-permute-start | bytes 221192 | tf_op jit(solution)/shard_map/ppermute | solution.py:483
  15.4 0.9 copy-start.2
  16.9 8.4 %collective-permute-start.4 = (bf16[37,16,128]{2,1,0:T(8,128)(2,1)S(1)}, bf16[37,16,128]{2,1,0:T(8,128)(2,1)S(1)}, u32[]{:S(2)}, u32[]{:S(2)}) collective-permute-start(bf16[37,16,128]{2,1,0:T(8,128)(2,1)S(1)} %get-tuple-element.34), channel_id=1, source_target_pairs={{0,32},{8,40},{16,48},{24,56},{32,0},{40,8},{48,16},{56,24},{64,96... | collective-permute-start | bytes 454664 | tf_op jit(solution)/shard_map/ppermute | solution.py:483
  19.8 5.5 %collective-permute-start.6 = (bf16[17,16,128]{2,1,0:T(8,128)(2,1)S(1)}, bf16[17,16,128]{2,1,0:T(8,128)(2,1)S(1)}, u32[]{:S(2)}, u32[]{:S(2)}) collective-permute-start(bf16[17,16,128]{2,1,0:T(8,128)(2,1)S(1)} %get-tuple-element.39), channel_id=1, source_target_pairs={{0,48},{8,56},{16,32},{24,40},{32,16},{40,24},{48,0},{56,8},{64,11... | collective-permute-start | bytes 208904 | tf_op jit(solution)/shard_map/ppermute | solution.py:483
  20.6 4.7 %collective-permute-start.5 = (bf16[17,16,128]{2,1,0:T(8,128)(2,1)S(1)}, bf16[17,16,128]{2,1,0:T(8,128)(2,1)S(1)}, u32[]{:S(2)}, u32[]{:S(2)}) collective-permute-start(bf16[17,16,128]{2,1,0:T(8,128)(2,1)S(1)} %get-tuple-element.31.q), channel_id=1, source_target_pairs={{0,16},{8,24},{16,0},{24,8},{32,48},{40,56},{48,32},{56,40},{64,80... | collective-permute-start | bytes 208904 | tf_op jit(solution)/shard_map/ppermute | solution.py:483
  29.5 4.1 %copy-start.3 = (bf16[18,16,128]{2,1,0:T(8,128)(2,1)S(1)}, bf16[18,16,128]{2,1,0:T(8,128)(2,1)}, u32[]{:S(2)}) copy-start(bf16[18,16,128]{2,1,0:T(8,128)(2,1)} %get-tuple-element.27.a0.s0) | copy-start | bytes 221188
  29.5 4.1 %collective-permute-start.7 = (bf16[33,16,128]{2,1,0:T(8,128)(2,1)S(1)}, bf16[33,16,128]{2,1,0:T(8,128)(2,1)S(1)}, u32[]{:S(2)}, u32[]{:S(2)}) collective-permute-start(bf16[33,16,128]{2,1,0:T(8,128)(2,1)S(1)} %prefix_send.1), channel_id=1, source_target_pairs={{0,16},{8,24},{16,0},{24,8},{32,48},{40,56},{48,32},{56,40},{64,80... | collective-permute-start | bytes 405512 | tf_op jit(solution)/shard_map/ppermute | solution.py:483
  32.3 21.8 %copy-start = (bf16[2048,512]{1,0:T(8,128)(2,1)S(1)}, bf16[2048,512]{1,0:T(8,128)(2,1)}, u32[]{:S(2)}) copy-start(bf16[2048,512]{1,0:T(8,128)(2,1)} %refs_2_.3) | copy-start | bytes 6291460
  34.8 5.1 %collective-permute-start.10 = (bf16[32,2048]{1,0:T(8,128)(2,1)S(1)}, bf16[32,2048]{1,0:T(8,128)(2,1)S(1)}, u32[]{:S(2)}, u32[]{:S(2)}) collective-permute-start(bf16[32,2048]{1,0:T(8,128)(2,1)S(1)} %combine.1), channel_id=1, source_target_pairs={{0,192},{8,56},{16,208},{24,40},{32,224},{40,24},{48,240},{56,8},{... | collective-permute-start | bytes 393224 | tf_op jit(solution)/shard_map/ppermute | solution.py:500
  36.1 5.3 %collective-permute-start.9 = (bf16[32,2048]{1,0:T(8,128)(2,1)S(1)}, bf16[32,2048]{1,0:T(8,128)(2,1)S(1)}, u32[]{:S(2)}, u32[]{:S(2)}) collective-permute-start(bf16[32,2048]{1,0:T(8,128)(2,1)S(1)} %combine.1), channel_id=1, source_target_pairs={{0,128},{8,40},{16,144},{24,56},{32,160},{40,8},{48,176},{56,24},{... | collective-permute-start | bytes 393224 | tf_op jit(solution)/shard_map/ppermute | solution.py:500
  37.1 4.8 %collective-permute-start.8 = (bf16[32,2048]{1,0:T(8,128)(2,1)S(1)}, bf16[32,2048]{1,0:T(8,128)(2,1)S(1)}, u32[]{:S(2)}, u32[]{:S(2)}) collective-permute-start(bf16[32,2048]{1,0:T(8,128)(2,1)S(1)} %combine.1), channel_id=1, source_target_pairs={{0,64},{8,24},{16,80},{24,8},{32,96},{40,56},{48,112},{56,40},{64,... | collective-permute-start | bytes 393224 | tf_op jit(solution)/shard_map/ppermute | solution.py:500
  41.9 9.7 %collective-permute-start.13 = (bf16[128,2048]{1,0:T(8,128)(2,1)S(1)}, bf16[128,2048]{1,0:T(8,128)(2,1)S(1)}, u32[]{:S(2)}, u32[]{:S(2)}) collective-permute-start(bf16[128,2048]{1,0:T(8,128)(2,1)S(1)} %pad_maximum_fusion.refs_0_), channel_id=1, source_target_pairs={{0,16},{8,72},{16,0},{24,88},{32,48},{40,104},{48,32},{56,120},{64... | collective-permute-start | bytes 1572872 | tf_op jit(solution)/shard_map/ppermute | solution.py:500
  43.8 10.1 %collective-permute-start.11 = (bf16[128,2048]{1,0:T(8,128)(2,1)S(1)}, bf16[128,2048]{1,0:T(8,128)(2,1)S(1)}, u32[]{:S(2)}, u32[]{:S(2)}) collective-permute-start(bf16[128,2048]{1,0:T(8,128)(2,1)S(1)} %pad_maximum_fusion.refs_0_), channel_id=1, source_target_pairs={{0,48},{8,200},{16,32},{24,216},{32,16},{40,232},{48,0},{56,248},{... | collective-permute-start | bytes 1572872 | tf_op jit(solution)/shard_map/ppermute | solution.py:500
  51.7 6.8 %collective-permute-start.14 = (bf16[64,2048]{1,0:T(8,128)(2,1)S(1)}, bf16[64,2048]{1,0:T(8,128)(2,1)S(1)}, u32[]{:S(2)}, u32[]{:S(2)}) collective-permute-start(bf16[64,2048]{1,0:T(8,128)(2,1)S(1)} %slice.25), channel_id=1, source_target_pairs={{0,48},{8,200},{16,32},{24,216},{32,16},{40,232},{48,0},{56,248},{... | collective-permute-start | bytes 786440 | tf_op jit(solution)/shard_map/ppermute | solution.py:500
  53.9 5.3 %collective-permute-start.12 = (bf16[64,2048]{1,0:T(8,128)(2,1)S(1)}, bf16[64,2048]{1,0:T(8,128)(2,1)S(1)}, u32[]{:S(2)}, u32[]{:S(2)}) collective-permute-start(bf16[64,2048]{1,0:T(8,128)(2,1)S(1)} %slice.24), channel_id=1, source_target_pairs={{0,16},{8,72},{16,0},{24,88},{32,48},{40,104},{48,32},{56,120},{64... | collective-permute-start | bytes 786440 | tf_op jit(solution)/shard_map/ppermute | solution.py:500
  60.0 12.7 %collective-permute-start.16 = (bf16[2,64,1024]{2,1,0:T(8,128)(2,1)S(1)}, bf16[2,64,1024]{2,1,0:T(8,128)(2,1)S(1)}, u32[]{:S(2)}, u32[]{:S(2)}) collective-permute-start(bf16[2,64,1024]{2,1,0:T(8,128)(2,1)S(1)} %get-tuple-element.41), channel_id=1, source_target_pairs={{0,1},{1,2},{2,3},{3,4},{4,5},{5,6},{6,7},{7,0},{8,9},{9,10},{10,1... | collective-permute-start | bytes 786440 | tf_op jit(solution)/shard_map/ppermute | solution.py:504
  62.0 10.7 %collective-permute-start.17 = (bf16[2,64,1024]{2,1,0:T(8,128)(2,1)S(1)}, bf16[2,64,1024]{2,1,0:T(8,128)(2,1)S(1)}, u32[]{:S(2)}, u32[]{:S(2)}) collective-permute-start(bf16[2,64,1024]{2,1,0:T(8,128)(2,1)S(1)} %get-tuple-element.42), channel_id=1, source_target_pairs={{0,7},{1,0},{2,1},{3,2},{4,3},{5,4},{6,5},{7,6},{8,15},{9,8},{10,9... | collective-permute-start | bytes 786440 | tf_op jit(solution)/shard_map/ppermute | solution.py:504
  65.8 6.1 %collective-permute-start.18 = (bf16[64,512]{1,0:T(8,128)(2,1)S(1)}, bf16[64,512]{1,0:T(8,128)(2,1)S(1)}, u32[]{:S(2)}, u32[]{:S(2)}) collective-permute-start(bf16[64,512]{1,0:T(8,128)(2,1)S(1)} %get-tuple-element.43), channel_id=1, source_target_pairs={{0,2},{1,3},{2,4},{3,5},{4,6},{5,7},{6,0},{7,1},{8,10},{9,11},{10,... | collective-permute-start | bytes 196616 | tf_op jit(solution)/shard_map/ppermute | solution.py:504
  65.8 7.0 %collective-permute-start.19 = (bf16[64,512]{1,0:T(8,128)(2,1)S(1)}, bf16[64,512]{1,0:T(8,128)(2,1)S(1)}, u32[]{:S(2)}, u32[]{:S(2)}) collective-permute-start(bf16[64,512]{1,0:T(8,128)(2,1)S(1)} %get-tuple-element.44), channel_id=1, source_target_pairs={{0,6},{1,7},{2,0},{3,1},{4,2},{5,3},{6,4},{7,5},{8,14},{9,15},{10,... | collective-permute-start | bytes 196616 | tf_op jit(solution)/shard_map/ppermute | solution.py:504
  72.8 13.9 %collective-permute-start.20 = (bf16[64,1024]{1,0:T(8,128)(2,1)S(1)}, bf16[64,1024]{1,0:T(8,128)(2,1)S(1)}, u32[]{:S(2)}, u32[]{:S(2)}) collective-permute-start(bf16[64,1024]{1,0:T(8,128)(2,1)S(1)} %get-tuple-element.45), channel_id=1, source_target_pairs={{0,2},{1,3},{2,4},{3,5},{4,6},{5,7},{6,0},{7,1},{8,10},{9,11},{10,... | collective-permute-start | bytes 393224 | tf_op jit(solution)/shard_map/ppermute | solution.py:504
  75.7 11.1 %collective-permute-start.21 = (bf16[64,1024]{1,0:T(8,128)(2,1)S(1)}, bf16[64,1024]{1,0:T(8,128)(2,1)S(1)}, u32[]{:S(2)}, u32[]{:S(2)}) collective-permute-start(bf16[64,1024]{1,0:T(8,128)(2,1)S(1)} %get-tuple-element.46), channel_id=1, source_target_pairs={{0,6},{1,7},{2,0},{3,1},{4,2},{5,3},{6,4},{7,5},{8,14},{9,15},{10,... | collective-permute-start | bytes 393224 | tf_op jit(solution)/shard_map/ppermute | solution.py:504
  76.5 15.9 %collective-permute-start.23 = (bf16[4,16,128]{2,1,0:T(8,128)(2,1)S(1)}, bf16[4,16,128]{2,1,0:T(8,128)(2,1)S(1)}, u32[]{:S(2)}, u32[]{:S(2)}) collective-permute-start(bf16[4,16,128]{2,1,0:T(8,128)(2,1)S(1)} %pad_maximum_fusion.1), channel_id=1, source_target_pairs={{0,8},{8,0},{16,24},{24,16},{32,40},{40,32},{48,56},{56,48},{64,72... | collective-permute-start | bytes 49160 | tf_op jit(solution)/shard_map/ppermute | solution.py:483
  86.8 6.5 %collective-permute-start.22 = (bf16[64,512]{1,0:T(8,128)(2,1)S(1)}, bf16[64,512]{1,0:T(8,128)(2,1)S(1)}, u32[]{:S(2)}, u32[]{:S(2)}) collective-permute-start(bf16[64,512]{1,0:T(8,128)(2,1)S(1)} %get-tuple-element.48), channel_id=1, source_target_pairs={{0,8},{8,0},{16,24},{24,16},{32,40},{40,32},{48,56},{56,48},{64,72... | collective-permute-start | bytes 196616 | tf_op jit(solution)/shard_map/ppermute | solution.py:483

commit v6 on v5

--- a/solution.py
+++ b/solution.py
@@ -139,7 +139,7 @@
             pltpu.SMEM((40,), jnp.int32),
             pltpu.SemaphoreType.DMA((7,)),
         ],
-        compiler_params=params(56),
+        compiler_params=params(54),
         name="local_parts",
     )(place, q, prompt, table, length, new, pool)
 
@@ -192,7 +192,7 @@
 COUNT = ROWS // GROUP
 
 
-def prefix_send_body(qa, qb, kv0, kv1, later, out):
+def prefix_send_body(qa, qb, kv0, kv1, after, later, out):
     lane = lanes()
     tile = jnp.zeros((GROUP, DH), F32)
     for half, q in enumerate((qa, qb)):
@@ -215,34 +215,22 @@
         masses[at : at + COUNT] = jnp.broadcast_to(mass, (ROWS, DH)).reshape(COUNT, GROUP, DH)
 
 
-def prefix_first_body(q, kv0_in, kv1_in, out, masses, kv0, kv1, sems):
-    copies = [
-        pltpu.make_async_copy(kv0_in, kv0, sems.at[0]),
-        pltpu.make_async_copy(kv1_in, kv1, sems.at[1]),
-    ]
-    for copy in copies:
-        copy.start()
-    for copy in copies:
-        copy.wait()
-    prefix_keep_body(q, kv0, kv1, out, masses)
-
-
 def prefix_cost(rows):
     return pl.CostEstimate(
         flops=4 * rows * 4096 * 128, bytes_accessed=2_500_000, transcendentals=rows * 4096
     )
 
 
-def prefix_send(qa, qb, kv0, kv1, later):
+def prefix_send(qa, qb, kv0, kv1, after, later):
     return pl.pallas_call(
         prefix_send_body,
         out_shape=jax.ShapeDtypeStruct((33, GROUP, DH), BF16),
-        in_specs=[VMEM] * 4 + [ANY],
+        in_specs=[VMEM] * 4 + [ANY] * 2,
         out_specs=VMEM,
         compiler_params=params(24),
         cost_estimate=prefix_cost(512),
         name="prefix_send",
-    )(qa, qb, kv0, kv1, later)
+    )(qa, qb, kv0, kv1, after, later)
 
 
 def prefix_keep(q, kv0, kv1):
@@ -255,21 +243,6 @@
         compiler_params=params(24),
         cost_estimate=prefix_cost(256),
         name="prefix_keep",
-    )(q, kv0, kv1)
-
-
-def prefix_first(q, kv0, kv1):
-    out = jax.ShapeDtypeStruct((16, GROUP, DH), F32)
-    held = jax.ShapeDtypeStruct(kv0.shape, BF16)
-    return pl.pallas_call(
-        prefix_first_body,
-        out_shape=[out, out, held, held],
-        in_specs=[VMEM, VMEM, VMEM],
-        out_specs=[VMEM] * 4,
-        scratch_shapes=[pltpu.SemaphoreType.DMA((2,))],
-        compiler_params=params(24),
-        cost_estimate=prefix_cost(256),
-        name="prefix_first",
     )(q, kv0, kv1)
 
 
@@ -299,7 +272,7 @@
                 ea, eb, es = jnp.exp(la - top), jnp.exp(lb - top), jnp.exp(ls - top)
                 row = (ea * a + eb * b + es * s) / (ea + eb + es)
                 target = (x ^ kx) * 2 + (y_high ^ g)
-                held[((target - z) & 7) * 4 + k] = row
+                held[((target - z - 2) & 7) * 4 + k] = row
     for h in range(GROUP):
         out[:, h * DH : (h + 1) * DH] = held[:, h, :].astype(BF16)
 
@@ -319,114 +292,98 @@
 def by_target(total):
     low = lax.broadcasted_iota(jnp.int32, (8, total.shape[1]), 0) < 4
     chunks = []
-    for g in range(4):
+    for g in range(2):
         even, odd = [], []
         for j in (0, 2):
-            first = total[j * 32 + g * 8 : j * 32 + g * 8 + 8]
-            second = total[(j + 1) * 32 + g * 8 : (j + 1) * 32 + g * 8 + 8]
+            first = total[j * 16 + g * 8 : j * 16 + g * 8 + 8]
+            second = total[(j + 1) * 16 + g * 8 : (j + 1) * 16 + g * 8 + 8]
             even.append(jnp.where(low, first, pltpu.roll(second, 4, 0)))
             odd.append(jnp.where(low, pltpu.roll(first, 4, 0), second))
         chunks += [jnp.concatenate(even, axis=0), jnp.concatenate(odd, axis=0)]
     return chunks
 
 
-def project_body(sizes, *refs):
-    blocks, weights, out = refs[: sum(sizes)], refs[sum(sizes) : sum(sizes) + 2], refs[-1]
-    at = 0
-    for i, size in enumerate(sizes):
-        block = jnp.concatenate([b[...] for b in blocks[at : at + size]], axis=0)
-        at += size
-        for side, weight in enumerate(weights):
-            for d, chunk in enumerate(by_target(dot(block, weight[...]))):
+def project_body(a, b, c, w0, w1, out):
+    rows = jnp.concatenate([a[...], b[...], c[...]], axis=0)
+    for side, weight in enumerate((w0, w1)):
+        total = dot(rows, weight[...])
+        for i in range(3):
+            for d, chunk in enumerate(by_target(total[64 * i : 64 * i + 64])):
                 out[d, i * 16 : i * 16 + 16, side * 512 : side * 512 + 512] = chunk
 
 
 def project(blocks, weights):
-    sizes = [len(block) for block in blocks]
-    pieces = [piece for block in blocks for piece in block]
-    return pl.pallas_call(
-        lambda *refs: project_body(sizes, *refs),
-        out_shape=jax.ShapeDtypeStruct((8, 16 * len(sizes), 1024), F32),
-        in_specs=[VMEM] * (len(pieces) + 2),
+    return pl.pallas_call(
+        project_body,
+        out_shape=jax.ShapeDtypeStruct((4, 48, 1024), F32),
+        in_specs=[VMEM] * 5,
         out_specs=VMEM,
         compiler_params=params(),
         cost_estimate=pl.CostEstimate(
-            flops=len(sizes) * 2 * 128 * 2048 * 1024, bytes_accessed=4_500_000, transcendentals=0
+            flops=2 * 192 * 2048 * 1024, bytes_accessed=4_500_000, transcendentals=0
         ),
         name="project",
-    )(*pieces, *weights)
-
-
-def last_body(*refs):
-    pieces, (w0, w1, first, second, up, down, up4, down4, keep) = refs[:-9], refs[-9:]
-    block = jnp.concatenate([piece[...] for piece in pieces], axis=0)
+    )(*blocks, *weights)
+
+
+def last_chunks(a, b, w0, w1, first):
+    rows = jnp.concatenate([a[...], b[...]], axis=0)
     for side, weight in enumerate((w0, w1)):
         columns = slice(side * 512, side * 512 + 512)
-        for d, chunk in enumerate(by_target(dot(block, weight[...]))):
-            whole = jnp.concatenate([first[d, :, columns], second[d, :, columns], chunk], axis=0)
-            if d in (0, 2, 6):
-                keep[(0, 2, 6).index(d), :, columns] = whole
-            elif d in (3, 1):
-                up[(3, 1).index(d), :, columns] = whole.astype(BF16)
-            elif d in (5, 7):
-                down[(5, 7).index(d), :, columns] = whole.astype(BF16)
-            elif side == 0:
-                up4[...] = whole.astype(BF16)
-            else:
-                down4[...] = whole.astype(BF16)
-
-
-def project_last(pieces, weights, first, second):
-    pair = jax.ShapeDtypeStruct((2, 64, 1024), BF16)
-    half = jax.ShapeDtypeStruct((64, 512), BF16)
-    return pl.pallas_call(
-        last_body,
-        out_shape=[pair, pair, half, half, jax.ShapeDtypeStruct((3, 64, 1024), F32)],
-        in_specs=[VMEM] * (len(pieces) + 4),
-        out_specs=[VMEM] * 5,
+        for d, chunk in enumerate(by_target(dot(rows, weight[...]))):
+            yield side, columns, d, jnp.concatenate([first[d, :, columns], chunk], axis=0)
+
+
+def far_body(a, b, w0, w1, first, keep, up, down, up4, down4):
+    for side, columns, d, whole in last_chunks(a, b, w0, w1, first):
+        if d == 0:
+            keep[:, columns] = whole
+        elif d == 1:
+            up[:, columns] = whole.astype(BF16)
+        elif d == 3:
+            down[:, columns] = whole.astype(BF16)
+        elif side == 0:
+            up4[...] = whole.astype(BF16)
+        else:
+            down4[...] = whole.astype(BF16)
+
+
+def near_body(a, b, w0, w1, first, keep6, down, keep0, up):
+    for _, columns, d, whole in last_chunks(a, b, w0, w1, first):
+        if d in (0, 2):
+            (keep6, keep0)[d // 2][:, columns] = whole
+        else:
+            (down, up)[d // 2][:, columns] = whole.astype(BF16)
+
+
+SUM = jax.ShapeDtypeStruct((64, 1024), F32)
+SENT = jax.ShapeDtypeStruct((64, 1024), BF16)
+HALF = jax.ShapeDtypeStruct((64, 512), BF16)
+
+
+def plain(body, out_shape, *args):
+    return pl.pallas_call(
+        body,
+        out_shape=out_shape,
+        in_specs=[VMEM] * len(args),
+        out_specs=[VMEM] * len(out_shape),
         compiler_params=params(),
-        name="project_last",
-    )(*pieces, *weights, first, second)
-
-
-def middle_body(keep, below, above, below4, above4, up, down):
-    u = keep[1] + below[0].astype(F32)
-    up[:, :512] = (u[:, :512] + below4[...].astype(F32)).astype(BF16)
-    up[:, 512:] = u[:, 512:].astype(BF16)
-    d = keep[2] + above[0].astype(F32)
-    down[:, :512] = d[:, :512].astype(BF16)
-    down[:, 512:] = (d[:, 512:] + above4[...].astype(F32)).astype(BF16)
-
-
-def middle(keep, below, above, below4, above4):
-    out = jax.ShapeDtypeStruct((64, 1024), BF16)
-    return pl.pallas_call(
-        middle_body,
-        out_shape=[out, out],
-        in_specs=[VMEM] * 5,
-        out_specs=[VMEM] * 2,
-        compiler_params=params(),
-        name="middle",
-    )(keep, below, above, below4, above4)
-
-
-def total_body(keep, below, above, below2, above2, own, other):
-    near = keep[0] + below[1].astype(F32) + above[1].astype(F32)
+        name=body.__name__[:-5],
+    )(*args)
+
+
+def middle_body(keep2, keep6, below, above, below4, above4, up, down):
+    up[:, :512] = (keep2[:, :512] + below[:, :512].astype(F32) + below4[...].astype(F32)).astype(BF16)
+    up[:, 512:] = (keep2[:, 512:] + below[:, 512:].astype(F32)).astype(BF16)
+    down[:, :512] = (keep6[:, :512] + above[:, :512].astype(F32)).astype(BF16)
+    down[:, 512:] = (keep6[:, 512:] + above[:, 512:].astype(F32) + above4[...].astype(F32)).astype(BF16)
+
+
+def total_body(keep, below1, above1, below2, above2, own, other):
+    near = keep[...] + below1[...].astype(F32) + above1[...].astype(F32)
     whole = (near + below2[...].astype(F32) + above2[...].astype(F32)).astype(BF16)
     own[...] = whole[:, :512]
     other[...] = whole[:, 512:]
-
-
-def total(keep, below, above, below2, above2):
-    out = jax.ShapeDtypeStruct((64, 512), BF16)
-    return pl.pallas_call(
-        total_body,
-        out_shape=[out, out],
-        in_specs=[VMEM] * 5,
-        out_specs=[VMEM] * 2,
-        compiler_params=params(),
-        name="total",
-    )(keep, below, above, below2, above2)
 
 
 def order_body(place, orders, pick):
@@ -500,6 +457,12 @@
     return lax.ppermute(value, "batch", pairs)
 
 
+def gathered(parts):
+    ring0 = jnp.concatenate(parts, axis=0)
+    ring1, ring3 = turned(ring0, 1, 1), turned(ring0, 3, 1)
+    return ring0, ring1, ring3, [turned(ring3[:32], 1, 1), turned(ring1[32:], 3, 1)]
+
+
 def along_z(value, k):
     return lax.ppermute(value, "head", [(i, (i + k) % HEADS) for i in range(HEADS)])
 
@@ -519,26 +482,30 @@
     same, other, across = regroup(place, by_x)
     from1, from3, from2 = along_y(same, 1), along_y(other, 3), along_y(across, 2)
 
-    *own, kv0, kv1 = prefix_first(same, prefix_kv, prefix_other)
-    message = along_y(prefix_send(from1, from3, kv0, kv1, from2), 1)
-    cross = prefix_keep(from2, kv0, kv1)
+    own = prefix_keep(same, prefix_kv, prefix_other)
+    message = along_y(prefix_send(from1, from3, prefix_kv, prefix_other, own[1], from2), 1)
+    cross = prefix_keep(from2, prefix_kv, prefix_other)
     attended = combine(place, own, cross, message, by_x, from2)
 
     orders = jnp.stack([same[16], from1[16], from2[16], from3[16]])
     orders = jnp.concatenate([orders, other_core(orders)], axis=0)
     pick = order_rows(place, orders)
 
-    ring0 = jnp.concatenate([attended] + [turned(attended, k, 0) for k in (1, 2, 3)], axis=0)
-    ring1, ring3 = turned(ring0, 1, 1), turned(ring0, 3, 1)
-    ring2 = [turned(ring3[:64], 1, 1), turned(ring1[64:], 3, 1)]
-    first = project([[ring0]], weights)
-    second = project([[ring1], [ring3]], weights)
-    up, down, up4, down4, keep = project_last(ring2, weights, first, second)
-
+    parts = [attended] + [turned(attended, k, 0) for k in (1, 2, 3)]
+    far, near = [gathered([a[i : i + 16] for a in parts]) for i in (0, 16)]
+    first_far, first_near = project(far[:3], weights), project(near[:3], weights)
+    keep2, up3, down3, up4, down4 = plain(
+        far_body, [SUM, SENT, SENT, HALF, HALF], *far[3], *weights, first_far
+    )
     below4, above4 = along_z(up4, 2), along_z(down4, -2)
-    below, above = along_z(up, 1), along_z(down, -1)
-    up2, down2 = middle(keep, below, above, below4, above4)
-    own, other = total(keep, below, above, along_z(up2, 2), along_z(down2, -2))
+    below3, above3 = along_z(up3, 1), along_z(down3, -1)
+    keep6, down1, keep0, up1 = plain(
+        near_body, [SUM, SENT, SUM, SENT], *near[3], *weights, first_near
+    )
+    below1, above1 = along_z(up1, 1), along_z(down1, -1)
+    up2, down2 = plain(middle_body, [SENT, SENT], keep2, keep6, below3, above3, below4, above4)
+    below2, above2 = along_z(up2, 2), along_z(down2, -2)
+    own, other = plain(total_body, [HALF, HALF], keep0, below1, above1, below2, above2)
     return finish(own, other_core(other), pick)
 
 

time: 94.5 us -> 90.2 us (0.954)
  waiting for transfers between devices: 22.4 us -> 16.2 us
  starting transfers between devices: 49.6 us -> 52.1 us
    ppermute x7 -> x11, waiting for transfers between devices: 13 us -> 9.51 us  [turned(): return lax.ppermute(value, 'batch', pairs)]
    ppermute x6 -> x8, waiting for transfers between devices: 3.41 us -> 0.16 us  [along_z(): lax.ppermute(value, 'head', [(i, (i + k) % HEADS) for i in range(HEADS)])]
    ppermute x6 -> x8, starting transfers between devices: 12.9 us -> 15.7 us  [along_z(): lax.ppermute(value, 'head', [(i, (i + k) % HEADS) for i in range(HEADS)])]
    pallas_call x6, Pallas kernels: 6.47 us -> 3.82 us  [the longest x2 1.97 us: project(): pl.pallas_call(project_body, out_shape=jax.ShapeDtypeStruct((4, 48, 1024)...]
    pallas_call x1 -> x2, Pallas kernels: 2.18 us -> 4.35 us  [prefix_keep(): pl.pallas_call(prefix_keep_body, out_shape=[out, out], in_specs=[VMEM] *...]
    ppermute x11, starting transfers between devices: 27.4 us -> 25.7 us  [along(): lax.ppermute(value, 'batch', [(i, i ^ k << shift) for i in range(BATCH)])]
    ppermute x7 -> x11, starting transfers between devices: 9.3 us -> 10.7 us  [turned(): return lax.ppermute(value, 'batch', pairs)]
  transfers between devices with their start and end apart: 24 -> 30, of which waited for: 13 -> 13; matrix products, arithmetic and copies ran while one was open for 1% -> 1% of each run, Pallas kernels for 20% -> 16%
where the time goes in v6:
time: 90.2 us; the launch traced here: 90.1 us
  starting transfers between devices  52.1 us (58%)
  Pallas kernels  19.8 us (22%)
  waiting for transfers between devices  16.2 us (18%)
  local copies, waits for them, and re-layouts  1.64 us (2%)
    ppermute x11, starting transfers between devices, along(): lax.ppermute(value, 'batch', [(i, i ^ k << shift) for i in range(BATCH)])  25.7 us
    ppermute x8, starting transfers between devices, along_z(): lax.ppermute(value, 'head', [(i, (i + k) % HEADS) for i in range(HEADS)])  15.7 us
    ppermute x11, starting transfers between devices, turned(): return lax.ppermute(value, 'batch', pairs)  10.7 us
    ppermute x11, waiting for transfers between devices, turned(): return lax.ppermute(value, 'batch', pairs)  9.51 us
    ppermute x11, waiting for transfers between devices, along(): lax.ppermute(value, 'batch', [(i, i ^ k << shift) for i in range(BATCH)])  6.52 us
    pallas_call x2, Pallas kernels, prefix_keep(): pl.pallas_call(prefix_keep_body, out_shape=[out, out], in_specs=[VMEM] *...  4.35 us
    pallas_call x1, Pallas kernels, local_parts(): pl.pallas_call(local_body, out_shape=[out] * 4, in_specs=[SMEM] + [HBM] *...  4.23 us
    pallas_call x1, Pallas kernels, prefix_send(): pl.pallas_call(prefix_send_body, out_shape=jax.ShapeDtypeStruct((33, GROU...  4.09 us
  transfers between devices with their start and end apart: 30, of which 13 were waited for; matrix products, arithmetic and copies ran while one was open for 1% of the time, Pallas kernels for 16%

profile of v6, /device:TPU:1, one launch (start us, length us, event | category | flops | bytes accessed | tf_op | source)
XLA Modules:
  0.0 90.1 jit_solution(12059188817873131042)
XLA Ops:
  0.0 3.2 %collective-permute-start.3 = (bf16[2,2048,128]{2,1,0:T(8,128)(2,1)}, bf16[2,2048,128]{2,1,0:T(8,128)(2,1)S(1)}, u32[]{:S(2)}, u32[]{:S(2)}) collective-permute-start(bf16[2,2048,128]{2,1,0:T(8,128)(2,1)} %kv0.5), channel_id=1, source_target_pairs={{0,8},{8,0},{16,24},{24,16},{32,40},{40,32},{48,56},{56,48},{64,72... | collective-permute-start | bytes 3145736 | tf_op jit(solution)/shard_map/ppermute | solution.py:440
  3.2 0.6 stack.34.place
  3.9 4.2 %local_parts.1 = (bf16[18,16,128]{2,1,0:T(8,128)(2,1)}, bf16[18,16,128]{2,1,0:T(8,128)(2,1)}, bf16[18,16,128]{2,1,0:T(8,128)(2,1)}, bf16[18,16,128]{2,1,0:T(8,128)(2,1)}) custom-call(s32[7]{0:T(128)} %stack.34.place, bf16[32,2048]{1,0:T(8,128)(2,1)} %q_in.1, s32[32]{0:T(128)} %prompt_in.1, s32[8,32]{1,0:T(8,128)} %bitcast.8, s32[32]{0:T(128)} %length_in.1, ...), custom_call_target="tpu_custom_call" | custom-call | tf_op jit(solution)/shard_map/local_parts/pallas_call | solution.py:124
  8.1 0.1 collective-permute-start
  8.2 1.9 %collective-permute-start.1 = (bf16[18,16,128]{2,1,0:T(8,128)(2,1)}, bf16[18,16,128]{2,1,0:T(8,128)(2,1)S(1)}, u32[]{:S(2)}, u32[]{:S(2)}) collective-permute-start(bf16[18,16,128]{2,1,0:T(8,128)(2,1)} %get-tuple-element.31), channel_id=1, source_target_pairs={{0,128},{8,136},{16,144},{24,152},{32,160},{40,168},{48,176},{56,1... | collective-permute-start | bytes 221192 | tf_op jit(solution)/shard_map/ppermute | solution.py:440
  10.1 1.9 %collective-permute-start.2 = (bf16[18,16,128]{2,1,0:T(8,128)(2,1)}, bf16[18,16,128]{2,1,0:T(8,128)(2,1)S(1)}, u32[]{:S(2)}, u32[]{:S(2)}) collective-permute-start(bf16[18,16,128]{2,1,0:T(8,128)(2,1)} %get-tuple-element.32), channel_id=1, source_target_pairs={{0,192},{8,200},{16,208},{24,216},{32,224},{40,232},{48,240},{56,2... | collective-permute-start | bytes 221192 | tf_op jit(solution)/shard_map/ppermute | solution.py:440
  12.1 0.2 collective-permute-done.a1.s1
  12.3 2.0 %collective-permute-done.1.a2.s2 = bf16[18,16,128]{2,1,0:T(8,128)(2,1)S(1)} collective-permute-done((bf16[18,16,128]{2,1,0:T(8,128)(2,1)}, bf16[18,16,128]{2,1,0:T(8,128)(2,1)S(1)}, u32[]{:S(2)}, u32[]{:S(2)}) %collective-permute-start.1) | collective-permute-done | bytes 73760 | tf_op jit(solution)/shard_map/ppermute | solution.py:440
  14.3 1.4 %collective-permute-done.2.a3.s3 = bf16[18,16,128]{2,1,0:T(8,128)(2,1)S(1)} collective-permute-done((bf16[18,16,128]{2,1,0:T(8,128)(2,1)}, bf16[18,16,128]{2,1,0:T(8,128)(2,1)S(1)}, u32[]{:S(2)}, u32[]{:S(2)}) %collective-permute-start.2) | collective-permute-done | bytes 73760 | tf_op jit(solution)/shard_map/ppermute | solution.py:440
  15.8 0.9 copy-done.2
  16.7 0.6 regroup.1
  17.2 3.0 %collective-permute-start.4 = (bf16[37,16,128]{2,1,0:T(8,128)(2,1)S(1)}, bf16[37,16,128]{2,1,0:T(8,128)(2,1)S(1)}, u32[]{:S(2)}, u32[]{:S(2)}) collective-permute-start(bf16[37,16,128]{2,1,0:T(8,128)(2,1)S(1)} %get-tuple-element.36), channel_id=1, source_target_pairs={{0,32},{8,40},{16,48},{24,56},{32,0},{40,8},{48,16},{56,24},{64,96... | collective-permute-start | bytes 454664 | tf_op jit(solution)/shard_map/ppermute | solution.py:440
  20.3 0.4 collective-permute-start.5
  20.6 0.4 collective-permute-start.6
  21.0 2.2 %prefix_keep.2 = (f32[16,16,128]{2,1,0:T(8,128)S(1)}, f32[16,16,128]{2,1,0:T(8,128)S(1)}) custom-call(bf16[17,16,128]{2,1,0:T(8,128)(2,1)S(1)} %get-tuple-element.33.q, bf16[2,2048,128]{2,1,0:T(8,128)(2,1)S(1)} %copy-done.1, bf16[2,2048,128]{2,1,0:T(8,128)(2,1)S(1)} %collective-permute-done.3.kv1), custom_call_target="tpu_custom_call" | custom-call | flops 536870912 | bytes 2500000 | tf_op jit(solution)/shard_map/prefix_keep/pallas_call | solution.py:238
  23.2 0.0 copy-start
  23.2 1.9 %collective-permute-done.5.qa = bf16[17,16,128]{2,1,0:T(8,128)(2,1)S(1)} collective-permute-done((bf16[17,16,128]{2,1,0:T(8,128)(2,1)S(1)}, bf16[17,16,128]{2,1,0:T(8,128)(2,1)S(1)}, u32[]{:S(2)}, u32[]{:S(2)}) %collective-permute-start.5) | collective-permute-done | bytes 69664 | tf_op jit(solution)/shard_map/ppermute | solution.py:440
  25.2 0.6 collective-permute-done.6.qb
  25.8 0.0 collective-permute-done.4.q.later.far
  25.8 4.1 %prefix_send.1 = bf16[33,16,128]{2,1,0:T(8,128)(2,1)S(1)} custom-call(bf16[17,16,128]{2,1,0:T(8,128)(2,1)S(1)} %collective-permute-done.5.qa, bf16[17,16,128]{2,1,0:T(8,128)(2,1)S(1)} %collective-permute-done.6.qb, bf16[2,2048,128]{2,1,0:T(8,128)(2,1)S(1)} %copy-done.1, bf16[2,2048,128]{2,1,0:T(8,128)(2,1)S(1)} %collective-permute-done.3.kv1, ...), custom_call_target="tpu_custom_call" | custom-call | flops 1073741824 | bytes 2500000 | tf_op jit(solution)/shard_map/prefix_send/pallas_call | solution.py:225
  29.9 0.6 collective-permute-start.7
  30.5 2.1 %collective-permute-start.15 = (bf16[2048,512]{1,0:T(8,128)(2,1)S(1)}, bf16[2048,512]{1,0:T(8,128)(2,1)S(1)}, u32[]{:S(2)}, u32[]{:S(2)}) collective-permute-start(bf16[2048,512]{1,0:T(8,128)(2,1)S(1)} %copy-done), channel_id=1, source_target_pairs={{0,8},{8,0},{16,24},{24,16},{32,40},{40,32},{48,56},{56,48},{64,72... | collective-permute-start | bytes 6291464 | tf_op jit(solution)/shard_map/ppermute | solution.py:440
  32.6 2.2 %prefix_keep.3 = (f32[16,16,128]{2,1,0:T(8,128)S(1)}, f32[16,16,128]{2,1,0:T(8,128)S(1)}) custom-call(bf16[37,16,128]{2,1,0:T(8,128)(2,1)S(1)} %collective-permute-done.4.q.later.far, bf16[2,2048,128]{2,1,0:T(8,128)(2,1)S(1)} %copy-done.1, bf16[2,2048,128]{2,1,0:T(8,128)(2,1)S(1)} %collective-permute-done.3.kv1), custom_call_target="tpu_custom_call" | custom-call | flops 536870912 | bytes 2500000 | tf_op jit(solution)/shard_map/prefix_keep/pallas_call | solution.py:238
  34.8 0.0 collective-permute-done.7.message
  34.8 1.2 %combine.1 = bf16[32,2048]{1,0:T(8,128)(2,1)S(1)} custom-call(s32[7]{0:T(128)S(1)} %copy-done.4, f32[16,16,128]{2,1,0:T(8,128)S(1)} %get-tuple-element.34.own, f32[16,16,128]{2,1,0:T(8,128)S(1)} %get-tuple-element.35.after.own_masses, f32[16,16,128]{2,1,0:T(8,128)S(1)} %get-tuple-element.37.cross, f32[16,16,128]{2,1,0:T(8,128)S(1)} %get-tuple-element.38.cross_masses, ...), custom_call_target="tpu_custom_call" | custom-call | tf_op jit(solution)/shard_map/combine/pallas_call | solution.py:281
  36.0 1.1 %collective-permute-start.8 = (bf16[32,2048]{1,0:T(8,128)(2,1)S(1)}, bf16[32,2048]{1,0:T(8,128)(2,1)S(1)}, u32[]{:S(2)}, u32[]{:S(2)}) collective-permute-start(bf16[32,2048]{1,0:T(8,128)(2,1)S(1)} %combine.1), channel_id=1, source_target_pairs={{0,64},{8,24},{16,80},{24,8},{32,96},{40,56},{48,112},{56,40},{64,... | collective-permute-start | bytes 393224 | tf_op jit(solution)/shard_map/ppermute | solution.py:457
  37.1 2.7 %collective-permute-start.9 = (bf16[32,2048]{1,0:T(8,128)(2,1)S(1)}, bf16[32,2048]{1,0:T(8,128)(2,1)S(1)}, u32[]{:S(2)}, u32[]{:S(2)}) collective-permute-start(bf16[32,2048]{1,0:T(8,128)(2,1)S(1)} %combine.1), channel_id=1, source_target_pairs={{0,128},{8,40},{16,144},{24,56},{32,160},{40,8},{48,176},{56,24},{... | collective-permute-start | bytes 393224 | tf_op jit(solution)/shard_map/ppermute | solution.py:457
  39.8 0.1 collective-permute-start.10
  40.0 3.9 %collective-permute-done.9 = bf16[32,2048]{1,0:T(8,128)(2,1)S(1)} collective-permute-done((bf16[32,2048]{1,0:T(8,128)(2,1)S(1)}, bf16[32,2048]{1,0:T(8,128)(2,1)S(1)}, u32[]{:S(2)}, u32[]{:S(2)}) %collective-permute-start.9) | collective-permute-done | bytes 131104 | tf_op jit(solution)/shard_map/ppermute | solution.py:457
  43.9 1.2 %collective-permute-done.10 = bf16[32,2048]{1,0:T(8,128)(2,1)S(1)} collective-permute-done((bf16[32,2048]{1,0:T(8,128)(2,1)S(1)}, bf16[32,2048]{1,0:T(8,128)(2,1)S(1)}, u32[]{:S(2)}, u32[]{:S(2)}) %collective-permute-start.10) | collective-permute-done | bytes 131104 | tf_op jit(solution)/shard_map/ppermute | solution.py:457
  45.1 1.5 %collective-permute-start.18 = (bf16[64,2048]{1,0:T(8,128)(2,1)S(1)}, bf16[64,2048]{1,0:T(8,128)(2,1)S(1)}, u32[]{:S(2)}, u32[]{:S(2)}) collective-permute-start(bf16[64,2048]{1,0:T(8,128)(2,1)S(1)} %pad_maximum_fusion.1.a), channel_id=1, source_target_pairs={{0,48},{8,200},{16,32},{24,216},{32,16},{40,232},{48,0},{56,248},{... | collective-permute-start | bytes 786440 | tf_op jit(solution)/shard_map/ppermute | solution.py:457
  46.6 1.4 %collective-permute-start.11 = (bf16[64,2048]{1,0:T(8,128)(2,1)S(1)}, bf16[64,2048]{1,0:T(8,128)(2,1)S(1)}, u32[]{:S(2)}, u32[]{:S(2)}) collective-permute-start(bf16[64,2048]{1,0:T(8,128)(2,1)S(1)} %pad_maximum_fusion.a), channel_id=1, source_target_pairs={{0,48},{8,200},{16,32},{24,216},{32,16},{40,232},{48,0},{56,248},{... | collective-permute-start | bytes 786440 | tf_op jit(solution)/shard_map/ppermute | solution.py:457
  48.0 0.9 collective-permute-start.13
  48.8 3.1 %collective-permute-done.18.c = bf16[64,2048]{1,0:T(8,128)(2,1)S(1)} collective-permute-done((bf16[64,2048]{1,0:T(8,128)(2,1)S(1)}, bf16[64,2048]{1,0:T(8,128)(2,1)S(1)}, u32[]{:S(2)}, u32[]{:S(2)}) %collective-permute-start.18) | collective-permute-done | bytes 262176 | tf_op jit(solution)/shard_map/ppermute | solution.py:457
  51.9 0.1 collective-permute-start.19
  52.0 0.1 collective-permute-done.20.b
  52.1 1.4 %collective-permute-start.21 = (bf16[32,2048]{1,0:T(8,128)(2,1)S(1)}, bf16[32,2048]{1,0:T(8,128)(2,1)S(1)}, u32[]{:S(2)}, u32[]{:S(2)}) collective-permute-start(bf16[32,2048]{1,0:T(8,128)(2,1)S(1)} %slice.75), channel_id=1, source_target_pairs={{0,48},{8,200},{16,32},{24,216},{32,16},{40,232},{48,0},{56,248},{... | collective-permute-start | bytes 393224 | tf_op jit(solution)/shard_map/ppermute | solution.py:457
  53.6 1.2 %collective-permute-done.11.c = bf16[64,2048]{1,0:T(8,128)(2,1)S(1)} collective-permute-done((bf16[64,2048]{1,0:T(8,128)(2,1)S(1)}, bf16[64,2048]{1,0:T(8,128)(2,1)S(1)}, u32[]{:S(2)}, u32[]{:S(2)}) %collective-permute-start.11) | collective-permute-done | bytes 262176 | tf_op jit(solution)/shard_map/ppermute | solution.py:457
  54.7 0.1 collective-permute-start.12
  54.8 0.1 collective-permute-done.13.b
  54.9 1.4 %collective-permute-start.14 = (bf16[32,2048]{1,0:T(8,128)(2,1)S(1)}, bf16[32,2048]{1,0:T(8,128)(2,1)S(1)}, u32[]{:S(2)}, u32[]{:S(2)}) collective-permute-start(bf16[32,2048]{1,0:T(8,128)(2,1)S(1)} %slice.69), channel_id=1, source_target_pairs={{0,48},{8,200},{16,32},{24,216},{32,16},{40,232},{48,0},{56,248},{... | collective-permute-start | bytes 393224 | tf_op jit(solution)/shard_map/ppermute | solution.py:457
  56.4 0.0 collective-permute-done.15.w1
  56.4 1.0 %project.3.first = f32[4,48,1024]{2,1,0:T(8,128)S(1)} custom-call(bf16[64,2048]{1,0:T(8,128)(2,1)S(1)} %pad_maximum_fusion.1.a, bf16[64,2048]{1,0:T(8,128)(2,1)S(1)} %collective-permute-done.20.b, bf16[64,2048]{1,0:T(8,128)(2,1)S(1)} %collective-permute-done.18.c, bf16[2048,512]{1,0:T(8,128)(2,1)S(1)} %copy-done, ...), custom_call_target="tpu_custom_call" | custom-call | flops 805306368 | bytes 4500000 | tf_op jit(solution)/shard_map/project/pallas_call | solution.py:316
  57.4 0.0 collective-permute-done.21.b
  57.4 0.8 far.1
  58.3 1.9 %collective-permute-start.22 = (bf16[64,1024]{1,0:T(8,128)(2,1)S(1)}, bf16[64,1024]{1,0:T(8,128)(2,1)S(1)}, u32[]{:S(2)}, u32[]{:S(2)}) collective-permute-start(bf16[64,1024]{1,0:T(8,128)(2,1)S(1)} %get-tuple-element.45), channel_id=1, source_target_pairs={{0,1},{1,2},{2,3},{3,4},{4,5},{5,6},{6,7},{7,0},{8,9},{9,10},{10,1... | collective-permute-start | bytes 393224 | tf_op jit(solution)/shard_map/ppermute | solution.py:467
  60.1 4.0 %collective-permute-start.23 = (bf16[64,1024]{1,0:T(8,128)(2,1)S(1)}, bf16[64,1024]{1,0:T(8,128)(2,1)S(1)}, u32[]{:S(2)}, u32[]{:S(2)}) collective-permute-start(bf16[64,1024]{1,0:T(8,128)(2,1)S(1)} %get-tuple-element.46), channel_id=1, source_target_pairs={{0,7},{1,0},{2,1},{3,2},{4,3},{5,4},{6,5},{7,6},{8,15},{9,8},{10,9... | collective-permute-start | bytes 393224 | tf_op jit(solution)/shard_map/ppermute | solution.py:467
  64.2 0.0 collective-permute-start.24
  64.2 3.6 %collective-permute-start.25 = (bf16[64,512]{1,0:T(8,128)(2,1)S(1)}, bf16[64,512]{1,0:T(8,128)(2,1)S(1)}, u32[]{:S(2)}, u32[]{:S(2)}) collective-permute-start(bf16[64,512]{1,0:T(8,128)(2,1)S(1)} %get-tuple-element.48), channel_id=1, source_target_pairs={{0,6},{1,7},{2,0},{3,1},{4,2},{5,3},{6,4},{7,5},{8,14},{9,15},{10,... | collective-permute-start | bytes 196616 | tf_op jit(solution)/shard_map/ppermute | solution.py:467
  67.8 1.0 %project.2.first = f32[4,48,1024]{2,1,0:T(8,128)S(1)} custom-call(bf16[64,2048]{1,0:T(8,128)(2,1)S(1)} %pad_maximum_fusion.a, bf16[64,2048]{1,0:T(8,128)(2,1)S(1)} %collective-permute-done.13.b, bf16[64,2048]{1,0:T(8,128)(2,1)S(1)} %collective-permute-done.11.c, bf16[2048,512]{1,0:T(8,128)(2,1)S(1)} %copy-done, bf16[2048,512]{1,0:T(8,128)(2,1)S(1)} %collective-permute-done.15.w1), custom_call_target="tpu_custom_call" | custom-call | flops 805306368 | bytes 4500000 | tf_op jit(solution)/shard_map/project/pallas_call | solution.py:316
  68.8 0.9 near.1
  69.6 0.1 collective-permute-start.16
  69.7 0.1 collective-permute-done.24.below4
  69.8 2.5 %collective-permute-start.17 = (bf16[64,1024]{1,0:T(8,128)(2,1)S(1)}, bf16[64,1024]{1,0:T(8,128)(2,1)S(1)}, u32[]{:S(2)}, u32[]{:S(2)}) collective-permute-start(bf16[64,1024]{1,0:T(8,128)(2,1)S(1)} %get-tuple-element.42), channel_id=1, source_target_pairs={{0,7},{1,0},{2,1},{3,2},{4,3},{5,4},{6,5},{7,6},{8,15},{9,8},{10,9... | collective-permute-start | bytes 393224 | tf_op jit(solution)/shard_map/ppermute | solution.py:467
  72.4 0.1 middle.1
  72.5 1.4 %collective-permute-start.26 = (bf16[64,1024]{1,0:T(8,128)(2,1)S(1)}, bf16[64,1024]{1,0:T(8,128)(2,1)S(1)}, u32[]{:S(2)}, u32[]{:S(2)}) collective-permute-start(bf16[64,1024]{1,0:T(8,128)(2,1)S(1)} %get-tuple-element.49), channel_id=1, source_target_pairs={{0,2},{1,3},{2,4},{3,5},{4,6},{5,7},{6,0},{7,1},{8,10},{9,11},{10,... | collective-permute-start | bytes 393224 | tf_op jit(solution)/shard_map/ppermute | solution.py:467
  73.9 2.2 %collective-permute-start.27 = (bf16[64,1024]{1,0:T(8,128)(2,1)S(1)}, bf16[64,1024]{1,0:T(8,128)(2,1)S(1)}, u32[]{:S(2)}, u32[]{:S(2)}) collective-permute-start(bf16[64,1024]{1,0:T(8,128)(2,1)S(1)} %get-tuple-element.50), channel_id=1, source_target_pairs={{0,6},{1,7},{2,0},{3,1},{4,2},{5,3},{6,4},{7,5},{8,14},{9,15},{10,... | collective-permute-start | bytes 393224 | tf_op jit(solution)/shard_map/ppermute | solution.py:467
  76.1 7.1 %collective-permute-start.29 = (bf16[4,16,128]{2,1,0:T(8,128)(2,1)S(1)}, bf16[4,16,128]{2,1,0:T(8,128)(2,1)S(1)}, u32[]{:S(2)}, u32[]{:S(2)}) collective-permute-start(bf16[4,16,128]{2,1,0:T(8,128)(2,1)S(1)} %pad_maximum_fusion.2), channel_id=1, source_target_pairs={{0,8},{8,0},{16,24},{24,16},{32,40},{40,32},{48,56},{56,48},{64,72... | collective-permute-start | bytes 49160 | tf_op jit(solution)/shard_map/ppermute | solution.py:440
  83.2 0.0 collective-permute-done.17.above1
  83.2 0.1 total.1
  83.3 4.9 %collective-permute-start.28 = (bf16[64,512]{1,0:T(8,128)(2,1)S(1)}, bf16[64,512]{1,0:T(8,128)(2,1)S(1)}, u32[]{:S(2)}, u32[]{:S(2)}) collective-permute-start(bf16[64,512]{1,0:T(8,128)(2,1)S(1)} %get-tuple-element.52), channel_id=1, source_target_pairs={{0,8},{8,0},{16,24},{24,16},{32,40},{40,32},{48,56},{56,48},{64,72... | collective-permute-start | bytes 196616 | tf_op jit(solution)/shard_map/ppermute | solution.py:440
  88.3 0.6 order_rows.1.pick
  88.9 0.2 collective-permute-done.28.other
  89.1 0.9 %finish.1 = bf16[128,512]{1,0:T(8,128)(2,1)} custom-call(bf16[64,512]{1,0:T(8,128)(2,1)S(1)} %get-tuple-element.51.own, bf16[64,512]{1,0:T(8,128)(2,1)S(1)} %collective-permute-done.28.other, bf16[128,128]{1,0:T(8,128)(2,1)S(1)} %order_rows.1.pick), custom_call_target="tpu_custom_call" | custom-call | tf_op jit(solution)/shard_map/finish/pallas_call | solution.py:429
  (37 shorter events, 0.2 us)
Async XLA Ops:
  0.0 21.0 %copy-start.1 = (bf16[2,2048,128]{2,1,0:T(8,128)(2,1)S(1)}, bf16[2,2048,128]{2,1,0:T(8,128)(2,1)}, u32[]{:S(2)}) copy-start(bf16[2,2048,128]{2,1,0:T(8,128)(2,1)} %kv0.5) | copy-start | bytes 3145732
  0.0 21.0 %collective-permute-start.3 = (bf16[2,2048,128]{2,1,0:T(8,128)(2,1)}, bf16[2,2048,128]{2,1,0:T(8,128)(2,1)S(1)}, u32[]{:S(2)}, u32[]{:S(2)}) collective-permute-start(bf16[2,2048,128]{2,1,0:T(8,128)(2,1)} %kv0.5), channel_id=1, source_target_pairs={{0,8},{8,0},{16,24},{24,16},{32,40},{40,32},{48,56},{56,48},{64,72... | collective-permute-start | bytes 3145736 | tf_op jit(solution)/shard_map/ppermute | solution.py:440
  3.9 11.9 %copy-start.4 = (s32[7]{0:T(128)S(1)}, s32[7]{0:T(128)}, u32[]{:S(2)}) copy-start(s32[7]{0:T(128)} %stack.34.place) | copy-start | bytes 88
  8.1 4.2 %collective-permute-start = (bf16[18,16,128]{2,1,0:T(8,128)(2,1)}, bf16[18,16,128]{2,1,0:T(8,128)(2,1)S(1)}, u32[]{:S(2)}, u32[]{:S(2)}) collective-permute-start(bf16[18,16,128]{2,1,0:T(8,128)(2,1)} %get-tuple-element.30), channel_id=1, source_target_pairs={{0,64},{8,72},{16,80},{24,88},{32,96},{40,104},{48,112},{56,120},{... | collective-permute-start | bytes 221192 | tf_op jit(solution)/shard_map/ppermute | solution.py:440
  8.2 6.1 %collective-permute-start.1 = (bf16[18,16,128]{2,1,0:T(8,128)(2,1)}, bf16[18,16,128]{2,1,0:T(8,128)(2,1)S(1)}, u32[]{:S(2)}, u32[]{:S(2)}) collective-permute-start(bf16[18,16,128]{2,1,0:T(8,128)(2,1)} %get-tuple-element.31), channel_id=1, source_target_pairs={{0,128},{8,136},{16,144},{24,152},{32,160},{40,168},{48,176},{56,1... | collective-permute-start | bytes 221192 | tf_op jit(solution)/shard_map/ppermute | solution.py:440
  10.1 5.6 %collective-permute-start.2 = (bf16[18,16,128]{2,1,0:T(8,128)(2,1)}, bf16[18,16,128]{2,1,0:T(8,128)(2,1)S(1)}, u32[]{:S(2)}, u32[]{:S(2)}) collective-permute-start(bf16[18,16,128]{2,1,0:T(8,128)(2,1)} %get-tuple-element.32), channel_id=1, source_target_pairs={{0,192},{8,200},{16,208},{24,216},{32,224},{40,232},{48,240},{56,2... | collective-permute-start | bytes 221192 | tf_op jit(solution)/shard_map/ppermute | solution.py:440
  15.8 0.9 copy-start.2
  17.2 8.6 %collective-permute-start.4 = (bf16[37,16,128]{2,1,0:T(8,128)(2,1)S(1)}, bf16[37,16,128]{2,1,0:T(8,128)(2,1)S(1)}, u32[]{:S(2)}, u32[]{:S(2)}) collective-permute-start(bf16[37,16,128]{2,1,0:T(8,128)(2,1)S(1)} %get-tuple-element.36), channel_id=1, source_target_pairs={{0,32},{8,40},{16,48},{24,56},{32,0},{40,8},{48,16},{56,24},{64,96... | collective-permute-start | bytes 454664 | tf_op jit(solution)/shard_map/ppermute | solution.py:440
  20.3 4.9 %collective-permute-start.5 = (bf16[17,16,128]{2,1,0:T(8,128)(2,1)S(1)}, bf16[17,16,128]{2,1,0:T(8,128)(2,1)S(1)}, u32[]{:S(2)}, u32[]{:S(2)}) collective-permute-start(bf16[17,16,128]{2,1,0:T(8,128)(2,1)S(1)} %get-tuple-element.33.q), channel_id=1, source_target_pairs={{0,16},{8,24},{16,0},{24,8},{32,48},{40,56},{48,32},{56,40},{64,80... | collective-permute-start | bytes 208904 | tf_op jit(solution)/shard_map/ppermute | solution.py:440
  20.6 5.1 %collective-permute-start.6 = (bf16[17,16,128]{2,1,0:T(8,128)(2,1)S(1)}, bf16[17,16,128]{2,1,0:T(8,128)(2,1)S(1)}, u32[]{:S(2)}, u32[]{:S(2)}) collective-permute-start(bf16[17,16,128]{2,1,0:T(8,128)(2,1)S(1)} %get-tuple-element.39), channel_id=1, source_target_pairs={{0,48},{8,56},{16,32},{24,40},{32,16},{40,24},{48,0},{56,8},{64,11... | collective-permute-start | bytes 208904 | tf_op jit(solution)/shard_map/ppermute | solution.py:440
  23.2 7.2 %copy-start = (bf16[2048,512]{1,0:T(8,128)(2,1)S(1)}, bf16[2048,512]{1,0:T(8,128)(2,1)}, u32[]{:S(2)}) copy-start(bf16[2048,512]{1,0:T(8,128)(2,1)} %w0.7) | copy-start | bytes 6291460
  29.9 4.9 %copy-start.3 = (bf16[18,16,128]{2,1,0:T(8,128)(2,1)S(1)}, bf16[18,16,128]{2,1,0:T(8,128)(2,1)}, u32[]{:S(2)}) copy-start(bf16[18,16,128]{2,1,0:T(8,128)(2,1)} %get-tuple-element.29.a0.s0) | copy-start | bytes 221188
  29.9 4.9 %collective-permute-start.7 = (bf16[33,16,128]{2,1,0:T(8,128)(2,1)S(1)}, bf16[33,16,128]{2,1,0:T(8,128)(2,1)S(1)}, u32[]{:S(2)}, u32[]{:S(2)}) collective-permute-start(bf16[33,16,128]{2,1,0:T(8,128)(2,1)S(1)} %prefix_send.1), channel_id=1, source_target_pairs={{0,16},{8,24},{16,0},{24,8},{32,48},{40,56},{48,32},{56,40},{64,80... | collective-permute-start | bytes 405512 | tf_op jit(solution)/shard_map/ppermute | solution.py:440
  30.5 25.9 %collective-permute-start.15 = (bf16[2048,512]{1,0:T(8,128)(2,1)S(1)}, bf16[2048,512]{1,0:T(8,128)(2,1)S(1)}, u32[]{:S(2)}, u32[]{:S(2)}) collective-permute-start(bf16[2048,512]{1,0:T(8,128)(2,1)S(1)} %copy-done), channel_id=1, source_target_pairs={{0,8},{8,0},{16,24},{24,16},{32,40},{40,32},{48,56},{56,48},{64,72... | collective-permute-start | bytes 6291464 | tf_op jit(solution)/shard_map/ppermute | solution.py:440
  36.0 4.0 %collective-permute-start.8 = (bf16[32,2048]{1,0:T(8,128)(2,1)S(1)}, bf16[32,2048]{1,0:T(8,128)(2,1)S(1)}, u32[]{:S(2)}, u32[]{:S(2)}) collective-permute-start(bf16[32,2048]{1,0:T(8,128)(2,1)S(1)} %combine.1), channel_id=1, source_target_pairs={{0,64},{8,24},{16,80},{24,8},{32,96},{40,56},{48,112},{56,40},{64,... | collective-permute-start | bytes 393224 | tf_op jit(solution)/shard_map/ppermute | solution.py:457
  37.1 6.8 %collective-permute-start.9 = (bf16[32,2048]{1,0:T(8,128)(2,1)S(1)}, bf16[32,2048]{1,0:T(8,128)(2,1)S(1)}, u32[]{:S(2)}, u32[]{:S(2)}) collective-permute-start(bf16[32,2048]{1,0:T(8,128)(2,1)S(1)} %combine.1), channel_id=1, source_target_pairs={{0,128},{8,40},{16,144},{24,56},{32,160},{40,8},{48,176},{56,24},{... | collective-permute-start | bytes 393224 | tf_op jit(solution)/shard_map/ppermute | solution.py:457
  39.8 5.2 %collective-permute-start.10 = (bf16[32,2048]{1,0:T(8,128)(2,1)S(1)}, bf16[32,2048]{1,0:T(8,128)(2,1)S(1)}, u32[]{:S(2)}, u32[]{:S(2)}) collective-permute-start(bf16[32,2048]{1,0:T(8,128)(2,1)S(1)} %combine.1), channel_id=1, source_target_pairs={{0,192},{8,56},{16,208},{24,40},{32,224},{40,24},{48,240},{56,8},{... | collective-permute-start | bytes 393224 | tf_op jit(solution)/shard_map/ppermute | solution.py:457
  45.1 6.8 %collective-permute-start.18 = (bf16[64,2048]{1,0:T(8,128)(2,1)S(1)}, bf16[64,2048]{1,0:T(8,128)(2,1)S(1)}, u32[]{:S(2)}, u32[]{:S(2)}) collective-permute-start(bf16[64,2048]{1,0:T(8,128)(2,1)S(1)} %pad_maximum_fusion.1.a), channel_id=1, source_target_pairs={{0,48},{8,200},{16,32},{24,216},{32,16},{40,232},{48,0},{56,248},{... | collective-permute-start | bytes 786440 | tf_op jit(solution)/shard_map/ppermute | solution.py:457
  46.6 5.5 %collective-permute-start.20 = (bf16[64,2048]{1,0:T(8,128)(2,1)S(1)}, bf16[64,2048]{1,0:T(8,128)(2,1)S(1)}, u32[]{:S(2)}, u32[]{:S(2)}) collective-permute-start(bf16[64,2048]{1,0:T(8,128)(2,1)S(1)} %pad_maximum_fusion.1.a), channel_id=1, source_target_pairs={{0,16},{8,72},{16,0},{24,88},{32,48},{40,104},{48,32},{56,120},{64... | collective-permute-start | bytes 786440 | tf_op jit(solution)/shard_map/ppermute | solution.py:457
  46.6 8.1 %collective-permute-start.11 = (bf16[64,2048]{1,0:T(8,128)(2,1)S(1)}, bf16[64,2048]{1,0:T(8,128)(2,1)S(1)}, u32[]{:S(2)}, u32[]{:S(2)}) collective-permute-start(bf16[64,2048]{1,0:T(8,128)(2,1)S(1)} %pad_maximum_fusion.a), channel_id=1, source_target_pairs={{0,48},{8,200},{16,32},{24,216},{32,16},{40,232},{48,0},{56,248},{... | collective-permute-start | bytes 786440 | tf_op jit(solution)/shard_map/ppermute | solution.py:457
  48.0 6.9 %collective-permute-start.13 = (bf16[64,2048]{1,0:T(8,128)(2,1)S(1)}, bf16[64,2048]{1,0:T(8,128)(2,1)S(1)}, u32[]{:S(2)}, u32[]{:S(2)}) collective-permute-start(bf16[64,2048]{1,0:T(8,128)(2,1)S(1)} %pad_maximum_fusion.a), channel_id=1, source_target_pairs={{0,16},{8,72},{16,0},{24,88},{32,48},{40,104},{48,32},{56,120},{64... | collective-permute-start | bytes 786440 | tf_op jit(solution)/shard_map/ppermute | solution.py:457
  51.9 5.4 %collective-permute-start.19 = (bf16[32,2048]{1,0:T(8,128)(2,1)S(1)}, bf16[32,2048]{1,0:T(8,128)(2,1)S(1)}, u32[]{:S(2)}, u32[]{:S(2)}) collective-permute-start(bf16[32,2048]{1,0:T(8,128)(2,1)S(1)} %slice.74), channel_id=1, source_target_pairs={{0,16},{8,72},{16,0},{24,88},{32,48},{40,104},{48,32},{56,120},{64... | collective-permute-start | bytes 393224 | tf_op jit(solution)/shard_map/ppermute | solution.py:457
  52.1 5.3 %collective-permute-start.21 = (bf16[32,2048]{1,0:T(8,128)(2,1)S(1)}, bf16[32,2048]{1,0:T(8,128)(2,1)S(1)}, u32[]{:S(2)}, u32[]{:S(2)}) collective-permute-start(bf16[32,2048]{1,0:T(8,128)(2,1)S(1)} %slice.75), channel_id=1, source_target_pairs={{0,48},{8,200},{16,32},{24,216},{32,16},{40,232},{48,0},{56,248},{... | collective-permute-start | bytes 393224 | tf_op jit(solution)/shard_map/ppermute | solution.py:457
  54.7 9.4 %collective-permute-start.12 = (bf16[32,2048]{1,0:T(8,128)(2,1)S(1)}, bf16[32,2048]{1,0:T(8,128)(2,1)S(1)}, u32[]{:S(2)}, u32[]{:S(2)}) collective-permute-start(bf16[32,2048]{1,0:T(8,128)(2,1)S(1)} %slice.68), channel_id=1, source_target_pairs={{0,16},{8,72},{16,0},{24,88},{32,48},{40,104},{48,32},{56,120},{64... | collective-permute-start | bytes 393224 | tf_op jit(solution)/shard_map/ppermute | solution.py:457
  54.9 13.8 %collective-permute-start.14 = (bf16[32,2048]{1,0:T(8,128)(2,1)S(1)}, bf16[32,2048]{1,0:T(8,128)(2,1)S(1)}, u32[]{:S(2)}, u32[]{:S(2)}) collective-permute-start(bf16[32,2048]{1,0:T(8,128)(2,1)S(1)} %slice.69), channel_id=1, source_target_pairs={{0,48},{8,200},{16,32},{24,216},{32,16},{40,232},{48,0},{56,248},{... | collective-permute-start | bytes 393224 | tf_op jit(solution)/shard_map/ppermute | solution.py:457
  58.3 14.1 %collective-permute-start.22 = (bf16[64,1024]{1,0:T(8,128)(2,1)S(1)}, bf16[64,1024]{1,0:T(8,128)(2,1)S(1)}, u32[]{:S(2)}, u32[]{:S(2)}) collective-permute-start(bf16[64,1024]{1,0:T(8,128)(2,1)S(1)} %get-tuple-element.45), channel_id=1, source_target_pairs={{0,1},{1,2},{2,3},{3,4},{4,5},{5,6},{6,7},{7,0},{8,9},{9,10},{10,1... | collective-permute-start | bytes 393224 | tf_op jit(solution)/shard_map/ppermute | solution.py:467
  60.1 12.2 %collective-permute-start.23 = (bf16[64,1024]{1,0:T(8,128)(2,1)S(1)}, bf16[64,1024]{1,0:T(8,128)(2,1)S(1)}, u32[]{:S(2)}, u32[]{:S(2)}) collective-permute-start(bf16[64,1024]{1,0:T(8,128)(2,1)S(1)} %get-tuple-element.46), channel_id=1, source_target_pairs={{0,7},{1,0},{2,1},{3,2},{4,3},{5,4},{6,5},{7,6},{8,15},{9,8},{10,9... | collective-permute-start | bytes 393224 | tf_op jit(solution)/shard_map/ppermute | solution.py:467
  64.2 5.7 %collective-permute-start.24 = (bf16[64,512]{1,0:T(8,128)(2,1)S(1)}, bf16[64,512]{1,0:T(8,128)(2,1)S(1)}, u32[]{:S(2)}, u32[]{:S(2)}) collective-permute-start(bf16[64,512]{1,0:T(8,128)(2,1)S(1)} %get-tuple-element.47), channel_id=1, source_target_pairs={{0,2},{1,3},{2,4},{3,5},{4,6},{5,7},{6,0},{7,1},{8,10},{9,11},{10,... | collective-permute-start | bytes 196616 | tf_op jit(solution)/shard_map/ppermute | solution.py:467
  64.2 8.2 %collective-permute-start.25 = (bf16[64,512]{1,0:T(8,128)(2,1)S(1)}, bf16[64,512]{1,0:T(8,128)(2,1)S(1)}, u32[]{:S(2)}, u32[]{:S(2)}) collective-permute-start(bf16[64,512]{1,0:T(8,128)(2,1)S(1)} %get-tuple-element.48), channel_id=1, source_target_pairs={{0,6},{1,7},{2,0},{3,1},{4,2},{5,3},{6,4},{7,5},{8,14},{9,15},{10,... | collective-permute-start | bytes 196616 | tf_op jit(solution)/shard_map/ppermute | solution.py:467
  69.6 13.6 %collective-permute-start.16 = (bf16[64,1024]{1,0:T(8,128)(2,1)S(1)}, bf16[64,1024]{1,0:T(8,128)(2,1)S(1)}, u32[]{:S(2)}, u32[]{:S(2)}) collective-permute-start(bf16[64,1024]{1,0:T(8,128)(2,1)S(1)} %get-tuple-element.41), channel_id=1, source_target_pairs={{0,1},{1,2},{2,3},{3,4},{4,5},{5,6},{6,7},{7,0},{8,9},{9,10},{10,1... | collective-permute-start | bytes 393224 | tf_op jit(solution)/shard_map/ppermute | solution.py:467
  69.8 13.4 %collective-permute-start.17 = (bf16[64,1024]{1,0:T(8,128)(2,1)S(1)}, bf16[64,1024]{1,0:T(8,128)(2,1)S(1)}, u32[]{:S(2)}, u32[]{:S(2)}) collective-permute-start(bf16[64,1024]{1,0:T(8,128)(2,1)S(1)} %get-tuple-element.42), channel_id=1, source_target_pairs={{0,7},{1,0},{2,1},{3,2},{4,3},{5,4},{6,5},{7,6},{8,15},{9,8},{10,9... | collective-permute-start | bytes 393224 | tf_op jit(solution)/shard_map/ppermute | solution.py:467
  72.5 10.8 %collective-permute-start.26 = (bf16[64,1024]{1,0:T(8,128)(2,1)S(1)}, bf16[64,1024]{1,0:T(8,128)(2,1)S(1)}, u32[]{:S(2)}, u32[]{:S(2)}) collective-permute-start(bf16[64,1024]{1,0:T(8,128)(2,1)S(1)} %get-tuple-element.49), channel_id=1, source_target_pairs={{0,2},{1,3},{2,4},{3,5},{4,6},{5,7},{6,0},{7,1},{8,10},{9,11},{10,... | collective-permute-start | bytes 393224 | tf_op jit(solution)/shard_map/ppermute | solution.py:467
  73.9 9.3 %collective-permute-start.27 = (bf16[64,1024]{1,0:T(8,128)(2,1)S(1)}, bf16[64,1024]{1,0:T(8,128)(2,1)S(1)}, u32[]{:S(2)}, u32[]{:S(2)}) collective-permute-start(bf16[64,1024]{1,0:T(8,128)(2,1)S(1)} %get-tuple-element.50), channel_id=1, source_target_pairs={{0,6},{1,7},{2,0},{3,1},{4,2},{5,3},{6,4},{7,5},{8,14},{9,15},{10,... | collective-permute-start | bytes 393224 | tf_op jit(solution)/shard_map/ppermute | solution.py:467
  76.1 12.1 %collective-permute-start.29 = (bf16[4,16,128]{2,1,0:T(8,128)(2,1)S(1)}, bf16[4,16,128]{2,1,0:T(8,128)(2,1)S(1)}, u32[]{:S(2)}, u32[]{:S(2)}) collective-permute-start(bf16[4,16,128]{2,1,0:T(8,128)(2,1)S(1)} %pad_maximum_fusion.2), channel_id=1, source_target_pairs={{0,8},{8,0},{16,24},{24,16},{32,40},{40,32},{48,56},{56,48},{64,72... | collective-permute-start | bytes 49160 | tf_op jit(solution)/shard_map/ppermute | solution.py:440
  83.3 5.8 %collective-permute-start.28 = (bf16[64,512]{1,0:T(8,128)(2,1)S(1)}, bf16[64,512]{1,0:T(8,128)(2,1)S(1)}, u32[]{:S(2)}, u32[]{:S(2)}) collective-permute-start(bf16[64,512]{1,0:T(8,128)(2,1)S(1)} %get-tuple-element.52), channel_id=1, source_target_pairs={{0,8},{8,0},{16,24},{24,16},{32,40},{40,32},{48,56},{56,48},{64,72... | collective-permute-start | bytes 196616 | tf_op jit(solution)/shard_map/ppermute | solution.py:440

commit v7 on v6

--- a/solution.py
+++ b/solution.py
@@ -334,31 +334,41 @@
             yield side, columns, d, jnp.concatenate([first[d, :, columns], chunk], axis=0)
 
 
-def far_body(a, b, w0, w1, first, keep, up, down, up4, down4):
+def far_body(a, b, w0, w1, first, keep, up, down):
     for side, columns, d, whole in last_chunks(a, b, w0, w1, first):
         if d == 0:
             keep[:, columns] = whole
         elif d == 1:
-            up[:, columns] = whole.astype(BF16)
+            up[side] = whole.astype(BF16)
         elif d == 3:
-            down[:, columns] = whole.astype(BF16)
-        elif side == 0:
-            up4[...] = whole.astype(BF16)
+            down[side] = whole.astype(BF16)
         else:
-            down4[...] = whole.astype(BF16)
-
-
-def near_body(a, b, w0, w1, first, keep6, down, keep0, up):
+            (up, down)[side][2] = whole.astype(BF16)
+
+
+def near_body(a, b, w0, w1, first, out):
     for _, columns, d, whole in last_chunks(a, b, w0, w1, first):
-        if d in (0, 2):
-            (keep6, keep0)[d // 2][:, columns] = whole
+        out[d, :, columns] = whole
+
+
+def join_body(near, below, above, keep2, up1, down1, up2, down2):
+    for side in range(2):
+        columns = slice(side * 512, side * 512 + 512)
+        up1[:, columns] = (near[3, :, columns] + below[side].astype(F32)).astype(BF16)
+        down1[:, columns] = (near[1, :, columns] + above[side].astype(F32)).astype(BF16)
+        low, high = keep2[:, columns], near[0, :, columns]
+        if side == 0:
+            low = low + below[2].astype(F32)
         else:
-            (down, up)[d // 2][:, columns] = whole.astype(BF16)
+            high = high + above[2].astype(F32)
+        up2[:, columns] = low.astype(BF16)
+        down2[:, columns] = high.astype(BF16)
 
 
 SUM = jax.ShapeDtypeStruct((64, 1024), F32)
 SENT = jax.ShapeDtypeStruct((64, 1024), BF16)
 HALF = jax.ShapeDtypeStruct((64, 512), BF16)
+THREE = jax.ShapeDtypeStruct((3, 64, 512), BF16)
 
 
 def plain(body, out_shape, *args):
@@ -372,16 +382,9 @@
     )(*args)
 
 
-def middle_body(keep2, keep6, below, above, below4, above4, up, down):
-    up[:, :512] = (keep2[:, :512] + below[:, :512].astype(F32) + below4[...].astype(F32)).astype(BF16)
-    up[:, 512:] = (keep2[:, 512:] + below[:, 512:].astype(F32)).astype(BF16)
-    down[:, :512] = (keep6[:, :512] + above[:, :512].astype(F32)).astype(BF16)
-    down[:, 512:] = (keep6[:, 512:] + above[:, 512:].astype(F32) + above4[...].astype(F32)).astype(BF16)
-
-
-def total_body(keep, below1, above1, below2, above2, own, other):
-    near = keep[...] + below1[...].astype(F32) + above1[...].astype(F32)
-    whole = (near + below2[...].astype(F32) + above2[...].astype(F32)).astype(BF16)
+def total_body(near, below1, above1, below2, above2, own, other):
+    whole = near[2] + below1[...].astype(F32) + above1[...].astype(F32)
+    whole = (whole + below2[...].astype(F32) + above2[...].astype(F32)).astype(BF16)
     own[...] = whole[:, :512]
     other[...] = whole[:, 512:]
 
@@ -492,20 +495,18 @@
     pick = order_rows(place, orders)
 
     parts = [attended] + [turned(attended, k, 0) for k in (1, 2, 3)]
-    far, near = [gathered([a[i : i + 16] for a in parts]) for i in (0, 16)]
+    far = gathered([a[:16] for a in parts])
+    late = lax.optimization_barrier((tuple(a[16:] for a in parts), far[1], far[2]))[0]
+    near = gathered(list(late))
     first_far, first_near = project(far[:3], weights), project(near[:3], weights)
-    keep2, up3, down3, up4, down4 = plain(
-        far_body, [SUM, SENT, SENT, HALF, HALF], *far[3], *weights, first_far
-    )
-    below4, above4 = along_z(up4, 2), along_z(down4, -2)
-    below3, above3 = along_z(up3, 1), along_z(down3, -1)
-    keep6, down1, keep0, up1 = plain(
-        near_body, [SUM, SENT, SUM, SENT], *near[3], *weights, first_near
-    )
+    keep2, up, down = plain(far_body, [SUM, THREE, THREE], *far[3], *weights, first_far)
+    below, above = along_z(up, 2), along_z(down, -2)
+    sums = jax.ShapeDtypeStruct((4, 64, 1024), F32)
+    (sums,) = plain(near_body, [sums], *near[3], *weights, first_near)
+    up1, down1, up2, down2 = plain(join_body, [SENT] * 4, sums, below, above, keep2)
     below1, above1 = along_z(up1, 1), along_z(down1, -1)
-    up2, down2 = plain(middle_body, [SENT, SENT], keep2, keep6, below3, above3, below4, above4)
     below2, above2 = along_z(up2, 2), along_z(down2, -2)
-    own, other = plain(total_body, [HALF, HALF], keep0, below1, above1, below2, above2)
+    own, other = plain(total_body, [HALF, HALF], sums, below1, above1, below2, above2)
     return finish(own, other_core(other), pick)
 
 

time: 90.2 us -> 96.8 us (1.073); the launches traced: 90.1 us -> 95 us
  waiting for transfers between devices: 16.2 us -> 22 us
  starting transfers between devices: 52.1 us -> 51.1 us
    ppermute x8 -> x6, waiting for transfers between devices: 0.16 us -> 4.17 us  [along_z(): lax.ppermute(value, 'head', [(i, (i + k) % HEADS) for i in range(HEADS)])]
    ppermute x8 -> x6, starting transfers between devices: 15.7 us -> 12.7 us  [along_z(): lax.ppermute(value, 'head', [(i, (i + k) % HEADS) for i in range(HEADS)])]
    ppermute x11, waiting for transfers between devices: 9.51 us -> 11.9 us  [turned(): return lax.ppermute(value, 'batch', pairs)]
    ppermute x11, starting transfers between devices: 25.7 us -> 27.7 us  [along(): lax.ppermute(value, 'batch', [(i, i ^ k << shift) for i in range(BATCH)])]
  transfers between devices with their start and end apart: 30 -> 28, of which waited for: 13 -> 13; matrix products, arithmetic and copies ran while one was open for 1% -> 1% of each run, Pallas kernels for 16% -> 16%
where the time goes in v7:
time: 96.8 us; the launch traced here: 95 us
  starting transfers between devices  51.1 us (53%)
  waiting for transfers between devices  22 us (23%)
  Pallas kernels  19.8 us (20%)
  local copies, waits for them, and re-layouts  1.71 us (2%)
    ppermute x11, starting transfers between devices, along(): lax.ppermute(value, 'batch', [(i, i ^ k << shift) for i in range(BATCH)])  27.7 us
    ppermute x6, starting transfers between devices, along_z(): lax.ppermute(value, 'head', [(i, (i + k) % HEADS) for i in range(HEADS)])  12.7 us
    ppermute x11, waiting for transfers between devices, turned(): return lax.ppermute(value, 'batch', pairs)  11.9 us
    ppermute x11, starting transfers between devices, turned(): return lax.ppermute(value, 'batch', pairs)  10.7 us
    ppermute x11, waiting for transfers between devices, along(): lax.ppermute(value, 'batch', [(i, i ^ k << shift) for i in range(BATCH)])  5.99 us
    pallas_call x2, Pallas kernels, prefix_keep(): pl.pallas_call(prefix_keep_body, out_shape=[out, out], in_specs=[VMEM] *...  4.34 us
    pallas_call x1, Pallas kernels, local_parts(): pl.pallas_call(local_body, out_shape=[out] * 4, in_specs=[SMEM] + [HBM] *...  4.23 us
    ppermute x6, waiting for transfers between devices, along_z(): lax.ppermute(value, 'head', [(i, (i + k) % HEADS) for i in range(HEADS)])  4.17 us
  transfers between devices with their start and end apart: 28, of which 13 were waited for; matrix products, arithmetic and copies ran while one was open for 1% of the time, Pallas kernels for 16%

profile of v7, /device:TPU:1, one launch (start us, length us, event | category | flops | bytes accessed | tf_op | source)
XLA Modules:
  0.0 95.0 jit_solution(2684292430223815279)
XLA Ops:
  0.0 3.2 %collective-permute-start.3 = (bf16[2,2048,128]{2,1,0:T(8,128)(2,1)}, bf16[2,2048,128]{2,1,0:T(8,128)(2,1)S(1)}, u32[]{:S(2)}, u32[]{:S(2)}) collective-permute-start(bf16[2,2048,128]{2,1,0:T(8,128)(2,1)} %kv0.5), channel_id=1, source_target_pairs={{0,8},{8,0},{16,24},{24,16},{32,40},{40,32},{48,56},{56,48},{64,72... | collective-permute-start | bytes 3145736 | tf_op jit(solution)/shard_map/ppermute | solution.py:443
  3.2 0.7 stack.34.place
  3.9 4.2 %local_parts.1 = (bf16[18,16,128]{2,1,0:T(8,128)(2,1)}, bf16[18,16,128]{2,1,0:T(8,128)(2,1)}, bf16[18,16,128]{2,1,0:T(8,128)(2,1)}, bf16[18,16,128]{2,1,0:T(8,128)(2,1)}) custom-call(s32[7]{0:T(128)} %stack.34.place, bf16[32,2048]{1,0:T(8,128)(2,1)} %q_in.1, s32[32]{0:T(128)} %prompt_in.1, s32[8,32]{1,0:T(8,128)} %bitcast.8, s32[32]{0:T(128)} %length_in.1, ...), custom_call_target="tpu_custom_call" | custom-call | tf_op jit(solution)/shard_map/local_parts/pallas_call | solution.py:124
  8.2 0.1 collective-permute-start
  8.3 1.9 %collective-permute-start.1 = (bf16[18,16,128]{2,1,0:T(8,128)(2,1)}, bf16[18,16,128]{2,1,0:T(8,128)(2,1)S(1)}, u32[]{:S(2)}, u32[]{:S(2)}) collective-permute-start(bf16[18,16,128]{2,1,0:T(8,128)(2,1)} %get-tuple-element.31), channel_id=1, source_target_pairs={{0,128},{8,136},{16,144},{24,152},{32,160},{40,168},{48,176},{56,1... | collective-permute-start | bytes 221192 | tf_op jit(solution)/shard_map/ppermute | solution.py:443
  10.2 1.9 %collective-permute-start.2 = (bf16[18,16,128]{2,1,0:T(8,128)(2,1)}, bf16[18,16,128]{2,1,0:T(8,128)(2,1)S(1)}, u32[]{:S(2)}, u32[]{:S(2)}) collective-permute-start(bf16[18,16,128]{2,1,0:T(8,128)(2,1)} %get-tuple-element.32), channel_id=1, source_target_pairs={{0,192},{8,200},{16,208},{24,216},{32,224},{40,232},{48,240},{56,2... | collective-permute-start | bytes 221192 | tf_op jit(solution)/shard_map/ppermute | solution.py:443
  12.1 0.2 collective-permute-done.a1.s1
  12.3 2.0 %collective-permute-done.1.a2.s2 = bf16[18,16,128]{2,1,0:T(8,128)(2,1)S(1)} collective-permute-done((bf16[18,16,128]{2,1,0:T(8,128)(2,1)}, bf16[18,16,128]{2,1,0:T(8,128)(2,1)S(1)}, u32[]{:S(2)}, u32[]{:S(2)}) %collective-permute-start.1) | collective-permute-done | bytes 73760 | tf_op jit(solution)/shard_map/ppermute | solution.py:443
  14.4 1.4 %collective-permute-done.2.a3.s3 = bf16[18,16,128]{2,1,0:T(8,128)(2,1)S(1)} collective-permute-done((bf16[18,16,128]{2,1,0:T(8,128)(2,1)}, bf16[18,16,128]{2,1,0:T(8,128)(2,1)S(1)}, u32[]{:S(2)}, u32[]{:S(2)}) %collective-permute-start.2) | collective-permute-done | bytes 73760 | tf_op jit(solution)/shard_map/ppermute | solution.py:443
  15.8 0.9 copy-done.2
  16.7 0.6 regroup.1
  17.3 3.0 %collective-permute-start.4 = (bf16[37,16,128]{2,1,0:T(8,128)(2,1)S(1)}, bf16[37,16,128]{2,1,0:T(8,128)(2,1)S(1)}, u32[]{:S(2)}, u32[]{:S(2)}) collective-permute-start(bf16[37,16,128]{2,1,0:T(8,128)(2,1)S(1)} %get-tuple-element.36), channel_id=1, source_target_pairs={{0,32},{8,40},{16,48},{24,56},{32,0},{40,8},{48,16},{56,24},{64,96... | collective-permute-start | bytes 454664 | tf_op jit(solution)/shard_map/ppermute | solution.py:443
  20.3 0.8 collective-permute-start.6
  21.1 0.0 collective-permute-start.5
  21.1 0.0 collective-permute-done.3.kv1
  21.1 2.2 %prefix_keep.2 = (f32[16,16,128]{2,1,0:T(8,128)S(1)}, f32[16,16,128]{2,1,0:T(8,128)S(1)}) custom-call(bf16[17,16,128]{2,1,0:T(8,128)(2,1)S(1)} %get-tuple-element.33.q, bf16[2,2048,128]{2,1,0:T(8,128)(2,1)S(1)} %copy-done.1, bf16[2,2048,128]{2,1,0:T(8,128)(2,1)S(1)} %collective-permute-done.3.kv1), custom_call_target="tpu_custom_call" | custom-call | flops 536870912 | bytes 2500000 | tf_op jit(solution)/shard_map/prefix_keep/pallas_call | solution.py:238
  23.3 0.0 copy-start
  23.3 2.0 %collective-permute-done.6.qb = bf16[17,16,128]{2,1,0:T(8,128)(2,1)S(1)} collective-permute-done((bf16[17,16,128]{2,1,0:T(8,128)(2,1)S(1)}, bf16[17,16,128]{2,1,0:T(8,128)(2,1)S(1)}, u32[]{:S(2)}, u32[]{:S(2)}) %collective-permute-start.6) | collective-permute-done | bytes 69664 | tf_op jit(solution)/shard_map/ppermute | solution.py:443
  25.3 4.1 %prefix_send.1 = bf16[33,16,128]{2,1,0:T(8,128)(2,1)S(1)} custom-call(bf16[17,16,128]{2,1,0:T(8,128)(2,1)S(1)} %collective-permute-done.5.qa, bf16[17,16,128]{2,1,0:T(8,128)(2,1)S(1)} %collective-permute-done.6.qb, bf16[2,2048,128]{2,1,0:T(8,128)(2,1)S(1)} %copy-done.1, bf16[2,2048,128]{2,1,0:T(8,128)(2,1)S(1)} %collective-permute-done.3.kv1, ...), custom_call_target="tpu_custom_call" | custom-call | flops 1073741824 | bytes 2500000 | tf_op jit(solution)/shard_map/prefix_send/pallas_call | solution.py:225
  29.4 0.0 copy-start.3
  29.4 2.3 %collective-permute-start.7 = (bf16[33,16,128]{2,1,0:T(8,128)(2,1)S(1)}, bf16[33,16,128]{2,1,0:T(8,128)(2,1)S(1)}, u32[]{:S(2)}, u32[]{:S(2)}) collective-permute-start(bf16[33,16,128]{2,1,0:T(8,128)(2,1)S(1)} %prefix_send.1), channel_id=1, source_target_pairs={{0,16},{8,24},{16,0},{24,8},{32,48},{40,56},{48,32},{56,40},{64,80... | collective-permute-start | bytes 405512 | tf_op jit(solution)/shard_map/ppermute | solution.py:443
  31.7 0.9 collective-permute-start.17
  32.6 2.2 %prefix_keep.3 = (f32[16,16,128]{2,1,0:T(8,128)S(1)}, f32[16,16,128]{2,1,0:T(8,128)S(1)}) custom-call(bf16[37,16,128]{2,1,0:T(8,128)(2,1)S(1)} %collective-permute-done.4.q.later.far, bf16[2,2048,128]{2,1,0:T(8,128)(2,1)S(1)} %copy-done.1, bf16[2,2048,128]{2,1,0:T(8,128)(2,1)S(1)} %collective-permute-done.3.kv1), custom_call_target="tpu_custom_call" | custom-call | flops 536870912 | bytes 2500000 | tf_op jit(solution)/shard_map/prefix_keep/pallas_call | solution.py:238
  34.8 0.0 collective-permute-done.7.message
  34.8 1.2 %combine.1 = bf16[32,2048]{1,0:T(8,128)(2,1)S(1)} custom-call(s32[7]{0:T(128)S(1)} %copy-done.4, f32[16,16,128]{2,1,0:T(8,128)S(1)} %get-tuple-element.34.own, f32[16,16,128]{2,1,0:T(8,128)S(1)} %get-tuple-element.35.after.own_masses, f32[16,16,128]{2,1,0:T(8,128)S(1)} %get-tuple-element.37.cross, f32[16,16,128]{2,1,0:T(8,128)S(1)} %get-tuple-element.38.cross_masses, ...), custom_call_target="tpu_custom_call" | custom-call | tf_op jit(solution)/shard_map/combine/pallas_call | solution.py:281
  36.0 2.8 %collective-permute-start.10 = (bf16[32,2048]{1,0:T(8,128)(2,1)S(1)}, bf16[32,2048]{1,0:T(8,128)(2,1)S(1)}, u32[]{:S(2)}, u32[]{:S(2)}) collective-permute-start(bf16[32,2048]{1,0:T(8,128)(2,1)S(1)} %combine.1), channel_id=1, source_target_pairs={{0,192},{8,56},{16,208},{24,40},{32,224},{40,24},{48,240},{56,8},{... | collective-permute-start | bytes 393224 | tf_op jit(solution)/shard_map/ppermute | solution.py:460
  38.8 0.6 collective-permute-start.9
  39.4 0.1 collective-permute-start.8
  39.5 2.6 %collective-permute-done.10 = bf16[32,2048]{1,0:T(8,128)(2,1)S(1)} collective-permute-done((bf16[32,2048]{1,0:T(8,128)(2,1)S(1)}, bf16[32,2048]{1,0:T(8,128)(2,1)S(1)}, u32[]{:S(2)}, u32[]{:S(2)}) %collective-permute-start.10) | collective-permute-done | bytes 131104 | tf_op jit(solution)/shard_map/ppermute | solution.py:460
  42.1 2.1 %collective-permute-done.9 = bf16[32,2048]{1,0:T(8,128)(2,1)S(1)} collective-permute-done((bf16[32,2048]{1,0:T(8,128)(2,1)S(1)}, bf16[32,2048]{1,0:T(8,128)(2,1)S(1)}, u32[]{:S(2)}, u32[]{:S(2)}) %collective-permute-start.9) | collective-permute-done | bytes 131104 | tf_op jit(solution)/shard_map/ppermute | solution.py:460
  44.2 0.0 collective-permute-done.8
  44.3 1.9 %collective-permute-start.12 = (bf16[64,2048]{1,0:T(8,128)(2,1)S(1)}, bf16[64,2048]{1,0:T(8,128)(2,1)S(1)}, u32[]{:S(2)}, u32[]{:S(2)}) collective-permute-start(bf16[64,2048]{1,0:T(8,128)(2,1)S(1)} %pad_maximum_fusion.a), channel_id=1, source_target_pairs={{0,48},{8,200},{16,32},{24,216},{32,16},{40,232},{48,0},{56,248},{... | collective-permute-start | bytes 786440 | tf_op jit(solution)/shard_map/ppermute | solution.py:460
  46.2 4.9 %collective-permute-done.12.c = bf16[64,2048]{1,0:T(8,128)(2,1)S(1)} collective-permute-done((bf16[64,2048]{1,0:T(8,128)(2,1)S(1)}, bf16[64,2048]{1,0:T(8,128)(2,1)S(1)}, u32[]{:S(2)}, u32[]{:S(2)}) %collective-permute-start.12) | collective-permute-done | bytes 262176 | tf_op jit(solution)/shard_map/ppermute | solution.py:460
  51.1 0.6 collective-permute-done.11.b
  51.8 0.1 collective-permute-start.15
  51.9 1.3 %collective-permute-start.13 = (bf16[64,2048]{1,0:T(8,128)(2,1)S(1)}, bf16[64,2048]{1,0:T(8,128)(2,1)S(1)}, u32[]{:S(2)}, u32[]{:S(2)}) collective-permute-start(bf16[64,2048]{1,0:T(8,128)(2,1)S(1)} %constant_dynamic-update-slice_fusion.a), channel_id=1, source_target_pairs={{0,48},{8,200},{16,32},{24,216},{32,16},{40,232},{48,0},{56,248},{... | collective-permute-start | bytes 786440 | tf_op jit(solution)/shard_map/ppermute | solution.py:460
  53.2 0.8 collective-permute-start.18
  54.0 1.5 %collective-permute-start.19 = (bf16[32,2048]{1,0:T(8,128)(2,1)S(1)}, bf16[32,2048]{1,0:T(8,128)(2,1)S(1)}, u32[]{:S(2)}, u32[]{:S(2)}) collective-permute-start(bf16[32,2048]{1,0:T(8,128)(2,1)S(1)} %slice.75), channel_id=1, source_target_pairs={{0,48},{8,200},{16,32},{24,216},{32,16},{40,232},{48,0},{56,248},{... | collective-permute-start | bytes 393224 | tf_op jit(solution)/shard_map/ppermute | solution.py:460
  55.6 1.5 %collective-permute-done.15.b = bf16[64,2048]{1,0:T(8,128)(2,1)S(1)} collective-permute-done((bf16[64,2048]{1,0:T(8,128)(2,1)S(1)}, bf16[64,2048]{1,0:T(8,128)(2,1)S(1)}, u32[]{:S(2)}, u32[]{:S(2)}) %collective-permute-start.15) | collective-permute-done | bytes 262176 | tf_op jit(solution)/shard_map/ppermute | solution.py:460
  57.1 1.3 %collective-permute-start.16 = (bf16[32,2048]{1,0:T(8,128)(2,1)S(1)}, bf16[32,2048]{1,0:T(8,128)(2,1)S(1)}, u32[]{:S(2)}, u32[]{:S(2)}) collective-permute-start(bf16[32,2048]{1,0:T(8,128)(2,1)S(1)} %slice.73), channel_id=1, source_target_pairs={{0,48},{8,200},{16,32},{24,216},{32,16},{40,232},{48,0},{56,248},{... | collective-permute-start | bytes 393224 | tf_op jit(solution)/shard_map/ppermute | solution.py:460
  58.4 0.2 collective-permute-start.14
  58.6 0.0 collective-permute-done.17.w1
  58.6 1.0 %project.3.first = f32[4,48,1024]{2,1,0:T(8,128)S(1)} custom-call(bf16[64,2048]{1,0:T(8,128)(2,1)S(1)} %pad_maximum_fusion.a, bf16[64,2048]{1,0:T(8,128)(2,1)S(1)} %collective-permute-done.11.b, bf16[64,2048]{1,0:T(8,128)(2,1)S(1)} %collective-permute-done.12.c, bf16[2048,512]{1,0:T(8,128)(2,1)S(1)} %copy-done, bf16[2048,512]{1,0:T(8,128)(2,1)S(1)} %collective-permute-done.17.w1), custom_call_target="tpu_custom_call" | custom-call | flops 805306368 | bytes 4500000 | tf_op jit(solution)/shard_map/project/pallas_call | solution.py:316
  59.6 0.0 collective-permute-done.18.a
  59.7 0.1 collective-permute-done.19.b
  59.8 0.8 far.1
  60.6 3.1 %collective-permute-start.20 = (bf16[3,64,512]{2,1,0:T(8,128)(2,1)S(1)}, bf16[3,64,512]{2,1,0:T(8,128)(2,1)S(1)}, u32[]{:S(2)}, u32[]{:S(2)}) collective-permute-start(bf16[3,64,512]{2,1,0:T(8,128)(2,1)S(1)} %get-tuple-element.44), channel_id=1, source_target_pairs={{0,2},{1,3},{2,4},{3,5},{4,6},{5,7},{6,0},{7,1},{8,10},{9,11},{10,... | collective-permute-start | bytes 589832 | tf_op jit(solution)/shard_map/ppermute | solution.py:470
  63.7 3.3 %collective-permute-start.21 = (bf16[3,64,512]{2,1,0:T(8,128)(2,1)S(1)}, bf16[3,64,512]{2,1,0:T(8,128)(2,1)S(1)}, u32[]{:S(2)}, u32[]{:S(2)}) collective-permute-start(bf16[3,64,512]{2,1,0:T(8,128)(2,1)S(1)} %get-tuple-element.45), channel_id=1, source_target_pairs={{0,6},{1,7},{2,0},{3,1},{4,2},{5,3},{6,4},{7,5},{8,14},{9,15},{10,... | collective-permute-start | bytes 589832 | tf_op jit(solution)/shard_map/ppermute | solution.py:470
  67.1 1.0 %project.2.first = f32[4,48,1024]{2,1,0:T(8,128)S(1)} custom-call(bf16[64,2048]{1,0:T(8,128)(2,1)S(1)} %constant_dynamic-update-slice_fusion.a, bf16[64,2048]{1,0:T(8,128)(2,1)S(1)} %collective-permute-done.15.b, bf16[64,2048]{1,0:T(8,128)(2,1)S(1)} %collective-permute-done.13.c, bf16[2048,512]{1,0:T(8,128)(2,1)S(1)} %copy-done, ...), custom_call_target="tpu_custom_call" | custom-call | flops 805306368 | bytes 4500000 | tf_op jit(solution)/shard_map/project/pallas_call | solution.py:316
  68.1 0.0 collective-permute-done.16.b
  68.1 0.8 near.1
  68.9 1.5 %collective-permute-done.20.below = bf16[3,64,512]{2,1,0:T(8,128)(2,1)S(1)} collective-permute-done((bf16[3,64,512]{2,1,0:T(8,128)(2,1)S(1)}, bf16[3,64,512]{2,1,0:T(8,128)(2,1)S(1)}, u32[]{:S(2)}, u32[]{:S(2)}) %collective-permute-start.20) | collective-permute-done | bytes 196640 | tf_op jit(solution)/shard_map/ppermute | solution.py:470
  70.4 2.7 %collective-permute-done.21.above = bf16[3,64,512]{2,1,0:T(8,128)(2,1)S(1)} collective-permute-done((bf16[3,64,512]{2,1,0:T(8,128)(2,1)S(1)}, bf16[3,64,512]{2,1,0:T(8,128)(2,1)S(1)}, u32[]{:S(2)}, u32[]{:S(2)}) %collective-permute-start.21) | collective-permute-done | bytes 196640 | tf_op jit(solution)/shard_map/ppermute | solution.py:470
  73.1 0.1 join.1
  73.2 0.1 collective-permute-start.22
  73.3 2.7 %collective-permute-start.23 = (bf16[64,1024]{1,0:T(8,128)(2,1)S(1)}, bf16[64,1024]{1,0:T(8,128)(2,1)S(1)}, u32[]{:S(2)}, u32[]{:S(2)}) collective-permute-start(bf16[64,1024]{1,0:T(8,128)(2,1)S(1)} %get-tuple-element.48), channel_id=1, source_target_pairs={{0,7},{1,0},{2,1},{3,2},{4,3},{5,4},{6,5},{7,6},{8,15},{9,8},{10,9... | collective-permute-start | bytes 393224 | tf_op jit(solution)/shard_map/ppermute | solution.py:470
  75.9 2.4 %collective-permute-start.24 = (bf16[64,1024]{1,0:T(8,128)(2,1)S(1)}, bf16[64,1024]{1,0:T(8,128)(2,1)S(1)}, u32[]{:S(2)}, u32[]{:S(2)}) collective-permute-start(bf16[64,1024]{1,0:T(8,128)(2,1)S(1)} %get-tuple-element.49), channel_id=1, source_target_pairs={{0,2},{1,3},{2,4},{3,5},{4,6},{5,7},{6,0},{7,1},{8,10},{9,11},{10,... | collective-permute-start | bytes 393224 | tf_op jit(solution)/shard_map/ppermute | solution.py:470
  78.3 1.2 %collective-permute-start.25 = (bf16[64,1024]{1,0:T(8,128)(2,1)S(1)}, bf16[64,1024]{1,0:T(8,128)(2,1)S(1)}, u32[]{:S(2)}, u32[]{:S(2)}) collective-permute-start(bf16[64,1024]{1,0:T(8,128)(2,1)S(1)} %get-tuple-element.50), channel_id=1, source_target_pairs={{0,6},{1,7},{2,0},{3,1},{4,2},{5,3},{6,4},{7,5},{8,14},{9,15},{10,... | collective-permute-start | bytes 393224 | tf_op jit(solution)/shard_map/ppermute | solution.py:470
  79.5 7.9 %collective-permute-start.27 = (bf16[4,16,128]{2,1,0:T(8,128)(2,1)S(1)}, bf16[4,16,128]{2,1,0:T(8,128)(2,1)S(1)}, u32[]{:S(2)}, u32[]{:S(2)}) collective-permute-start(bf16[4,16,128]{2,1,0:T(8,128)(2,1)S(1)} %pad_maximum_fusion.1), channel_id=1, source_target_pairs={{0,8},{8,0},{16,24},{24,16},{32,40},{40,32},{48,56},{56,48},{64,72... | collective-permute-start | bytes 49160 | tf_op jit(solution)/shard_map/ppermute | solution.py:443
  87.5 0.1 total.1
  87.6 5.5 %collective-permute-start.26 = (bf16[64,512]{1,0:T(8,128)(2,1)S(1)}, bf16[64,512]{1,0:T(8,128)(2,1)S(1)}, u32[]{:S(2)}, u32[]{:S(2)}) collective-permute-start(bf16[64,512]{1,0:T(8,128)(2,1)S(1)} %get-tuple-element.52), channel_id=1, source_target_pairs={{0,8},{8,0},{16,24},{24,16},{32,40},{40,32},{48,56},{56,48},{64,72... | collective-permute-start | bytes 196616 | tf_op jit(solution)/shard_map/ppermute | solution.py:443
  93.2 0.6 order_rows.1.pick
  93.8 0.2 collective-permute-done.26.other
  94.0 0.9 finish.1
  (36 shorter events, 0.2 us)
Async XLA Ops:
  0.0 21.1 %copy-start.1 = (bf16[2,2048,128]{2,1,0:T(8,128)(2,1)S(1)}, bf16[2,2048,128]{2,1,0:T(8,128)(2,1)}, u32[]{:S(2)}) copy-start(bf16[2,2048,128]{2,1,0:T(8,128)(2,1)} %kv0.5) | copy-start | bytes 3145732
  0.0 21.1 %collective-permute-start.3 = (bf16[2,2048,128]{2,1,0:T(8,128)(2,1)}, bf16[2,2048,128]{2,1,0:T(8,128)(2,1)S(1)}, u32[]{:S(2)}, u32[]{:S(2)}) collective-permute-start(bf16[2,2048,128]{2,1,0:T(8,128)(2,1)} %kv0.5), channel_id=1, source_target_pairs={{0,8},{8,0},{16,24},{24,16},{32,40},{40,32},{48,56},{56,48},{64,72... | collective-permute-start | bytes 3145736 | tf_op jit(solution)/shard_map/ppermute | solution.py:443
  3.9 11.9 %copy-start.4 = (s32[7]{0:T(128)S(1)}, s32[7]{0:T(128)}, u32[]{:S(2)}) copy-start(s32[7]{0:T(128)} %stack.34.place) | copy-start | bytes 88
  8.2 4.2 %collective-permute-start = (bf16[18,16,128]{2,1,0:T(8,128)(2,1)}, bf16[18,16,128]{2,1,0:T(8,128)(2,1)S(1)}, u32[]{:S(2)}, u32[]{:S(2)}) collective-permute-start(bf16[18,16,128]{2,1,0:T(8,128)(2,1)} %get-tuple-element.30), channel_id=1, source_target_pairs={{0,64},{8,72},{16,80},{24,88},{32,96},{40,104},{48,112},{56,120},{... | collective-permute-start | bytes 221192 | tf_op jit(solution)/shard_map/ppermute | solution.py:443
  8.3 6.1 %collective-permute-start.1 = (bf16[18,16,128]{2,1,0:T(8,128)(2,1)}, bf16[18,16,128]{2,1,0:T(8,128)(2,1)S(1)}, u32[]{:S(2)}, u32[]{:S(2)}) collective-permute-start(bf16[18,16,128]{2,1,0:T(8,128)(2,1)} %get-tuple-element.31), channel_id=1, source_target_pairs={{0,128},{8,136},{16,144},{24,152},{32,160},{40,168},{48,176},{56,1... | collective-permute-start | bytes 221192 | tf_op jit(solution)/shard_map/ppermute | solution.py:443
  10.2 5.6 %collective-permute-start.2 = (bf16[18,16,128]{2,1,0:T(8,128)(2,1)}, bf16[18,16,128]{2,1,0:T(8,128)(2,1)S(1)}, u32[]{:S(2)}, u32[]{:S(2)}) collective-permute-start(bf16[18,16,128]{2,1,0:T(8,128)(2,1)} %get-tuple-element.32), channel_id=1, source_target_pairs={{0,192},{8,200},{16,208},{24,216},{32,224},{40,232},{48,240},{56,2... | collective-permute-start | bytes 221192 | tf_op jit(solution)/shard_map/ppermute | solution.py:443
  15.8 0.9 copy-start.2
  17.3 8.0 %collective-permute-start.4 = (bf16[37,16,128]{2,1,0:T(8,128)(2,1)S(1)}, bf16[37,16,128]{2,1,0:T(8,128)(2,1)S(1)}, u32[]{:S(2)}, u32[]{:S(2)}) collective-permute-start(bf16[37,16,128]{2,1,0:T(8,128)(2,1)S(1)} %get-tuple-element.36), channel_id=1, source_target_pairs={{0,32},{8,40},{16,48},{24,56},{32,0},{40,8},{48,16},{56,24},{64,96... | collective-permute-start | bytes 454664 | tf_op jit(solution)/shard_map/ppermute | solution.py:443
  20.3 5.0 %collective-permute-start.6 = (bf16[17,16,128]{2,1,0:T(8,128)(2,1)S(1)}, bf16[17,16,128]{2,1,0:T(8,128)(2,1)S(1)}, u32[]{:S(2)}, u32[]{:S(2)}) collective-permute-start(bf16[17,16,128]{2,1,0:T(8,128)(2,1)S(1)} %get-tuple-element.39), channel_id=1, source_target_pairs={{0,48},{8,56},{16,32},{24,40},{32,16},{40,24},{48,0},{56,8},{64,11... | collective-permute-start | bytes 208904 | tf_op jit(solution)/shard_map/ppermute | solution.py:443
  21.1 4.2 %collective-permute-start.5 = (bf16[17,16,128]{2,1,0:T(8,128)(2,1)S(1)}, bf16[17,16,128]{2,1,0:T(8,128)(2,1)S(1)}, u32[]{:S(2)}, u32[]{:S(2)}) collective-permute-start(bf16[17,16,128]{2,1,0:T(8,128)(2,1)S(1)} %get-tuple-element.33.q), channel_id=1, source_target_pairs={{0,16},{8,24},{16,0},{24,8},{32,48},{40,56},{48,32},{56,40},{64,80... | collective-permute-start | bytes 208904 | tf_op jit(solution)/shard_map/ppermute | solution.py:443
  23.3 8.4 %copy-start = (bf16[2048,512]{1,0:T(8,128)(2,1)S(1)}, bf16[2048,512]{1,0:T(8,128)(2,1)}, u32[]{:S(2)}) copy-start(bf16[2048,512]{1,0:T(8,128)(2,1)} %w0.7) | copy-start | bytes 6291460
  29.4 5.4 %copy-start.3 = (bf16[18,16,128]{2,1,0:T(8,128)(2,1)S(1)}, bf16[18,16,128]{2,1,0:T(8,128)(2,1)}, u32[]{:S(2)}) copy-start(bf16[18,16,128]{2,1,0:T(8,128)(2,1)} %get-tuple-element.29.a0.s0) | copy-start | bytes 221188
  29.4 5.4 %collective-permute-start.7 = (bf16[33,16,128]{2,1,0:T(8,128)(2,1)S(1)}, bf16[33,16,128]{2,1,0:T(8,128)(2,1)S(1)}, u32[]{:S(2)}, u32[]{:S(2)}) collective-permute-start(bf16[33,16,128]{2,1,0:T(8,128)(2,1)S(1)} %prefix_send.1), channel_id=1, source_target_pairs={{0,16},{8,24},{16,0},{24,8},{32,48},{40,56},{48,32},{56,40},{64,80... | collective-permute-start | bytes 405512 | tf_op jit(solution)/shard_map/ppermute | solution.py:443
  31.7 26.9 %collective-permute-start.17 = (bf16[2048,512]{1,0:T(8,128)(2,1)S(1)}, bf16[2048,512]{1,0:T(8,128)(2,1)S(1)}, u32[]{:S(2)}, u32[]{:S(2)}) collective-permute-start(bf16[2048,512]{1,0:T(8,128)(2,1)S(1)} %copy-done), channel_id=1, source_target_pairs={{0,8},{8,0},{16,24},{24,16},{32,40},{40,32},{48,56},{56,48},{64,72... | collective-permute-start | bytes 6291464 | tf_op jit(solution)/shard_map/ppermute | solution.py:443
  36.0 6.1 %collective-permute-start.10 = (bf16[32,2048]{1,0:T(8,128)(2,1)S(1)}, bf16[32,2048]{1,0:T(8,128)(2,1)S(1)}, u32[]{:S(2)}, u32[]{:S(2)}) collective-permute-start(bf16[32,2048]{1,0:T(8,128)(2,1)S(1)} %combine.1), channel_id=1, source_target_pairs={{0,192},{8,56},{16,208},{24,40},{32,224},{40,24},{48,240},{56,8},{... | collective-permute-start | bytes 393224 | tf_op jit(solution)/shard_map/ppermute | solution.py:460
  38.8 5.4 %collective-permute-start.9 = (bf16[32,2048]{1,0:T(8,128)(2,1)S(1)}, bf16[32,2048]{1,0:T(8,128)(2,1)S(1)}, u32[]{:S(2)}, u32[]{:S(2)}) collective-permute-start(bf16[32,2048]{1,0:T(8,128)(2,1)S(1)} %combine.1), channel_id=1, source_target_pairs={{0,128},{8,40},{16,144},{24,56},{32,160},{40,8},{48,176},{56,24},{... | collective-permute-start | bytes 393224 | tf_op jit(solution)/shard_map/ppermute | solution.py:460
  39.4 4.8 %collective-permute-start.8 = (bf16[32,2048]{1,0:T(8,128)(2,1)S(1)}, bf16[32,2048]{1,0:T(8,128)(2,1)S(1)}, u32[]{:S(2)}, u32[]{:S(2)}) collective-permute-start(bf16[32,2048]{1,0:T(8,128)(2,1)S(1)} %combine.1), channel_id=1, source_target_pairs={{0,64},{8,24},{16,80},{24,8},{32,96},{40,56},{48,112},{56,40},{64,... | collective-permute-start | bytes 393224 | tf_op jit(solution)/shard_map/ppermute | solution.py:460
  44.3 6.8 %collective-permute-start.12 = (bf16[64,2048]{1,0:T(8,128)(2,1)S(1)}, bf16[64,2048]{1,0:T(8,128)(2,1)S(1)}, u32[]{:S(2)}, u32[]{:S(2)}) collective-permute-start(bf16[64,2048]{1,0:T(8,128)(2,1)S(1)} %pad_maximum_fusion.a), channel_id=1, source_target_pairs={{0,48},{8,200},{16,32},{24,216},{32,16},{40,232},{48,0},{56,248},{... | collective-permute-start | bytes 786440 | tf_op jit(solution)/shard_map/ppermute | solution.py:460
  46.2 5.5 %collective-permute-start.11 = (bf16[64,2048]{1,0:T(8,128)(2,1)S(1)}, bf16[64,2048]{1,0:T(8,128)(2,1)S(1)}, u32[]{:S(2)}, u32[]{:S(2)}) collective-permute-start(bf16[64,2048]{1,0:T(8,128)(2,1)S(1)} %pad_maximum_fusion.a), channel_id=1, source_target_pairs={{0,16},{8,72},{16,0},{24,88},{32,48},{40,104},{48,32},{56,120},{64... | collective-permute-start | bytes 786440 | tf_op jit(solution)/shard_map/ppermute | solution.py:460
  51.8 5.3 %collective-permute-start.15 = (bf16[64,2048]{1,0:T(8,128)(2,1)S(1)}, bf16[64,2048]{1,0:T(8,128)(2,1)S(1)}, u32[]{:S(2)}, u32[]{:S(2)}) collective-permute-start(bf16[64,2048]{1,0:T(8,128)(2,1)S(1)} %constant_dynamic-update-slice_fusion.a), channel_id=1, source_target_pairs={{0,16},{8,72},{16,0},{24,88},{32,48},{40,104},{48,32},{56,120},{64... | collective-permute-start | bytes 786440 | tf_op jit(solution)/shard_map/ppermute | solution.py:460
  51.9 6.5 %collective-permute-start.13 = (bf16[64,2048]{1,0:T(8,128)(2,1)S(1)}, bf16[64,2048]{1,0:T(8,128)(2,1)S(1)}, u32[]{:S(2)}, u32[]{:S(2)}) collective-permute-start(bf16[64,2048]{1,0:T(8,128)(2,1)S(1)} %constant_dynamic-update-slice_fusion.a), channel_id=1, source_target_pairs={{0,48},{8,200},{16,32},{24,216},{32,16},{40,232},{48,0},{56,248},{... | collective-permute-start | bytes 786440 | tf_op jit(solution)/shard_map/ppermute | solution.py:460
  53.2 6.5 %collective-permute-start.18 = (bf16[32,2048]{1,0:T(8,128)(2,1)S(1)}, bf16[32,2048]{1,0:T(8,128)(2,1)S(1)}, u32[]{:S(2)}, u32[]{:S(2)}) collective-permute-start(bf16[32,2048]{1,0:T(8,128)(2,1)S(1)} %slice.74), channel_id=1, source_target_pairs={{0,16},{8,72},{16,0},{24,88},{32,48},{40,104},{48,32},{56,120},{64... | collective-permute-start | bytes 393224 | tf_op jit(solution)/shard_map/ppermute | solution.py:460
  54.0 5.7 %collective-permute-start.19 = (bf16[32,2048]{1,0:T(8,128)(2,1)S(1)}, bf16[32,2048]{1,0:T(8,128)(2,1)S(1)}, u32[]{:S(2)}, u32[]{:S(2)}) collective-permute-start(bf16[32,2048]{1,0:T(8,128)(2,1)S(1)} %slice.75), channel_id=1, source_target_pairs={{0,48},{8,200},{16,32},{24,216},{32,16},{40,232},{48,0},{56,248},{... | collective-permute-start | bytes 393224 | tf_op jit(solution)/shard_map/ppermute | solution.py:460
  57.1 11.0 %collective-permute-start.16 = (bf16[32,2048]{1,0:T(8,128)(2,1)S(1)}, bf16[32,2048]{1,0:T(8,128)(2,1)S(1)}, u32[]{:S(2)}, u32[]{:S(2)}) collective-permute-start(bf16[32,2048]{1,0:T(8,128)(2,1)S(1)} %slice.73), channel_id=1, source_target_pairs={{0,48},{8,200},{16,32},{24,216},{32,16},{40,232},{48,0},{56,248},{... | collective-permute-start | bytes 393224 | tf_op jit(solution)/shard_map/ppermute | solution.py:460
  58.4 9.7 %collective-permute-start.14 = (bf16[32,2048]{1,0:T(8,128)(2,1)S(1)}, bf16[32,2048]{1,0:T(8,128)(2,1)S(1)}, u32[]{:S(2)}, u32[]{:S(2)}) collective-permute-start(bf16[32,2048]{1,0:T(8,128)(2,1)S(1)} %slice.72), channel_id=1, source_target_pairs={{0,16},{8,72},{16,0},{24,88},{32,48},{40,104},{48,32},{56,120},{64... | collective-permute-start | bytes 393224 | tf_op jit(solution)/shard_map/ppermute | solution.py:460
  60.6 9.8 %collective-permute-start.20 = (bf16[3,64,512]{2,1,0:T(8,128)(2,1)S(1)}, bf16[3,64,512]{2,1,0:T(8,128)(2,1)S(1)}, u32[]{:S(2)}, u32[]{:S(2)}) collective-permute-start(bf16[3,64,512]{2,1,0:T(8,128)(2,1)S(1)} %get-tuple-element.44), channel_id=1, source_target_pairs={{0,2},{1,3},{2,4},{3,5},{4,6},{5,7},{6,0},{7,1},{8,10},{9,11},{10,... | collective-permute-start | bytes 589832 | tf_op jit(solution)/shard_map/ppermute | solution.py:470
  63.7 9.4 %collective-permute-start.21 = (bf16[3,64,512]{2,1,0:T(8,128)(2,1)S(1)}, bf16[3,64,512]{2,1,0:T(8,128)(2,1)S(1)}, u32[]{:S(2)}, u32[]{:S(2)}) collective-permute-start(bf16[3,64,512]{2,1,0:T(8,128)(2,1)S(1)} %get-tuple-element.45), channel_id=1, source_target_pairs={{0,6},{1,7},{2,0},{3,1},{4,2},{5,3},{6,4},{7,5},{8,14},{9,15},{10,... | collective-permute-start | bytes 589832 | tf_op jit(solution)/shard_map/ppermute | solution.py:470
  73.2 14.3 %collective-permute-start.22 = (bf16[64,1024]{1,0:T(8,128)(2,1)S(1)}, bf16[64,1024]{1,0:T(8,128)(2,1)S(1)}, u32[]{:S(2)}, u32[]{:S(2)}) collective-permute-start(bf16[64,1024]{1,0:T(8,128)(2,1)S(1)} %get-tuple-element.47), channel_id=1, source_target_pairs={{0,1},{1,2},{2,3},{3,4},{4,5},{5,6},{6,7},{7,0},{8,9},{9,10},{10,1... | collective-permute-start | bytes 393224 | tf_op jit(solution)/shard_map/ppermute | solution.py:470
  73.3 14.2 %collective-permute-start.23 = (bf16[64,1024]{1,0:T(8,128)(2,1)S(1)}, bf16[64,1024]{1,0:T(8,128)(2,1)S(1)}, u32[]{:S(2)}, u32[]{:S(2)}) collective-permute-start(bf16[64,1024]{1,0:T(8,128)(2,1)S(1)} %get-tuple-element.48), channel_id=1, source_target_pairs={{0,7},{1,0},{2,1},{3,2},{4,3},{5,4},{6,5},{7,6},{8,15},{9,8},{10,9... | collective-permute-start | bytes 393224 | tf_op jit(solution)/shard_map/ppermute | solution.py:470
  75.9 11.5 %collective-permute-start.24 = (bf16[64,1024]{1,0:T(8,128)(2,1)S(1)}, bf16[64,1024]{1,0:T(8,128)(2,1)S(1)}, u32[]{:S(2)}, u32[]{:S(2)}) collective-permute-start(bf16[64,1024]{1,0:T(8,128)(2,1)S(1)} %get-tuple-element.49), channel_id=1, source_target_pairs={{0,2},{1,3},{2,4},{3,5},{4,6},{5,7},{6,0},{7,1},{8,10},{9,11},{10,... | collective-permute-start | bytes 393224 | tf_op jit(solution)/shard_map/ppermute | solution.py:470
  78.3 9.2 %collective-permute-start.25 = (bf16[64,1024]{1,0:T(8,128)(2,1)S(1)}, bf16[64,1024]{1,0:T(8,128)(2,1)S(1)}, u32[]{:S(2)}, u32[]{:S(2)}) collective-permute-start(bf16[64,1024]{1,0:T(8,128)(2,1)S(1)} %get-tuple-element.50), channel_id=1, source_target_pairs={{0,6},{1,7},{2,0},{3,1},{4,2},{5,3},{6,4},{7,5},{8,14},{9,15},{10,... | collective-permute-start | bytes 393224 | tf_op jit(solution)/shard_map/ppermute | solution.py:470
  79.5 13.6 %collective-permute-start.27 = (bf16[4,16,128]{2,1,0:T(8,128)(2,1)S(1)}, bf16[4,16,128]{2,1,0:T(8,128)(2,1)S(1)}, u32[]{:S(2)}, u32[]{:S(2)}) collective-permute-start(bf16[4,16,128]{2,1,0:T(8,128)(2,1)S(1)} %pad_maximum_fusion.1), channel_id=1, source_target_pairs={{0,8},{8,0},{16,24},{24,16},{32,40},{40,32},{48,56},{56,48},{64,72... | collective-permute-start | bytes 49160 | tf_op jit(solution)/shard_map/ppermute | solution.py:443
  87.6 6.5 %collective-permute-start.26 = (bf16[64,512]{1,0:T(8,128)(2,1)S(1)}, bf16[64,512]{1,0:T(8,128)(2,1)S(1)}, u32[]{:S(2)}, u32[]{:S(2)}) collective-permute-start(bf16[64,512]{1,0:T(8,128)(2,1)S(1)} %get-tuple-element.52), channel_id=1, source_target_pairs={{0,8},{8,0},{16,24},{24,16},{32,40},{40,32},{48,56},{56,48},{64,72... | collective-permute-start | bytes 196616 | tf_op jit(solution)/shard_map/ppermute | solution.py:443

commit v8 on v6

--- a/solution.py
+++ b/solution.py
@@ -334,18 +334,12 @@
             yield side, columns, d, jnp.concatenate([first[d, :, columns], chunk], axis=0)
 
 
-def far_body(a, b, w0, w1, first, keep, up, down, up4, down4):
-    for side, columns, d, whole in last_chunks(a, b, w0, w1, first):
+def far_body(a, b, w0, w1, first, keep, up, down, direct):
+    for _, columns, d, whole in last_chunks(a, b, w0, w1, first):
         if d == 0:
             keep[:, columns] = whole
-        elif d == 1:
-            up[:, columns] = whole.astype(BF16)
-        elif d == 3:
-            down[:, columns] = whole.astype(BF16)
-        elif side == 0:
-            up4[...] = whole.astype(BF16)
         else:
-            down4[...] = whole.astype(BF16)
+            (up, direct, down)[d - 1][:, columns] = whole.astype(BF16)
 
 
 def near_body(a, b, w0, w1, first, keep6, down, keep0, up):
@@ -372,16 +366,15 @@
     )(*args)
 
 
-def middle_body(keep2, keep6, below, above, below4, above4, up, down):
-    up[:, :512] = (keep2[:, :512] + below[:, :512].astype(F32) + below4[...].astype(F32)).astype(BF16)
-    up[:, 512:] = (keep2[:, 512:] + below[:, 512:].astype(F32)).astype(BF16)
-    down[:, :512] = (keep6[:, :512] + above[:, :512].astype(F32)).astype(BF16)
-    down[:, 512:] = (keep6[:, 512:] + above[:, 512:].astype(F32) + above4[...].astype(F32)).astype(BF16)
-
-
-def total_body(keep, below1, above1, below2, above2, own, other):
+def middle_body(keep2, keep6, below, above, up, down):
+    up[...] = (keep2[...] + below[...].astype(F32)).astype(BF16)
+    down[...] = (keep6[...] + above[...].astype(F32)).astype(BF16)
+
+
+def total_body(keep, below1, above1, below2, above2, opposite, own, other):
     near = keep[...] + below1[...].astype(F32) + above1[...].astype(F32)
-    whole = (near + below2[...].astype(F32) + above2[...].astype(F32)).astype(BF16)
+    whole = near + below2[...].astype(F32) + above2[...].astype(F32)
+    whole = (whole + opposite[...].astype(F32)).astype(BF16)
     own[...] = whole[:, :512]
     other[...] = whole[:, 512:]
 
@@ -494,18 +487,18 @@
     parts = [attended] + [turned(attended, k, 0) for k in (1, 2, 3)]
     far, near = [gathered([a[i : i + 16] for a in parts]) for i in (0, 16)]
     first_far, first_near = project(far[:3], weights), project(near[:3], weights)
-    keep2, up3, down3, up4, down4 = plain(
-        far_body, [SUM, SENT, SENT, HALF, HALF], *far[3], *weights, first_far
+    keep2, up3, down3, up4 = plain(
+        far_body, [SUM, SENT, SENT, SENT], *far[3], *weights, first_far
     )
-    below4, above4 = along_z(up4, 2), along_z(down4, -2)
     below3, above3 = along_z(up3, 1), along_z(down3, -1)
+    opposite = along_z(up4, 4)
     keep6, down1, keep0, up1 = plain(
         near_body, [SUM, SENT, SUM, SENT], *near[3], *weights, first_near
     )
     below1, above1 = along_z(up1, 1), along_z(down1, -1)
-    up2, down2 = plain(middle_body, [SENT, SENT], keep2, keep6, below3, above3, below4, above4)
+    up2, down2 = plain(middle_body, [SENT, SENT], keep2, keep6, below3, above3)
     below2, above2 = along_z(up2, 2), along_z(down2, -2)
-    own, other = plain(total_body, [HALF, HALF], keep0, below1, above1, below2, above2)
+    own, other = plain(total_body, [HALF, HALF], keep0, below1, above1, below2, above2, opposite)
     return finish(own, other_core(other), pick)
 
 

time: 90.2 us -> 89.9 us (level)
    ppermute x8 -> x7, starting transfers between devices: 15.7 us -> 16.2 us  [along_z(): lax.ppermute(value, 'head', [(i, (i + k) % HEADS) for i in range(HEADS)])]
  transfers between devices with their start and end apart: 30 -> 29, of which waited for: 13 -> 12; matrix products, arithmetic and copies ran while one was open for 1% -> 1% of each run, Pallas kernels for 16% -> 17%
where the time goes in v8:
time: 89.9 us; the launch traced here: 89.8 us
  starting transfers between devices  51.9 us (58%)
  Pallas kernels  19.9 us (22%)
  waiting for transfers between devices  16.1 us (18%)
  local copies, waits for them, and re-layouts  1.61 us (2%)
    ppermute x11, starting transfers between devices, along(): lax.ppermute(value, 'batch', [(i, i ^ k << shift) for i in range(BATCH)])  25 us
    ppermute x7, starting transfers between devices, along_z(): lax.ppermute(value, 'head', [(i, (i + k) % HEADS) for i in range(HEADS)])  16.2 us
    ppermute x11, starting transfers between devices, turned(): return lax.ppermute(value, 'batch', pairs)  10.7 us
    ppermute x11, waiting for transfers between devices, turned(): return lax.ppermute(value, 'batch', pairs)  9.51 us
    ppermute x11, waiting for transfers between devices, along(): lax.ppermute(value, 'batch', [(i, i ^ k << shift) for i in range(BATCH)])  6.54 us
    pallas_call x2, Pallas kernels, prefix_keep(): pl.pallas_call(prefix_keep_body, out_shape=[out, out], in_specs=[VMEM] *...  4.36 us
    pallas_call x1, Pallas kernels, local_parts(): pl.pallas_call(local_body, out_shape=[out] * 4, in_specs=[SMEM] + [HBM] *...  4.23 us
    pallas_call x1, Pallas kernels, prefix_send(): pl.pallas_call(prefix_send_body, out_shape=jax.ShapeDtypeStruct((33, GROU...  4.1 us
  transfers between devices with their start and end apart: 29, of which 12 were waited for; matrix products, arithmetic and copies ran while one was open for 1% of the time, Pallas kernels for 17%

profile of v8, /device:TPU:1, one launch (start us, length us, event | category | flops | bytes accessed | tf_op | source)
XLA Modules:
  0.0 89.8 jit_solution(7092704837740400394)
XLA Ops:
  0.0 3.2 %collective-permute-start.3 = (bf16[2,2048,128]{2,1,0:T(8,128)(2,1)}, bf16[2,2048,128]{2,1,0:T(8,128)(2,1)S(1)}, u32[]{:S(2)}, u32[]{:S(2)}) collective-permute-start(bf16[2,2048,128]{2,1,0:T(8,128)(2,1)} %kv0.5), channel_id=1, source_target_pairs={{0,8},{8,0},{16,24},{24,16},{32,40},{40,32},{48,56},{56,48},{64,72... | collective-permute-start | bytes 3145736 | tf_op jit(solution)/shard_map/ppermute | solution.py:433
  3.2 0.6 stack.34.place
  3.8 4.2 %local_parts.1 = (bf16[18,16,128]{2,1,0:T(8,128)(2,1)}, bf16[18,16,128]{2,1,0:T(8,128)(2,1)}, bf16[18,16,128]{2,1,0:T(8,128)(2,1)}, bf16[18,16,128]{2,1,0:T(8,128)(2,1)}) custom-call(s32[7]{0:T(128)} %stack.34.place, bf16[32,2048]{1,0:T(8,128)(2,1)} %q_in.1, s32[32]{0:T(128)} %prompt_in.1, s32[8,32]{1,0:T(8,128)} %bitcast.8, s32[32]{0:T(128)} %length_in.1, ...), custom_call_target="tpu_custom_call" | custom-call | tf_op jit(solution)/shard_map/local_parts/pallas_call | solution.py:124
  8.1 0.1 collective-permute-start
  8.2 1.9 %collective-permute-start.1 = (bf16[18,16,128]{2,1,0:T(8,128)(2,1)}, bf16[18,16,128]{2,1,0:T(8,128)(2,1)S(1)}, u32[]{:S(2)}, u32[]{:S(2)}) collective-permute-start(bf16[18,16,128]{2,1,0:T(8,128)(2,1)} %get-tuple-element.30), channel_id=1, source_target_pairs={{0,128},{8,136},{16,144},{24,152},{32,160},{40,168},{48,176},{56,1... | collective-permute-start | bytes 221192 | tf_op jit(solution)/shard_map/ppermute | solution.py:433
  10.1 1.9 %collective-permute-start.2 = (bf16[18,16,128]{2,1,0:T(8,128)(2,1)}, bf16[18,16,128]{2,1,0:T(8,128)(2,1)S(1)}, u32[]{:S(2)}, u32[]{:S(2)}) collective-permute-start(bf16[18,16,128]{2,1,0:T(8,128)(2,1)} %get-tuple-element.31), channel_id=1, source_target_pairs={{0,192},{8,200},{16,208},{24,216},{32,224},{40,232},{48,240},{56,2... | collective-permute-start | bytes 221192 | tf_op jit(solution)/shard_map/ppermute | solution.py:433
  12.0 0.2 collective-permute-done.a1.s1
  12.3 2.0 %collective-permute-done.1.a2.s2 = bf16[18,16,128]{2,1,0:T(8,128)(2,1)S(1)} collective-permute-done((bf16[18,16,128]{2,1,0:T(8,128)(2,1)}, bf16[18,16,128]{2,1,0:T(8,128)(2,1)S(1)}, u32[]{:S(2)}, u32[]{:S(2)}) %collective-permute-start.1) | collective-permute-done | bytes 73760 | tf_op jit(solution)/shard_map/ppermute | solution.py:433
  14.3 1.4 %collective-permute-done.2.a3.s3 = bf16[18,16,128]{2,1,0:T(8,128)(2,1)S(1)} collective-permute-done((bf16[18,16,128]{2,1,0:T(8,128)(2,1)}, bf16[18,16,128]{2,1,0:T(8,128)(2,1)S(1)}, u32[]{:S(2)}, u32[]{:S(2)}) %collective-permute-start.2) | collective-permute-done | bytes 73760 | tf_op jit(solution)/shard_map/ppermute | solution.py:433
  15.8 0.9 copy-done.2
  16.6 0.6 regroup.1
  17.2 3.0 %collective-permute-start.4 = (bf16[37,16,128]{2,1,0:T(8,128)(2,1)S(1)}, bf16[37,16,128]{2,1,0:T(8,128)(2,1)S(1)}, u32[]{:S(2)}, u32[]{:S(2)}) collective-permute-start(bf16[37,16,128]{2,1,0:T(8,128)(2,1)S(1)} %get-tuple-element.35), channel_id=1, source_target_pairs={{0,32},{8,40},{16,48},{24,56},{32,0},{40,8},{48,16},{56,24},{64,96... | collective-permute-start | bytes 454664 | tf_op jit(solution)/shard_map/ppermute | solution.py:433
  20.2 0.4 collective-permute-start.5
  20.6 0.4 collective-permute-start.6
  21.0 2.2 %prefix_keep.2 = (f32[16,16,128]{2,1,0:T(8,128)S(1)}, f32[16,16,128]{2,1,0:T(8,128)S(1)}) custom-call(bf16[17,16,128]{2,1,0:T(8,128)(2,1)S(1)} %get-tuple-element.32.q, bf16[2,2048,128]{2,1,0:T(8,128)(2,1)S(1)} %copy-done.1, bf16[2,2048,128]{2,1,0:T(8,128)(2,1)S(1)} %collective-permute-done.3.kv1), custom_call_target="tpu_custom_call" | custom-call | flops 536870912 | bytes 2500000 | tf_op jit(solution)/shard_map/prefix_keep/pallas_call | solution.py:238
  23.2 0.0 copy-start
  23.2 1.9 %collective-permute-done.5.qa = bf16[17,16,128]{2,1,0:T(8,128)(2,1)S(1)} collective-permute-done((bf16[17,16,128]{2,1,0:T(8,128)(2,1)S(1)}, bf16[17,16,128]{2,1,0:T(8,128)(2,1)S(1)}, u32[]{:S(2)}, u32[]{:S(2)}) %collective-permute-start.5) | collective-permute-done | bytes 69664 | tf_op jit(solution)/shard_map/ppermute | solution.py:433
  25.1 0.6 collective-permute-done.6.qb
  25.8 4.1 %prefix_send.1 = bf16[33,16,128]{2,1,0:T(8,128)(2,1)S(1)} custom-call(bf16[17,16,128]{2,1,0:T(8,128)(2,1)S(1)} %collective-permute-done.5.qa, bf16[17,16,128]{2,1,0:T(8,128)(2,1)S(1)} %collective-permute-done.6.qb, bf16[2,2048,128]{2,1,0:T(8,128)(2,1)S(1)} %copy-done.1, bf16[2,2048,128]{2,1,0:T(8,128)(2,1)S(1)} %collective-permute-done.3.kv1, ...), custom_call_target="tpu_custom_call" | custom-call | flops 1073741824 | bytes 2500000 | tf_op jit(solution)/shard_map/prefix_send/pallas_call | solution.py:225
  29.9 0.5 collective-permute-start.7
  30.4 2.1 %collective-permute-start.15 = (bf16[2048,512]{1,0:T(8,128)(2,1)S(1)}, bf16[2048,512]{1,0:T(8,128)(2,1)S(1)}, u32[]{:S(2)}, u32[]{:S(2)}) collective-permute-start(bf16[2048,512]{1,0:T(8,128)(2,1)S(1)} %copy-done), channel_id=1, source_target_pairs={{0,8},{8,0},{16,24},{24,16},{32,40},{40,32},{48,56},{56,48},{64,72... | collective-permute-start | bytes 6291464 | tf_op jit(solution)/shard_map/ppermute | solution.py:433
  32.6 2.2 %prefix_keep.3 = (f32[16,16,128]{2,1,0:T(8,128)S(1)}, f32[16,16,128]{2,1,0:T(8,128)S(1)}) custom-call(bf16[37,16,128]{2,1,0:T(8,128)(2,1)S(1)} %collective-permute-done.4.q.later.far, bf16[2,2048,128]{2,1,0:T(8,128)(2,1)S(1)} %copy-done.1, bf16[2,2048,128]{2,1,0:T(8,128)(2,1)S(1)} %collective-permute-done.3.kv1), custom_call_target="tpu_custom_call" | custom-call | flops 536870912 | bytes 2500000 | tf_op jit(solution)/shard_map/prefix_keep/pallas_call | solution.py:238
  34.7 0.0 collective-permute-done.7.message
  34.8 1.2 %combine.1 = bf16[32,2048]{1,0:T(8,128)(2,1)S(1)} custom-call(s32[7]{0:T(128)S(1)} %copy-done.4, f32[16,16,128]{2,1,0:T(8,128)S(1)} %get-tuple-element.33.own, f32[16,16,128]{2,1,0:T(8,128)S(1)} %get-tuple-element.34.after.own_masses, f32[16,16,128]{2,1,0:T(8,128)S(1)} %get-tuple-element.36.cross, f32[16,16,128]{2,1,0:T(8,128)S(1)} %get-tuple-element.37.cross_masses, ...), custom_call_target="tpu_custom_call" | custom-call | tf_op jit(solution)/shard_map/combine/pallas_call | solution.py:281
  36.0 1.1 %collective-permute-start.8 = (bf16[32,2048]{1,0:T(8,128)(2,1)S(1)}, bf16[32,2048]{1,0:T(8,128)(2,1)S(1)}, u32[]{:S(2)}, u32[]{:S(2)}) collective-permute-start(bf16[32,2048]{1,0:T(8,128)(2,1)S(1)} %combine.1), channel_id=1, source_target_pairs={{0,64},{8,24},{16,80},{24,8},{32,96},{40,56},{48,112},{56,40},{64,... | collective-permute-start | bytes 393224 | tf_op jit(solution)/shard_map/ppermute | solution.py:450
  37.1 2.8 %collective-permute-start.9 = (bf16[32,2048]{1,0:T(8,128)(2,1)S(1)}, bf16[32,2048]{1,0:T(8,128)(2,1)S(1)}, u32[]{:S(2)}, u32[]{:S(2)}) collective-permute-start(bf16[32,2048]{1,0:T(8,128)(2,1)S(1)} %combine.1), channel_id=1, source_target_pairs={{0,128},{8,40},{16,144},{24,56},{32,160},{40,8},{48,176},{56,24},{... | collective-permute-start | bytes 393224 | tf_op jit(solution)/shard_map/ppermute | solution.py:450
  39.8 0.1 collective-permute-start.10
  39.9 0.0 collective-permute-done.8
  40.0 3.9 %collective-permute-done.9 = bf16[32,2048]{1,0:T(8,128)(2,1)S(1)} collective-permute-done((bf16[32,2048]{1,0:T(8,128)(2,1)S(1)}, bf16[32,2048]{1,0:T(8,128)(2,1)S(1)}, u32[]{:S(2)}, u32[]{:S(2)}) %collective-permute-start.9) | collective-permute-done | bytes 131104 | tf_op jit(solution)/shard_map/ppermute | solution.py:450
  43.9 1.1 %collective-permute-done.10 = bf16[32,2048]{1,0:T(8,128)(2,1)S(1)} collective-permute-done((bf16[32,2048]{1,0:T(8,128)(2,1)S(1)}, bf16[32,2048]{1,0:T(8,128)(2,1)S(1)}, u32[]{:S(2)}, u32[]{:S(2)}) %collective-permute-start.10) | collective-permute-done | bytes 131104 | tf_op jit(solution)/shard_map/ppermute | solution.py:450
  45.1 1.5 %collective-permute-start.18 = (bf16[64,2048]{1,0:T(8,128)(2,1)S(1)}, bf16[64,2048]{1,0:T(8,128)(2,1)S(1)}, u32[]{:S(2)}, u32[]{:S(2)}) collective-permute-start(bf16[64,2048]{1,0:T(8,128)(2,1)S(1)} %pad_maximum_fusion.1.a), channel_id=1, source_target_pairs={{0,48},{8,200},{16,32},{24,216},{32,16},{40,232},{48,0},{56,248},{... | collective-permute-start | bytes 786440 | tf_op jit(solution)/shard_map/ppermute | solution.py:450
  46.6 1.3 %collective-permute-start.11 = (bf16[64,2048]{1,0:T(8,128)(2,1)S(1)}, bf16[64,2048]{1,0:T(8,128)(2,1)S(1)}, u32[]{:S(2)}, u32[]{:S(2)}) collective-permute-start(bf16[64,2048]{1,0:T(8,128)(2,1)S(1)} %pad_maximum_fusion.a), channel_id=1, source_target_pairs={{0,48},{8,200},{16,32},{24,216},{32,16},{40,232},{48,0},{56,248},{... | collective-permute-start | bytes 786440 | tf_op jit(solution)/shard_map/ppermute | solution.py:450
  48.0 0.9 collective-permute-start.13
  48.8 3.1 %collective-permute-done.18.c = bf16[64,2048]{1,0:T(8,128)(2,1)S(1)} collective-permute-done((bf16[64,2048]{1,0:T(8,128)(2,1)S(1)}, bf16[64,2048]{1,0:T(8,128)(2,1)S(1)}, u32[]{:S(2)}, u32[]{:S(2)}) %collective-permute-start.18) | collective-permute-done | bytes 262176 | tf_op jit(solution)/shard_map/ppermute | solution.py:450
  51.9 0.1 collective-permute-start.19
  52.0 0.1 collective-permute-done.20.b
  52.1 1.4 %collective-permute-start.21 = (bf16[32,2048]{1,0:T(8,128)(2,1)S(1)}, bf16[32,2048]{1,0:T(8,128)(2,1)S(1)}, u32[]{:S(2)}, u32[]{:S(2)}) collective-permute-start(bf16[32,2048]{1,0:T(8,128)(2,1)S(1)} %slice.75), channel_id=1, source_target_pairs={{0,48},{8,200},{16,32},{24,216},{32,16},{40,232},{48,0},{56,248},{... | collective-permute-start | bytes 393224 | tf_op jit(solution)/shard_map/ppermute | solution.py:450
  53.6 1.1 %collective-permute-done.11.c = bf16[64,2048]{1,0:T(8,128)(2,1)S(1)} collective-permute-done((bf16[64,2048]{1,0:T(8,128)(2,1)S(1)}, bf16[64,2048]{1,0:T(8,128)(2,1)S(1)}, u32[]{:S(2)}, u32[]{:S(2)}) %collective-permute-start.11) | collective-permute-done | bytes 262176 | tf_op jit(solution)/shard_map/ppermute | solution.py:450
  54.7 0.1 collective-permute-start.12
  54.8 0.1 collective-permute-done.13.b
  54.9 1.4 %collective-permute-start.14 = (bf16[32,2048]{1,0:T(8,128)(2,1)S(1)}, bf16[32,2048]{1,0:T(8,128)(2,1)S(1)}, u32[]{:S(2)}, u32[]{:S(2)}) collective-permute-start(bf16[32,2048]{1,0:T(8,128)(2,1)S(1)} %slice.69), channel_id=1, source_target_pairs={{0,48},{8,200},{16,32},{24,216},{32,16},{40,232},{48,0},{56,248},{... | collective-permute-start | bytes 393224 | tf_op jit(solution)/shard_map/ppermute | solution.py:450
  56.4 1.0 %project.3.first = f32[4,48,1024]{2,1,0:T(8,128)S(1)} custom-call(bf16[64,2048]{1,0:T(8,128)(2,1)S(1)} %pad_maximum_fusion.1.a, bf16[64,2048]{1,0:T(8,128)(2,1)S(1)} %collective-permute-done.20.b, bf16[64,2048]{1,0:T(8,128)(2,1)S(1)} %collective-permute-done.18.c, bf16[2048,512]{1,0:T(8,128)(2,1)S(1)} %copy-done, ...), custom_call_target="tpu_custom_call" | custom-call | flops 805306368 | bytes 4500000 | tf_op jit(solution)/shard_map/project/pallas_call | solution.py:316
  57.4 0.0 collective-permute-done.19.a
  57.4 0.0 collective-permute-done.21.b
  57.4 0.9 far.1
  58.3 1.9 %collective-permute-start.22 = (bf16[64,1024]{1,0:T(8,128)(2,1)S(1)}, bf16[64,1024]{1,0:T(8,128)(2,1)S(1)}, u32[]{:S(2)}, u32[]{:S(2)}) collective-permute-start(bf16[64,1024]{1,0:T(8,128)(2,1)S(1)} %get-tuple-element.44), channel_id=1, source_target_pairs={{0,1},{1,2},{2,3},{3,4},{4,5},{5,6},{6,7},{7,0},{8,9},{9,10},{10,1... | collective-permute-start | bytes 393224 | tf_op jit(solution)/shard_map/ppermute | solution.py:460
  60.1 4.0 %collective-permute-start.23 = (bf16[64,1024]{1,0:T(8,128)(2,1)S(1)}, bf16[64,1024]{1,0:T(8,128)(2,1)S(1)}, u32[]{:S(2)}, u32[]{:S(2)}) collective-permute-start(bf16[64,1024]{1,0:T(8,128)(2,1)S(1)} %get-tuple-element.45), channel_id=1, source_target_pairs={{0,7},{1,0},{2,1},{3,2},{4,3},{5,4},{6,5},{7,6},{8,15},{9,8},{10,9... | collective-permute-start | bytes 393224 | tf_op jit(solution)/shard_map/ppermute | solution.py:460
  64.2 3.9 %collective-permute-start.26 = (bf16[64,1024]{1,0:T(8,128)(2,1)S(1)}, bf16[64,1024]{1,0:T(8,128)(2,1)S(1)}, u32[]{:S(2)}, u32[]{:S(2)}) collective-permute-start(bf16[64,1024]{1,0:T(8,128)(2,1)S(1)} %get-tuple-element.48), channel_id=1, source_target_pairs={{0,4},{1,5},{2,6},{3,7},{4,0},{5,1},{6,2},{7,3},{8,12},{9,13},{10,... | collective-permute-start | bytes 393224 | tf_op jit(solution)/shard_map/ppermute | solution.py:460
  68.1 1.0 %project.2.first = f32[4,48,1024]{2,1,0:T(8,128)S(1)} custom-call(bf16[64,2048]{1,0:T(8,128)(2,1)S(1)} %pad_maximum_fusion.a, bf16[64,2048]{1,0:T(8,128)(2,1)S(1)} %collective-permute-done.13.b, bf16[64,2048]{1,0:T(8,128)(2,1)S(1)} %collective-permute-done.11.c, bf16[2048,512]{1,0:T(8,128)(2,1)S(1)} %copy-done, bf16[2048,512]{1,0:T(8,128)(2,1)S(1)} %collective-permute-done.15.w1), custom_call_target="tpu_custom_call" | custom-call | flops 805306368 | bytes 4500000 | tf_op jit(solution)/shard_map/project/pallas_call | solution.py:316
  69.1 0.0 collective-permute-done.12.a
  69.1 0.0 collective-permute-done.14.b
  69.1 0.9 near.1
  70.0 0.1 collective-permute-start.16
  70.0 2.7 %collective-permute-start.17 = (bf16[64,1024]{1,0:T(8,128)(2,1)S(1)}, bf16[64,1024]{1,0:T(8,128)(2,1)S(1)}, u32[]{:S(2)}, u32[]{:S(2)}) collective-permute-start(bf16[64,1024]{1,0:T(8,128)(2,1)S(1)} %get-tuple-element.41), channel_id=1, source_target_pairs={{0,7},{1,0},{2,1},{3,2},{4,3},{5,4},{6,5},{7,6},{8,15},{9,8},{10,9... | collective-permute-start | bytes 393224 | tf_op jit(solution)/shard_map/ppermute | solution.py:460
  72.7 0.0 collective-permute-done.22.below
  72.7 0.1 middle.1
  72.8 0.1 collective-permute-start.24
  72.9 3.6 %collective-permute-start.25 = (bf16[64,1024]{1,0:T(8,128)(2,1)S(1)}, bf16[64,1024]{1,0:T(8,128)(2,1)S(1)}, u32[]{:S(2)}, u32[]{:S(2)}) collective-permute-start(bf16[64,1024]{1,0:T(8,128)(2,1)S(1)} %get-tuple-element.47), channel_id=1, source_target_pairs={{0,6},{1,7},{2,0},{3,1},{4,2},{5,3},{6,4},{7,5},{8,14},{9,15},{10,... | collective-permute-start | bytes 393224 | tf_op jit(solution)/shard_map/ppermute | solution.py:460
  76.5 7.1 %collective-permute-start.28 = (bf16[4,16,128]{2,1,0:T(8,128)(2,1)S(1)}, bf16[4,16,128]{2,1,0:T(8,128)(2,1)S(1)}, u32[]{:S(2)}, u32[]{:S(2)}) collective-permute-start(bf16[4,16,128]{2,1,0:T(8,128)(2,1)S(1)} %pad_maximum_fusion.2), channel_id=1, source_target_pairs={{0,8},{8,0},{16,24},{24,16},{32,40},{40,32},{48,56},{56,48},{64,72... | collective-permute-start | bytes 49160 | tf_op jit(solution)/shard_map/ppermute | solution.py:433
  83.6 0.1 total.1
  83.7 4.3 %collective-permute-start.27 = (bf16[64,512]{1,0:T(8,128)(2,1)S(1)}, bf16[64,512]{1,0:T(8,128)(2,1)S(1)}, u32[]{:S(2)}, u32[]{:S(2)}) collective-permute-start(bf16[64,512]{1,0:T(8,128)(2,1)S(1)} %get-tuple-element.50), channel_id=1, source_target_pairs={{0,8},{8,0},{16,24},{24,16},{32,40},{40,32},{48,56},{56,48},{64,72... | collective-permute-start | bytes 196616 | tf_op jit(solution)/shard_map/ppermute | solution.py:433
  88.0 0.6 order_rows.1.pick
  88.6 0.2 collective-permute-done.27.other
  88.9 0.9 %finish.1 = bf16[128,512]{1,0:T(8,128)(2,1)} custom-call(bf16[64,512]{1,0:T(8,128)(2,1)S(1)} %get-tuple-element.49.own, bf16[64,512]{1,0:T(8,128)(2,1)S(1)} %collective-permute-done.27.other, bf16[128,128]{1,0:T(8,128)(2,1)S(1)} %order_rows.1.pick), custom_call_target="tpu_custom_call" | custom-call | tf_op jit(solution)/shard_map/finish/pallas_call | solution.py:422
  (35 shorter events, 0.2 us)
Async XLA Ops:
  0.0 21.0 %copy-start.1 = (bf16[2,2048,128]{2,1,0:T(8,128)(2,1)S(1)}, bf16[2,2048,128]{2,1,0:T(8,128)(2,1)}, u32[]{:S(2)}) copy-start(bf16[2,2048,128]{2,1,0:T(8,128)(2,1)} %kv0.5) | copy-start | bytes 3145732
  0.0 21.0 %collective-permute-start.3 = (bf16[2,2048,128]{2,1,0:T(8,128)(2,1)}, bf16[2,2048,128]{2,1,0:T(8,128)(2,1)S(1)}, u32[]{:S(2)}, u32[]{:S(2)}) collective-permute-start(bf16[2,2048,128]{2,1,0:T(8,128)(2,1)} %kv0.5), channel_id=1, source_target_pairs={{0,8},{8,0},{16,24},{24,16},{32,40},{40,32},{48,56},{56,48},{64,72... | collective-permute-start | bytes 3145736 | tf_op jit(solution)/shard_map/ppermute | solution.py:433
  3.8 11.9 %copy-start.4 = (s32[7]{0:T(128)S(1)}, s32[7]{0:T(128)}, u32[]{:S(2)}) copy-start(s32[7]{0:T(128)} %stack.34.place) | copy-start | bytes 88
  8.1 4.2 %collective-permute-start = (bf16[18,16,128]{2,1,0:T(8,128)(2,1)}, bf16[18,16,128]{2,1,0:T(8,128)(2,1)S(1)}, u32[]{:S(2)}, u32[]{:S(2)}) collective-permute-start(bf16[18,16,128]{2,1,0:T(8,128)(2,1)} %get-tuple-element.29), channel_id=1, source_target_pairs={{0,64},{8,72},{16,80},{24,88},{32,96},{40,104},{48,112},{56,120},{... | collective-permute-start | bytes 221192 | tf_op jit(solution)/shard_map/ppermute | solution.py:433
  8.2 6.1 %collective-permute-start.1 = (bf16[18,16,128]{2,1,0:T(8,128)(2,1)}, bf16[18,16,128]{2,1,0:T(8,128)(2,1)S(1)}, u32[]{:S(2)}, u32[]{:S(2)}) collective-permute-start(bf16[18,16,128]{2,1,0:T(8,128)(2,1)} %get-tuple-element.30), channel_id=1, source_target_pairs={{0,128},{8,136},{16,144},{24,152},{32,160},{40,168},{48,176},{56,1... | collective-permute-start | bytes 221192 | tf_op jit(solution)/shard_map/ppermute | solution.py:433
  10.1 5.6 %collective-permute-start.2 = (bf16[18,16,128]{2,1,0:T(8,128)(2,1)}, bf16[18,16,128]{2,1,0:T(8,128)(2,1)S(1)}, u32[]{:S(2)}, u32[]{:S(2)}) collective-permute-start(bf16[18,16,128]{2,1,0:T(8,128)(2,1)} %get-tuple-element.31), channel_id=1, source_target_pairs={{0,192},{8,200},{16,208},{24,216},{32,224},{40,232},{48,240},{56,2... | collective-permute-start | bytes 221192 | tf_op jit(solution)/shard_map/ppermute | solution.py:433
  15.8 0.9 copy-start.2
  17.2 8.6 %collective-permute-start.4 = (bf16[37,16,128]{2,1,0:T(8,128)(2,1)S(1)}, bf16[37,16,128]{2,1,0:T(8,128)(2,1)S(1)}, u32[]{:S(2)}, u32[]{:S(2)}) collective-permute-start(bf16[37,16,128]{2,1,0:T(8,128)(2,1)S(1)} %get-tuple-element.35), channel_id=1, source_target_pairs={{0,32},{8,40},{16,48},{24,56},{32,0},{40,8},{48,16},{56,24},{64,96... | collective-permute-start | bytes 454664 | tf_op jit(solution)/shard_map/ppermute | solution.py:433
  20.2 4.9 %collective-permute-start.5 = (bf16[17,16,128]{2,1,0:T(8,128)(2,1)S(1)}, bf16[17,16,128]{2,1,0:T(8,128)(2,1)S(1)}, u32[]{:S(2)}, u32[]{:S(2)}) collective-permute-start(bf16[17,16,128]{2,1,0:T(8,128)(2,1)S(1)} %get-tuple-element.32.q), channel_id=1, source_target_pairs={{0,16},{8,24},{16,0},{24,8},{32,48},{40,56},{48,32},{56,40},{64,80... | collective-permute-start | bytes 208904 | tf_op jit(solution)/shard_map/ppermute | solution.py:433
  20.6 5.2 %collective-permute-start.6 = (bf16[17,16,128]{2,1,0:T(8,128)(2,1)S(1)}, bf16[17,16,128]{2,1,0:T(8,128)(2,1)S(1)}, u32[]{:S(2)}, u32[]{:S(2)}) collective-permute-start(bf16[17,16,128]{2,1,0:T(8,128)(2,1)S(1)} %get-tuple-element.38), channel_id=1, source_target_pairs={{0,48},{8,56},{16,32},{24,40},{32,16},{40,24},{48,0},{56,8},{64,11... | collective-permute-start | bytes 208904 | tf_op jit(solution)/shard_map/ppermute | solution.py:433
  23.2 7.2 %copy-start = (bf16[2048,512]{1,0:T(8,128)(2,1)S(1)}, bf16[2048,512]{1,0:T(8,128)(2,1)}, u32[]{:S(2)}) copy-start(bf16[2048,512]{1,0:T(8,128)(2,1)} %w0.7) | copy-start | bytes 6291460
  29.9 4.9 %copy-start.3 = (bf16[18,16,128]{2,1,0:T(8,128)(2,1)S(1)}, bf16[18,16,128]{2,1,0:T(8,128)(2,1)}, u32[]{:S(2)}) copy-start(bf16[18,16,128]{2,1,0:T(8,128)(2,1)} %get-tuple-element.28.a0.s0) | copy-start | bytes 221188
  29.9 4.9 %collective-permute-start.7 = (bf16[33,16,128]{2,1,0:T(8,128)(2,1)S(1)}, bf16[33,16,128]{2,1,0:T(8,128)(2,1)S(1)}, u32[]{:S(2)}, u32[]{:S(2)}) collective-permute-start(bf16[33,16,128]{2,1,0:T(8,128)(2,1)S(1)} %prefix_send.1), channel_id=1, source_target_pairs={{0,16},{8,24},{16,0},{24,8},{32,48},{40,56},{48,32},{56,40},{64,80... | collective-permute-start | bytes 405512 | tf_op jit(solution)/shard_map/ppermute | solution.py:433
  30.4 25.9 %collective-permute-start.15 = (bf16[2048,512]{1,0:T(8,128)(2,1)S(1)}, bf16[2048,512]{1,0:T(8,128)(2,1)S(1)}, u32[]{:S(2)}, u32[]{:S(2)}) collective-permute-start(bf16[2048,512]{1,0:T(8,128)(2,1)S(1)} %copy-done), channel_id=1, source_target_pairs={{0,8},{8,0},{16,24},{24,16},{32,40},{40,32},{48,56},{56,48},{64,72... | collective-permute-start | bytes 6291464 | tf_op jit(solution)/shard_map/ppermute | solution.py:433
  36.0 4.0 %collective-permute-start.8 = (bf16[32,2048]{1,0:T(8,128)(2,1)S(1)}, bf16[32,2048]{1,0:T(8,128)(2,1)S(1)}, u32[]{:S(2)}, u32[]{:S(2)}) collective-permute-start(bf16[32,2048]{1,0:T(8,128)(2,1)S(1)} %combine.1), channel_id=1, source_target_pairs={{0,64},{8,24},{16,80},{24,8},{32,96},{40,56},{48,112},{56,40},{64,... | collective-permute-start | bytes 393224 | tf_op jit(solution)/shard_map/ppermute | solution.py:450
  37.1 6.8 %collective-permute-start.9 = (bf16[32,2048]{1,0:T(8,128)(2,1)S(1)}, bf16[32,2048]{1,0:T(8,128)(2,1)S(1)}, u32[]{:S(2)}, u32[]{:S(2)}) collective-permute-start(bf16[32,2048]{1,0:T(8,128)(2,1)S(1)} %combine.1), channel_id=1, source_target_pairs={{0,128},{8,40},{16,144},{24,56},{32,160},{40,8},{48,176},{56,24},{... | collective-permute-start | bytes 393224 | tf_op jit(solution)/shard_map/ppermute | solution.py:450
  39.8 5.2 %collective-permute-start.10 = (bf16[32,2048]{1,0:T(8,128)(2,1)S(1)}, bf16[32,2048]{1,0:T(8,128)(2,1)S(1)}, u32[]{:S(2)}, u32[]{:S(2)}) collective-permute-start(bf16[32,2048]{1,0:T(8,128)(2,1)S(1)} %combine.1), channel_id=1, source_target_pairs={{0,192},{8,56},{16,208},{24,40},{32,224},{40,24},{48,240},{56,8},{... | collective-permute-start | bytes 393224 | tf_op jit(solution)/shard_map/ppermute | solution.py:450
  45.1 6.8 %collective-permute-start.18 = (bf16[64,2048]{1,0:T(8,128)(2,1)S(1)}, bf16[64,2048]{1,0:T(8,128)(2,1)S(1)}, u32[]{:S(2)}, u32[]{:S(2)}) collective-permute-start(bf16[64,2048]{1,0:T(8,128)(2,1)S(1)} %pad_maximum_fusion.1.a), channel_id=1, source_target_pairs={{0,48},{8,200},{16,32},{24,216},{32,16},{40,232},{48,0},{56,248},{... | collective-permute-start | bytes 786440 | tf_op jit(solution)/shard_map/ppermute | solution.py:450
  46.6 5.5 %collective-permute-start.20 = (bf16[64,2048]{1,0:T(8,128)(2,1)S(1)}, bf16[64,2048]{1,0:T(8,128)(2,1)S(1)}, u32[]{:S(2)}, u32[]{:S(2)}) collective-permute-start(bf16[64,2048]{1,0:T(8,128)(2,1)S(1)} %pad_maximum_fusion.1.a), channel_id=1, source_target_pairs={{0,16},{8,72},{16,0},{24,88},{32,48},{40,104},{48,32},{56,120},{64... | collective-permute-start | bytes 786440 | tf_op jit(solution)/shard_map/ppermute | solution.py:450
  46.6 8.1 %collective-permute-start.11 = (bf16[64,2048]{1,0:T(8,128)(2,1)S(1)}, bf16[64,2048]{1,0:T(8,128)(2,1)S(1)}, u32[]{:S(2)}, u32[]{:S(2)}) collective-permute-start(bf16[64,2048]{1,0:T(8,128)(2,1)S(1)} %pad_maximum_fusion.a), channel_id=1, source_target_pairs={{0,48},{8,200},{16,32},{24,216},{32,16},{40,232},{48,0},{56,248},{... | collective-permute-start | bytes 786440 | tf_op jit(solution)/shard_map/ppermute | solution.py:450
  48.0 7.0 %collective-permute-start.13 = (bf16[64,2048]{1,0:T(8,128)(2,1)S(1)}, bf16[64,2048]{1,0:T(8,128)(2,1)S(1)}, u32[]{:S(2)}, u32[]{:S(2)}) collective-permute-start(bf16[64,2048]{1,0:T(8,128)(2,1)S(1)} %pad_maximum_fusion.a), channel_id=1, source_target_pairs={{0,16},{8,72},{16,0},{24,88},{32,48},{40,104},{48,32},{56,120},{64... | collective-permute-start | bytes 786440 | tf_op jit(solution)/shard_map/ppermute | solution.py:450
  51.9 5.5 %collective-permute-start.19 = (bf16[32,2048]{1,0:T(8,128)(2,1)S(1)}, bf16[32,2048]{1,0:T(8,128)(2,1)S(1)}, u32[]{:S(2)}, u32[]{:S(2)}) collective-permute-start(bf16[32,2048]{1,0:T(8,128)(2,1)S(1)} %slice.74), channel_id=1, source_target_pairs={{0,16},{8,72},{16,0},{24,88},{32,48},{40,104},{48,32},{56,120},{64... | collective-permute-start | bytes 393224 | tf_op jit(solution)/shard_map/ppermute | solution.py:450
  52.1 5.3 %collective-permute-start.21 = (bf16[32,2048]{1,0:T(8,128)(2,1)S(1)}, bf16[32,2048]{1,0:T(8,128)(2,1)S(1)}, u32[]{:S(2)}, u32[]{:S(2)}) collective-permute-start(bf16[32,2048]{1,0:T(8,128)(2,1)S(1)} %slice.75), channel_id=1, source_target_pairs={{0,48},{8,200},{16,32},{24,216},{32,16},{40,232},{48,0},{56,248},{... | collective-permute-start | bytes 393224 | tf_op jit(solution)/shard_map/ppermute | solution.py:450
  54.7 14.4 %collective-permute-start.12 = (bf16[32,2048]{1,0:T(8,128)(2,1)S(1)}, bf16[32,2048]{1,0:T(8,128)(2,1)S(1)}, u32[]{:S(2)}, u32[]{:S(2)}) collective-permute-start(bf16[32,2048]{1,0:T(8,128)(2,1)S(1)} %slice.68), channel_id=1, source_target_pairs={{0,16},{8,72},{16,0},{24,88},{32,48},{40,104},{48,32},{56,120},{64... | collective-permute-start | bytes 393224 | tf_op jit(solution)/shard_map/ppermute | solution.py:450
  54.9 14.2 %collective-permute-start.14 = (bf16[32,2048]{1,0:T(8,128)(2,1)S(1)}, bf16[32,2048]{1,0:T(8,128)(2,1)S(1)}, u32[]{:S(2)}, u32[]{:S(2)}) collective-permute-start(bf16[32,2048]{1,0:T(8,128)(2,1)S(1)} %slice.69), channel_id=1, source_target_pairs={{0,48},{8,200},{16,32},{24,216},{32,16},{40,232},{48,0},{56,248},{... | collective-permute-start | bytes 393224 | tf_op jit(solution)/shard_map/ppermute | solution.py:450
  58.3 14.5 %collective-permute-start.22 = (bf16[64,1024]{1,0:T(8,128)(2,1)S(1)}, bf16[64,1024]{1,0:T(8,128)(2,1)S(1)}, u32[]{:S(2)}, u32[]{:S(2)}) collective-permute-start(bf16[64,1024]{1,0:T(8,128)(2,1)S(1)} %get-tuple-element.44), channel_id=1, source_target_pairs={{0,1},{1,2},{2,3},{3,4},{4,5},{5,6},{6,7},{7,0},{8,9},{9,10},{10,1... | collective-permute-start | bytes 393224 | tf_op jit(solution)/shard_map/ppermute | solution.py:460
  60.1 12.6 %collective-permute-start.23 = (bf16[64,1024]{1,0:T(8,128)(2,1)S(1)}, bf16[64,1024]{1,0:T(8,128)(2,1)S(1)}, u32[]{:S(2)}, u32[]{:S(2)}) collective-permute-start(bf16[64,1024]{1,0:T(8,128)(2,1)S(1)} %get-tuple-element.45), channel_id=1, source_target_pairs={{0,7},{1,0},{2,1},{3,2},{4,3},{5,4},{6,5},{7,6},{8,15},{9,8},{10,9... | collective-permute-start | bytes 393224 | tf_op jit(solution)/shard_map/ppermute | solution.py:460
  64.2 12.3 %collective-permute-start.26 = (bf16[64,1024]{1,0:T(8,128)(2,1)S(1)}, bf16[64,1024]{1,0:T(8,128)(2,1)S(1)}, u32[]{:S(2)}, u32[]{:S(2)}) collective-permute-start(bf16[64,1024]{1,0:T(8,128)(2,1)S(1)} %get-tuple-element.48), channel_id=1, source_target_pairs={{0,4},{1,5},{2,6},{3,7},{4,0},{5,1},{6,2},{7,3},{8,12},{9,13},{10,... | collective-permute-start | bytes 393224 | tf_op jit(solution)/shard_map/ppermute | solution.py:460
  70.0 13.6 %collective-permute-start.16 = (bf16[64,1024]{1,0:T(8,128)(2,1)S(1)}, bf16[64,1024]{1,0:T(8,128)(2,1)S(1)}, u32[]{:S(2)}, u32[]{:S(2)}) collective-permute-start(bf16[64,1024]{1,0:T(8,128)(2,1)S(1)} %get-tuple-element.40), channel_id=1, source_target_pairs={{0,1},{1,2},{2,3},{3,4},{4,5},{5,6},{6,7},{7,0},{8,9},{9,10},{10,1... | collective-permute-start | bytes 393224 | tf_op jit(solution)/shard_map/ppermute | solution.py:460
  70.0 13.5 %collective-permute-start.17 = (bf16[64,1024]{1,0:T(8,128)(2,1)S(1)}, bf16[64,1024]{1,0:T(8,128)(2,1)S(1)}, u32[]{:S(2)}, u32[]{:S(2)}) collective-permute-start(bf16[64,1024]{1,0:T(8,128)(2,1)S(1)} %get-tuple-element.41), channel_id=1, source_target_pairs={{0,7},{1,0},{2,1},{3,2},{4,3},{5,4},{6,5},{7,6},{8,15},{9,8},{10,9... | collective-permute-start | bytes 393224 | tf_op jit(solution)/shard_map/ppermute | solution.py:460
  72.8 10.8 %collective-permute-start.24 = (bf16[64,1024]{1,0:T(8,128)(2,1)S(1)}, bf16[64,1024]{1,0:T(8,128)(2,1)S(1)}, u32[]{:S(2)}, u32[]{:S(2)}) collective-permute-start(bf16[64,1024]{1,0:T(8,128)(2,1)S(1)} %get-tuple-element.46), channel_id=1, source_target_pairs={{0,2},{1,3},{2,4},{3,5},{4,6},{5,7},{6,0},{7,1},{8,10},{9,11},{10,... | collective-permute-start | bytes 393224 | tf_op jit(solution)/shard_map/ppermute | solution.py:460
  72.9 10.7 %collective-permute-start.25 = (bf16[64,1024]{1,0:T(8,128)(2,1)S(1)}, bf16[64,1024]{1,0:T(8,128)(2,1)S(1)}, u32[]{:S(2)}, u32[]{:S(2)}) collective-permute-start(bf16[64,1024]{1,0:T(8,128)(2,1)S(1)} %get-tuple-element.47), channel_id=1, source_target_pairs={{0,6},{1,7},{2,0},{3,1},{4,2},{5,3},{6,4},{7,5},{8,14},{9,15},{10,... | collective-permute-start | bytes 393224 | tf_op jit(solution)/shard_map/ppermute | solution.py:460
  76.5 11.5 %collective-permute-start.28 = (bf16[4,16,128]{2,1,0:T(8,128)(2,1)S(1)}, bf16[4,16,128]{2,1,0:T(8,128)(2,1)S(1)}, u32[]{:S(2)}, u32[]{:S(2)}) collective-permute-start(bf16[4,16,128]{2,1,0:T(8,128)(2,1)S(1)} %pad_maximum_fusion.2), channel_id=1, source_target_pairs={{0,8},{8,0},{16,24},{24,16},{32,40},{40,32},{48,56},{56,48},{64,72... | collective-permute-start | bytes 49160 | tf_op jit(solution)/shard_map/ppermute | solution.py:433
  83.7 5.2 %collective-permute-start.27 = (bf16[64,512]{1,0:T(8,128)(2,1)S(1)}, bf16[64,512]{1,0:T(8,128)(2,1)S(1)}, u32[]{:S(2)}, u32[]{:S(2)}) collective-permute-start(bf16[64,512]{1,0:T(8,128)(2,1)S(1)} %get-tuple-element.50), channel_id=1, source_target_pairs={{0,8},{8,0},{16,24},{24,16},{32,40},{40,32},{48,56},{56,48},{64,72... | collective-permute-start | bytes 196616 | tf_op jit(solution)/shard_map/ppermute | solution.py:433

commit v9 on v8

--- a/solution.py
+++ b/solution.py
@@ -144,27 +144,27 @@
     )(place, q, prompt, table, length, new, pool)
 
 
-def regroup_body(place, a0, a1, a2, a3, same, other, across):
+def regroup_body(place, a0, a1, a2, a3, same, across):
     for i, a in enumerate((a0, a1, a2, a3)):
         same[4 * i : 4 * i + 4] = a[0:4]
-        other[4 * i : 4 * i + 4] = a[4:8]
         across[4 * i : 4 * i + 4] = a[4:8]
         across[17 + 5 * i : 22 + 5 * i] = a[13:18]
 
         @pl.when(place[2] ^ (place[4] >> 1) == i)
         def _(a=a):
             same[16] = a[8]
-            other[16] = a[8]
             across[16] = a[8]
 
 
 def regroup(place, parts):
-    out = jax.ShapeDtypeStruct((17, GROUP, DH), BF16)
     return pl.pallas_call(
         regroup_body,
-        out_shape=[out, out, jax.ShapeDtypeStruct((37, GROUP, DH), BF16)],
+        out_shape=[
+            jax.ShapeDtypeStruct((17, GROUP, DH), BF16),
+            jax.ShapeDtypeStruct((37, GROUP, DH), BF16),
+        ],
         in_specs=[SMEM] + [VMEM] * 4,
-        out_specs=[VMEM] * 3,
+        out_specs=[VMEM] * 2,
         compiler_params=params(),
         name="regroup",
     )(place, *parts)
@@ -192,7 +192,7 @@
 COUNT = ROWS // GROUP
 
 
-def prefix_send_body(qa, qb, kv0, kv1, after, later, out):
+def prefix_send_body(qa, qb, kv0, kv1, after, out):
     lane = lanes()
     tile = jnp.zeros((GROUP, DH), F32)
     for half, q in enumerate((qa, qb)):
@@ -221,16 +221,16 @@
     )
 
 
-def prefix_send(qa, qb, kv0, kv1, after, later):
+def prefix_send(qa, qb, kv0, kv1, after):
     return pl.pallas_call(
         prefix_send_body,
         out_shape=jax.ShapeDtypeStruct((33, GROUP, DH), BF16),
-        in_specs=[VMEM] * 4 + [ANY] * 2,
+        in_specs=[VMEM] * 4 + [ANY],
         out_specs=VMEM,
         compiler_params=params(24),
         cost_estimate=prefix_cost(512),
         name="prefix_send",
-    )(qa, qb, kv0, kv1, after, later)
+    )(qa, qb, kv0, kv1, after)
 
 
 def prefix_keep(q, kv0, kv1):
@@ -472,11 +472,15 @@
 
     sent = local_parts(place, queries, prompt_of, page_table.T, suffix_len, new_kv, suffix_kv)
     by_x = [sent[0]] + [along_x(sent[k], k) for k in (1, 2, 3)]
-    same, other, across = regroup(place, by_x)
-    from1, from3, from2 = along_y(same, 1), along_y(other, 3), along_y(across, 2)
+    same, across = regroup(place, by_x)
+    from1, from3 = along_y(same, 1), along_y(across, 3)
 
     own = prefix_keep(same, prefix_kv, prefix_other)
-    message = along_y(prefix_send(from1, from3, prefix_kv, prefix_other, own[1], from2), 1)
+    passed, own = lax.optimization_barrier((from3, own))
+    from2 = along_y(passed, 1)
+    message = prefix_send(from1, from3, prefix_kv, prefix_other, own[1])
+    message, from2 = lax.optimization_barrier((message, from2))
+    message = along_y(message, 1)
     cross = prefix_keep(from2, prefix_kv, prefix_other)
     attended = combine(place, own, cross, message, by_x, from2)
 

time: 89.9 us -> 88.2 us (0.981)
  waiting for transfers between devices: 16.1 us -> 14.8 us
    ppermute x11, waiting for transfers between devices: 6.54 us -> 4.89 us  [along(): lax.ppermute(value, 'batch', [(i, i ^ k << shift) for i in range(BATCH)])]
  transfers between devices with their start and end apart: 29 -> 29, of which waited for: 12 -> 10; matrix products, arithmetic and copies ran while one was open for 1% -> 1% of each run, Pallas kernels for 17% -> 22%
where the time goes in v9:
time: 88.2 us; the launch traced here: 88 us
  starting transfers between devices  51.4 us (58%)
  Pallas kernels  19.9 us (23%)
  waiting for transfers between devices  14.8 us (17%)
  local copies, waits for them, and re-layouts  1.62 us (2%)
    ppermute x11, starting transfers between devices, along(): lax.ppermute(value, 'batch', [(i, i ^ k << shift) for i in range(BATCH)])  24.6 us
    ppermute x7, starting transfers between devices, along_z(): lax.ppermute(value, 'head', [(i, (i + k) % HEADS) for i in range(HEADS)])  16.1 us
    ppermute x11, starting transfers between devices, turned(): return lax.ppermute(value, 'batch', pairs)  10.7 us
    ppermute x11, waiting for transfers between devices, turned(): return lax.ppermute(value, 'batch', pairs)  9.85 us
    ppermute x11, waiting for transfers between devices, along(): lax.ppermute(value, 'batch', [(i, i ^ k << shift) for i in range(BATCH)])  4.89 us
    pallas_call x2, Pallas kernels, prefix_keep(): pl.pallas_call(prefix_keep_body, out_shape=[out, out], in_specs=[VMEM] *...  4.34 us
    pallas_call x1, Pallas kernels, local_parts(): pl.pallas_call(local_body, out_shape=[out] * 4, in_specs=[SMEM] + [HBM] *...  4.23 us
    pallas_call x1, Pallas kernels, prefix_send(): pl.pallas_call(prefix_send_body, out_shape=jax.ShapeDtypeStruct((33, GROU...  4.09 us
  transfers between devices with their start and end apart: 29, of which 10 were waited for; matrix products, arithmetic and copies ran while one was open for 1% of the time, Pallas kernels for 22%

profile of v9, /device:TPU:1, one launch (start us, length us, event | category | flops | bytes accessed | tf_op | source)
XLA Modules:
  0.0 88.0 jit_solution(7577633463321180109)
XLA Ops:
  0.0 3.2 %collective-permute-start.4 = (bf16[2,2048,128]{2,1,0:T(8,128)(2,1)}, bf16[2,2048,128]{2,1,0:T(8,128)(2,1)S(1)}, u32[]{:S(2)}, u32[]{:S(2)}) collective-permute-start(bf16[2,2048,128]{2,1,0:T(8,128)(2,1)} %kv0.5), channel_id=1, source_target_pairs={{0,8},{8,0},{16,24},{24,16},{32,40},{40,32},{48,56},{56,48},{64,72... | collective-permute-start | bytes 3145736 | tf_op jit(solution)/shard_map/ppermute | solution.py:433
  3.2 0.6 stack.34.place
  3.8 4.2 %local_parts.1 = (bf16[18,16,128]{2,1,0:T(8,128)(2,1)}, bf16[18,16,128]{2,1,0:T(8,128)(2,1)}, bf16[18,16,128]{2,1,0:T(8,128)(2,1)}, bf16[18,16,128]{2,1,0:T(8,128)(2,1)}) custom-call(s32[7]{0:T(128)} %stack.34.place, bf16[32,2048]{1,0:T(8,128)(2,1)} %q_in.1, s32[32]{0:T(128)} %prompt_in.1, s32[8,32]{1,0:T(8,128)} %bitcast.8, s32[32]{0:T(128)} %length_in.1, ...), custom_call_target="tpu_custom_call" | custom-call | tf_op jit(solution)/shard_map/local_parts/pallas_call | solution.py:124
  8.1 0.1 collective-permute-start
  8.2 1.9 %collective-permute-start.1 = (bf16[18,16,128]{2,1,0:T(8,128)(2,1)}, bf16[18,16,128]{2,1,0:T(8,128)(2,1)S(1)}, u32[]{:S(2)}, u32[]{:S(2)}) collective-permute-start(bf16[18,16,128]{2,1,0:T(8,128)(2,1)} %get-tuple-element.34), channel_id=1, source_target_pairs={{0,128},{8,136},{16,144},{24,152},{32,160},{40,168},{48,176},{56,1... | collective-permute-start | bytes 221192 | tf_op jit(solution)/shard_map/ppermute | solution.py:433
  10.1 1.9 %collective-permute-start.2 = (bf16[18,16,128]{2,1,0:T(8,128)(2,1)}, bf16[18,16,128]{2,1,0:T(8,128)(2,1)S(1)}, u32[]{:S(2)}, u32[]{:S(2)}) collective-permute-start(bf16[18,16,128]{2,1,0:T(8,128)(2,1)} %get-tuple-element.35), channel_id=1, source_target_pairs={{0,192},{8,200},{16,208},{24,216},{32,224},{40,232},{48,240},{56,2... | collective-permute-start | bytes 221192 | tf_op jit(solution)/shard_map/ppermute | solution.py:433
  12.0 0.3 collective-permute-done.a1.s1
  12.3 2.0 %collective-permute-done.1.a2.s2 = bf16[18,16,128]{2,1,0:T(8,128)(2,1)S(1)} collective-permute-done((bf16[18,16,128]{2,1,0:T(8,128)(2,1)}, bf16[18,16,128]{2,1,0:T(8,128)(2,1)S(1)}, u32[]{:S(2)}, u32[]{:S(2)}) %collective-permute-start.1) | collective-permute-done | bytes 73760 | tf_op jit(solution)/shard_map/ppermute | solution.py:433
  14.3 1.4 %collective-permute-done.2.a3.s3 = bf16[18,16,128]{2,1,0:T(8,128)(2,1)S(1)} collective-permute-done((bf16[18,16,128]{2,1,0:T(8,128)(2,1)}, bf16[18,16,128]{2,1,0:T(8,128)(2,1)S(1)}, u32[]{:S(2)}, u32[]{:S(2)}) %collective-permute-start.2) | collective-permute-done | bytes 73760 | tf_op jit(solution)/shard_map/ppermute | solution.py:433
  15.8 0.9 %copy-done.2 = bf16[18,16,128]{2,1,0:T(8,128)(2,1)S(1)} copy-done((bf16[18,16,128]{2,1,0:T(8,128)(2,1)S(1)}, bf16[18,16,128]{2,1,0:T(8,128)(2,1)}, u32[]{:S(2)}) %copy-start.2) | copy-done | bytes 73752
  16.6 0.6 regroup.1
  17.2 2.8 %collective-permute-start.3 = (bf16[37,16,128]{2,1,0:T(8,128)(2,1)S(1)}, bf16[37,16,128]{2,1,0:T(8,128)(2,1)S(1)}, u32[]{:S(2)}, u32[]{:S(2)}) collective-permute-start(bf16[37,16,128]{2,1,0:T(8,128)(2,1)S(1)} %get-tuple-element.36), channel_id=1, source_target_pairs={{0,48},{8,56},{16,32},{24,40},{32,16},{40,24},{48,0},{56,8},{64,11... | collective-permute-start | bytes 454664 | tf_op jit(solution)/shard_map/ppermute | solution.py:433
  20.1 2.2 %prefix_keep.2 = (f32[16,16,128]{2,1,0:T(8,128)S(1)}, f32[16,16,128]{2,1,0:T(8,128)S(1)}) custom-call(bf16[17,16,128]{2,1,0:T(8,128)(2,1)S(1)} %get-tuple-element.37.q, bf16[2,2048,128]{2,1,0:T(8,128)(2,1)S(1)} %copy-done.1, bf16[2,2048,128]{2,1,0:T(8,128)(2,1)S(1)} %collective-permute-done.4.kv1), custom_call_target="tpu_custom_call" | custom-call | flops 536870912 | bytes 2500000 | tf_op jit(solution)/shard_map/prefix_keep/pallas_call | solution.py:238
  22.2 0.0 copy-start
  22.2 0.9 %collective-permute-done.3.qb = bf16[37,16,128]{2,1,0:T(8,128)(2,1)S(1)} collective-permute-done((bf16[37,16,128]{2,1,0:T(8,128)(2,1)S(1)}, bf16[37,16,128]{2,1,0:T(8,128)(2,1)S(1)}, u32[]{:S(2)}, u32[]{:S(2)}) %collective-permute-start.3) | collective-permute-done | bytes 151584 | tf_op jit(solution)/shard_map/ppermute | solution.py:433
  23.2 0.6 collective-permute-start.6
  23.8 4.1 %prefix_send.1 = bf16[33,16,128]{2,1,0:T(8,128)(2,1)S(1)} custom-call(bf16[17,16,128]{2,1,0:T(8,128)(2,1)S(1)} %collective-permute-done.5.qa, bf16[37,16,128]{2,1,0:T(8,128)(2,1)S(1)} %collective-permute-done.3.qb, bf16[2,2048,128]{2,1,0:T(8,128)(2,1)S(1)} %copy-done.1, bf16[2,2048,128]{2,1,0:T(8,128)(2,1)S(1)} %collective-permute-done.4.kv1, ...), custom_call_target="tpu_custom_call" | custom-call | flops 1073741824 | bytes 2500000 | tf_op jit(solution)/shard_map/prefix_send/pallas_call | solution.py:225
  27.9 0.0 copy-start.3
  27.9 0.0 collective-permute-done.6.q.far
  27.9 0.9 %collective-permute-start.7 = (bf16[33,16,128]{2,1,0:T(8,128)(2,1)S(1)}, bf16[33,16,128]{2,1,0:T(8,128)(2,1)S(1)}, u32[]{:S(2)}, u32[]{:S(2)}) collective-permute-start(bf16[33,16,128]{2,1,0:T(8,128)(2,1)S(1)} %prefix_send.1), channel_id=1, source_target_pairs={{0,16},{8,24},{16,0},{24,8},{32,48},{40,56},{48,32},{56,40},{64,80... | collective-permute-start | bytes 405512 | tf_op jit(solution)/shard_map/ppermute | solution.py:433
  28.8 2.3 %collective-permute-start.15 = (bf16[2048,512]{1,0:T(8,128)(2,1)S(1)}, bf16[2048,512]{1,0:T(8,128)(2,1)S(1)}, u32[]{:S(2)}, u32[]{:S(2)}) collective-permute-start(bf16[2048,512]{1,0:T(8,128)(2,1)S(1)} %copy-done), channel_id=1, source_target_pairs={{0,8},{8,0},{16,24},{24,16},{32,40},{40,32},{48,56},{56,48},{64,72... | collective-permute-start | bytes 6291464 | tf_op jit(solution)/shard_map/ppermute | solution.py:433
  31.2 2.2 %prefix_keep.3 = (f32[16,16,128]{2,1,0:T(8,128)S(1)}, f32[16,16,128]{2,1,0:T(8,128)S(1)}) custom-call(bf16[37,16,128]{2,1,0:T(8,128)(2,1)S(1)} %collective-permute-done.6.q.far, bf16[2,2048,128]{2,1,0:T(8,128)(2,1)S(1)} %copy-done.1, bf16[2,2048,128]{2,1,0:T(8,128)(2,1)S(1)} %collective-permute-done.4.kv1), custom_call_target="tpu_custom_call" | custom-call | flops 536870912 | bytes 2500000 | tf_op jit(solution)/shard_map/prefix_keep/pallas_call | solution.py:238
  33.3 1.2 %combine.1 = bf16[32,2048]{1,0:T(8,128)(2,1)S(1)} custom-call(s32[7]{0:T(128)S(1)} %copy-done.4, f32[16,16,128]{2,1,0:T(8,128)S(1)} %get-tuple-element.40.own, f32[16,16,128]{2,1,0:T(8,128)S(1)} %get-tuple-element.41.after.own_masses, f32[16,16,128]{2,1,0:T(8,128)S(1)} %get-tuple-element.44.cross, f32[16,16,128]{2,1,0:T(8,128)S(1)} %get-tuple-element.45.cross_masses, ...), custom_call_target="tpu_custom_call" | custom-call | tf_op jit(solution)/shard_map/combine/pallas_call | solution.py:281
  34.6 0.8 collective-permute-start.8
  35.4 3.2 %collective-permute-start.9 = (bf16[32,2048]{1,0:T(8,128)(2,1)S(1)}, bf16[32,2048]{1,0:T(8,128)(2,1)S(1)}, u32[]{:S(2)}, u32[]{:S(2)}) collective-permute-start(bf16[32,2048]{1,0:T(8,128)(2,1)S(1)} %combine.1), channel_id=1, source_target_pairs={{0,128},{8,40},{16,144},{24,56},{32,160},{40,8},{48,176},{56,24},{... | collective-permute-start | bytes 393224 | tf_op jit(solution)/shard_map/ppermute | solution.py:450
  38.6 3.7 %collective-permute-done.9 = bf16[32,2048]{1,0:T(8,128)(2,1)S(1)} collective-permute-done((bf16[32,2048]{1,0:T(8,128)(2,1)S(1)}, bf16[32,2048]{1,0:T(8,128)(2,1)S(1)}, u32[]{:S(2)}, u32[]{:S(2)}) %collective-permute-start.9) | collective-permute-done | bytes 131104 | tf_op jit(solution)/shard_map/ppermute | solution.py:450
  42.3 1.7 %collective-permute-done.10 = bf16[32,2048]{1,0:T(8,128)(2,1)S(1)} collective-permute-done((bf16[32,2048]{1,0:T(8,128)(2,1)S(1)}, bf16[32,2048]{1,0:T(8,128)(2,1)S(1)}, u32[]{:S(2)}, u32[]{:S(2)}) %collective-permute-start.10) | collective-permute-done | bytes 131104 | tf_op jit(solution)/shard_map/ppermute | solution.py:450
  44.0 1.0 %collective-permute-start.18 = (bf16[64,2048]{1,0:T(8,128)(2,1)S(1)}, bf16[64,2048]{1,0:T(8,128)(2,1)S(1)}, u32[]{:S(2)}, u32[]{:S(2)}) collective-permute-start(bf16[64,2048]{1,0:T(8,128)(2,1)S(1)} %pad_maximum_fusion.1.a), channel_id=1, source_target_pairs={{0,48},{8,200},{16,32},{24,216},{32,16},{40,232},{48,0},{56,248},{... | collective-permute-start | bytes 786440 | tf_op jit(solution)/shard_map/ppermute | solution.py:450
  45.0 0.0 collective-permute-start.20
  45.0 1.9 %collective-permute-start.11 = (bf16[64,2048]{1,0:T(8,128)(2,1)S(1)}, bf16[64,2048]{1,0:T(8,128)(2,1)S(1)}, u32[]{:S(2)}, u32[]{:S(2)}) collective-permute-start(bf16[64,2048]{1,0:T(8,128)(2,1)S(1)} %pad_maximum_fusion.a), channel_id=1, source_target_pairs={{0,48},{8,200},{16,32},{24,216},{32,16},{40,232},{48,0},{56,248},{... | collective-permute-start | bytes 786440 | tf_op jit(solution)/shard_map/ppermute | solution.py:450
  46.9 0.9 collective-permute-start.13
  47.8 3.1 %collective-permute-done.18.c = bf16[64,2048]{1,0:T(8,128)(2,1)S(1)} collective-permute-done((bf16[64,2048]{1,0:T(8,128)(2,1)S(1)}, bf16[64,2048]{1,0:T(8,128)(2,1)S(1)}, u32[]{:S(2)}, u32[]{:S(2)}) %collective-permute-start.18) | collective-permute-done | bytes 262176 | tf_op jit(solution)/shard_map/ppermute | solution.py:450
  50.8 0.1 collective-permute-start.19
  50.9 0.0 collective-permute-done.20.b
  51.0 1.4 %collective-permute-start.21 = (bf16[32,2048]{1,0:T(8,128)(2,1)S(1)}, bf16[32,2048]{1,0:T(8,128)(2,1)S(1)}, u32[]{:S(2)}, u32[]{:S(2)}) collective-permute-start(bf16[32,2048]{1,0:T(8,128)(2,1)S(1)} %slice.75), channel_id=1, source_target_pairs={{0,48},{8,200},{16,32},{24,216},{32,16},{40,232},{48,0},{56,248},{... | collective-permute-start | bytes 393224 | tf_op jit(solution)/shard_map/ppermute | solution.py:450
  52.4 1.2 %collective-permute-done.11.c = bf16[64,2048]{1,0:T(8,128)(2,1)S(1)} collective-permute-done((bf16[64,2048]{1,0:T(8,128)(2,1)S(1)}, bf16[64,2048]{1,0:T(8,128)(2,1)S(1)}, u32[]{:S(2)}, u32[]{:S(2)}) %collective-permute-start.11) | collective-permute-done | bytes 262176 | tf_op jit(solution)/shard_map/ppermute | solution.py:450
  53.7 0.1 collective-permute-start.12
  53.8 1.4 %collective-permute-start.14 = (bf16[32,2048]{1,0:T(8,128)(2,1)S(1)}, bf16[32,2048]{1,0:T(8,128)(2,1)S(1)}, u32[]{:S(2)}, u32[]{:S(2)}) collective-permute-start(bf16[32,2048]{1,0:T(8,128)(2,1)S(1)} %slice.69), channel_id=1, source_target_pairs={{0,48},{8,200},{16,32},{24,216},{32,16},{40,232},{48,0},{56,248},{... | collective-permute-start | bytes 393224 | tf_op jit(solution)/shard_map/ppermute | solution.py:450
  55.2 1.0 %project.3.first = f32[4,48,1024]{2,1,0:T(8,128)S(1)} custom-call(bf16[64,2048]{1,0:T(8,128)(2,1)S(1)} %pad_maximum_fusion.1.a, bf16[64,2048]{1,0:T(8,128)(2,1)S(1)} %collective-permute-done.20.b, bf16[64,2048]{1,0:T(8,128)(2,1)S(1)} %collective-permute-done.18.c, bf16[2048,512]{1,0:T(8,128)(2,1)S(1)} %copy-done, ...), custom_call_target="tpu_custom_call" | custom-call | flops 805306368 | bytes 4500000 | tf_op jit(solution)/shard_map/project/pallas_call | solution.py:316
  56.2 0.0 collective-permute-done.19.a
  56.3 0.1 collective-permute-done.21.b
  56.4 0.9 far.1
  57.3 1.7 %collective-permute-start.22 = (bf16[64,1024]{1,0:T(8,128)(2,1)S(1)}, bf16[64,1024]{1,0:T(8,128)(2,1)S(1)}, u32[]{:S(2)}, u32[]{:S(2)}) collective-permute-start(bf16[64,1024]{1,0:T(8,128)(2,1)S(1)} %get-tuple-element.52), channel_id=1, source_target_pairs={{0,1},{1,2},{2,3},{3,4},{4,5},{5,6},{6,7},{7,0},{8,9},{9,10},{10,1... | collective-permute-start | bytes 393224 | tf_op jit(solution)/shard_map/ppermute | solution.py:460
  59.0 4.0 %collective-permute-start.23 = (bf16[64,1024]{1,0:T(8,128)(2,1)S(1)}, bf16[64,1024]{1,0:T(8,128)(2,1)S(1)}, u32[]{:S(2)}, u32[]{:S(2)}) collective-permute-start(bf16[64,1024]{1,0:T(8,128)(2,1)S(1)} %get-tuple-element.53), channel_id=1, source_target_pairs={{0,7},{1,0},{2,1},{3,2},{4,3},{5,4},{6,5},{7,6},{8,15},{9,8},{10,9... | collective-permute-start | bytes 393224 | tf_op jit(solution)/shard_map/ppermute | solution.py:460
  63.0 3.9 %collective-permute-start.26 = (bf16[64,1024]{1,0:T(8,128)(2,1)S(1)}, bf16[64,1024]{1,0:T(8,128)(2,1)S(1)}, u32[]{:S(2)}, u32[]{:S(2)}) collective-permute-start(bf16[64,1024]{1,0:T(8,128)(2,1)S(1)} %get-tuple-element.56), channel_id=1, source_target_pairs={{0,4},{1,5},{2,6},{3,7},{4,0},{5,1},{6,2},{7,3},{8,12},{9,13},{10,... | collective-permute-start | bytes 393224 | tf_op jit(solution)/shard_map/ppermute | solution.py:460
  66.9 1.0 %project.2.first = f32[4,48,1024]{2,1,0:T(8,128)S(1)} custom-call(bf16[64,2048]{1,0:T(8,128)(2,1)S(1)} %pad_maximum_fusion.a, bf16[64,2048]{1,0:T(8,128)(2,1)S(1)} %collective-permute-done.13.b, bf16[64,2048]{1,0:T(8,128)(2,1)S(1)} %collective-permute-done.11.c, bf16[2048,512]{1,0:T(8,128)(2,1)S(1)} %copy-done, bf16[2048,512]{1,0:T(8,128)(2,1)S(1)} %collective-permute-done.15.w1), custom_call_target="tpu_custom_call" | custom-call | flops 805306368 | bytes 4500000 | tf_op jit(solution)/shard_map/project/pallas_call | solution.py:316
  68.0 0.0 collective-permute-done.14.b
  68.0 0.9 near.1
  68.9 0.1 collective-permute-start.16
  68.9 2.7 %collective-permute-start.17 = (bf16[64,1024]{1,0:T(8,128)(2,1)S(1)}, bf16[64,1024]{1,0:T(8,128)(2,1)S(1)}, u32[]{:S(2)}, u32[]{:S(2)}) collective-permute-start(bf16[64,1024]{1,0:T(8,128)(2,1)S(1)} %get-tuple-element.49), channel_id=1, source_target_pairs={{0,7},{1,0},{2,1},{3,2},{4,3},{5,4},{6,5},{7,6},{8,15},{9,8},{10,9... | collective-permute-start | bytes 393224 | tf_op jit(solution)/shard_map/ppermute | solution.py:460
  71.6 0.0 collective-permute-done.22.below
  71.6 0.1 middle.1
  71.7 0.1 collective-permute-start.24
  71.8 3.6 %collective-permute-start.25 = (bf16[64,1024]{1,0:T(8,128)(2,1)S(1)}, bf16[64,1024]{1,0:T(8,128)(2,1)S(1)}, u32[]{:S(2)}, u32[]{:S(2)}) collective-permute-start(bf16[64,1024]{1,0:T(8,128)(2,1)S(1)} %get-tuple-element.55), channel_id=1, source_target_pairs={{0,6},{1,7},{2,0},{3,1},{4,2},{5,3},{6,4},{7,5},{8,14},{9,15},{10,... | collective-permute-start | bytes 393224 | tf_op jit(solution)/shard_map/ppermute | solution.py:460
  75.3 7.0 %collective-permute-start.28 = (bf16[4,16,128]{2,1,0:T(8,128)(2,1)S(1)}, bf16[4,16,128]{2,1,0:T(8,128)(2,1)S(1)}, u32[]{:S(2)}, u32[]{:S(2)}) collective-permute-start(bf16[4,16,128]{2,1,0:T(8,128)(2,1)S(1)} %pad_maximum_fusion.2), channel_id=1, source_target_pairs={{0,8},{8,0},{16,24},{24,16},{32,40},{40,32},{48,56},{56,48},{64,72... | collective-permute-start | bytes 49160 | tf_op jit(solution)/shard_map/ppermute | solution.py:433
  82.3 0.0 collective-permute-done.16.below1
  82.3 0.0 collective-permute-done.17.above1
  82.3 0.0 collective-permute-done.24.below2
  82.3 0.1 total.1
  82.4 3.8 %collective-permute-start.27 = (bf16[64,512]{1,0:T(8,128)(2,1)S(1)}, bf16[64,512]{1,0:T(8,128)(2,1)S(1)}, u32[]{:S(2)}, u32[]{:S(2)}) collective-permute-start(bf16[64,512]{1,0:T(8,128)(2,1)S(1)} %get-tuple-element.58), channel_id=1, source_target_pairs={{0,8},{8,0},{16,24},{24,16},{32,40},{40,32},{48,56},{56,48},{64,72... | collective-permute-start | bytes 196616 | tf_op jit(solution)/shard_map/ppermute | solution.py:433
  86.2 0.0 collective-permute-done.28
  86.2 0.6 order_rows.1.pick
  86.9 0.2 collective-permute-done.27.other
  87.1 0.9 %finish.1 = bf16[128,512]{1,0:T(8,128)(2,1)} custom-call(bf16[64,512]{1,0:T(8,128)(2,1)S(1)} %get-tuple-element.57.own, bf16[64,512]{1,0:T(8,128)(2,1)S(1)} %collective-permute-done.27.other, bf16[128,128]{1,0:T(8,128)(2,1)S(1)} %order_rows.1.pick), custom_call_target="tpu_custom_call" | custom-call | tf_op jit(solution)/shard_map/finish/pallas_call | solution.py:422
  (35 shorter events, 0.2 us)
Async XLA Ops:
  0.0 20.0 %copy-start.1 = (bf16[2,2048,128]{2,1,0:T(8,128)(2,1)S(1)}, bf16[2,2048,128]{2,1,0:T(8,128)(2,1)}, u32[]{:S(2)}) copy-start(bf16[2,2048,128]{2,1,0:T(8,128)(2,1)} %kv0.5) | copy-start | bytes 3145732
  0.0 20.0 %collective-permute-start.4 = (bf16[2,2048,128]{2,1,0:T(8,128)(2,1)}, bf16[2,2048,128]{2,1,0:T(8,128)(2,1)S(1)}, u32[]{:S(2)}, u32[]{:S(2)}) collective-permute-start(bf16[2,2048,128]{2,1,0:T(8,128)(2,1)} %kv0.5), channel_id=1, source_target_pairs={{0,8},{8,0},{16,24},{24,16},{32,40},{40,32},{48,56},{56,48},{64,72... | collective-permute-start | bytes 3145736 | tf_op jit(solution)/shard_map/ppermute | solution.py:433
  3.8 11.9 %copy-start.4 = (s32[7]{0:T(128)S(1)}, s32[7]{0:T(128)}, u32[]{:S(2)}) copy-start(s32[7]{0:T(128)} %stack.34.place) | copy-start | bytes 88
  8.1 4.2 %collective-permute-start = (bf16[18,16,128]{2,1,0:T(8,128)(2,1)}, bf16[18,16,128]{2,1,0:T(8,128)(2,1)S(1)}, u32[]{:S(2)}, u32[]{:S(2)}) collective-permute-start(bf16[18,16,128]{2,1,0:T(8,128)(2,1)} %get-tuple-element.33), channel_id=1, source_target_pairs={{0,64},{8,72},{16,80},{24,88},{32,96},{40,104},{48,112},{56,120},{... | collective-permute-start | bytes 221192 | tf_op jit(solution)/shard_map/ppermute | solution.py:433
  8.2 6.1 %collective-permute-start.1 = (bf16[18,16,128]{2,1,0:T(8,128)(2,1)}, bf16[18,16,128]{2,1,0:T(8,128)(2,1)S(1)}, u32[]{:S(2)}, u32[]{:S(2)}) collective-permute-start(bf16[18,16,128]{2,1,0:T(8,128)(2,1)} %get-tuple-element.34), channel_id=1, source_target_pairs={{0,128},{8,136},{16,144},{24,152},{32,160},{40,168},{48,176},{56,1... | collective-permute-start | bytes 221192 | tf_op jit(solution)/shard_map/ppermute | solution.py:433
  10.1 5.6 %collective-permute-start.2 = (bf16[18,16,128]{2,1,0:T(8,128)(2,1)}, bf16[18,16,128]{2,1,0:T(8,128)(2,1)S(1)}, u32[]{:S(2)}, u32[]{:S(2)}) collective-permute-start(bf16[18,16,128]{2,1,0:T(8,128)(2,1)} %get-tuple-element.35), channel_id=1, source_target_pairs={{0,192},{8,200},{16,208},{24,216},{32,224},{40,232},{48,240},{56,2... | collective-permute-start | bytes 221192 | tf_op jit(solution)/shard_map/ppermute | solution.py:433
  15.8 0.9 %copy-start.2 = (bf16[18,16,128]{2,1,0:T(8,128)(2,1)S(1)}, bf16[18,16,128]{2,1,0:T(8,128)(2,1)}, u32[]{:S(2)}) copy-start(bf16[18,16,128]{2,1,0:T(8,128)(2,1)} %get-tuple-element.32.a0.s0) | copy-start | bytes 221188
  17.2 5.9 %collective-permute-start.3 = (bf16[37,16,128]{2,1,0:T(8,128)(2,1)S(1)}, bf16[37,16,128]{2,1,0:T(8,128)(2,1)S(1)}, u32[]{:S(2)}, u32[]{:S(2)}) collective-permute-start(bf16[37,16,128]{2,1,0:T(8,128)(2,1)S(1)} %get-tuple-element.36), channel_id=1, source_target_pairs={{0,48},{8,56},{16,32},{24,40},{32,16},{40,24},{48,0},{56,8},{64,11... | collective-permute-start | bytes 454664 | tf_op jit(solution)/shard_map/ppermute | solution.py:433
  20.0 3.8 %collective-permute-start.5 = (bf16[17,16,128]{2,1,0:T(8,128)(2,1)S(1)}, bf16[17,16,128]{2,1,0:T(8,128)(2,1)S(1)}, u32[]{:S(2)}, u32[]{:S(2)}) collective-permute-start(bf16[17,16,128]{2,1,0:T(8,128)(2,1)S(1)} %get-tuple-element.37.q), channel_id=1, source_target_pairs={{0,16},{8,24},{16,0},{24,8},{32,48},{40,56},{48,32},{56,40},{64,80... | collective-permute-start | bytes 208904 | tf_op jit(solution)/shard_map/ppermute | solution.py:433
  22.2 6.6 %copy-start = (bf16[2048,512]{1,0:T(8,128)(2,1)S(1)}, bf16[2048,512]{1,0:T(8,128)(2,1)}, u32[]{:S(2)}) copy-start(bf16[2048,512]{1,0:T(8,128)(2,1)} %w0.7) | copy-start | bytes 6291460
  23.2 4.8 %collective-permute-start.6 = (bf16[37,16,128]{2,1,0:T(8,128)(2,1)S(1)}, bf16[37,16,128]{2,1,0:T(8,128)(2,1)S(1)}, u32[]{:S(2)}, u32[]{:S(2)}) collective-permute-start(bf16[37,16,128]{2,1,0:T(8,128)(2,1)S(1)} %collective-permute-done.3.qb), channel_id=1, source_target_pairs={{0,16},{8,24},{16,0},{24,8},{32,48},{40,56},{48,32},{56,40},{64,80... | collective-permute-start | bytes 454664 | tf_op jit(solution)/shard_map/ppermute | solution.py:433
  27.9 5.4 %copy-start.3 = (bf16[18,16,128]{2,1,0:T(8,128)(2,1)S(1)}, bf16[18,16,128]{2,1,0:T(8,128)(2,1)}, u32[]{:S(2)}) copy-start(bf16[18,16,128]{2,1,0:T(8,128)(2,1)} %get-tuple-element.32.a0.s0) | copy-start | bytes 221188
  27.9 5.4 %collective-permute-start.7 = (bf16[33,16,128]{2,1,0:T(8,128)(2,1)S(1)}, bf16[33,16,128]{2,1,0:T(8,128)(2,1)S(1)}, u32[]{:S(2)}, u32[]{:S(2)}) collective-permute-start(bf16[33,16,128]{2,1,0:T(8,128)(2,1)S(1)} %prefix_send.1), channel_id=1, source_target_pairs={{0,16},{8,24},{16,0},{24,8},{32,48},{40,56},{48,32},{56,40},{64,80... | collective-permute-start | bytes 405512 | tf_op jit(solution)/shard_map/ppermute | solution.py:433
  28.8 26.4 %collective-permute-start.15 = (bf16[2048,512]{1,0:T(8,128)(2,1)S(1)}, bf16[2048,512]{1,0:T(8,128)(2,1)S(1)}, u32[]{:S(2)}, u32[]{:S(2)}) collective-permute-start(bf16[2048,512]{1,0:T(8,128)(2,1)S(1)} %copy-done), channel_id=1, source_target_pairs={{0,8},{8,0},{16,24},{24,16},{32,40},{40,32},{48,56},{56,48},{64,72... | collective-permute-start | bytes 6291464 | tf_op jit(solution)/shard_map/ppermute | solution.py:433
  34.6 4.0 %collective-permute-start.8 = (bf16[32,2048]{1,0:T(8,128)(2,1)S(1)}, bf16[32,2048]{1,0:T(8,128)(2,1)S(1)}, u32[]{:S(2)}, u32[]{:S(2)}) collective-permute-start(bf16[32,2048]{1,0:T(8,128)(2,1)S(1)} %combine.1), channel_id=1, source_target_pairs={{0,64},{8,24},{16,80},{24,8},{32,96},{40,56},{48,112},{56,40},{64,... | collective-permute-start | bytes 393224 | tf_op jit(solution)/shard_map/ppermute | solution.py:450
  35.4 6.9 %collective-permute-start.9 = (bf16[32,2048]{1,0:T(8,128)(2,1)S(1)}, bf16[32,2048]{1,0:T(8,128)(2,1)S(1)}, u32[]{:S(2)}, u32[]{:S(2)}) collective-permute-start(bf16[32,2048]{1,0:T(8,128)(2,1)S(1)} %combine.1), channel_id=1, source_target_pairs={{0,128},{8,40},{16,144},{24,56},{32,160},{40,8},{48,176},{56,24},{... | collective-permute-start | bytes 393224 | tf_op jit(solution)/shard_map/ppermute | solution.py:450
  38.5 5.5 %collective-permute-start.10 = (bf16[32,2048]{1,0:T(8,128)(2,1)S(1)}, bf16[32,2048]{1,0:T(8,128)(2,1)S(1)}, u32[]{:S(2)}, u32[]{:S(2)}) collective-permute-start(bf16[32,2048]{1,0:T(8,128)(2,1)S(1)} %combine.1), channel_id=1, source_target_pairs={{0,192},{8,56},{16,208},{24,40},{32,224},{40,24},{48,240},{56,8},{... | collective-permute-start | bytes 393224 | tf_op jit(solution)/shard_map/ppermute | solution.py:450
  44.0 6.8 %collective-permute-start.18 = (bf16[64,2048]{1,0:T(8,128)(2,1)S(1)}, bf16[64,2048]{1,0:T(8,128)(2,1)S(1)}, u32[]{:S(2)}, u32[]{:S(2)}) collective-permute-start(bf16[64,2048]{1,0:T(8,128)(2,1)S(1)} %pad_maximum_fusion.1.a), channel_id=1, source_target_pairs={{0,48},{8,200},{16,32},{24,216},{32,16},{40,232},{48,0},{56,248},{... | collective-permute-start | bytes 786440 | tf_op jit(solution)/shard_map/ppermute | solution.py:450
  45.0 5.9 %collective-permute-start.20 = (bf16[64,2048]{1,0:T(8,128)(2,1)S(1)}, bf16[64,2048]{1,0:T(8,128)(2,1)S(1)}, u32[]{:S(2)}, u32[]{:S(2)}) collective-permute-start(bf16[64,2048]{1,0:T(8,128)(2,1)S(1)} %pad_maximum_fusion.1.a), channel_id=1, source_target_pairs={{0,16},{8,72},{16,0},{24,88},{32,48},{40,104},{48,32},{56,120},{64... | collective-permute-start | bytes 786440 | tf_op jit(solution)/shard_map/ppermute | solution.py:450
  45.0 8.6 %collective-permute-start.11 = (bf16[64,2048]{1,0:T(8,128)(2,1)S(1)}, bf16[64,2048]{1,0:T(8,128)(2,1)S(1)}, u32[]{:S(2)}, u32[]{:S(2)}) collective-permute-start(bf16[64,2048]{1,0:T(8,128)(2,1)S(1)} %pad_maximum_fusion.a), channel_id=1, source_target_pairs={{0,48},{8,200},{16,32},{24,216},{32,16},{40,232},{48,0},{56,248},{... | collective-permute-start | bytes 786440 | tf_op jit(solution)/shard_map/ppermute | solution.py:450
  46.9 6.9 %collective-permute-start.13 = (bf16[64,2048]{1,0:T(8,128)(2,1)S(1)}, bf16[64,2048]{1,0:T(8,128)(2,1)S(1)}, u32[]{:S(2)}, u32[]{:S(2)}) collective-permute-start(bf16[64,2048]{1,0:T(8,128)(2,1)S(1)} %pad_maximum_fusion.a), channel_id=1, source_target_pairs={{0,16},{8,72},{16,0},{24,88},{32,48},{40,104},{48,32},{56,120},{64... | collective-permute-start | bytes 786440 | tf_op jit(solution)/shard_map/ppermute | solution.py:450
  50.8 5.4 %collective-permute-start.19 = (bf16[32,2048]{1,0:T(8,128)(2,1)S(1)}, bf16[32,2048]{1,0:T(8,128)(2,1)S(1)}, u32[]{:S(2)}, u32[]{:S(2)}) collective-permute-start(bf16[32,2048]{1,0:T(8,128)(2,1)S(1)} %slice.74), channel_id=1, source_target_pairs={{0,16},{8,72},{16,0},{24,88},{32,48},{40,104},{48,32},{56,120},{64... | collective-permute-start | bytes 393224 | tf_op jit(solution)/shard_map/ppermute | solution.py:450
  51.0 5.4 %collective-permute-start.21 = (bf16[32,2048]{1,0:T(8,128)(2,1)S(1)}, bf16[32,2048]{1,0:T(8,128)(2,1)S(1)}, u32[]{:S(2)}, u32[]{:S(2)}) collective-permute-start(bf16[32,2048]{1,0:T(8,128)(2,1)S(1)} %slice.75), channel_id=1, source_target_pairs={{0,48},{8,200},{16,32},{24,216},{32,16},{40,232},{48,0},{56,248},{... | collective-permute-start | bytes 393224 | tf_op jit(solution)/shard_map/ppermute | solution.py:450
  53.7 14.3 %collective-permute-start.12 = (bf16[32,2048]{1,0:T(8,128)(2,1)S(1)}, bf16[32,2048]{1,0:T(8,128)(2,1)S(1)}, u32[]{:S(2)}, u32[]{:S(2)}) collective-permute-start(bf16[32,2048]{1,0:T(8,128)(2,1)S(1)} %slice.68), channel_id=1, source_target_pairs={{0,16},{8,72},{16,0},{24,88},{32,48},{40,104},{48,32},{56,120},{64... | collective-permute-start | bytes 393224 | tf_op jit(solution)/shard_map/ppermute | solution.py:450
  53.8 14.2 %collective-permute-start.14 = (bf16[32,2048]{1,0:T(8,128)(2,1)S(1)}, bf16[32,2048]{1,0:T(8,128)(2,1)S(1)}, u32[]{:S(2)}, u32[]{:S(2)}) collective-permute-start(bf16[32,2048]{1,0:T(8,128)(2,1)S(1)} %slice.69), channel_id=1, source_target_pairs={{0,48},{8,200},{16,32},{24,216},{32,16},{40,232},{48,0},{56,248},{... | collective-permute-start | bytes 393224 | tf_op jit(solution)/shard_map/ppermute | solution.py:450
  57.3 14.4 %collective-permute-start.22 = (bf16[64,1024]{1,0:T(8,128)(2,1)S(1)}, bf16[64,1024]{1,0:T(8,128)(2,1)S(1)}, u32[]{:S(2)}, u32[]{:S(2)}) collective-permute-start(bf16[64,1024]{1,0:T(8,128)(2,1)S(1)} %get-tuple-element.52), channel_id=1, source_target_pairs={{0,1},{1,2},{2,3},{3,4},{4,5},{5,6},{6,7},{7,0},{8,9},{9,10},{10,1... | collective-permute-start | bytes 393224 | tf_op jit(solution)/shard_map/ppermute | solution.py:460
  59.0 12.6 %collective-permute-start.23 = (bf16[64,1024]{1,0:T(8,128)(2,1)S(1)}, bf16[64,1024]{1,0:T(8,128)(2,1)S(1)}, u32[]{:S(2)}, u32[]{:S(2)}) collective-permute-start(bf16[64,1024]{1,0:T(8,128)(2,1)S(1)} %get-tuple-element.53), channel_id=1, source_target_pairs={{0,7},{1,0},{2,1},{3,2},{4,3},{5,4},{6,5},{7,6},{8,15},{9,8},{10,9... | collective-permute-start | bytes 393224 | tf_op jit(solution)/shard_map/ppermute | solution.py:460
  63.0 12.3 %collective-permute-start.26 = (bf16[64,1024]{1,0:T(8,128)(2,1)S(1)}, bf16[64,1024]{1,0:T(8,128)(2,1)S(1)}, u32[]{:S(2)}, u32[]{:S(2)}) collective-permute-start(bf16[64,1024]{1,0:T(8,128)(2,1)S(1)} %get-tuple-element.56), channel_id=1, source_target_pairs={{0,4},{1,5},{2,6},{3,7},{4,0},{5,1},{6,2},{7,3},{8,12},{9,13},{10,... | collective-permute-start | bytes 393224 | tf_op jit(solution)/shard_map/ppermute | solution.py:460
  68.9 13.5 %collective-permute-start.16 = (bf16[64,1024]{1,0:T(8,128)(2,1)S(1)}, bf16[64,1024]{1,0:T(8,128)(2,1)S(1)}, u32[]{:S(2)}, u32[]{:S(2)}) collective-permute-start(bf16[64,1024]{1,0:T(8,128)(2,1)S(1)} %get-tuple-element.48), channel_id=1, source_target_pairs={{0,1},{1,2},{2,3},{3,4},{4,5},{5,6},{6,7},{7,0},{8,9},{9,10},{10,1... | collective-permute-start | bytes 393224 | tf_op jit(solution)/shard_map/ppermute | solution.py:460
  68.9 13.4 %collective-permute-start.17 = (bf16[64,1024]{1,0:T(8,128)(2,1)S(1)}, bf16[64,1024]{1,0:T(8,128)(2,1)S(1)}, u32[]{:S(2)}, u32[]{:S(2)}) collective-permute-start(bf16[64,1024]{1,0:T(8,128)(2,1)S(1)} %get-tuple-element.49), channel_id=1, source_target_pairs={{0,7},{1,0},{2,1},{3,2},{4,3},{5,4},{6,5},{7,6},{8,15},{9,8},{10,9... | collective-permute-start | bytes 393224 | tf_op jit(solution)/shard_map/ppermute | solution.py:460
  71.7 10.7 %collective-permute-start.24 = (bf16[64,1024]{1,0:T(8,128)(2,1)S(1)}, bf16[64,1024]{1,0:T(8,128)(2,1)S(1)}, u32[]{:S(2)}, u32[]{:S(2)}) collective-permute-start(bf16[64,1024]{1,0:T(8,128)(2,1)S(1)} %get-tuple-element.54), channel_id=1, source_target_pairs={{0,2},{1,3},{2,4},{3,5},{4,6},{5,7},{6,0},{7,1},{8,10},{9,11},{10,... | collective-permute-start | bytes 393224 | tf_op jit(solution)/shard_map/ppermute | solution.py:460
  71.8 10.6 %collective-permute-start.25 = (bf16[64,1024]{1,0:T(8,128)(2,1)S(1)}, bf16[64,1024]{1,0:T(8,128)(2,1)S(1)}, u32[]{:S(2)}, u32[]{:S(2)}) collective-permute-start(bf16[64,1024]{1,0:T(8,128)(2,1)S(1)} %get-tuple-element.55), channel_id=1, source_target_pairs={{0,6},{1,7},{2,0},{3,1},{4,2},{5,3},{6,4},{7,5},{8,14},{9,15},{10,... | collective-permute-start | bytes 393224 | tf_op jit(solution)/shard_map/ppermute | solution.py:460
  75.3 10.9 %collective-permute-start.28 = (bf16[4,16,128]{2,1,0:T(8,128)(2,1)S(1)}, bf16[4,16,128]{2,1,0:T(8,128)(2,1)S(1)}, u32[]{:S(2)}, u32[]{:S(2)}) collective-permute-start(bf16[4,16,128]{2,1,0:T(8,128)(2,1)S(1)} %pad_maximum_fusion.2), channel_id=1, source_target_pairs={{0,8},{8,0},{16,24},{24,16},{32,40},{40,32},{48,56},{56,48},{64,72... | collective-permute-start | bytes 49160 | tf_op jit(solution)/shard_map/ppermute | solution.py:433
  82.4 4.7 %collective-permute-start.27 = (bf16[64,512]{1,0:T(8,128)(2,1)S(1)}, bf16[64,512]{1,0:T(8,128)(2,1)S(1)}, u32[]{:S(2)}, u32[]{:S(2)}) collective-permute-start(bf16[64,512]{1,0:T(8,128)(2,1)S(1)} %get-tuple-element.58), channel_id=1, source_target_pairs={{0,8},{8,0},{16,24},{24,16},{32,40},{40,32},{48,56},{56,48},{64,72... | collective-permute-start | bytes 196616 | tf_op jit(solution)/shard_map/ppermute | solution.py:433

commit v10 on v9

--- a/solution.py
+++ b/solution.py
@@ -170,7 +170,7 @@
     )(place, *parts)
 
 
-ROWS = 128
+ROWS = 256
 
 
 def prefix_part(q, kv):
@@ -489,10 +489,13 @@
     pick = order_rows(place, orders)
 
     parts = [attended] + [turned(attended, k, 0) for k in (1, 2, 3)]
-    far, near = [gathered([a[i : i + 16] for a in parts]) for i in (0, 16)]
-    first_far, first_near = project(far[:3], weights), project(near[:3], weights)
+    far = gathered([a[:16] for a in parts])
+    first_far = project(far[:3], weights)
+    late, last_far = lax.optimization_barrier(([a[16:] for a in parts], far[3]))
+    near = gathered(late)
+    first_near = project(near[:3], weights)
     keep2, up3, down3, up4 = plain(
-        far_body, [SUM, SENT, SENT, SENT], *far[3], *weights, first_far
+        far_body, [SUM, SENT, SENT, SENT], *last_far, *weights, first_far
     )
     below3, above3 = along_z(up3, 1), along_z(down3, -1)
     opposite = along_z(up4, 4)

time: 88.2 us -> 93.8 us (1.063)
  waiting for transfers between devices: 14.8 us -> 19.6 us
  starting transfers between devices: 51.4 us -> 53.6 us
  Pallas kernels: 19.9 us -> 18.5 us
    ppermute x11, waiting for transfers between devices: 9.85 us -> 14.1 us  [turned(): return lax.ppermute(value, 'batch', pairs)]
    ppermute x11, starting transfers between devices: 24.6 us -> 26.1 us  [along(): lax.ppermute(value, 'batch', [(i, i ^ k << shift) for i in range(BATCH)])]
  transfers between devices with their start and end apart: 29 -> 29, of which waited for: 10 -> 11; matrix products, arithmetic and copies ran while one was open for 1% -> 1% of each run, Pallas kernels for 22% -> 19%
where the time goes in v10:
time: 93.8 us; the launch traced here: 93.7 us
  starting transfers between devices  53.6 us (57%)
  waiting for transfers between devices  19.6 us (21%)
  Pallas kernels  18.5 us (20%)
  local copies, waits for them, and re-layouts  1.64 us (2%)
    ppermute x11, starting transfers between devices, along(): lax.ppermute(value, 'batch', [(i, i ^ k << shift) for i in range(BATCH)])  26.1 us
    ppermute x7, starting transfers between devices, along_z(): lax.ppermute(value, 'head', [(i, (i + k) % HEADS) for i in range(HEADS)])  16 us
    ppermute x11, waiting for transfers between devices, turned(): return lax.ppermute(value, 'batch', pairs)  14.1 us
    ppermute x11, starting transfers between devices, turned(): return lax.ppermute(value, 'batch', pairs)  11.4 us
    ppermute x11, waiting for transfers between devices, along(): lax.ppermute(value, 'batch', [(i, i ^ k << shift) for i in range(BATCH)])  5.55 us
    pallas_call x1, Pallas kernels, local_parts(): pl.pallas_call(local_body, out_shape=[out] * 4, in_specs=[SMEM] + [HBM] *...  4.23 us
    pallas_call x2, Pallas kernels, prefix_keep(): pl.pallas_call(prefix_keep_body, out_shape=[out, out], in_specs=[VMEM] *...  3.67 us
    pallas_call x1, Pallas kernels, prefix_send(): pl.pallas_call(prefix_send_body, out_shape=jax.ShapeDtypeStruct((33, GROU...  3.38 us
  transfers between devices with their start and end apart: 29, of which 11 were waited for; matrix products, arithmetic and copies ran while one was open for 1% of the time, Pallas kernels for 19%

profile of v10, /device:TPU:1, one launch (start us, length us, event | category | flops | bytes accessed | tf_op | source)
XLA Modules:
  0.0 93.7 jit_solution(16957173168597517195)
XLA Ops:
  0.0 3.2 %collective-permute-start.4 = (bf16[2,2048,128]{2,1,0:T(8,128)(2,1)}, bf16[2,2048,128]{2,1,0:T(8,128)(2,1)S(1)}, u32[]{:S(2)}, u32[]{:S(2)}) collective-permute-start(bf16[2,2048,128]{2,1,0:T(8,128)(2,1)} %kv0.5), channel_id=1, source_target_pairs={{0,8},{8,0},{16,24},{24,16},{32,40},{40,32},{48,56},{56,48},{64,72... | collective-permute-start | bytes 3145736 | tf_op jit(solution)/shard_map/ppermute | solution.py:433
  3.2 0.6 stack.34.place
  3.8 4.2 %local_parts.1 = (bf16[18,16,128]{2,1,0:T(8,128)(2,1)}, bf16[18,16,128]{2,1,0:T(8,128)(2,1)}, bf16[18,16,128]{2,1,0:T(8,128)(2,1)}, bf16[18,16,128]{2,1,0:T(8,128)(2,1)}) custom-call(s32[7]{0:T(128)} %stack.34.place, bf16[32,2048]{1,0:T(8,128)(2,1)} %q_in.1, s32[32]{0:T(128)} %prompt_in.1, s32[8,32]{1,0:T(8,128)} %bitcast.8, s32[32]{0:T(128)} %length_in.1, ...), custom_call_target="tpu_custom_call" | custom-call | tf_op jit(solution)/shard_map/local_parts/pallas_call | solution.py:124
  8.1 0.1 collective-permute-start
  8.2 1.9 %collective-permute-start.1 = (bf16[18,16,128]{2,1,0:T(8,128)(2,1)}, bf16[18,16,128]{2,1,0:T(8,128)(2,1)S(1)}, u32[]{:S(2)}, u32[]{:S(2)}) collective-permute-start(bf16[18,16,128]{2,1,0:T(8,128)(2,1)} %get-tuple-element.40), channel_id=1, source_target_pairs={{0,128},{8,136},{16,144},{24,152},{32,160},{40,168},{48,176},{56,1... | collective-permute-start | bytes 221192 | tf_op jit(solution)/shard_map/ppermute | solution.py:433
  10.1 1.9 %collective-permute-start.2 = (bf16[18,16,128]{2,1,0:T(8,128)(2,1)}, bf16[18,16,128]{2,1,0:T(8,128)(2,1)S(1)}, u32[]{:S(2)}, u32[]{:S(2)}) collective-permute-start(bf16[18,16,128]{2,1,0:T(8,128)(2,1)} %get-tuple-element.41), channel_id=1, source_target_pairs={{0,192},{8,200},{16,208},{24,216},{32,224},{40,232},{48,240},{56,2... | collective-permute-start | bytes 221192 | tf_op jit(solution)/shard_map/ppermute | solution.py:433
  12.0 0.2 collective-permute-done.a1.s1
  12.3 2.0 %collective-permute-done.1.a2.s2 = bf16[18,16,128]{2,1,0:T(8,128)(2,1)S(1)} collective-permute-done((bf16[18,16,128]{2,1,0:T(8,128)(2,1)}, bf16[18,16,128]{2,1,0:T(8,128)(2,1)S(1)}, u32[]{:S(2)}, u32[]{:S(2)}) %collective-permute-start.1) | collective-permute-done | bytes 73760 | tf_op jit(solution)/shard_map/ppermute | solution.py:433
  14.3 1.4 %collective-permute-done.2.a3.s3 = bf16[18,16,128]{2,1,0:T(8,128)(2,1)S(1)} collective-permute-done((bf16[18,16,128]{2,1,0:T(8,128)(2,1)}, bf16[18,16,128]{2,1,0:T(8,128)(2,1)S(1)}, u32[]{:S(2)}, u32[]{:S(2)}) %collective-permute-start.2) | collective-permute-done | bytes 73760 | tf_op jit(solution)/shard_map/ppermute | solution.py:433
  15.8 0.9 copy-done.2
  16.6 0.6 regroup.1
  17.2 2.8 %collective-permute-start.3 = (bf16[37,16,128]{2,1,0:T(8,128)(2,1)S(1)}, bf16[37,16,128]{2,1,0:T(8,128)(2,1)S(1)}, u32[]{:S(2)}, u32[]{:S(2)}) collective-permute-start(bf16[37,16,128]{2,1,0:T(8,128)(2,1)S(1)} %get-tuple-element.42), channel_id=1, source_target_pairs={{0,48},{8,56},{16,32},{24,40},{32,16},{40,24},{48,0},{56,8},{64,11... | collective-permute-start | bytes 454664 | tf_op jit(solution)/shard_map/ppermute | solution.py:433
  20.0 0.0 collective-permute-start.5
  20.0 0.0 collective-permute-done.4.kv1
  20.0 1.8 %prefix_keep.2 = (f32[16,16,128]{2,1,0:T(8,128)S(1)}, f32[16,16,128]{2,1,0:T(8,128)S(1)}) custom-call(bf16[17,16,128]{2,1,0:T(8,128)(2,1)S(1)} %get-tuple-element.43.q, bf16[2,2048,128]{2,1,0:T(8,128)(2,1)S(1)} %copy-done.1, bf16[2,2048,128]{2,1,0:T(8,128)(2,1)S(1)} %collective-permute-done.4.kv1), custom_call_target="tpu_custom_call" | custom-call | flops 536870912 | bytes 2500000 | tf_op jit(solution)/shard_map/prefix_keep/pallas_call | solution.py:238
  21.9 0.0 copy-start
  21.9 1.2 %collective-permute-done.3.qb = bf16[37,16,128]{2,1,0:T(8,128)(2,1)S(1)} collective-permute-done((bf16[37,16,128]{2,1,0:T(8,128)(2,1)S(1)}, bf16[37,16,128]{2,1,0:T(8,128)(2,1)S(1)}, u32[]{:S(2)}, u32[]{:S(2)}) %collective-permute-start.3) | collective-permute-done | bytes 151584 | tf_op jit(solution)/shard_map/ppermute | solution.py:433
  23.2 0.3 collective-permute-start.6
  23.5 0.0 collective-permute-done.5.qa
  23.5 3.4 %prefix_send.1 = bf16[33,16,128]{2,1,0:T(8,128)(2,1)S(1)} custom-call(bf16[17,16,128]{2,1,0:T(8,128)(2,1)S(1)} %collective-permute-done.5.qa, bf16[37,16,128]{2,1,0:T(8,128)(2,1)S(1)} %collective-permute-done.3.qb, bf16[2,2048,128]{2,1,0:T(8,128)(2,1)S(1)} %copy-done.1, bf16[2,2048,128]{2,1,0:T(8,128)(2,1)S(1)} %collective-permute-done.4.kv1, ...), custom_call_target="tpu_custom_call" | custom-call | flops 1073741824 | bytes 2500000 | tf_op jit(solution)/shard_map/prefix_send/pallas_call | solution.py:225
  26.9 0.0 copy-start.3
  26.9 0.3 collective-permute-done.6.q.far
  27.2 0.9 collective-permute-start.7
  28.1 2.3 %collective-permute-start.19 = (bf16[2048,512]{1,0:T(8,128)(2,1)S(1)}, bf16[2048,512]{1,0:T(8,128)(2,1)S(1)}, u32[]{:S(2)}, u32[]{:S(2)}) collective-permute-start(bf16[2048,512]{1,0:T(8,128)(2,1)S(1)} %copy-done), channel_id=1, source_target_pairs={{0,8},{8,0},{16,24},{24,16},{32,40},{40,32},{48,56},{56,48},{64,72... | collective-permute-start | bytes 6291464 | tf_op jit(solution)/shard_map/ppermute | solution.py:433
  30.4 1.8 %prefix_keep.3 = (f32[16,16,128]{2,1,0:T(8,128)S(1)}, f32[16,16,128]{2,1,0:T(8,128)S(1)}) custom-call(bf16[37,16,128]{2,1,0:T(8,128)(2,1)S(1)} %collective-permute-done.6.q.far, bf16[2,2048,128]{2,1,0:T(8,128)(2,1)S(1)} %copy-done.1, bf16[2,2048,128]{2,1,0:T(8,128)(2,1)S(1)} %collective-permute-done.4.kv1), custom_call_target="tpu_custom_call" | custom-call | flops 536870912 | bytes 2500000 | tf_op jit(solution)/shard_map/prefix_keep/pallas_call | solution.py:238
  32.3 1.2 %combine.1 = bf16[32,2048]{1,0:T(8,128)(2,1)S(1)} custom-call(s32[7]{0:T(128)S(1)} %copy-done.4, f32[16,16,128]{2,1,0:T(8,128)S(1)} %get-tuple-element.46.own, f32[16,16,128]{2,1,0:T(8,128)S(1)} %get-tuple-element.47.after.own_masses, f32[16,16,128]{2,1,0:T(8,128)S(1)} %get-tuple-element.50.cross, f32[16,16,128]{2,1,0:T(8,128)S(1)} %get-tuple-element.51.cross_masses, ...), custom_call_target="tpu_custom_call" | custom-call | tf_op jit(solution)/shard_map/combine/pallas_call | solution.py:281
  33.5 1.5 %collective-permute-start.8 = (bf16[32,2048]{1,0:T(8,128)(2,1)S(1)}, bf16[32,2048]{1,0:T(8,128)(2,1)S(1)}, u32[]{:S(2)}, u32[]{:S(2)}) collective-permute-start(bf16[32,2048]{1,0:T(8,128)(2,1)S(1)} %combine.1), channel_id=1, source_target_pairs={{0,64},{8,24},{16,80},{24,8},{32,96},{40,56},{48,112},{56,40},{64,... | collective-permute-start | bytes 393224 | tf_op jit(solution)/shard_map/ppermute | solution.py:450
  35.0 2.5 %collective-permute-start.9 = (bf16[32,2048]{1,0:T(8,128)(2,1)S(1)}, bf16[32,2048]{1,0:T(8,128)(2,1)S(1)}, u32[]{:S(2)}, u32[]{:S(2)}) collective-permute-start(bf16[32,2048]{1,0:T(8,128)(2,1)S(1)} %combine.1), channel_id=1, source_target_pairs={{0,128},{8,40},{16,144},{24,56},{32,160},{40,8},{48,176},{56,24},{... | collective-permute-start | bytes 393224 | tf_op jit(solution)/shard_map/ppermute | solution.py:450
  37.5 0.2 collective-permute-start.10
  37.7 3.5 %collective-permute-done.9 = bf16[32,2048]{1,0:T(8,128)(2,1)S(1)} collective-permute-done((bf16[32,2048]{1,0:T(8,128)(2,1)S(1)}, bf16[32,2048]{1,0:T(8,128)(2,1)S(1)}, u32[]{:S(2)}, u32[]{:S(2)}) %collective-permute-start.9) | collective-permute-done | bytes 131104 | tf_op jit(solution)/shard_map/ppermute | solution.py:450
  41.2 1.7 %collective-permute-done.10 = bf16[32,2048]{1,0:T(8,128)(2,1)S(1)} collective-permute-done((bf16[32,2048]{1,0:T(8,128)(2,1)S(1)}, bf16[32,2048]{1,0:T(8,128)(2,1)S(1)}, u32[]{:S(2)}, u32[]{:S(2)}) %collective-permute-start.10) | collective-permute-done | bytes 131104 | tf_op jit(solution)/shard_map/ppermute | solution.py:450
  43.0 1.3 %collective-permute-start.11 = (bf16[64,2048]{1,0:T(8,128)(2,1)S(1)}, bf16[64,2048]{1,0:T(8,128)(2,1)S(1)}, u32[]{:S(2)}, u32[]{:S(2)}) collective-permute-start(bf16[64,2048]{1,0:T(8,128)(2,1)S(1)} %pad_maximum_fusion.a), channel_id=1, source_target_pairs={{0,48},{8,200},{16,32},{24,216},{32,16},{40,232},{48,0},{56,248},{... | collective-permute-start | bytes 786440 | tf_op jit(solution)/shard_map/ppermute | solution.py:450
  44.3 5.2 %collective-permute-done.11.c = bf16[64,2048]{1,0:T(8,128)(2,1)S(1)} collective-permute-done((bf16[64,2048]{1,0:T(8,128)(2,1)S(1)}, bf16[64,2048]{1,0:T(8,128)(2,1)S(1)}, u32[]{:S(2)}, u32[]{:S(2)}) %collective-permute-start.11) | collective-permute-done | bytes 262176 | tf_op jit(solution)/shard_map/ppermute | solution.py:450
  49.5 0.1 collective-permute-start.12
  49.6 1.4 %collective-permute-start.14 = (bf16[32,2048]{1,0:T(8,128)(2,1)S(1)}, bf16[32,2048]{1,0:T(8,128)(2,1)S(1)}, u32[]{:S(2)}, u32[]{:S(2)}) collective-permute-start(bf16[32,2048]{1,0:T(8,128)(2,1)S(1)} %slice.73), channel_id=1, source_target_pairs={{0,48},{8,200},{16,32},{24,216},{32,16},{40,232},{48,0},{56,248},{... | collective-permute-start | bytes 393224 | tf_op jit(solution)/shard_map/ppermute | solution.py:450
  51.0 2.6 %collective-permute-done.12.a = bf16[32,2048]{1,0:T(8,128)(2,1)S(1)} collective-permute-done((bf16[32,2048]{1,0:T(8,128)(2,1)S(1)}, bf16[32,2048]{1,0:T(8,128)(2,1)S(1)}, u32[]{:S(2)}, u32[]{:S(2)}) %collective-permute-start.12) | collective-permute-done | bytes 131104 | tf_op jit(solution)/shard_map/ppermute | solution.py:450
  53.7 1.0 %collective-permute-done.14.b = bf16[32,2048]{1,0:T(8,128)(2,1)S(1)} collective-permute-done((bf16[32,2048]{1,0:T(8,128)(2,1)S(1)}, bf16[32,2048]{1,0:T(8,128)(2,1)S(1)}, u32[]{:S(2)}, u32[]{:S(2)}) %collective-permute-start.14) | collective-permute-done | bytes 131104 | tf_op jit(solution)/shard_map/ppermute | solution.py:450
  54.8 1.4 %collective-permute-start.15 = (bf16[64,2048]{1,0:T(8,128)(2,1)S(1)}, bf16[64,2048]{1,0:T(8,128)(2,1)S(1)}, u32[]{:S(2)}, u32[]{:S(2)}) collective-permute-start(bf16[64,2048]{1,0:T(8,128)(2,1)S(1)} %constant_dynamic-update-slice_fusion.a), channel_id=1, source_target_pairs={{0,48},{8,200},{16,32},{24,216},{32,16},{40,232},{48,0},{56,248},{... | collective-permute-start | bytes 786440 | tf_op jit(solution)/shard_map/ppermute | solution.py:450
  56.2 1.0 %project.3.first = f32[4,48,1024]{2,1,0:T(8,128)S(1)} custom-call(bf16[64,2048]{1,0:T(8,128)(2,1)S(1)} %pad_maximum_fusion.a, bf16[64,2048]{1,0:T(8,128)(2,1)S(1)} %collective-permute-done.13.b, bf16[64,2048]{1,0:T(8,128)(2,1)S(1)} %collective-permute-done.11.c, bf16[2048,512]{1,0:T(8,128)(2,1)S(1)} %copy-done, bf16[2048,512]{1,0:T(8,128)(2,1)S(1)} %collective-permute-done.19.w1), custom_call_target="tpu_custom_call" | custom-call | flops 805306368 | bytes 4500000 | tf_op jit(solution)/shard_map/project/pallas_call | solution.py:316
  57.2 0.9 far.1
  58.1 1.7 %collective-permute-start.22 = (bf16[64,1024]{1,0:T(8,128)(2,1)S(1)}, bf16[64,1024]{1,0:T(8,128)(2,1)S(1)}, u32[]{:S(2)}, u32[]{:S(2)}) collective-permute-start(bf16[64,1024]{1,0:T(8,128)(2,1)S(1)} %get-tuple-element.64), channel_id=1, source_target_pairs={{0,1},{1,2},{2,3},{3,4},{4,5},{5,6},{6,7},{7,0},{8,9},{9,10},{10,1... | collective-permute-start | bytes 393224 | tf_op jit(solution)/shard_map/ppermute | solution.py:460
  59.8 4.0 %collective-permute-start.23 = (bf16[64,1024]{1,0:T(8,128)(2,1)S(1)}, bf16[64,1024]{1,0:T(8,128)(2,1)S(1)}, u32[]{:S(2)}, u32[]{:S(2)}) collective-permute-start(bf16[64,1024]{1,0:T(8,128)(2,1)S(1)} %get-tuple-element.65), channel_id=1, source_target_pairs={{0,7},{1,0},{2,1},{3,2},{4,3},{5,4},{6,5},{7,6},{8,15},{9,8},{10,9... | collective-permute-start | bytes 393224 | tf_op jit(solution)/shard_map/ppermute | solution.py:460
  63.9 0.0 collective-permute-done.15.c
  63.9 1.5 %collective-permute-start.16 = (bf16[32,2048]{1,0:T(8,128)(2,1)S(1)}, bf16[32,2048]{1,0:T(8,128)(2,1)S(1)}, u32[]{:S(2)}, u32[]{:S(2)}) collective-permute-start(bf16[32,2048]{1,0:T(8,128)(2,1)S(1)} %slice.74), channel_id=1, source_target_pairs={{0,16},{8,72},{16,0},{24,88},{32,48},{40,104},{48,32},{56,120},{64... | collective-permute-start | bytes 393224 | tf_op jit(solution)/shard_map/ppermute | solution.py:450
  65.4 0.0 collective-permute-done.17.b
  65.4 1.4 %collective-permute-start.18 = (bf16[32,2048]{1,0:T(8,128)(2,1)S(1)}, bf16[32,2048]{1,0:T(8,128)(2,1)S(1)}, u32[]{:S(2)}, u32[]{:S(2)}) collective-permute-start(bf16[32,2048]{1,0:T(8,128)(2,1)S(1)} %slice.75), channel_id=1, source_target_pairs={{0,48},{8,200},{16,32},{24,216},{32,16},{40,232},{48,0},{56,248},{... | collective-permute-start | bytes 393224 | tf_op jit(solution)/shard_map/ppermute | solution.py:450
  66.9 4.0 %collective-permute-start.26 = (bf16[64,1024]{1,0:T(8,128)(2,1)S(1)}, bf16[64,1024]{1,0:T(8,128)(2,1)S(1)}, u32[]{:S(2)}, u32[]{:S(2)}) collective-permute-start(bf16[64,1024]{1,0:T(8,128)(2,1)S(1)} %get-tuple-element.68), channel_id=1, source_target_pairs={{0,4},{1,5},{2,6},{3,7},{4,0},{5,1},{6,2},{7,3},{8,12},{9,13},{10,... | collective-permute-start | bytes 393224 | tf_op jit(solution)/shard_map/ppermute | solution.py:460
  70.8 1.0 %project.2.first = f32[4,48,1024]{2,1,0:T(8,128)S(1)} custom-call(bf16[64,2048]{1,0:T(8,128)(2,1)S(1)} %constant_dynamic-update-slice_fusion.a, bf16[64,2048]{1,0:T(8,128)(2,1)S(1)} %collective-permute-done.17.b, bf16[64,2048]{1,0:T(8,128)(2,1)S(1)} %collective-permute-done.15.c, bf16[2048,512]{1,0:T(8,128)(2,1)S(1)} %copy-done, ...), custom_call_target="tpu_custom_call" | custom-call | flops 805306368 | bytes 4500000 | tf_op jit(solution)/shard_map/project/pallas_call | solution.py:316
  71.9 0.0 collective-permute-done.16.a
  71.9 0.0 collective-permute-done.18.b
  71.9 0.9 near.1
  72.8 0.1 middle.1
  72.8 0.2 collective-permute-start.24
  73.0 3.4 %collective-permute-start.25 = (bf16[64,1024]{1,0:T(8,128)(2,1)S(1)}, bf16[64,1024]{1,0:T(8,128)(2,1)S(1)}, u32[]{:S(2)}, u32[]{:S(2)}) collective-permute-start(bf16[64,1024]{1,0:T(8,128)(2,1)S(1)} %get-tuple-element.67), channel_id=1, source_target_pairs={{0,6},{1,7},{2,0},{3,1},{4,2},{5,3},{6,4},{7,5},{8,14},{9,15},{10,... | collective-permute-start | bytes 393224 | tf_op jit(solution)/shard_map/ppermute | solution.py:460
  76.5 0.0 collective-permute-start.20
  76.5 2.7 %collective-permute-start.21 = (bf16[64,1024]{1,0:T(8,128)(2,1)S(1)}, bf16[64,1024]{1,0:T(8,128)(2,1)S(1)}, u32[]{:S(2)}, u32[]{:S(2)}) collective-permute-start(bf16[64,1024]{1,0:T(8,128)(2,1)S(1)} %get-tuple-element.59), channel_id=1, source_target_pairs={{0,7},{1,0},{2,1},{3,2},{4,3},{5,4},{6,5},{7,6},{8,15},{9,8},{10,9... | collective-permute-start | bytes 393224 | tf_op jit(solution)/shard_map/ppermute | solution.py:460
  79.2 0.0 collective-permute-done.26.opposite
  79.2 9.7 %collective-permute-start.28 = (bf16[4,16,128]{2,1,0:T(8,128)(2,1)S(1)}, bf16[4,16,128]{2,1,0:T(8,128)(2,1)S(1)}, u32[]{:S(2)}, u32[]{:S(2)}) collective-permute-start(bf16[4,16,128]{2,1,0:T(8,128)(2,1)S(1)} %pad_maximum_fusion.1), channel_id=1, source_target_pairs={{0,8},{8,0},{16,24},{24,16},{32,40},{40,32},{48,56},{56,48},{64,72... | collective-permute-start | bytes 49160 | tf_op jit(solution)/shard_map/ppermute | solution.py:433
  88.9 0.0 collective-permute-done.25.above2
  88.9 0.1 total.1
  89.0 2.9 %collective-permute-start.27 = (bf16[64,512]{1,0:T(8,128)(2,1)S(1)}, bf16[64,512]{1,0:T(8,128)(2,1)S(1)}, u32[]{:S(2)}, u32[]{:S(2)}) collective-permute-start(bf16[64,512]{1,0:T(8,128)(2,1)S(1)} %get-tuple-element.70), channel_id=1, source_target_pairs={{0,8},{8,0},{16,24},{24,16},{32,40},{40,32},{48,56},{56,48},{64,72... | collective-permute-start | bytes 196616 | tf_op jit(solution)/shard_map/ppermute | solution.py:433
  91.9 0.6 order_rows.1.pick
  92.5 0.2 collective-permute-done.27.other
  92.8 0.9 finish.1
  (38 shorter events, 0.2 us)
Async XLA Ops:
  0.0 20.0 %copy-start.1 = (bf16[2,2048,128]{2,1,0:T(8,128)(2,1)S(1)}, bf16[2,2048,128]{2,1,0:T(8,128)(2,1)}, u32[]{:S(2)}) copy-start(bf16[2,2048,128]{2,1,0:T(8,128)(2,1)} %kv0.5) | copy-start | bytes 3145732
  0.0 20.0 %collective-permute-start.4 = (bf16[2,2048,128]{2,1,0:T(8,128)(2,1)}, bf16[2,2048,128]{2,1,0:T(8,128)(2,1)S(1)}, u32[]{:S(2)}, u32[]{:S(2)}) collective-permute-start(bf16[2,2048,128]{2,1,0:T(8,128)(2,1)} %kv0.5), channel_id=1, source_target_pairs={{0,8},{8,0},{16,24},{24,16},{32,40},{40,32},{48,56},{56,48},{64,72... | collective-permute-start | bytes 3145736 | tf_op jit(solution)/shard_map/ppermute | solution.py:433
  3.8 11.9 %copy-start.4 = (s32[7]{0:T(128)S(1)}, s32[7]{0:T(128)}, u32[]{:S(2)}) copy-start(s32[7]{0:T(128)} %stack.34.place) | copy-start | bytes 88
  8.1 4.2 %collective-permute-start = (bf16[18,16,128]{2,1,0:T(8,128)(2,1)}, bf16[18,16,128]{2,1,0:T(8,128)(2,1)S(1)}, u32[]{:S(2)}, u32[]{:S(2)}) collective-permute-start(bf16[18,16,128]{2,1,0:T(8,128)(2,1)} %get-tuple-element.39), channel_id=1, source_target_pairs={{0,64},{8,72},{16,80},{24,88},{32,96},{40,104},{48,112},{56,120},{... | collective-permute-start | bytes 221192 | tf_op jit(solution)/shard_map/ppermute | solution.py:433
  8.2 6.1 %collective-permute-start.1 = (bf16[18,16,128]{2,1,0:T(8,128)(2,1)}, bf16[18,16,128]{2,1,0:T(8,128)(2,1)S(1)}, u32[]{:S(2)}, u32[]{:S(2)}) collective-permute-start(bf16[18,16,128]{2,1,0:T(8,128)(2,1)} %get-tuple-element.40), channel_id=1, source_target_pairs={{0,128},{8,136},{16,144},{24,152},{32,160},{40,168},{48,176},{56,1... | collective-permute-start | bytes 221192 | tf_op jit(solution)/shard_map/ppermute | solution.py:433
  10.1 5.6 %collective-permute-start.2 = (bf16[18,16,128]{2,1,0:T(8,128)(2,1)}, bf16[18,16,128]{2,1,0:T(8,128)(2,1)S(1)}, u32[]{:S(2)}, u32[]{:S(2)}) collective-permute-start(bf16[18,16,128]{2,1,0:T(8,128)(2,1)} %get-tuple-element.41), channel_id=1, source_target_pairs={{0,192},{8,200},{16,208},{24,216},{32,224},{40,232},{48,240},{56,2... | collective-permute-start | bytes 221192 | tf_op jit(solution)/shard_map/ppermute | solution.py:433
  15.8 0.9 copy-start.2
  17.2 5.9 %collective-permute-start.3 = (bf16[37,16,128]{2,1,0:T(8,128)(2,1)S(1)}, bf16[37,16,128]{2,1,0:T(8,128)(2,1)S(1)}, u32[]{:S(2)}, u32[]{:S(2)}) collective-permute-start(bf16[37,16,128]{2,1,0:T(8,128)(2,1)S(1)} %get-tuple-element.42), channel_id=1, source_target_pairs={{0,48},{8,56},{16,32},{24,40},{32,16},{40,24},{48,0},{56,8},{64,11... | collective-permute-start | bytes 454664 | tf_op jit(solution)/shard_map/ppermute | solution.py:433
  20.0 3.5 %collective-permute-start.5 = (bf16[17,16,128]{2,1,0:T(8,128)(2,1)S(1)}, bf16[17,16,128]{2,1,0:T(8,128)(2,1)S(1)}, u32[]{:S(2)}, u32[]{:S(2)}) collective-permute-start(bf16[17,16,128]{2,1,0:T(8,128)(2,1)S(1)} %get-tuple-element.43.q), channel_id=1, source_target_pairs={{0,16},{8,24},{16,0},{24,8},{32,48},{40,56},{48,32},{56,40},{64,80... | collective-permute-start | bytes 208904 | tf_op jit(solution)/shard_map/ppermute | solution.py:433
  21.9 6.2 %copy-start = (bf16[2048,512]{1,0:T(8,128)(2,1)S(1)}, bf16[2048,512]{1,0:T(8,128)(2,1)}, u32[]{:S(2)}) copy-start(bf16[2048,512]{1,0:T(8,128)(2,1)} %w0.7) | copy-start | bytes 6291460
  23.2 4.0 %collective-permute-start.6 = (bf16[37,16,128]{2,1,0:T(8,128)(2,1)S(1)}, bf16[37,16,128]{2,1,0:T(8,128)(2,1)S(1)}, u32[]{:S(2)}, u32[]{:S(2)}) collective-permute-start(bf16[37,16,128]{2,1,0:T(8,128)(2,1)S(1)} %collective-permute-done.3.qb), channel_id=1, source_target_pairs={{0,16},{8,24},{16,0},{24,8},{32,48},{40,56},{48,32},{56,40},{64,80... | collective-permute-start | bytes 454664 | tf_op jit(solution)/shard_map/ppermute | solution.py:433
  26.9 5.4 %copy-start.3 = (bf16[18,16,128]{2,1,0:T(8,128)(2,1)S(1)}, bf16[18,16,128]{2,1,0:T(8,128)(2,1)}, u32[]{:S(2)}) copy-start(bf16[18,16,128]{2,1,0:T(8,128)(2,1)} %get-tuple-element.38.a0.s0) | copy-start | bytes 221188
  27.2 5.1 %collective-permute-start.7 = (bf16[33,16,128]{2,1,0:T(8,128)(2,1)S(1)}, bf16[33,16,128]{2,1,0:T(8,128)(2,1)S(1)}, u32[]{:S(2)}, u32[]{:S(2)}) collective-permute-start(bf16[33,16,128]{2,1,0:T(8,128)(2,1)S(1)} %prefix_send.1), channel_id=1, source_target_pairs={{0,16},{8,24},{16,0},{24,8},{32,48},{40,56},{48,32},{56,40},{64,80... | collective-permute-start | bytes 405512 | tf_op jit(solution)/shard_map/ppermute | solution.py:433
  28.1 28.1 %collective-permute-start.19 = (bf16[2048,512]{1,0:T(8,128)(2,1)S(1)}, bf16[2048,512]{1,0:T(8,128)(2,1)S(1)}, u32[]{:S(2)}, u32[]{:S(2)}) collective-permute-start(bf16[2048,512]{1,0:T(8,128)(2,1)S(1)} %copy-done), channel_id=1, source_target_pairs={{0,8},{8,0},{16,24},{24,16},{32,40},{40,32},{48,56},{56,48},{64,72... | collective-permute-start | bytes 6291464 | tf_op jit(solution)/shard_map/ppermute | solution.py:433
  33.5 4.2 %collective-permute-start.8 = (bf16[32,2048]{1,0:T(8,128)(2,1)S(1)}, bf16[32,2048]{1,0:T(8,128)(2,1)S(1)}, u32[]{:S(2)}, u32[]{:S(2)}) collective-permute-start(bf16[32,2048]{1,0:T(8,128)(2,1)S(1)} %combine.1), channel_id=1, source_target_pairs={{0,64},{8,24},{16,80},{24,8},{32,96},{40,56},{48,112},{56,40},{64,... | collective-permute-start | bytes 393224 | tf_op jit(solution)/shard_map/ppermute | solution.py:450
  35.0 6.2 %collective-permute-start.9 = (bf16[32,2048]{1,0:T(8,128)(2,1)S(1)}, bf16[32,2048]{1,0:T(8,128)(2,1)S(1)}, u32[]{:S(2)}, u32[]{:S(2)}) collective-permute-start(bf16[32,2048]{1,0:T(8,128)(2,1)S(1)} %combine.1), channel_id=1, source_target_pairs={{0,128},{8,40},{16,144},{24,56},{32,160},{40,8},{48,176},{56,24},{... | collective-permute-start | bytes 393224 | tf_op jit(solution)/shard_map/ppermute | solution.py:450
  37.5 5.4 %collective-permute-start.10 = (bf16[32,2048]{1,0:T(8,128)(2,1)S(1)}, bf16[32,2048]{1,0:T(8,128)(2,1)S(1)}, u32[]{:S(2)}, u32[]{:S(2)}) collective-permute-start(bf16[32,2048]{1,0:T(8,128)(2,1)S(1)} %combine.1), channel_id=1, source_target_pairs={{0,192},{8,56},{16,208},{24,40},{32,224},{40,24},{48,240},{56,8},{... | collective-permute-start | bytes 393224 | tf_op jit(solution)/shard_map/ppermute | solution.py:450
  43.0 6.5 %collective-permute-start.11 = (bf16[64,2048]{1,0:T(8,128)(2,1)S(1)}, bf16[64,2048]{1,0:T(8,128)(2,1)S(1)}, u32[]{:S(2)}, u32[]{:S(2)}) collective-permute-start(bf16[64,2048]{1,0:T(8,128)(2,1)S(1)} %pad_maximum_fusion.a), channel_id=1, source_target_pairs={{0,48},{8,200},{16,32},{24,216},{32,16},{40,232},{48,0},{56,248},{... | collective-permute-start | bytes 786440 | tf_op jit(solution)/shard_map/ppermute | solution.py:450
  44.2 5.3 %collective-permute-start.13 = (bf16[64,2048]{1,0:T(8,128)(2,1)S(1)}, bf16[64,2048]{1,0:T(8,128)(2,1)S(1)}, u32[]{:S(2)}, u32[]{:S(2)}) collective-permute-start(bf16[64,2048]{1,0:T(8,128)(2,1)S(1)} %pad_maximum_fusion.a), channel_id=1, source_target_pairs={{0,16},{8,72},{16,0},{24,88},{32,48},{40,104},{48,32},{56,120},{64... | collective-permute-start | bytes 786440 | tf_op jit(solution)/shard_map/ppermute | solution.py:450
  49.5 4.2 %collective-permute-start.12 = (bf16[32,2048]{1,0:T(8,128)(2,1)S(1)}, bf16[32,2048]{1,0:T(8,128)(2,1)S(1)}, u32[]{:S(2)}, u32[]{:S(2)}) collective-permute-start(bf16[32,2048]{1,0:T(8,128)(2,1)S(1)} %slice.72), channel_id=1, source_target_pairs={{0,16},{8,72},{16,0},{24,88},{32,48},{40,104},{48,32},{56,120},{64... | collective-permute-start | bytes 393224 | tf_op jit(solution)/shard_map/ppermute | solution.py:450
  49.6 5.1 %collective-permute-start.14 = (bf16[32,2048]{1,0:T(8,128)(2,1)S(1)}, bf16[32,2048]{1,0:T(8,128)(2,1)S(1)}, u32[]{:S(2)}, u32[]{:S(2)}) collective-permute-start(bf16[32,2048]{1,0:T(8,128)(2,1)S(1)} %slice.73), channel_id=1, source_target_pairs={{0,48},{8,200},{16,32},{24,216},{32,16},{40,232},{48,0},{56,248},{... | collective-permute-start | bytes 393224 | tf_op jit(solution)/shard_map/ppermute | solution.py:450
  54.8 9.1 %collective-permute-start.15 = (bf16[64,2048]{1,0:T(8,128)(2,1)S(1)}, bf16[64,2048]{1,0:T(8,128)(2,1)S(1)}, u32[]{:S(2)}, u32[]{:S(2)}) collective-permute-start(bf16[64,2048]{1,0:T(8,128)(2,1)S(1)} %constant_dynamic-update-slice_fusion.a), channel_id=1, source_target_pairs={{0,48},{8,200},{16,32},{24,216},{32,16},{40,232},{48,0},{56,248},{... | collective-permute-start | bytes 786440 | tf_op jit(solution)/shard_map/ppermute | solution.py:450
  56.2 9.2 %collective-permute-start.17 = (bf16[64,2048]{1,0:T(8,128)(2,1)S(1)}, bf16[64,2048]{1,0:T(8,128)(2,1)S(1)}, u32[]{:S(2)}, u32[]{:S(2)}) collective-permute-start(bf16[64,2048]{1,0:T(8,128)(2,1)S(1)} %constant_dynamic-update-slice_fusion.a), channel_id=1, source_target_pairs={{0,16},{8,72},{16,0},{24,88},{32,48},{40,104},{48,32},{56,120},{64... | collective-permute-start | bytes 786440 | tf_op jit(solution)/shard_map/ppermute | solution.py:450
  58.1 14.6 %collective-permute-start.22 = (bf16[64,1024]{1,0:T(8,128)(2,1)S(1)}, bf16[64,1024]{1,0:T(8,128)(2,1)S(1)}, u32[]{:S(2)}, u32[]{:S(2)}) collective-permute-start(bf16[64,1024]{1,0:T(8,128)(2,1)S(1)} %get-tuple-element.64), channel_id=1, source_target_pairs={{0,1},{1,2},{2,3},{3,4},{4,5},{5,6},{6,7},{7,0},{8,9},{9,10},{10,1... | collective-permute-start | bytes 393224 | tf_op jit(solution)/shard_map/ppermute | solution.py:460
  59.8 12.9 %collective-permute-start.23 = (bf16[64,1024]{1,0:T(8,128)(2,1)S(1)}, bf16[64,1024]{1,0:T(8,128)(2,1)S(1)}, u32[]{:S(2)}, u32[]{:S(2)}) collective-permute-start(bf16[64,1024]{1,0:T(8,128)(2,1)S(1)} %get-tuple-element.65), channel_id=1, source_target_pairs={{0,7},{1,0},{2,1},{3,2},{4,3},{5,4},{6,5},{7,6},{8,15},{9,8},{10,9... | collective-permute-start | bytes 393224 | tf_op jit(solution)/shard_map/ppermute | solution.py:460
  63.9 8.0 %collective-permute-start.16 = (bf16[32,2048]{1,0:T(8,128)(2,1)S(1)}, bf16[32,2048]{1,0:T(8,128)(2,1)S(1)}, u32[]{:S(2)}, u32[]{:S(2)}) collective-permute-start(bf16[32,2048]{1,0:T(8,128)(2,1)S(1)} %slice.74), channel_id=1, source_target_pairs={{0,16},{8,72},{16,0},{24,88},{32,48},{40,104},{48,32},{56,120},{64... | collective-permute-start | bytes 393224 | tf_op jit(solution)/shard_map/ppermute | solution.py:450
  65.4 6.4 %collective-permute-start.18 = (bf16[32,2048]{1,0:T(8,128)(2,1)S(1)}, bf16[32,2048]{1,0:T(8,128)(2,1)S(1)}, u32[]{:S(2)}, u32[]{:S(2)}) collective-permute-start(bf16[32,2048]{1,0:T(8,128)(2,1)S(1)} %slice.75), channel_id=1, source_target_pairs={{0,48},{8,200},{16,32},{24,216},{32,16},{40,232},{48,0},{56,248},{... | collective-permute-start | bytes 393224 | tf_op jit(solution)/shard_map/ppermute | solution.py:450
  66.9 12.3 %collective-permute-start.26 = (bf16[64,1024]{1,0:T(8,128)(2,1)S(1)}, bf16[64,1024]{1,0:T(8,128)(2,1)S(1)}, u32[]{:S(2)}, u32[]{:S(2)}) collective-permute-start(bf16[64,1024]{1,0:T(8,128)(2,1)S(1)} %get-tuple-element.68), channel_id=1, source_target_pairs={{0,4},{1,5},{2,6},{3,7},{4,0},{5,1},{6,2},{7,3},{8,12},{9,13},{10,... | collective-permute-start | bytes 393224 | tf_op jit(solution)/shard_map/ppermute | solution.py:460
  72.8 16.0 %collective-permute-start.24 = (bf16[64,1024]{1,0:T(8,128)(2,1)S(1)}, bf16[64,1024]{1,0:T(8,128)(2,1)S(1)}, u32[]{:S(2)}, u32[]{:S(2)}) collective-permute-start(bf16[64,1024]{1,0:T(8,128)(2,1)S(1)} %get-tuple-element.66), channel_id=1, source_target_pairs={{0,2},{1,3},{2,4},{3,5},{4,6},{5,7},{6,0},{7,1},{8,10},{9,11},{10,... | collective-permute-start | bytes 393224 | tf_op jit(solution)/shard_map/ppermute | solution.py:460
  73.0 15.8 %collective-permute-start.25 = (bf16[64,1024]{1,0:T(8,128)(2,1)S(1)}, bf16[64,1024]{1,0:T(8,128)(2,1)S(1)}, u32[]{:S(2)}, u32[]{:S(2)}) collective-permute-start(bf16[64,1024]{1,0:T(8,128)(2,1)S(1)} %get-tuple-element.67), channel_id=1, source_target_pairs={{0,6},{1,7},{2,0},{3,1},{4,2},{5,3},{6,4},{7,5},{8,14},{9,15},{10,... | collective-permute-start | bytes 393224 | tf_op jit(solution)/shard_map/ppermute | solution.py:460
  76.5 12.4 %collective-permute-start.20 = (bf16[64,1024]{1,0:T(8,128)(2,1)S(1)}, bf16[64,1024]{1,0:T(8,128)(2,1)S(1)}, u32[]{:S(2)}, u32[]{:S(2)}) collective-permute-start(bf16[64,1024]{1,0:T(8,128)(2,1)S(1)} %get-tuple-element.58), channel_id=1, source_target_pairs={{0,1},{1,2},{2,3},{3,4},{4,5},{5,6},{6,7},{7,0},{8,9},{9,10},{10,1... | collective-permute-start | bytes 393224 | tf_op jit(solution)/shard_map/ppermute | solution.py:460
  76.5 12.4 %collective-permute-start.21 = (bf16[64,1024]{1,0:T(8,128)(2,1)S(1)}, bf16[64,1024]{1,0:T(8,128)(2,1)S(1)}, u32[]{:S(2)}, u32[]{:S(2)}) collective-permute-start(bf16[64,1024]{1,0:T(8,128)(2,1)S(1)} %get-tuple-element.59), channel_id=1, source_target_pairs={{0,7},{1,0},{2,1},{3,2},{4,3},{5,4},{6,5},{7,6},{8,15},{9,8},{10,9... | collective-permute-start | bytes 393224 | tf_op jit(solution)/shard_map/ppermute | solution.py:460
  79.2 12.7 %collective-permute-start.28 = (bf16[4,16,128]{2,1,0:T(8,128)(2,1)S(1)}, bf16[4,16,128]{2,1,0:T(8,128)(2,1)S(1)}, u32[]{:S(2)}, u32[]{:S(2)}) collective-permute-start(bf16[4,16,128]{2,1,0:T(8,128)(2,1)S(1)} %pad_maximum_fusion.1), channel_id=1, source_target_pairs={{0,8},{8,0},{16,24},{24,16},{32,40},{40,32},{48,56},{56,48},{64,72... | collective-permute-start | bytes 49160 | tf_op jit(solution)/shard_map/ppermute | solution.py:433
  89.0 3.8 %collective-permute-start.27 = (bf16[64,512]{1,0:T(8,128)(2,1)S(1)}, bf16[64,512]{1,0:T(8,128)(2,1)S(1)}, u32[]{:S(2)}, u32[]{:S(2)}) collective-permute-start(bf16[64,512]{1,0:T(8,128)(2,1)S(1)} %get-tuple-element.70), channel_id=1, source_target_pairs={{0,8},{8,0},{16,24},{24,16},{32,40},{40,32},{48,56},{56,48},{64,72... | collective-permute-start | bytes 196616 | tf_op jit(solution)/shard_map/ppermute | solution.py:433

commit v11 on v9

--- a/solution.py
+++ b/solution.py
@@ -31,6 +31,11 @@
     return lax.dot_general(a, b, dims, preferred_element_type=F32)
 
 
+def position():
+    index = lax.axis_index("batch")
+    return index >> 3, (index >> 1) & 3, index & 1, lax.axis_index("head")
+
+
 def lanes():
     return lax.broadcasted_iota(jnp.int32, (GROUP, DH), 1)
 
@@ -50,7 +55,7 @@
 
 
 def local_body(
-    place, q_in, prompt_in, table_in, length_in, new_in, pool_in, o0, o1, o2, o3,
+    q_in, prompt_in, table_in, length_in, new_in, pool_in, o0, o1, o2, o3,
     q, prompt, table, length, new, pool, wide, scores, weights, slots, sems,
 ):
     pairs = [
@@ -67,6 +72,8 @@
         copy.start()
     outs = (o0, o1, o2, o3)
     lane = lanes()
+    x, y, _, _ = position()
+    mask = 8 * x + 4 * (y >> 1)
     copies[0].wait()
     for h in range(GROUP):
         wide[:, h, :] = q[:, h * DH : (h + 1) * DH].astype(F32)
@@ -78,11 +85,11 @@
         p = prompt[n]
         k = slots[32 + p]
         slots[32 + p] = k + 1
-        slots[n] = (4 * p + k) ^ place[0]
+        slots[n] = (4 * p + k) ^ mask
         order = jnp.where(lane == n, (4 * p + k).astype(F32), order)
     for copy in copies[2:6]:
         copy.wait()
-    base = place[1]
+    base = lax.axis_index("batch") * 256
     for n in range(32):
         keys = jnp.concatenate([pool[0, table[j, n] - base] for j in range(8)], axis=0)
         s = dot(wide[n].astype(BF16), keys, NT) * SCALE
@@ -119,12 +126,12 @@
         out[17] = split_tile(jnp.where(lane < 8, held[i], 0.0), 8)
 
 
-def local_parts(place, q, prompt, table, length, new, pool):
+def local_parts(q, prompt, table, length, new, pool):
     out = jax.ShapeDtypeStruct((18, GROUP, DH), BF16)
     return pl.pallas_call(
         local_body,
         out_shape=[out] * 4,
-        in_specs=[SMEM] + [HBM] * 6,
+        in_specs=[HBM] * 6,
         out_specs=[VMEM] * 4,
         scratch_shapes=[
             pltpu.VMEM((32, GROUP * DH), BF16),
@@ -141,36 +148,37 @@
         ],
         compiler_params=params(54),
         name="local_parts",
-    )(place, q, prompt, table, length, new, pool)
-
-
-def regroup_body(place, a0, a1, a2, a3, same, across):
+    )(q, prompt, table, length, new, pool)
+
+
+def regroup_body(a0, a1, a2, a3, same, across):
+    x, _, _, z = position()
     for i, a in enumerate((a0, a1, a2, a3)):
         same[4 * i : 4 * i + 4] = a[0:4]
         across[4 * i : 4 * i + 4] = a[4:8]
         across[17 + 5 * i : 22 + 5 * i] = a[13:18]
 
-        @pl.when(place[2] ^ (place[4] >> 1) == i)
+        @pl.when(x ^ (z >> 1) == i)
         def _(a=a):
             same[16] = a[8]
             across[16] = a[8]
 
 
-def regroup(place, parts):
+def regroup(parts):
     return pl.pallas_call(
         regroup_body,
         out_shape=[
             jax.ShapeDtypeStruct((17, GROUP, DH), BF16),
             jax.ShapeDtypeStruct((37, GROUP, DH), BF16),
         ],
-        in_specs=[SMEM] + [VMEM] * 4,
+        in_specs=[VMEM] * 4,
         out_specs=[VMEM] * 2,
         compiler_params=params(),
         name="regroup",
-    )(place, *parts)
-
-
-ROWS = 128
+    )(*parts)
+
+
+ROWS = 256
 
 
 def prefix_part(q, kv):
@@ -246,10 +254,14 @@
     )(q, kv0, kv1)
 
 
+PLACES = 0x47210635
+
+
 def combine_body(
-    place, own, own_masses, cross, cross_masses, message, s0, s1, s2, s3, far, out, held
+    own, own_masses, cross, cross_masses, message, s0, s1, s2, s3, far, after, out, held
 ):
-    x, y_high, z = place[2], place[3], place[4]
+    x, y, _, z = position()
+    y_high = y >> 1
     theirs = join_tile(message[32], 32)
     near = [join_tile(s[17], 8) for s in (s0, s1, s2, s3)]
     across = [join_tile(far[21 + 5 * i], 8) for i in range(4)]
@@ -272,31 +284,31 @@
                 ea, eb, es = jnp.exp(la - top), jnp.exp(lb - top), jnp.exp(ls - top)
                 row = (ea * a + eb * b + es * s) / (ea + eb + es)
                 target = (x ^ kx) * 2 + (y_high ^ g)
-                held[((target - z - 2) & 7) * 4 + k] = row
+                held[((PLACES >> (4 * ((target - z) & 7))) & 7) * 4 + k] = row
     for h in range(GROUP):
         out[:, h * DH : (h + 1) * DH] = held[:, h, :].astype(BF16)
 
 
-def combine(place, own, cross, message, near, far):
+def combine(own, cross, message, near, far, after):
     return pl.pallas_call(
         combine_body,
         out_shape=jax.ShapeDtypeStruct((32, GROUP * DH), BF16),
-        in_specs=[SMEM] + [VMEM] * 10,
+        in_specs=[VMEM] * 10 + [ANY],
         out_specs=VMEM,
         scratch_shapes=[pltpu.VMEM((32, GROUP, DH), F32)],
         compiler_params=params(),
         name="combine",
-    )(place, *own, *cross, message, *near, far)
-
-
-def by_target(total):
+    )(*own, *cross, message, *near, far, after)
+
+
+def by_target(total, count):
     low = lax.broadcasted_iota(jnp.int32, (8, total.shape[1]), 0) < 4
     chunks = []
-    for g in range(2):
+    for g in range(count // 2):
         even, odd = [], []
         for j in (0, 2):
-            first = total[j * 16 + g * 8 : j * 16 + g * 8 + 8]
-            second = total[(j + 1) * 16 + g * 8 : (j + 1) * 16 + g * 8 + 8]
+            at = j * 4 * count + g * 8
+            first, second = total[at : at + 8], total[at + 4 * count : at + 4 * count + 8]
             even.append(jnp.where(low, first, pltpu.roll(second, 4, 0)))
             odd.append(jnp.where(low, pltpu.roll(first, 4, 0), second))
         chunks += [jnp.concatenate(even, axis=0), jnp.concatenate(odd, axis=0)]
@@ -304,23 +316,25 @@
 
 
 def project_body(a, b, c, w0, w1, out):
+    count, size = out.shape[0], a.shape[0]
     rows = jnp.concatenate([a[...], b[...], c[...]], axis=0)
     for side, weight in enumerate((w0, w1)):
         total = dot(rows, weight[...])
         for i in range(3):
-            for d, chunk in enumerate(by_target(total[64 * i : 64 * i + 64])):
+            for d, chunk in enumerate(by_target(total[size * i : size * i + size], count)):
                 out[d, i * 16 : i * 16 + 16, side * 512 : side * 512 + 512] = chunk
 
 
 def project(blocks, weights):
+    size = blocks[0].shape[0]
     return pl.pallas_call(
         project_body,
-        out_shape=jax.ShapeDtypeStruct((4, 48, 1024), F32),
+        out_shape=jax.ShapeDtypeStruct((size // 16, 48, 1024), F32),
         in_specs=[VMEM] * 5,
         out_specs=VMEM,
         compiler_params=params(),
         cost_estimate=pl.CostEstimate(
-            flops=2 * 192 * 2048 * 1024, bytes_accessed=4_500_000, transcendentals=0
+            flops=2 * 3 * size * 2048 * 1024, bytes_accessed=4_500_000, transcendentals=0
         ),
         name="project",
     )(*blocks, *weights)
@@ -330,29 +344,30 @@
     rows = jnp.concatenate([a[...], b[...]], axis=0)
     for side, weight in enumerate((w0, w1)):
         columns = slice(side * 512, side * 512 + 512)
-        for d, chunk in enumerate(by_target(dot(rows, weight[...]))):
-            yield side, columns, d, jnp.concatenate([first[d, :, columns], chunk], axis=0)
+        for d, chunk in enumerate(by_target(dot(rows, weight[...]), first.shape[0])):
+            yield columns, d, jnp.concatenate([first[d, :, columns], chunk], axis=0)
 
 
 def far_body(a, b, w0, w1, first, keep, up, down, direct):
-    for _, columns, d, whole in last_chunks(a, b, w0, w1, first):
-        if d == 0:
+    for columns, d, whole in last_chunks(a, b, w0, w1, first):
+        if d == 5:
             keep[:, columns] = whole
+        elif d == 1:
+            direct[:, columns] = whole.astype(BF16)
         else:
-            (up, direct, down)[d - 1][:, columns] = whole.astype(BF16)
-
-
-def near_body(a, b, w0, w1, first, keep6, down, keep0, up):
-    for _, columns, d, whole in last_chunks(a, b, w0, w1, first):
-        if d in (0, 2):
-            (keep6, keep0)[d // 2][:, columns] = whole
-        else:
-            (down, up)[d // 2][:, columns] = whole.astype(BF16)
+            out = up if d in (0, 3) else down
+            out[d // 3, :, columns] = whole.astype(BF16)
+
+
+def near_body(a, b, w0, w1, first, keep2, keep6):
+    for columns, d, whole in last_chunks(a, b, w0, w1, first):
+        (keep2, keep6)[d][:, columns] = whole
 
 
 SUM = jax.ShapeDtypeStruct((64, 1024), F32)
 SENT = jax.ShapeDtypeStruct((64, 1024), BF16)
 HALF = jax.ShapeDtypeStruct((64, 512), BF16)
+TWO = jax.ShapeDtypeStruct((2, 64, 1024), BF16)
 
 
 def plain(body, out_shape, *args):
@@ -367,20 +382,20 @@
 
 
 def middle_body(keep2, keep6, below, above, up, down):
-    up[...] = (keep2[...] + below[...].astype(F32)).astype(BF16)
-    down[...] = (keep6[...] + above[...].astype(F32)).astype(BF16)
-
-
-def total_body(keep, below1, above1, below2, above2, opposite, own, other):
-    near = keep[...] + below1[...].astype(F32) + above1[...].astype(F32)
+    up[...] = (keep2[...] + below[0].astype(F32)).astype(BF16)
+    down[...] = (keep6[...] + above[0].astype(F32)).astype(BF16)
+
+
+def total_body(keep, below, above, below2, above2, opposite, own, other):
+    near = keep[...] + below[1].astype(F32) + above[1].astype(F32)
     whole = near + below2[...].astype(F32) + above2[...].astype(F32)
     whole = (whole + opposite[...].astype(F32)).astype(BF16)
     own[...] = whole[:, :512]
     other[...] = whole[:, 512:]
 
 
-def order_body(place, orders, pick):
-    x, y, core, z = place[2], place[3] * 2 + place[5], place[6], place[4]
+def order_body(orders, pick):
+    x, y, core, z = position()
     lane = lanes()
     order = jnp.zeros((GROUP, DH), F32)
     for block in range(4):
@@ -401,15 +416,15 @@
     pick[...] = (row == source[0:1]).astype(F32).astype(BF16)
 
 
-def order_rows(place, orders):
+def order_rows(orders):
     return pl.pallas_call(
         order_body,
         out_shape=jax.ShapeDtypeStruct((128, 128), BF16),
-        in_specs=[SMEM, VMEM],
+        in_specs=[VMEM],
         out_specs=VMEM,
         compiler_params=params(),
         name="order_rows",
-    )(place, orders)
+    )(orders)
 
 
 def finish_body(own, other, pick, out):
@@ -453,7 +468,8 @@
 def gathered(parts):
     ring0 = jnp.concatenate(parts, axis=0)
     ring1, ring3 = turned(ring0, 1, 1), turned(ring0, 3, 1)
-    return ring0, ring1, ring3, [turned(ring3[:32], 1, 1), turned(ring1[32:], 3, 1)]
+    half = ring0.shape[0] // 2
+    return ring0, ring1, ring3, [turned(ring3[:half], 1, 1), turned(ring1[half:], 3, 1)]
 
 
 def along_z(value, k):
@@ -461,18 +477,12 @@
 
 
 def shards(queries, new_kv, prefix_kv, suffix_kv, page_table, suffix_len, prompt_of, out_weight):
-    me = lax.axis_index("batch")
-    z = lax.axis_index("head")
-    x, y, core = me // 8, (me // 2) % 4, me % 2
-    place = [8 * x + 4 * (y // 2), me * 256, x, y // 2, z, y % 2, core]
-    place = jnp.stack(place).astype(jnp.int32)
-
     prefix_other = other_core(prefix_kv)
     weights = [out_weight, other_core(out_weight)]
 
-    sent = local_parts(place, queries, prompt_of, page_table.T, suffix_len, new_kv, suffix_kv)
+    sent = local_parts(queries, prompt_of, page_table.T, suffix_len, new_kv, suffix_kv)
     by_x = [sent[0]] + [along_x(sent[k], k) for k in (1, 2, 3)]
-    same, across = regroup(place, by_x)
+    same, across = regroup(by_x)
     from1, from3 = along_y(same, 1), along_y(across, 3)
 
     own = prefix_keep(same, prefix_kv, prefix_other)
@@ -482,27 +492,23 @@
     message, from2 = lax.optimization_barrier((message, from2))
     message = along_y(message, 1)
     cross = prefix_keep(from2, prefix_kv, prefix_other)
-    attended = combine(place, own, cross, message, by_x, from2)
-
     orders = jnp.stack([same[16], from1[16], from2[16], from3[16]])
     orders = jnp.concatenate([orders, other_core(orders)], axis=0)
-    pick = order_rows(place, orders)
+    pick = order_rows(orders)
+    attended = combine(own, cross, message, by_x, from2, pick)
 
     parts = [attended] + [turned(attended, k, 0) for k in (1, 2, 3)]
-    far, near = [gathered([a[i : i + 16] for a in parts]) for i in (0, 16)]
+    far, near = gathered([a[:24] for a in parts]), gathered([a[24:] for a in parts])
     first_far, first_near = project(far[:3], weights), project(near[:3], weights)
-    keep2, up3, down3, up4 = plain(
-        far_body, [SUM, SENT, SENT, SENT], *far[3], *weights, first_far
+    keep0, up, down, direct = plain(
+        far_body, [SUM, TWO, TWO, SENT], *far[3], *weights, first_far
     )
-    below3, above3 = along_z(up3, 1), along_z(down3, -1)
-    opposite = along_z(up4, 4)
-    keep6, down1, keep0, up1 = plain(
-        near_body, [SUM, SENT, SUM, SENT], *near[3], *weights, first_near
-    )
-    below1, above1 = along_z(up1, 1), along_z(down1, -1)
-    up2, down2 = plain(middle_body, [SENT, SENT], keep2, keep6, below3, above3)
+    below, above = along_z(up, 1), along_z(down, -1)
+    opposite = along_z(direct, 4)
+    keep2, keep6 = plain(near_body, [SUM, SUM], *near[3], *weights, first_near)
+    up2, down2 = plain(middle_body, [SENT, SENT], keep2, keep6, below, above)
     below2, above2 = along_z(up2, 2), along_z(down2, -2)
-    own, other = plain(total_body, [HALF, HALF], keep0, below1, above1, below2, above2, opposite)
+    own, other = plain(total_body, [HALF, HALF], keep0, below, above, below2, above2, opposite)
     return finish(own, other_core(other), pick)
 
 

time: 88.2 us -> 94 us (1.066)
  waiting for transfers between devices: 14.8 us -> 30.5 us
  starting transfers between devices: 51.4 us -> 44.4 us
  Pallas kernels: 19.9 us -> 16.3 us
    ppermute x11, waiting for transfers between devices: 9.85 us -> 19.2 us  [turned(): return lax.ppermute(value, 'batch', pairs)]
    ppermute x7 -> x5, waiting for transfers between devices: 0.02 us -> 6.34 us  [along_z(): lax.ppermute(value, 'head', [(i, (i + k) % HEADS) for i in range(HEADS)])]
    ppermute x7 -> x5, starting transfers between devices: 16.1 us -> 13 us  [along_z(): lax.ppermute(value, 'head', [(i, (i + k) % HEADS) for i in range(HEADS)])]
    ppermute x11, starting transfers between devices: 24.6 us -> 21.7 us  [along(): lax.ppermute(value, 'batch', [(i, i ^ k << shift) for i in range(BATCH)])]
    unnamed x10 -> x16, local copies, waits for them, and re-layouts: 0.9 us -> 2.13 us
    ppermute x11, starting transfers between devices: 10.7 us -> 9.71 us  [turned(): return lax.ppermute(value, 'batch', pairs)]
  transfers between devices with their start and end apart: 29 -> 27, of which waited for: 10 -> 13; matrix products, arithmetic and copies ran while one was open for 1% -> 0% of each run, Pallas kernels for 22% -> 15%
where the time goes in v11:
time: 94 us; the launch traced here: 93.8 us
  starting transfers between devices  44.4 us (47%)
  waiting for transfers between devices  30.5 us (32%)
  Pallas kernels  16.3 us (17%)
  local copies, waits for them, and re-layouts  2.25 us (2%)
    ppermute x11, starting transfers between devices, along(): lax.ppermute(value, 'batch', [(i, i ^ k << shift) for i in range(BATCH)])  21.7 us
    ppermute x11, waiting for transfers between devices, turned(): return lax.ppermute(value, 'batch', pairs)  19.2 us
    ppermute x5, starting transfers between devices, along_z(): lax.ppermute(value, 'head', [(i, (i + k) % HEADS) for i in range(HEADS)])  13 us
    ppermute x11, starting transfers between devices, turned(): return lax.ppermute(value, 'batch', pairs)  9.71 us
    ppermute x5, waiting for transfers between devices, along_z(): lax.ppermute(value, 'head', [(i, (i + k) % HEADS) for i in range(HEADS)])  6.34 us
    ppermute x11, waiting for transfers between devices, along(): lax.ppermute(value, 'batch', [(i, i ^ k << shift) for i in range(BATCH)])  4.93 us
    pallas_call x2, Pallas kernels, prefix_keep(): pl.pallas_call(prefix_keep_body, out_shape=[out, out], in_specs=[VMEM] *...  3.71 us
    pallas_call x1, Pallas kernels, local_parts(): pl.pallas_call(local_body, out_shape=[out] * 4, in_specs=[HBM] * 6, out_s...  3.48 us
  transfers between devices with their start and end apart: 27, of which 13 were waited for; matrix products, arithmetic and copies ran while one was open for 0% of the time, Pallas kernels for 15%

profile of v11, /device:TPU:1, one launch (start us, length us, event | category | flops | bytes accessed | tf_op | source)
XLA Modules:
  0.0 93.8 jit_solution(16449891873542333833)
XLA Ops:
  0.0 3.2 %collective-permute-start.4 = (bf16[2,2048,128]{2,1,0:T(8,128)(2,1)}, bf16[2,2048,128]{2,1,0:T(8,128)(2,1)S(1)}, u32[]{:S(2)}, u32[]{:S(2)}) collective-permute-start(bf16[2,2048,128]{2,1,0:T(8,128)(2,1)} %kv0.5), channel_id=1, source_target_pairs={{0,8},{8,0},{16,24},{24,16},{32,40},{40,32},{48,56},{56,48},{64,72... | collective-permute-start | bytes 3145736 | tf_op jit(solution)/shard_map/ppermute | solution.py:448
  3.2 3.5 %local_parts.1 = (bf16[18,16,128]{2,1,0:T(8,128)(2,1)}, bf16[18,16,128]{2,1,0:T(8,128)(2,1)}, bf16[18,16,128]{2,1,0:T(8,128)(2,1)}, bf16[18,16,128]{2,1,0:T(8,128)(2,1)}) custom-call(bf16[32,2048]{1,0:T(8,128)(2,1)} %q_in.1, s32[32]{0:T(128)} %prompt_in.1, s32[8,32]{1,0:T(8,128)} %bitcast.1, s32[32]{0:T(128)} %length_in.1, bf16[2,32,128]{2,1,0:T(8,128)(2,1)} %new_in.1, ...), custom_call_target="tpu_custom_call" | custom-call | tf_op jit(solution)/shard_map/local_parts/pallas_call | solution.py:131
  6.7 0.1 collective-permute-start
  6.8 1.9 %collective-permute-start.1 = (bf16[18,16,128]{2,1,0:T(8,128)(2,1)}, bf16[18,16,128]{2,1,0:T(8,128)(2,1)S(1)}, u32[]{:S(2)}, u32[]{:S(2)}) collective-permute-start(bf16[18,16,128]{2,1,0:T(8,128)(2,1)} %get-tuple-element.32), channel_id=1, source_target_pairs={{0,128},{8,136},{16,144},{24,152},{32,160},{40,168},{48,176},{56,1... | collective-permute-start | bytes 221192 | tf_op jit(solution)/shard_map/ppermute | solution.py:448
  8.7 1.9 %collective-permute-start.2 = (bf16[18,16,128]{2,1,0:T(8,128)(2,1)}, bf16[18,16,128]{2,1,0:T(8,128)(2,1)S(1)}, u32[]{:S(2)}, u32[]{:S(2)}) collective-permute-start(bf16[18,16,128]{2,1,0:T(8,128)(2,1)} %get-tuple-element.33), channel_id=1, source_target_pairs={{0,192},{8,200},{16,208},{24,216},{32,224},{40,232},{48,240},{56,2... | collective-permute-start | bytes 221192 | tf_op jit(solution)/shard_map/ppermute | solution.py:448
  10.7 1.0 %collective-permute-start.16 = (bf16[2048,512]{1,0:T(8,128)(2,1)S(1)}, bf16[2048,512]{1,0:T(8,128)(2,1)S(1)}, u32[]{:S(2)}, u32[]{:S(2)}) collective-permute-start(bf16[2048,512]{1,0:T(8,128)(2,1)S(1)} %copy-done), channel_id=1, source_target_pairs={{0,8},{8,0},{16,24},{24,16},{32,40},{40,32},{48,56},{56,48},{64,72... | collective-permute-start | bytes 6291464 | tf_op jit(solution)/shard_map/ppermute | solution.py:448
  11.7 1.2 %collective-permute-done.1.a2.s2 = bf16[18,16,128]{2,1,0:T(8,128)(2,1)S(1)} collective-permute-done((bf16[18,16,128]{2,1,0:T(8,128)(2,1)}, bf16[18,16,128]{2,1,0:T(8,128)(2,1)S(1)}, u32[]{:S(2)}, u32[]{:S(2)}) %collective-permute-start.1) | collective-permute-done | bytes 73760 | tf_op jit(solution)/shard_map/ppermute | solution.py:448
  12.9 1.4 %collective-permute-done.2.a3.s3 = bf16[18,16,128]{2,1,0:T(8,128)(2,1)S(1)} collective-permute-done((bf16[18,16,128]{2,1,0:T(8,128)(2,1)}, bf16[18,16,128]{2,1,0:T(8,128)(2,1)S(1)}, u32[]{:S(2)}, u32[]{:S(2)}) %collective-permute-start.2) | collective-permute-done | bytes 73760 | tf_op jit(solution)/shard_map/ppermute | solution.py:448
  14.2 0.9 copy-done.3
  15.1 2.8 %collective-permute-start.3 = (bf16[37,16,128]{2,1,0:T(8,128)(2,1)S(1)}, bf16[37,16,128]{2,1,0:T(8,128)(2,1)S(1)}, u32[]{:S(2)}, u32[]{:S(2)}) collective-permute-start(bf16[37,16,128]{2,1,0:T(8,128)(2,1)S(1)} %get-tuple-element.34), channel_id=1, source_target_pairs={{0,48},{8,56},{16,32},{24,40},{32,16},{40,24},{48,0},{56,8},{64,11... | collective-permute-start | bytes 454664 | tf_op jit(solution)/shard_map/ppermute | solution.py:448
  18.0 0.0 collective-permute-done.4.kv1
  18.0 0.0 copy-start.1
  18.0 1.2 %copy-done.1 = bf16[2,2048,128]{2,1,0:T(8,128)(2,1)S(1)} copy-done((bf16[2,2048,128]{2,1,0:T(8,128)(2,1)S(1)}, bf16[2,2048,128]{2,1,0:T(8,128)(2,1)}, u32[]{:S(2)}) %copy-start.1) | copy-done | bytes 1048600
  19.2 1.9 %prefix_keep.2 = (f32[16,16,128]{2,1,0:T(8,128)S(1)}, f32[16,16,128]{2,1,0:T(8,128)S(1)}) custom-call(bf16[17,16,128]{2,1,0:T(8,128)(2,1)S(1)} %get-tuple-element.35.q, bf16[2,2048,128]{2,1,0:T(8,128)(2,1)S(1)} %copy-done.1, bf16[2,2048,128]{2,1,0:T(8,128)(2,1)S(1)} %collective-permute-done.4.kv1), custom_call_target="tpu_custom_call" | custom-call | flops 536870912 | bytes 2500000 | tf_op jit(solution)/shard_map/prefix_keep/pallas_call | solution.py:246
  21.1 0.0 collective-permute-done.3.qb
  21.1 1.5 %collective-permute-start.6 = (bf16[37,16,128]{2,1,0:T(8,128)(2,1)S(1)}, bf16[37,16,128]{2,1,0:T(8,128)(2,1)S(1)}, u32[]{:S(2)}, u32[]{:S(2)}) collective-permute-start(bf16[37,16,128]{2,1,0:T(8,128)(2,1)S(1)} %collective-permute-done.3.qb), channel_id=1, source_target_pairs={{0,16},{8,24},{16,0},{24,8},{32,48},{40,56},{48,32},{56,40},{64,80... | collective-permute-start | bytes 454664 | tf_op jit(solution)/shard_map/ppermute | solution.py:448
  22.6 0.0 collective-permute-done.5.qa
  22.6 3.4 %prefix_send.1 = bf16[33,16,128]{2,1,0:T(8,128)(2,1)S(1)} custom-call(bf16[17,16,128]{2,1,0:T(8,128)(2,1)S(1)} %collective-permute-done.5.qa, bf16[37,16,128]{2,1,0:T(8,128)(2,1)S(1)} %collective-permute-done.3.qb, bf16[2,2048,128]{2,1,0:T(8,128)(2,1)S(1)} %copy-done.2, bf16[2,2048,128]{2,1,0:T(8,128)(2,1)S(1)} %collective-permute-done.4.kv1, ...), custom_call_target="tpu_custom_call" | custom-call | flops 1073741824 | bytes 2500000 | tf_op jit(solution)/shard_map/prefix_send/pallas_call | solution.py:233
  26.0 0.0 copy-start.4
  26.1 2.0 %collective-permute-start.8 = (bf16[4,16,128]{2,1,0:T(8,128)(2,1)S(1)}, bf16[4,16,128]{2,1,0:T(8,128)(2,1)S(1)}, u32[]{:S(2)}, u32[]{:S(2)}) collective-permute-start(bf16[4,16,128]{2,1,0:T(8,128)(2,1)S(1)} %pad_maximum_fusion.2), channel_id=1, source_target_pairs={{0,8},{8,0},{16,24},{24,16},{32,40},{40,32},{48,56},{56,48},{64,72... | collective-permute-start | bytes 49160 | tf_op jit(solution)/shard_map/ppermute | solution.py:448
  28.1 1.4 %collective-permute-start.7 = (bf16[33,16,128]{2,1,0:T(8,128)(2,1)S(1)}, bf16[33,16,128]{2,1,0:T(8,128)(2,1)S(1)}, u32[]{:S(2)}, u32[]{:S(2)}) collective-permute-start(bf16[33,16,128]{2,1,0:T(8,128)(2,1)S(1)} %prefix_send.1), channel_id=1, source_target_pairs={{0,16},{8,24},{16,0},{24,8},{32,48},{40,56},{48,32},{56,40},{64,80... | collective-permute-start | bytes 405512 | tf_op jit(solution)/shard_map/ppermute | solution.py:448
  29.6 1.9 %prefix_keep.3 = (f32[16,16,128]{2,1,0:T(8,128)S(1)}, f32[16,16,128]{2,1,0:T(8,128)S(1)}) custom-call(bf16[37,16,128]{2,1,0:T(8,128)(2,1)S(1)} %collective-permute-done.6.q.far, bf16[2,2048,128]{2,1,0:T(8,128)(2,1)S(1)} %copy-done.2, bf16[2,2048,128]{2,1,0:T(8,128)(2,1)S(1)} %collective-permute-done.4.kv1), custom_call_target="tpu_custom_call" | custom-call | flops 536870912 | bytes 2500000 | tf_op jit(solution)/shard_map/prefix_keep/pallas_call | solution.py:246
  31.4 0.0 collective-permute-done.8
  31.5 0.1 order_rows.1.after.pick
  31.6 1.5 %collective-permute-done.7.message = bf16[33,16,128]{2,1,0:T(8,128)(2,1)S(1)} collective-permute-done((bf16[33,16,128]{2,1,0:T(8,128)(2,1)S(1)}, bf16[33,16,128]{2,1,0:T(8,128)(2,1)S(1)}, u32[]{:S(2)}, u32[]{:S(2)}) %collective-permute-start.7) | collective-permute-done | bytes 135200 | tf_op jit(solution)/shard_map/ppermute | solution.py:448
  33.1 0.7 combine.1
  33.7 1.5 %collective-permute-start.9 = (bf16[32,2048]{1,0:T(8,128)(2,1)S(1)}, bf16[32,2048]{1,0:T(8,128)(2,1)S(1)}, u32[]{:S(2)}, u32[]{:S(2)}) collective-permute-start(bf16[32,2048]{1,0:T(8,128)(2,1)S(1)} %combine.1), channel_id=1, source_target_pairs={{0,64},{8,24},{16,80},{24,8},{32,96},{40,56},{48,112},{56,40},{64,... | collective-permute-start | bytes 393224 | tf_op jit(solution)/shard_map/ppermute | solution.py:465
  35.2 2.4 %collective-permute-start.10 = (bf16[32,2048]{1,0:T(8,128)(2,1)S(1)}, bf16[32,2048]{1,0:T(8,128)(2,1)S(1)}, u32[]{:S(2)}, u32[]{:S(2)}) collective-permute-start(bf16[32,2048]{1,0:T(8,128)(2,1)S(1)} %combine.1), channel_id=1, source_target_pairs={{0,128},{8,40},{16,144},{24,56},{32,160},{40,8},{48,176},{56,24},{... | collective-permute-start | bytes 393224 | tf_op jit(solution)/shard_map/ppermute | solution.py:465
  37.7 0.1 collective-permute-start.11
  37.7 0.0 collective-permute-done.9
  37.8 3.9 %collective-permute-done.10 = bf16[32,2048]{1,0:T(8,128)(2,1)S(1)} collective-permute-done((bf16[32,2048]{1,0:T(8,128)(2,1)S(1)}, bf16[32,2048]{1,0:T(8,128)(2,1)S(1)}, u32[]{:S(2)}, u32[]{:S(2)}) %collective-permute-start.10) | collective-permute-done | bytes 131104 | tf_op jit(solution)/shard_map/ppermute | solution.py:465
  41.7 1.4 %collective-permute-done.11 = bf16[32,2048]{1,0:T(8,128)(2,1)S(1)} collective-permute-done((bf16[32,2048]{1,0:T(8,128)(2,1)S(1)}, bf16[32,2048]{1,0:T(8,128)(2,1)S(1)}, u32[]{:S(2)}, u32[]{:S(2)}) %collective-permute-start.11) | collective-permute-done | bytes 131104 | tf_op jit(solution)/shard_map/ppermute | solution.py:465
  43.2 1.4 %collective-permute-start.12 = (bf16[96,2048]{1,0:T(8,128)(2,1)S(1)}, bf16[96,2048]{1,0:T(8,128)(2,1)S(1)}, u32[]{:S(2)}, u32[]{:S(2)}) collective-permute-start(bf16[96,2048]{1,0:T(8,128)(2,1)S(1)} %pad_maximum_fusion.a), channel_id=1, source_target_pairs={{0,48},{8,200},{16,32},{24,216},{32,16},{40,232},{48,0},{56,248},{... | collective-permute-start | bytes 1179656 | tf_op jit(solution)/shard_map/ppermute | solution.py:465
  44.6 0.0 collective-permute-start.14
  44.6 6.8 %collective-permute-done.12.c = bf16[96,2048]{1,0:T(8,128)(2,1)S(1)} collective-permute-done((bf16[96,2048]{1,0:T(8,128)(2,1)S(1)}, bf16[96,2048]{1,0:T(8,128)(2,1)S(1)}, u32[]{:S(2)}, u32[]{:S(2)}) %collective-permute-start.12) | collective-permute-done | bytes 393248 | tf_op jit(solution)/shard_map/ppermute | solution.py:465
  51.4 0.1 collective-permute-start.13
  51.5 1.4 %collective-permute-start.15 = (bf16[48,2048]{1,0:T(8,128)(2,1)S(1)}, bf16[48,2048]{1,0:T(8,128)(2,1)S(1)}, u32[]{:S(2)}, u32[]{:S(2)}) collective-permute-start(bf16[48,2048]{1,0:T(8,128)(2,1)S(1)} %slice.71), channel_id=1, source_target_pairs={{0,48},{8,200},{16,32},{24,216},{32,16},{40,232},{48,0},{56,248},{... | collective-permute-start | bytes 589832 | tf_op jit(solution)/shard_map/ppermute | solution.py:465
  53.0 0.0 collective-permute-done.16.w1
  53.0 1.4 %project.2.first = f32[6,48,1024]{2,1,0:T(8,128)S(1)} custom-call(bf16[96,2048]{1,0:T(8,128)(2,1)S(1)} %pad_maximum_fusion.a, bf16[96,2048]{1,0:T(8,128)(2,1)S(1)} %collective-permute-done.14.b, bf16[96,2048]{1,0:T(8,128)(2,1)S(1)} %collective-permute-done.12.c, bf16[2048,512]{1,0:T(8,128)(2,1)S(1)} %copy-done, bf16[2048,512]{1,0:T(8,128)(2,1)S(1)} %collective-permute-done.16.w1), custom_call_target="tpu_custom_call" | custom-call | flops 1207959552 | bytes 4500000 | tf_op jit(solution)/shard_map/project/pallas_call | solution.py:330
  54.4 1.6 %collective-permute-done.13.a = bf16[48,2048]{1,0:T(8,128)(2,1)S(1)} collective-permute-done((bf16[48,2048]{1,0:T(8,128)(2,1)S(1)}, bf16[48,2048]{1,0:T(8,128)(2,1)S(1)}, u32[]{:S(2)}, u32[]{:S(2)}) %collective-permute-start.13) | collective-permute-done | bytes 196640 | tf_op jit(solution)/shard_map/ppermute | solution.py:465
  56.0 1.3 %collective-permute-done.15.b = bf16[48,2048]{1,0:T(8,128)(2,1)S(1)} collective-permute-done((bf16[48,2048]{1,0:T(8,128)(2,1)S(1)}, bf16[48,2048]{1,0:T(8,128)(2,1)S(1)}, u32[]{:S(2)}, u32[]{:S(2)}) %collective-permute-start.15) | collective-permute-done | bytes 196640 | tf_op jit(solution)/shard_map/ppermute | solution.py:465
  57.4 0.8 far.1
  58.2 1.7 %collective-permute-start.17 = (bf16[2,64,1024]{2,1,0:T(8,128)(2,1)S(1)}, bf16[2,64,1024]{2,1,0:T(8,128)(2,1)S(1)}, u32[]{:S(2)}, u32[]{:S(2)}) collective-permute-start(bf16[2,64,1024]{2,1,0:T(8,128)(2,1)S(1)} %get-tuple-element.46), channel_id=1, source_target_pairs={{0,1},{1,2},{2,3},{3,4},{4,5},{5,6},{6,7},{7,0},{8,9},{9,10},{10,1... | collective-permute-start | bytes 786440 | tf_op jit(solution)/shard_map/ppermute | solution.py:476
  59.9 4.0 %collective-permute-start.18 = (bf16[2,64,1024]{2,1,0:T(8,128)(2,1)S(1)}, bf16[2,64,1024]{2,1,0:T(8,128)(2,1)S(1)}, u32[]{:S(2)}, u32[]{:S(2)}) collective-permute-start(bf16[2,64,1024]{2,1,0:T(8,128)(2,1)S(1)} %get-tuple-element.47), channel_id=1, source_target_pairs={{0,7},{1,0},{2,1},{3,2},{4,3},{5,4},{6,5},{7,6},{8,15},{9,8},{10,9... | collective-permute-start | bytes 786440 | tf_op jit(solution)/shard_map/ppermute | solution.py:476
  64.0 1.4 %collective-permute-start.19 = (bf16[32,2048]{1,0:T(8,128)(2,1)S(1)}, bf16[32,2048]{1,0:T(8,128)(2,1)S(1)}, u32[]{:S(2)}, u32[]{:S(2)}) collective-permute-start(bf16[32,2048]{1,0:T(8,128)(2,1)S(1)} %pad_maximum_fusion.1.a), channel_id=1, source_target_pairs={{0,48},{8,200},{16,32},{24,216},{32,16},{40,232},{48,0},{56,248},{... | collective-permute-start | bytes 393224 | tf_op jit(solution)/shard_map/ppermute | solution.py:465
  65.4 0.0 collective-permute-start.21
  65.4 3.7 %collective-permute-done.19.c = bf16[32,2048]{1,0:T(8,128)(2,1)S(1)} collective-permute-done((bf16[32,2048]{1,0:T(8,128)(2,1)S(1)}, bf16[32,2048]{1,0:T(8,128)(2,1)S(1)}, u32[]{:S(2)}, u32[]{:S(2)}) %collective-permute-start.19) | collective-permute-done | bytes 131104 | tf_op jit(solution)/shard_map/ppermute | solution.py:465
  69.1 0.0 collective-permute-start.20
  69.1 0.4 collective-permute-done.21.b
  69.5 1.4 %collective-permute-start.22 = (bf16[16,2048]{1,0:T(8,128)(2,1)S(1)}, bf16[16,2048]{1,0:T(8,128)(2,1)S(1)}, u32[]{:S(2)}, u32[]{:S(2)}) collective-permute-start(bf16[16,2048]{1,0:T(8,128)(2,1)S(1)} %slice.77), channel_id=1, source_target_pairs={{0,48},{8,200},{16,32},{24,216},{32,16},{40,232},{48,0},{56,248},{... | collective-permute-start | bytes 196616 | tf_op jit(solution)/shard_map/ppermute | solution.py:465
  70.8 3.6 %collective-permute-start.25 = (bf16[64,1024]{1,0:T(8,128)(2,1)S(1)}, bf16[64,1024]{1,0:T(8,128)(2,1)S(1)}, u32[]{:S(2)}, u32[]{:S(2)}) collective-permute-start(bf16[64,1024]{1,0:T(8,128)(2,1)S(1)} %get-tuple-element.52), channel_id=1, source_target_pairs={{0,4},{1,5},{2,6},{3,7},{4,0},{5,1},{6,2},{7,3},{8,12},{9,13},{10,... | collective-permute-start | bytes 393224 | tf_op jit(solution)/shard_map/ppermute | solution.py:476
  74.5 0.8 project.3.first
  75.3 0.0 collective-permute-done.22.b
  75.3 0.8 near.1
  76.1 0.0 collective-permute-done.17.below
  76.2 0.0 collective-permute-done.18.above
  76.2 0.1 collective-permute-start.23
  76.3 3.6 %collective-permute-start.24 = (bf16[64,1024]{1,0:T(8,128)(2,1)S(1)}, bf16[64,1024]{1,0:T(8,128)(2,1)S(1)}, u32[]{:S(2)}, u32[]{:S(2)}) collective-permute-start(bf16[64,1024]{1,0:T(8,128)(2,1)S(1)} %get-tuple-element.51), channel_id=1, source_target_pairs={{0,6},{1,7},{2,0},{3,1},{4,2},{5,3},{6,4},{7,5},{8,14},{9,15},{10,... | collective-permute-start | bytes 393224 | tf_op jit(solution)/shard_map/ppermute | solution.py:476
  79.9 0.2 collective-permute-done.25.opposite
  80.1 6.1 %collective-permute-done.23.below2 = bf16[64,1024]{1,0:T(8,128)(2,1)S(1)} collective-permute-done((bf16[64,1024]{1,0:T(8,128)(2,1)S(1)}, bf16[64,1024]{1,0:T(8,128)(2,1)S(1)}, u32[]{:S(2)}, u32[]{:S(2)}) %collective-permute-start.23) | collective-permute-done | bytes 131104 | tf_op jit(solution)/shard_map/ppermute | solution.py:476
  86.2 0.1 total.1
  86.3 5.7 %collective-permute-start.26 = (bf16[64,512]{1,0:T(8,128)(2,1)S(1)}, bf16[64,512]{1,0:T(8,128)(2,1)S(1)}, u32[]{:S(2)}, u32[]{:S(2)}) collective-permute-start(bf16[64,512]{1,0:T(8,128)(2,1)S(1)} %get-tuple-element.54), channel_id=1, source_target_pairs={{0,8},{8,0},{16,24},{24,16},{32,40},{40,32},{48,56},{56,48},{64,72... | collective-permute-start | bytes 196616 | tf_op jit(solution)/shard_map/ppermute | solution.py:448
  92.0 0.9 collective-permute-done.26.other
  92.9 0.9 finish.1
  (43 shorter events, 0.3 us)
Async XLA Ops:
  0.0 10.7 %copy-start = (bf16[2048,512]{1,0:T(8,128)(2,1)S(1)}, bf16[2048,512]{1,0:T(8,128)(2,1)}, u32[]{:S(2)}) copy-start(bf16[2048,512]{1,0:T(8,128)(2,1)} %w0.7) | copy-start | bytes 6291460
  0.0 18.0 %collective-permute-start.4 = (bf16[2,2048,128]{2,1,0:T(8,128)(2,1)}, bf16[2,2048,128]{2,1,0:T(8,128)(2,1)S(1)}, u32[]{:S(2)}, u32[]{:S(2)}) collective-permute-start(bf16[2,2048,128]{2,1,0:T(8,128)(2,1)} %kv0.5), channel_id=1, source_target_pairs={{0,8},{8,0},{16,24},{24,16},{32,40},{40,32},{48,56},{56,48},{64,72... | collective-permute-start | bytes 3145736 | tf_op jit(solution)/shard_map/ppermute | solution.py:448
  6.7 4.9 %collective-permute-start = (bf16[18,16,128]{2,1,0:T(8,128)(2,1)}, bf16[18,16,128]{2,1,0:T(8,128)(2,1)S(1)}, u32[]{:S(2)}, u32[]{:S(2)}) collective-permute-start(bf16[18,16,128]{2,1,0:T(8,128)(2,1)} %get-tuple-element.31), channel_id=1, source_target_pairs={{0,64},{8,72},{16,80},{24,88},{32,96},{40,104},{48,112},{56,120},{... | collective-permute-start | bytes 221192 | tf_op jit(solution)/shard_map/ppermute | solution.py:448
  6.8 6.0 %collective-permute-start.1 = (bf16[18,16,128]{2,1,0:T(8,128)(2,1)}, bf16[18,16,128]{2,1,0:T(8,128)(2,1)S(1)}, u32[]{:S(2)}, u32[]{:S(2)}) collective-permute-start(bf16[18,16,128]{2,1,0:T(8,128)(2,1)} %get-tuple-element.32), channel_id=1, source_target_pairs={{0,128},{8,136},{16,144},{24,152},{32,160},{40,168},{48,176},{56,1... | collective-permute-start | bytes 221192 | tf_op jit(solution)/shard_map/ppermute | solution.py:448
  8.7 5.5 %collective-permute-start.2 = (bf16[18,16,128]{2,1,0:T(8,128)(2,1)}, bf16[18,16,128]{2,1,0:T(8,128)(2,1)S(1)}, u32[]{:S(2)}, u32[]{:S(2)}) collective-permute-start(bf16[18,16,128]{2,1,0:T(8,128)(2,1)} %get-tuple-element.33), channel_id=1, source_target_pairs={{0,192},{8,200},{16,208},{24,216},{32,224},{40,232},{48,240},{56,2... | collective-permute-start | bytes 221192 | tf_op jit(solution)/shard_map/ppermute | solution.py:448
  10.7 42.3 %collective-permute-start.16 = (bf16[2048,512]{1,0:T(8,128)(2,1)S(1)}, bf16[2048,512]{1,0:T(8,128)(2,1)S(1)}, u32[]{:S(2)}, u32[]{:S(2)}) collective-permute-start(bf16[2048,512]{1,0:T(8,128)(2,1)S(1)} %copy-done), channel_id=1, source_target_pairs={{0,8},{8,0},{16,24},{24,16},{32,40},{40,32},{48,56},{56,48},{64,72... | collective-permute-start | bytes 6291464 | tf_op jit(solution)/shard_map/ppermute | solution.py:448
  14.2 0.9 copy-start.3
  15.1 5.9 %collective-permute-start.3 = (bf16[37,16,128]{2,1,0:T(8,128)(2,1)S(1)}, bf16[37,16,128]{2,1,0:T(8,128)(2,1)S(1)}, u32[]{:S(2)}, u32[]{:S(2)}) collective-permute-start(bf16[37,16,128]{2,1,0:T(8,128)(2,1)S(1)} %get-tuple-element.34), channel_id=1, source_target_pairs={{0,48},{8,56},{16,32},{24,40},{32,16},{40,24},{48,0},{56,8},{64,11... | collective-permute-start | bytes 454664 | tf_op jit(solution)/shard_map/ppermute | solution.py:448
  18.0 4.7 %collective-permute-start.5 = (bf16[17,16,128]{2,1,0:T(8,128)(2,1)S(1)}, bf16[17,16,128]{2,1,0:T(8,128)(2,1)S(1)}, u32[]{:S(2)}, u32[]{:S(2)}) collective-permute-start(bf16[17,16,128]{2,1,0:T(8,128)(2,1)S(1)} %get-tuple-element.35.q), channel_id=1, source_target_pairs={{0,16},{8,24},{16,0},{24,8},{32,48},{40,56},{48,32},{56,40},{64,80... | collective-permute-start | bytes 208904 | tf_op jit(solution)/shard_map/ppermute | solution.py:448
  18.0 1.2 %copy-start.1 = (bf16[2,2048,128]{2,1,0:T(8,128)(2,1)S(1)}, bf16[2,2048,128]{2,1,0:T(8,128)(2,1)}, u32[]{:S(2)}) copy-start(bf16[2,2048,128]{2,1,0:T(8,128)(2,1)} %kv0.5) | copy-start | bytes 3145732
  19.2 3.4 %copy-start.2 = (bf16[2,2048,128]{2,1,0:T(8,128)(2,1)S(1)}, bf16[2,2048,128]{2,1,0:T(8,128)(2,1)}, u32[]{:S(2)}) copy-start(bf16[2,2048,128]{2,1,0:T(8,128)(2,1)} %kv0.5) | copy-start | bytes 3145732
  21.1 5.0 %collective-permute-start.6 = (bf16[37,16,128]{2,1,0:T(8,128)(2,1)S(1)}, bf16[37,16,128]{2,1,0:T(8,128)(2,1)S(1)}, u32[]{:S(2)}, u32[]{:S(2)}) collective-permute-start(bf16[37,16,128]{2,1,0:T(8,128)(2,1)S(1)} %collective-permute-done.3.qb), channel_id=1, source_target_pairs={{0,16},{8,24},{16,0},{24,8},{32,48},{40,56},{48,32},{56,40},{64,80... | collective-permute-start | bytes 454664 | tf_op jit(solution)/shard_map/ppermute | solution.py:448
  26.0 7.0 %copy-start.4 = (bf16[18,16,128]{2,1,0:T(8,128)(2,1)S(1)}, bf16[18,16,128]{2,1,0:T(8,128)(2,1)}, u32[]{:S(2)}) copy-start(bf16[18,16,128]{2,1,0:T(8,128)(2,1)} %get-tuple-element.30.a0.s0) | copy-start | bytes 221188
  26.1 5.3 %collective-permute-start.8 = (bf16[4,16,128]{2,1,0:T(8,128)(2,1)S(1)}, bf16[4,16,128]{2,1,0:T(8,128)(2,1)S(1)}, u32[]{:S(2)}, u32[]{:S(2)}) collective-permute-start(bf16[4,16,128]{2,1,0:T(8,128)(2,1)S(1)} %pad_maximum_fusion.2), channel_id=1, source_target_pairs={{0,8},{8,0},{16,24},{24,16},{32,40},{40,32},{48,56},{56,48},{64,72... | collective-permute-start | bytes 49160 | tf_op jit(solution)/shard_map/ppermute | solution.py:448
  28.1 4.9 %collective-permute-start.7 = (bf16[33,16,128]{2,1,0:T(8,128)(2,1)S(1)}, bf16[33,16,128]{2,1,0:T(8,128)(2,1)S(1)}, u32[]{:S(2)}, u32[]{:S(2)}) collective-permute-start(bf16[33,16,128]{2,1,0:T(8,128)(2,1)S(1)} %prefix_send.1), channel_id=1, source_target_pairs={{0,16},{8,24},{16,0},{24,8},{32,48},{40,56},{48,32},{56,40},{64,80... | collective-permute-start | bytes 405512 | tf_op jit(solution)/shard_map/ppermute | solution.py:448
  33.7 4.0 %collective-permute-start.9 = (bf16[32,2048]{1,0:T(8,128)(2,1)S(1)}, bf16[32,2048]{1,0:T(8,128)(2,1)S(1)}, u32[]{:S(2)}, u32[]{:S(2)}) collective-permute-start(bf16[32,2048]{1,0:T(8,128)(2,1)S(1)} %combine.1), channel_id=1, source_target_pairs={{0,64},{8,24},{16,80},{24,8},{32,96},{40,56},{48,112},{56,40},{64,... | collective-permute-start | bytes 393224 | tf_op jit(solution)/shard_map/ppermute | solution.py:465
  35.2 6.5 %collective-permute-start.10 = (bf16[32,2048]{1,0:T(8,128)(2,1)S(1)}, bf16[32,2048]{1,0:T(8,128)(2,1)S(1)}, u32[]{:S(2)}, u32[]{:S(2)}) collective-permute-start(bf16[32,2048]{1,0:T(8,128)(2,1)S(1)} %combine.1), channel_id=1, source_target_pairs={{0,128},{8,40},{16,144},{24,56},{32,160},{40,8},{48,176},{56,24},{... | collective-permute-start | bytes 393224 | tf_op jit(solution)/shard_map/ppermute | solution.py:465
  37.7 5.5 %collective-permute-start.11 = (bf16[32,2048]{1,0:T(8,128)(2,1)S(1)}, bf16[32,2048]{1,0:T(8,128)(2,1)S(1)}, u32[]{:S(2)}, u32[]{:S(2)}) collective-permute-start(bf16[32,2048]{1,0:T(8,128)(2,1)S(1)} %combine.1), channel_id=1, source_target_pairs={{0,192},{8,56},{16,208},{24,40},{32,224},{40,24},{48,240},{56,8},{... | collective-permute-start | bytes 393224 | tf_op jit(solution)/shard_map/ppermute | solution.py:465
  37.7 16.6 %copy-start.5 = (bf16[32,2048]{1,0:T(8,128)(2,1)}, bf16[32,2048]{1,0:T(8,128)(2,1)S(1)}, u32[]{:S(2)}) copy-start(bf16[32,2048]{1,0:T(8,128)(2,1)S(1)} %collective-permute-done.9) | copy-start | bytes 393220
  41.7 12.7 %copy-start.6 = (bf16[32,2048]{1,0:T(8,128)(2,1)}, bf16[32,2048]{1,0:T(8,128)(2,1)S(1)}, u32[]{:S(2)}) copy-start(bf16[32,2048]{1,0:T(8,128)(2,1)S(1)} %collective-permute-done.10) | copy-start | bytes 393220
  43.1 11.3 %copy-start.7 = (bf16[32,2048]{1,0:T(8,128)(2,1)}, bf16[32,2048]{1,0:T(8,128)(2,1)S(1)}, u32[]{:S(2)}) copy-start(bf16[32,2048]{1,0:T(8,128)(2,1)S(1)} %collective-permute-done.11) | copy-start | bytes 393220
  43.2 8.2 %collective-permute-start.12 = (bf16[96,2048]{1,0:T(8,128)(2,1)S(1)}, bf16[96,2048]{1,0:T(8,128)(2,1)S(1)}, u32[]{:S(2)}, u32[]{:S(2)}) collective-permute-start(bf16[96,2048]{1,0:T(8,128)(2,1)S(1)} %pad_maximum_fusion.a), channel_id=1, source_target_pairs={{0,48},{8,200},{16,32},{24,216},{32,16},{40,232},{48,0},{56,248},{... | collective-permute-start | bytes 1179656 | tf_op jit(solution)/shard_map/ppermute | solution.py:465
  44.6 6.9 %collective-permute-start.14 = (bf16[96,2048]{1,0:T(8,128)(2,1)S(1)}, bf16[96,2048]{1,0:T(8,128)(2,1)S(1)}, u32[]{:S(2)}, u32[]{:S(2)}) collective-permute-start(bf16[96,2048]{1,0:T(8,128)(2,1)S(1)} %pad_maximum_fusion.a), channel_id=1, source_target_pairs={{0,16},{8,72},{16,0},{24,88},{32,48},{40,104},{48,32},{56,120},{64... | collective-permute-start | bytes 1179656 | tf_op jit(solution)/shard_map/ppermute | solution.py:465
  51.4 4.6 %collective-permute-start.13 = (bf16[48,2048]{1,0:T(8,128)(2,1)S(1)}, bf16[48,2048]{1,0:T(8,128)(2,1)S(1)}, u32[]{:S(2)}, u32[]{:S(2)}) collective-permute-start(bf16[48,2048]{1,0:T(8,128)(2,1)S(1)} %slice.70), channel_id=1, source_target_pairs={{0,16},{8,72},{16,0},{24,88},{32,48},{40,104},{48,32},{56,120},{64... | collective-permute-start | bytes 589832 | tf_op jit(solution)/shard_map/ppermute | solution.py:465
  51.5 5.8 %collective-permute-start.15 = (bf16[48,2048]{1,0:T(8,128)(2,1)S(1)}, bf16[48,2048]{1,0:T(8,128)(2,1)S(1)}, u32[]{:S(2)}, u32[]{:S(2)}) collective-permute-start(bf16[48,2048]{1,0:T(8,128)(2,1)S(1)} %slice.71), channel_id=1, source_target_pairs={{0,48},{8,200},{16,32},{24,216},{32,16},{40,232},{48,0},{56,248},{... | collective-permute-start | bytes 589832 | tf_op jit(solution)/shard_map/ppermute | solution.py:465
  56.0 7.9 %slice-start = ((bf16[32,2048]{1,0:T(8,128)(2,1)}), bf16[8,2048]{1,0:T(8,128)(2,1)S(1)}, s32[]{:S(2)}) async-start(bf16[32,2048]{1,0:T(8,128)(2,1)} %copy-done.5), calls=%async_computation | async-start | bytes 65536 | tf_op jit(solution)/shard_map/slice | solution.py:501
  56.0 7.9 %slice-start.1 = ((bf16[32,2048]{1,0:T(8,128)(2,1)}), bf16[8,2048]{1,0:T(8,128)(2,1)S(1)}, s32[]{:S(2)}) async-start(bf16[32,2048]{1,0:T(8,128)(2,1)} %copy-done.6), calls=%async_computation.1 | async-start | bytes 65536 | tf_op jit(solution)/shard_map/slice | solution.py:501
  56.0 7.9 %slice-start.2 = ((bf16[32,2048]{1,0:T(8,128)(2,1)}), bf16[8,2048]{1,0:T(8,128)(2,1)S(1)}, s32[]{:S(2)}) async-start(bf16[32,2048]{1,0:T(8,128)(2,1)} %copy-done.7), calls=%async_computation.2 | async-start | bytes 65536 | tf_op jit(solution)/shard_map/slice | solution.py:501
  58.2 17.9 %collective-permute-start.17 = (bf16[2,64,1024]{2,1,0:T(8,128)(2,1)S(1)}, bf16[2,64,1024]{2,1,0:T(8,128)(2,1)S(1)}, u32[]{:S(2)}, u32[]{:S(2)}) collective-permute-start(bf16[2,64,1024]{2,1,0:T(8,128)(2,1)S(1)} %get-tuple-element.46), channel_id=1, source_target_pairs={{0,1},{1,2},{2,3},{3,4},{4,5},{5,6},{6,7},{7,0},{8,9},{9,10},{10,1... | collective-permute-start | bytes 786440 | tf_op jit(solution)/shard_map/ppermute | solution.py:476
  59.9 16.2 %collective-permute-start.18 = (bf16[2,64,1024]{2,1,0:T(8,128)(2,1)S(1)}, bf16[2,64,1024]{2,1,0:T(8,128)(2,1)S(1)}, u32[]{:S(2)}, u32[]{:S(2)}) collective-permute-start(bf16[2,64,1024]{2,1,0:T(8,128)(2,1)S(1)} %get-tuple-element.47), channel_id=1, source_target_pairs={{0,7},{1,0},{2,1},{3,2},{4,3},{5,4},{6,5},{7,6},{8,15},{9,8},{10,9... | collective-permute-start | bytes 786440 | tf_op jit(solution)/shard_map/ppermute | solution.py:476
  64.0 5.1 %collective-permute-start.19 = (bf16[32,2048]{1,0:T(8,128)(2,1)S(1)}, bf16[32,2048]{1,0:T(8,128)(2,1)S(1)}, u32[]{:S(2)}, u32[]{:S(2)}) collective-permute-start(bf16[32,2048]{1,0:T(8,128)(2,1)S(1)} %pad_maximum_fusion.1.a), channel_id=1, source_target_pairs={{0,48},{8,200},{16,32},{24,216},{32,16},{40,232},{48,0},{56,248},{... | collective-permute-start | bytes 393224 | tf_op jit(solution)/shard_map/ppermute | solution.py:465
  65.4 4.1 %collective-permute-start.21 = (bf16[32,2048]{1,0:T(8,128)(2,1)S(1)}, bf16[32,2048]{1,0:T(8,128)(2,1)S(1)}, u32[]{:S(2)}, u32[]{:S(2)}) collective-permute-start(bf16[32,2048]{1,0:T(8,128)(2,1)S(1)} %pad_maximum_fusion.1.a), channel_id=1, source_target_pairs={{0,16},{8,72},{16,0},{24,88},{32,48},{40,104},{48,32},{56,120},{64... | collective-permute-start | bytes 393224 | tf_op jit(solution)/shard_map/ppermute | solution.py:465
  69.1 6.2 %collective-permute-start.20 = (bf16[16,2048]{1,0:T(8,128)(2,1)S(1)}, bf16[16,2048]{1,0:T(8,128)(2,1)S(1)}, u32[]{:S(2)}, u32[]{:S(2)}) collective-permute-start(bf16[16,2048]{1,0:T(8,128)(2,1)S(1)} %slice.76), channel_id=1, source_target_pairs={{0,16},{8,72},{16,0},{24,88},{32,48},{40,104},{48,32},{56,120},{64... | collective-permute-start | bytes 196616 | tf_op jit(solution)/shard_map/ppermute | solution.py:465
  69.5 5.8 %collective-permute-start.22 = (bf16[16,2048]{1,0:T(8,128)(2,1)S(1)}, bf16[16,2048]{1,0:T(8,128)(2,1)S(1)}, u32[]{:S(2)}, u32[]{:S(2)}) collective-permute-start(bf16[16,2048]{1,0:T(8,128)(2,1)S(1)} %slice.77), channel_id=1, source_target_pairs={{0,48},{8,200},{16,32},{24,216},{32,16},{40,232},{48,0},{56,248},{... | collective-permute-start | bytes 196616 | tf_op jit(solution)/shard_map/ppermute | solution.py:465
  70.8 9.3 %collective-permute-start.25 = (bf16[64,1024]{1,0:T(8,128)(2,1)S(1)}, bf16[64,1024]{1,0:T(8,128)(2,1)S(1)}, u32[]{:S(2)}, u32[]{:S(2)}) collective-permute-start(bf16[64,1024]{1,0:T(8,128)(2,1)S(1)} %get-tuple-element.52), channel_id=1, source_target_pairs={{0,4},{1,5},{2,6},{3,7},{4,0},{5,1},{6,2},{7,3},{8,12},{9,13},{10,... | collective-permute-start | bytes 393224 | tf_op jit(solution)/shard_map/ppermute | solution.py:476
  76.2 10.0 %collective-permute-start.23 = (bf16[64,1024]{1,0:T(8,128)(2,1)S(1)}, bf16[64,1024]{1,0:T(8,128)(2,1)S(1)}, u32[]{:S(2)}, u32[]{:S(2)}) collective-permute-start(bf16[64,1024]{1,0:T(8,128)(2,1)S(1)} %get-tuple-element.50), channel_id=1, source_target_pairs={{0,2},{1,3},{2,4},{3,5},{4,6},{5,7},{6,0},{7,1},{8,10},{9,11},{10,... | collective-permute-start | bytes 393224 | tf_op jit(solution)/shard_map/ppermute | solution.py:476
  76.3 9.9 %collective-permute-start.24 = (bf16[64,1024]{1,0:T(8,128)(2,1)S(1)}, bf16[64,1024]{1,0:T(8,128)(2,1)S(1)}, u32[]{:S(2)}, u32[]{:S(2)}) collective-permute-start(bf16[64,1024]{1,0:T(8,128)(2,1)S(1)} %get-tuple-element.51), channel_id=1, source_target_pairs={{0,6},{1,7},{2,0},{3,1},{4,2},{5,3},{6,4},{7,5},{8,14},{9,15},{10,... | collective-permute-start | bytes 393224 | tf_op jit(solution)/shard_map/ppermute | solution.py:476
  86.3 6.6 %collective-permute-start.26 = (bf16[64,512]{1,0:T(8,128)(2,1)S(1)}, bf16[64,512]{1,0:T(8,128)(2,1)S(1)}, u32[]{:S(2)}, u32[]{:S(2)}) collective-permute-start(bf16[64,512]{1,0:T(8,128)(2,1)S(1)} %get-tuple-element.54), channel_id=1, source_target_pairs={{0,8},{8,0},{16,24},{24,16},{32,40},{40,32},{48,56},{56,48},{64,72... | collective-permute-start | bytes 196616 | tf_op jit(solution)/shard_map/ppermute | solution.py:448

commit v12 on v11

--- a/solution.py
+++ b/solution.py
@@ -258,7 +258,7 @@
 
 
 def combine_body(
-    own, own_masses, cross, cross_masses, message, s0, s1, s2, s3, far, after, out, held
+    own, own_masses, cross, cross_masses, message, s0, s1, s2, s3, far, out, held
 ):
     x, y, _, z = position()
     y_high = y >> 1
@@ -289,16 +289,16 @@
         out[:, h * DH : (h + 1) * DH] = held[:, h, :].astype(BF16)
 
 
-def combine(own, cross, message, near, far, after):
+def combine(own, cross, message, near, far):
     return pl.pallas_call(
         combine_body,
         out_shape=jax.ShapeDtypeStruct((32, GROUP * DH), BF16),
-        in_specs=[VMEM] * 10 + [ANY],
+        in_specs=[VMEM] * 10,
         out_specs=VMEM,
         scratch_shapes=[pltpu.VMEM((32, GROUP, DH), F32)],
         compiler_params=params(),
         name="combine",
-    )(*own, *cross, message, *near, far, after)
+    )(*own, *cross, message, *near, far)
 
 
 def by_target(total, count):
@@ -492,16 +492,19 @@
     message, from2 = lax.optimization_barrier((message, from2))
     message = along_y(message, 1)
     cross = prefix_keep(from2, prefix_kv, prefix_other)
+    attended = combine(own, cross, message, by_x, from2)
     orders = jnp.stack([same[16], from1[16], from2[16], from3[16]])
     orders = jnp.concatenate([orders, other_core(orders)], axis=0)
     pick = order_rows(orders)
-    attended = combine(own, cross, message, by_x, from2, pick)
 
     parts = [attended] + [turned(attended, k, 0) for k in (1, 2, 3)]
     far, near = gathered([a[:24] for a in parts]), gathered([a[24:] for a in parts])
-    first_far, first_near = project(far[:3], weights), project(near[:3], weights)
+    first_far = project(far[:3], weights)
+    three, first_far = lax.optimization_barrier((near[:3], first_far))
+    first_near = project(three, weights)
+    last_far, first_near = lax.optimization_barrier((far[3], first_near))
     keep0, up, down, direct = plain(
-        far_body, [SUM, TWO, TWO, SENT], *far[3], *weights, first_far
+        far_body, [SUM, TWO, TWO, SENT], *last_far, *weights, first_far
     )
     below, above = along_z(up, 1), along_z(down, -1)
     opposite = along_z(direct, 4)

time: 94 us -> 91.7 us (0.976)
  the two profiles are of different devices: /device:TPU:1 before, /device:TPU:33 now
where the time goes in v12:
time: 91.7 us; the launch traced here: 91.5 us
  starting transfers between devices  53.1 us (58%)
  waiting for transfers between devices  20.9 us (23%)
  Pallas kernels  16.2 us (18%)
  local copies, waits for them, and re-layouts  1.02 us (1%)
    ppermute x11, starting transfers between devices, along(): lax.ppermute(value, 'batch', [(i, i ^ k << shift) for i in range(BATCH)])  30.3 us
    ppermute x11, waiting for transfers between devices, turned(): return lax.ppermute(value, 'batch', pairs)  12.4 us
    ppermute x11, starting transfers between devices, turned(): return lax.ppermute(value, 'batch', pairs)  11.6 us
    ppermute x5, starting transfers between devices, along_z(): lax.ppermute(value, 'head', [(i, (i + k) % HEADS) for i in range(HEADS)])  11.2 us
    ppermute x11, waiting for transfers between devices, along(): lax.ppermute(value, 'batch', [(i, i ^ k << shift) for i in range(BATCH)])  8.46 us
    pallas_call x2, Pallas kernels, prefix_keep(): pl.pallas_call(prefix_keep_body, out_shape=[out, out], in_specs=[VMEM] *...  3.68 us
    pallas_call x1, Pallas kernels, local_parts(): pl.pallas_call(local_body, out_shape=[out] * 4, in_specs=[HBM] * 6, out_s...  3.49 us
    pallas_call x1, Pallas kernels, prefix_send(): pl.pallas_call(prefix_send_body, out_shape=jax.ShapeDtypeStruct((33, GROU...  3.37 us
  transfers between devices with their start and end apart: 27, of which 12 were waited for; matrix products, arithmetic and copies ran while one was open for 0% of the time, Pallas kernels for 16%

profile of v12, /device:TPU:33, one launch (start us, length us, event | category | flops | bytes accessed | tf_op | source)
XLA Modules:
  0.0 91.5 jit_solution(4984344628238437947)
XLA Ops:
  0.0 0.7 collective-permute-start.4
  0.7 0.1 collective-permute-start.17
  0.8 3.5 %local_parts.1 = (bf16[18,16,128]{2,1,0:T(8,128)(2,1)}, bf16[18,16,128]{2,1,0:T(8,128)(2,1)}, bf16[18,16,128]{2,1,0:T(8,128)(2,1)}, bf16[18,16,128]{2,1,0:T(8,128)(2,1)}) custom-call(bf16[32,2048]{1,0:T(8,128)(2,1)} %q_in.1, s32[32]{0:T(128)} %prompt_in.1, s32[8,32]{1,0:T(8,128)} %bitcast.1, s32[32]{0:T(128)} %length_in.1, bf16[2,32,128]{2,1,0:T(8,128)(2,1)} %new_in.1, ...), custom_call_target="tpu_custom_call" | custom-call | tf_op jit(solution)/shard_map/local_parts/pallas_call | solution.py:131
  4.3 1.3 %collective-permute-start = (bf16[18,16,128]{2,1,0:T(8,128)(2,1)}, bf16[18,16,128]{2,1,0:T(8,128)(2,1)S(1)}, u32[]{:S(2)}, u32[]{:S(2)}) collective-permute-start(bf16[18,16,128]{2,1,0:T(8,128)(2,1)} %get-tuple-element.38), channel_id=1, source_target_pairs={{0,64},{8,72},{16,80},{24,88},{32,96},{40,104},{48,112},{56,120},{... | collective-permute-start | bytes 221192 | tf_op jit(solution)/shard_map/ppermute | solution.py:448
  5.6 2.4 %collective-permute-start.1 = (bf16[18,16,128]{2,1,0:T(8,128)(2,1)}, bf16[18,16,128]{2,1,0:T(8,128)(2,1)S(1)}, u32[]{:S(2)}, u32[]{:S(2)}) collective-permute-start(bf16[18,16,128]{2,1,0:T(8,128)(2,1)} %get-tuple-element.39), channel_id=1, source_target_pairs={{0,128},{8,136},{16,144},{24,152},{32,160},{40,168},{48,176},{56,1... | collective-permute-start | bytes 221192 | tf_op jit(solution)/shard_map/ppermute | solution.py:448
  8.0 0.2 collective-permute-start.2
  8.2 0.0 collective-permute-done.a1.s1
  8.2 3.2 %collective-permute-done.1.a2.s2 = bf16[18,16,128]{2,1,0:T(8,128)(2,1)S(1)} collective-permute-done((bf16[18,16,128]{2,1,0:T(8,128)(2,1)}, bf16[18,16,128]{2,1,0:T(8,128)(2,1)S(1)}, u32[]{:S(2)}, u32[]{:S(2)}) %collective-permute-start.1) | collective-permute-done | bytes 73760 | tf_op jit(solution)/shard_map/ppermute | solution.py:448
  11.5 1.7 %collective-permute-done.2.a3.s3 = bf16[18,16,128]{2,1,0:T(8,128)(2,1)S(1)} collective-permute-done((bf16[18,16,128]{2,1,0:T(8,128)(2,1)}, bf16[18,16,128]{2,1,0:T(8,128)(2,1)S(1)}, u32[]{:S(2)}, u32[]{:S(2)}) %collective-permute-start.2) | collective-permute-done | bytes 73760 | tf_op jit(solution)/shard_map/ppermute | solution.py:448
  13.1 0.9 copy-done.2
  14.0 2.8 %collective-permute-start.3 = (bf16[37,16,128]{2,1,0:T(8,128)(2,1)S(1)}, bf16[37,16,128]{2,1,0:T(8,128)(2,1)S(1)}, u32[]{:S(2)}, u32[]{:S(2)}) collective-permute-start(bf16[37,16,128]{2,1,0:T(8,128)(2,1)S(1)} %get-tuple-element.41), channel_id=1, source_target_pairs={{0,48},{8,56},{16,32},{24,40},{32,16},{40,24},{48,0},{56,8},{64,11... | collective-permute-start | bytes 454664 | tf_op jit(solution)/shard_map/ppermute | solution.py:448
  16.9 0.0 collective-permute-start.5
  16.9 0.0 collective-permute-done.4.kv1
  16.9 1.8 %prefix_keep.2 = (f32[16,16,128]{2,1,0:T(8,128)S(1)}, f32[16,16,128]{2,1,0:T(8,128)S(1)}) custom-call(bf16[17,16,128]{2,1,0:T(8,128)(2,1)S(1)} %get-tuple-element.42.q, bf16[2,2048,128]{2,1,0:T(8,128)(2,1)S(1)} %copy-done.1, bf16[2,2048,128]{2,1,0:T(8,128)(2,1)S(1)} %collective-permute-done.4.kv1), custom_call_target="tpu_custom_call" | custom-call | flops 536870912 | bytes 2500000 | tf_op jit(solution)/shard_map/prefix_keep/pallas_call | solution.py:246
  18.7 0.7 collective-permute-done.3.qb
  19.4 0.8 collective-permute-start.6
  20.3 0.0 collective-permute-done.5.qa
  20.3 3.4 %prefix_send.1 = bf16[33,16,128]{2,1,0:T(8,128)(2,1)S(1)} custom-call(bf16[17,16,128]{2,1,0:T(8,128)(2,1)S(1)} %collective-permute-done.5.qa, bf16[37,16,128]{2,1,0:T(8,128)(2,1)S(1)} %collective-permute-done.3.qb, bf16[2,2048,128]{2,1,0:T(8,128)(2,1)S(1)} %copy-done.1, bf16[2,2048,128]{2,1,0:T(8,128)(2,1)S(1)} %collective-permute-done.4.kv1, ...), custom_call_target="tpu_custom_call" | custom-call | flops 1073741824 | bytes 2500000 | tf_op jit(solution)/shard_map/prefix_send/pallas_call | solution.py:233
  23.7 0.0 copy-start.3
  23.7 0.3 collective-permute-done.6.q.far
  24.0 0.5 collective-permute-start.7
  24.6 1.8 %prefix_keep.3 = (f32[16,16,128]{2,1,0:T(8,128)S(1)}, f32[16,16,128]{2,1,0:T(8,128)S(1)}) custom-call(bf16[37,16,128]{2,1,0:T(8,128)(2,1)S(1)} %collective-permute-done.6.q.far, bf16[2,2048,128]{2,1,0:T(8,128)(2,1)S(1)} %copy-done.1, bf16[2,2048,128]{2,1,0:T(8,128)(2,1)S(1)} %collective-permute-done.4.kv1), custom_call_target="tpu_custom_call" | custom-call | flops 536870912 | bytes 2500000 | tf_op jit(solution)/shard_map/prefix_keep/pallas_call | solution.py:246
  26.4 0.0 copy-start
  26.4 1.7 %collective-permute-done.7.message = bf16[33,16,128]{2,1,0:T(8,128)(2,1)S(1)} collective-permute-done((bf16[33,16,128]{2,1,0:T(8,128)(2,1)S(1)}, bf16[33,16,128]{2,1,0:T(8,128)(2,1)S(1)}, u32[]{:S(2)}, u32[]{:S(2)}) %collective-permute-start.7) | collective-permute-done | bytes 135200 | tf_op jit(solution)/shard_map/ppermute | solution.py:448
  28.1 0.7 combine.1
  28.8 0.4 collective-permute-start.8
  29.2 3.6 %collective-permute-start.9 = (bf16[32,2048]{1,0:T(8,128)(2,1)S(1)}, bf16[32,2048]{1,0:T(8,128)(2,1)S(1)}, u32[]{:S(2)}, u32[]{:S(2)}) collective-permute-start(bf16[32,2048]{1,0:T(8,128)(2,1)S(1)} %combine.1), channel_id=1, source_target_pairs={{0,128},{8,40},{16,144},{24,56},{32,160},{40,8},{48,176},{56,24},{... | collective-permute-start | bytes 393224 | tf_op jit(solution)/shard_map/ppermute | solution.py:465
  32.8 0.0 collective-permute-start.10
  32.8 0.4 collective-permute-done.8
  33.3 4.7 %collective-permute-done.9 = bf16[32,2048]{1,0:T(8,128)(2,1)S(1)} collective-permute-done((bf16[32,2048]{1,0:T(8,128)(2,1)S(1)}, bf16[32,2048]{1,0:T(8,128)(2,1)S(1)}, u32[]{:S(2)}, u32[]{:S(2)}) %collective-permute-start.9) | collective-permute-done | bytes 131104 | tf_op jit(solution)/shard_map/ppermute | solution.py:465
  37.9 1.6 %collective-permute-done.10 = bf16[32,2048]{1,0:T(8,128)(2,1)S(1)} collective-permute-done((bf16[32,2048]{1,0:T(8,128)(2,1)S(1)}, bf16[32,2048]{1,0:T(8,128)(2,1)S(1)}, u32[]{:S(2)}, u32[]{:S(2)}) %collective-permute-start.10) | collective-permute-done | bytes 131104 | tf_op jit(solution)/shard_map/ppermute | solution.py:465
  39.6 0.1 collective-permute-start.11
  39.7 0.1 collective-permute-start.13
  39.8 1.5 %collective-permute-start.15 = (bf16[32,2048]{1,0:T(8,128)(2,1)S(1)}, bf16[32,2048]{1,0:T(8,128)(2,1)S(1)}, u32[]{:S(2)}, u32[]{:S(2)}) collective-permute-start(bf16[32,2048]{1,0:T(8,128)(2,1)S(1)} %pad_maximum_fusion.1.a), channel_id=1, source_target_pairs={{0,16},{8,72},{16,0},{24,88},{32,48},{40,104},{48,32},{56,120},{64... | collective-permute-start | bytes 393224 | tf_op jit(solution)/shard_map/ppermute | solution.py:465
  41.3 2.6 %collective-permute-start.16 = (bf16[32,2048]{1,0:T(8,128)(2,1)S(1)}, bf16[32,2048]{1,0:T(8,128)(2,1)S(1)}, u32[]{:S(2)}, u32[]{:S(2)}) collective-permute-start(bf16[32,2048]{1,0:T(8,128)(2,1)S(1)} %pad_maximum_fusion.1.a), channel_id=1, source_target_pairs={{0,48},{8,200},{16,32},{24,216},{32,16},{40,232},{48,0},{56,248},{... | collective-permute-start | bytes 393224 | tf_op jit(solution)/shard_map/ppermute | solution.py:465
  43.9 3.6 %collective-permute-done.11.c = bf16[96,2048]{1,0:T(8,128)(2,1)S(1)} collective-permute-done((bf16[96,2048]{1,0:T(8,128)(2,1)S(1)}, bf16[96,2048]{1,0:T(8,128)(2,1)S(1)}, u32[]{:S(2)}, u32[]{:S(2)}) %collective-permute-start.11) | collective-permute-done | bytes 393248 | tf_op jit(solution)/shard_map/ppermute | solution.py:465
  47.5 0.1 collective-permute-start.12
  47.6 0.0 collective-permute-done.13.b
  47.6 1.4 %collective-permute-start.14 = (bf16[48,2048]{1,0:T(8,128)(2,1)S(1)}, bf16[48,2048]{1,0:T(8,128)(2,1)S(1)}, u32[]{:S(2)}, u32[]{:S(2)}) collective-permute-start(bf16[48,2048]{1,0:T(8,128)(2,1)S(1)} %slice.69), channel_id=1, source_target_pairs={{0,48},{8,200},{16,32},{24,216},{32,16},{40,232},{48,0},{56,248},{... | collective-permute-start | bytes 589832 | tf_op jit(solution)/shard_map/ppermute | solution.py:465
  49.1 0.0 collective-permute-done.17.w1
  49.1 1.4 %project.2.first = f32[6,48,1024]{2,1,0:T(8,128)S(1)} custom-call(bf16[96,2048]{1,0:T(8,128)(2,1)S(1)} %pad_maximum_fusion.a, bf16[96,2048]{1,0:T(8,128)(2,1)S(1)} %collective-permute-done.13.b, bf16[96,2048]{1,0:T(8,128)(2,1)S(1)} %collective-permute-done.11.c, bf16[2048,512]{1,0:T(8,128)(2,1)S(1)} %copy-done, bf16[2048,512]{1,0:T(8,128)(2,1)S(1)} %collective-permute-done.17.w1), custom_call_target="tpu_custom_call" | custom-call | flops 1207959552 | bytes 4500000 | tf_op jit(solution)/shard_map/project/pallas_call | solution.py:330
  50.4 0.0 collective-permute-done.15.b
  50.5 0.0 collective-permute-done.16.c
  50.5 0.8 project.3.first
  51.3 1.1 %collective-permute-done.12.a = bf16[48,2048]{1,0:T(8,128)(2,1)S(1)} collective-permute-done((bf16[48,2048]{1,0:T(8,128)(2,1)S(1)}, bf16[48,2048]{1,0:T(8,128)(2,1)S(1)}, u32[]{:S(2)}, u32[]{:S(2)}) %collective-permute-start.12) | collective-permute-done | bytes 196640 | tf_op jit(solution)/shard_map/ppermute | solution.py:465
  52.4 1.0 %collective-permute-done.14.b = bf16[48,2048]{1,0:T(8,128)(2,1)S(1)} collective-permute-done((bf16[48,2048]{1,0:T(8,128)(2,1)S(1)}, bf16[48,2048]{1,0:T(8,128)(2,1)S(1)}, u32[]{:S(2)}, u32[]{:S(2)}) %collective-permute-start.14) | collective-permute-done | bytes 196640 | tf_op jit(solution)/shard_map/ppermute | solution.py:465
  53.4 0.8 far.1
  54.3 1.7 %collective-permute-start.18 = (bf16[2,64,1024]{2,1,0:T(8,128)(2,1)S(1)}, bf16[2,64,1024]{2,1,0:T(8,128)(2,1)S(1)}, u32[]{:S(2)}, u32[]{:S(2)}) collective-permute-start(bf16[2,64,1024]{2,1,0:T(8,128)(2,1)S(1)} %get-tuple-element.59), channel_id=1, source_target_pairs={{0,1},{1,2},{2,3},{3,4},{4,5},{5,6},{6,7},{7,0},{8,9},{9,10},{10,1... | collective-permute-start | bytes 786440 | tf_op jit(solution)/shard_map/ppermute | solution.py:476
  56.0 0.0 collective-permute-start.19
  56.0 0.6 collective-permute-start.20
  56.6 1.2 %collective-permute-start.21 = (bf16[16,2048]{1,0:T(8,128)(2,1)S(1)}, bf16[16,2048]{1,0:T(8,128)(2,1)S(1)}, u32[]{:S(2)}, u32[]{:S(2)}) collective-permute-start(bf16[16,2048]{1,0:T(8,128)(2,1)S(1)} %slice.75), channel_id=1, source_target_pairs={{0,48},{8,200},{16,32},{24,216},{32,16},{40,232},{48,0},{56,248},{... | collective-permute-start | bytes 196616 | tf_op jit(solution)/shard_map/ppermute | solution.py:465
  57.8 5.8 %collective-permute-start.24 = (bf16[64,1024]{1,0:T(8,128)(2,1)S(1)}, bf16[64,1024]{1,0:T(8,128)(2,1)S(1)}, u32[]{:S(2)}, u32[]{:S(2)}) collective-permute-start(bf16[64,1024]{1,0:T(8,128)(2,1)S(1)} %get-tuple-element.66), channel_id=1, source_target_pairs={{0,4},{1,5},{2,6},{3,7},{4,0},{5,1},{6,2},{7,3},{8,12},{9,13},{10,... | collective-permute-start | bytes 393224 | tf_op jit(solution)/shard_map/ppermute | solution.py:476
  63.7 0.0 collective-permute-done.20.a
  63.7 0.8 near.1
  64.5 0.0 collective-permute-done.18.below
  64.6 3.6 %collective-permute-start.22 = (bf16[64,1024]{1,0:T(8,128)(2,1)S(1)}, bf16[64,1024]{1,0:T(8,128)(2,1)S(1)}, u32[]{:S(2)}, u32[]{:S(2)}) collective-permute-start(bf16[64,1024]{1,0:T(8,128)(2,1)S(1)} %get-tuple-element.64), channel_id=1, source_target_pairs={{0,2},{1,3},{2,4},{3,5},{4,6},{5,7},{6,0},{7,1},{8,10},{9,11},{10,... | collective-permute-start | bytes 393224 | tf_op jit(solution)/shard_map/ppermute | solution.py:476
  68.2 0.1 collective-permute-start.23
  68.3 14.5 %collective-permute-start.26 = (bf16[4,16,128]{2,1,0:T(8,128)(2,1)S(1)}, bf16[4,16,128]{2,1,0:T(8,128)(2,1)S(1)}, u32[]{:S(2)}, u32[]{:S(2)}) collective-permute-start(bf16[4,16,128]{2,1,0:T(8,128)(2,1)S(1)} %pad_maximum_fusion.2), channel_id=1, source_target_pairs={{0,8},{8,0},{16,24},{24,16},{32,40},{40,32},{48,56},{56,48},{64,72... | collective-permute-start | bytes 49160 | tf_op jit(solution)/shard_map/ppermute | solution.py:448
  82.8 0.0 collective-permute-done.24.opposite
  82.8 0.1 total.1
  82.9 6.8 %collective-permute-start.25 = (bf16[64,512]{1,0:T(8,128)(2,1)S(1)}, bf16[64,512]{1,0:T(8,128)(2,1)S(1)}, u32[]{:S(2)}, u32[]{:S(2)}) collective-permute-start(bf16[64,512]{1,0:T(8,128)(2,1)S(1)} %get-tuple-element.68), channel_id=1, source_target_pairs={{0,8},{8,0},{16,24},{24,16},{32,40},{40,32},{48,56},{56,48},{64,72... | collective-permute-start | bytes 196616 | tf_op jit(solution)/shard_map/ppermute | solution.py:448
  89.7 0.1 order_rows.1.pick
  89.8 0.8 collective-permute-done.25.other
  90.6 0.9 finish.1
  (32 shorter events, 0.3 us)
Async XLA Ops:
  0.0 16.9 %copy-start.1 = (bf16[2,2048,128]{2,1,0:T(8,128)(2,1)S(1)}, bf16[2,2048,128]{2,1,0:T(8,128)(2,1)}, u32[]{:S(2)}) copy-start(bf16[2,2048,128]{2,1,0:T(8,128)(2,1)} %kv0.5) | copy-start | bytes 3145732
  0.0 16.9 %collective-permute-start.4 = (bf16[2,2048,128]{2,1,0:T(8,128)(2,1)}, bf16[2,2048,128]{2,1,0:T(8,128)(2,1)S(1)}, u32[]{:S(2)}, u32[]{:S(2)}) collective-permute-start(bf16[2,2048,128]{2,1,0:T(8,128)(2,1)} %kv0.5), channel_id=1, source_target_pairs={{0,8},{8,0},{16,24},{24,16},{32,40},{40,32},{48,56},{56,48},{64,72... | collective-permute-start | bytes 3145736 | tf_op jit(solution)/shard_map/ppermute | solution.py:448
  0.7 48.4 %collective-permute-start.17 = (bf16[2048,512]{1,0:T(8,128)(2,1)}, bf16[2048,512]{1,0:T(8,128)(2,1)S(1)}, u32[]{:S(2)}, u32[]{:S(2)}) collective-permute-start(bf16[2048,512]{1,0:T(8,128)(2,1)} %w0.7), channel_id=1, source_target_pairs={{0,8},{8,0},{16,24},{24,16},{32,40},{40,32},{48,56},{56,48},{64,72... | collective-permute-start | bytes 6291464 | tf_op jit(solution)/shard_map/ppermute | solution.py:448
  4.3 3.9 %collective-permute-start = (bf16[18,16,128]{2,1,0:T(8,128)(2,1)}, bf16[18,16,128]{2,1,0:T(8,128)(2,1)S(1)}, u32[]{:S(2)}, u32[]{:S(2)}) collective-permute-start(bf16[18,16,128]{2,1,0:T(8,128)(2,1)} %get-tuple-element.38), channel_id=1, source_target_pairs={{0,64},{8,72},{16,80},{24,88},{32,96},{40,104},{48,112},{56,120},{... | collective-permute-start | bytes 221192 | tf_op jit(solution)/shard_map/ppermute | solution.py:448
  5.6 5.9 %collective-permute-start.1 = (bf16[18,16,128]{2,1,0:T(8,128)(2,1)}, bf16[18,16,128]{2,1,0:T(8,128)(2,1)S(1)}, u32[]{:S(2)}, u32[]{:S(2)}) collective-permute-start(bf16[18,16,128]{2,1,0:T(8,128)(2,1)} %get-tuple-element.39), channel_id=1, source_target_pairs={{0,128},{8,136},{16,144},{24,152},{32,160},{40,168},{48,176},{56,1... | collective-permute-start | bytes 221192 | tf_op jit(solution)/shard_map/ppermute | solution.py:448
  8.0 5.1 %collective-permute-start.2 = (bf16[18,16,128]{2,1,0:T(8,128)(2,1)}, bf16[18,16,128]{2,1,0:T(8,128)(2,1)S(1)}, u32[]{:S(2)}, u32[]{:S(2)}) collective-permute-start(bf16[18,16,128]{2,1,0:T(8,128)(2,1)} %get-tuple-element.40), channel_id=1, source_target_pairs={{0,192},{8,200},{16,208},{24,216},{32,224},{40,232},{48,240},{56,2... | collective-permute-start | bytes 221192 | tf_op jit(solution)/shard_map/ppermute | solution.py:448
  13.1 0.9 copy-start.2
  14.0 5.4 %collective-permute-start.3 = (bf16[37,16,128]{2,1,0:T(8,128)(2,1)S(1)}, bf16[37,16,128]{2,1,0:T(8,128)(2,1)S(1)}, u32[]{:S(2)}, u32[]{:S(2)}) collective-permute-start(bf16[37,16,128]{2,1,0:T(8,128)(2,1)S(1)} %get-tuple-element.41), channel_id=1, source_target_pairs={{0,48},{8,56},{16,32},{24,40},{32,16},{40,24},{48,0},{56,8},{64,11... | collective-permute-start | bytes 454664 | tf_op jit(solution)/shard_map/ppermute | solution.py:448
  16.9 3.5 %collective-permute-start.5 = (bf16[17,16,128]{2,1,0:T(8,128)(2,1)S(1)}, bf16[17,16,128]{2,1,0:T(8,128)(2,1)S(1)}, u32[]{:S(2)}, u32[]{:S(2)}) collective-permute-start(bf16[17,16,128]{2,1,0:T(8,128)(2,1)S(1)} %get-tuple-element.42.q), channel_id=1, source_target_pairs={{0,16},{8,24},{16,0},{24,8},{32,48},{40,56},{48,32},{56,40},{64,80... | collective-permute-start | bytes 208904 | tf_op jit(solution)/shard_map/ppermute | solution.py:448
  19.4 4.6 %collective-permute-start.6 = (bf16[37,16,128]{2,1,0:T(8,128)(2,1)S(1)}, bf16[37,16,128]{2,1,0:T(8,128)(2,1)S(1)}, u32[]{:S(2)}, u32[]{:S(2)}) collective-permute-start(bf16[37,16,128]{2,1,0:T(8,128)(2,1)S(1)} %collective-permute-done.3.qb), channel_id=1, source_target_pairs={{0,16},{8,24},{16,0},{24,8},{32,48},{40,56},{48,32},{56,40},{64,80... | collective-permute-start | bytes 454664 | tf_op jit(solution)/shard_map/ppermute | solution.py:448
  23.7 4.4 %copy-start.3 = (bf16[18,16,128]{2,1,0:T(8,128)(2,1)S(1)}, bf16[18,16,128]{2,1,0:T(8,128)(2,1)}, u32[]{:S(2)}) copy-start(bf16[18,16,128]{2,1,0:T(8,128)(2,1)} %get-tuple-element.37.a0.s0) | copy-start | bytes 221188
  24.0 4.1 %collective-permute-start.7 = (bf16[33,16,128]{2,1,0:T(8,128)(2,1)S(1)}, bf16[33,16,128]{2,1,0:T(8,128)(2,1)S(1)}, u32[]{:S(2)}, u32[]{:S(2)}) collective-permute-start(bf16[33,16,128]{2,1,0:T(8,128)(2,1)S(1)} %prefix_send.1), channel_id=1, source_target_pairs={{0,16},{8,24},{16,0},{24,8},{32,48},{40,56},{48,32},{56,40},{64,80... | collective-permute-start | bytes 405512 | tf_op jit(solution)/shard_map/ppermute | solution.py:448
  26.4 22.6 %copy-start = (bf16[2048,512]{1,0:T(8,128)(2,1)S(1)}, bf16[2048,512]{1,0:T(8,128)(2,1)}, u32[]{:S(2)}) copy-start(bf16[2048,512]{1,0:T(8,128)(2,1)} %w0.7) | copy-start | bytes 6291460
  28.8 4.5 %collective-permute-start.8 = (bf16[32,2048]{1,0:T(8,128)(2,1)S(1)}, bf16[32,2048]{1,0:T(8,128)(2,1)S(1)}, u32[]{:S(2)}, u32[]{:S(2)}) collective-permute-start(bf16[32,2048]{1,0:T(8,128)(2,1)S(1)} %combine.1), channel_id=1, source_target_pairs={{0,64},{8,24},{16,80},{24,8},{32,96},{40,56},{48,112},{56,40},{64,... | collective-permute-start | bytes 393224 | tf_op jit(solution)/shard_map/ppermute | solution.py:465
  29.2 8.7 %collective-permute-start.9 = (bf16[32,2048]{1,0:T(8,128)(2,1)S(1)}, bf16[32,2048]{1,0:T(8,128)(2,1)S(1)}, u32[]{:S(2)}, u32[]{:S(2)}) collective-permute-start(bf16[32,2048]{1,0:T(8,128)(2,1)S(1)} %combine.1), channel_id=1, source_target_pairs={{0,128},{8,40},{16,144},{24,56},{32,160},{40,8},{48,176},{56,24},{... | collective-permute-start | bytes 393224 | tf_op jit(solution)/shard_map/ppermute | solution.py:465
  32.8 6.7 %collective-permute-start.10 = (bf16[32,2048]{1,0:T(8,128)(2,1)S(1)}, bf16[32,2048]{1,0:T(8,128)(2,1)S(1)}, u32[]{:S(2)}, u32[]{:S(2)}) collective-permute-start(bf16[32,2048]{1,0:T(8,128)(2,1)S(1)} %combine.1), channel_id=1, source_target_pairs={{0,192},{8,56},{16,208},{24,40},{32,224},{40,24},{48,240},{56,8},{... | collective-permute-start | bytes 393224 | tf_op jit(solution)/shard_map/ppermute | solution.py:465
  39.6 7.9 %collective-permute-start.11 = (bf16[96,2048]{1,0:T(8,128)(2,1)S(1)}, bf16[96,2048]{1,0:T(8,128)(2,1)S(1)}, u32[]{:S(2)}, u32[]{:S(2)}) collective-permute-start(bf16[96,2048]{1,0:T(8,128)(2,1)S(1)} %pad_maximum_fusion.a), channel_id=1, source_target_pairs={{0,48},{8,200},{16,32},{24,216},{32,16},{40,232},{48,0},{56,248},{... | collective-permute-start | bytes 1179656 | tf_op jit(solution)/shard_map/ppermute | solution.py:465
  39.7 7.9 %collective-permute-start.13 = (bf16[96,2048]{1,0:T(8,128)(2,1)S(1)}, bf16[96,2048]{1,0:T(8,128)(2,1)S(1)}, u32[]{:S(2)}, u32[]{:S(2)}) collective-permute-start(bf16[96,2048]{1,0:T(8,128)(2,1)S(1)} %pad_maximum_fusion.a), channel_id=1, source_target_pairs={{0,16},{8,72},{16,0},{24,88},{32,48},{40,104},{48,32},{56,120},{64... | collective-permute-start | bytes 1179656 | tf_op jit(solution)/shard_map/ppermute | solution.py:465
  39.8 10.6 %collective-permute-start.15 = (bf16[32,2048]{1,0:T(8,128)(2,1)S(1)}, bf16[32,2048]{1,0:T(8,128)(2,1)S(1)}, u32[]{:S(2)}, u32[]{:S(2)}) collective-permute-start(bf16[32,2048]{1,0:T(8,128)(2,1)S(1)} %pad_maximum_fusion.1.a), channel_id=1, source_target_pairs={{0,16},{8,72},{16,0},{24,88},{32,48},{40,104},{48,32},{56,120},{64... | collective-permute-start | bytes 393224 | tf_op jit(solution)/shard_map/ppermute | solution.py:465
  41.3 9.1 %collective-permute-start.16 = (bf16[32,2048]{1,0:T(8,128)(2,1)S(1)}, bf16[32,2048]{1,0:T(8,128)(2,1)S(1)}, u32[]{:S(2)}, u32[]{:S(2)}) collective-permute-start(bf16[32,2048]{1,0:T(8,128)(2,1)S(1)} %pad_maximum_fusion.1.a), channel_id=1, source_target_pairs={{0,48},{8,200},{16,32},{24,216},{32,16},{40,232},{48,0},{56,248},{... | collective-permute-start | bytes 393224 | tf_op jit(solution)/shard_map/ppermute | solution.py:465
  47.5 4.9 %collective-permute-start.12 = (bf16[48,2048]{1,0:T(8,128)(2,1)S(1)}, bf16[48,2048]{1,0:T(8,128)(2,1)S(1)}, u32[]{:S(2)}, u32[]{:S(2)}) collective-permute-start(bf16[48,2048]{1,0:T(8,128)(2,1)S(1)} %slice.68), channel_id=1, source_target_pairs={{0,16},{8,72},{16,0},{24,88},{32,48},{40,104},{48,32},{56,120},{64... | collective-permute-start | bytes 589832 | tf_op jit(solution)/shard_map/ppermute | solution.py:465
  47.6 5.8 %collective-permute-start.14 = (bf16[48,2048]{1,0:T(8,128)(2,1)S(1)}, bf16[48,2048]{1,0:T(8,128)(2,1)S(1)}, u32[]{:S(2)}, u32[]{:S(2)}) collective-permute-start(bf16[48,2048]{1,0:T(8,128)(2,1)S(1)} %slice.69), channel_id=1, source_target_pairs={{0,48},{8,200},{16,32},{24,216},{32,16},{40,232},{48,0},{56,248},{... | collective-permute-start | bytes 589832 | tf_op jit(solution)/shard_map/ppermute | solution.py:465
  54.3 10.2 %collective-permute-start.18 = (bf16[2,64,1024]{2,1,0:T(8,128)(2,1)S(1)}, bf16[2,64,1024]{2,1,0:T(8,128)(2,1)S(1)}, u32[]{:S(2)}, u32[]{:S(2)}) collective-permute-start(bf16[2,64,1024]{2,1,0:T(8,128)(2,1)S(1)} %get-tuple-element.59), channel_id=1, source_target_pairs={{0,1},{1,2},{2,3},{3,4},{4,5},{5,6},{6,7},{7,0},{8,9},{9,10},{10,1... | collective-permute-start | bytes 786440 | tf_op jit(solution)/shard_map/ppermute | solution.py:476
  56.0 8.5 %collective-permute-start.19 = (bf16[2,64,1024]{2,1,0:T(8,128)(2,1)S(1)}, bf16[2,64,1024]{2,1,0:T(8,128)(2,1)S(1)}, u32[]{:S(2)}, u32[]{:S(2)}) collective-permute-start(bf16[2,64,1024]{2,1,0:T(8,128)(2,1)S(1)} %get-tuple-element.60), channel_id=1, source_target_pairs={{0,7},{1,0},{2,1},{3,2},{4,3},{5,4},{6,5},{7,6},{8,15},{9,8},{10,9... | collective-permute-start | bytes 786440 | tf_op jit(solution)/shard_map/ppermute | solution.py:476
  56.0 7.7 %collective-permute-start.20 = (bf16[16,2048]{1,0:T(8,128)(2,1)S(1)}, bf16[16,2048]{1,0:T(8,128)(2,1)S(1)}, u32[]{:S(2)}, u32[]{:S(2)}) collective-permute-start(bf16[16,2048]{1,0:T(8,128)(2,1)S(1)} %slice.74), channel_id=1, source_target_pairs={{0,16},{8,72},{16,0},{24,88},{32,48},{40,104},{48,32},{56,120},{64... | collective-permute-start | bytes 196616 | tf_op jit(solution)/shard_map/ppermute | solution.py:465
  56.6 7.1 %collective-permute-start.21 = (bf16[16,2048]{1,0:T(8,128)(2,1)S(1)}, bf16[16,2048]{1,0:T(8,128)(2,1)S(1)}, u32[]{:S(2)}, u32[]{:S(2)}) collective-permute-start(bf16[16,2048]{1,0:T(8,128)(2,1)S(1)} %slice.75), channel_id=1, source_target_pairs={{0,48},{8,200},{16,32},{24,216},{32,16},{40,232},{48,0},{56,248},{... | collective-permute-start | bytes 196616 | tf_op jit(solution)/shard_map/ppermute | solution.py:465
  57.8 25.0 %collective-permute-start.24 = (bf16[64,1024]{1,0:T(8,128)(2,1)S(1)}, bf16[64,1024]{1,0:T(8,128)(2,1)S(1)}, u32[]{:S(2)}, u32[]{:S(2)}) collective-permute-start(bf16[64,1024]{1,0:T(8,128)(2,1)S(1)} %get-tuple-element.66), channel_id=1, source_target_pairs={{0,4},{1,5},{2,6},{3,7},{4,0},{5,1},{6,2},{7,3},{8,12},{9,13},{10,... | collective-permute-start | bytes 393224 | tf_op jit(solution)/shard_map/ppermute | solution.py:476
  64.6 18.2 %collective-permute-start.22 = (bf16[64,1024]{1,0:T(8,128)(2,1)S(1)}, bf16[64,1024]{1,0:T(8,128)(2,1)S(1)}, u32[]{:S(2)}, u32[]{:S(2)}) collective-permute-start(bf16[64,1024]{1,0:T(8,128)(2,1)S(1)} %get-tuple-element.64), channel_id=1, source_target_pairs={{0,2},{1,3},{2,4},{3,5},{4,6},{5,7},{6,0},{7,1},{8,10},{9,11},{10,... | collective-permute-start | bytes 393224 | tf_op jit(solution)/shard_map/ppermute | solution.py:476
  68.2 14.6 %collective-permute-start.23 = (bf16[64,1024]{1,0:T(8,128)(2,1)S(1)}, bf16[64,1024]{1,0:T(8,128)(2,1)S(1)}, u32[]{:S(2)}, u32[]{:S(2)}) collective-permute-start(bf16[64,1024]{1,0:T(8,128)(2,1)S(1)} %get-tuple-element.65), channel_id=1, source_target_pairs={{0,6},{1,7},{2,0},{3,1},{4,2},{5,3},{6,4},{7,5},{8,14},{9,15},{10,... | collective-permute-start | bytes 393224 | tf_op jit(solution)/shard_map/ppermute | solution.py:476
  68.3 21.5 %collective-permute-start.26 = (bf16[4,16,128]{2,1,0:T(8,128)(2,1)S(1)}, bf16[4,16,128]{2,1,0:T(8,128)(2,1)S(1)}, u32[]{:S(2)}, u32[]{:S(2)}) collective-permute-start(bf16[4,16,128]{2,1,0:T(8,128)(2,1)S(1)} %pad_maximum_fusion.2), channel_id=1, source_target_pairs={{0,8},{8,0},{16,24},{24,16},{32,40},{40,32},{48,56},{56,48},{64,72... | collective-permute-start | bytes 49160 | tf_op jit(solution)/shard_map/ppermute | solution.py:448
  82.9 7.7 %collective-permute-start.25 = (bf16[64,512]{1,0:T(8,128)(2,1)S(1)}, bf16[64,512]{1,0:T(8,128)(2,1)S(1)}, u32[]{:S(2)}, u32[]{:S(2)}) collective-permute-start(bf16[64,512]{1,0:T(8,128)(2,1)S(1)} %get-tuple-element.68), channel_id=1, source_target_pairs={{0,8},{8,0},{16,24},{24,16},{32,40},{40,32},{48,56},{56,48},{64,72... | collective-permute-start | bytes 196616 | tf_op jit(solution)/shard_map/ppermute | solution.py:448

commit v13 on v9

--- a/solution.py
+++ b/solution.py
@@ -31,6 +31,11 @@
     return lax.dot_general(a, b, dims, preferred_element_type=F32)
 
 
+def position():
+    index = lax.axis_index("batch")
+    return index >> 3, (index >> 1) & 3, index & 1, lax.axis_index("head")
+
+
 def lanes():
     return lax.broadcasted_iota(jnp.int32, (GROUP, DH), 1)
 
@@ -50,7 +55,7 @@
 
 
 def local_body(
-    place, q_in, prompt_in, table_in, length_in, new_in, pool_in, o0, o1, o2, o3,
+    q_in, prompt_in, table_in, length_in, new_in, pool_in, o0, o1, o2, o3,
     q, prompt, table, length, new, pool, wide, scores, weights, slots, sems,
 ):
     pairs = [
@@ -67,6 +72,8 @@
         copy.start()
     outs = (o0, o1, o2, o3)
     lane = lanes()
+    x, y, _, _ = position()
+    mask = 8 * x + 4 * (y >> 1)
     copies[0].wait()
     for h in range(GROUP):
         wide[:, h, :] = q[:, h * DH : (h + 1) * DH].astype(F32)
@@ -78,11 +85,11 @@
         p = prompt[n]
         k = slots[32 + p]
         slots[32 + p] = k + 1
-        slots[n] = (4 * p + k) ^ place[0]
+        slots[n] = (4 * p + k) ^ mask
         order = jnp.where(lane == n, (4 * p + k).astype(F32), order)
     for copy in copies[2:6]:
         copy.wait()
-    base = place[1]
+    base = lax.axis_index("batch") * 256
     for n in range(32):
         keys = jnp.concatenate([pool[0, table[j, n] - base] for j in range(8)], axis=0)
         s = dot(wide[n].astype(BF16), keys, NT) * SCALE
@@ -119,12 +126,12 @@
         out[17] = split_tile(jnp.where(lane < 8, held[i], 0.0), 8)
 
 
-def local_parts(place, q, prompt, table, length, new, pool):
+def local_parts(q, prompt, table, length, new, pool):
     out = jax.ShapeDtypeStruct((18, GROUP, DH), BF16)
     return pl.pallas_call(
         local_body,
         out_shape=[out] * 4,
-        in_specs=[SMEM] + [HBM] * 6,
+        in_specs=[HBM] * 6,
         out_specs=[VMEM] * 4,
         scratch_shapes=[
             pltpu.VMEM((32, GROUP * DH), BF16),
@@ -141,36 +148,37 @@
         ],
         compiler_params=params(54),
         name="local_parts",
-    )(place, q, prompt, table, length, new, pool)
-
-
-def regroup_body(place, a0, a1, a2, a3, same, across):
+    )(q, prompt, table, length, new, pool)
+
+
+def regroup_body(a0, a1, a2, a3, same, across):
+    x, _, _, z = position()
     for i, a in enumerate((a0, a1, a2, a3)):
         same[4 * i : 4 * i + 4] = a[0:4]
         across[4 * i : 4 * i + 4] = a[4:8]
         across[17 + 5 * i : 22 + 5 * i] = a[13:18]
 
-        @pl.when(place[2] ^ (place[4] >> 1) == i)
+        @pl.when(x ^ (z >> 1) == i)
         def _(a=a):
             same[16] = a[8]
             across[16] = a[8]
 
 
-def regroup(place, parts):
+def regroup(parts):
     return pl.pallas_call(
         regroup_body,
         out_shape=[
             jax.ShapeDtypeStruct((17, GROUP, DH), BF16),
             jax.ShapeDtypeStruct((37, GROUP, DH), BF16),
         ],
-        in_specs=[SMEM] + [VMEM] * 4,
+        in_specs=[VMEM] * 4,
         out_specs=[VMEM] * 2,
         compiler_params=params(),
         name="regroup",
-    )(place, *parts)
-
-
-ROWS = 128
+    )(*parts)
+
+
+ROWS = 256
 
 
 def prefix_part(q, kv):
@@ -247,9 +255,10 @@
 
 
 def combine_body(
-    place, own, own_masses, cross, cross_masses, message, s0, s1, s2, s3, far, out, held
+    own, own_masses, cross, cross_masses, message, s0, s1, s2, s3, far, out, held
 ):
-    x, y_high, z = place[2], place[3], place[4]
+    x, y, _, z = position()
+    y_high = y >> 1
     theirs = join_tile(message[32], 32)
     near = [join_tile(s[17], 8) for s in (s0, s1, s2, s3)]
     across = [join_tile(far[21 + 5 * i], 8) for i in range(4)]
@@ -277,16 +286,16 @@
         out[:, h * DH : (h + 1) * DH] = held[:, h, :].astype(BF16)
 
 
-def combine(place, own, cross, message, near, far):
+def combine(own, cross, message, near, far):
     return pl.pallas_call(
         combine_body,
         out_shape=jax.ShapeDtypeStruct((32, GROUP * DH), BF16),
-        in_specs=[SMEM] + [VMEM] * 10,
+        in_specs=[VMEM] * 10,
         out_specs=VMEM,
         scratch_shapes=[pltpu.VMEM((32, GROUP, DH), F32)],
         compiler_params=params(),
         name="combine",
-    )(place, *own, *cross, message, *near, far)
+    )(*own, *cross, message, *near, far)
 
 
 def by_target(total):
@@ -379,8 +388,8 @@
     other[...] = whole[:, 512:]
 
 
-def order_body(place, orders, pick):
-    x, y, core, z = place[2], place[3] * 2 + place[5], place[6], place[4]
+def order_body(orders, pick):
+    x, y, core, z = position()
     lane = lanes()
     order = jnp.zeros((GROUP, DH), F32)
     for block in range(4):
@@ -401,15 +410,15 @@
     pick[...] = (row == source[0:1]).astype(F32).astype(BF16)
 
 
-def order_rows(place, orders):
+def order_rows(orders):
     return pl.pallas_call(
         order_body,
         out_shape=jax.ShapeDtypeStruct((128, 128), BF16),
-        in_specs=[SMEM, VMEM],
+        in_specs=[VMEM],
         out_specs=VMEM,
         compiler_params=params(),
         name="order_rows",
-    )(place, orders)
+    )(orders)
 
 
 def finish_body(own, other, pick, out):
@@ -461,18 +470,12 @@
 
 
 def shards(queries, new_kv, prefix_kv, suffix_kv, page_table, suffix_len, prompt_of, out_weight):
-    me = lax.axis_index("batch")
-    z = lax.axis_index("head")
-    x, y, core = me // 8, (me // 2) % 4, me % 2
-    place = [8 * x + 4 * (y // 2), me * 256, x, y // 2, z, y % 2, core]
-    place = jnp.stack(place).astype(jnp.int32)
-
     prefix_other = other_core(prefix_kv)
     weights = [out_weight, other_core(out_weight)]
 
-    sent = local_parts(place, queries, prompt_of, page_table.T, suffix_len, new_kv, suffix_kv)
+    sent = local_parts(queries, prompt_of, page_table.T, suffix_len, new_kv, suffix_kv)
     by_x = [sent[0]] + [along_x(sent[k], k) for k in (1, 2, 3)]
-    same, across = regroup(place, by_x)
+    same, across = regroup(by_x)
     from1, from3 = along_y(same, 1), along_y(across, 3)
 
     own = prefix_keep(same, prefix_kv, prefix_other)
@@ -482,11 +485,11 @@
     message, from2 = lax.optimization_barrier((message, from2))
     message = along_y(message, 1)
     cross = prefix_keep(from2, prefix_kv, prefix_other)
-    attended = combine(place, own, cross, message, by_x, from2)
+    attended = combine(own, cross, message, by_x, from2)
 
     orders = jnp.stack([same[16], from1[16], from2[16], from3[16]])
     orders = jnp.concatenate([orders, other_core(orders)], axis=0)
-    pick = order_rows(place, orders)
+    pick = order_rows(orders)
 
     parts = [attended] + [turned(attended, k, 0) for k in (1, 2, 3)]
     far, near = [gathered([a[i : i + 16] for a in parts]) for i in (0, 16)]

time: 88.2 us -> 86.7 us (0.983); the launches traced: 88 us -> 85.5 us
  Pallas kernels: 19.9 us -> 16.2 us
  starting transfers between devices: 51.4 us -> 52.6 us
    ppermute x11, starting transfers between devices: 24.6 us -> 25.7 us  [along(): lax.ppermute(value, 'batch', [(i, i ^ k << shift) for i in range(BATCH)])]
    ppermute x11, waiting for transfers between devices: 4.89 us -> 5.85 us  [along(): lax.ppermute(value, 'batch', [(i, i ^ k << shift) for i in range(BATCH)])]
  transfers between devices with their start and end apart: 29 -> 29, of which waited for: 10 -> 10; matrix products, arithmetic and copies ran while one was open for 1% -> 0% of each run, Pallas kernels for 22% -> 18%
where the time goes in v13:
time: 86.7 us; the launch traced here: 85.5 us
  starting transfers between devices  52.6 us (61%)
  Pallas kernels  16.2 us (19%)
  waiting for transfers between devices  15.4 us (18%)
  local copies, waits for them, and re-layouts  1.01 us (1%)
    ppermute x11, starting transfers between devices, along(): lax.ppermute(value, 'batch', [(i, i ^ k << shift) for i in range(BATCH)])  25.7 us
    ppermute x7, starting transfers between devices, along_z(): lax.ppermute(value, 'head', [(i, (i + k) % HEADS) for i in range(HEADS)])  16.1 us
    ppermute x11, starting transfers between devices, turned(): return lax.ppermute(value, 'batch', pairs)  10.9 us
    ppermute x11, waiting for transfers between devices, turned(): return lax.ppermute(value, 'batch', pairs)  9.49 us
    ppermute x11, waiting for transfers between devices, along(): lax.ppermute(value, 'batch', [(i, i ^ k << shift) for i in range(BATCH)])  5.85 us
    pallas_call x2, Pallas kernels, prefix_keep(): pl.pallas_call(prefix_keep_body, out_shape=[out, out], in_specs=[VMEM] *...  3.68 us
    pallas_call x1, Pallas kernels, local_parts(): pl.pallas_call(local_body, out_shape=[out] * 4, in_specs=[HBM] * 6, out_s...  3.52 us
    pallas_call x1, Pallas kernels, prefix_send(): pl.pallas_call(prefix_send_body, out_shape=jax.ShapeDtypeStruct((33, GROU...  3.37 us
  transfers between devices with their start and end apart: 29, of which 10 were waited for; matrix products, arithmetic and copies ran while one was open for 0% of the time, Pallas kernels for 18%

profile of v13, /device:TPU:1, one launch (start us, length us, event | category | flops | bytes accessed | tf_op | source)
XLA Modules:
  0.0 85.5 jit_solution(17972005910171398752)
XLA Ops:
  0.0 3.2 %collective-permute-start.4 = (bf16[2,2048,128]{2,1,0:T(8,128)(2,1)}, bf16[2,2048,128]{2,1,0:T(8,128)(2,1)S(1)}, u32[]{:S(2)}, u32[]{:S(2)}) collective-permute-start(bf16[2,2048,128]{2,1,0:T(8,128)(2,1)} %kv0.5), channel_id=1, source_target_pairs={{0,8},{8,0},{16,24},{24,16},{32,40},{40,32},{48,56},{56,48},{64,72... | collective-permute-start | bytes 3145736 | tf_op jit(solution)/shard_map/ppermute | solution.py:442
  3.2 3.5 %local_parts.1 = (bf16[18,16,128]{2,1,0:T(8,128)(2,1)}, bf16[18,16,128]{2,1,0:T(8,128)(2,1)}, bf16[18,16,128]{2,1,0:T(8,128)(2,1)}, bf16[18,16,128]{2,1,0:T(8,128)(2,1)}) custom-call(bf16[32,2048]{1,0:T(8,128)(2,1)} %q_in.1, s32[32]{0:T(128)} %prompt_in.1, s32[8,32]{1,0:T(8,128)} %bitcast.1, s32[32]{0:T(128)} %length_in.1, bf16[2,32,128]{2,1,0:T(8,128)(2,1)} %new_in.1, ...), custom_call_target="tpu_custom_call" | custom-call | tf_op jit(solution)/shard_map/local_parts/pallas_call | solution.py:131
  6.8 0.1 collective-permute-start
  6.9 1.9 %collective-permute-start.1 = (bf16[18,16,128]{2,1,0:T(8,128)(2,1)}, bf16[18,16,128]{2,1,0:T(8,128)(2,1)S(1)}, u32[]{:S(2)}, u32[]{:S(2)}) collective-permute-start(bf16[18,16,128]{2,1,0:T(8,128)(2,1)} %get-tuple-element.34), channel_id=1, source_target_pairs={{0,128},{8,136},{16,144},{24,152},{32,160},{40,168},{48,176},{56,1... | collective-permute-start | bytes 221192 | tf_op jit(solution)/shard_map/ppermute | solution.py:442
  8.8 1.9 %collective-permute-start.2 = (bf16[18,16,128]{2,1,0:T(8,128)(2,1)}, bf16[18,16,128]{2,1,0:T(8,128)(2,1)S(1)}, u32[]{:S(2)}, u32[]{:S(2)}) collective-permute-start(bf16[18,16,128]{2,1,0:T(8,128)(2,1)} %get-tuple-element.35), channel_id=1, source_target_pairs={{0,192},{8,200},{16,208},{24,216},{32,224},{40,232},{48,240},{56,2... | collective-permute-start | bytes 221192 | tf_op jit(solution)/shard_map/ppermute | solution.py:442
  10.7 0.2 collective-permute-done.a1.s1
  10.9 2.0 %collective-permute-done.1.a2.s2 = bf16[18,16,128]{2,1,0:T(8,128)(2,1)S(1)} collective-permute-done((bf16[18,16,128]{2,1,0:T(8,128)(2,1)}, bf16[18,16,128]{2,1,0:T(8,128)(2,1)S(1)}, u32[]{:S(2)}, u32[]{:S(2)}) %collective-permute-start.1) | collective-permute-done | bytes 73760 | tf_op jit(solution)/shard_map/ppermute | solution.py:442
  12.9 1.5 %collective-permute-done.2.a3.s3 = bf16[18,16,128]{2,1,0:T(8,128)(2,1)S(1)} collective-permute-done((bf16[18,16,128]{2,1,0:T(8,128)(2,1)}, bf16[18,16,128]{2,1,0:T(8,128)(2,1)S(1)}, u32[]{:S(2)}, u32[]{:S(2)}) %collective-permute-start.2) | collective-permute-done | bytes 73760 | tf_op jit(solution)/shard_map/ppermute | solution.py:442
  14.4 0.9 %copy-done.2 = bf16[18,16,128]{2,1,0:T(8,128)(2,1)S(1)} copy-done((bf16[18,16,128]{2,1,0:T(8,128)(2,1)S(1)}, bf16[18,16,128]{2,1,0:T(8,128)(2,1)}, u32[]{:S(2)}) %copy-start.2) | copy-done | bytes 73752
  15.3 2.8 %collective-permute-start.3 = (bf16[37,16,128]{2,1,0:T(8,128)(2,1)S(1)}, bf16[37,16,128]{2,1,0:T(8,128)(2,1)S(1)}, u32[]{:S(2)}, u32[]{:S(2)}) collective-permute-start(bf16[37,16,128]{2,1,0:T(8,128)(2,1)S(1)} %get-tuple-element.36), channel_id=1, source_target_pairs={{0,48},{8,56},{16,32},{24,40},{32,16},{40,24},{48,0},{56,8},{64,11... | collective-permute-start | bytes 454664 | tf_op jit(solution)/shard_map/ppermute | solution.py:442
  18.1 0.0 collective-permute-start.5
  18.1 0.0 collective-permute-done.4.kv1
  18.1 1.8 %prefix_keep.2 = (f32[16,16,128]{2,1,0:T(8,128)S(1)}, f32[16,16,128]{2,1,0:T(8,128)S(1)}) custom-call(bf16[17,16,128]{2,1,0:T(8,128)(2,1)S(1)} %get-tuple-element.37.q, bf16[2,2048,128]{2,1,0:T(8,128)(2,1)S(1)} %copy-done.1, bf16[2,2048,128]{2,1,0:T(8,128)(2,1)S(1)} %collective-permute-done.4.kv1), custom_call_target="tpu_custom_call" | custom-call | flops 536870912 | bytes 2500000 | tf_op jit(solution)/shard_map/prefix_keep/pallas_call | solution.py:246
  20.0 0.0 copy-start
  20.0 1.2 %collective-permute-done.3.qb = bf16[37,16,128]{2,1,0:T(8,128)(2,1)S(1)} collective-permute-done((bf16[37,16,128]{2,1,0:T(8,128)(2,1)S(1)}, bf16[37,16,128]{2,1,0:T(8,128)(2,1)S(1)}, u32[]{:S(2)}, u32[]{:S(2)}) %collective-permute-start.3) | collective-permute-done | bytes 151584 | tf_op jit(solution)/shard_map/ppermute | solution.py:442
  21.1 0.4 collective-permute-start.6
  21.5 0.0 collective-permute-done.5.qa
  21.5 3.4 %prefix_send.1 = bf16[33,16,128]{2,1,0:T(8,128)(2,1)S(1)} custom-call(bf16[17,16,128]{2,1,0:T(8,128)(2,1)S(1)} %collective-permute-done.5.qa, bf16[37,16,128]{2,1,0:T(8,128)(2,1)S(1)} %collective-permute-done.3.qb, bf16[2,2048,128]{2,1,0:T(8,128)(2,1)S(1)} %copy-done.1, bf16[2,2048,128]{2,1,0:T(8,128)(2,1)S(1)} %collective-permute-done.4.kv1, ...), custom_call_target="tpu_custom_call" | custom-call | flops 1073741824 | bytes 2500000 | tf_op jit(solution)/shard_map/prefix_send/pallas_call | solution.py:233
  24.9 0.0 copy-start.3
  24.9 0.2 collective-permute-done.6.q.far
  25.2 0.9 %collective-permute-start.7 = (bf16[33,16,128]{2,1,0:T(8,128)(2,1)S(1)}, bf16[33,16,128]{2,1,0:T(8,128)(2,1)S(1)}, u32[]{:S(2)}, u32[]{:S(2)}) collective-permute-start(bf16[33,16,128]{2,1,0:T(8,128)(2,1)S(1)} %prefix_send.1), channel_id=1, source_target_pairs={{0,16},{8,24},{16,0},{24,8},{32,48},{40,56},{48,32},{56,40},{64,80... | collective-permute-start | bytes 405512 | tf_op jit(solution)/shard_map/ppermute | solution.py:442
  26.1 2.5 %collective-permute-start.15 = (bf16[2048,512]{1,0:T(8,128)(2,1)S(1)}, bf16[2048,512]{1,0:T(8,128)(2,1)S(1)}, u32[]{:S(2)}, u32[]{:S(2)}) collective-permute-start(bf16[2048,512]{1,0:T(8,128)(2,1)S(1)} %copy-done), channel_id=1, source_target_pairs={{0,8},{8,0},{16,24},{24,16},{32,40},{40,32},{48,56},{56,48},{64,72... | collective-permute-start | bytes 6291464 | tf_op jit(solution)/shard_map/ppermute | solution.py:442
  28.6 1.8 %prefix_keep.3 = (f32[16,16,128]{2,1,0:T(8,128)S(1)}, f32[16,16,128]{2,1,0:T(8,128)S(1)}) custom-call(bf16[37,16,128]{2,1,0:T(8,128)(2,1)S(1)} %collective-permute-done.6.q.far, bf16[2,2048,128]{2,1,0:T(8,128)(2,1)S(1)} %copy-done.1, bf16[2,2048,128]{2,1,0:T(8,128)(2,1)S(1)} %collective-permute-done.4.kv1), custom_call_target="tpu_custom_call" | custom-call | flops 536870912 | bytes 2500000 | tf_op jit(solution)/shard_map/prefix_keep/pallas_call | solution.py:246
  30.4 0.7 combine.1
  31.1 1.4 %collective-permute-start.8 = (bf16[32,2048]{1,0:T(8,128)(2,1)S(1)}, bf16[32,2048]{1,0:T(8,128)(2,1)S(1)}, u32[]{:S(2)}, u32[]{:S(2)}) collective-permute-start(bf16[32,2048]{1,0:T(8,128)(2,1)S(1)} %combine.1), channel_id=1, source_target_pairs={{0,64},{8,24},{16,80},{24,8},{32,96},{40,56},{48,112},{56,40},{64,... | collective-permute-start | bytes 393224 | tf_op jit(solution)/shard_map/ppermute | solution.py:459
  32.5 2.5 %collective-permute-start.9 = (bf16[32,2048]{1,0:T(8,128)(2,1)S(1)}, bf16[32,2048]{1,0:T(8,128)(2,1)S(1)}, u32[]{:S(2)}, u32[]{:S(2)}) collective-permute-start(bf16[32,2048]{1,0:T(8,128)(2,1)S(1)} %combine.1), channel_id=1, source_target_pairs={{0,128},{8,40},{16,144},{24,56},{32,160},{40,8},{48,176},{56,24},{... | collective-permute-start | bytes 393224 | tf_op jit(solution)/shard_map/ppermute | solution.py:459
  35.0 0.2 collective-permute-start.10
  35.2 0.0 collective-permute-done.8
  35.3 3.5 %collective-permute-done.9 = bf16[32,2048]{1,0:T(8,128)(2,1)S(1)} collective-permute-done((bf16[32,2048]{1,0:T(8,128)(2,1)S(1)}, bf16[32,2048]{1,0:T(8,128)(2,1)S(1)}, u32[]{:S(2)}, u32[]{:S(2)}) %collective-permute-start.9) | collective-permute-done | bytes 131104 | tf_op jit(solution)/shard_map/ppermute | solution.py:459
  38.7 1.7 %collective-permute-done.10 = bf16[32,2048]{1,0:T(8,128)(2,1)S(1)} collective-permute-done((bf16[32,2048]{1,0:T(8,128)(2,1)S(1)}, bf16[32,2048]{1,0:T(8,128)(2,1)S(1)}, u32[]{:S(2)}, u32[]{:S(2)}) %collective-permute-start.10) | collective-permute-done | bytes 131104 | tf_op jit(solution)/shard_map/ppermute | solution.py:459
  40.5 1.4 %collective-permute-start.18 = (bf16[64,2048]{1,0:T(8,128)(2,1)S(1)}, bf16[64,2048]{1,0:T(8,128)(2,1)S(1)}, u32[]{:S(2)}, u32[]{:S(2)}) collective-permute-start(bf16[64,2048]{1,0:T(8,128)(2,1)S(1)} %pad_maximum_fusion.1.a), channel_id=1, source_target_pairs={{0,48},{8,200},{16,32},{24,216},{32,16},{40,232},{48,0},{56,248},{... | collective-permute-start | bytes 786440 | tf_op jit(solution)/shard_map/ppermute | solution.py:459
  41.8 0.0 collective-permute-start.20
  41.9 1.4 %collective-permute-start.11 = (bf16[64,2048]{1,0:T(8,128)(2,1)S(1)}, bf16[64,2048]{1,0:T(8,128)(2,1)S(1)}, u32[]{:S(2)}, u32[]{:S(2)}) collective-permute-start(bf16[64,2048]{1,0:T(8,128)(2,1)S(1)} %pad_maximum_fusion.a), channel_id=1, source_target_pairs={{0,48},{8,200},{16,32},{24,216},{32,16},{40,232},{48,0},{56,248},{... | collective-permute-start | bytes 786440 | tf_op jit(solution)/shard_map/ppermute | solution.py:459
  43.3 0.9 %collective-permute-start.13 = (bf16[64,2048]{1,0:T(8,128)(2,1)S(1)}, bf16[64,2048]{1,0:T(8,128)(2,1)S(1)}, u32[]{:S(2)}, u32[]{:S(2)}) collective-permute-start(bf16[64,2048]{1,0:T(8,128)(2,1)S(1)} %pad_maximum_fusion.a), channel_id=1, source_target_pairs={{0,16},{8,72},{16,0},{24,88},{32,48},{40,104},{48,32},{56,120},{64... | collective-permute-start | bytes 786440 | tf_op jit(solution)/shard_map/ppermute | solution.py:459
  44.2 2.8 %collective-permute-done.18.c = bf16[64,2048]{1,0:T(8,128)(2,1)S(1)} collective-permute-done((bf16[64,2048]{1,0:T(8,128)(2,1)S(1)}, bf16[64,2048]{1,0:T(8,128)(2,1)S(1)}, u32[]{:S(2)}, u32[]{:S(2)}) %collective-permute-start.18) | collective-permute-done | bytes 262176 | tf_op jit(solution)/shard_map/ppermute | solution.py:459
  47.0 0.1 collective-permute-start.19
  47.1 0.0 collective-permute-done.20.b
  47.1 1.4 %collective-permute-start.21 = (bf16[32,2048]{1,0:T(8,128)(2,1)S(1)}, bf16[32,2048]{1,0:T(8,128)(2,1)S(1)}, u32[]{:S(2)}, u32[]{:S(2)}) collective-permute-start(bf16[32,2048]{1,0:T(8,128)(2,1)S(1)} %slice.75), channel_id=1, source_target_pairs={{0,48},{8,200},{16,32},{24,216},{32,16},{40,232},{48,0},{56,248},{... | collective-permute-start | bytes 393224 | tf_op jit(solution)/shard_map/ppermute | solution.py:459
  48.6 1.5 %collective-permute-done.11.c = bf16[64,2048]{1,0:T(8,128)(2,1)S(1)} collective-permute-done((bf16[64,2048]{1,0:T(8,128)(2,1)S(1)}, bf16[64,2048]{1,0:T(8,128)(2,1)S(1)}, u32[]{:S(2)}, u32[]{:S(2)}) %collective-permute-start.11) | collective-permute-done | bytes 262176 | tf_op jit(solution)/shard_map/ppermute | solution.py:459
  50.1 0.1 collective-permute-start.12
  50.2 0.0 collective-permute-done.13.b
  50.2 1.4 %collective-permute-start.14 = (bf16[32,2048]{1,0:T(8,128)(2,1)S(1)}, bf16[32,2048]{1,0:T(8,128)(2,1)S(1)}, u32[]{:S(2)}, u32[]{:S(2)}) collective-permute-start(bf16[32,2048]{1,0:T(8,128)(2,1)S(1)} %slice.69), channel_id=1, source_target_pairs={{0,48},{8,200},{16,32},{24,216},{32,16},{40,232},{48,0},{56,248},{... | collective-permute-start | bytes 393224 | tf_op jit(solution)/shard_map/ppermute | solution.py:459
  51.7 0.0 collective-permute-done.15.w1
  51.7 1.0 %project.3.first = f32[4,48,1024]{2,1,0:T(8,128)S(1)} custom-call(bf16[64,2048]{1,0:T(8,128)(2,1)S(1)} %pad_maximum_fusion.1.a, bf16[64,2048]{1,0:T(8,128)(2,1)S(1)} %collective-permute-done.20.b, bf16[64,2048]{1,0:T(8,128)(2,1)S(1)} %collective-permute-done.18.c, bf16[2048,512]{1,0:T(8,128)(2,1)S(1)} %copy-done, ...), custom_call_target="tpu_custom_call" | custom-call | flops 805306368 | bytes 4500000 | tf_op jit(solution)/shard_map/project/pallas_call | solution.py:325
  52.7 0.9 %far.1 = (f32[64,1024]{1,0:T(8,128)S(1)}, bf16[64,1024]{1,0:T(8,128)(2,1)S(1)}, bf16[64,1024]{1,0:T(8,128)(2,1)S(1)}, bf16[64,1024]{1,0:T(8,128)(2,1)S(1)}) custom-call(bf16[32,2048]{1,0:T(8,128)(2,1)S(1)} %collective-permute-done.19.a, bf16[32,2048]{1,0:T(8,128)(2,1)S(1)} %collective-permute-done.21.b, bf16[2048,512]{1,0:T(8,128)(2,1)S(1)} %copy-done, ...), custom_call_target="tpu_custom_call" | custom-call | tf_op jit(solution)/shard_map/far/pallas_call | solution.py:368
  53.6 1.7 %collective-permute-start.22 = (bf16[64,1024]{1,0:T(8,128)(2,1)S(1)}, bf16[64,1024]{1,0:T(8,128)(2,1)S(1)}, u32[]{:S(2)}, u32[]{:S(2)}) collective-permute-start(bf16[64,1024]{1,0:T(8,128)(2,1)S(1)} %get-tuple-element.52), channel_id=1, source_target_pairs={{0,1},{1,2},{2,3},{3,4},{4,5},{5,6},{6,7},{7,0},{8,9},{9,10},{10,1... | collective-permute-start | bytes 393224 | tf_op jit(solution)/shard_map/ppermute | solution.py:469
  55.3 4.0 %collective-permute-start.23 = (bf16[64,1024]{1,0:T(8,128)(2,1)S(1)}, bf16[64,1024]{1,0:T(8,128)(2,1)S(1)}, u32[]{:S(2)}, u32[]{:S(2)}) collective-permute-start(bf16[64,1024]{1,0:T(8,128)(2,1)S(1)} %get-tuple-element.53), channel_id=1, source_target_pairs={{0,7},{1,0},{2,1},{3,2},{4,3},{5,4},{6,5},{7,6},{8,15},{9,8},{10,9... | collective-permute-start | bytes 393224 | tf_op jit(solution)/shard_map/ppermute | solution.py:469
  59.3 3.9 %collective-permute-start.26 = (bf16[64,1024]{1,0:T(8,128)(2,1)S(1)}, bf16[64,1024]{1,0:T(8,128)(2,1)S(1)}, u32[]{:S(2)}, u32[]{:S(2)}) collective-permute-start(bf16[64,1024]{1,0:T(8,128)(2,1)S(1)} %get-tuple-element.56), channel_id=1, source_target_pairs={{0,4},{1,5},{2,6},{3,7},{4,0},{5,1},{6,2},{7,3},{8,12},{9,13},{10,... | collective-permute-start | bytes 393224 | tf_op jit(solution)/shard_map/ppermute | solution.py:469
  63.3 1.0 %project.2.first = f32[4,48,1024]{2,1,0:T(8,128)S(1)} custom-call(bf16[64,2048]{1,0:T(8,128)(2,1)S(1)} %pad_maximum_fusion.a, bf16[64,2048]{1,0:T(8,128)(2,1)S(1)} %collective-permute-done.13.b, bf16[64,2048]{1,0:T(8,128)(2,1)S(1)} %collective-permute-done.11.c, bf16[2048,512]{1,0:T(8,128)(2,1)S(1)} %copy-done, bf16[2048,512]{1,0:T(8,128)(2,1)S(1)} %collective-permute-done.15.w1), custom_call_target="tpu_custom_call" | custom-call | flops 805306368 | bytes 4500000 | tf_op jit(solution)/shard_map/project/pallas_call | solution.py:325
  64.3 0.0 collective-permute-done.14.b
  64.3 0.9 %near.1 = (f32[64,1024]{1,0:T(8,128)S(1)}, bf16[64,1024]{1,0:T(8,128)(2,1)S(1)}, f32[64,1024]{1,0:T(8,128)S(1)}, bf16[64,1024]{1,0:T(8,128)(2,1)S(1)}) custom-call(bf16[32,2048]{1,0:T(8,128)(2,1)S(1)} %collective-permute-done.12.a, bf16[32,2048]{1,0:T(8,128)(2,1)S(1)} %collective-permute-done.14.b, bf16[2048,512]{1,0:T(8,128)(2,1)S(1)} %copy-done, ...), custom_call_target="tpu_custom_call" | custom-call | tf_op jit(solution)/shard_map/near/pallas_call | solution.py:368
  65.2 0.1 collective-permute-start.16
  65.3 2.7 %collective-permute-start.17 = (bf16[64,1024]{1,0:T(8,128)(2,1)S(1)}, bf16[64,1024]{1,0:T(8,128)(2,1)S(1)}, u32[]{:S(2)}, u32[]{:S(2)}) collective-permute-start(bf16[64,1024]{1,0:T(8,128)(2,1)S(1)} %get-tuple-element.49), channel_id=1, source_target_pairs={{0,7},{1,0},{2,1},{3,2},{4,3},{5,4},{6,5},{7,6},{8,15},{9,8},{10,9... | collective-permute-start | bytes 393224 | tf_op jit(solution)/shard_map/ppermute | solution.py:469
  68.0 0.0 collective-permute-done.23.above
  68.0 0.1 middle.1
  68.0 0.1 collective-permute-start.24
  68.1 3.6 %collective-permute-start.25 = (bf16[64,1024]{1,0:T(8,128)(2,1)S(1)}, bf16[64,1024]{1,0:T(8,128)(2,1)S(1)}, u32[]{:S(2)}, u32[]{:S(2)}) collective-permute-start(bf16[64,1024]{1,0:T(8,128)(2,1)S(1)} %get-tuple-element.55), channel_id=1, source_target_pairs={{0,6},{1,7},{2,0},{3,1},{4,2},{5,3},{6,4},{7,5},{8,14},{9,15},{10,... | collective-permute-start | bytes 393224 | tf_op jit(solution)/shard_map/ppermute | solution.py:469
  71.7 0.0 collective-permute-done.26.opposite
  71.7 8.2 %collective-permute-start.28 = (bf16[4,16,128]{2,1,0:T(8,128)(2,1)S(1)}, bf16[4,16,128]{2,1,0:T(8,128)(2,1)S(1)}, u32[]{:S(2)}, u32[]{:S(2)}) collective-permute-start(bf16[4,16,128]{2,1,0:T(8,128)(2,1)S(1)} %pad_maximum_fusion.2), channel_id=1, source_target_pairs={{0,8},{8,0},{16,24},{24,16},{32,40},{40,32},{48,56},{56,48},{64,72... | collective-permute-start | bytes 49160 | tf_op jit(solution)/shard_map/ppermute | solution.py:442
  79.9 0.1 total.1
  80.0 3.7 %collective-permute-start.27 = (bf16[64,512]{1,0:T(8,128)(2,1)S(1)}, bf16[64,512]{1,0:T(8,128)(2,1)S(1)}, u32[]{:S(2)}, u32[]{:S(2)}) collective-permute-start(bf16[64,512]{1,0:T(8,128)(2,1)S(1)} %get-tuple-element.58), channel_id=1, source_target_pairs={{0,8},{8,0},{16,24},{24,16},{32,40},{40,32},{48,56},{56,48},{64,72... | collective-permute-start | bytes 196616 | tf_op jit(solution)/shard_map/ppermute | solution.py:442
  83.8 0.1 order_rows.1.pick
  83.9 0.8 collective-permute-done.27.other
  84.6 0.9 %finish.1 = bf16[128,512]{1,0:T(8,128)(2,1)} custom-call(bf16[64,512]{1,0:T(8,128)(2,1)S(1)} %get-tuple-element.57.own, bf16[64,512]{1,0:T(8,128)(2,1)S(1)} %collective-permute-done.27.other, bf16[128,128]{1,0:T(8,128)(2,1)S(1)} %order_rows.1.pick), custom_call_target="tpu_custom_call" | custom-call | tf_op jit(solution)/shard_map/finish/pallas_call | solution.py:431
  (32 shorter events, 0.2 us)
Async XLA Ops:
  0.0 18.1 %copy-start.1 = (bf16[2,2048,128]{2,1,0:T(8,128)(2,1)S(1)}, bf16[2,2048,128]{2,1,0:T(8,128)(2,1)}, u32[]{:S(2)}) copy-start(bf16[2,2048,128]{2,1,0:T(8,128)(2,1)} %kv0.5) | copy-start | bytes 3145732
  0.0 18.1 %collective-permute-start.4 = (bf16[2,2048,128]{2,1,0:T(8,128)(2,1)}, bf16[2,2048,128]{2,1,0:T(8,128)(2,1)S(1)}, u32[]{:S(2)}, u32[]{:S(2)}) collective-permute-start(bf16[2,2048,128]{2,1,0:T(8,128)(2,1)} %kv0.5), channel_id=1, source_target_pairs={{0,8},{8,0},{16,24},{24,16},{32,40},{40,32},{48,56},{56,48},{64,72... | collective-permute-start | bytes 3145736 | tf_op jit(solution)/shard_map/ppermute | solution.py:442
  6.8 4.1 %collective-permute-start = (bf16[18,16,128]{2,1,0:T(8,128)(2,1)}, bf16[18,16,128]{2,1,0:T(8,128)(2,1)S(1)}, u32[]{:S(2)}, u32[]{:S(2)}) collective-permute-start(bf16[18,16,128]{2,1,0:T(8,128)(2,1)} %get-tuple-element.33), channel_id=1, source_target_pairs={{0,64},{8,72},{16,80},{24,88},{32,96},{40,104},{48,112},{56,120},{... | collective-permute-start | bytes 221192 | tf_op jit(solution)/shard_map/ppermute | solution.py:442
  6.9 6.0 %collective-permute-start.1 = (bf16[18,16,128]{2,1,0:T(8,128)(2,1)}, bf16[18,16,128]{2,1,0:T(8,128)(2,1)S(1)}, u32[]{:S(2)}, u32[]{:S(2)}) collective-permute-start(bf16[18,16,128]{2,1,0:T(8,128)(2,1)} %get-tuple-element.34), channel_id=1, source_target_pairs={{0,128},{8,136},{16,144},{24,152},{32,160},{40,168},{48,176},{56,1... | collective-permute-start | bytes 221192 | tf_op jit(solution)/shard_map/ppermute | solution.py:442
  8.8 5.6 %collective-permute-start.2 = (bf16[18,16,128]{2,1,0:T(8,128)(2,1)}, bf16[18,16,128]{2,1,0:T(8,128)(2,1)S(1)}, u32[]{:S(2)}, u32[]{:S(2)}) collective-permute-start(bf16[18,16,128]{2,1,0:T(8,128)(2,1)} %get-tuple-element.35), channel_id=1, source_target_pairs={{0,192},{8,200},{16,208},{24,216},{32,224},{40,232},{48,240},{56,2... | collective-permute-start | bytes 221192 | tf_op jit(solution)/shard_map/ppermute | solution.py:442
  14.4 0.9 %copy-start.2 = (bf16[18,16,128]{2,1,0:T(8,128)(2,1)S(1)}, bf16[18,16,128]{2,1,0:T(8,128)(2,1)}, u32[]{:S(2)}) copy-start(bf16[18,16,128]{2,1,0:T(8,128)(2,1)} %get-tuple-element.32.a0.s0) | copy-start | bytes 221188
  15.3 5.8 %collective-permute-start.3 = (bf16[37,16,128]{2,1,0:T(8,128)(2,1)S(1)}, bf16[37,16,128]{2,1,0:T(8,128)(2,1)S(1)}, u32[]{:S(2)}, u32[]{:S(2)}) collective-permute-start(bf16[37,16,128]{2,1,0:T(8,128)(2,1)S(1)} %get-tuple-element.36), channel_id=1, source_target_pairs={{0,48},{8,56},{16,32},{24,40},{32,16},{40,24},{48,0},{56,8},{64,11... | collective-permute-start | bytes 454664 | tf_op jit(solution)/shard_map/ppermute | solution.py:442
  18.1 3.5 %collective-permute-start.5 = (bf16[17,16,128]{2,1,0:T(8,128)(2,1)S(1)}, bf16[17,16,128]{2,1,0:T(8,128)(2,1)S(1)}, u32[]{:S(2)}, u32[]{:S(2)}) collective-permute-start(bf16[17,16,128]{2,1,0:T(8,128)(2,1)S(1)} %get-tuple-element.37.q), channel_id=1, source_target_pairs={{0,16},{8,24},{16,0},{24,8},{32,48},{40,56},{48,32},{56,40},{64,80... | collective-permute-start | bytes 208904 | tf_op jit(solution)/shard_map/ppermute | solution.py:442
  20.0 6.1 %copy-start = (bf16[2048,512]{1,0:T(8,128)(2,1)S(1)}, bf16[2048,512]{1,0:T(8,128)(2,1)}, u32[]{:S(2)}) copy-start(bf16[2048,512]{1,0:T(8,128)(2,1)} %w0.7) | copy-start | bytes 6291460
  21.1 4.0 %collective-permute-start.6 = (bf16[37,16,128]{2,1,0:T(8,128)(2,1)S(1)}, bf16[37,16,128]{2,1,0:T(8,128)(2,1)S(1)}, u32[]{:S(2)}, u32[]{:S(2)}) collective-permute-start(bf16[37,16,128]{2,1,0:T(8,128)(2,1)S(1)} %collective-permute-done.3.qb), channel_id=1, source_target_pairs={{0,16},{8,24},{16,0},{24,8},{32,48},{40,56},{48,32},{56,40},{64,80... | collective-permute-start | bytes 454664 | tf_op jit(solution)/shard_map/ppermute | solution.py:442
  24.9 5.5 %copy-start.3 = (bf16[18,16,128]{2,1,0:T(8,128)(2,1)S(1)}, bf16[18,16,128]{2,1,0:T(8,128)(2,1)}, u32[]{:S(2)}) copy-start(bf16[18,16,128]{2,1,0:T(8,128)(2,1)} %get-tuple-element.32.a0.s0) | copy-start | bytes 221188
  25.2 5.3 %collective-permute-start.7 = (bf16[33,16,128]{2,1,0:T(8,128)(2,1)S(1)}, bf16[33,16,128]{2,1,0:T(8,128)(2,1)S(1)}, u32[]{:S(2)}, u32[]{:S(2)}) collective-permute-start(bf16[33,16,128]{2,1,0:T(8,128)(2,1)S(1)} %prefix_send.1), channel_id=1, source_target_pairs={{0,16},{8,24},{16,0},{24,8},{32,48},{40,56},{48,32},{56,40},{64,80... | collective-permute-start | bytes 405512 | tf_op jit(solution)/shard_map/ppermute | solution.py:442
  26.1 25.6 %collective-permute-start.15 = (bf16[2048,512]{1,0:T(8,128)(2,1)S(1)}, bf16[2048,512]{1,0:T(8,128)(2,1)S(1)}, u32[]{:S(2)}, u32[]{:S(2)}) collective-permute-start(bf16[2048,512]{1,0:T(8,128)(2,1)S(1)} %copy-done), channel_id=1, source_target_pairs={{0,8},{8,0},{16,24},{24,16},{32,40},{40,32},{48,56},{56,48},{64,72... | collective-permute-start | bytes 6291464 | tf_op jit(solution)/shard_map/ppermute | solution.py:442
  31.1 4.1 %collective-permute-start.8 = (bf16[32,2048]{1,0:T(8,128)(2,1)S(1)}, bf16[32,2048]{1,0:T(8,128)(2,1)S(1)}, u32[]{:S(2)}, u32[]{:S(2)}) collective-permute-start(bf16[32,2048]{1,0:T(8,128)(2,1)S(1)} %combine.1), channel_id=1, source_target_pairs={{0,64},{8,24},{16,80},{24,8},{32,96},{40,56},{48,112},{56,40},{64,... | collective-permute-start | bytes 393224 | tf_op jit(solution)/shard_map/ppermute | solution.py:459
  32.5 6.2 %collective-permute-start.9 = (bf16[32,2048]{1,0:T(8,128)(2,1)S(1)}, bf16[32,2048]{1,0:T(8,128)(2,1)S(1)}, u32[]{:S(2)}, u32[]{:S(2)}) collective-permute-start(bf16[32,2048]{1,0:T(8,128)(2,1)S(1)} %combine.1), channel_id=1, source_target_pairs={{0,128},{8,40},{16,144},{24,56},{32,160},{40,8},{48,176},{56,24},{... | collective-permute-start | bytes 393224 | tf_op jit(solution)/shard_map/ppermute | solution.py:459
  35.0 5.4 %collective-permute-start.10 = (bf16[32,2048]{1,0:T(8,128)(2,1)S(1)}, bf16[32,2048]{1,0:T(8,128)(2,1)S(1)}, u32[]{:S(2)}, u32[]{:S(2)}) collective-permute-start(bf16[32,2048]{1,0:T(8,128)(2,1)S(1)} %combine.1), channel_id=1, source_target_pairs={{0,192},{8,56},{16,208},{24,40},{32,224},{40,24},{48,240},{56,8},{... | collective-permute-start | bytes 393224 | tf_op jit(solution)/shard_map/ppermute | solution.py:459
  40.5 6.5 %collective-permute-start.18 = (bf16[64,2048]{1,0:T(8,128)(2,1)S(1)}, bf16[64,2048]{1,0:T(8,128)(2,1)S(1)}, u32[]{:S(2)}, u32[]{:S(2)}) collective-permute-start(bf16[64,2048]{1,0:T(8,128)(2,1)S(1)} %pad_maximum_fusion.1.a), channel_id=1, source_target_pairs={{0,48},{8,200},{16,32},{24,216},{32,16},{40,232},{48,0},{56,248},{... | collective-permute-start | bytes 786440 | tf_op jit(solution)/shard_map/ppermute | solution.py:459
  41.8 5.3 %collective-permute-start.20 = (bf16[64,2048]{1,0:T(8,128)(2,1)S(1)}, bf16[64,2048]{1,0:T(8,128)(2,1)S(1)}, u32[]{:S(2)}, u32[]{:S(2)}) collective-permute-start(bf16[64,2048]{1,0:T(8,128)(2,1)S(1)} %pad_maximum_fusion.1.a), channel_id=1, source_target_pairs={{0,16},{8,72},{16,0},{24,88},{32,48},{40,104},{48,32},{56,120},{64... | collective-permute-start | bytes 786440 | tf_op jit(solution)/shard_map/ppermute | solution.py:459
  41.9 8.2 %collective-permute-start.11 = (bf16[64,2048]{1,0:T(8,128)(2,1)S(1)}, bf16[64,2048]{1,0:T(8,128)(2,1)S(1)}, u32[]{:S(2)}, u32[]{:S(2)}) collective-permute-start(bf16[64,2048]{1,0:T(8,128)(2,1)S(1)} %pad_maximum_fusion.a), channel_id=1, source_target_pairs={{0,48},{8,200},{16,32},{24,216},{32,16},{40,232},{48,0},{56,248},{... | collective-permute-start | bytes 786440 | tf_op jit(solution)/shard_map/ppermute | solution.py:459
  43.3 6.9 %collective-permute-start.13 = (bf16[64,2048]{1,0:T(8,128)(2,1)S(1)}, bf16[64,2048]{1,0:T(8,128)(2,1)S(1)}, u32[]{:S(2)}, u32[]{:S(2)}) collective-permute-start(bf16[64,2048]{1,0:T(8,128)(2,1)S(1)} %pad_maximum_fusion.a), channel_id=1, source_target_pairs={{0,16},{8,72},{16,0},{24,88},{32,48},{40,104},{48,32},{56,120},{64... | collective-permute-start | bytes 786440 | tf_op jit(solution)/shard_map/ppermute | solution.py:459
  47.0 5.7 %collective-permute-start.19 = (bf16[32,2048]{1,0:T(8,128)(2,1)S(1)}, bf16[32,2048]{1,0:T(8,128)(2,1)S(1)}, u32[]{:S(2)}, u32[]{:S(2)}) collective-permute-start(bf16[32,2048]{1,0:T(8,128)(2,1)S(1)} %slice.74), channel_id=1, source_target_pairs={{0,16},{8,72},{16,0},{24,88},{32,48},{40,104},{48,32},{56,120},{64... | collective-permute-start | bytes 393224 | tf_op jit(solution)/shard_map/ppermute | solution.py:459
  47.1 5.6 %collective-permute-start.21 = (bf16[32,2048]{1,0:T(8,128)(2,1)S(1)}, bf16[32,2048]{1,0:T(8,128)(2,1)S(1)}, u32[]{:S(2)}, u32[]{:S(2)}) collective-permute-start(bf16[32,2048]{1,0:T(8,128)(2,1)S(1)} %slice.75), channel_id=1, source_target_pairs={{0,48},{8,200},{16,32},{24,216},{32,16},{40,232},{48,0},{56,248},{... | collective-permute-start | bytes 393224 | tf_op jit(solution)/shard_map/ppermute | solution.py:459
  50.1 14.2 %collective-permute-start.12 = (bf16[32,2048]{1,0:T(8,128)(2,1)S(1)}, bf16[32,2048]{1,0:T(8,128)(2,1)S(1)}, u32[]{:S(2)}, u32[]{:S(2)}) collective-permute-start(bf16[32,2048]{1,0:T(8,128)(2,1)S(1)} %slice.68), channel_id=1, source_target_pairs={{0,16},{8,72},{16,0},{24,88},{32,48},{40,104},{48,32},{56,120},{64... | collective-permute-start | bytes 393224 | tf_op jit(solution)/shard_map/ppermute | solution.py:459
  50.2 14.1 %collective-permute-start.14 = (bf16[32,2048]{1,0:T(8,128)(2,1)S(1)}, bf16[32,2048]{1,0:T(8,128)(2,1)S(1)}, u32[]{:S(2)}, u32[]{:S(2)}) collective-permute-start(bf16[32,2048]{1,0:T(8,128)(2,1)S(1)} %slice.69), channel_id=1, source_target_pairs={{0,48},{8,200},{16,32},{24,216},{32,16},{40,232},{48,0},{56,248},{... | collective-permute-start | bytes 393224 | tf_op jit(solution)/shard_map/ppermute | solution.py:459
  53.6 14.4 %collective-permute-start.22 = (bf16[64,1024]{1,0:T(8,128)(2,1)S(1)}, bf16[64,1024]{1,0:T(8,128)(2,1)S(1)}, u32[]{:S(2)}, u32[]{:S(2)}) collective-permute-start(bf16[64,1024]{1,0:T(8,128)(2,1)S(1)} %get-tuple-element.52), channel_id=1, source_target_pairs={{0,1},{1,2},{2,3},{3,4},{4,5},{5,6},{6,7},{7,0},{8,9},{9,10},{10,1... | collective-permute-start | bytes 393224 | tf_op jit(solution)/shard_map/ppermute | solution.py:469
  55.3 12.6 %collective-permute-start.23 = (bf16[64,1024]{1,0:T(8,128)(2,1)S(1)}, bf16[64,1024]{1,0:T(8,128)(2,1)S(1)}, u32[]{:S(2)}, u32[]{:S(2)}) collective-permute-start(bf16[64,1024]{1,0:T(8,128)(2,1)S(1)} %get-tuple-element.53), channel_id=1, source_target_pairs={{0,7},{1,0},{2,1},{3,2},{4,3},{5,4},{6,5},{7,6},{8,15},{9,8},{10,9... | collective-permute-start | bytes 393224 | tf_op jit(solution)/shard_map/ppermute | solution.py:469
  59.3 12.4 %collective-permute-start.26 = (bf16[64,1024]{1,0:T(8,128)(2,1)S(1)}, bf16[64,1024]{1,0:T(8,128)(2,1)S(1)}, u32[]{:S(2)}, u32[]{:S(2)}) collective-permute-start(bf16[64,1024]{1,0:T(8,128)(2,1)S(1)} %get-tuple-element.56), channel_id=1, source_target_pairs={{0,4},{1,5},{2,6},{3,7},{4,0},{5,1},{6,2},{7,3},{8,12},{9,13},{10,... | collective-permute-start | bytes 393224 | tf_op jit(solution)/shard_map/ppermute | solution.py:469
  65.2 14.7 %collective-permute-start.16 = (bf16[64,1024]{1,0:T(8,128)(2,1)S(1)}, bf16[64,1024]{1,0:T(8,128)(2,1)S(1)}, u32[]{:S(2)}, u32[]{:S(2)}) collective-permute-start(bf16[64,1024]{1,0:T(8,128)(2,1)S(1)} %get-tuple-element.48), channel_id=1, source_target_pairs={{0,1},{1,2},{2,3},{3,4},{4,5},{5,6},{6,7},{7,0},{8,9},{9,10},{10,1... | collective-permute-start | bytes 393224 | tf_op jit(solution)/shard_map/ppermute | solution.py:469
  65.3 14.6 %collective-permute-start.17 = (bf16[64,1024]{1,0:T(8,128)(2,1)S(1)}, bf16[64,1024]{1,0:T(8,128)(2,1)S(1)}, u32[]{:S(2)}, u32[]{:S(2)}) collective-permute-start(bf16[64,1024]{1,0:T(8,128)(2,1)S(1)} %get-tuple-element.49), channel_id=1, source_target_pairs={{0,7},{1,0},{2,1},{3,2},{4,3},{5,4},{6,5},{7,6},{8,15},{9,8},{10,9... | collective-permute-start | bytes 393224 | tf_op jit(solution)/shard_map/ppermute | solution.py:469
  68.0 11.9 %collective-permute-start.24 = (bf16[64,1024]{1,0:T(8,128)(2,1)S(1)}, bf16[64,1024]{1,0:T(8,128)(2,1)S(1)}, u32[]{:S(2)}, u32[]{:S(2)}) collective-permute-start(bf16[64,1024]{1,0:T(8,128)(2,1)S(1)} %get-tuple-element.54), channel_id=1, source_target_pairs={{0,2},{1,3},{2,4},{3,5},{4,6},{5,7},{6,0},{7,1},{8,10},{9,11},{10,... | collective-permute-start | bytes 393224 | tf_op jit(solution)/shard_map/ppermute | solution.py:469
  68.1 11.8 %collective-permute-start.25 = (bf16[64,1024]{1,0:T(8,128)(2,1)S(1)}, bf16[64,1024]{1,0:T(8,128)(2,1)S(1)}, u32[]{:S(2)}, u32[]{:S(2)}) collective-permute-start(bf16[64,1024]{1,0:T(8,128)(2,1)S(1)} %get-tuple-element.55), channel_id=1, source_target_pairs={{0,6},{1,7},{2,0},{3,1},{4,2},{5,3},{6,4},{7,5},{8,14},{9,15},{10,... | collective-permute-start | bytes 393224 | tf_op jit(solution)/shard_map/ppermute | solution.py:469
  71.7 12.0 %collective-permute-start.28 = (bf16[4,16,128]{2,1,0:T(8,128)(2,1)S(1)}, bf16[4,16,128]{2,1,0:T(8,128)(2,1)S(1)}, u32[]{:S(2)}, u32[]{:S(2)}) collective-permute-start(bf16[4,16,128]{2,1,0:T(8,128)(2,1)S(1)} %pad_maximum_fusion.2), channel_id=1, source_target_pairs={{0,8},{8,0},{16,24},{24,16},{32,40},{40,32},{48,56},{56,48},{64,72... | collective-permute-start | bytes 49160 | tf_op jit(solution)/shard_map/ppermute | solution.py:442
  80.0 4.6 %collective-permute-start.27 = (bf16[64,512]{1,0:T(8,128)(2,1)S(1)}, bf16[64,512]{1,0:T(8,128)(2,1)S(1)}, u32[]{:S(2)}, u32[]{:S(2)}) collective-permute-start(bf16[64,512]{1,0:T(8,128)(2,1)S(1)} %get-tuple-element.58), channel_id=1, source_target_pairs={{0,8},{8,0},{16,24},{24,16},{32,40},{40,32},{48,56},{56,48},{64,72... | collective-permute-start | bytes 196616 | tf_op jit(solution)/shard_map/ppermute | solution.py:442

commit v14 on v13

--- a/solution.py
+++ b/solution.py
@@ -151,7 +151,7 @@
     )(q, prompt, table, length, new, pool)
 
 
-def regroup_body(a0, a1, a2, a3, same, across):
+def regroup_body(a2, a1, a3, a0, same, across):
     x, _, _, z = position()
     for i, a in enumerate((a0, a1, a2, a3)):
         same[4 * i : 4 * i + 4] = a[0:4]
@@ -175,7 +175,7 @@
         out_specs=[VMEM] * 2,
         compiler_params=params(),
         name="regroup",
-    )(*parts)
+    )(parts[2], parts[1], parts[3], parts[0])
 
 
 ROWS = 256
@@ -404,6 +404,7 @@
     dy = (2 * (prompt & 1) + (block >> 1)) ^ y
     first = jnp.where(far == 0, dx, dy)
     second = jnp.where(far == 0, dy, dx)
+    first = jnp.where((first == 1) | (first == 2), 3 - first, first)
     second = jnp.where(second >= 2, 5 - second, second)
     source = ((far ^ core) * 16 + second * 4 + first) * 4 + k
     row = lax.broadcasted_iota(jnp.int32, (128, 128), 0)
@@ -474,7 +475,8 @@
     weights = [out_weight, other_core(out_weight)]
 
     sent = local_parts(queries, prompt_of, page_table.T, suffix_len, new_kv, suffix_kv)
-    by_x = [sent[0]] + [along_x(sent[k], k) for k in (1, 2, 3)]
+    x2, x1, x3 = (along_x(sent[k], k) for k in (2, 1, 3))
+    by_x = [sent[0], x1, x2, x3]
     same, across = regroup(by_x)
     from1, from3 = along_y(same, 1), along_y(across, 3)
 
@@ -491,7 +493,8 @@
     orders = jnp.concatenate([orders, other_core(orders)], axis=0)
     pick = order_rows(orders)
 
-    parts = [attended] + [turned(attended, k, 0) for k in (1, 2, 3)]
+    next2, next1, next3 = (turned(attended, k, 0) for k in (2, 1, 3))
+    parts = [attended, next2, next1, next3]
     far, near = [gathered([a[i : i + 16] for a in parts]) for i in (0, 16)]
     first_far, first_near = project(far[:3], weights), project(near[:3], weights)
     keep2, up3, down3, up4 = plain(
@@ -502,9 +505,10 @@
     keep6, down1, keep0, up1 = plain(
         near_body, [SUM, SENT, SUM, SENT], *near[3], *weights, first_near
     )
-    below1, above1 = along_z(up1, 1), along_z(down1, -1)
     up2, down2 = plain(middle_body, [SENT, SENT], keep2, keep6, below3, above3)
     below2, above2 = along_z(up2, 2), along_z(down2, -2)
+    up1, down1, opposite = lax.optimization_barrier((up1, down1, opposite))
+    below1, above1 = along_z(up1, 1), along_z(down1, -1)
     own, other = plain(total_body, [HALF, HALF], keep0, below1, above1, below2, above2, opposite)
     return finish(own, other_core(other), pick)
 

time: 86.7 us -> 86.4 us (level)
  starting transfers between devices: 52.6 us -> 51.3 us
  waiting for transfers between devices: 15.4 us -> 16.4 us
    ppermute x11, starting transfers between devices: 25.7 us -> 23.4 us  [along(): lax.ppermute(value, 'batch', [(i, i ^ k << shift) for i in range(BATCH)])]
    ppermute x11, waiting for transfers between devices: 5.85 us -> 7.43 us  [along(): lax.ppermute(value, 'batch', [(i, i ^ k << shift) for i in range(BATCH)])]
where the time goes in v14:
time: 86.4 us; the launch traced here: 85.2 us
  starting transfers between devices  51.3 us (59%)
  waiting for transfers between devices  16.4 us (19%)
  Pallas kernels  16.2 us (19%)
  local copies, waits for them, and re-layouts  1.01 us (1%)
    ppermute x11, starting transfers between devices, along(): lax.ppermute(value, 'batch', [(i, i ^ k << shift) for i in range(BATCH)])  23.4 us
    ppermute x7, starting transfers between devices, along_z(): lax.ppermute(value, 'head', [(i, (i + k) % HEADS) for i in range(HEADS)])  16.3 us
    ppermute x11, starting transfers between devices, turned(): return lax.ppermute(value, 'batch', pairs)  11.6 us
    ppermute x11, waiting for transfers between devices, turned(): return lax.ppermute(value, 'batch', pairs)  8.94 us
    ppermute x11, waiting for transfers between devices, along(): lax.ppermute(value, 'batch', [(i, i ^ k << shift) for i in range(BATCH)])  7.43 us
    pallas_call x2, Pallas kernels, prefix_keep(): pl.pallas_call(prefix_keep_body, out_shape=[out, out], in_specs=[VMEM] *...  3.67 us
    pallas_call x1, Pallas kernels, local_parts(): pl.pallas_call(local_body, out_shape=[out] * 4, in_specs=[HBM] * 6, out_s...  3.52 us
    pallas_call x1, Pallas kernels, prefix_send(): pl.pallas_call(prefix_send_body, out_shape=jax.ShapeDtypeStruct((33, GROU...  3.37 us
  transfers between devices with their start and end apart: 29, of which 10 were waited for; matrix products, arithmetic and copies ran while one was open for 0% of the time, Pallas kernels for 18%

profile of v14, /device:TPU:1, one launch (start us, length us, event | category | flops | bytes accessed | tf_op | source)
XLA Modules:
  0.0 85.2 jit_solution(13218425629520346243)
XLA Ops:
  0.0 3.2 %collective-permute-start.4 = (bf16[2,2048,128]{2,1,0:T(8,128)(2,1)}, bf16[2,2048,128]{2,1,0:T(8,128)(2,1)S(1)}, u32[]{:S(2)}, u32[]{:S(2)}) collective-permute-start(bf16[2,2048,128]{2,1,0:T(8,128)(2,1)} %kv0.5), channel_id=1, source_target_pairs={{0,8},{8,0},{16,24},{24,16},{32,40},{40,32},{48,56},{56,48},{64,72... | collective-permute-start | bytes 3145736 | tf_op jit(solution)/shard_map/ppermute | solution.py:443
  3.2 3.5 %local_parts.1 = (bf16[18,16,128]{2,1,0:T(8,128)(2,1)}, bf16[18,16,128]{2,1,0:T(8,128)(2,1)}, bf16[18,16,128]{2,1,0:T(8,128)(2,1)}, bf16[18,16,128]{2,1,0:T(8,128)(2,1)}) custom-call(bf16[32,2048]{1,0:T(8,128)(2,1)} %q_in.1, s32[32]{0:T(128)} %prompt_in.1, s32[8,32]{1,0:T(8,128)} %bitcast.1, s32[32]{0:T(128)} %length_in.1, bf16[2,32,128]{2,1,0:T(8,128)(2,1)} %new_in.1, ...), custom_call_target="tpu_custom_call" | custom-call | tf_op jit(solution)/shard_map/local_parts/pallas_call | solution.py:131
  6.8 1.1 %collective-permute-start = (bf16[18,16,128]{2,1,0:T(8,128)(2,1)}, bf16[18,16,128]{2,1,0:T(8,128)(2,1)S(1)}, u32[]{:S(2)}, u32[]{:S(2)}) collective-permute-start(bf16[18,16,128]{2,1,0:T(8,128)(2,1)} %get-tuple-element.35), channel_id=1, source_target_pairs={{0,128},{8,136},{16,144},{24,152},{32,160},{40,168},{48,176},{56,1... | collective-permute-start | bytes 221192 | tf_op jit(solution)/shard_map/ppermute | solution.py:443
  7.9 0.3 collective-permute-start.1
  8.2 1.9 %collective-permute-start.2 = (bf16[18,16,128]{2,1,0:T(8,128)(2,1)}, bf16[18,16,128]{2,1,0:T(8,128)(2,1)S(1)}, u32[]{:S(2)}, u32[]{:S(2)}) collective-permute-start(bf16[18,16,128]{2,1,0:T(8,128)(2,1)} %get-tuple-element.37), channel_id=1, source_target_pairs={{0,192},{8,200},{16,208},{24,216},{32,224},{40,232},{48,240},{56,2... | collective-permute-start | bytes 221192 | tf_op jit(solution)/shard_map/ppermute | solution.py:443
  10.1 2.3 %collective-permute-done.a2.s2 = bf16[18,16,128]{2,1,0:T(8,128)(2,1)S(1)} collective-permute-done((bf16[18,16,128]{2,1,0:T(8,128)(2,1)}, bf16[18,16,128]{2,1,0:T(8,128)(2,1)S(1)}, u32[]{:S(2)}, u32[]{:S(2)}) %collective-permute-start) | collective-permute-done | bytes 73760 | tf_op jit(solution)/shard_map/ppermute | solution.py:443
  12.4 0.0 collective-permute-done.1.a1.s1
  12.4 1.5 %collective-permute-done.2.a3.s3 = bf16[18,16,128]{2,1,0:T(8,128)(2,1)S(1)} collective-permute-done((bf16[18,16,128]{2,1,0:T(8,128)(2,1)}, bf16[18,16,128]{2,1,0:T(8,128)(2,1)S(1)}, u32[]{:S(2)}, u32[]{:S(2)}) %collective-permute-start.2) | collective-permute-done | bytes 73760 | tf_op jit(solution)/shard_map/ppermute | solution.py:443
  13.9 0.9 %copy-done.2 = bf16[18,16,128]{2,1,0:T(8,128)(2,1)S(1)} copy-done((bf16[18,16,128]{2,1,0:T(8,128)(2,1)S(1)}, bf16[18,16,128]{2,1,0:T(8,128)(2,1)}, u32[]{:S(2)}) %copy-start.2) | copy-done | bytes 73752
  14.8 1.7 %collective-permute-start.3 = (bf16[37,16,128]{2,1,0:T(8,128)(2,1)S(1)}, bf16[37,16,128]{2,1,0:T(8,128)(2,1)S(1)}, u32[]{:S(2)}, u32[]{:S(2)}) collective-permute-start(bf16[37,16,128]{2,1,0:T(8,128)(2,1)S(1)} %get-tuple-element.39), channel_id=1, source_target_pairs={{0,48},{8,56},{16,32},{24,40},{32,16},{40,24},{48,0},{56,8},{64,11... | collective-permute-start | bytes 454664 | tf_op jit(solution)/shard_map/ppermute | solution.py:443
  16.5 0.0 collective-permute-start.5
  16.5 0.0 collective-permute-done.4.kv1
  16.6 1.8 %prefix_keep.2 = (f32[16,16,128]{2,1,0:T(8,128)S(1)}, f32[16,16,128]{2,1,0:T(8,128)S(1)}) custom-call(bf16[17,16,128]{2,1,0:T(8,128)(2,1)S(1)} %get-tuple-element.40.q, bf16[2,2048,128]{2,1,0:T(8,128)(2,1)S(1)} %copy-done.1, bf16[2,2048,128]{2,1,0:T(8,128)(2,1)S(1)} %collective-permute-done.4.kv1), custom_call_target="tpu_custom_call" | custom-call | flops 536870912 | bytes 2500000 | tf_op jit(solution)/shard_map/prefix_keep/pallas_call | solution.py:246
  18.4 0.0 copy-start
  18.4 2.2 %collective-permute-done.3.qb = bf16[37,16,128]{2,1,0:T(8,128)(2,1)S(1)} collective-permute-done((bf16[37,16,128]{2,1,0:T(8,128)(2,1)S(1)}, bf16[37,16,128]{2,1,0:T(8,128)(2,1)S(1)}, u32[]{:S(2)}, u32[]{:S(2)}) %collective-permute-start.3) | collective-permute-done | bytes 151584 | tf_op jit(solution)/shard_map/ppermute | solution.py:443
  20.6 0.0 collective-permute-start.6
  20.6 3.4 %prefix_send.1 = bf16[33,16,128]{2,1,0:T(8,128)(2,1)S(1)} custom-call(bf16[17,16,128]{2,1,0:T(8,128)(2,1)S(1)} %collective-permute-done.5.qa, bf16[37,16,128]{2,1,0:T(8,128)(2,1)S(1)} %collective-permute-done.3.qb, bf16[2,2048,128]{2,1,0:T(8,128)(2,1)S(1)} %copy-done.1, bf16[2,2048,128]{2,1,0:T(8,128)(2,1)S(1)} %collective-permute-done.4.kv1, ...), custom_call_target="tpu_custom_call" | custom-call | flops 1073741824 | bytes 2500000 | tf_op jit(solution)/shard_map/prefix_send/pallas_call | solution.py:233
  24.0 0.0 copy-start.3
  24.0 0.6 collective-permute-done.6.q.far
  24.7 0.9 %collective-permute-start.7 = (bf16[33,16,128]{2,1,0:T(8,128)(2,1)S(1)}, bf16[33,16,128]{2,1,0:T(8,128)(2,1)S(1)}, u32[]{:S(2)}, u32[]{:S(2)}) collective-permute-start(bf16[33,16,128]{2,1,0:T(8,128)(2,1)S(1)} %prefix_send.1), channel_id=1, source_target_pairs={{0,16},{8,24},{16,0},{24,8},{32,48},{40,56},{48,32},{56,40},{64,80... | collective-permute-start | bytes 405512 | tf_op jit(solution)/shard_map/ppermute | solution.py:443
  25.6 2.4 %collective-permute-start.15 = (bf16[2048,512]{1,0:T(8,128)(2,1)S(1)}, bf16[2048,512]{1,0:T(8,128)(2,1)S(1)}, u32[]{:S(2)}, u32[]{:S(2)}) collective-permute-start(bf16[2048,512]{1,0:T(8,128)(2,1)S(1)} %copy-done), channel_id=1, source_target_pairs={{0,8},{8,0},{16,24},{24,16},{32,40},{40,32},{48,56},{56,48},{64,72... | collective-permute-start | bytes 6291464 | tf_op jit(solution)/shard_map/ppermute | solution.py:443
  28.0 1.8 %prefix_keep.3 = (f32[16,16,128]{2,1,0:T(8,128)S(1)}, f32[16,16,128]{2,1,0:T(8,128)S(1)}) custom-call(bf16[37,16,128]{2,1,0:T(8,128)(2,1)S(1)} %collective-permute-done.6.q.far, bf16[2,2048,128]{2,1,0:T(8,128)(2,1)S(1)} %copy-done.1, bf16[2,2048,128]{2,1,0:T(8,128)(2,1)S(1)} %collective-permute-done.4.kv1), custom_call_target="tpu_custom_call" | custom-call | flops 536870912 | bytes 2500000 | tf_op jit(solution)/shard_map/prefix_keep/pallas_call | solution.py:246
  29.9 0.7 combine.1
  30.5 4.5 %collective-permute-start.8 = (bf16[32,2048]{1,0:T(8,128)(2,1)S(1)}, bf16[32,2048]{1,0:T(8,128)(2,1)S(1)}, u32[]{:S(2)}, u32[]{:S(2)}) collective-permute-start(bf16[32,2048]{1,0:T(8,128)(2,1)S(1)} %combine.1), channel_id=1, source_target_pairs={{0,128},{8,40},{16,144},{24,56},{32,160},{40,8},{48,176},{56,24},{... | collective-permute-start | bytes 393224 | tf_op jit(solution)/shard_map/ppermute | solution.py:460
  35.0 0.4 collective-permute-start.10
  35.4 2.0 %collective-permute-done.8 = bf16[32,2048]{1,0:T(8,128)(2,1)S(1)} collective-permute-done((bf16[32,2048]{1,0:T(8,128)(2,1)S(1)}, bf16[32,2048]{1,0:T(8,128)(2,1)S(1)}, u32[]{:S(2)}, u32[]{:S(2)}) %collective-permute-start.8) | collective-permute-done | bytes 131104 | tf_op jit(solution)/shard_map/ppermute | solution.py:460
  37.4 1.7 %collective-permute-done.9 = bf16[32,2048]{1,0:T(8,128)(2,1)S(1)} collective-permute-done((bf16[32,2048]{1,0:T(8,128)(2,1)S(1)}, bf16[32,2048]{1,0:T(8,128)(2,1)S(1)}, u32[]{:S(2)}, u32[]{:S(2)}) %collective-permute-start.9) | collective-permute-done | bytes 131104 | tf_op jit(solution)/shard_map/ppermute | solution.py:460
  39.1 0.9 %collective-permute-done.10 = bf16[32,2048]{1,0:T(8,128)(2,1)S(1)} collective-permute-done((bf16[32,2048]{1,0:T(8,128)(2,1)S(1)}, bf16[32,2048]{1,0:T(8,128)(2,1)S(1)}, u32[]{:S(2)}, u32[]{:S(2)}) %collective-permute-start.10) | collective-permute-done | bytes 131104 | tf_op jit(solution)/shard_map/ppermute | solution.py:460
  40.1 0.9 %collective-permute-start.16 = (bf16[64,2048]{1,0:T(8,128)(2,1)S(1)}, bf16[64,2048]{1,0:T(8,128)(2,1)S(1)}, u32[]{:S(2)}, u32[]{:S(2)}) collective-permute-start(bf16[64,2048]{1,0:T(8,128)(2,1)S(1)} %pad_maximum_fusion.1.a), channel_id=1, source_target_pairs={{0,48},{8,200},{16,32},{24,216},{32,16},{40,232},{48,0},{56,248},{... | collective-permute-start | bytes 786440 | tf_op jit(solution)/shard_map/ppermute | solution.py:460
  41.0 2.0 %collective-permute-start.11 = (bf16[64,2048]{1,0:T(8,128)(2,1)S(1)}, bf16[64,2048]{1,0:T(8,128)(2,1)S(1)}, u32[]{:S(2)}, u32[]{:S(2)}) collective-permute-start(bf16[64,2048]{1,0:T(8,128)(2,1)S(1)} %pad_maximum_fusion.a), channel_id=1, source_target_pairs={{0,48},{8,200},{16,32},{24,216},{32,16},{40,232},{48,0},{56,248},{... | collective-permute-start | bytes 786440 | tf_op jit(solution)/shard_map/ppermute | solution.py:460
  43.0 0.9 %collective-permute-start.13 = (bf16[64,2048]{1,0:T(8,128)(2,1)S(1)}, bf16[64,2048]{1,0:T(8,128)(2,1)S(1)}, u32[]{:S(2)}, u32[]{:S(2)}) collective-permute-start(bf16[64,2048]{1,0:T(8,128)(2,1)S(1)} %pad_maximum_fusion.a), channel_id=1, source_target_pairs={{0,16},{8,72},{16,0},{24,88},{32,48},{40,104},{48,32},{56,120},{64... | collective-permute-start | bytes 786440 | tf_op jit(solution)/shard_map/ppermute | solution.py:460
  43.8 2.8 %collective-permute-done.16.c = bf16[64,2048]{1,0:T(8,128)(2,1)S(1)} collective-permute-done((bf16[64,2048]{1,0:T(8,128)(2,1)S(1)}, bf16[64,2048]{1,0:T(8,128)(2,1)S(1)}, u32[]{:S(2)}, u32[]{:S(2)}) %collective-permute-start.16) | collective-permute-done | bytes 262176 | tf_op jit(solution)/shard_map/ppermute | solution.py:460
  46.6 0.1 collective-permute-start.17
  46.7 1.4 %collective-permute-start.19 = (bf16[32,2048]{1,0:T(8,128)(2,1)S(1)}, bf16[32,2048]{1,0:T(8,128)(2,1)S(1)}, u32[]{:S(2)}, u32[]{:S(2)}) collective-permute-start(bf16[32,2048]{1,0:T(8,128)(2,1)S(1)} %slice.75), channel_id=1, source_target_pairs={{0,48},{8,200},{16,32},{24,216},{32,16},{40,232},{48,0},{56,248},{... | collective-permute-start | bytes 393224 | tf_op jit(solution)/shard_map/ppermute | solution.py:460
  48.2 1.5 %collective-permute-done.11.c = bf16[64,2048]{1,0:T(8,128)(2,1)S(1)} collective-permute-done((bf16[64,2048]{1,0:T(8,128)(2,1)S(1)}, bf16[64,2048]{1,0:T(8,128)(2,1)S(1)}, u32[]{:S(2)}, u32[]{:S(2)}) %collective-permute-start.11) | collective-permute-done | bytes 262176 | tf_op jit(solution)/shard_map/ppermute | solution.py:460
  49.7 0.1 collective-permute-start.12
  49.8 1.4 %collective-permute-start.14 = (bf16[32,2048]{1,0:T(8,128)(2,1)S(1)}, bf16[32,2048]{1,0:T(8,128)(2,1)S(1)}, u32[]{:S(2)}, u32[]{:S(2)}) collective-permute-start(bf16[32,2048]{1,0:T(8,128)(2,1)S(1)} %slice.69), channel_id=1, source_target_pairs={{0,48},{8,200},{16,32},{24,216},{32,16},{40,232},{48,0},{56,248},{... | collective-permute-start | bytes 393224 | tf_op jit(solution)/shard_map/ppermute | solution.py:460
  51.3 1.0 %project.3.first = f32[4,48,1024]{2,1,0:T(8,128)S(1)} custom-call(bf16[64,2048]{1,0:T(8,128)(2,1)S(1)} %pad_maximum_fusion.1.a, bf16[64,2048]{1,0:T(8,128)(2,1)S(1)} %collective-permute-done.18.b, bf16[64,2048]{1,0:T(8,128)(2,1)S(1)} %collective-permute-done.16.c, bf16[2048,512]{1,0:T(8,128)(2,1)S(1)} %copy-done, ...), custom_call_target="tpu_custom_call" | custom-call | flops 805306368 | bytes 4500000 | tf_op jit(solution)/shard_map/project/pallas_call | solution.py:325
  52.3 0.0 collective-permute-done.17.a
  52.3 0.0 collective-permute-done.19.b
  52.3 0.9 %far.1 = (f32[64,1024]{1,0:T(8,128)S(1)}, bf16[64,1024]{1,0:T(8,128)(2,1)S(1)}, bf16[64,1024]{1,0:T(8,128)(2,1)S(1)}, bf16[64,1024]{1,0:T(8,128)(2,1)S(1)}) custom-call(bf16[32,2048]{1,0:T(8,128)(2,1)S(1)} %collective-permute-done.17.a, bf16[32,2048]{1,0:T(8,128)(2,1)S(1)} %collective-permute-done.19.b, bf16[2048,512]{1,0:T(8,128)(2,1)S(1)} %copy-done, ...), custom_call_target="tpu_custom_call" | custom-call | tf_op jit(solution)/shard_map/far/pallas_call | solution.py:368
  53.2 2.0 %collective-permute-start.23 = (bf16[64,1024]{1,0:T(8,128)(2,1)S(1)}, bf16[64,1024]{1,0:T(8,128)(2,1)S(1)}, u32[]{:S(2)}, u32[]{:S(2)}) collective-permute-start(bf16[64,1024]{1,0:T(8,128)(2,1)S(1)} %get-tuple-element.58), channel_id=1, source_target_pairs={{0,1},{1,2},{2,3},{3,4},{4,5},{5,6},{6,7},{7,0},{8,9},{9,10},{10,1... | collective-permute-start | bytes 393224 | tf_op jit(solution)/shard_map/ppermute | solution.py:470
  55.2 4.0 %collective-permute-start.24 = (bf16[64,1024]{1,0:T(8,128)(2,1)S(1)}, bf16[64,1024]{1,0:T(8,128)(2,1)S(1)}, u32[]{:S(2)}, u32[]{:S(2)}) collective-permute-start(bf16[64,1024]{1,0:T(8,128)(2,1)S(1)} %get-tuple-element.59), channel_id=1, source_target_pairs={{0,7},{1,0},{2,1},{3,2},{4,3},{5,4},{6,5},{7,6},{8,15},{9,8},{10,9... | collective-permute-start | bytes 393224 | tf_op jit(solution)/shard_map/ppermute | solution.py:470
  59.2 3.9 %collective-permute-start.20 = (bf16[64,1024]{1,0:T(8,128)(2,1)S(1)}, bf16[64,1024]{1,0:T(8,128)(2,1)S(1)}, u32[]{:S(2)}, u32[]{:S(2)}) collective-permute-start(bf16[64,1024]{1,0:T(8,128)(2,1)S(1)} %get-tuple-element.53), channel_id=1, source_target_pairs={{0,4},{1,5},{2,6},{3,7},{4,0},{5,1},{6,2},{7,3},{8,12},{9,13},{10,... | collective-permute-start | bytes 393224 | tf_op jit(solution)/shard_map/ppermute | solution.py:470
  63.2 1.0 %project.2.first = f32[4,48,1024]{2,1,0:T(8,128)S(1)} custom-call(bf16[64,2048]{1,0:T(8,128)(2,1)S(1)} %pad_maximum_fusion.a, bf16[64,2048]{1,0:T(8,128)(2,1)S(1)} %collective-permute-done.13.b, bf16[64,2048]{1,0:T(8,128)(2,1)S(1)} %collective-permute-done.11.c, bf16[2048,512]{1,0:T(8,128)(2,1)S(1)} %copy-done, bf16[2048,512]{1,0:T(8,128)(2,1)S(1)} %collective-permute-done.15.w1), custom_call_target="tpu_custom_call" | custom-call | flops 805306368 | bytes 4500000 | tf_op jit(solution)/shard_map/project/pallas_call | solution.py:325
  64.2 0.0 collective-permute-done.14.b
  64.2 0.9 %near.1 = (f32[64,1024]{1,0:T(8,128)S(1)}, bf16[64,1024]{1,0:T(8,128)(2,1)S(1)}, f32[64,1024]{1,0:T(8,128)S(1)}, bf16[64,1024]{1,0:T(8,128)(2,1)S(1)}) custom-call(bf16[32,2048]{1,0:T(8,128)(2,1)S(1)} %collective-permute-done.12.a, bf16[32,2048]{1,0:T(8,128)(2,1)S(1)} %collective-permute-done.14.b, bf16[2048,512]{1,0:T(8,128)(2,1)S(1)} %copy-done, ...), custom_call_target="tpu_custom_call" | custom-call | tf_op jit(solution)/shard_map/near/pallas_call | solution.py:368
  65.1 0.0 collective-permute-done.24.above
  65.1 0.1 middle.1
  65.2 0.1 collective-permute-start.25
  65.3 3.6 %collective-permute-start.26 = (bf16[64,1024]{1,0:T(8,128)(2,1)S(1)}, bf16[64,1024]{1,0:T(8,128)(2,1)S(1)}, u32[]{:S(2)}, u32[]{:S(2)}) collective-permute-start(bf16[64,1024]{1,0:T(8,128)(2,1)S(1)} %get-tuple-element.61), channel_id=1, source_target_pairs={{0,6},{1,7},{2,0},{3,1},{4,2},{5,3},{6,4},{7,5},{8,14},{9,15},{10,... | collective-permute-start | bytes 393224 | tf_op jit(solution)/shard_map/ppermute | solution.py:470
  68.8 0.0 collective-permute-done.20.opposite
  68.8 0.2 collective-permute-start.21
  69.0 2.5 %collective-permute-start.22 = (bf16[64,1024]{1,0:T(8,128)(2,1)S(1)}, bf16[64,1024]{1,0:T(8,128)(2,1)S(1)}, u32[]{:S(2)}, u32[]{:S(2)}) collective-permute-start(bf16[64,1024]{1,0:T(8,128)(2,1)S(1)} %get-tuple-element.55), channel_id=1, source_target_pairs={{0,7},{1,0},{2,1},{3,2},{4,3},{5,4},{6,5},{7,6},{8,15},{9,8},{10,9... | collective-permute-start | bytes 393224 | tf_op jit(solution)/shard_map/ppermute | solution.py:470
  71.5 8.7 %collective-permute-start.28 = (bf16[4,16,128]{2,1,0:T(8,128)(2,1)S(1)}, bf16[4,16,128]{2,1,0:T(8,128)(2,1)S(1)}, u32[]{:S(2)}, u32[]{:S(2)}) collective-permute-start(bf16[4,16,128]{2,1,0:T(8,128)(2,1)S(1)} %pad_maximum_fusion.2), channel_id=1, source_target_pairs={{0,8},{8,0},{16,24},{24,16},{32,40},{40,32},{48,56},{56,48},{64,72... | collective-permute-start | bytes 49160 | tf_op jit(solution)/shard_map/ppermute | solution.py:443
  80.2 0.0 collective-permute-done.25.below2
  80.2 0.0 collective-permute-done.26.above2
  80.2 0.0 collective-permute-done.22.above1
  80.2 0.1 total.1
  80.3 3.0 %collective-permute-start.27 = (bf16[64,512]{1,0:T(8,128)(2,1)S(1)}, bf16[64,512]{1,0:T(8,128)(2,1)S(1)}, u32[]{:S(2)}, u32[]{:S(2)}) collective-permute-start(bf16[64,512]{1,0:T(8,128)(2,1)S(1)} %get-tuple-element.64), channel_id=1, source_target_pairs={{0,8},{8,0},{16,24},{24,16},{32,40},{40,32},{48,56},{56,48},{64,72... | collective-permute-start | bytes 196616 | tf_op jit(solution)/shard_map/ppermute | solution.py:443
  83.4 0.0 collective-permute-done.28
  83.4 0.1 order_rows.1.pick
  83.5 0.8 collective-permute-done.27.other
  84.3 0.9 %finish.1 = bf16[128,512]{1,0:T(8,128)(2,1)} custom-call(bf16[64,512]{1,0:T(8,128)(2,1)S(1)} %get-tuple-element.63.own, bf16[64,512]{1,0:T(8,128)(2,1)S(1)} %collective-permute-done.27.other, bf16[128,128]{1,0:T(8,128)(2,1)S(1)} %order_rows.1.pick), custom_call_target="tpu_custom_call" | custom-call | tf_op jit(solution)/shard_map/finish/pallas_call | solution.py:432
  (32 shorter events, 0.2 us)
Async XLA Ops:
  0.0 16.5 %copy-start.1 = (bf16[2,2048,128]{2,1,0:T(8,128)(2,1)S(1)}, bf16[2,2048,128]{2,1,0:T(8,128)(2,1)}, u32[]{:S(2)}) copy-start(bf16[2,2048,128]{2,1,0:T(8,128)(2,1)} %kv0.5) | copy-start | bytes 3145732
  0.0 16.5 %collective-permute-start.4 = (bf16[2,2048,128]{2,1,0:T(8,128)(2,1)}, bf16[2,2048,128]{2,1,0:T(8,128)(2,1)S(1)}, u32[]{:S(2)}, u32[]{:S(2)}) collective-permute-start(bf16[2,2048,128]{2,1,0:T(8,128)(2,1)} %kv0.5), channel_id=1, source_target_pairs={{0,8},{8,0},{16,24},{24,16},{32,40},{40,32},{48,56},{56,48},{64,72... | collective-permute-start | bytes 3145736 | tf_op jit(solution)/shard_map/ppermute | solution.py:443
  6.8 5.6 %collective-permute-start = (bf16[18,16,128]{2,1,0:T(8,128)(2,1)}, bf16[18,16,128]{2,1,0:T(8,128)(2,1)S(1)}, u32[]{:S(2)}, u32[]{:S(2)}) collective-permute-start(bf16[18,16,128]{2,1,0:T(8,128)(2,1)} %get-tuple-element.35), channel_id=1, source_target_pairs={{0,128},{8,136},{16,144},{24,152},{32,160},{40,168},{48,176},{56,1... | collective-permute-start | bytes 221192 | tf_op jit(solution)/shard_map/ppermute | solution.py:443
  7.9 4.6 %collective-permute-start.1 = (bf16[18,16,128]{2,1,0:T(8,128)(2,1)}, bf16[18,16,128]{2,1,0:T(8,128)(2,1)S(1)}, u32[]{:S(2)}, u32[]{:S(2)}) collective-permute-start(bf16[18,16,128]{2,1,0:T(8,128)(2,1)} %get-tuple-element.36), channel_id=1, source_target_pairs={{0,64},{8,72},{16,80},{24,88},{32,96},{40,104},{48,112},{56,120},{... | collective-permute-start | bytes 221192 | tf_op jit(solution)/shard_map/ppermute | solution.py:443
  8.2 5.7 %collective-permute-start.2 = (bf16[18,16,128]{2,1,0:T(8,128)(2,1)}, bf16[18,16,128]{2,1,0:T(8,128)(2,1)S(1)}, u32[]{:S(2)}, u32[]{:S(2)}) collective-permute-start(bf16[18,16,128]{2,1,0:T(8,128)(2,1)} %get-tuple-element.37), channel_id=1, source_target_pairs={{0,192},{8,200},{16,208},{24,216},{32,224},{40,232},{48,240},{56,2... | collective-permute-start | bytes 221192 | tf_op jit(solution)/shard_map/ppermute | solution.py:443
  13.9 0.9 %copy-start.2 = (bf16[18,16,128]{2,1,0:T(8,128)(2,1)S(1)}, bf16[18,16,128]{2,1,0:T(8,128)(2,1)}, u32[]{:S(2)}) copy-start(bf16[18,16,128]{2,1,0:T(8,128)(2,1)} %get-tuple-element.38.a0.s0) | copy-start | bytes 221188
  14.8 5.8 %collective-permute-start.3 = (bf16[37,16,128]{2,1,0:T(8,128)(2,1)S(1)}, bf16[37,16,128]{2,1,0:T(8,128)(2,1)S(1)}, u32[]{:S(2)}, u32[]{:S(2)}) collective-permute-start(bf16[37,16,128]{2,1,0:T(8,128)(2,1)S(1)} %get-tuple-element.39), channel_id=1, source_target_pairs={{0,48},{8,56},{16,32},{24,40},{32,16},{40,24},{48,0},{56,8},{64,11... | collective-permute-start | bytes 454664 | tf_op jit(solution)/shard_map/ppermute | solution.py:443
  16.5 4.1 %collective-permute-start.5 = (bf16[17,16,128]{2,1,0:T(8,128)(2,1)S(1)}, bf16[17,16,128]{2,1,0:T(8,128)(2,1)S(1)}, u32[]{:S(2)}, u32[]{:S(2)}) collective-permute-start(bf16[17,16,128]{2,1,0:T(8,128)(2,1)S(1)} %get-tuple-element.40.q), channel_id=1, source_target_pairs={{0,16},{8,24},{16,0},{24,8},{32,48},{40,56},{48,32},{56,40},{64,80... | collective-permute-start | bytes 208904 | tf_op jit(solution)/shard_map/ppermute | solution.py:443
  18.4 7.2 %copy-start = (bf16[2048,512]{1,0:T(8,128)(2,1)S(1)}, bf16[2048,512]{1,0:T(8,128)(2,1)}, u32[]{:S(2)}) copy-start(bf16[2048,512]{1,0:T(8,128)(2,1)} %w0.7) | copy-start | bytes 6291460
  20.6 4.0 %collective-permute-start.6 = (bf16[37,16,128]{2,1,0:T(8,128)(2,1)S(1)}, bf16[37,16,128]{2,1,0:T(8,128)(2,1)S(1)}, u32[]{:S(2)}, u32[]{:S(2)}) collective-permute-start(bf16[37,16,128]{2,1,0:T(8,128)(2,1)S(1)} %collective-permute-done.3.qb), channel_id=1, source_target_pairs={{0,16},{8,24},{16,0},{24,8},{32,48},{40,56},{48,32},{56,40},{64,80... | collective-permute-start | bytes 454664 | tf_op jit(solution)/shard_map/ppermute | solution.py:443
  24.0 5.8 %copy-start.3 = (bf16[18,16,128]{2,1,0:T(8,128)(2,1)S(1)}, bf16[18,16,128]{2,1,0:T(8,128)(2,1)}, u32[]{:S(2)}) copy-start(bf16[18,16,128]{2,1,0:T(8,128)(2,1)} %get-tuple-element.38.a0.s0) | copy-start | bytes 221188
  24.7 5.2 %collective-permute-start.7 = (bf16[33,16,128]{2,1,0:T(8,128)(2,1)S(1)}, bf16[33,16,128]{2,1,0:T(8,128)(2,1)S(1)}, u32[]{:S(2)}, u32[]{:S(2)}) collective-permute-start(bf16[33,16,128]{2,1,0:T(8,128)(2,1)S(1)} %prefix_send.1), channel_id=1, source_target_pairs={{0,16},{8,24},{16,0},{24,8},{32,48},{40,56},{48,32},{56,40},{64,80... | collective-permute-start | bytes 405512 | tf_op jit(solution)/shard_map/ppermute | solution.py:443
  25.6 25.7 %collective-permute-start.15 = (bf16[2048,512]{1,0:T(8,128)(2,1)S(1)}, bf16[2048,512]{1,0:T(8,128)(2,1)S(1)}, u32[]{:S(2)}, u32[]{:S(2)}) collective-permute-start(bf16[2048,512]{1,0:T(8,128)(2,1)S(1)} %copy-done), channel_id=1, source_target_pairs={{0,8},{8,0},{16,24},{24,16},{32,40},{40,32},{48,56},{56,48},{64,72... | collective-permute-start | bytes 6291464 | tf_op jit(solution)/shard_map/ppermute | solution.py:443
  30.5 6.8 %collective-permute-start.8 = (bf16[32,2048]{1,0:T(8,128)(2,1)S(1)}, bf16[32,2048]{1,0:T(8,128)(2,1)S(1)}, u32[]{:S(2)}, u32[]{:S(2)}) collective-permute-start(bf16[32,2048]{1,0:T(8,128)(2,1)S(1)} %combine.1), channel_id=1, source_target_pairs={{0,128},{8,40},{16,144},{24,56},{32,160},{40,8},{48,176},{56,24},{... | collective-permute-start | bytes 393224 | tf_op jit(solution)/shard_map/ppermute | solution.py:460
  35.0 4.1 %collective-permute-start.9 = (bf16[32,2048]{1,0:T(8,128)(2,1)S(1)}, bf16[32,2048]{1,0:T(8,128)(2,1)S(1)}, u32[]{:S(2)}, u32[]{:S(2)}) collective-permute-start(bf16[32,2048]{1,0:T(8,128)(2,1)S(1)} %combine.1), channel_id=1, source_target_pairs={{0,64},{8,24},{16,80},{24,8},{32,96},{40,56},{48,112},{56,40},{64,... | collective-permute-start | bytes 393224 | tf_op jit(solution)/shard_map/ppermute | solution.py:460
  35.0 5.0 %collective-permute-start.10 = (bf16[32,2048]{1,0:T(8,128)(2,1)S(1)}, bf16[32,2048]{1,0:T(8,128)(2,1)S(1)}, u32[]{:S(2)}, u32[]{:S(2)}) collective-permute-start(bf16[32,2048]{1,0:T(8,128)(2,1)S(1)} %combine.1), channel_id=1, source_target_pairs={{0,192},{8,56},{16,208},{24,40},{32,224},{40,24},{48,240},{56,8},{... | collective-permute-start | bytes 393224 | tf_op jit(solution)/shard_map/ppermute | solution.py:460
  40.1 6.5 %collective-permute-start.16 = (bf16[64,2048]{1,0:T(8,128)(2,1)S(1)}, bf16[64,2048]{1,0:T(8,128)(2,1)S(1)}, u32[]{:S(2)}, u32[]{:S(2)}) collective-permute-start(bf16[64,2048]{1,0:T(8,128)(2,1)S(1)} %pad_maximum_fusion.1.a), channel_id=1, source_target_pairs={{0,48},{8,200},{16,32},{24,216},{32,16},{40,232},{48,0},{56,248},{... | collective-permute-start | bytes 786440 | tf_op jit(solution)/shard_map/ppermute | solution.py:460
  40.9 5.8 %collective-permute-start.18 = (bf16[64,2048]{1,0:T(8,128)(2,1)S(1)}, bf16[64,2048]{1,0:T(8,128)(2,1)S(1)}, u32[]{:S(2)}, u32[]{:S(2)}) collective-permute-start(bf16[64,2048]{1,0:T(8,128)(2,1)S(1)} %pad_maximum_fusion.1.a), channel_id=1, source_target_pairs={{0,16},{8,72},{16,0},{24,88},{32,48},{40,104},{48,32},{56,120},{64... | collective-permute-start | bytes 786440 | tf_op jit(solution)/shard_map/ppermute | solution.py:460
  41.0 8.7 %collective-permute-start.11 = (bf16[64,2048]{1,0:T(8,128)(2,1)S(1)}, bf16[64,2048]{1,0:T(8,128)(2,1)S(1)}, u32[]{:S(2)}, u32[]{:S(2)}) collective-permute-start(bf16[64,2048]{1,0:T(8,128)(2,1)S(1)} %pad_maximum_fusion.a), channel_id=1, source_target_pairs={{0,48},{8,200},{16,32},{24,216},{32,16},{40,232},{48,0},{56,248},{... | collective-permute-start | bytes 786440 | tf_op jit(solution)/shard_map/ppermute | solution.py:460
  43.0 6.9 %collective-permute-start.13 = (bf16[64,2048]{1,0:T(8,128)(2,1)S(1)}, bf16[64,2048]{1,0:T(8,128)(2,1)S(1)}, u32[]{:S(2)}, u32[]{:S(2)}) collective-permute-start(bf16[64,2048]{1,0:T(8,128)(2,1)S(1)} %pad_maximum_fusion.a), channel_id=1, source_target_pairs={{0,16},{8,72},{16,0},{24,88},{32,48},{40,104},{48,32},{56,120},{64... | collective-permute-start | bytes 786440 | tf_op jit(solution)/shard_map/ppermute | solution.py:460
  46.6 5.7 %collective-permute-start.17 = (bf16[32,2048]{1,0:T(8,128)(2,1)S(1)}, bf16[32,2048]{1,0:T(8,128)(2,1)S(1)}, u32[]{:S(2)}, u32[]{:S(2)}) collective-permute-start(bf16[32,2048]{1,0:T(8,128)(2,1)S(1)} %slice.74), channel_id=1, source_target_pairs={{0,16},{8,72},{16,0},{24,88},{32,48},{40,104},{48,32},{56,120},{64... | collective-permute-start | bytes 393224 | tf_op jit(solution)/shard_map/ppermute | solution.py:460
  46.7 5.6 %collective-permute-start.19 = (bf16[32,2048]{1,0:T(8,128)(2,1)S(1)}, bf16[32,2048]{1,0:T(8,128)(2,1)S(1)}, u32[]{:S(2)}, u32[]{:S(2)}) collective-permute-start(bf16[32,2048]{1,0:T(8,128)(2,1)S(1)} %slice.75), channel_id=1, source_target_pairs={{0,48},{8,200},{16,32},{24,216},{32,16},{40,232},{48,0},{56,248},{... | collective-permute-start | bytes 393224 | tf_op jit(solution)/shard_map/ppermute | solution.py:460
  49.7 14.5 %collective-permute-start.12 = (bf16[32,2048]{1,0:T(8,128)(2,1)S(1)}, bf16[32,2048]{1,0:T(8,128)(2,1)S(1)}, u32[]{:S(2)}, u32[]{:S(2)}) collective-permute-start(bf16[32,2048]{1,0:T(8,128)(2,1)S(1)} %slice.68), channel_id=1, source_target_pairs={{0,16},{8,72},{16,0},{24,88},{32,48},{40,104},{48,32},{56,120},{64... | collective-permute-start | bytes 393224 | tf_op jit(solution)/shard_map/ppermute | solution.py:460
  49.8 14.4 %collective-permute-start.14 = (bf16[32,2048]{1,0:T(8,128)(2,1)S(1)}, bf16[32,2048]{1,0:T(8,128)(2,1)S(1)}, u32[]{:S(2)}, u32[]{:S(2)}) collective-permute-start(bf16[32,2048]{1,0:T(8,128)(2,1)S(1)} %slice.69), channel_id=1, source_target_pairs={{0,48},{8,200},{16,32},{24,216},{32,16},{40,232},{48,0},{56,248},{... | collective-permute-start | bytes 393224 | tf_op jit(solution)/shard_map/ppermute | solution.py:460
  53.2 11.9 %collective-permute-start.23 = (bf16[64,1024]{1,0:T(8,128)(2,1)S(1)}, bf16[64,1024]{1,0:T(8,128)(2,1)S(1)}, u32[]{:S(2)}, u32[]{:S(2)}) collective-permute-start(bf16[64,1024]{1,0:T(8,128)(2,1)S(1)} %get-tuple-element.58), channel_id=1, source_target_pairs={{0,1},{1,2},{2,3},{3,4},{4,5},{5,6},{6,7},{7,0},{8,9},{9,10},{10,1... | collective-permute-start | bytes 393224 | tf_op jit(solution)/shard_map/ppermute | solution.py:470
  55.2 9.9 %collective-permute-start.24 = (bf16[64,1024]{1,0:T(8,128)(2,1)S(1)}, bf16[64,1024]{1,0:T(8,128)(2,1)S(1)}, u32[]{:S(2)}, u32[]{:S(2)}) collective-permute-start(bf16[64,1024]{1,0:T(8,128)(2,1)S(1)} %get-tuple-element.59), channel_id=1, source_target_pairs={{0,7},{1,0},{2,1},{3,2},{4,3},{5,4},{6,5},{7,6},{8,15},{9,8},{10,9... | collective-permute-start | bytes 393224 | tf_op jit(solution)/shard_map/ppermute | solution.py:470
  59.2 9.6 %collective-permute-start.20 = (bf16[64,1024]{1,0:T(8,128)(2,1)S(1)}, bf16[64,1024]{1,0:T(8,128)(2,1)S(1)}, u32[]{:S(2)}, u32[]{:S(2)}) collective-permute-start(bf16[64,1024]{1,0:T(8,128)(2,1)S(1)} %get-tuple-element.53), channel_id=1, source_target_pairs={{0,4},{1,5},{2,6},{3,7},{4,0},{5,1},{6,2},{7,3},{8,12},{9,13},{10,... | collective-permute-start | bytes 393224 | tf_op jit(solution)/shard_map/ppermute | solution.py:470
  65.2 15.0 %collective-permute-start.25 = (bf16[64,1024]{1,0:T(8,128)(2,1)S(1)}, bf16[64,1024]{1,0:T(8,128)(2,1)S(1)}, u32[]{:S(2)}, u32[]{:S(2)}) collective-permute-start(bf16[64,1024]{1,0:T(8,128)(2,1)S(1)} %get-tuple-element.60), channel_id=1, source_target_pairs={{0,2},{1,3},{2,4},{3,5},{4,6},{5,7},{6,0},{7,1},{8,10},{9,11},{10,... | collective-permute-start | bytes 393224 | tf_op jit(solution)/shard_map/ppermute | solution.py:470
  65.3 14.9 %collective-permute-start.26 = (bf16[64,1024]{1,0:T(8,128)(2,1)S(1)}, bf16[64,1024]{1,0:T(8,128)(2,1)S(1)}, u32[]{:S(2)}, u32[]{:S(2)}) collective-permute-start(bf16[64,1024]{1,0:T(8,128)(2,1)S(1)} %get-tuple-element.61), channel_id=1, source_target_pairs={{0,6},{1,7},{2,0},{3,1},{4,2},{5,3},{6,4},{7,5},{8,14},{9,15},{10,... | collective-permute-start | bytes 393224 | tf_op jit(solution)/shard_map/ppermute | solution.py:470
  68.8 11.4 %collective-permute-start.21 = (bf16[64,1024]{1,0:T(8,128)(2,1)S(1)}, bf16[64,1024]{1,0:T(8,128)(2,1)S(1)}, u32[]{:S(2)}, u32[]{:S(2)}) collective-permute-start(bf16[64,1024]{1,0:T(8,128)(2,1)S(1)} %get-tuple-element.54), channel_id=1, source_target_pairs={{0,1},{1,2},{2,3},{3,4},{4,5},{5,6},{6,7},{7,0},{8,9},{9,10},{10,1... | collective-permute-start | bytes 393224 | tf_op jit(solution)/shard_map/ppermute | solution.py:470
  69.0 11.2 %collective-permute-start.22 = (bf16[64,1024]{1,0:T(8,128)(2,1)S(1)}, bf16[64,1024]{1,0:T(8,128)(2,1)S(1)}, u32[]{:S(2)}, u32[]{:S(2)}) collective-permute-start(bf16[64,1024]{1,0:T(8,128)(2,1)S(1)} %get-tuple-element.55), channel_id=1, source_target_pairs={{0,7},{1,0},{2,1},{3,2},{4,3},{5,4},{6,5},{7,6},{8,15},{9,8},{10,9... | collective-permute-start | bytes 393224 | tf_op jit(solution)/shard_map/ppermute | solution.py:470
  71.5 11.8 %collective-permute-start.28 = (bf16[4,16,128]{2,1,0:T(8,128)(2,1)S(1)}, bf16[4,16,128]{2,1,0:T(8,128)(2,1)S(1)}, u32[]{:S(2)}, u32[]{:S(2)}) collective-permute-start(bf16[4,16,128]{2,1,0:T(8,128)(2,1)S(1)} %pad_maximum_fusion.2), channel_id=1, source_target_pairs={{0,8},{8,0},{16,24},{24,16},{32,40},{40,32},{48,56},{56,48},{64,72... | collective-permute-start | bytes 49160 | tf_op jit(solution)/shard_map/ppermute | solution.py:443
  80.3 4.0 %collective-permute-start.27 = (bf16[64,512]{1,0:T(8,128)(2,1)S(1)}, bf16[64,512]{1,0:T(8,128)(2,1)S(1)}, u32[]{:S(2)}, u32[]{:S(2)}) collective-permute-start(bf16[64,512]{1,0:T(8,128)(2,1)S(1)} %get-tuple-element.64), channel_id=1, source_target_pairs={{0,8},{8,0},{16,24},{24,16},{32,40},{40,32},{48,56},{56,48},{64,72... | collective-permute-start | bytes 196616 | tf_op jit(solution)/shard_map/ppermute | solution.py:443

commit v15 on v14

--- a/solution.py
+++ b/solution.py
@@ -380,7 +380,7 @@
     down[...] = (keep6[...] + above[...].astype(F32)).astype(BF16)
 
 
-def total_body(keep, below1, above1, below2, above2, opposite, own, other):
+def total_body(keep, below2, above2, below1, above1, opposite, own, other):
     near = keep[...] + below1[...].astype(F32) + above1[...].astype(F32)
     whole = near + below2[...].astype(F32) + above2[...].astype(F32)
     whole = (whole + opposite[...].astype(F32)).astype(BF16)
@@ -506,10 +506,10 @@
         near_body, [SUM, SENT, SUM, SENT], *near[3], *weights, first_near
     )
     up2, down2 = plain(middle_body, [SENT, SENT], keep2, keep6, below3, above3)
+    up1, down1, up2, down2 = lax.optimization_barrier((up1, down1, up2, down2))
     below2, above2 = along_z(up2, 2), along_z(down2, -2)
-    up1, down1, opposite = lax.optimization_barrier((up1, down1, opposite))
     below1, above1 = along_z(up1, 1), along_z(down1, -1)
-    own, other = plain(total_body, [HALF, HALF], keep0, below1, above1, below2, above2, opposite)
+    own, other = plain(total_body, [HALF, HALF], keep0, below2, above2, below1, above1, opposite)
     return finish(own, other_core(other), pick)
 
 

time: 86.4 us -> 86.5 us (level)
  no operation moved by 1% of the time
where the time goes in v15:
time: 86.5 us; the launch traced here: 85.1 us
  starting transfers between devices  51.3 us (59%)
  waiting for transfers between devices  16.3 us (19%)
  Pallas kernels  16.2 us (19%)
  local copies, waits for them, and re-layouts  1.01 us (1%)
    ppermute x11, starting transfers between devices, along(): lax.ppermute(value, 'batch', [(i, i ^ k << shift) for i in range(BATCH)])  23.3 us
    ppermute x7, starting transfers between devices, along_z(): lax.ppermute(value, 'head', [(i, (i + k) % HEADS) for i in range(HEADS)])  16.3 us
    ppermute x11, starting transfers between devices, turned(): return lax.ppermute(value, 'batch', pairs)  11.7 us
    ppermute x11, waiting for transfers between devices, turned(): return lax.ppermute(value, 'batch', pairs)  8.94 us
    ppermute x11, waiting for transfers between devices, along(): lax.ppermute(value, 'batch', [(i, i ^ k << shift) for i in range(BATCH)])  7.37 us
    pallas_call x2, Pallas kernels, prefix_keep(): pl.pallas_call(prefix_keep_body, out_shape=[out, out], in_specs=[VMEM] *...  3.67 us
    pallas_call x1, Pallas kernels, local_parts(): pl.pallas_call(local_body, out_shape=[out] * 4, in_specs=[HBM] * 6, out_s...  3.51 us
    pallas_call x1, Pallas kernels, prefix_send(): pl.pallas_call(prefix_send_body, out_shape=jax.ShapeDtypeStruct((33, GROU...  3.38 us
  transfers between devices with their start and end apart: 29, of which 10 were waited for; matrix products, arithmetic and copies ran while one was open for 0% of the time, Pallas kernels for 18%

profile of v15, /device:TPU:1, one launch (start us, length us, event | category | flops | bytes accessed | tf_op | source)
XLA Modules:
  0.0 85.1 jit_solution(9049221730617834363)
XLA Ops:
  0.0 3.2 %collective-permute-start.4 = (bf16[2,2048,128]{2,1,0:T(8,128)(2,1)}, bf16[2,2048,128]{2,1,0:T(8,128)(2,1)S(1)}, u32[]{:S(2)}, u32[]{:S(2)}) collective-permute-start(bf16[2,2048,128]{2,1,0:T(8,128)(2,1)} %kv0.5), channel_id=1, source_target_pairs={{0,8},{8,0},{16,24},{24,16},{32,40},{40,32},{48,56},{56,48},{64,72... | collective-permute-start | bytes 3145736 | tf_op jit(solution)/shard_map/ppermute | solution.py:443
  3.2 3.5 %local_parts.1 = (bf16[18,16,128]{2,1,0:T(8,128)(2,1)}, bf16[18,16,128]{2,1,0:T(8,128)(2,1)}, bf16[18,16,128]{2,1,0:T(8,128)(2,1)}, bf16[18,16,128]{2,1,0:T(8,128)(2,1)}) custom-call(bf16[32,2048]{1,0:T(8,128)(2,1)} %q_in.1, s32[32]{0:T(128)} %prompt_in.1, s32[8,32]{1,0:T(8,128)} %bitcast.1, s32[32]{0:T(128)} %length_in.1, bf16[2,32,128]{2,1,0:T(8,128)(2,1)} %new_in.1, ...), custom_call_target="tpu_custom_call" | custom-call | tf_op jit(solution)/shard_map/local_parts/pallas_call | solution.py:131
  6.8 1.1 %collective-permute-start = (bf16[18,16,128]{2,1,0:T(8,128)(2,1)}, bf16[18,16,128]{2,1,0:T(8,128)(2,1)S(1)}, u32[]{:S(2)}, u32[]{:S(2)}) collective-permute-start(bf16[18,16,128]{2,1,0:T(8,128)(2,1)} %get-tuple-element.36), channel_id=1, source_target_pairs={{0,128},{8,136},{16,144},{24,152},{32,160},{40,168},{48,176},{56,1... | collective-permute-start | bytes 221192 | tf_op jit(solution)/shard_map/ppermute | solution.py:443
  7.9 0.3 collective-permute-start.1
  8.2 1.9 %collective-permute-start.2 = (bf16[18,16,128]{2,1,0:T(8,128)(2,1)}, bf16[18,16,128]{2,1,0:T(8,128)(2,1)S(1)}, u32[]{:S(2)}, u32[]{:S(2)}) collective-permute-start(bf16[18,16,128]{2,1,0:T(8,128)(2,1)} %get-tuple-element.38), channel_id=1, source_target_pairs={{0,192},{8,200},{16,208},{24,216},{32,224},{40,232},{48,240},{56,2... | collective-permute-start | bytes 221192 | tf_op jit(solution)/shard_map/ppermute | solution.py:443
  10.1 2.3 %collective-permute-done.a2.s2 = bf16[18,16,128]{2,1,0:T(8,128)(2,1)S(1)} collective-permute-done((bf16[18,16,128]{2,1,0:T(8,128)(2,1)}, bf16[18,16,128]{2,1,0:T(8,128)(2,1)S(1)}, u32[]{:S(2)}, u32[]{:S(2)}) %collective-permute-start) | collective-permute-done | bytes 73760 | tf_op jit(solution)/shard_map/ppermute | solution.py:443
  12.4 0.0 collective-permute-done.1.a1.s1
  12.4 1.5 %collective-permute-done.2.a3.s3 = bf16[18,16,128]{2,1,0:T(8,128)(2,1)S(1)} collective-permute-done((bf16[18,16,128]{2,1,0:T(8,128)(2,1)}, bf16[18,16,128]{2,1,0:T(8,128)(2,1)S(1)}, u32[]{:S(2)}, u32[]{:S(2)}) %collective-permute-start.2) | collective-permute-done | bytes 73760 | tf_op jit(solution)/shard_map/ppermute | solution.py:443
  13.9 0.9 %copy-done.2 = bf16[18,16,128]{2,1,0:T(8,128)(2,1)S(1)} copy-done((bf16[18,16,128]{2,1,0:T(8,128)(2,1)S(1)}, bf16[18,16,128]{2,1,0:T(8,128)(2,1)}, u32[]{:S(2)}) %copy-start.2) | copy-done | bytes 73752
  14.8 1.8 %collective-permute-start.3 = (bf16[37,16,128]{2,1,0:T(8,128)(2,1)S(1)}, bf16[37,16,128]{2,1,0:T(8,128)(2,1)S(1)}, u32[]{:S(2)}, u32[]{:S(2)}) collective-permute-start(bf16[37,16,128]{2,1,0:T(8,128)(2,1)S(1)} %get-tuple-element.40), channel_id=1, source_target_pairs={{0,48},{8,56},{16,32},{24,40},{32,16},{40,24},{48,0},{56,8},{64,11... | collective-permute-start | bytes 454664 | tf_op jit(solution)/shard_map/ppermute | solution.py:443
  16.6 1.8 %prefix_keep.2 = (f32[16,16,128]{2,1,0:T(8,128)S(1)}, f32[16,16,128]{2,1,0:T(8,128)S(1)}) custom-call(bf16[17,16,128]{2,1,0:T(8,128)(2,1)S(1)} %get-tuple-element.41.q, bf16[2,2048,128]{2,1,0:T(8,128)(2,1)S(1)} %copy-done.1, bf16[2,2048,128]{2,1,0:T(8,128)(2,1)S(1)} %collective-permute-done.4.kv1), custom_call_target="tpu_custom_call" | custom-call | flops 536870912 | bytes 2500000 | tf_op jit(solution)/shard_map/prefix_keep/pallas_call | solution.py:246
  18.4 0.0 copy-start
  18.4 2.2 %collective-permute-done.3.qb = bf16[37,16,128]{2,1,0:T(8,128)(2,1)S(1)} collective-permute-done((bf16[37,16,128]{2,1,0:T(8,128)(2,1)S(1)}, bf16[37,16,128]{2,1,0:T(8,128)(2,1)S(1)}, u32[]{:S(2)}, u32[]{:S(2)}) %collective-permute-start.3) | collective-permute-done | bytes 151584 | tf_op jit(solution)/shard_map/ppermute | solution.py:443
  20.6 0.0 collective-permute-start.6
  20.6 0.0 collective-permute-done.5.qa
  20.6 3.4 %prefix_send.1 = bf16[33,16,128]{2,1,0:T(8,128)(2,1)S(1)} custom-call(bf16[17,16,128]{2,1,0:T(8,128)(2,1)S(1)} %collective-permute-done.5.qa, bf16[37,16,128]{2,1,0:T(8,128)(2,1)S(1)} %collective-permute-done.3.qb, bf16[2,2048,128]{2,1,0:T(8,128)(2,1)S(1)} %copy-done.1, bf16[2,2048,128]{2,1,0:T(8,128)(2,1)S(1)} %collective-permute-done.4.kv1, ...), custom_call_target="tpu_custom_call" | custom-call | flops 1073741824 | bytes 2500000 | tf_op jit(solution)/shard_map/prefix_send/pallas_call | solution.py:233
  24.0 0.0 copy-start.3
  24.0 0.6 collective-permute-done.6.q.far
  24.6 0.9 %collective-permute-start.7 = (bf16[33,16,128]{2,1,0:T(8,128)(2,1)S(1)}, bf16[33,16,128]{2,1,0:T(8,128)(2,1)S(1)}, u32[]{:S(2)}, u32[]{:S(2)}) collective-permute-start(bf16[33,16,128]{2,1,0:T(8,128)(2,1)S(1)} %prefix_send.1), channel_id=1, source_target_pairs={{0,16},{8,24},{16,0},{24,8},{32,48},{40,56},{48,32},{56,40},{64,80... | collective-permute-start | bytes 405512 | tf_op jit(solution)/shard_map/ppermute | solution.py:443
  25.5 2.4 %collective-permute-start.15 = (bf16[2048,512]{1,0:T(8,128)(2,1)S(1)}, bf16[2048,512]{1,0:T(8,128)(2,1)S(1)}, u32[]{:S(2)}, u32[]{:S(2)}) collective-permute-start(bf16[2048,512]{1,0:T(8,128)(2,1)S(1)} %copy-done), channel_id=1, source_target_pairs={{0,8},{8,0},{16,24},{24,16},{32,40},{40,32},{48,56},{56,48},{64,72... | collective-permute-start | bytes 6291464 | tf_op jit(solution)/shard_map/ppermute | solution.py:443
  28.0 1.8 %prefix_keep.3 = (f32[16,16,128]{2,1,0:T(8,128)S(1)}, f32[16,16,128]{2,1,0:T(8,128)S(1)}) custom-call(bf16[37,16,128]{2,1,0:T(8,128)(2,1)S(1)} %collective-permute-done.6.q.far, bf16[2,2048,128]{2,1,0:T(8,128)(2,1)S(1)} %copy-done.1, bf16[2,2048,128]{2,1,0:T(8,128)(2,1)S(1)} %collective-permute-done.4.kv1), custom_call_target="tpu_custom_call" | custom-call | flops 536870912 | bytes 2500000 | tf_op jit(solution)/shard_map/prefix_keep/pallas_call | solution.py:246
  29.8 0.0 collective-permute-done.7.message
  29.8 0.7 combine.1
  30.5 4.5 %collective-permute-start.8 = (bf16[32,2048]{1,0:T(8,128)(2,1)S(1)}, bf16[32,2048]{1,0:T(8,128)(2,1)S(1)}, u32[]{:S(2)}, u32[]{:S(2)}) collective-permute-start(bf16[32,2048]{1,0:T(8,128)(2,1)S(1)} %combine.1), channel_id=1, source_target_pairs={{0,128},{8,40},{16,144},{24,56},{32,160},{40,8},{48,176},{56,24},{... | collective-permute-start | bytes 393224 | tf_op jit(solution)/shard_map/ppermute | solution.py:460
  35.0 0.0 collective-permute-start.9
  35.0 0.4 collective-permute-start.10
  35.4 2.0 %collective-permute-done.8 = bf16[32,2048]{1,0:T(8,128)(2,1)S(1)} collective-permute-done((bf16[32,2048]{1,0:T(8,128)(2,1)S(1)}, bf16[32,2048]{1,0:T(8,128)(2,1)S(1)}, u32[]{:S(2)}, u32[]{:S(2)}) %collective-permute-start.8) | collective-permute-done | bytes 131104 | tf_op jit(solution)/shard_map/ppermute | solution.py:460
  37.4 1.7 %collective-permute-done.9 = bf16[32,2048]{1,0:T(8,128)(2,1)S(1)} collective-permute-done((bf16[32,2048]{1,0:T(8,128)(2,1)S(1)}, bf16[32,2048]{1,0:T(8,128)(2,1)S(1)}, u32[]{:S(2)}, u32[]{:S(2)}) %collective-permute-start.9) | collective-permute-done | bytes 131104 | tf_op jit(solution)/shard_map/ppermute | solution.py:460
  39.1 0.9 %collective-permute-done.10 = bf16[32,2048]{1,0:T(8,128)(2,1)S(1)} collective-permute-done((bf16[32,2048]{1,0:T(8,128)(2,1)S(1)}, bf16[32,2048]{1,0:T(8,128)(2,1)S(1)}, u32[]{:S(2)}, u32[]{:S(2)}) %collective-permute-start.10) | collective-permute-done | bytes 131104 | tf_op jit(solution)/shard_map/ppermute | solution.py:460
  40.1 0.8 collective-permute-start.16
  41.0 2.0 %collective-permute-start.11 = (bf16[64,2048]{1,0:T(8,128)(2,1)S(1)}, bf16[64,2048]{1,0:T(8,128)(2,1)S(1)}, u32[]{:S(2)}, u32[]{:S(2)}) collective-permute-start(bf16[64,2048]{1,0:T(8,128)(2,1)S(1)} %pad_maximum_fusion.a), channel_id=1, source_target_pairs={{0,48},{8,200},{16,32},{24,216},{32,16},{40,232},{48,0},{56,248},{... | collective-permute-start | bytes 786440 | tf_op jit(solution)/shard_map/ppermute | solution.py:460
  43.0 0.9 %collective-permute-start.13 = (bf16[64,2048]{1,0:T(8,128)(2,1)S(1)}, bf16[64,2048]{1,0:T(8,128)(2,1)S(1)}, u32[]{:S(2)}, u32[]{:S(2)}) collective-permute-start(bf16[64,2048]{1,0:T(8,128)(2,1)S(1)} %pad_maximum_fusion.a), channel_id=1, source_target_pairs={{0,16},{8,72},{16,0},{24,88},{32,48},{40,104},{48,32},{56,120},{64... | collective-permute-start | bytes 786440 | tf_op jit(solution)/shard_map/ppermute | solution.py:460
  43.8 2.8 %collective-permute-done.16.c = bf16[64,2048]{1,0:T(8,128)(2,1)S(1)} collective-permute-done((bf16[64,2048]{1,0:T(8,128)(2,1)S(1)}, bf16[64,2048]{1,0:T(8,128)(2,1)S(1)}, u32[]{:S(2)}, u32[]{:S(2)}) %collective-permute-start.16) | collective-permute-done | bytes 262176 | tf_op jit(solution)/shard_map/ppermute | solution.py:460
  46.6 0.1 collective-permute-start.17
  46.7 0.0 collective-permute-done.18.b
  46.7 1.4 %collective-permute-start.19 = (bf16[32,2048]{1,0:T(8,128)(2,1)S(1)}, bf16[32,2048]{1,0:T(8,128)(2,1)S(1)}, u32[]{:S(2)}, u32[]{:S(2)}) collective-permute-start(bf16[32,2048]{1,0:T(8,128)(2,1)S(1)} %slice.75), channel_id=1, source_target_pairs={{0,48},{8,200},{16,32},{24,216},{32,16},{40,232},{48,0},{56,248},{... | collective-permute-start | bytes 393224 | tf_op jit(solution)/shard_map/ppermute | solution.py:460
  48.2 1.5 %collective-permute-done.11.c = bf16[64,2048]{1,0:T(8,128)(2,1)S(1)} collective-permute-done((bf16[64,2048]{1,0:T(8,128)(2,1)S(1)}, bf16[64,2048]{1,0:T(8,128)(2,1)S(1)}, u32[]{:S(2)}, u32[]{:S(2)}) %collective-permute-start.11) | collective-permute-done | bytes 262176 | tf_op jit(solution)/shard_map/ppermute | solution.py:460
  49.7 0.1 collective-permute-start.12
  49.8 0.0 collective-permute-done.13.b
  49.9 1.4 %collective-permute-start.14 = (bf16[32,2048]{1,0:T(8,128)(2,1)S(1)}, bf16[32,2048]{1,0:T(8,128)(2,1)S(1)}, u32[]{:S(2)}, u32[]{:S(2)}) collective-permute-start(bf16[32,2048]{1,0:T(8,128)(2,1)S(1)} %slice.69), channel_id=1, source_target_pairs={{0,48},{8,200},{16,32},{24,216},{32,16},{40,232},{48,0},{56,248},{... | collective-permute-start | bytes 393224 | tf_op jit(solution)/shard_map/ppermute | solution.py:460
  51.3 0.0 collective-permute-done.15.w1
  51.3 1.0 %project.3.first = f32[4,48,1024]{2,1,0:T(8,128)S(1)} custom-call(bf16[64,2048]{1,0:T(8,128)(2,1)S(1)} %pad_maximum_fusion.1.a, bf16[64,2048]{1,0:T(8,128)(2,1)S(1)} %collective-permute-done.18.b, bf16[64,2048]{1,0:T(8,128)(2,1)S(1)} %collective-permute-done.16.c, bf16[2048,512]{1,0:T(8,128)(2,1)S(1)} %copy-done, ...), custom_call_target="tpu_custom_call" | custom-call | flops 805306368 | bytes 4500000 | tf_op jit(solution)/shard_map/project/pallas_call | solution.py:325
  52.3 0.0 collective-permute-done.17.a
  52.3 0.9 %far.1 = (f32[64,1024]{1,0:T(8,128)S(1)}, bf16[64,1024]{1,0:T(8,128)(2,1)S(1)}, bf16[64,1024]{1,0:T(8,128)(2,1)S(1)}, bf16[64,1024]{1,0:T(8,128)(2,1)S(1)}) custom-call(bf16[32,2048]{1,0:T(8,128)(2,1)S(1)} %collective-permute-done.17.a, bf16[32,2048]{1,0:T(8,128)(2,1)S(1)} %collective-permute-done.19.b, bf16[2048,512]{1,0:T(8,128)(2,1)S(1)} %copy-done, ...), custom_call_target="tpu_custom_call" | custom-call | tf_op jit(solution)/shard_map/far/pallas_call | solution.py:368
  53.2 2.0 %collective-permute-start.20 = (bf16[64,1024]{1,0:T(8,128)(2,1)S(1)}, bf16[64,1024]{1,0:T(8,128)(2,1)S(1)}, u32[]{:S(2)}, u32[]{:S(2)}) collective-permute-start(bf16[64,1024]{1,0:T(8,128)(2,1)S(1)} %get-tuple-element.56), channel_id=1, source_target_pairs={{0,1},{1,2},{2,3},{3,4},{4,5},{5,6},{6,7},{7,0},{8,9},{9,10},{10,1... | collective-permute-start | bytes 393224 | tf_op jit(solution)/shard_map/ppermute | solution.py:470
  55.2 4.0 %collective-permute-start.21 = (bf16[64,1024]{1,0:T(8,128)(2,1)S(1)}, bf16[64,1024]{1,0:T(8,128)(2,1)S(1)}, u32[]{:S(2)}, u32[]{:S(2)}) collective-permute-start(bf16[64,1024]{1,0:T(8,128)(2,1)S(1)} %get-tuple-element.57), channel_id=1, source_target_pairs={{0,7},{1,0},{2,1},{3,2},{4,3},{5,4},{6,5},{7,6},{8,15},{9,8},{10,9... | collective-permute-start | bytes 393224 | tf_op jit(solution)/shard_map/ppermute | solution.py:470
  59.3 3.9 %collective-permute-start.26 = (bf16[64,1024]{1,0:T(8,128)(2,1)S(1)}, bf16[64,1024]{1,0:T(8,128)(2,1)S(1)}, u32[]{:S(2)}, u32[]{:S(2)}) collective-permute-start(bf16[64,1024]{1,0:T(8,128)(2,1)S(1)} %get-tuple-element.64), channel_id=1, source_target_pairs={{0,4},{1,5},{2,6},{3,7},{4,0},{5,1},{6,2},{7,3},{8,12},{9,13},{10,... | collective-permute-start | bytes 393224 | tf_op jit(solution)/shard_map/ppermute | solution.py:470
  63.2 1.0 %project.2.first = f32[4,48,1024]{2,1,0:T(8,128)S(1)} custom-call(bf16[64,2048]{1,0:T(8,128)(2,1)S(1)} %pad_maximum_fusion.a, bf16[64,2048]{1,0:T(8,128)(2,1)S(1)} %collective-permute-done.13.b, bf16[64,2048]{1,0:T(8,128)(2,1)S(1)} %collective-permute-done.11.c, bf16[2048,512]{1,0:T(8,128)(2,1)S(1)} %copy-done, bf16[2048,512]{1,0:T(8,128)(2,1)S(1)} %collective-permute-done.15.w1), custom_call_target="tpu_custom_call" | custom-call | flops 805306368 | bytes 4500000 | tf_op jit(solution)/shard_map/project/pallas_call | solution.py:325
  64.2 0.0 collective-permute-done.14.b
  64.2 0.9 %near.1 = (f32[64,1024]{1,0:T(8,128)S(1)}, bf16[64,1024]{1,0:T(8,128)(2,1)S(1)}, f32[64,1024]{1,0:T(8,128)S(1)}, bf16[64,1024]{1,0:T(8,128)(2,1)S(1)}) custom-call(bf16[32,2048]{1,0:T(8,128)(2,1)S(1)} %collective-permute-done.12.a, bf16[32,2048]{1,0:T(8,128)(2,1)S(1)} %collective-permute-done.14.b, bf16[2048,512]{1,0:T(8,128)(2,1)S(1)} %copy-done, ...), custom_call_target="tpu_custom_call" | custom-call | tf_op jit(solution)/shard_map/near/pallas_call | solution.py:368
  65.1 0.0 collective-permute-done.20.below
  65.1 0.1 middle.1
  65.2 0.1 collective-permute-start.22
  65.3 3.6 %collective-permute-start.23 = (bf16[64,1024]{1,0:T(8,128)(2,1)S(1)}, bf16[64,1024]{1,0:T(8,128)(2,1)S(1)}, u32[]{:S(2)}, u32[]{:S(2)}) collective-permute-start(bf16[64,1024]{1,0:T(8,128)(2,1)S(1)} %get-tuple-element.61), channel_id=1, source_target_pairs={{0,6},{1,7},{2,0},{3,1},{4,2},{5,3},{6,4},{7,5},{8,14},{9,15},{10,... | collective-permute-start | bytes 393224 | tf_op jit(solution)/shard_map/ppermute | solution.py:470
  68.8 0.2 collective-permute-start.24
  69.0 2.5 %collective-permute-start.25 = (bf16[64,1024]{1,0:T(8,128)(2,1)S(1)}, bf16[64,1024]{1,0:T(8,128)(2,1)S(1)}, u32[]{:S(2)}, u32[]{:S(2)}) collective-permute-start(bf16[64,1024]{1,0:T(8,128)(2,1)S(1)} %get-tuple-element.63), channel_id=1, source_target_pairs={{0,7},{1,0},{2,1},{3,2},{4,3},{5,4},{6,5},{7,6},{8,15},{9,8},{10,9... | collective-permute-start | bytes 393224 | tf_op jit(solution)/shard_map/ppermute | solution.py:470
  71.5 8.7 %collective-permute-start.28 = (bf16[4,16,128]{2,1,0:T(8,128)(2,1)S(1)}, bf16[4,16,128]{2,1,0:T(8,128)(2,1)S(1)}, u32[]{:S(2)}, u32[]{:S(2)}) collective-permute-start(bf16[4,16,128]{2,1,0:T(8,128)(2,1)S(1)} %pad_maximum_fusion.2), channel_id=1, source_target_pairs={{0,8},{8,0},{16,24},{24,16},{32,40},{40,32},{48,56},{56,48},{64,72... | collective-permute-start | bytes 49160 | tf_op jit(solution)/shard_map/ppermute | solution.py:443
  80.2 0.0 collective-permute-done.25.above1
  80.2 0.1 total.1
  80.3 3.0 %collective-permute-start.27 = (bf16[64,512]{1,0:T(8,128)(2,1)S(1)}, bf16[64,512]{1,0:T(8,128)(2,1)S(1)}, u32[]{:S(2)}, u32[]{:S(2)}) collective-permute-start(bf16[64,512]{1,0:T(8,128)(2,1)S(1)} %get-tuple-element.66), channel_id=1, source_target_pairs={{0,8},{8,0},{16,24},{24,16},{32,40},{40,32},{48,56},{56,48},{64,72... | collective-permute-start | bytes 196616 | tf_op jit(solution)/shard_map/ppermute | solution.py:443
  83.3 0.0 collective-permute-done.28
  83.3 0.1 order_rows.1.pick
  83.5 0.8 collective-permute-done.27.other
  84.2 0.9 %finish.1 = bf16[128,512]{1,0:T(8,128)(2,1)} custom-call(bf16[64,512]{1,0:T(8,128)(2,1)S(1)} %get-tuple-element.65.own, bf16[64,512]{1,0:T(8,128)(2,1)S(1)} %collective-permute-done.27.other, bf16[128,128]{1,0:T(8,128)(2,1)S(1)} %order_rows.1.pick), custom_call_target="tpu_custom_call" | custom-call | tf_op jit(solution)/shard_map/finish/pallas_call | solution.py:432
  (32 shorter events, 0.2 us)
Async XLA Ops:
  0.0 16.5 %copy-start.1 = (bf16[2,2048,128]{2,1,0:T(8,128)(2,1)S(1)}, bf16[2,2048,128]{2,1,0:T(8,128)(2,1)}, u32[]{:S(2)}) copy-start(bf16[2,2048,128]{2,1,0:T(8,128)(2,1)} %kv0.5) | copy-start | bytes 3145732
  0.0 16.5 %collective-permute-start.4 = (bf16[2,2048,128]{2,1,0:T(8,128)(2,1)}, bf16[2,2048,128]{2,1,0:T(8,128)(2,1)S(1)}, u32[]{:S(2)}, u32[]{:S(2)}) collective-permute-start(bf16[2,2048,128]{2,1,0:T(8,128)(2,1)} %kv0.5), channel_id=1, source_target_pairs={{0,8},{8,0},{16,24},{24,16},{32,40},{40,32},{48,56},{56,48},{64,72... | collective-permute-start | bytes 3145736 | tf_op jit(solution)/shard_map/ppermute | solution.py:443
  6.8 5.6 %collective-permute-start = (bf16[18,16,128]{2,1,0:T(8,128)(2,1)}, bf16[18,16,128]{2,1,0:T(8,128)(2,1)S(1)}, u32[]{:S(2)}, u32[]{:S(2)}) collective-permute-start(bf16[18,16,128]{2,1,0:T(8,128)(2,1)} %get-tuple-element.36), channel_id=1, source_target_pairs={{0,128},{8,136},{16,144},{24,152},{32,160},{40,168},{48,176},{56,1... | collective-permute-start | bytes 221192 | tf_op jit(solution)/shard_map/ppermute | solution.py:443
  7.9 4.5 %collective-permute-start.1 = (bf16[18,16,128]{2,1,0:T(8,128)(2,1)}, bf16[18,16,128]{2,1,0:T(8,128)(2,1)S(1)}, u32[]{:S(2)}, u32[]{:S(2)}) collective-permute-start(bf16[18,16,128]{2,1,0:T(8,128)(2,1)} %get-tuple-element.37), channel_id=1, source_target_pairs={{0,64},{8,72},{16,80},{24,88},{32,96},{40,104},{48,112},{56,120},{... | collective-permute-start | bytes 221192 | tf_op jit(solution)/shard_map/ppermute | solution.py:443
  8.2 5.7 %collective-permute-start.2 = (bf16[18,16,128]{2,1,0:T(8,128)(2,1)}, bf16[18,16,128]{2,1,0:T(8,128)(2,1)S(1)}, u32[]{:S(2)}, u32[]{:S(2)}) collective-permute-start(bf16[18,16,128]{2,1,0:T(8,128)(2,1)} %get-tuple-element.38), channel_id=1, source_target_pairs={{0,192},{8,200},{16,208},{24,216},{32,224},{40,232},{48,240},{56,2... | collective-permute-start | bytes 221192 | tf_op jit(solution)/shard_map/ppermute | solution.py:443
  13.9 0.9 %copy-start.2 = (bf16[18,16,128]{2,1,0:T(8,128)(2,1)S(1)}, bf16[18,16,128]{2,1,0:T(8,128)(2,1)}, u32[]{:S(2)}) copy-start(bf16[18,16,128]{2,1,0:T(8,128)(2,1)} %get-tuple-element.39.a0.s0) | copy-start | bytes 221188
  14.8 5.8 %collective-permute-start.3 = (bf16[37,16,128]{2,1,0:T(8,128)(2,1)S(1)}, bf16[37,16,128]{2,1,0:T(8,128)(2,1)S(1)}, u32[]{:S(2)}, u32[]{:S(2)}) collective-permute-start(bf16[37,16,128]{2,1,0:T(8,128)(2,1)S(1)} %get-tuple-element.40), channel_id=1, source_target_pairs={{0,48},{8,56},{16,32},{24,40},{32,16},{40,24},{48,0},{56,8},{64,11... | collective-permute-start | bytes 454664 | tf_op jit(solution)/shard_map/ppermute | solution.py:443
  16.5 4.0 %collective-permute-start.5 = (bf16[17,16,128]{2,1,0:T(8,128)(2,1)S(1)}, bf16[17,16,128]{2,1,0:T(8,128)(2,1)S(1)}, u32[]{:S(2)}, u32[]{:S(2)}) collective-permute-start(bf16[17,16,128]{2,1,0:T(8,128)(2,1)S(1)} %get-tuple-element.41.q), channel_id=1, source_target_pairs={{0,16},{8,24},{16,0},{24,8},{32,48},{40,56},{48,32},{56,40},{64,80... | collective-permute-start | bytes 208904 | tf_op jit(solution)/shard_map/ppermute | solution.py:443
  18.4 7.1 %copy-start = (bf16[2048,512]{1,0:T(8,128)(2,1)S(1)}, bf16[2048,512]{1,0:T(8,128)(2,1)}, u32[]{:S(2)}) copy-start(bf16[2048,512]{1,0:T(8,128)(2,1)} %w0.7) | copy-start | bytes 6291460
  20.6 4.0 %collective-permute-start.6 = (bf16[37,16,128]{2,1,0:T(8,128)(2,1)S(1)}, bf16[37,16,128]{2,1,0:T(8,128)(2,1)S(1)}, u32[]{:S(2)}, u32[]{:S(2)}) collective-permute-start(bf16[37,16,128]{2,1,0:T(8,128)(2,1)S(1)} %collective-permute-done.3.qb), channel_id=1, source_target_pairs={{0,16},{8,24},{16,0},{24,8},{32,48},{40,56},{48,32},{56,40},{64,80... | collective-permute-start | bytes 454664 | tf_op jit(solution)/shard_map/ppermute | solution.py:443
  24.0 5.8 %copy-start.3 = (bf16[18,16,128]{2,1,0:T(8,128)(2,1)S(1)}, bf16[18,16,128]{2,1,0:T(8,128)(2,1)}, u32[]{:S(2)}) copy-start(bf16[18,16,128]{2,1,0:T(8,128)(2,1)} %get-tuple-element.39.a0.s0) | copy-start | bytes 221188
  24.6 5.2 %collective-permute-start.7 = (bf16[33,16,128]{2,1,0:T(8,128)(2,1)S(1)}, bf16[33,16,128]{2,1,0:T(8,128)(2,1)S(1)}, u32[]{:S(2)}, u32[]{:S(2)}) collective-permute-start(bf16[33,16,128]{2,1,0:T(8,128)(2,1)S(1)} %prefix_send.1), channel_id=1, source_target_pairs={{0,16},{8,24},{16,0},{24,8},{32,48},{40,56},{48,32},{56,40},{64,80... | collective-permute-start | bytes 405512 | tf_op jit(solution)/shard_map/ppermute | solution.py:443
  25.5 25.8 %collective-permute-start.15 = (bf16[2048,512]{1,0:T(8,128)(2,1)S(1)}, bf16[2048,512]{1,0:T(8,128)(2,1)S(1)}, u32[]{:S(2)}, u32[]{:S(2)}) collective-permute-start(bf16[2048,512]{1,0:T(8,128)(2,1)S(1)} %copy-done), channel_id=1, source_target_pairs={{0,8},{8,0},{16,24},{24,16},{32,40},{40,32},{48,56},{56,48},{64,72... | collective-permute-start | bytes 6291464 | tf_op jit(solution)/shard_map/ppermute | solution.py:443
  30.5 6.9 %collective-permute-start.8 = (bf16[32,2048]{1,0:T(8,128)(2,1)S(1)}, bf16[32,2048]{1,0:T(8,128)(2,1)S(1)}, u32[]{:S(2)}, u32[]{:S(2)}) collective-permute-start(bf16[32,2048]{1,0:T(8,128)(2,1)S(1)} %combine.1), channel_id=1, source_target_pairs={{0,128},{8,40},{16,144},{24,56},{32,160},{40,8},{48,176},{56,24},{... | collective-permute-start | bytes 393224 | tf_op jit(solution)/shard_map/ppermute | solution.py:460
  35.0 4.1 %collective-permute-start.9 = (bf16[32,2048]{1,0:T(8,128)(2,1)S(1)}, bf16[32,2048]{1,0:T(8,128)(2,1)S(1)}, u32[]{:S(2)}, u32[]{:S(2)}) collective-permute-start(bf16[32,2048]{1,0:T(8,128)(2,1)S(1)} %combine.1), channel_id=1, source_target_pairs={{0,64},{8,24},{16,80},{24,8},{32,96},{40,56},{48,112},{56,40},{64,... | collective-permute-start | bytes 393224 | tf_op jit(solution)/shard_map/ppermute | solution.py:460
  35.0 5.0 %collective-permute-start.10 = (bf16[32,2048]{1,0:T(8,128)(2,1)S(1)}, bf16[32,2048]{1,0:T(8,128)(2,1)S(1)}, u32[]{:S(2)}, u32[]{:S(2)}) collective-permute-start(bf16[32,2048]{1,0:T(8,128)(2,1)S(1)} %combine.1), channel_id=1, source_target_pairs={{0,192},{8,56},{16,208},{24,40},{32,224},{40,24},{48,240},{56,8},{... | collective-permute-start | bytes 393224 | tf_op jit(solution)/shard_map/ppermute | solution.py:460
  40.1 6.5 %collective-permute-start.16 = (bf16[64,2048]{1,0:T(8,128)(2,1)S(1)}, bf16[64,2048]{1,0:T(8,128)(2,1)S(1)}, u32[]{:S(2)}, u32[]{:S(2)}) collective-permute-start(bf16[64,2048]{1,0:T(8,128)(2,1)S(1)} %pad_maximum_fusion.1.a), channel_id=1, source_target_pairs={{0,48},{8,200},{16,32},{24,216},{32,16},{40,232},{48,0},{56,248},{... | collective-permute-start | bytes 786440 | tf_op jit(solution)/shard_map/ppermute | solution.py:460
  40.9 5.8 %collective-permute-start.18 = (bf16[64,2048]{1,0:T(8,128)(2,1)S(1)}, bf16[64,2048]{1,0:T(8,128)(2,1)S(1)}, u32[]{:S(2)}, u32[]{:S(2)}) collective-permute-start(bf16[64,2048]{1,0:T(8,128)(2,1)S(1)} %pad_maximum_fusion.1.a), channel_id=1, source_target_pairs={{0,16},{8,72},{16,0},{24,88},{32,48},{40,104},{48,32},{56,120},{64... | collective-permute-start | bytes 786440 | tf_op jit(solution)/shard_map/ppermute | solution.py:460
  41.0 8.8 %collective-permute-start.11 = (bf16[64,2048]{1,0:T(8,128)(2,1)S(1)}, bf16[64,2048]{1,0:T(8,128)(2,1)S(1)}, u32[]{:S(2)}, u32[]{:S(2)}) collective-permute-start(bf16[64,2048]{1,0:T(8,128)(2,1)S(1)} %pad_maximum_fusion.a), channel_id=1, source_target_pairs={{0,48},{8,200},{16,32},{24,216},{32,16},{40,232},{48,0},{56,248},{... | collective-permute-start | bytes 786440 | tf_op jit(solution)/shard_map/ppermute | solution.py:460
  43.0 6.9 %collective-permute-start.13 = (bf16[64,2048]{1,0:T(8,128)(2,1)S(1)}, bf16[64,2048]{1,0:T(8,128)(2,1)S(1)}, u32[]{:S(2)}, u32[]{:S(2)}) collective-permute-start(bf16[64,2048]{1,0:T(8,128)(2,1)S(1)} %pad_maximum_fusion.a), channel_id=1, source_target_pairs={{0,16},{8,72},{16,0},{24,88},{32,48},{40,104},{48,32},{56,120},{64... | collective-permute-start | bytes 786440 | tf_op jit(solution)/shard_map/ppermute | solution.py:460
  46.6 5.7 %collective-permute-start.17 = (bf16[32,2048]{1,0:T(8,128)(2,1)S(1)}, bf16[32,2048]{1,0:T(8,128)(2,1)S(1)}, u32[]{:S(2)}, u32[]{:S(2)}) collective-permute-start(bf16[32,2048]{1,0:T(8,128)(2,1)S(1)} %slice.74), channel_id=1, source_target_pairs={{0,16},{8,72},{16,0},{24,88},{32,48},{40,104},{48,32},{56,120},{64... | collective-permute-start | bytes 393224 | tf_op jit(solution)/shard_map/ppermute | solution.py:460
  46.7 5.6 %collective-permute-start.19 = (bf16[32,2048]{1,0:T(8,128)(2,1)S(1)}, bf16[32,2048]{1,0:T(8,128)(2,1)S(1)}, u32[]{:S(2)}, u32[]{:S(2)}) collective-permute-start(bf16[32,2048]{1,0:T(8,128)(2,1)S(1)} %slice.75), channel_id=1, source_target_pairs={{0,48},{8,200},{16,32},{24,216},{32,16},{40,232},{48,0},{56,248},{... | collective-permute-start | bytes 393224 | tf_op jit(solution)/shard_map/ppermute | solution.py:460
  49.7 14.5 %collective-permute-start.12 = (bf16[32,2048]{1,0:T(8,128)(2,1)S(1)}, bf16[32,2048]{1,0:T(8,128)(2,1)S(1)}, u32[]{:S(2)}, u32[]{:S(2)}) collective-permute-start(bf16[32,2048]{1,0:T(8,128)(2,1)S(1)} %slice.68), channel_id=1, source_target_pairs={{0,16},{8,72},{16,0},{24,88},{32,48},{40,104},{48,32},{56,120},{64... | collective-permute-start | bytes 393224 | tf_op jit(solution)/shard_map/ppermute | solution.py:460
  49.9 14.4 %collective-permute-start.14 = (bf16[32,2048]{1,0:T(8,128)(2,1)S(1)}, bf16[32,2048]{1,0:T(8,128)(2,1)S(1)}, u32[]{:S(2)}, u32[]{:S(2)}) collective-permute-start(bf16[32,2048]{1,0:T(8,128)(2,1)S(1)} %slice.69), channel_id=1, source_target_pairs={{0,48},{8,200},{16,32},{24,216},{32,16},{40,232},{48,0},{56,248},{... | collective-permute-start | bytes 393224 | tf_op jit(solution)/shard_map/ppermute | solution.py:460
  53.2 11.9 %collective-permute-start.20 = (bf16[64,1024]{1,0:T(8,128)(2,1)S(1)}, bf16[64,1024]{1,0:T(8,128)(2,1)S(1)}, u32[]{:S(2)}, u32[]{:S(2)}) collective-permute-start(bf16[64,1024]{1,0:T(8,128)(2,1)S(1)} %get-tuple-element.56), channel_id=1, source_target_pairs={{0,1},{1,2},{2,3},{3,4},{4,5},{5,6},{6,7},{7,0},{8,9},{9,10},{10,1... | collective-permute-start | bytes 393224 | tf_op jit(solution)/shard_map/ppermute | solution.py:470
  55.2 9.9 %collective-permute-start.21 = (bf16[64,1024]{1,0:T(8,128)(2,1)S(1)}, bf16[64,1024]{1,0:T(8,128)(2,1)S(1)}, u32[]{:S(2)}, u32[]{:S(2)}) collective-permute-start(bf16[64,1024]{1,0:T(8,128)(2,1)S(1)} %get-tuple-element.57), channel_id=1, source_target_pairs={{0,7},{1,0},{2,1},{3,2},{4,3},{5,4},{6,5},{7,6},{8,15},{9,8},{10,9... | collective-permute-start | bytes 393224 | tf_op jit(solution)/shard_map/ppermute | solution.py:470
  59.3 12.3 %collective-permute-start.26 = (bf16[64,1024]{1,0:T(8,128)(2,1)S(1)}, bf16[64,1024]{1,0:T(8,128)(2,1)S(1)}, u32[]{:S(2)}, u32[]{:S(2)}) collective-permute-start(bf16[64,1024]{1,0:T(8,128)(2,1)S(1)} %get-tuple-element.64), channel_id=1, source_target_pairs={{0,4},{1,5},{2,6},{3,7},{4,0},{5,1},{6,2},{7,3},{8,12},{9,13},{10,... | collective-permute-start | bytes 393224 | tf_op jit(solution)/shard_map/ppermute | solution.py:470
  65.2 15.0 %collective-permute-start.22 = (bf16[64,1024]{1,0:T(8,128)(2,1)S(1)}, bf16[64,1024]{1,0:T(8,128)(2,1)S(1)}, u32[]{:S(2)}, u32[]{:S(2)}) collective-permute-start(bf16[64,1024]{1,0:T(8,128)(2,1)S(1)} %get-tuple-element.60), channel_id=1, source_target_pairs={{0,2},{1,3},{2,4},{3,5},{4,6},{5,7},{6,0},{7,1},{8,10},{9,11},{10,... | collective-permute-start | bytes 393224 | tf_op jit(solution)/shard_map/ppermute | solution.py:470
  65.3 14.9 %collective-permute-start.23 = (bf16[64,1024]{1,0:T(8,128)(2,1)S(1)}, bf16[64,1024]{1,0:T(8,128)(2,1)S(1)}, u32[]{:S(2)}, u32[]{:S(2)}) collective-permute-start(bf16[64,1024]{1,0:T(8,128)(2,1)S(1)} %get-tuple-element.61), channel_id=1, source_target_pairs={{0,6},{1,7},{2,0},{3,1},{4,2},{5,3},{6,4},{7,5},{8,14},{9,15},{10,... | collective-permute-start | bytes 393224 | tf_op jit(solution)/shard_map/ppermute | solution.py:470
  68.8 11.4 %collective-permute-start.24 = (bf16[64,1024]{1,0:T(8,128)(2,1)S(1)}, bf16[64,1024]{1,0:T(8,128)(2,1)S(1)}, u32[]{:S(2)}, u32[]{:S(2)}) collective-permute-start(bf16[64,1024]{1,0:T(8,128)(2,1)S(1)} %get-tuple-element.62), channel_id=1, source_target_pairs={{0,1},{1,2},{2,3},{3,4},{4,5},{5,6},{6,7},{7,0},{8,9},{9,10},{10,1... | collective-permute-start | bytes 393224 | tf_op jit(solution)/shard_map/ppermute | solution.py:470
  69.0 11.2 %collective-permute-start.25 = (bf16[64,1024]{1,0:T(8,128)(2,1)S(1)}, bf16[64,1024]{1,0:T(8,128)(2,1)S(1)}, u32[]{:S(2)}, u32[]{:S(2)}) collective-permute-start(bf16[64,1024]{1,0:T(8,128)(2,1)S(1)} %get-tuple-element.63), channel_id=1, source_target_pairs={{0,7},{1,0},{2,1},{3,2},{4,3},{5,4},{6,5},{7,6},{8,15},{9,8},{10,9... | collective-permute-start | bytes 393224 | tf_op jit(solution)/shard_map/ppermute | solution.py:470
  71.5 11.8 %collective-permute-start.28 = (bf16[4,16,128]{2,1,0:T(8,128)(2,1)S(1)}, bf16[4,16,128]{2,1,0:T(8,128)(2,1)S(1)}, u32[]{:S(2)}, u32[]{:S(2)}) collective-permute-start(bf16[4,16,128]{2,1,0:T(8,128)(2,1)S(1)} %pad_maximum_fusion.2), channel_id=1, source_target_pairs={{0,8},{8,0},{16,24},{24,16},{32,40},{40,32},{48,56},{56,48},{64,72... | collective-permute-start | bytes 49160 | tf_op jit(solution)/shard_map/ppermute | solution.py:443
  80.3 3.9 %collective-permute-start.27 = (bf16[64,512]{1,0:T(8,128)(2,1)S(1)}, bf16[64,512]{1,0:T(8,128)(2,1)S(1)}, u32[]{:S(2)}, u32[]{:S(2)}) collective-permute-start(bf16[64,512]{1,0:T(8,128)(2,1)S(1)} %get-tuple-element.66), channel_id=1, source_target_pairs={{0,8},{8,0},{16,24},{24,16},{32,40},{40,32},{48,56},{56,48},{64,72... | collective-permute-start | bytes 196616 | tf_op jit(solution)/shard_map/ppermute | solution.py:443

commit v16 on v14

--- a/solution.py
+++ b/solution.py
@@ -505,10 +505,9 @@
     keep6, down1, keep0, up1 = plain(
         near_body, [SUM, SENT, SUM, SENT], *near[3], *weights, first_near
     )
+    below1, above1 = along_z(up1, 1), along_z(down1, -1)
     up2, down2 = plain(middle_body, [SENT, SENT], keep2, keep6, below3, above3)
     below2, above2 = along_z(up2, 2), along_z(down2, -2)
-    up1, down1, opposite = lax.optimization_barrier((up1, down1, opposite))
-    below1, above1 = along_z(up1, 1), along_z(down1, -1)
     own, other = plain(total_body, [HALF, HALF], keep0, below1, above1, below2, above2, opposite)
     return finish(own, other_core(other), pick)
 

time: 86.4 us -> 85.4 us (0.988)
  no operation moved by 1% of the time
where the time goes in v16:
time: 85.4 us; the launch traced here: 84.9 us
  starting transfers between devices  51 us (60%)
  waiting for transfers between devices  16.4 us (19%)
  Pallas kernels  16.2 us (19%)
  local copies, waits for them, and re-layouts  1.01 us (1%)
    ppermute x11, starting transfers between devices, along(): lax.ppermute(value, 'batch', [(i, i ^ k << shift) for i in range(BATCH)])  23 us
    ppermute x7, starting transfers between devices, along_z(): lax.ppermute(value, 'head', [(i, (i + k) % HEADS) for i in range(HEADS)])  16.3 us
    ppermute x11, starting transfers between devices, turned(): return lax.ppermute(value, 'batch', pairs)  11.6 us
    ppermute x11, waiting for transfers between devices, turned(): return lax.ppermute(value, 'batch', pairs)  8.94 us
    ppermute x11, waiting for transfers between devices, along(): lax.ppermute(value, 'batch', [(i, i ^ k << shift) for i in range(BATCH)])  7.44 us
    pallas_call x2, Pallas kernels, prefix_keep(): pl.pallas_call(prefix_keep_body, out_shape=[out, out], in_specs=[VMEM] *...  3.67 us
    pallas_call x1, Pallas kernels, local_parts(): pl.pallas_call(local_body, out_shape=[out] * 4, in_specs=[HBM] * 6, out_s...  3.51 us
    pallas_call x1, Pallas kernels, prefix_send(): pl.pallas_call(prefix_send_body, out_shape=jax.ShapeDtypeStruct((33, GROU...  3.37 us
  transfers between devices with their start and end apart: 29, of which 10 were waited for; matrix products, arithmetic and copies ran while one was open for 0% of the time, Pallas kernels for 18%

profile of v16, /device:TPU:1, one launch (start us, length us, event | category | flops | bytes accessed | tf_op | source)
XLA Modules:
  0.0 84.9 jit_solution(7595061751987538582)
XLA Ops:
  0.0 3.2 %collective-permute-start.4 = (bf16[2,2048,128]{2,1,0:T(8,128)(2,1)}, bf16[2,2048,128]{2,1,0:T(8,128)(2,1)S(1)}, u32[]{:S(2)}, u32[]{:S(2)}) collective-permute-start(bf16[2,2048,128]{2,1,0:T(8,128)(2,1)} %kv0.5), channel_id=1, source_target_pairs={{0,8},{8,0},{16,24},{24,16},{32,40},{40,32},{48,56},{56,48},{64,72... | collective-permute-start | bytes 3145736 | tf_op jit(solution)/shard_map/ppermute | solution.py:443
  3.2 3.5 %local_parts.1 = (bf16[18,16,128]{2,1,0:T(8,128)(2,1)}, bf16[18,16,128]{2,1,0:T(8,128)(2,1)}, bf16[18,16,128]{2,1,0:T(8,128)(2,1)}, bf16[18,16,128]{2,1,0:T(8,128)(2,1)}) custom-call(bf16[32,2048]{1,0:T(8,128)(2,1)} %q_in.1, s32[32]{0:T(128)} %prompt_in.1, s32[8,32]{1,0:T(8,128)} %bitcast.1, s32[32]{0:T(128)} %length_in.1, bf16[2,32,128]{2,1,0:T(8,128)(2,1)} %new_in.1, ...), custom_call_target="tpu_custom_call" | custom-call | tf_op jit(solution)/shard_map/local_parts/pallas_call | solution.py:131
  6.8 1.1 %collective-permute-start = (bf16[18,16,128]{2,1,0:T(8,128)(2,1)}, bf16[18,16,128]{2,1,0:T(8,128)(2,1)S(1)}, u32[]{:S(2)}, u32[]{:S(2)}) collective-permute-start(bf16[18,16,128]{2,1,0:T(8,128)(2,1)} %get-tuple-element.32), channel_id=1, source_target_pairs={{0,128},{8,136},{16,144},{24,152},{32,160},{40,168},{48,176},{56,1... | collective-permute-start | bytes 221192 | tf_op jit(solution)/shard_map/ppermute | solution.py:443
  7.9 0.3 collective-permute-start.1
  8.2 1.9 %collective-permute-start.2 = (bf16[18,16,128]{2,1,0:T(8,128)(2,1)}, bf16[18,16,128]{2,1,0:T(8,128)(2,1)S(1)}, u32[]{:S(2)}, u32[]{:S(2)}) collective-permute-start(bf16[18,16,128]{2,1,0:T(8,128)(2,1)} %get-tuple-element.34), channel_id=1, source_target_pairs={{0,192},{8,200},{16,208},{24,216},{32,224},{40,232},{48,240},{56,2... | collective-permute-start | bytes 221192 | tf_op jit(solution)/shard_map/ppermute | solution.py:443
  10.1 2.3 %collective-permute-done.a2.s2 = bf16[18,16,128]{2,1,0:T(8,128)(2,1)S(1)} collective-permute-done((bf16[18,16,128]{2,1,0:T(8,128)(2,1)}, bf16[18,16,128]{2,1,0:T(8,128)(2,1)S(1)}, u32[]{:S(2)}, u32[]{:S(2)}) %collective-permute-start) | collective-permute-done | bytes 73760 | tf_op jit(solution)/shard_map/ppermute | solution.py:443
  12.4 0.0 collective-permute-done.1.a1.s1
  12.4 1.5 %collective-permute-done.2.a3.s3 = bf16[18,16,128]{2,1,0:T(8,128)(2,1)S(1)} collective-permute-done((bf16[18,16,128]{2,1,0:T(8,128)(2,1)}, bf16[18,16,128]{2,1,0:T(8,128)(2,1)S(1)}, u32[]{:S(2)}, u32[]{:S(2)}) %collective-permute-start.2) | collective-permute-done | bytes 73760 | tf_op jit(solution)/shard_map/ppermute | solution.py:443
  13.9 0.9 %copy-done.2 = bf16[18,16,128]{2,1,0:T(8,128)(2,1)S(1)} copy-done((bf16[18,16,128]{2,1,0:T(8,128)(2,1)S(1)}, bf16[18,16,128]{2,1,0:T(8,128)(2,1)}, u32[]{:S(2)}) %copy-start.2) | copy-done | bytes 73752
  14.8 1.7 %collective-permute-start.3 = (bf16[37,16,128]{2,1,0:T(8,128)(2,1)S(1)}, bf16[37,16,128]{2,1,0:T(8,128)(2,1)S(1)}, u32[]{:S(2)}, u32[]{:S(2)}) collective-permute-start(bf16[37,16,128]{2,1,0:T(8,128)(2,1)S(1)} %get-tuple-element.36), channel_id=1, source_target_pairs={{0,48},{8,56},{16,32},{24,40},{32,16},{40,24},{48,0},{56,8},{64,11... | collective-permute-start | bytes 454664 | tf_op jit(solution)/shard_map/ppermute | solution.py:443
  16.5 0.0 collective-permute-start.5
  16.5 0.0 collective-permute-done.4.kv1
  16.6 1.8 %prefix_keep.2 = (f32[16,16,128]{2,1,0:T(8,128)S(1)}, f32[16,16,128]{2,1,0:T(8,128)S(1)}) custom-call(bf16[17,16,128]{2,1,0:T(8,128)(2,1)S(1)} %get-tuple-element.37.q, bf16[2,2048,128]{2,1,0:T(8,128)(2,1)S(1)} %copy-done.1, bf16[2,2048,128]{2,1,0:T(8,128)(2,1)S(1)} %collective-permute-done.4.kv1), custom_call_target="tpu_custom_call" | custom-call | flops 536870912 | bytes 2500000 | tf_op jit(solution)/shard_map/prefix_keep/pallas_call | solution.py:246
  18.4 0.0 copy-start
  18.4 2.2 %collective-permute-done.3.qb = bf16[37,16,128]{2,1,0:T(8,128)(2,1)S(1)} collective-permute-done((bf16[37,16,128]{2,1,0:T(8,128)(2,1)S(1)}, bf16[37,16,128]{2,1,0:T(8,128)(2,1)S(1)}, u32[]{:S(2)}, u32[]{:S(2)}) %collective-permute-start.3) | collective-permute-done | bytes 151584 | tf_op jit(solution)/shard_map/ppermute | solution.py:443
  20.6 0.0 collective-permute-start.6
  20.6 0.0 collective-permute-done.5.qa
  20.6 3.4 %prefix_send.1 = bf16[33,16,128]{2,1,0:T(8,128)(2,1)S(1)} custom-call(bf16[17,16,128]{2,1,0:T(8,128)(2,1)S(1)} %collective-permute-done.5.qa, bf16[37,16,128]{2,1,0:T(8,128)(2,1)S(1)} %collective-permute-done.3.qb, bf16[2,2048,128]{2,1,0:T(8,128)(2,1)S(1)} %copy-done.1, bf16[2,2048,128]{2,1,0:T(8,128)(2,1)S(1)} %collective-permute-done.4.kv1, ...), custom_call_target="tpu_custom_call" | custom-call | flops 1073741824 | bytes 2500000 | tf_op jit(solution)/shard_map/prefix_send/pallas_call | solution.py:233
  24.0 0.0 copy-start.3
  24.0 0.6 collective-permute-done.6.q.far
  24.7 0.9 %collective-permute-start.7 = (bf16[33,16,128]{2,1,0:T(8,128)(2,1)S(1)}, bf16[33,16,128]{2,1,0:T(8,128)(2,1)S(1)}, u32[]{:S(2)}, u32[]{:S(2)}) collective-permute-start(bf16[33,16,128]{2,1,0:T(8,128)(2,1)S(1)} %prefix_send.1), channel_id=1, source_target_pairs={{0,16},{8,24},{16,0},{24,8},{32,48},{40,56},{48,32},{56,40},{64,80... | collective-permute-start | bytes 405512 | tf_op jit(solution)/shard_map/ppermute | solution.py:443
  25.6 2.4 %collective-permute-start.15 = (bf16[2048,512]{1,0:T(8,128)(2,1)S(1)}, bf16[2048,512]{1,0:T(8,128)(2,1)S(1)}, u32[]{:S(2)}, u32[]{:S(2)}) collective-permute-start(bf16[2048,512]{1,0:T(8,128)(2,1)S(1)} %copy-done), channel_id=1, source_target_pairs={{0,8},{8,0},{16,24},{24,16},{32,40},{40,32},{48,56},{56,48},{64,72... | collective-permute-start | bytes 6291464 | tf_op jit(solution)/shard_map/ppermute | solution.py:443
  28.0 1.8 %prefix_keep.3 = (f32[16,16,128]{2,1,0:T(8,128)S(1)}, f32[16,16,128]{2,1,0:T(8,128)S(1)}) custom-call(bf16[37,16,128]{2,1,0:T(8,128)(2,1)S(1)} %collective-permute-done.6.q.far, bf16[2,2048,128]{2,1,0:T(8,128)(2,1)S(1)} %copy-done.1, bf16[2,2048,128]{2,1,0:T(8,128)(2,1)S(1)} %collective-permute-done.4.kv1), custom_call_target="tpu_custom_call" | custom-call | flops 536870912 | bytes 2500000 | tf_op jit(solution)/shard_map/prefix_keep/pallas_call | solution.py:246
  29.9 0.7 combine.1
  30.5 4.5 %collective-permute-start.8 = (bf16[32,2048]{1,0:T(8,128)(2,1)S(1)}, bf16[32,2048]{1,0:T(8,128)(2,1)S(1)}, u32[]{:S(2)}, u32[]{:S(2)}) collective-permute-start(bf16[32,2048]{1,0:T(8,128)(2,1)S(1)} %combine.1), channel_id=1, source_target_pairs={{0,128},{8,40},{16,144},{24,56},{32,160},{40,8},{48,176},{56,24},{... | collective-permute-start | bytes 393224 | tf_op jit(solution)/shard_map/ppermute | solution.py:460
  35.0 0.4 collective-permute-start.10
  35.4 2.0 %collective-permute-done.8 = bf16[32,2048]{1,0:T(8,128)(2,1)S(1)} collective-permute-done((bf16[32,2048]{1,0:T(8,128)(2,1)S(1)}, bf16[32,2048]{1,0:T(8,128)(2,1)S(1)}, u32[]{:S(2)}, u32[]{:S(2)}) %collective-permute-start.8) | collective-permute-done | bytes 131104 | tf_op jit(solution)/shard_map/ppermute | solution.py:460
  37.4 1.7 %collective-permute-done.9 = bf16[32,2048]{1,0:T(8,128)(2,1)S(1)} collective-permute-done((bf16[32,2048]{1,0:T(8,128)(2,1)S(1)}, bf16[32,2048]{1,0:T(8,128)(2,1)S(1)}, u32[]{:S(2)}, u32[]{:S(2)}) %collective-permute-start.9) | collective-permute-done | bytes 131104 | tf_op jit(solution)/shard_map/ppermute | solution.py:460
  39.1 0.9 %collective-permute-done.10 = bf16[32,2048]{1,0:T(8,128)(2,1)S(1)} collective-permute-done((bf16[32,2048]{1,0:T(8,128)(2,1)S(1)}, bf16[32,2048]{1,0:T(8,128)(2,1)S(1)}, u32[]{:S(2)}, u32[]{:S(2)}) %collective-permute-start.10) | collective-permute-done | bytes 131104 | tf_op jit(solution)/shard_map/ppermute | solution.py:460
  40.1 0.9 %collective-permute-start.18 = (bf16[64,2048]{1,0:T(8,128)(2,1)S(1)}, bf16[64,2048]{1,0:T(8,128)(2,1)S(1)}, u32[]{:S(2)}, u32[]{:S(2)}) collective-permute-start(bf16[64,2048]{1,0:T(8,128)(2,1)S(1)} %pad_maximum_fusion.1.a), channel_id=1, source_target_pairs={{0,48},{8,200},{16,32},{24,216},{32,16},{40,232},{48,0},{56,248},{... | collective-permute-start | bytes 786440 | tf_op jit(solution)/shard_map/ppermute | solution.py:460
  41.0 2.0 %collective-permute-start.11 = (bf16[64,2048]{1,0:T(8,128)(2,1)S(1)}, bf16[64,2048]{1,0:T(8,128)(2,1)S(1)}, u32[]{:S(2)}, u32[]{:S(2)}) collective-permute-start(bf16[64,2048]{1,0:T(8,128)(2,1)S(1)} %pad_maximum_fusion.a), channel_id=1, source_target_pairs={{0,48},{8,200},{16,32},{24,216},{32,16},{40,232},{48,0},{56,248},{... | collective-permute-start | bytes 786440 | tf_op jit(solution)/shard_map/ppermute | solution.py:460
  43.0 0.9 %collective-permute-start.13 = (bf16[64,2048]{1,0:T(8,128)(2,1)S(1)}, bf16[64,2048]{1,0:T(8,128)(2,1)S(1)}, u32[]{:S(2)}, u32[]{:S(2)}) collective-permute-start(bf16[64,2048]{1,0:T(8,128)(2,1)S(1)} %pad_maximum_fusion.a), channel_id=1, source_target_pairs={{0,16},{8,72},{16,0},{24,88},{32,48},{40,104},{48,32},{56,120},{64... | collective-permute-start | bytes 786440 | tf_op jit(solution)/shard_map/ppermute | solution.py:460
  43.8 2.8 %collective-permute-done.18.c = bf16[64,2048]{1,0:T(8,128)(2,1)S(1)} collective-permute-done((bf16[64,2048]{1,0:T(8,128)(2,1)S(1)}, bf16[64,2048]{1,0:T(8,128)(2,1)S(1)}, u32[]{:S(2)}, u32[]{:S(2)}) %collective-permute-start.18) | collective-permute-done | bytes 262176 | tf_op jit(solution)/shard_map/ppermute | solution.py:460
  46.6 0.1 collective-permute-start.19
  46.7 1.4 %collective-permute-start.21 = (bf16[32,2048]{1,0:T(8,128)(2,1)S(1)}, bf16[32,2048]{1,0:T(8,128)(2,1)S(1)}, u32[]{:S(2)}, u32[]{:S(2)}) collective-permute-start(bf16[32,2048]{1,0:T(8,128)(2,1)S(1)} %slice.75), channel_id=1, source_target_pairs={{0,48},{8,200},{16,32},{24,216},{32,16},{40,232},{48,0},{56,248},{... | collective-permute-start | bytes 393224 | tf_op jit(solution)/shard_map/ppermute | solution.py:460
  48.2 1.5 %collective-permute-done.11.c = bf16[64,2048]{1,0:T(8,128)(2,1)S(1)} collective-permute-done((bf16[64,2048]{1,0:T(8,128)(2,1)S(1)}, bf16[64,2048]{1,0:T(8,128)(2,1)S(1)}, u32[]{:S(2)}, u32[]{:S(2)}) %collective-permute-start.11) | collective-permute-done | bytes 262176 | tf_op jit(solution)/shard_map/ppermute | solution.py:460
  49.7 0.1 collective-permute-start.12
  49.8 1.4 %collective-permute-start.14 = (bf16[32,2048]{1,0:T(8,128)(2,1)S(1)}, bf16[32,2048]{1,0:T(8,128)(2,1)S(1)}, u32[]{:S(2)}, u32[]{:S(2)}) collective-permute-start(bf16[32,2048]{1,0:T(8,128)(2,1)S(1)} %slice.69), channel_id=1, source_target_pairs={{0,48},{8,200},{16,32},{24,216},{32,16},{40,232},{48,0},{56,248},{... | collective-permute-start | bytes 393224 | tf_op jit(solution)/shard_map/ppermute | solution.py:460
  51.3 1.0 %project.3.first = f32[4,48,1024]{2,1,0:T(8,128)S(1)} custom-call(bf16[64,2048]{1,0:T(8,128)(2,1)S(1)} %pad_maximum_fusion.1.a, bf16[64,2048]{1,0:T(8,128)(2,1)S(1)} %collective-permute-done.20.b, bf16[64,2048]{1,0:T(8,128)(2,1)S(1)} %collective-permute-done.18.c, bf16[2048,512]{1,0:T(8,128)(2,1)S(1)} %copy-done, ...), custom_call_target="tpu_custom_call" | custom-call | flops 805306368 | bytes 4500000 | tf_op jit(solution)/shard_map/project/pallas_call | solution.py:325
  52.3 0.0 collective-permute-done.19.a
  52.3 0.0 collective-permute-done.21.b
  52.3 0.9 %far.1 = (f32[64,1024]{1,0:T(8,128)S(1)}, bf16[64,1024]{1,0:T(8,128)(2,1)S(1)}, bf16[64,1024]{1,0:T(8,128)(2,1)S(1)}, bf16[64,1024]{1,0:T(8,128)(2,1)S(1)}) custom-call(bf16[32,2048]{1,0:T(8,128)(2,1)S(1)} %collective-permute-done.19.a, bf16[32,2048]{1,0:T(8,128)(2,1)S(1)} %collective-permute-done.21.b, bf16[2048,512]{1,0:T(8,128)(2,1)S(1)} %copy-done, ...), custom_call_target="tpu_custom_call" | custom-call | tf_op jit(solution)/shard_map/far/pallas_call | solution.py:368
  53.2 2.0 %collective-permute-start.22 = (bf16[64,1024]{1,0:T(8,128)(2,1)S(1)}, bf16[64,1024]{1,0:T(8,128)(2,1)S(1)}, u32[]{:S(2)}, u32[]{:S(2)}) collective-permute-start(bf16[64,1024]{1,0:T(8,128)(2,1)S(1)} %get-tuple-element.52), channel_id=1, source_target_pairs={{0,1},{1,2},{2,3},{3,4},{4,5},{5,6},{6,7},{7,0},{8,9},{9,10},{10,1... | collective-permute-start | bytes 393224 | tf_op jit(solution)/shard_map/ppermute | solution.py:470
  55.2 4.0 %collective-permute-start.23 = (bf16[64,1024]{1,0:T(8,128)(2,1)S(1)}, bf16[64,1024]{1,0:T(8,128)(2,1)S(1)}, u32[]{:S(2)}, u32[]{:S(2)}) collective-permute-start(bf16[64,1024]{1,0:T(8,128)(2,1)S(1)} %get-tuple-element.53), channel_id=1, source_target_pairs={{0,7},{1,0},{2,1},{3,2},{4,3},{5,4},{6,5},{7,6},{8,15},{9,8},{10,9... | collective-permute-start | bytes 393224 | tf_op jit(solution)/shard_map/ppermute | solution.py:470
  59.2 3.9 %collective-permute-start.26 = (bf16[64,1024]{1,0:T(8,128)(2,1)S(1)}, bf16[64,1024]{1,0:T(8,128)(2,1)S(1)}, u32[]{:S(2)}, u32[]{:S(2)}) collective-permute-start(bf16[64,1024]{1,0:T(8,128)(2,1)S(1)} %get-tuple-element.56), channel_id=1, source_target_pairs={{0,4},{1,5},{2,6},{3,7},{4,0},{5,1},{6,2},{7,3},{8,12},{9,13},{10,... | collective-permute-start | bytes 393224 | tf_op jit(solution)/shard_map/ppermute | solution.py:470
  63.2 1.0 %project.2.first = f32[4,48,1024]{2,1,0:T(8,128)S(1)} custom-call(bf16[64,2048]{1,0:T(8,128)(2,1)S(1)} %pad_maximum_fusion.a, bf16[64,2048]{1,0:T(8,128)(2,1)S(1)} %collective-permute-done.13.b, bf16[64,2048]{1,0:T(8,128)(2,1)S(1)} %collective-permute-done.11.c, bf16[2048,512]{1,0:T(8,128)(2,1)S(1)} %copy-done, bf16[2048,512]{1,0:T(8,128)(2,1)S(1)} %collective-permute-done.15.w1), custom_call_target="tpu_custom_call" | custom-call | flops 805306368 | bytes 4500000 | tf_op jit(solution)/shard_map/project/pallas_call | solution.py:325
  64.2 0.0 collective-permute-done.12.a
  64.2 0.0 collective-permute-done.14.b
  64.2 0.9 %near.1 = (f32[64,1024]{1,0:T(8,128)S(1)}, bf16[64,1024]{1,0:T(8,128)(2,1)S(1)}, f32[64,1024]{1,0:T(8,128)S(1)}, bf16[64,1024]{1,0:T(8,128)(2,1)S(1)}) custom-call(bf16[32,2048]{1,0:T(8,128)(2,1)S(1)} %collective-permute-done.12.a, bf16[32,2048]{1,0:T(8,128)(2,1)S(1)} %collective-permute-done.14.b, bf16[2048,512]{1,0:T(8,128)(2,1)S(1)} %copy-done, ...), custom_call_target="tpu_custom_call" | custom-call | tf_op jit(solution)/shard_map/near/pallas_call | solution.py:368
  65.1 0.1 collective-permute-start.16
  65.2 2.7 %collective-permute-start.17 = (bf16[64,1024]{1,0:T(8,128)(2,1)S(1)}, bf16[64,1024]{1,0:T(8,128)(2,1)S(1)}, u32[]{:S(2)}, u32[]{:S(2)}) collective-permute-start(bf16[64,1024]{1,0:T(8,128)(2,1)S(1)} %get-tuple-element.49), channel_id=1, source_target_pairs={{0,7},{1,0},{2,1},{3,2},{4,3},{5,4},{6,5},{7,6},{8,15},{9,8},{10,9... | collective-permute-start | bytes 393224 | tf_op jit(solution)/shard_map/ppermute | solution.py:470
  67.8 0.0 collective-permute-done.22.below
  67.9 0.0 collective-permute-done.23.above
  67.9 0.1 middle.1
  67.9 0.1 collective-permute-start.24
  68.0 3.6 %collective-permute-start.25 = (bf16[64,1024]{1,0:T(8,128)(2,1)S(1)}, bf16[64,1024]{1,0:T(8,128)(2,1)S(1)}, u32[]{:S(2)}, u32[]{:S(2)}) collective-permute-start(bf16[64,1024]{1,0:T(8,128)(2,1)S(1)} %get-tuple-element.55), channel_id=1, source_target_pairs={{0,6},{1,7},{2,0},{3,1},{4,2},{5,3},{6,4},{7,5},{8,14},{9,15},{10,... | collective-permute-start | bytes 393224 | tf_op jit(solution)/shard_map/ppermute | solution.py:470
  71.6 0.0 collective-permute-done.26.opposite
  71.6 7.1 %collective-permute-start.28 = (bf16[4,16,128]{2,1,0:T(8,128)(2,1)S(1)}, bf16[4,16,128]{2,1,0:T(8,128)(2,1)S(1)}, u32[]{:S(2)}, u32[]{:S(2)}) collective-permute-start(bf16[4,16,128]{2,1,0:T(8,128)(2,1)S(1)} %pad_maximum_fusion.2), channel_id=1, source_target_pairs={{0,8},{8,0},{16,24},{24,16},{32,40},{40,32},{48,56},{56,48},{64,72... | collective-permute-start | bytes 49160 | tf_op jit(solution)/shard_map/ppermute | solution.py:443
  78.7 0.0 collective-permute-done.25.above2
  78.7 0.1 total.1
  78.8 4.3 %collective-permute-start.27 = (bf16[64,512]{1,0:T(8,128)(2,1)S(1)}, bf16[64,512]{1,0:T(8,128)(2,1)S(1)}, u32[]{:S(2)}, u32[]{:S(2)}) collective-permute-start(bf16[64,512]{1,0:T(8,128)(2,1)S(1)} %get-tuple-element.58), channel_id=1, source_target_pairs={{0,8},{8,0},{16,24},{24,16},{32,40},{40,32},{48,56},{56,48},{64,72... | collective-permute-start | bytes 196616 | tf_op jit(solution)/shard_map/ppermute | solution.py:443
  83.1 0.1 order_rows.1.pick
  83.2 0.8 collective-permute-done.27.other
  84.0 0.9 %finish.1 = bf16[128,512]{1,0:T(8,128)(2,1)} custom-call(bf16[64,512]{1,0:T(8,128)(2,1)S(1)} %get-tuple-element.57.own, bf16[64,512]{1,0:T(8,128)(2,1)S(1)} %collective-permute-done.27.other, bf16[128,128]{1,0:T(8,128)(2,1)S(1)} %order_rows.1.pick), custom_call_target="tpu_custom_call" | custom-call | tf_op jit(solution)/shard_map/finish/pallas_call | solution.py:432
  (32 shorter events, 0.2 us)
Async XLA Ops:
  0.0 16.6 %copy-start.1 = (bf16[2,2048,128]{2,1,0:T(8,128)(2,1)S(1)}, bf16[2,2048,128]{2,1,0:T(8,128)(2,1)}, u32[]{:S(2)}) copy-start(bf16[2,2048,128]{2,1,0:T(8,128)(2,1)} %kv0.5) | copy-start | bytes 3145732
  0.0 16.5 %collective-permute-start.4 = (bf16[2,2048,128]{2,1,0:T(8,128)(2,1)}, bf16[2,2048,128]{2,1,0:T(8,128)(2,1)S(1)}, u32[]{:S(2)}, u32[]{:S(2)}) collective-permute-start(bf16[2,2048,128]{2,1,0:T(8,128)(2,1)} %kv0.5), channel_id=1, source_target_pairs={{0,8},{8,0},{16,24},{24,16},{32,40},{40,32},{48,56},{56,48},{64,72... | collective-permute-start | bytes 3145736 | tf_op jit(solution)/shard_map/ppermute | solution.py:443
  6.8 5.6 %collective-permute-start = (bf16[18,16,128]{2,1,0:T(8,128)(2,1)}, bf16[18,16,128]{2,1,0:T(8,128)(2,1)S(1)}, u32[]{:S(2)}, u32[]{:S(2)}) collective-permute-start(bf16[18,16,128]{2,1,0:T(8,128)(2,1)} %get-tuple-element.32), channel_id=1, source_target_pairs={{0,128},{8,136},{16,144},{24,152},{32,160},{40,168},{48,176},{56,1... | collective-permute-start | bytes 221192 | tf_op jit(solution)/shard_map/ppermute | solution.py:443
  7.9 4.5 %collective-permute-start.1 = (bf16[18,16,128]{2,1,0:T(8,128)(2,1)}, bf16[18,16,128]{2,1,0:T(8,128)(2,1)S(1)}, u32[]{:S(2)}, u32[]{:S(2)}) collective-permute-start(bf16[18,16,128]{2,1,0:T(8,128)(2,1)} %get-tuple-element.33), channel_id=1, source_target_pairs={{0,64},{8,72},{16,80},{24,88},{32,96},{40,104},{48,112},{56,120},{... | collective-permute-start | bytes 221192 | tf_op jit(solution)/shard_map/ppermute | solution.py:443
  8.2 5.7 %collective-permute-start.2 = (bf16[18,16,128]{2,1,0:T(8,128)(2,1)}, bf16[18,16,128]{2,1,0:T(8,128)(2,1)S(1)}, u32[]{:S(2)}, u32[]{:S(2)}) collective-permute-start(bf16[18,16,128]{2,1,0:T(8,128)(2,1)} %get-tuple-element.34), channel_id=1, source_target_pairs={{0,192},{8,200},{16,208},{24,216},{32,224},{40,232},{48,240},{56,2... | collective-permute-start | bytes 221192 | tf_op jit(solution)/shard_map/ppermute | solution.py:443
  13.9 0.9 %copy-start.2 = (bf16[18,16,128]{2,1,0:T(8,128)(2,1)S(1)}, bf16[18,16,128]{2,1,0:T(8,128)(2,1)}, u32[]{:S(2)}) copy-start(bf16[18,16,128]{2,1,0:T(8,128)(2,1)} %get-tuple-element.35.a0.s0) | copy-start | bytes 221188
  14.8 5.8 %collective-permute-start.3 = (bf16[37,16,128]{2,1,0:T(8,128)(2,1)S(1)}, bf16[37,16,128]{2,1,0:T(8,128)(2,1)S(1)}, u32[]{:S(2)}, u32[]{:S(2)}) collective-permute-start(bf16[37,16,128]{2,1,0:T(8,128)(2,1)S(1)} %get-tuple-element.36), channel_id=1, source_target_pairs={{0,48},{8,56},{16,32},{24,40},{32,16},{40,24},{48,0},{56,8},{64,11... | collective-permute-start | bytes 454664 | tf_op jit(solution)/shard_map/ppermute | solution.py:443
  16.5 4.1 %collective-permute-start.5 = (bf16[17,16,128]{2,1,0:T(8,128)(2,1)S(1)}, bf16[17,16,128]{2,1,0:T(8,128)(2,1)S(1)}, u32[]{:S(2)}, u32[]{:S(2)}) collective-permute-start(bf16[17,16,128]{2,1,0:T(8,128)(2,1)S(1)} %get-tuple-element.37.q), channel_id=1, source_target_pairs={{0,16},{8,24},{16,0},{24,8},{32,48},{40,56},{48,32},{56,40},{64,80... | collective-permute-start | bytes 208904 | tf_op jit(solution)/shard_map/ppermute | solution.py:443
  18.4 7.2 %copy-start = (bf16[2048,512]{1,0:T(8,128)(2,1)S(1)}, bf16[2048,512]{1,0:T(8,128)(2,1)}, u32[]{:S(2)}) copy-start(bf16[2048,512]{1,0:T(8,128)(2,1)} %w0.7) | copy-start | bytes 6291460
  20.6 4.0 %collective-permute-start.6 = (bf16[37,16,128]{2,1,0:T(8,128)(2,1)S(1)}, bf16[37,16,128]{2,1,0:T(8,128)(2,1)S(1)}, u32[]{:S(2)}, u32[]{:S(2)}) collective-permute-start(bf16[37,16,128]{2,1,0:T(8,128)(2,1)S(1)} %collective-permute-done.3.qb), channel_id=1, source_target_pairs={{0,16},{8,24},{16,0},{24,8},{32,48},{40,56},{48,32},{56,40},{64,80... | collective-permute-start | bytes 454664 | tf_op jit(solution)/shard_map/ppermute | solution.py:443
  24.0 5.8 %copy-start.3 = (bf16[18,16,128]{2,1,0:T(8,128)(2,1)S(1)}, bf16[18,16,128]{2,1,0:T(8,128)(2,1)}, u32[]{:S(2)}) copy-start(bf16[18,16,128]{2,1,0:T(8,128)(2,1)} %get-tuple-element.35.a0.s0) | copy-start | bytes 221188
  24.7 5.2 %collective-permute-start.7 = (bf16[33,16,128]{2,1,0:T(8,128)(2,1)S(1)}, bf16[33,16,128]{2,1,0:T(8,128)(2,1)S(1)}, u32[]{:S(2)}, u32[]{:S(2)}) collective-permute-start(bf16[33,16,128]{2,1,0:T(8,128)(2,1)S(1)} %prefix_send.1), channel_id=1, source_target_pairs={{0,16},{8,24},{16,0},{24,8},{32,48},{40,56},{48,32},{56,40},{64,80... | collective-permute-start | bytes 405512 | tf_op jit(solution)/shard_map/ppermute | solution.py:443
  25.6 25.7 %collective-permute-start.15 = (bf16[2048,512]{1,0:T(8,128)(2,1)S(1)}, bf16[2048,512]{1,0:T(8,128)(2,1)S(1)}, u32[]{:S(2)}, u32[]{:S(2)}) collective-permute-start(bf16[2048,512]{1,0:T(8,128)(2,1)S(1)} %copy-done), channel_id=1, source_target_pairs={{0,8},{8,0},{16,24},{24,16},{32,40},{40,32},{48,56},{56,48},{64,72... | collective-permute-start | bytes 6291464 | tf_op jit(solution)/shard_map/ppermute | solution.py:443
  30.5 6.8 %collective-permute-start.8 = (bf16[32,2048]{1,0:T(8,128)(2,1)S(1)}, bf16[32,2048]{1,0:T(8,128)(2,1)S(1)}, u32[]{:S(2)}, u32[]{:S(2)}) collective-permute-start(bf16[32,2048]{1,0:T(8,128)(2,1)S(1)} %combine.1), channel_id=1, source_target_pairs={{0,128},{8,40},{16,144},{24,56},{32,160},{40,8},{48,176},{56,24},{... | collective-permute-start | bytes 393224 | tf_op jit(solution)/shard_map/ppermute | solution.py:460
  35.0 4.1 %collective-permute-start.9 = (bf16[32,2048]{1,0:T(8,128)(2,1)S(1)}, bf16[32,2048]{1,0:T(8,128)(2,1)S(1)}, u32[]{:S(2)}, u32[]{:S(2)}) collective-permute-start(bf16[32,2048]{1,0:T(8,128)(2,1)S(1)} %combine.1), channel_id=1, source_target_pairs={{0,64},{8,24},{16,80},{24,8},{32,96},{40,56},{48,112},{56,40},{64,... | collective-permute-start | bytes 393224 | tf_op jit(solution)/shard_map/ppermute | solution.py:460
  35.0 5.0 %collective-permute-start.10 = (bf16[32,2048]{1,0:T(8,128)(2,1)S(1)}, bf16[32,2048]{1,0:T(8,128)(2,1)S(1)}, u32[]{:S(2)}, u32[]{:S(2)}) collective-permute-start(bf16[32,2048]{1,0:T(8,128)(2,1)S(1)} %combine.1), channel_id=1, source_target_pairs={{0,192},{8,56},{16,208},{24,40},{32,224},{40,24},{48,240},{56,8},{... | collective-permute-start | bytes 393224 | tf_op jit(solution)/shard_map/ppermute | solution.py:460
  40.1 6.5 %collective-permute-start.18 = (bf16[64,2048]{1,0:T(8,128)(2,1)S(1)}, bf16[64,2048]{1,0:T(8,128)(2,1)S(1)}, u32[]{:S(2)}, u32[]{:S(2)}) collective-permute-start(bf16[64,2048]{1,0:T(8,128)(2,1)S(1)} %pad_maximum_fusion.1.a), channel_id=1, source_target_pairs={{0,48},{8,200},{16,32},{24,216},{32,16},{40,232},{48,0},{56,248},{... | collective-permute-start | bytes 786440 | tf_op jit(solution)/shard_map/ppermute | solution.py:460
  40.9 5.8 %collective-permute-start.20 = (bf16[64,2048]{1,0:T(8,128)(2,1)S(1)}, bf16[64,2048]{1,0:T(8,128)(2,1)S(1)}, u32[]{:S(2)}, u32[]{:S(2)}) collective-permute-start(bf16[64,2048]{1,0:T(8,128)(2,1)S(1)} %pad_maximum_fusion.1.a), channel_id=1, source_target_pairs={{0,16},{8,72},{16,0},{24,88},{32,48},{40,104},{48,32},{56,120},{64... | collective-permute-start | bytes 786440 | tf_op jit(solution)/shard_map/ppermute | solution.py:460
  41.0 8.7 %collective-permute-start.11 = (bf16[64,2048]{1,0:T(8,128)(2,1)S(1)}, bf16[64,2048]{1,0:T(8,128)(2,1)S(1)}, u32[]{:S(2)}, u32[]{:S(2)}) collective-permute-start(bf16[64,2048]{1,0:T(8,128)(2,1)S(1)} %pad_maximum_fusion.a), channel_id=1, source_target_pairs={{0,48},{8,200},{16,32},{24,216},{32,16},{40,232},{48,0},{56,248},{... | collective-permute-start | bytes 786440 | tf_op jit(solution)/shard_map/ppermute | solution.py:460
  43.0 6.9 %collective-permute-start.13 = (bf16[64,2048]{1,0:T(8,128)(2,1)S(1)}, bf16[64,2048]{1,0:T(8,128)(2,1)S(1)}, u32[]{:S(2)}, u32[]{:S(2)}) collective-permute-start(bf16[64,2048]{1,0:T(8,128)(2,1)S(1)} %pad_maximum_fusion.a), channel_id=1, source_target_pairs={{0,16},{8,72},{16,0},{24,88},{32,48},{40,104},{48,32},{56,120},{64... | collective-permute-start | bytes 786440 | tf_op jit(solution)/shard_map/ppermute | solution.py:460
  46.6 5.7 %collective-permute-start.19 = (bf16[32,2048]{1,0:T(8,128)(2,1)S(1)}, bf16[32,2048]{1,0:T(8,128)(2,1)S(1)}, u32[]{:S(2)}, u32[]{:S(2)}) collective-permute-start(bf16[32,2048]{1,0:T(8,128)(2,1)S(1)} %slice.74), channel_id=1, source_target_pairs={{0,16},{8,72},{16,0},{24,88},{32,48},{40,104},{48,32},{56,120},{64... | collective-permute-start | bytes 393224 | tf_op jit(solution)/shard_map/ppermute | solution.py:460
  46.7 5.6 %collective-permute-start.21 = (bf16[32,2048]{1,0:T(8,128)(2,1)S(1)}, bf16[32,2048]{1,0:T(8,128)(2,1)S(1)}, u32[]{:S(2)}, u32[]{:S(2)}) collective-permute-start(bf16[32,2048]{1,0:T(8,128)(2,1)S(1)} %slice.75), channel_id=1, source_target_pairs={{0,48},{8,200},{16,32},{24,216},{32,16},{40,232},{48,0},{56,248},{... | collective-permute-start | bytes 393224 | tf_op jit(solution)/shard_map/ppermute | solution.py:460
  49.7 14.5 %collective-permute-start.12 = (bf16[32,2048]{1,0:T(8,128)(2,1)S(1)}, bf16[32,2048]{1,0:T(8,128)(2,1)S(1)}, u32[]{:S(2)}, u32[]{:S(2)}) collective-permute-start(bf16[32,2048]{1,0:T(8,128)(2,1)S(1)} %slice.68), channel_id=1, source_target_pairs={{0,16},{8,72},{16,0},{24,88},{32,48},{40,104},{48,32},{56,120},{64... | collective-permute-start | bytes 393224 | tf_op jit(solution)/shard_map/ppermute | solution.py:460
  49.8 14.4 %collective-permute-start.14 = (bf16[32,2048]{1,0:T(8,128)(2,1)S(1)}, bf16[32,2048]{1,0:T(8,128)(2,1)S(1)}, u32[]{:S(2)}, u32[]{:S(2)}) collective-permute-start(bf16[32,2048]{1,0:T(8,128)(2,1)S(1)} %slice.69), channel_id=1, source_target_pairs={{0,48},{8,200},{16,32},{24,216},{32,16},{40,232},{48,0},{56,248},{... | collective-permute-start | bytes 393224 | tf_op jit(solution)/shard_map/ppermute | solution.py:460
  53.2 14.6 %collective-permute-start.22 = (bf16[64,1024]{1,0:T(8,128)(2,1)S(1)}, bf16[64,1024]{1,0:T(8,128)(2,1)S(1)}, u32[]{:S(2)}, u32[]{:S(2)}) collective-permute-start(bf16[64,1024]{1,0:T(8,128)(2,1)S(1)} %get-tuple-element.52), channel_id=1, source_target_pairs={{0,1},{1,2},{2,3},{3,4},{4,5},{5,6},{6,7},{7,0},{8,9},{9,10},{10,1... | collective-permute-start | bytes 393224 | tf_op jit(solution)/shard_map/ppermute | solution.py:470
  55.2 12.6 %collective-permute-start.23 = (bf16[64,1024]{1,0:T(8,128)(2,1)S(1)}, bf16[64,1024]{1,0:T(8,128)(2,1)S(1)}, u32[]{:S(2)}, u32[]{:S(2)}) collective-permute-start(bf16[64,1024]{1,0:T(8,128)(2,1)S(1)} %get-tuple-element.53), channel_id=1, source_target_pairs={{0,7},{1,0},{2,1},{3,2},{4,3},{5,4},{6,5},{7,6},{8,15},{9,8},{10,9... | collective-permute-start | bytes 393224 | tf_op jit(solution)/shard_map/ppermute | solution.py:470
  59.2 12.3 %collective-permute-start.26 = (bf16[64,1024]{1,0:T(8,128)(2,1)S(1)}, bf16[64,1024]{1,0:T(8,128)(2,1)S(1)}, u32[]{:S(2)}, u32[]{:S(2)}) collective-permute-start(bf16[64,1024]{1,0:T(8,128)(2,1)S(1)} %get-tuple-element.56), channel_id=1, source_target_pairs={{0,4},{1,5},{2,6},{3,7},{4,0},{5,1},{6,2},{7,3},{8,12},{9,13},{10,... | collective-permute-start | bytes 393224 | tf_op jit(solution)/shard_map/ppermute | solution.py:470
  65.1 13.6 %collective-permute-start.16 = (bf16[64,1024]{1,0:T(8,128)(2,1)S(1)}, bf16[64,1024]{1,0:T(8,128)(2,1)S(1)}, u32[]{:S(2)}, u32[]{:S(2)}) collective-permute-start(bf16[64,1024]{1,0:T(8,128)(2,1)S(1)} %get-tuple-element.48), channel_id=1, source_target_pairs={{0,1},{1,2},{2,3},{3,4},{4,5},{5,6},{6,7},{7,0},{8,9},{9,10},{10,1... | collective-permute-start | bytes 393224 | tf_op jit(solution)/shard_map/ppermute | solution.py:470
  65.2 13.5 %collective-permute-start.17 = (bf16[64,1024]{1,0:T(8,128)(2,1)S(1)}, bf16[64,1024]{1,0:T(8,128)(2,1)S(1)}, u32[]{:S(2)}, u32[]{:S(2)}) collective-permute-start(bf16[64,1024]{1,0:T(8,128)(2,1)S(1)} %get-tuple-element.49), channel_id=1, source_target_pairs={{0,7},{1,0},{2,1},{3,2},{4,3},{5,4},{6,5},{7,6},{8,15},{9,8},{10,9... | collective-permute-start | bytes 393224 | tf_op jit(solution)/shard_map/ppermute | solution.py:470
  67.9 10.8 %collective-permute-start.24 = (bf16[64,1024]{1,0:T(8,128)(2,1)S(1)}, bf16[64,1024]{1,0:T(8,128)(2,1)S(1)}, u32[]{:S(2)}, u32[]{:S(2)}) collective-permute-start(bf16[64,1024]{1,0:T(8,128)(2,1)S(1)} %get-tuple-element.54), channel_id=1, source_target_pairs={{0,2},{1,3},{2,4},{3,5},{4,6},{5,7},{6,0},{7,1},{8,10},{9,11},{10,... | collective-permute-start | bytes 393224 | tf_op jit(solution)/shard_map/ppermute | solution.py:470
  68.0 10.7 %collective-permute-start.25 = (bf16[64,1024]{1,0:T(8,128)(2,1)S(1)}, bf16[64,1024]{1,0:T(8,128)(2,1)S(1)}, u32[]{:S(2)}, u32[]{:S(2)}) collective-permute-start(bf16[64,1024]{1,0:T(8,128)(2,1)S(1)} %get-tuple-element.55), channel_id=1, source_target_pairs={{0,6},{1,7},{2,0},{3,1},{4,2},{5,3},{6,4},{7,5},{8,14},{9,15},{10,... | collective-permute-start | bytes 393224 | tf_op jit(solution)/shard_map/ppermute | solution.py:470
  71.6 11.5 %collective-permute-start.28 = (bf16[4,16,128]{2,1,0:T(8,128)(2,1)S(1)}, bf16[4,16,128]{2,1,0:T(8,128)(2,1)S(1)}, u32[]{:S(2)}, u32[]{:S(2)}) collective-permute-start(bf16[4,16,128]{2,1,0:T(8,128)(2,1)S(1)} %pad_maximum_fusion.2), channel_id=1, source_target_pairs={{0,8},{8,0},{16,24},{24,16},{32,40},{40,32},{48,56},{56,48},{64,72... | collective-permute-start | bytes 49160 | tf_op jit(solution)/shard_map/ppermute | solution.py:443
  78.8 5.2 %collective-permute-start.27 = (bf16[64,512]{1,0:T(8,128)(2,1)S(1)}, bf16[64,512]{1,0:T(8,128)(2,1)S(1)}, u32[]{:S(2)}, u32[]{:S(2)}) collective-permute-start(bf16[64,512]{1,0:T(8,128)(2,1)S(1)} %get-tuple-element.58), channel_id=1, source_target_pairs={{0,8},{8,0},{16,24},{24,16},{32,40},{40,32},{48,56},{56,48},{64,72... | collective-permute-start | bytes 196616 | tf_op jit(solution)/shard_map/ppermute | solution.py:443
